TPU v7x, 128 devices: a whole 4x4x4 slice. The times are simulated.
128 devices in a mesh: dp: 64 (over z, y, x_lo, core), owner: 2 (over x_hi).
Axes of the slice: x: 4 (x_hi: 2, x_lo: 2; x = x_hi * 2 + x_lo), y: 4, z: 4, core: 2. Of those that a mesh axis runs over, the one named last changes fastest.
Arguments:
- hidden: bfloat16 [49152, 2560], P('dp'), may hold values from -16 to 16
- out_grad: bfloat16 [49152, 2560], P('dp'), may hold values from -0.078125 to 0.078125
- left_inverse: bfloat16 [2560, 2560], P(None, 'owner'), as said below
- right_inverse: bfloat16 [2560, 2560], P(None, 'owner'), as said below
Outputs:
- factors: float32 [2, 2560, 2560], P('owner', 'dp')
- update: float32 [2560, 2560], P('dp', 'owner')
Inputs may be any that keep to these rules, and one draw needn't show every extreme that they name: `left_inverse`: symmetric and positive definite. `right_inverse`: symmetric and positive definite.
All inputs are finite; a program needn't handle non-finite values.
Results may differ from a plain program's by a relative error of at most 0.004.
Values may be sent and summed in bfloat16 or wider, within the bound.
No kernel may reach another device: no remote copies, remote signals or barrier semaphores. Data moves between devices by JAX's collectives and lax.ppermute only.
A program may use at most 192 MiB of HBM per device.

v0:
```python
import functools

import jax
import jax.numpy as jnp
from jax import lax
from jax.experimental import pallas as pl
from jax.experimental.pallas import tpu as pltpu
from jax.sharding import Mesh, PartitionSpec as P

BF = jnp.bfloat16
F32 = jnp.float32
TILE = 640


def contract(first_rows, second_rows):
    return lax.dot_general(
        first_rows, second_rows, (((0,), (0,)), ((), ())), preferred_element_type=F32
    )


def shift(x, axis, step):
    size = lax.axis_size(axis)
    return lax.ppermute(x, axis, [(i, (i + step) % size) for i in range(size)])


def turn(x, step, stage):
    pairs = []
    for z in range(4):
        for y in range(4):
            for c in range(2):
                along_z = (c == 0) == (stage == 0)
                there = ((z + step) % 4, y) if along_z else (z, (y + step) % 4)
                pairs.append(((z * 4 + y) * 2 + c, (there[0] * 4 + there[1]) * 2 + c))
    return lax.ppermute(x, ("z", "y", "c"), pairs)


def pick(x, dim, index):
    return lax.dynamic_index_in_dim(x, index, dim, keepdims=False)


def split_pair(x):
    high = lax.reduce_precision(x, 8, 7)
    return high.astype(BF), (x - high).astype(BF)


def place_blocks(place, buffer, sems, outs, step, zs, finish):
    core, z_me, y_me = place[1], place[2], place[3]
    rows = buffer.shape[1] // (zs * 4)
    for a in range(zs):
        for k in range(4):
            z = step * zs + a
            ahead = jnp.where(core == 0, z - z_me + 4, k - y_me + 4) & 3
            slot = jnp.where(core == 0, k, z)
            part = a * 4 + k
            block = buffer.at[step, pl.ds(part * rows, rows), :]

            def move(target):
                copy = pltpu.make_async_copy(block, target, sems.at[step, part])
                if finish:
                    copy.wait()
                else:
                    copy.start()

            for r, out in enumerate(outs):
                if isinstance(out, (list, tuple)):
                    for side, ref in enumerate(out):
                        pl.when((ahead == r) & ((slot >> 1) == side))(
                            functools.partial(lambda ref: move(ref.at[slot & 1]), ref)
                        )
                else:
                    pl.when(ahead == r)(functools.partial(lambda ref: move(ref.at[slot]), out))


def finish_blocks(place, buffer, sems, outs, steps, zs):
    for step in range(steps):
        place_blocks(place, buffer, sems, outs, step, zs, True)


def cross_kernel(place, a0, a1, b0, b1, own, ahead1, ahead2, ahead3, buffer, sems):
    step = pl.program_id(0)
    outs = [own, ahead1, ahead2, ahead3]
    buffer[step] = (contract(a0[...], b0[...]) + contract(a1[...], b1[...])).astype(BF)
    place_blocks(place, buffer, sems, outs, step, 2, False)

    @pl.when(step == 1)
    def _():
        finish_blocks(place, buffer, sems, outs, 2, 2)


def cross_term(place, grads, grads_next, acts, acts_next):
    tokens, width = grads.shape
    half = width // 2
    left = pl.BlockSpec((tokens, TILE), lambda m, p: (0, p[1] * 2 + m))
    right = pl.BlockSpec((tokens, half), lambda m, p: (0, p[1] ^ p[0]))
    out = jax.ShapeDtypeStruct((4, half // 16, half), BF)
    return pl.pallas_call(
        cross_kernel,
        out_shape=[out] * 4,
        grid_spec=pltpu.PrefetchScalarGridSpec(
            num_scalar_prefetch=1,
            grid=(2,),
            in_specs=[left, left, right, right],
            out_specs=[pl.BlockSpec(memory_space=pl.ANY)] * 4,
            scratch_shapes=[pltpu.VMEM((2, TILE, half), BF), pltpu.SemaphoreType.DMA((2, 8))],
        ),
        compiler_params=pltpu.CompilerParams(vmem_limit_bytes=48 * 2**20),
        cost_estimate=pl.CostEstimate(
            flops=4 * tokens * half * half, bytes_accessed=10 * tokens * half, transcendentals=0
        ),
        name="cross_term",
    )(place, grads, grads_next, acts, acts_next)


def factor_kernel(
    place, ha0, ha1, ga0, ga1, hb0, hb1, gb0, gb1, own, right, far_a, far_b, left, buffer, sems
):
    step = pl.program_id(0)
    outs = [own, right, (far_a, far_b), left]

    def term(a0, a1, b0, b1):
        buffer[step] = (contract(a0[...], b0[...]) + contract(a1[...], b1[...])).astype(BF)

    pl.when(place[0] == 0)(lambda: term(ha0, ha1, hb0, hb1))
    pl.when(place[0] == 1)(lambda: term(ga0, ga1, gb0, gb1))
    place_blocks(place, buffer, sems, outs, step, 1, False)

    @pl.when(step == 3)
    def _():
        finish_blocks(place, buffer, sems, outs, 4, 1)


def factor_term(place, acts, acts_next, grads, grads_next):
    tokens, width = acts.shape
    half = width // 2
    a_acts = pl.BlockSpec((tokens, TILE), lambda m, p: (0, m * (1 - p[0])))
    a_grads = pl.BlockSpec((tokens, TILE), lambda m, p: (0, m * p[0]))
    b = pl.BlockSpec((tokens, half), lambda m, p: (0, p[1]))
    out = jax.ShapeDtypeStruct((4, width // 16, half), BF)
    side = jax.ShapeDtypeStruct((2, width // 16, half), BF)
    return pl.pallas_call(
        factor_kernel,
        out_shape=[out, out, side, side, out],
        grid_spec=pltpu.PrefetchScalarGridSpec(
            num_scalar_prefetch=1,
            grid=(4,),
            in_specs=[a_acts, a_acts, a_grads, a_grads, b, b, b, b],
            out_specs=[pl.BlockSpec(memory_space=pl.ANY)] * 5,
            scratch_shapes=[pltpu.VMEM((4, TILE, half), BF), pltpu.SemaphoreType.DMA((4, 4))],
        ),
        compiler_params=pltpu.CompilerParams(vmem_limit_bytes=56 * 2**20),
        cost_estimate=pl.CostEstimate(
            flops=4 * tokens * width * half, bytes_accessed=16 * tokens * half, transcendentals=0
        ),
        name="factor_term",
    )(place, acts, acts_next, grads, grads_next, acts, acts_next, grads, grads_next)


def add(first, *rest):
    total = first.astype(F32)
    for x in rest:
        total = total + x.astype(F32)
    return total


def second_sum(x, me):
    received = [turn(pick(x, 0, (me + step) & 3).astype(BF), step, 1) for step in (1, 2, 3)]
    return add(pick(x, 0, me), *received)


def per_device(hidden, out_grad, left_inverse, right_inverse):
    z, y, xl, c, o = (lax.axis_index(n) for n in ("z", "y", "xl", "c", "o"))
    tokens, width = hidden.shape
    half = width // 2
    token_total = tokens * 64
    first = o == 0
    place = jnp.stack([o, c, z, y]).astype(jnp.int32)
    second_me = jnp.where(c == 0, y, z)

    grads_next = shift(out_grad, "c", 1)
    acts_next = shift(hidden, "c", 1)

    own, m1, m2, m3 = cross_term(place, out_grad, grads_next, hidden, acts_next)
    m = add(own, turn(m1, 1, 0), turn(m2, 2, 0), turn(m3, 3, 0))
    m = second_sum(m, second_me).reshape(2, half // 32, half)
    mine, theirs = pick(m, 0, xl), pick(m, 0, 1 - xl)
    own = mine + shift(theirs, "xl", 1)
    partner = shift(mine, "o", 1) + lax.ppermute(
        theirs, ("xl", "o"), [(i, 3 - i) for i in range(4)]
    )
    swap = (c ^ o) == 0
    mrow = jnp.concatenate(
        [jnp.where(swap, own, partner), jnp.where(swap, partner, own)], axis=1
    )
    rows = mrow.shape[0]
    stacked = jnp.concatenate(split_pair(mrow))
    pt = jnp.dot(stacked, left_inverse, preferred_element_type=F32)
    pt = pt[:rows] + pt[rows:]
    pt_other = shift(pt, "o", 1)
    pt = jnp.concatenate(
        [jnp.where(first, pt, pt_other), jnp.where(first, pt_other, pt)], axis=1
    )
    blocks = pt.reshape(rows, 64, rows).transpose(1, 0, 2)
    blocks = lax.all_to_all(blocks, ("z", "y", "xl", "c"), 0, 0, tiled=True)
    blocks = blocks.reshape(32, 2, rows, rows).transpose(1, 0, 2, 3).reshape(width, rows)
    stacked = jnp.concatenate(split_pair(blocks), axis=1)
    update = contract(stacked, right_inverse)
    update = update[:rows] + update[rows:]

    own, right, far_a, far_b, left = factor_term(place, hidden, acts_next, out_grad, grads_next)
    from_left, from_right = turn(far_a, 1, 0), turn(far_b, -1, 0)
    right = jnp.concatenate([add(right[:2], from_left).astype(BF), right[2:]])
    left = jnp.concatenate([left[:2], add(left[2:], from_right).astype(BF)])
    f = add(own, turn(right, 1, 0), turn(left, -1, 0))
    f = second_sum(f, second_me).reshape(2, width // 32, half)
    f = pick(f, 0, xl) + shift(pick(f, 0, 1 - xl).astype(BF), "xl", 1).astype(F32)
    f = f * jnp.where(first, 1.0 / token_total, 1.0).astype(F32)
    f = f.reshape(2, width // 64, half)
    mine = pick(f, 0, c)
    theirs = shift(pick(f, 0, 1 - c), "c", 1)
    factors = jnp.concatenate(
        [jnp.where(c == 0, mine, theirs), jnp.where(c == 0, theirs, mine)], axis=1
    )[None]
    return factors, update


def solution(mesh):
    fine = Mesh(mesh.devices.reshape(4, 4, 2, 2, 2), ("z", "y", "xl", "c", "o"))
    dp = ("z", "y", "xl", "c")
    in_specs = (P(dp, None), P(dp, None), P(None, "o"), P(None, "o"))
    out_specs = (P("o", dp, None), P(dp, "o"))
    return jax.shard_map(
        per_device, mesh=fine, in_specs=in_specs, out_specs=out_specs, check_vma=False
    )
```

profile of v0, /device:TPU:1, one launch (start us, length us, event | category | flops | bytes accessed | tf_op | source)
XLA Modules:
  0.0 151.2 jit_solution(8186446289177756009)
XLA Ops:
  0.6 1.5 collective-permute-start
  2.3 6.6 %collective-permute-done.ha1.hb1.b1 = bf16[768,2560]{1,0:T(8,128)(2,1)} collective-permute-done((bf16[768,2560]{1,0:T(8,128)(2,1)}, bf16[768,2560]{1,0:T(8,128)(2,1)}, u32[]{:S(2)}, u32[]{:S(2)}) %collective-permute-start) | collective-permute-done | bytes 3932192 | tf_op jit(solution)/shard_map/ppermute | solution.py:23
  8.9 5.6 %collective-permute-done.1.ga1.gb1.a1 = bf16[768,2560]{1,0:T(8,128)(2,1)} collective-permute-done((bf16[768,2560]{1,0:T(8,128)(2,1)}, bf16[768,2560]{1,0:T(8,128)(2,1)}, u32[]{:S(2)}, u32[]{:S(2)}) %collective-permute-start.1) | collective-permute-done | bytes 3932192 | tf_op jit(solution)/shard_map/ppermute | solution.py:23
  14.5 13.6 %cross_term.1 = (bf16[4,80,1280]{2,1,0:T(8,128)(2,1)S(1)}, bf16[4,80,1280]{2,1,0:T(8,128)(2,1)S(1)}, bf16[4,80,1280]{2,1,0:T(8,128)(2,1)S(1)}, bf16[4,80,1280]{2,1,0:T(8,128)(2,1)S(1)}) custom-call(s32[4]{0:T(128)S(1)} %pad_add_fusion.place, bf16[768,2560]{1,0:T(8,128)(2,1)} %a0.1, bf16[768,2560]{1,0:T(8,128)(2,1)} %collective-permute-done.1.ga1.gb1.a1, ...), custom_call_target="tpu_custom_call" | custom-call | flops 5033164800 | bytes 9830400 | tf_op jit(solution)/shard_map/cross_term/pallas_call | solution.py:96
  28.2 1.4 collective-permute-start.11
  29.6 2.6 %collective-permute-start.12 = (bf16[4,80,1280]{2,1,0:T(8,128)(2,1)S(1)}, bf16[4,80,1280]{2,1,0:T(8,128)(2,1)S(1)}, u32[]{:S(2)}, u32[]{:S(2)}) collective-permute-start(bf16[4,80,1280]{2,1,0:T(8,128)(2,1)S(1)} %get-tuple-element.18), channel_id=1, source_target_pairs={{0,64},{2,18},{8,72},{10,26},{16,80},{18,2},{24,88},{26,10},{32,96... | collective-permute-start | bytes 2457608 | tf_op jit(solution)/shard_map/ppermute | solution.py:34
  32.2 1.1 collective-permute-start.13
  33.3 18.1 %factor_term.1 = (bf16[4,160,1280]{2,1,0:T(8,128)(2,1)}, bf16[4,160,1280]{2,1,0:T(8,128)(2,1)}, bf16[2,160,1280]{2,1,0:T(8,128)(2,1)}, bf16[2,160,1280]{2,1,0:T(8,128)(2,1)}, bf16[4,160,1280]{2,1,0:T(8,128)(2,1)}) custom-call(s32[4]{0:T(128)} %copy-done, bf16[768,2560]{1,0:T(8,128)(2,1)} %b0.1, bf16[768,2560]{1,0:T(8,128)(2,1)} %collective-permute-done.ha1.hb1.b1, ...), custom_call_target="tpu_custom_call" | custom-call | flops 10066329600 | bytes 15728640 | tf_op jit(solution)/shard_map/factor_term/pallas_call | solution.py:140
  51.4 0.5 collective-permute-start.2
  51.9 1.2 slice.25
  53.1 2.3 %collective-permute-start.4 = (bf16[2,160,1280]{2,1,0:T(8,128)(2,1)}, bf16[2,160,1280]{2,1,0:T(8,128)(2,1)S(1)}, u32[]{:S(2)}, u32[]{:S(2)}) collective-permute-start(bf16[2,160,1280]{2,1,0:T(8,128)(2,1)} %get-tuple-element.15), channel_id=1, source_target_pairs={{0,96},{2,26},{8,104},{10,2},{16,112},{18,10},{24,120},{26,18},{32... | collective-permute-start | bytes 2457608 | tf_op jit(solution)/shard_map/ppermute | solution.py:34
  56.0 1.7 %collective-permute-start.14 = (bf16[80,1280]{1,0:T(8,128)(2,1)S(1)}, bf16[80,1280]{1,0:T(8,128)(2,1)S(1)}, u32[]{:S(2)}, u32[]{:S(2)}) collective-permute-start(bf16[80,1280]{1,0:T(8,128)(2,1)S(1)} %get-tuple-element.23), channel_id=1, source_target_pairs={{0,8},{2,34},{8,16},{10,42},{16,24},{18,50},{24,0},{26,58},{32,40}... | collective-permute-start | bytes 614408 | tf_op jit(solution)/shard_map/ppermute | solution.py:34
  57.7 3.3 %collective-permute-start.15 = (bf16[80,1280]{1,0:T(8,128)(2,1)S(1)}, bf16[80,1280]{1,0:T(8,128)(2,1)S(1)}, u32[]{:S(2)}, u32[]{:S(2)}) collective-permute-start(bf16[80,1280]{1,0:T(8,128)(2,1)S(1)} %get-tuple-element.25), channel_id=1, source_target_pairs={{0,16},{2,66},{8,24},{10,74},{16,0},{18,82},{24,8},{26,90},{32,48}... | collective-permute-start | bytes 614408 | tf_op jit(solution)/shard_map/ppermute | solution.py:34
  61.0 0.7 collective-permute-start.16
  61.8 3.9 %collective-permute-done.2 = bf16[2,160,1280]{2,1,0:T(8,128)(2,1)S(1)} collective-permute-done((bf16[2,160,1280]{2,1,0:T(8,128)(2,1)}, bf16[2,160,1280]{2,1,0:T(8,128)(2,1)S(1)}, u32[]{:S(2)}, u32[]{:S(2)}) %collective-permute-start.2) | collective-permute-done | bytes 819232 | tf_op jit(solution)/shard_map/ppermute | solution.py:34
  65.9 1.3 pad_maximum_fusion
  67.2 0.9 collective-permute-done.4
  68.4 0.9 collective-permute-done.15
  69.3 1.3 collective-permute-done.16
  70.7 1.3 collective-permute-start.17
  72.0 1.5 %collective-permute-start.19 = (f32[40,1280]{1,0:T(8,128)S(1)}, f32[40,1280]{1,0:T(8,128)S(1)}, u32[]{:S(2)}, u32[]{:S(2)}) collective-permute-start(f32[40,1280]{1,0:T(8,128)S(1)} %get-tuple-element.36), channel_id=1, source_target_pairs={{0,5},{1,4},{4,1},{5,0},{2,7},{3,6},{6,3},{7,2},{8,13},{9,12},{12,... | collective-permute-start | bytes 614408 | tf_op jit(solution)/shard_map/ppermute | solution.py:187
  73.6 0.6 collective-permute-start.18
  74.2 1.3 pad_maximum_fusion.1
  75.5 1.1 collective-permute-start.5
  76.6 4.3 %collective-permute-done.18 = f32[40,1280]{1,0:T(8,128)S(1)} collective-permute-done((f32[40,1280]{1,0:T(8,128)S(1)}, f32[40,1280]{1,0:T(8,128)S(1)}, u32[]{:S(2)}, u32[]{:S(2)}) %collective-permute-start.18) | collective-permute-done | bytes 204832 | tf_op jit(solution)/shard_map/ppermute | solution.py:23
  81.1 1.3 fusion.7
  82.4 0.9 collective-permute-start.20
  83.3 5.3 %collective-permute-done.20 = f32[40,1280]{1,0:T(8,128)S(1)} collective-permute-done((f32[40,1280]{1,0:T(8,128)S(1)}, f32[40,1280]{1,0:T(8,128)S(1)}, u32[]{:S(2)}, u32[]{:S(2)}) %collective-permute-start.20) | collective-permute-done | bytes 204832 | tf_op jit(solution)/shard_map/ppermute | solution.py:23
  88.7 1.0 reshape.32
  89.7 0.8 copy.7
  90.5 1.9 %reshape.35 = f32[64,1,1600]{2,1,0:T(1,128)} reshape(f32[64,40,40]{2,1,0:T(8,128)S(1)} %copy.7) | data formatting | bytes 819200
  92.3 13.6 %all-to-all-start = ((f32[64,1,1600]{2,1,0:T(1,128)}), f32[64,1,1600]{2,1,0:T(1,128)S(1)}, u32[]{:S(2)}, u32[]{:S(2)}) async-start(f32[64,1,1600]{2,1,0:T(1,128)} %reshape.35), calls=%async_computation | async-start | bytes 851968 | tf_op jit(solution)/shard_map/all_to_all | solution.py:203
  106.0 11.7 %all-to-all-done = f32[64,1,1600]{2,1,0:T(1,128)S(1)} async-done(((f32[64,1,1600]{2,1,0:T(1,128)}), f32[64,1,1600]{2,1,0:T(1,128)S(1)}, u32[]{:S(2)}, u32[]{:S(2)}) %all-to-all-start) | async-done | bytes 409632 | tf_op jit(solution)/shard_map/all_to_all | solution.py:203
  117.7 0.5 broadcast
  118.2 1.7 %reduce = f32[64,1600]{1,0:T(8,128)S(1)} reduce(f32[64,1,1600]{2,1,0:T(1,128)S(1)} %all-to-all-done, f32[]{:T(128)} %broadcast), dimensions={1}, to_apply=%all_to_all.3.reduce_sub_computation | reduce | bytes 819204 | tf_op jit(solution)/shard_map/all_to_all | solution.py:203
  119.9 0.5 reshape.36
  120.4 2.0 %copy.8 = f32[32,2,40,40]{2,0,1,3:T(8,128)} copy(f32[32,2,40,40]{3,2,1,0:T(8,128)S(1)} %bitcast.62) | data formatting | bytes 819200 | tf_op jit(solution)/shard_map/reshape | solution.py:204
  122.5 2.2 %reshape.34 = f32[2560,40]{0,1:T(8,128)S(1)} reshape(f32[2,32,40,40]{2,1,0,3:T(8,128)} %bitcast.63) | data formatting | bytes 819200 | tf_op jit(solution)/shard_map/reshape | solution.py:204
  124.7 3.1 %convert_add_fusion = f32[4,160,1280]{2,1,0:T(8,128)S(1)} fusion(bf16[4,160,1280]{2,1,0:T(8,128)(2,1)} %collective-permute-done.5, bf16[4,160,1280]{2,1,0:T(8,128)(2,1)} %collective-permute-done.3, bf16[4,160,1280]{2,1,0:T(8,128)(2,1)} %get-tuple-element.11), kind=kLoop, calls=%fused_computation | loop fusion | flops 4096000 | bytes 8192000 | tf_op jit(solution)/shard_map/add | solution.py:161
  128.2 1.6 %collective-permute-start.7 = (bf16[160,1280]{1,0:T(8,128)(2,1)S(1)}, bf16[160,1280]{1,0:T(8,128)(2,1)S(1)}, u32[]{:S(2)}, u32[]{:S(2)}) collective-permute-start(bf16[160,1280]{1,0:T(8,128)(2,1)S(1)} %get-tuple-element.22), channel_id=1, source_target_pairs={{0,16},{2,66},{8,24},{10,74},{16,0},{18,82},{24,8},{26,90},{32,48}... | collective-permute-start | bytes 1228808 | tf_op jit(solution)/shard_map/ppermute | solution.py:34
  129.7 0.9 collective-permute-start.8
  130.7 10.0 %collective-permute-done.6 = bf16[160,1280]{1,0:T(8,128)(2,1)S(1)} collective-permute-done((bf16[160,1280]{1,0:T(8,128)(2,1)S(1)}, bf16[160,1280]{1,0:T(8,128)(2,1)S(1)}, u32[]{:S(2)}, u32[]{:S(2)}) %collective-permute-start.6) | collective-permute-done | bytes 409632 | tf_op jit(solution)/shard_map/ppermute | solution.py:34
  140.7 0.6 collective-permute-done.8
  141.7 1.3 fusion.11
  142.9 3.7 %collective-permute-done.9 = bf16[80,1280]{1,0:T(8,128)(2,1)S(1)} collective-permute-done((bf16[80,1280]{1,0:T(8,128)(2,1)S(1)}, bf16[80,1280]{1,0:T(8,128)(2,1)S(1)}, u32[]{:S(2)}, u32[]{:S(2)}) %collective-permute-start.9) | collective-permute-done | bytes 204832 | tf_op jit(solution)/shard_map/ppermute | solution.py:23
  146.7 2.6 %collective-permute-start.10 = (f32[40,1280]{1,0:T(8,128)S(1)}, f32[40,1280]{1,0:T(8,128)S(1)}, u32[]{:S(2)}, u32[]{:S(2)}) collective-permute-start(f32[40,1280]{1,0:T(8,128)S(1)} %dynamic-slice_bitcast_fusion.2), channel_id=1, source_target_pairs={{0,2},{2,0},{1,3},{3,1},{4,6},{6,4},{5,7},{7,5},{8,10},{10,8},{9,1... | collective-permute-start | bytes 614408 | tf_op jit(solution)/shard_map/ppermute | solution.py:23
  149.3 0.7 slice_add_fusion
  150.4 0.8 maximum_bitcast_fusion
  (50 shorter events, 2.7 us)
Async XLA Ops:
  0.6 8.3 %collective-permute-start = (bf16[768,2560]{1,0:T(8,128)(2,1)}, bf16[768,2560]{1,0:T(8,128)(2,1)}, u32[]{:S(2)}, u32[]{:S(2)}) collective-permute-start(bf16[768,2560]{1,0:T(8,128)(2,1)} %b0.1), channel_id=1, source_target_pairs={{0,2},{2,0},{1,3},{3,1},{4,6},{6,4},{5,7},{7,5},{8,10},{10,8},{9,1... | collective-permute-start | bytes 11796488 | tf_op jit(solution)/shard_map/ppermute | solution.py:23
  2.1 12.4 %collective-permute-start.1 = (bf16[768,2560]{1,0:T(8,128)(2,1)}, bf16[768,2560]{1,0:T(8,128)(2,1)}, u32[]{:S(2)}, u32[]{:S(2)}) collective-permute-start(bf16[768,2560]{1,0:T(8,128)(2,1)} %a0.1), channel_id=1, source_target_pairs={{0,2},{2,0},{1,3},{3,1},{4,6},{6,4},{5,7},{7,5},{8,10},{10,8},{9,1... | collective-permute-start | bytes 11796488 | tf_op jit(solution)/shard_map/ppermute | solution.py:23
  2.3 25.8 %copy-start = (s32[4]{0:T(128)}, s32[4]{0:T(128)S(1)}, u32[]{:S(2)}) copy-start(s32[4]{0:T(128)S(1)} %pad_add_fusion.place) | copy-start | bytes 52
  28.2 27.4 %collective-permute-start.11 = (bf16[4,80,1280]{2,1,0:T(8,128)(2,1)S(1)}, bf16[4,80,1280]{2,1,0:T(8,128)(2,1)S(1)}, u32[]{:S(2)}, u32[]{:S(2)}) collective-permute-start(bf16[4,80,1280]{2,1,0:T(8,128)(2,1)S(1)} %get-tuple-element.17), channel_id=1, source_target_pairs={{0,32},{2,10},{8,40},{10,18},{16,48},{18,26},{24,56},{26,2},{32,64... | collective-permute-start | bytes 2457608 | tf_op jit(solution)/shard_map/ppermute | solution.py:34
  29.6 25.9 %collective-permute-start.12 = (bf16[4,80,1280]{2,1,0:T(8,128)(2,1)S(1)}, bf16[4,80,1280]{2,1,0:T(8,128)(2,1)S(1)}, u32[]{:S(2)}, u32[]{:S(2)}) collective-permute-start(bf16[4,80,1280]{2,1,0:T(8,128)(2,1)S(1)} %get-tuple-element.18), channel_id=1, source_target_pairs={{0,64},{2,18},{8,72},{10,26},{16,80},{18,2},{24,88},{26,10},{32,96... | collective-permute-start | bytes 2457608 | tf_op jit(solution)/shard_map/ppermute | solution.py:34
  32.2 23.3 %collective-permute-start.13 = (bf16[4,80,1280]{2,1,0:T(8,128)(2,1)S(1)}, bf16[4,80,1280]{2,1,0:T(8,128)(2,1)S(1)}, u32[]{:S(2)}, u32[]{:S(2)}) collective-permute-start(bf16[4,80,1280]{2,1,0:T(8,128)(2,1)S(1)} %get-tuple-element.19), channel_id=1, source_target_pairs={{0,96},{2,26},{8,104},{10,2},{16,112},{18,10},{24,120},{26,18},{32... | collective-permute-start | bytes 2457608 | tf_op jit(solution)/shard_map/ppermute | solution.py:34
  51.4 4.0 %copy-start.1 = (bf16[4,160,1280]{2,1,0:T(8,128)(2,1)S(1)}, bf16[4,160,1280]{2,1,0:T(8,128)(2,1)}, u32[]{:S(2)}) copy-start(bf16[4,160,1280]{2,1,0:T(8,128)(2,1)} %get-tuple-element.14) | copy-start | bytes 4915204
  51.4 14.2 %collective-permute-start.2 = (bf16[2,160,1280]{2,1,0:T(8,128)(2,1)}, bf16[2,160,1280]{2,1,0:T(8,128)(2,1)S(1)}, u32[]{:S(2)}, u32[]{:S(2)}) collective-permute-start(bf16[2,160,1280]{2,1,0:T(8,128)(2,1)} %get-tuple-element.13), channel_id=1, source_target_pairs={{0,32},{2,10},{8,40},{10,18},{16,48},{18,26},{24,56},{26,2},{32,64... | collective-permute-start | bytes 2457608 | tf_op jit(solution)/shard_map/ppermute | solution.py:34
  53.1 15.0 %collective-permute-start.4 = (bf16[2,160,1280]{2,1,0:T(8,128)(2,1)}, bf16[2,160,1280]{2,1,0:T(8,128)(2,1)S(1)}, u32[]{:S(2)}, u32[]{:S(2)}) collective-permute-start(bf16[2,160,1280]{2,1,0:T(8,128)(2,1)} %get-tuple-element.15), channel_id=1, source_target_pairs={{0,96},{2,26},{8,104},{10,2},{16,112},{18,10},{24,120},{26,18},{32... | collective-permute-start | bytes 2457608 | tf_op jit(solution)/shard_map/ppermute | solution.py:34
  55.5 10.1 %copy-start.2 = (bf16[4,160,1280]{2,1,0:T(8,128)(2,1)S(1)}, bf16[4,160,1280]{2,1,0:T(8,128)(2,1)}, u32[]{:S(2)}) copy-start(bf16[4,160,1280]{2,1,0:T(8,128)(2,1)} %get-tuple-element.12) | copy-start | bytes 4915204
  56.0 12.3 %collective-permute-start.14 = (bf16[80,1280]{1,0:T(8,128)(2,1)S(1)}, bf16[80,1280]{1,0:T(8,128)(2,1)S(1)}, u32[]{:S(2)}, u32[]{:S(2)}) collective-permute-start(bf16[80,1280]{1,0:T(8,128)(2,1)S(1)} %get-tuple-element.23), channel_id=1, source_target_pairs={{0,8},{2,34},{8,16},{10,42},{16,24},{18,50},{24,0},{26,58},{32,40}... | collective-permute-start | bytes 614408 | tf_op jit(solution)/shard_map/ppermute | solution.py:34
  57.7 11.6 %collective-permute-start.15 = (bf16[80,1280]{1,0:T(8,128)(2,1)S(1)}, bf16[80,1280]{1,0:T(8,128)(2,1)S(1)}, u32[]{:S(2)}, u32[]{:S(2)}) collective-permute-start(bf16[80,1280]{1,0:T(8,128)(2,1)S(1)} %get-tuple-element.25), channel_id=1, source_target_pairs={{0,16},{2,66},{8,24},{10,74},{16,0},{18,82},{24,8},{26,90},{32,48}... | collective-permute-start | bytes 614408 | tf_op jit(solution)/shard_map/ppermute | solution.py:34
  61.0 9.6 %collective-permute-start.16 = (bf16[80,1280]{1,0:T(8,128)(2,1)S(1)}, bf16[80,1280]{1,0:T(8,128)(2,1)S(1)}, u32[]{:S(2)}, u32[]{:S(2)}) collective-permute-start(bf16[80,1280]{1,0:T(8,128)(2,1)S(1)} %get-tuple-element.24), channel_id=1, source_target_pairs={{0,24},{2,98},{8,0},{10,106},{16,8},{18,114},{24,16},{26,122},{32,... | collective-permute-start | bytes 614408 | tf_op jit(solution)/shard_map/ppermute | solution.py:34
  65.9 15.2 %slice-start = ((s8[6553600]{0:T(1024)(128)(4,1)}), s8[4194304]{0:T(1024)(128)(4,1)S(1)}, s32[]{:S(2)}) async-start(s8[6553600]{0:T(1024)(128)(4,1)} %bitcast.57), calls=%async_computation.1 | async-start | bytes 8388608
  67.2 57.4 %collective-permute-start.3 = (bf16[4,160,1280]{2,1,0:T(8,128)(2,1)}, bf16[4,160,1280]{2,1,0:T(8,128)(2,1)}, u32[]{:S(2)}, u32[]{:S(2)}) collective-permute-start(bf16[4,160,1280]{2,1,0:T(8,128)(2,1)} %pad_maximum_fusion), channel_id=1, source_target_pairs={{0,32},{2,10},{8,40},{10,18},{16,48},{18,26},{24,56},{26,2},{32,64... | collective-permute-start | bytes 4915208 | tf_op jit(solution)/shard_map/ppermute | solution.py:34
  68.3 12.7 %slice-start.1 = ((s8[6553600]{0:T(1024)(128)(4,1)}), s8[2359296]{0:T(1024)(128)(4,1)S(1)}, s32[]{:S(2)}) async-start(s8[6553600]{0:T(1024)(128)(4,1)} %bitcast.57), calls=%async_computation.2 | async-start | bytes 4718592
  70.7 5.9 %collective-permute-start.17 = (f32[40,1280]{1,0:T(8,128)S(1)}, f32[40,1280]{1,0:T(8,128)S(1)}, u32[]{:S(2)}, u32[]{:S(2)}) collective-permute-start(f32[40,1280]{1,0:T(8,128)S(1)} %get-tuple-element.36), channel_id=1, source_target_pairs={{0,4},{4,0},{1,5},{5,1},{2,6},{6,2},{3,7},{7,3},{8,12},{12,8},{9,1... | collective-permute-start | bytes 614408 | tf_op jit(solution)/shard_map/ppermute | solution.py:23
  72.0 8.9 %collective-permute-start.19 = (f32[40,1280]{1,0:T(8,128)S(1)}, f32[40,1280]{1,0:T(8,128)S(1)}, u32[]{:S(2)}, u32[]{:S(2)}) collective-permute-start(f32[40,1280]{1,0:T(8,128)S(1)} %get-tuple-element.36), channel_id=1, source_target_pairs={{0,5},{1,4},{4,1},{5,0},{2,7},{3,6},{6,3},{7,2},{8,13},{9,12},{12,... | collective-permute-start | bytes 614408 | tf_op jit(solution)/shard_map/ppermute | solution.py:187
  73.6 7.4 %collective-permute-start.18 = (f32[40,1280]{1,0:T(8,128)S(1)}, f32[40,1280]{1,0:T(8,128)S(1)}, u32[]{:S(2)}, u32[]{:S(2)}) collective-permute-start(f32[40,1280]{1,0:T(8,128)S(1)} %get-tuple-element.37), channel_id=1, source_target_pairs={{0,1},{1,0},{2,3},{3,2},{4,5},{5,4},{6,7},{7,6},{8,9},{9,8},{10,11... | collective-permute-start | bytes 614408 | tf_op jit(solution)/shard_map/ppermute | solution.py:23
  75.5 49.1 %collective-permute-start.5 = (bf16[4,160,1280]{2,1,0:T(8,128)(2,1)}, bf16[4,160,1280]{2,1,0:T(8,128)(2,1)}, u32[]{:S(2)}, u32[]{:S(2)}) collective-permute-start(bf16[4,160,1280]{2,1,0:T(8,128)(2,1)} %pad_maximum_fusion.1), channel_id=1, source_target_pairs={{0,96},{2,26},{8,104},{10,2},{16,112},{18,10},{24,120},{26,18},{32... | collective-permute-start | bytes 4915208 | tf_op jit(solution)/shard_map/ppermute | solution.py:34
  82.4 6.2 %collective-permute-start.20 = (f32[40,1280]{1,0:T(8,128)S(1)}, f32[40,1280]{1,0:T(8,128)S(1)}, u32[]{:S(2)}, u32[]{:S(2)}) collective-permute-start(f32[40,1280]{1,0:T(8,128)S(1)} %slice_add_fusion.1), channel_id=1, source_target_pairs={{0,1},{1,0},{2,3},{3,2},{4,5},{5,4},{6,7},{7,6},{8,9},{9,8},{10,11... | collective-permute-start | bytes 614408 | tf_op jit(solution)/shard_map/ppermute | solution.py:23
  92.3 25.4 %all-to-all-start = ((f32[64,1,1600]{2,1,0:T(1,128)}), f32[64,1,1600]{2,1,0:T(1,128)S(1)}, u32[]{:S(2)}, u32[]{:S(2)}) async-start(f32[64,1,1600]{2,1,0:T(1,128)} %reshape.35), calls=%async_computation | async-start | bytes 851968 | tf_op jit(solution)/shard_map/all_to_all | solution.py:203
  122.5 19.2 %slice-start.2 = ((s8[6553600]{0:T(1024)(128)(4,1)}), s8[2359296]{0:T(1024)(128)(4,1)S(1)}, s32[]{:S(2)}) async-start(s8[6553600]{0:T(1024)(128)(4,1)} %bitcast.59), calls=%async_computation.3 | async-start | bytes 4718592
  124.7 17.0 %slice-start.3 = ((s8[6553600]{0:T(1024)(128)(4,1)}), s8[4194304]{0:T(1024)(128)(4,1)S(1)}, s32[]{:S(2)}) async-start(s8[6553600]{0:T(1024)(128)(4,1)} %bitcast.59), calls=%async_computation.4 | async-start | bytes 8388608
  127.9 12.8 %collective-permute-start.6 = (bf16[160,1280]{1,0:T(8,128)(2,1)S(1)}, bf16[160,1280]{1,0:T(8,128)(2,1)S(1)}, u32[]{:S(2)}, u32[]{:S(2)}) collective-permute-start(bf16[160,1280]{1,0:T(8,128)(2,1)S(1)} %get-tuple-element.20), channel_id=1, source_target_pairs={{0,8},{2,34},{8,16},{10,42},{16,24},{18,50},{24,0},{26,58},{32,40}... | collective-permute-start | bytes 1228808 | tf_op jit(solution)/shard_map/ppermute | solution.py:34
  128.2 12.5 %collective-permute-start.7 = (bf16[160,1280]{1,0:T(8,128)(2,1)S(1)}, bf16[160,1280]{1,0:T(8,128)(2,1)S(1)}, u32[]{:S(2)}, u32[]{:S(2)}) collective-permute-start(bf16[160,1280]{1,0:T(8,128)(2,1)S(1)} %get-tuple-element.22), channel_id=1, source_target_pairs={{0,16},{2,66},{8,24},{10,74},{16,0},{18,82},{24,8},{26,90},{32,48}... | collective-permute-start | bytes 1228808 | tf_op jit(solution)/shard_map/ppermute | solution.py:34
  129.7 11.6 %collective-permute-start.8 = (bf16[160,1280]{1,0:T(8,128)(2,1)S(1)}, bf16[160,1280]{1,0:T(8,128)(2,1)S(1)}, u32[]{:S(2)}, u32[]{:S(2)}) collective-permute-start(bf16[160,1280]{1,0:T(8,128)(2,1)S(1)} %get-tuple-element.21), channel_id=1, source_target_pairs={{0,24},{2,98},{8,0},{10,106},{16,8},{18,114},{24,16},{26,122},{32,... | collective-permute-start | bytes 1228808 | tf_op jit(solution)/shard_map/ppermute | solution.py:34
  141.5 5.0 %collective-permute-start.9 = (bf16[80,1280]{1,0:T(8,128)(2,1)S(1)}, bf16[80,1280]{1,0:T(8,128)(2,1)S(1)}, u32[]{:S(2)}, u32[]{:S(2)}) collective-permute-start(bf16[80,1280]{1,0:T(8,128)(2,1)S(1)} %fusion.18), channel_id=1, source_target_pairs={{0,4},{4,0},{1,5},{5,1},{2,6},{6,2},{3,7},{7,3},{8,12},{12,8},{9,1... | collective-permute-start | bytes 614408 | tf_op jit(solution)/shard_map/ppermute | solution.py:23
  146.7 3.7 %collective-permute-start.10 = (f32[40,1280]{1,0:T(8,128)S(1)}, f32[40,1280]{1,0:T(8,128)S(1)}, u32[]{:S(2)}, u32[]{:S(2)}) collective-permute-start(f32[40,1280]{1,0:T(8,128)S(1)} %dynamic-slice_bitcast_fusion.2), channel_id=1, source_target_pairs={{0,2},{2,0},{1,3},{3,1},{4,6},{6,4},{5,7},{7,5},{8,10},{10,8},{9,1... | collective-permute-start | bytes 614408 | tf_op jit(solution)/shard_map/ppermute | solution.py:23
where the time goes:
time: 151 us
  waiting for transfers between devices  55.2 us (37%)
  starting transfers between devices  39.8 us (26%)
  Pallas kernels  31.8 us (21%)
  local copies, waits for them, and re-layouts  10.6 us (7%)
  other arithmetic  10.3 us (7%)
  matrix products  2.51 us (2%)
    ppermute x7, waiting for transfers between devices, shift(): return lax.ppermute(x, axis, [(i, (i + step) % size) for i in range(size)])  25.8 us
    pallas_call x1, Pallas kernels, factor_term(): pl.pallas_call(factor_kernel, out_shape=[out, out, side, side, out], grid...  18.1 us
    ppermute x13, waiting for transfers between devices, turn(): return lax.ppermute(x, ('z', 'y', 'c'), pairs)  17.7 us
    ppermute x13, starting transfers between devices, turn(): return lax.ppermute(x, ('z', 'y', 'c'), pairs)  17.5 us
    all_to_all x1, starting transfers between devices, per_device(): blocks = lax.all_to_all(blocks, ('z', 'y', 'xl', 'c'), 0, 0, tiled=True)  13.6 us
    pallas_call x1, Pallas kernels, cross_term(): pl.pallas_call(cross_kernel, out_shape=[out] * 4, grid_spec=pltpu.Prefetc...  13.6 us
    all_to_all x1, waiting for transfers between devices, per_device(): blocks = lax.all_to_all(blocks, ('z', 'y', 'xl', 'c'), 0, 0, tiled=True)  11.7 us
    ppermute x7, starting transfers between devices, shift(): return lax.ppermute(x, axis, [(i, (i + step) % size) for i in range(size)])  7.14 us
  transfers between devices with their start and end apart: 22, of which 13 were waited for; matrix products, arithmetic and copies ran while one was open for 13% of the time, Pallas kernels for 12%

commit v1 on v0

v1 whole, which is shorter than its diff:
```python
import functools

import jax
import jax.numpy as jnp
from jax import lax
from jax.experimental import pallas as pl
from jax.experimental.pallas import tpu as pltpu
from jax.sharding import Mesh, PartitionSpec as P

BF = jnp.bfloat16
F32 = jnp.float32
TILE = 640


def contract(first_rows, second_rows):
    return lax.dot_general(
        first_rows, second_rows, (((0,), (0,)), ((), ())), preferred_element_type=F32
    )


def shift(x, axis, step):
    size = lax.axis_size(axis)
    return lax.ppermute(x, axis, [(i, (i + step) % size) for i in range(size)])


def turn(x, step, stage):
    pairs = []
    for z in range(4):
        for y in range(4):
            for c in range(2):
                along_z = (c == 0) == (stage == 0)
                there = ((z + step) % 4, y) if along_z else (z, (y + step) % 4)
                pairs.append(((z * 4 + y) * 2 + c, (there[0] * 4 + there[1]) * 2 + c))
    return lax.ppermute(x, ("z", "y", "c"), pairs)


def pick(x, dim, index):
    return lax.dynamic_index_in_dim(x, index, dim, keepdims=False)


def split_pair(x):
    high = lax.reduce_precision(x, 8, 7)
    return high.astype(BF), (x - high).astype(BF)


def place_blocks(place, buffer, sems, outs, m, n, zs, finish):
    core, z_me, y_me = place[1], place[2], place[3]
    rows = TILE // (zs * 4)
    lanes = pl.ds(pl.multiple_of(n * TILE, TILE), TILE)
    for a in range(zs):
        for k in range(4):
            z = m * zs + a
            ahead = jnp.where(core == 0, z - z_me + 4, k - y_me + 4) & 3
            slot = jnp.where(core == 0, k, z)
            part = a * 4 + k
            block = buffer.at[m, pl.ds(part * rows, rows), lanes]

            def move(out):
                copy = pltpu.make_async_copy(block, out.at[slot, :, lanes], sems.at[m, n, part])
                if finish:
                    copy.wait()
                else:
                    copy.start()

            for r, out in enumerate(outs):
                pl.when(ahead == r)(functools.partial(move, out))


def store_tile(place, buffer, sems, outs, tile, steps, zs):
    m, n = pl.program_id(0), pl.program_id(1)
    for lane in range(2):

        @pl.when(n == lane)
        def _():
            buffer[m, :, lane * TILE : (lane + 1) * TILE] = tile()

    place_blocks(place, buffer, sems, outs, m, n, zs, False)

    @pl.when((m == steps - 1) & (n == 1))
    def _():
        for i in range(steps):
            for j in range(2):
                place_blocks(place, buffer, sems, outs, i, j, zs, True)


def cross_kernel(place, a0, a1, b0, b1, own, ahead1, ahead2, ahead3, buffer, sems):
    def tile():
        return (contract(a0[...], b0[...]) + contract(a1[...], b1[...])).astype(BF)

    store_tile(place, buffer, sems, [own, ahead1, ahead2, ahead3], tile, 2, 2)


def cross_term(place, grads, grads_next, acts, acts_next):
    tokens, width = grads.shape
    half = width // 2
    left = pl.BlockSpec((tokens, TILE), lambda m, n, p: (0, p[1] * 2 + m))
    right = pl.BlockSpec((tokens, TILE), lambda m, n, p: (0, (p[1] ^ p[0]) * 2 + n))
    out = jax.ShapeDtypeStruct((4, half // 16, half), BF)
    return pl.pallas_call(
        cross_kernel,
        out_shape=[out] * 4,
        grid_spec=pltpu.PrefetchScalarGridSpec(
            num_scalar_prefetch=1,
            grid=(2, 2),
            in_specs=[left, left, right, right],
            out_specs=[pl.BlockSpec(memory_space=pl.ANY)] * 4,
            scratch_shapes=[pltpu.VMEM((2, TILE, half), BF), pltpu.SemaphoreType.DMA((2, 2, 8))],
        ),
        compiler_params=pltpu.CompilerParams(vmem_limit_bytes=48 * 2**20),
        cost_estimate=pl.CostEstimate(
            flops=4 * tokens * half * half, bytes_accessed=10 * tokens * half, transcendentals=0
        ),
        name="cross_term",
    )(place, grads, grads_next, acts, acts_next)


def factor_kernel(
    place, ha0, ha1, ga0, ga1, hb0, hb1, gb0, gb1, own, ahead1, ahead2, ahead3, buffer, sems
):
    def tile():
        def term(a0, a1, b0, b1):
            return (contract(a0[...], b0[...]) + contract(a1[...], b1[...])).astype(BF)

        return lax.cond(
            place[0] == 0,
            lambda: term(ha0, ha1, hb0, hb1),
            lambda: term(ga0, ga1, gb0, gb1),
        )

    store_tile(place, buffer, sems, [own, ahead1, ahead2, ahead3], tile, 4, 1)


def factor_term(place, acts, acts_next, grads, grads_next):
    tokens, width = acts.shape
    half = width // 2
    a_acts = pl.BlockSpec((tokens, TILE), lambda m, n, p: (0, m * (1 - p[0])))
    a_grads = pl.BlockSpec((tokens, TILE), lambda m, n, p: (0, m * p[0]))
    b_acts = pl.BlockSpec((tokens, TILE), lambda m, n, p: (0, (p[1] * 2 + n) * (1 - p[0])))
    b_grads = pl.BlockSpec((tokens, TILE), lambda m, n, p: (0, (p[1] * 2 + n) * p[0]))
    out = jax.ShapeDtypeStruct((4, width // 16, half), BF)
    return pl.pallas_call(
        factor_kernel,
        out_shape=[out] * 4,
        grid_spec=pltpu.PrefetchScalarGridSpec(
            num_scalar_prefetch=1,
            grid=(4, 2),
            in_specs=[a_acts, a_acts, a_grads, a_grads, b_acts, b_acts, b_grads, b_grads],
            out_specs=[pl.BlockSpec(memory_space=pl.ANY)] * 4,
            scratch_shapes=[pltpu.VMEM((4, TILE, half), BF), pltpu.SemaphoreType.DMA((4, 2, 4))],
        ),
        compiler_params=pltpu.CompilerParams(vmem_limit_bytes=56 * 2**20),
        cost_estimate=pl.CostEstimate(
            flops=4 * tokens * width * half, bytes_accessed=16 * tokens * half, transcendentals=0
        ),
        name="factor_term",
    )(place, acts, acts_next, grads, grads_next, acts, acts_next, grads, grads_next)


def add(first, *rest):
    total = first.astype(F32)
    for x in rest:
        total = total + x.astype(F32)
    return total


def send_second(x, me):
    pieces = [pick(x, 0, (me + step) & 3).astype(BF) for step in (1, 2, 3)]
    return pieces, [turn(piece, step, 1) for step, piece in zip((1, 2, 3), pieces)]


def per_device(hidden, out_grad, left_inverse, right_inverse):
    z, y, xl, c, o = (lax.axis_index(n) for n in ("z", "y", "xl", "c", "o"))
    tokens, width = hidden.shape
    half = width // 2
    token_total = tokens * 64
    first = o == 0
    place = jnp.stack([o, c, z, y]).astype(jnp.int32)
    second_me = jnp.where(c == 0, y, z)

    grads_next = shift(out_grad, "c", 1)
    acts_next = shift(hidden, "c", 1)

    own, m1, m2, m3 = cross_term(place, out_grad, grads_next, hidden, acts_next)
    m_parts = [own, turn(m1, 1, 0), turn(m2, 2, 0), turn(m3, 3, 0)]

    piece = lax.dynamic_slice_in_dim(left_inverse, o * half + c * TILE, TILE, 0)
    piece = shift(piece, "o", 1)
    piece_next = shift(piece, "c", 1)

    own, f1, f2, f3 = factor_term(place, hidden, acts_next, out_grad, grads_next)

    m = add(*m_parts)
    _, received = send_second(m, second_me)
    f_parts = [own, turn(f1, 1, 0), turn(f2, 2, 0), turn(f3, 3, 0)]
    m = add(pick(m, 0, second_me), *received).reshape(2, half // 32, half)
    mine, theirs = pick(m, 0, xl), pick(m, 0, 1 - xl)
    m_own = mine + shift(theirs, "xl", 1)
    partner = shift(mine, "o", 1) + lax.ppermute(
        theirs, ("xl", "o"), [(i, 3 - i) for i in range(4)]
    )
    swap = (c ^ o) == 0
    mrow = jnp.concatenate(
        [jnp.where(swap, m_own, partner), jnp.where(swap, partner, m_own)], axis=1
    )
    rows = mrow.shape[0]
    stacked = jnp.concatenate(split_pair(mrow))
    pt = jnp.dot(stacked, left_inverse, preferred_element_type=F32)
    beside = lax.dynamic_slice_in_dim(left_inverse, (1 - o) * half, half, 0)
    at_own = lax.dynamic_slice_in_dim(stacked, o * half, half, 1)
    at_piece = lax.dynamic_slice_in_dim(stacked, (1 - o) * half + c * TILE, TILE, 1)
    at_next = lax.dynamic_slice_in_dim(stacked, (1 - o) * half + (1 - c) * TILE, TILE, 1)
    pt_other = (
        lax.dot_general(at_own, beside, (((1,), (1,)), ((), ())), preferred_element_type=F32)
        + jnp.dot(at_piece, piece, preferred_element_type=F32)
        + jnp.dot(at_next, piece_next, preferred_element_type=F32)
    )
    pt = pt[:rows] + pt[rows:]
    pt_other = pt_other[:rows] + pt_other[rows:]
    pt = jnp.concatenate(
        [jnp.where(first, pt, pt_other), jnp.where(first, pt_other, pt)], axis=1
    )
    blocks = pt.reshape(rows, 32, 2, rows).transpose(2, 1, 0, 3).reshape(64, rows, rows)
    blocks = lax.all_to_all(blocks, ("c", "z", "y", "xl"), 0, 0, tiled=True)

    f = add(*f_parts)
    pieces, received = send_second(f, second_me)
    blocks = lax.optimization_barrier((blocks, pieces))[0].reshape(width, rows)
    stacked = jnp.concatenate(split_pair(blocks), axis=1)
    update = contract(stacked, right_inverse)
    update = update[:rows] + update[rows:]

    f = add(pick(f, 0, second_me), *received).reshape(2, width // 32, half)
    f = pick(f, 0, xl) + shift(pick(f, 0, 1 - xl).astype(BF), "xl", 1).astype(F32)
    f = f * jnp.where(first, 1.0 / token_total, 1.0).astype(F32)
    f = f.reshape(2, width // 64, half)
    mine = pick(f, 0, c)
    theirs = shift(pick(f, 0, 1 - c), "c", 1)
    factors = jnp.concatenate(
        [jnp.where(c == 0, mine, theirs), jnp.where(c == 0, theirs, mine)], axis=1
    )[None]
    return factors, update


def solution(mesh):
    fine = Mesh(mesh.devices.reshape(4, 4, 2, 2, 2), ("z", "y", "xl", "c", "o"))
    dp = ("z", "y", "xl", "c")
    in_specs = (P(dp, None), P(dp, None), P(None, "o"), P(None, "o"))
    out_specs = (P("o", dp, None), P(dp, "o"))
    return jax.shard_map(
        per_device, mesh=fine, in_specs=in_specs, out_specs=out_specs, check_vma=False
    )
```

time: 151 us -> 181 us (1.20)
  waiting for transfers between devices: 55.2 us -> 75 us
  matrix products: 2.51 us -> 5.75 us
  Pallas kernels: 31.8 us -> 34.9 us
    all_to_all x1, waiting for transfers between devices: 11.7 us -> 24.1 us  [per_device(): blocks = lax.all_to_all(blocks, ('c', 'z', 'y', 'xl'), 0, 0, tiled=True)]
    all_to_all x1, starting transfers between devices: 13.6 us -> 7.42 us  [per_device(): blocks = lax.all_to_all(blocks, ('c', 'z', 'y', 'xl'), 0, 0, tiled=True)]
    pallas_call x1, Pallas kernels: 18.1 us -> 23.4 us  [factor_term(): pl.pallas_call(factor_kernel, out_shape=[out] * 4, grid_spec=pltpu.Prefet...]
    ppermute x7 -> x8, starting transfers between devices: 7.14 us -> 12.2 us  [shift(): return lax.ppermute(x, axis, [(i, (i + step) % size) for i in range(size)])]
    ppermute x13 -> x12, waiting for transfers between devices: 17.7 us -> 21.4 us  [turn(): return lax.ppermute(x, ('z', 'y', 'c'), pairs)]
    ppermute x7 -> x8, waiting for transfers between devices: 25.8 us -> 29.5 us  [shift(): return lax.ppermute(x, axis, [(i, (i + step) % size) for i in range(size)])]
    add x4, other arithmetic: 3.75 us -> 7.2 us  [add(): total = total + x.astype(F32)]
    dot_general x0 -> x3, matrix products: none -> 3.33 us  [the longest x1 1.82 us: per_device(): jnp.dot(at_piece, piece, preferred_element_type=F32)]
  transfers between devices with their start and end apart: 22 -> 22, of which waited for: 13 -> 10; matrix products, arithmetic and copies ran while one was open for 13% -> 14% of each run, Pallas kernels for 12% -> 13%
where the time goes in v1:
time: 181 us; the launch traced here: 180 us
  waiting for transfers between devices  75 us (41%)
  starting transfers between devices  39.9 us (22%)
  Pallas kernels  34.9 us (19%)
  other arithmetic  12.1 us (7%)
  local copies, waits for them, and re-layouts  11.7 us (6%)
  matrix products  5.75 us (3%)
    ppermute x8, waiting for transfers between devices, shift(): return lax.ppermute(x, axis, [(i, (i + step) % size) for i in range(size)])  29.5 us
    all_to_all x1, waiting for transfers between devices, per_device(): blocks = lax.all_to_all(blocks, ('c', 'z', 'y', 'xl'), 0, 0, tiled=True)  24.1 us
    pallas_call x1, Pallas kernels, factor_term(): pl.pallas_call(factor_kernel, out_shape=[out] * 4, grid_spec=pltpu.Prefet...  23.4 us
    ppermute x12, waiting for transfers between devices, turn(): return lax.ppermute(x, ('z', 'y', 'c'), pairs)  21.4 us
    ppermute x12, starting transfers between devices, turn(): return lax.ppermute(x, ('z', 'y', 'c'), pairs)  18.4 us
    ppermute x8, starting transfers between devices, shift(): return lax.ppermute(x, axis, [(i, (i + step) % size) for i in range(size)])  12.2 us
    pallas_call x1, Pallas kernels, cross_term(): pl.pallas_call(cross_kernel, out_shape=[out] * 4, grid_spec=pltpu.Prefetc...  11.5 us
    all_to_all x1, starting transfers between devices, per_device(): blocks = lax.all_to_all(blocks, ('c', 'z', 'y', 'xl'), 0, 0, tiled=True)  7.42 us
  transfers between devices with their start and end apart: 22, of which 10 were waited for; matrix products, arithmetic and copies ran while one was open for 14% of the time, Pallas kernels for 13%

profile of v1, /device:TPU:1, one launch (start us, length us, event | category | flops | bytes accessed | tf_op | source)
XLA Modules:
  0.0 180.2 jit_solution(11305205213727767451)
XLA Ops:
  0.6 1.5 collective-permute-start
  2.3 6.6 %collective-permute-done.ha1.hb1.b1 = bf16[768,2560]{1,0:T(8,128)(2,1)} collective-permute-done((bf16[768,2560]{1,0:T(8,128)(2,1)}, bf16[768,2560]{1,0:T(8,128)(2,1)}, u32[]{:S(2)}, u32[]{:S(2)}) %collective-permute-start) | collective-permute-done | bytes 3932192 | tf_op jit(solution)/shard_map/ppermute | solution.py:23
  8.9 5.6 %collective-permute-done.1.ga1.gb1.a1 = bf16[768,2560]{1,0:T(8,128)(2,1)} collective-permute-done((bf16[768,2560]{1,0:T(8,128)(2,1)}, bf16[768,2560]{1,0:T(8,128)(2,1)}, u32[]{:S(2)}, u32[]{:S(2)}) %collective-permute-start.1) | collective-permute-done | bytes 3932192 | tf_op jit(solution)/shard_map/ppermute | solution.py:23
  14.5 11.5 %cross_term.1 = (bf16[4,80,1280]{2,1,0:T(8,128)(2,1)S(1)}, bf16[4,80,1280]{2,1,0:T(8,128)(2,1)S(1)}, bf16[4,80,1280]{2,1,0:T(8,128)(2,1)S(1)}, bf16[4,80,1280]{2,1,0:T(8,128)(2,1)S(1)}) custom-call(s32[4]{0:T(128)S(1)} %pad_add_fusion.place, bf16[768,2560]{1,0:T(8,128)(2,1)} %a0.1, bf16[768,2560]{1,0:T(8,128)(2,1)} %collective-permute-done.1.ga1.gb1.a1, ...), custom_call_target="tpu_custom_call" | custom-call | flops 5033164800 | bytes 9830400 | tf_op jit(solution)/shard_map/cross_term/pallas_call | solution.py:99
  26.0 1.4 collective-permute-start.10
  27.5 2.6 %collective-permute-start.11 = (bf16[4,80,1280]{2,1,0:T(8,128)(2,1)S(1)}, bf16[4,80,1280]{2,1,0:T(8,128)(2,1)}, u32[]{:S(2)}, u32[]{:S(2)}) collective-permute-start(bf16[4,80,1280]{2,1,0:T(8,128)(2,1)S(1)} %get-tuple-element.17), channel_id=1, source_target_pairs={{0,64},{2,18},{8,72},{10,26},{16,80},{18,2},{24,88},{26,10},{32,96... | collective-permute-start | bytes 2457608 | tf_op jit(solution)/shard_map/ppermute | solution.py:34
  30.1 1.1 collective-permute-start.12
  31.2 2.7 %constant_dynamic-slice_fusion = bf16[640,1280]{1,0:T(8,128)(2,1)} fusion(bf16[2560,1280]{1,0:T(8,128)(2,1)} %param.6, s32[]{:T(128)S(6)} %select_n.109), kind=kLoop, calls=%fused_computation.65 | loop fusion | bytes 3276804 | tf_op jit(solution)/shard_map/dynamic_slice | solution.py:186
  33.9 2.8 %collective-permute-start.19 = (bf16[640,1280]{1,0:T(8,128)(2,1)}, bf16[640,1280]{1,0:T(8,128)(2,1)}, u32[]{:S(2)}, u32[]{:S(2)}) collective-permute-start(bf16[640,1280]{1,0:T(8,128)(2,1)} %constant_dynamic-slice_fusion), channel_id=1, source_target_pairs={{0,1},{1,0},{2,3},{3,2},{4,5},{5,4},{6,7},{7,6},{8,9},{9,8},{10,11... | collective-permute-start | bytes 4915208 | tf_op jit(solution)/shard_map/ppermute | solution.py:23
  36.7 2.4 %collective-permute-done.10 = bf16[4,80,1280]{2,1,0:T(8,128)(2,1)} collective-permute-done((bf16[4,80,1280]{2,1,0:T(8,128)(2,1)S(1)}, bf16[4,80,1280]{2,1,0:T(8,128)(2,1)}, u32[]{:S(2)}, u32[]{:S(2)}) %collective-permute-start.10) | collective-permute-done | bytes 819232 | tf_op jit(solution)/shard_map/ppermute | solution.py:34
  39.1 10.0 %collective-permute-done.11 = bf16[4,80,1280]{2,1,0:T(8,128)(2,1)} collective-permute-done((bf16[4,80,1280]{2,1,0:T(8,128)(2,1)S(1)}, bf16[4,80,1280]{2,1,0:T(8,128)(2,1)}, u32[]{:S(2)}, u32[]{:S(2)}) %collective-permute-start.11) | collective-permute-done | bytes 819232 | tf_op jit(solution)/shard_map/ppermute | solution.py:34
  49.0 2.0 %convert_add_fusion.1 = f32[4,80,1280]{2,1,0:T(8,128)S(1)} fusion(bf16[4,80,1280]{2,1,0:T(8,128)(2,1)} %collective-permute-done.12, bf16[4,80,1280]{2,1,0:T(8,128)(2,1)} %collective-permute-done.11, bf16[4,80,1280]{2,1,0:T(8,128)(2,1)} %collective-permute-done.10, bf16[4,80,1280]{2,1,0:T(8,128)(2,1)S(1)} %get-tuple-element.15), kind=kLoop, calls=%fused_computation.7 | loop fusion | flops 2867200 | bytes 4915200 | tf_op jit(solution)/shard_map/add | solution.py:162
  51.0 0.8 fusion.18
  51.9 1.6 collective-permute-start.13
  53.5 3.3 %collective-permute-start.14 = (bf16[80,1280]{1,0:T(8,128)(2,1)}, bf16[80,1280]{1,0:T(8,128)(2,1)}, u32[]{:S(2)}, u32[]{:S(2)}) collective-permute-start(bf16[80,1280]{1,0:T(8,128)(2,1)} %get-tuple-element.25), channel_id=1, source_target_pairs={{0,16},{2,66},{8,24},{10,74},{16,0},{18,82},{24,8},{26,90},{32,48}... | collective-permute-start | bytes 614408 | tf_op jit(solution)/shard_map/ppermute | solution.py:34
  56.8 0.7 collective-permute-start.15
  57.5 13.6 %collective-permute-done.19 = bf16[640,1280]{1,0:T(8,128)(2,1)} collective-permute-done((bf16[640,1280]{1,0:T(8,128)(2,1)}, bf16[640,1280]{1,0:T(8,128)(2,1)}, u32[]{:S(2)}, u32[]{:S(2)}) %collective-permute-start.19) | collective-permute-done | bytes 1638432 | tf_op jit(solution)/shard_map/ppermute | solution.py:23
  71.1 2.8 %collective-permute-start.20 = (bf16[640,1280]{1,0:T(8,128)(2,1)}, bf16[640,1280]{1,0:T(8,128)(2,1)S(1)}, u32[]{:S(2)}, u32[]{:S(2)}) collective-permute-start(bf16[640,1280]{1,0:T(8,128)(2,1)} %collective-permute-done.19), channel_id=1, source_target_pairs={{0,2},{2,0},{1,3},{3,1},{4,6},{6,4},{5,7},{7,5},{8,10},{10,8},{9,1... | collective-permute-start | bytes 4915208 | tf_op jit(solution)/shard_map/ppermute | solution.py:23
  73.9 1.2 fusion.15
  75.2 0.8 dynamic-slice_bitcast_fusion
  76.0 1.2 collective-permute-start.16
  77.2 1.9 %collective-permute-start.18 = (f32[40,1280]{1,0:T(8,128)}, f32[40,1280]{1,0:T(8,128)}, u32[]{:S(2)}, u32[]{:S(2)}) collective-permute-start(f32[40,1280]{1,0:T(8,128)} %get-tuple-element.36), channel_id=1, source_target_pairs={{0,5},{1,4},{4,1},{5,0},{2,7},{3,6},{6,3},{7,2},{8,13},{9,12},{12,... | collective-permute-start | bytes 614408 | tf_op jit(solution)/shard_map/ppermute | solution.py:198
  79.7 23.4 %factor_term.1 = (bf16[4,160,1280]{2,1,0:T(8,128)(2,1)}, bf16[4,160,1280]{2,1,0:T(8,128)(2,1)}, bf16[4,160,1280]{2,1,0:T(8,128)(2,1)}, bf16[4,160,1280]{2,1,0:T(8,128)(2,1)}) custom-call(s32[4]{0:T(128)} %copy-done, bf16[768,2560]{1,0:T(8,128)(2,1)} %b0.1, bf16[768,2560]{1,0:T(8,128)(2,1)} %collective-permute-done.ha1.hb1.b1, bf16[768,2560]{1,0:T(8,128)(2,1)} %a0.1, ...), custom_call_target="tpu_custom_call" | custom-call | flops 10066329600 | bytes 15728640 | tf_op jit(solution)/shard_map/factor_term/pallas_call | solution.py:141
  103.6 0.7 collective-permute-start.3
  104.4 1.8 %collective-permute-start.4 = (bf16[4,160,1280]{2,1,0:T(8,128)(2,1)}, bf16[4,160,1280]{2,1,0:T(8,128)(2,1)}, u32[]{:S(2)}, u32[]{:S(2)}) collective-permute-start(bf16[4,160,1280]{2,1,0:T(8,128)(2,1)} %get-tuple-element.14), channel_id=1, source_target_pairs={{0,96},{2,26},{8,104},{10,2},{16,112},{18,10},{24,120},{26,18},{32... | collective-permute-start | bytes 4915208 | tf_op jit(solution)/shard_map/ppermute | solution.py:34
  106.2 1.3 broadcast_select_fusion.1
  107.5 1.1 fusion
  108.7 1.8 %convolution_add_fusion.1 = f32[80,1280]{1,0:T(8,128)S(1)} fusion(f32[80,1280]{1,0:T(8,128)S(1)} %fusion, bf16[640,1280]{1,0:T(8,128)(2,1)} %collective-permute-done.19, s32[]{:T(128)S(6)} %select_n.108, bf16[40,2560]{1,0:T(8,128)(2,1)S(1)} %get-tuple-element.34, bf16[40,2560]{1,0:T(8,128)(2,1)S(1)} %get-tuple-element.35), kind=kOutput, calls=%fused_computation.4 | convolution fusion | flops 131379200 | bytes 2867204 | tf_op jit(solution)/shard_map/dot_general | solution.py:214
  110.9 1.3 fusion.9
  112.2 2.3 %reshape.32 = f32[40,32,2,40]{3,2,1,0:T(2,128)S(1)} reshape(f32[40,2560]{1,0:T(8,128)S(1)} %pad_maximum_fusion.3) | data formatting | bytes 819200 | tf_op jit(solution)/shard_map/reshape | solution.py:222
  114.5 0.8 copy.6
  115.3 1.9 %reshape.35 = f32[64,1,1600]{2,1,0:T(1,128)} reshape(f32[64,40,40]{2,1,0:T(8,128)S(1)} %bitcast.62) | data formatting | bytes 819200
  117.2 7.4 %all-to-all-start = ((f32[64,1,1600]{2,1,0:T(1,128)}), f32[64,1,1600]{2,1,0:T(1,128)S(1)}, u32[]{:S(2)}, u32[]{:S(2)}) async-start(f32[64,1,1600]{2,1,0:T(1,128)} %reshape.35), calls=%async_computation | async-start | bytes 851968 | tf_op jit(solution)/shard_map/all_to_all | solution.py:223
  124.6 24.1 %all-to-all-done = f32[64,1,1600]{2,1,0:T(1,128)S(1)} async-done(((f32[64,1,1600]{2,1,0:T(1,128)}), f32[64,1,1600]{2,1,0:T(1,128)S(1)}, u32[]{:S(2)}, u32[]{:S(2)}) %all-to-all-start) | async-done | bytes 409632 | tf_op jit(solution)/shard_map/all_to_all | solution.py:223
  149.3 1.7 reduce
  150.9 1.6 reshape.36
  152.6 3.8 %convert_add_fusion = f32[4,160,1280]{2,1,0:T(8,128)S(1)} fusion(bf16[4,160,1280]{2,1,0:T(8,128)(2,1)} %collective-permute-done.4, bf16[4,160,1280]{2,1,0:T(8,128)(2,1)} %collective-permute-done.3, bf16[4,160,1280]{2,1,0:T(8,128)(2,1)} %collective-permute-done.2, bf16[4,160,1280]{2,1,0:T(8,128)(2,1)} %get-tuple-element.11), kind=kLoop, calls=%fused_computation.2 | loop fusion | flops 5734400 | bytes 9830400 | tf_op jit(solution)/shard_map/add | solution.py:162
  156.6 1.8 %collective-permute-start.5 = (bf16[160,1280]{1,0:T(8,128)(2,1)S(1)}, bf16[160,1280]{1,0:T(8,128)(2,1)S(1)}, u32[]{:S(2)}, u32[]{:S(2)}) collective-permute-start(bf16[160,1280]{1,0:T(8,128)(2,1)S(1)} %get-tuple-element.20), channel_id=1, source_target_pairs={{0,8},{2,34},{8,16},{10,42},{16,24},{18,50},{24,0},{26,58},{32,40}... | collective-permute-start | bytes 1228808 | tf_op jit(solution)/shard_map/ppermute | solution.py:34
  158.4 1.9 %collective-permute-start.6 = (bf16[160,1280]{1,0:T(8,128)(2,1)S(1)}, bf16[160,1280]{1,0:T(8,128)(2,1)S(1)}, u32[]{:S(2)}, u32[]{:S(2)}) collective-permute-start(bf16[160,1280]{1,0:T(8,128)(2,1)S(1)} %get-tuple-element.22), channel_id=1, source_target_pairs={{0,16},{2,66},{8,24},{10,74},{16,0},{18,82},{24,8},{26,90},{32,48}... | collective-permute-start | bytes 1228808 | tf_op jit(solution)/shard_map/ppermute | solution.py:34
  160.3 0.8 collective-permute-start.7
  161.3 3.6 %collective-permute-done.5 = bf16[160,1280]{1,0:T(8,128)(2,1)S(1)} collective-permute-done((bf16[160,1280]{1,0:T(8,128)(2,1)S(1)}, bf16[160,1280]{1,0:T(8,128)(2,1)S(1)}, u32[]{:S(2)}, u32[]{:S(2)}) %collective-permute-start.5) | collective-permute-done | bytes 409632 | tf_op jit(solution)/shard_map/ppermute | solution.py:34
  164.9 5.4 %collective-permute-done.6 = bf16[160,1280]{1,0:T(8,128)(2,1)S(1)} collective-permute-done((bf16[160,1280]{1,0:T(8,128)(2,1)S(1)}, bf16[160,1280]{1,0:T(8,128)(2,1)S(1)}, u32[]{:S(2)}, u32[]{:S(2)}) %collective-permute-start.6) | collective-permute-done | bytes 409632 | tf_op jit(solution)/shard_map/ppermute | solution.py:34
  170.5 0.8 collective-permute-start.8
  171.4 1.2 fusion.5
  172.5 3.3 %collective-permute-done.8 = bf16[80,1280]{1,0:T(8,128)(2,1)S(1)} collective-permute-done((bf16[80,1280]{1,0:T(8,128)(2,1)S(1)}, bf16[80,1280]{1,0:T(8,128)(2,1)S(1)}, u32[]{:S(2)}, u32[]{:S(2)}) %collective-permute-start.8) | collective-permute-done | bytes 204832 | tf_op jit(solution)/shard_map/ppermute | solution.py:23
  175.9 2.3 %collective-permute-start.9 = (f32[40,1280]{1,0:T(8,128)S(1)}, f32[40,1280]{1,0:T(8,128)S(1)}, u32[]{:S(2)}, u32[]{:S(2)}) collective-permute-start(f32[40,1280]{1,0:T(8,128)S(1)} %dynamic-slice_bitcast_fusion.2), channel_id=1, source_target_pairs={{0,2},{2,0},{1,3},{3,1},{4,6},{6,4},{5,7},{7,5},{8,10},{10,8},{9,1... | collective-permute-start | bytes 614408 | tf_op jit(solution)/shard_map/ppermute | solution.py:23
  178.3 0.7 slice_add_fusion
  179.4 0.8 maximum_bitcast_fusion
  (43 shorter events, 3.4 us)
Async XLA Ops:
  0.6 8.3 %collective-permute-start = (bf16[768,2560]{1,0:T(8,128)(2,1)}, bf16[768,2560]{1,0:T(8,128)(2,1)}, u32[]{:S(2)}, u32[]{:S(2)}) collective-permute-start(bf16[768,2560]{1,0:T(8,128)(2,1)} %b0.1), channel_id=1, source_target_pairs={{0,2},{2,0},{1,3},{3,1},{4,6},{6,4},{5,7},{7,5},{8,10},{10,8},{9,1... | collective-permute-start | bytes 11796488 | tf_op jit(solution)/shard_map/ppermute | solution.py:23
  2.1 12.4 %collective-permute-start.1 = (bf16[768,2560]{1,0:T(8,128)(2,1)}, bf16[768,2560]{1,0:T(8,128)(2,1)}, u32[]{:S(2)}, u32[]{:S(2)}) collective-permute-start(bf16[768,2560]{1,0:T(8,128)(2,1)} %a0.1), channel_id=1, source_target_pairs={{0,2},{2,0},{1,3},{3,1},{4,6},{6,4},{5,7},{7,5},{8,10},{10,8},{9,1... | collective-permute-start | bytes 11796488 | tf_op jit(solution)/shard_map/ppermute | solution.py:23
  2.3 23.7 %copy-start = (s32[4]{0:T(128)}, s32[4]{0:T(128)S(1)}, u32[]{:S(2)}) copy-start(s32[4]{0:T(128)S(1)} %pad_add_fusion.place) | copy-start | bytes 52
  26.0 13.0 %collective-permute-start.10 = (bf16[4,80,1280]{2,1,0:T(8,128)(2,1)S(1)}, bf16[4,80,1280]{2,1,0:T(8,128)(2,1)}, u32[]{:S(2)}, u32[]{:S(2)}) collective-permute-start(bf16[4,80,1280]{2,1,0:T(8,128)(2,1)S(1)} %get-tuple-element.16), channel_id=1, source_target_pairs={{0,32},{2,10},{8,40},{10,18},{16,48},{18,26},{24,56},{26,2},{32,64... | collective-permute-start | bytes 2457608 | tf_op jit(solution)/shard_map/ppermute | solution.py:34
  27.5 21.5 %collective-permute-start.11 = (bf16[4,80,1280]{2,1,0:T(8,128)(2,1)S(1)}, bf16[4,80,1280]{2,1,0:T(8,128)(2,1)}, u32[]{:S(2)}, u32[]{:S(2)}) collective-permute-start(bf16[4,80,1280]{2,1,0:T(8,128)(2,1)S(1)} %get-tuple-element.17), channel_id=1, source_target_pairs={{0,64},{2,18},{8,72},{10,26},{16,80},{18,2},{24,88},{26,10},{32,96... | collective-permute-start | bytes 2457608 | tf_op jit(solution)/shard_map/ppermute | solution.py:34
  30.1 18.9 %collective-permute-start.12 = (bf16[4,80,1280]{2,1,0:T(8,128)(2,1)S(1)}, bf16[4,80,1280]{2,1,0:T(8,128)(2,1)}, u32[]{:S(2)}, u32[]{:S(2)}) collective-permute-start(bf16[4,80,1280]{2,1,0:T(8,128)(2,1)S(1)} %get-tuple-element.18), channel_id=1, source_target_pairs={{0,96},{2,26},{8,104},{10,2},{16,112},{18,10},{24,120},{26,18},{32... | collective-permute-start | bytes 2457608 | tf_op jit(solution)/shard_map/ppermute | solution.py:34
  33.9 37.2 %collective-permute-start.19 = (bf16[640,1280]{1,0:T(8,128)(2,1)}, bf16[640,1280]{1,0:T(8,128)(2,1)}, u32[]{:S(2)}, u32[]{:S(2)}) collective-permute-start(bf16[640,1280]{1,0:T(8,128)(2,1)} %constant_dynamic-slice_fusion), channel_id=1, source_target_pairs={{0,1},{1,0},{2,3},{3,2},{4,5},{5,4},{6,7},{7,6},{8,9},{9,8},{10,11... | collective-permute-start | bytes 4915208 | tf_op jit(solution)/shard_map/ppermute | solution.py:23
  51.9 22.0 %collective-permute-start.13 = (bf16[80,1280]{1,0:T(8,128)(2,1)}, bf16[80,1280]{1,0:T(8,128)(2,1)}, u32[]{:S(2)}, u32[]{:S(2)}) collective-permute-start(bf16[80,1280]{1,0:T(8,128)(2,1)} %get-tuple-element.23), channel_id=1, source_target_pairs={{0,8},{2,34},{8,16},{10,42},{16,24},{18,50},{24,0},{26,58},{32,40}... | collective-permute-start | bytes 614408 | tf_op jit(solution)/shard_map/ppermute | solution.py:34
  53.5 20.4 %collective-permute-start.14 = (bf16[80,1280]{1,0:T(8,128)(2,1)}, bf16[80,1280]{1,0:T(8,128)(2,1)}, u32[]{:S(2)}, u32[]{:S(2)}) collective-permute-start(bf16[80,1280]{1,0:T(8,128)(2,1)} %get-tuple-element.25), channel_id=1, source_target_pairs={{0,16},{2,66},{8,24},{10,74},{16,0},{18,82},{24,8},{26,90},{32,48}... | collective-permute-start | bytes 614408 | tf_op jit(solution)/shard_map/ppermute | solution.py:34
  56.8 17.1 %collective-permute-start.15 = (bf16[80,1280]{1,0:T(8,128)(2,1)}, bf16[80,1280]{1,0:T(8,128)(2,1)}, u32[]{:S(2)}, u32[]{:S(2)}) collective-permute-start(bf16[80,1280]{1,0:T(8,128)(2,1)} %get-tuple-element.24), channel_id=1, source_target_pairs={{0,24},{2,98},{8,0},{10,106},{16,8},{18,114},{24,16},{26,122},{32,... | collective-permute-start | bytes 614408 | tf_op jit(solution)/shard_map/ppermute | solution.py:34
  71.1 39.4 %collective-permute-start.20 = (bf16[640,1280]{1,0:T(8,128)(2,1)}, bf16[640,1280]{1,0:T(8,128)(2,1)S(1)}, u32[]{:S(2)}, u32[]{:S(2)}) collective-permute-start(bf16[640,1280]{1,0:T(8,128)(2,1)} %collective-permute-done.19), channel_id=1, source_target_pairs={{0,2},{2,0},{1,3},{3,1},{4,6},{6,4},{5,7},{7,5},{8,10},{10,8},{9,1... | collective-permute-start | bytes 4915208 | tf_op jit(solution)/shard_map/ppermute | solution.py:23
  76.0 27.7 %collective-permute-start.16 = (f32[40,1280]{1,0:T(8,128)}, f32[40,1280]{1,0:T(8,128)}, u32[]{:S(2)}, u32[]{:S(2)}) collective-permute-start(f32[40,1280]{1,0:T(8,128)} %get-tuple-element.36), channel_id=1, source_target_pairs={{0,4},{4,0},{1,5},{5,1},{2,6},{6,2},{3,7},{7,3},{8,12},{12,8},{9,1... | collective-permute-start | bytes 614408 | tf_op jit(solution)/shard_map/ppermute | solution.py:23
  77.2 29.0 %collective-permute-start.18 = (f32[40,1280]{1,0:T(8,128)}, f32[40,1280]{1,0:T(8,128)}, u32[]{:S(2)}, u32[]{:S(2)}) collective-permute-start(f32[40,1280]{1,0:T(8,128)} %get-tuple-element.36), channel_id=1, source_target_pairs={{0,5},{1,4},{4,1},{5,0},{2,7},{3,6},{6,3},{7,2},{8,13},{9,12},{12,... | collective-permute-start | bytes 614408 | tf_op jit(solution)/shard_map/ppermute | solution.py:198
  79.0 28.5 %slice-start = ((s8[6553600]{0:T(1024)(128)(4,1)}), s8[4194304]{0:T(1024)(128)(4,1)S(1)}, s32[]{:S(2)}) async-start(s8[6553600]{0:T(1024)(128)(4,1)} %bitcast.58), calls=%async_computation.1 | async-start | bytes 8388608
  79.0 28.5 %slice-start.1 = ((s8[6553600]{0:T(1024)(128)(4,1)}), s8[2359296]{0:T(1024)(128)(4,1)S(1)}, s32[]{:S(2)}) async-start(s8[6553600]{0:T(1024)(128)(4,1)} %bitcast.58), calls=%async_computation.2 | async-start | bytes 4718592
  79.0 25.3 %collective-permute-start.17 = (f32[40,1280]{1,0:T(8,128)}, f32[40,1280]{1,0:T(8,128)}, u32[]{:S(2)}, u32[]{:S(2)}) collective-permute-start(f32[40,1280]{1,0:T(8,128)} %get-tuple-element.37), channel_id=1, source_target_pairs={{0,1},{1,0},{2,3},{3,2},{4,5},{5,4},{6,7},{7,6},{8,9},{9,8},{10,11... | collective-permute-start | bytes 614408 | tf_op jit(solution)/shard_map/ppermute | solution.py:23
  103.1 49.5 %collective-permute-start.2 = (bf16[4,160,1280]{2,1,0:T(8,128)(2,1)}, bf16[4,160,1280]{2,1,0:T(8,128)(2,1)}, u32[]{:S(2)}, u32[]{:S(2)}) collective-permute-start(bf16[4,160,1280]{2,1,0:T(8,128)(2,1)} %get-tuple-element.12), channel_id=1, source_target_pairs={{0,32},{2,10},{8,40},{10,18},{16,48},{18,26},{24,56},{26,2},{32,64... | collective-permute-start | bytes 4915208 | tf_op jit(solution)/shard_map/ppermute | solution.py:34
  103.6 49.0 %collective-permute-start.3 = (bf16[4,160,1280]{2,1,0:T(8,128)(2,1)}, bf16[4,160,1280]{2,1,0:T(8,128)(2,1)}, u32[]{:S(2)}, u32[]{:S(2)}) collective-permute-start(bf16[4,160,1280]{2,1,0:T(8,128)(2,1)} %get-tuple-element.13), channel_id=1, source_target_pairs={{0,64},{2,18},{8,72},{10,26},{16,80},{18,2},{24,88},{26,10},{32,96... | collective-permute-start | bytes 4915208 | tf_op jit(solution)/shard_map/ppermute | solution.py:34
  104.4 48.2 %collective-permute-start.4 = (bf16[4,160,1280]{2,1,0:T(8,128)(2,1)}, bf16[4,160,1280]{2,1,0:T(8,128)(2,1)}, u32[]{:S(2)}, u32[]{:S(2)}) collective-permute-start(bf16[4,160,1280]{2,1,0:T(8,128)(2,1)} %get-tuple-element.14), channel_id=1, source_target_pairs={{0,96},{2,26},{8,104},{10,2},{16,112},{18,10},{24,120},{26,18},{32... | collective-permute-start | bytes 4915208 | tf_op jit(solution)/shard_map/ppermute | solution.py:34
  117.2 31.5 %all-to-all-start = ((f32[64,1,1600]{2,1,0:T(1,128)}), f32[64,1,1600]{2,1,0:T(1,128)S(1)}, u32[]{:S(2)}, u32[]{:S(2)}) async-start(f32[64,1,1600]{2,1,0:T(1,128)} %reshape.35), calls=%async_computation | async-start | bytes 851968 | tf_op jit(solution)/shard_map/all_to_all | solution.py:223
  150.9 20.5 %slice-start.2 = ((s8[6553600]{0:T(1024)(128)(4,1)}), s8[2359296]{0:T(1024)(128)(4,1)S(1)}, s32[]{:S(2)}) async-start(s8[6553600]{0:T(1024)(128)(4,1)} %bitcast.60), calls=%async_computation.3 | async-start | bytes 4718592
  152.6 18.8 %slice-start.3 = ((s8[6553600]{0:T(1024)(128)(4,1)}), s8[4194304]{0:T(1024)(128)(4,1)S(1)}, s32[]{:S(2)}) async-start(s8[6553600]{0:T(1024)(128)(4,1)} %bitcast.60), calls=%async_computation.4 | async-start | bytes 8388608
  156.4 4.7 %copy-start.1 = (f32[64,40,40]{2,1,0:T(8,128)S(1)}, f32[64,40,40]{2,1,0:T(8,128)}, u32[]{:S(2)}) copy-start(f32[64,40,40]{2,1,0:T(8,128)} %reshape.36) | copy-start | bytes 1228804
  156.6 8.4 %collective-permute-start.5 = (bf16[160,1280]{1,0:T(8,128)(2,1)S(1)}, bf16[160,1280]{1,0:T(8,128)(2,1)S(1)}, u32[]{:S(2)}, u32[]{:S(2)}) collective-permute-start(bf16[160,1280]{1,0:T(8,128)(2,1)S(1)} %get-tuple-element.20), channel_id=1, source_target_pairs={{0,8},{2,34},{8,16},{10,42},{16,24},{18,50},{24,0},{26,58},{32,40}... | collective-permute-start | bytes 1228808 | tf_op jit(solution)/shard_map/ppermute | solution.py:34
  158.4 12.0 %collective-permute-start.6 = (bf16[160,1280]{1,0:T(8,128)(2,1)S(1)}, bf16[160,1280]{1,0:T(8,128)(2,1)S(1)}, u32[]{:S(2)}, u32[]{:S(2)}) collective-permute-start(bf16[160,1280]{1,0:T(8,128)(2,1)S(1)} %get-tuple-element.22), channel_id=1, source_target_pairs={{0,16},{2,66},{8,24},{10,74},{16,0},{18,82},{24,8},{26,90},{32,48}... | collective-permute-start | bytes 1228808 | tf_op jit(solution)/shard_map/ppermute | solution.py:34
  160.3 10.0 %collective-permute-start.7 = (bf16[160,1280]{1,0:T(8,128)(2,1)S(1)}, bf16[160,1280]{1,0:T(8,128)(2,1)S(1)}, u32[]{:S(2)}, u32[]{:S(2)}) collective-permute-start(bf16[160,1280]{1,0:T(8,128)(2,1)S(1)} %get-tuple-element.21), channel_id=1, source_target_pairs={{0,24},{2,98},{8,0},{10,106},{16,8},{18,114},{24,16},{26,122},{32,... | collective-permute-start | bytes 1228808 | tf_op jit(solution)/shard_map/ppermute | solution.py:34
  170.5 5.3 %collective-permute-start.8 = (bf16[80,1280]{1,0:T(8,128)(2,1)S(1)}, bf16[80,1280]{1,0:T(8,128)(2,1)S(1)}, u32[]{:S(2)}, u32[]{:S(2)}) collective-permute-start(bf16[80,1280]{1,0:T(8,128)(2,1)S(1)} %fusion.17), channel_id=1, source_target_pairs={{0,4},{4,0},{1,5},{5,1},{2,6},{6,2},{3,7},{7,3},{8,12},{12,8},{9,1... | collective-permute-start | bytes 614408 | tf_op jit(solution)/shard_map/ppermute | solution.py:23
  175.9 3.4 %collective-permute-start.9 = (f32[40,1280]{1,0:T(8,128)S(1)}, f32[40,1280]{1,0:T(8,128)S(1)}, u32[]{:S(2)}, u32[]{:S(2)}) collective-permute-start(f32[40,1280]{1,0:T(8,128)S(1)} %dynamic-slice_bitcast_fusion.2), channel_id=1, source_target_pairs={{0,2},{2,0},{1,3},{3,1},{4,6},{6,4},{5,7},{7,5},{8,10},{10,8},{9,1... | collective-permute-start | bytes 614408 | tf_op jit(solution)/shard_map/ppermute | solution.py:23

commit v2 on v1

--- a/solution.py
+++ b/solution.py
@@ -46,7 +46,8 @@
 def place_blocks(place, buffer, sems, outs, m, n, zs, finish):
     core, z_me, y_me = place[1], place[2], place[3]
     rows = TILE // (zs * 4)
-    lanes = pl.ds(pl.multiple_of(n * TILE, TILE), TILE)
+    wide = buffer.shape[2] // sems.shape[1]
+    lanes = pl.ds(pl.multiple_of(n * wide, wide), wide)
     for a in range(zs):
         for k in range(4):
             z = m * zs + a
@@ -66,28 +67,26 @@
                 pl.when(ahead == r)(functools.partial(move, out))
 
 
-def store_tile(place, buffer, sems, outs, tile, steps, zs):
+def store_tile(place, buffer, sems, outs, m, n, steps, lanes, zs):
+    place_blocks(place, buffer, sems, outs, m, n, zs, False)
+
+    @pl.when((m == steps - 1) & (n == lanes - 1))
+    def _():
+        for i in range(steps):
+            for j in range(lanes):
+                place_blocks(place, buffer, sems, outs, i, j, zs, True)
+
+
+def cross_kernel(place, a0, a1, b0, b1, own, ahead1, ahead2, ahead3, buffer, sems):
     m, n = pl.program_id(0), pl.program_id(1)
+    tile = (contract(a0[...], b0[...]) + contract(a1[...], b1[...])).astype(BF)
     for lane in range(2):
 
         @pl.when(n == lane)
         def _():
-            buffer[m, :, lane * TILE : (lane + 1) * TILE] = tile()
-
-    place_blocks(place, buffer, sems, outs, m, n, zs, False)
-
-    @pl.when((m == steps - 1) & (n == 1))
-    def _():
-        for i in range(steps):
-            for j in range(2):
-                place_blocks(place, buffer, sems, outs, i, j, zs, True)
-
-
-def cross_kernel(place, a0, a1, b0, b1, own, ahead1, ahead2, ahead3, buffer, sems):
-    def tile():
-        return (contract(a0[...], b0[...]) + contract(a1[...], b1[...])).astype(BF)
-
-    store_tile(place, buffer, sems, [own, ahead1, ahead2, ahead3], tile, 2, 2)
+            buffer[m, :, lane * TILE : (lane + 1) * TILE] = tile
+
+    store_tile(place, buffer, sems, [own, ahead1, ahead2, ahead3], m, n, 2, 2, 2)
 
 
 def cross_term(place, grads, grads_next, acts, acts_next):
@@ -117,36 +116,32 @@
 def factor_kernel(
     place, ha0, ha1, ga0, ga1, hb0, hb1, gb0, gb1, own, ahead1, ahead2, ahead3, buffer, sems
 ):
-    def tile():
-        def term(a0, a1, b0, b1):
-            return (contract(a0[...], b0[...]) + contract(a1[...], b1[...])).astype(BF)
-
-        return lax.cond(
-            place[0] == 0,
-            lambda: term(ha0, ha1, hb0, hb1),
-            lambda: term(ga0, ga1, gb0, gb1),
-        )
-
-    store_tile(place, buffer, sems, [own, ahead1, ahead2, ahead3], tile, 4, 1)
+    m = pl.program_id(0)
+
+    def tile(a0, a1, b0, b1):
+        buffer[m] = (contract(a0[...], b0[...]) + contract(a1[...], b1[...])).astype(BF)
+
+    pl.when(place[0] == 0)(lambda: tile(ha0, ha1, hb0, hb1))
+    pl.when(place[0] == 1)(lambda: tile(ga0, ga1, gb0, gb1))
+    store_tile(place, buffer, sems, [own, ahead1, ahead2, ahead3], m, 0, 4, 1, 1)
 
 
 def factor_term(place, acts, acts_next, grads, grads_next):
     tokens, width = acts.shape
     half = width // 2
-    a_acts = pl.BlockSpec((tokens, TILE), lambda m, n, p: (0, m * (1 - p[0])))
-    a_grads = pl.BlockSpec((tokens, TILE), lambda m, n, p: (0, m * p[0]))
-    b_acts = pl.BlockSpec((tokens, TILE), lambda m, n, p: (0, (p[1] * 2 + n) * (1 - p[0])))
-    b_grads = pl.BlockSpec((tokens, TILE), lambda m, n, p: (0, (p[1] * 2 + n) * p[0]))
+    a_acts = pl.BlockSpec((tokens, TILE), lambda m, p: (0, m * (1 - p[0])))
+    a_grads = pl.BlockSpec((tokens, TILE), lambda m, p: (0, m * p[0]))
+    b = pl.BlockSpec((tokens, half), lambda m, p: (0, p[1]))
     out = jax.ShapeDtypeStruct((4, width // 16, half), BF)
     return pl.pallas_call(
         factor_kernel,
         out_shape=[out] * 4,
         grid_spec=pltpu.PrefetchScalarGridSpec(
             num_scalar_prefetch=1,
-            grid=(4, 2),
-            in_specs=[a_acts, a_acts, a_grads, a_grads, b_acts, b_acts, b_grads, b_grads],
+            grid=(4,),
+            in_specs=[a_acts, a_acts, a_grads, a_grads, b, b, b, b],
             out_specs=[pl.BlockSpec(memory_space=pl.ANY)] * 4,
-            scratch_shapes=[pltpu.VMEM((4, TILE, half), BF), pltpu.SemaphoreType.DMA((4, 2, 4))],
+            scratch_shapes=[pltpu.VMEM((4, TILE, half), BF), pltpu.SemaphoreType.DMA((4, 1, 4))],
         ),
         compiler_params=pltpu.CompilerParams(vmem_limit_bytes=56 * 2**20),
         cost_estimate=pl.CostEstimate(
@@ -161,6 +156,18 @@
     for x in rest:
         total = total + x.astype(F32)
     return total
+
+
+def gate(x, *others):
+    anywhere = pl.BlockSpec(memory_space=pl.ANY)
+    return pl.pallas_call(
+        lambda *refs: None,
+        out_shape=jax.ShapeDtypeStruct(x.shape, x.dtype),
+        in_specs=[anywhere] * (1 + len(others)),
+        out_specs=anywhere,
+        input_output_aliases={0: 0},
+        name="gate",
+    )(x, *others)
 
 
 def send_second(x, me):
@@ -183,12 +190,9 @@
     own, m1, m2, m3 = cross_term(place, out_grad, grads_next, hidden, acts_next)
     m_parts = [own, turn(m1, 1, 0), turn(m2, 2, 0), turn(m3, 3, 0)]
 
-    piece = lax.dynamic_slice_in_dim(left_inverse, o * half + c * TILE, TILE, 0)
-    piece = shift(piece, "o", 1)
-    piece_next = shift(piece, "c", 1)
-
     own, f1, f2, f3 = factor_term(place, hidden, acts_next, out_grad, grads_next)
 
+    m_parts[0] = gate(m_parts[0], own)
     m = add(*m_parts)
     _, received = send_second(m, second_me)
     f_parts = [own, turn(f1, 1, 0), turn(f2, 2, 0), turn(f3, 3, 0)]
@@ -205,17 +209,8 @@
     rows = mrow.shape[0]
     stacked = jnp.concatenate(split_pair(mrow))
     pt = jnp.dot(stacked, left_inverse, preferred_element_type=F32)
-    beside = lax.dynamic_slice_in_dim(left_inverse, (1 - o) * half, half, 0)
-    at_own = lax.dynamic_slice_in_dim(stacked, o * half, half, 1)
-    at_piece = lax.dynamic_slice_in_dim(stacked, (1 - o) * half + c * TILE, TILE, 1)
-    at_next = lax.dynamic_slice_in_dim(stacked, (1 - o) * half + (1 - c) * TILE, TILE, 1)
-    pt_other = (
-        lax.dot_general(at_own, beside, (((1,), (1,)), ((), ())), preferred_element_type=F32)
-        + jnp.dot(at_piece, piece, preferred_element_type=F32)
-        + jnp.dot(at_next, piece_next, preferred_element_type=F32)
-    )
     pt = pt[:rows] + pt[rows:]
-    pt_other = pt_other[:rows] + pt_other[rows:]
+    pt_other = shift(pt, "o", 1)
     pt = jnp.concatenate(
         [jnp.where(first, pt, pt_other), jnp.where(first, pt_other, pt)], axis=1
     )
@@ -224,7 +219,7 @@
 
     f = add(*f_parts)
     pieces, received = send_second(f, second_me)
-    blocks = lax.optimization_barrier((blocks, pieces))[0].reshape(width, rows)
+    blocks = gate(blocks, pieces[0]).reshape(width, rows)
     stacked = jnp.concatenate(split_pair(blocks), axis=1)
     update = contract(stacked, right_inverse)
     update = update[:rows] + update[rows:]

time: 181 us -> 149 us (0.82)
  waiting for transfers between devices: 75 us -> 49.5 us
  Pallas kernels: 34.9 us -> 29.9 us
  starting transfers between devices: 39.9 us -> 35.4 us
  matrix products: 5.75 us -> 8.13 us
  other arithmetic: 12.1 us -> 14 us
    all_to_all x1, waiting for transfers between devices: 24.1 us -> 0.01 us  [per_device(): blocks = lax.all_to_all(blocks, ('c', 'z', 'y', 'xl'), 0, 0, tiled=True)]
    ppermute x8 -> x7, waiting for transfers between devices: 29.5 us -> 18.7 us  [shift(): return lax.ppermute(x, axis, [(i, (i + step) % size) for i in range(size)])]
    ppermute x12, starting transfers between devices: 18.4 us -> 10.4 us  [turn(): return lax.ppermute(x, ('z', 'y', 'c'), pairs)]
    pallas_call x1, Pallas kernels: 23.4 us -> 18.1 us  [factor_term(): pl.pallas_call(factor_kernel, out_shape=[out] * 4, grid_spec=pltpu.Prefet...]
    ppermute x12, waiting for transfers between devices: 21.4 us -> 26.6 us  [turn(): return lax.ppermute(x, ('z', 'y', 'c'), pairs)]
    ppermute x1, waiting for transfers between devices: 0.01 us -> 4.22 us  [per_device(): lax.ppermute(theirs, ('xl', 'o'), [(i, 3 - i) for i in range(4)])]
    unnamed x13 -> x6, local copies, waits for them, and re-layouts: 1.92 us -> 5.4 us
    dot_general x3 -> x0, matrix products: 3.33 us -> none  [the longest x1 1.82 us: per_device(): jnp.dot(at_piece, piece, preferred_element_type=F32)]
  transfers between devices with their start and end apart: 22 -> 21, of which waited for: 10 -> 12; matrix products, arithmetic and copies ran while one was open for 14% -> 18% of each run, Pallas kernels for 13% -> 12%
where the time goes in v2:
time: 149 us; the launch traced here: 148 us
  waiting for transfers between devices  49.5 us (33%)
  starting transfers between devices  35.4 us (24%)
  Pallas kernels  29.9 us (20%)
  other arithmetic  14 us (9%)
  local copies, waits for them, and re-layouts  10.3 us (7%)
  matrix products  8.13 us (5%)
    ppermute x12, waiting for transfers between devices, turn(): return lax.ppermute(x, ('z', 'y', 'c'), pairs)  26.6 us
    ppermute x7, waiting for transfers between devices, shift(): return lax.ppermute(x, axis, [(i, (i + step) % size) for i in range(size)])  18.7 us
    pallas_call x1, Pallas kernels, factor_term(): pl.pallas_call(factor_kernel, out_shape=[out] * 4, grid_spec=pltpu.Prefet...  18.1 us
    ppermute x7, starting transfers between devices, shift(): return lax.ppermute(x, axis, [(i, (i + step) % size) for i in range(size)])  15.1 us
    pallas_call x1, Pallas kernels, cross_term(): pl.pallas_call(cross_kernel, out_shape=[out] * 4, grid_spec=pltpu.Prefetc...  11.8 us
    ppermute x12, starting transfers between devices, turn(): return lax.ppermute(x, ('z', 'y', 'c'), pairs)  10.4 us
    all_to_all x1, starting transfers between devices, per_device(): blocks = lax.all_to_all(blocks, ('c', 'z', 'y', 'xl'), 0, 0, tiled=True)  9.09 us
    add x4, other arithmetic, add(): total = total + x.astype(F32)  7.16 us
  transfers between devices with their start and end apart: 21, of which 12 were waited for; matrix products, arithmetic and copies ran while one was open for 18% of the time, Pallas kernels for 12%

profile of v2, /device:TPU:1, one launch (start us, length us, event | category | flops | bytes accessed | tf_op | source)
XLA Modules:
  0.0 148.0 jit_solution(3486095637231724413)
XLA Ops:
  0.6 1.5 %collective-permute-start = (bf16[768,2560]{1,0:T(8,128)(2,1)}, bf16[768,2560]{1,0:T(8,128)(2,1)}, u32[]{:S(2)}, u32[]{:S(2)}) collective-permute-start(bf16[768,2560]{1,0:T(8,128)(2,1)} %b0.1), channel_id=1, source_target_pairs={{0,2},{2,0},{1,3},{3,1},{4,6},{6,4},{5,7},{7,5},{8,10},{10,8},{9,1... | collective-permute-start | bytes 11796488 | tf_op jit(solution)/shard_map/ppermute | solution.py:23
  2.1 0.1 collective-permute-start.1
  2.3 6.6 %collective-permute-done.ha1.hb1.b1 = bf16[768,2560]{1,0:T(8,128)(2,1)} collective-permute-done((bf16[768,2560]{1,0:T(8,128)(2,1)}, bf16[768,2560]{1,0:T(8,128)(2,1)}, u32[]{:S(2)}, u32[]{:S(2)}) %collective-permute-start) | collective-permute-done | bytes 3932192 | tf_op jit(solution)/shard_map/ppermute | solution.py:23
  8.9 5.6 %collective-permute-done.1.ga1.gb1.a1 = bf16[768,2560]{1,0:T(8,128)(2,1)} collective-permute-done((bf16[768,2560]{1,0:T(8,128)(2,1)}, bf16[768,2560]{1,0:T(8,128)(2,1)}, u32[]{:S(2)}, u32[]{:S(2)}) %collective-permute-start.1) | collective-permute-done | bytes 3932192 | tf_op jit(solution)/shard_map/ppermute | solution.py:23
  14.5 11.8 %cross_term.1 = (bf16[4,80,1280]{2,1,0:T(8,128)(2,1)S(1)}, bf16[4,80,1280]{2,1,0:T(8,128)(2,1)S(1)}, bf16[4,80,1280]{2,1,0:T(8,128)(2,1)S(1)}, bf16[4,80,1280]{2,1,0:T(8,128)(2,1)S(1)}) custom-call(s32[4]{0:T(128)S(1)} %pad_add_fusion.place, bf16[768,2560]{1,0:T(8,128)(2,1)} %a0.1, bf16[768,2560]{1,0:T(8,128)(2,1)} %collective-permute-done.1.ga1.gb1.a1, ...), custom_call_target="tpu_custom_call" | custom-call | flops 5033164800 | bytes 9830400 | tf_op jit(solution)/shard_map/cross_term/pallas_call | solution.py:98
  26.3 0.9 copy-done
  27.2 2.8 %collective-permute-start.12 = (bf16[4,80,1280]{2,1,0:T(8,128)(2,1)S(1)}, bf16[4,80,1280]{2,1,0:T(8,128)(2,1)S(1)}, u32[]{:S(2)}, u32[]{:S(2)}) collective-permute-start(bf16[4,80,1280]{2,1,0:T(8,128)(2,1)S(1)} %get-tuple-element.17), channel_id=1, source_target_pairs={{0,96},{2,26},{8,104},{10,2},{16,112},{18,10},{24,120},{26,18},{32... | collective-permute-start | bytes 2457608 | tf_op jit(solution)/shard_map/ppermute | solution.py:34
  30.1 0.3 collective-permute-start.11
  30.4 0.7 collective-permute-start.10
  31.1 18.1 %factor_term.1 = (bf16[4,160,1280]{2,1,0:T(8,128)(2,1)}, bf16[4,160,1280]{2,1,0:T(8,128)(2,1)}, bf16[4,160,1280]{2,1,0:T(8,128)(2,1)}, bf16[4,160,1280]{2,1,0:T(8,128)(2,1)}) custom-call(s32[4]{0:T(128)} %copy-done.1, bf16[768,2560]{1,0:T(8,128)(2,1)} %b0.1, bf16[768,2560]{1,0:T(8,128)(2,1)} %collective-permute-done.ha1.hb1.b1, bf16[768,2560]{1,0:T(8,128)(2,1)} %a0.1, ...), custom_call_target="tpu_custom_call" | custom-call | flops 10066329600 | bytes 15728640 | tf_op jit(solution)/shard_map/factor_term/pallas_call | solution.py:136
  49.2 2.7 %collective-permute-done.10 = bf16[4,80,1280]{2,1,0:T(8,128)(2,1)} collective-permute-done((bf16[4,80,1280]{2,1,0:T(8,128)(2,1)S(1)}, bf16[4,80,1280]{2,1,0:T(8,128)(2,1)}, u32[]{:S(2)}, u32[]{:S(2)}) %collective-permute-start.10) | collective-permute-done | bytes 819232 | tf_op jit(solution)/shard_map/ppermute | solution.py:34
  51.9 2.0 %convert_add_fusion.1 = f32[4,80,1280]{2,1,0:T(8,128)S(1)} fusion(bf16[4,80,1280]{2,1,0:T(8,128)(2,1)S(1)} %collective-permute-done.12, bf16[4,80,1280]{2,1,0:T(8,128)(2,1)} %collective-permute-done.11, bf16[4,80,1280]{2,1,0:T(8,128)(2,1)} %collective-permute-done.10, bf16[4,80,1280]{2,1,0:T(8,128)(2,1)} %gate.2), kind=kLoop, calls=%fused_computation.3 | loop fusion | flops 2867200 | bytes 4915200 | tf_op jit(solution)/shard_map/add | solution.py:157
  54.0 3.5 %collective-permute-start.15 = (bf16[80,1280]{1,0:T(8,128)(2,1)S(1)}, bf16[80,1280]{1,0:T(8,128)(2,1)S(1)}, u32[]{:S(2)}, u32[]{:S(2)}) collective-permute-start(bf16[80,1280]{1,0:T(8,128)(2,1)S(1)} %get-tuple-element.22), channel_id=1, source_target_pairs={{0,24},{2,98},{8,0},{10,106},{16,8},{18,114},{24,16},{26,122},{32,... | collective-permute-start | bytes 614408 | tf_op jit(solution)/shard_map/ppermute | solution.py:34
  57.6 0.7 collective-permute-start.13
  58.3 4.2 %collective-permute-done.15 = bf16[80,1280]{1,0:T(8,128)(2,1)S(1)} collective-permute-done((bf16[80,1280]{1,0:T(8,128)(2,1)S(1)}, bf16[80,1280]{1,0:T(8,128)(2,1)S(1)}, u32[]{:S(2)}, u32[]{:S(2)}) %collective-permute-start.15) | collective-permute-done | bytes 204832 | tf_op jit(solution)/shard_map/ppermute | solution.py:34
  62.5 1.3 collective-permute-done.14
  63.8 2.1 %collective-permute-done.13 = bf16[80,1280]{1,0:T(8,128)(2,1)S(1)} collective-permute-done((bf16[80,1280]{1,0:T(8,128)(2,1)S(1)}, bf16[80,1280]{1,0:T(8,128)(2,1)S(1)}, u32[]{:S(2)}, u32[]{:S(2)}) %collective-permute-start.13) | collective-permute-done | bytes 204832 | tf_op jit(solution)/shard_map/ppermute | solution.py:34
  65.9 0.1 fusion.16
  66.0 2.8 %collective-permute-start.17 = (f32[40,1280]{1,0:T(8,128)S(1)}, f32[40,1280]{1,0:T(8,128)S(1)}, u32[]{:S(2)}, u32[]{:S(2)}) collective-permute-start(f32[40,1280]{1,0:T(8,128)S(1)} %get-tuple-element.35), channel_id=1, source_target_pairs={{0,1},{1,0},{2,3},{3,2},{4,5},{5,4},{6,7},{7,6},{8,9},{9,8},{10,11... | collective-permute-start | bytes 614408 | tf_op jit(solution)/shard_map/ppermute | solution.py:23
  68.8 0.9 collective-permute-start.18
  69.7 0.6 collective-permute-start.4
  70.3 0.2 collective-permute-start.3
  70.5 1.7 %collective-permute-done.17 = f32[40,1280]{1,0:T(8,128)S(1)} collective-permute-done((f32[40,1280]{1,0:T(8,128)S(1)}, f32[40,1280]{1,0:T(8,128)S(1)}, u32[]{:S(2)}, u32[]{:S(2)}) %collective-permute-start.17) | collective-permute-done | bytes 204832 | tf_op jit(solution)/shard_map/ppermute | solution.py:23
  72.2 4.2 %collective-permute-done.18 = f32[40,1280]{1,0:T(8,128)S(1)} collective-permute-done((f32[40,1280]{1,0:T(8,128)S(1)}, f32[40,1280]{1,0:T(8,128)S(1)}, u32[]{:S(2)}, u32[]{:S(2)}) %collective-permute-start.18) | collective-permute-done | bytes 204832 | tf_op jit(solution)/shard_map/ppermute | solution.py:202
  76.6 4.1 %fusion.11 = f32[80,1280]{1,0:T(8,128)S(1)} fusion(bf16[2560,1280]{1,0:T(8,128)(2,1)} %param.6, bf16[40,2560]{1,0:T(8,128)(2,1)S(1)} %get-tuple-element.33, bf16[40,2560]{1,0:T(8,128)(2,1)S(1)} %get-tuple-element.32), kind=kOutput, calls=%fused_computation.23 | convolution fusion | flops 525107200 | bytes 7372800 | tf_op jit(solution)/shard_map/dot_general | solution.py:211
  80.7 2.1 %collective-permute-start.19 = (f32[40,1280]{1,0:T(8,128)S(1)}, f32[40,1280]{1,0:T(8,128)S(1)}, u32[]{:S(2)}, u32[]{:S(2)}) collective-permute-start(f32[40,1280]{1,0:T(8,128)S(1)} %slice_add_fusion.1), channel_id=1, source_target_pairs={{0,1},{1,0},{2,3},{3,2},{4,5},{5,4},{6,7},{7,6},{8,9},{9,8},{10,11... | collective-permute-start | bytes 614408 | tf_op jit(solution)/shard_map/ppermute | solution.py:23
  82.8 4.5 %collective-permute-done.19 = f32[40,1280]{1,0:T(8,128)S(1)} collective-permute-done((f32[40,1280]{1,0:T(8,128)S(1)}, f32[40,1280]{1,0:T(8,128)S(1)}, u32[]{:S(2)}, u32[]{:S(2)}) %collective-permute-start.19) | collective-permute-done | bytes 204832 | tf_op jit(solution)/shard_map/ppermute | solution.py:23
  87.4 2.3 %reshape.32 = f32[40,32,2,40]{3,2,1,0:T(2,128)S(1)} reshape(f32[40,2560]{1,0:T(8,128)S(1)} %pad_maximum_fusion.1) | data formatting | bytes 819200 | tf_op jit(solution)/shard_map/reshape | solution.py:217
  89.7 0.8 copy.8
  90.4 1.9 %reshape.35 = f32[64,1,1600]{2,1,0:T(1,128)} reshape(f32[64,40,40]{2,1,0:T(8,128)S(1)} %bitcast.56) | data formatting | bytes 819200
  92.3 9.1 %all-to-all-start = ((f32[64,1,1600]{2,1,0:T(1,128)}), f32[64,1,1600]{2,1,0:T(1,128)}, u32[]{:S(2)}, u32[]{:S(2)}) async-start(f32[64,1,1600]{2,1,0:T(1,128)} %reshape.35), calls=%async_computation | async-start | bytes 851968 | tf_op jit(solution)/shard_map/all_to_all | solution.py:218
  101.4 11.9 %collective-permute-done.2 = bf16[4,160,1280]{2,1,0:T(8,128)(2,1)} collective-permute-done((bf16[4,160,1280]{2,1,0:T(8,128)(2,1)}, bf16[4,160,1280]{2,1,0:T(8,128)(2,1)}, u32[]{:S(2)}, u32[]{:S(2)}) %collective-permute-start.2) | collective-permute-done | bytes 1638432 | tf_op jit(solution)/shard_map/ppermute | solution.py:34
  113.4 3.7 %convert_add_fusion = f32[4,160,1280]{2,1,0:T(8,128)S(1)} fusion(bf16[4,160,1280]{2,1,0:T(8,128)(2,1)} %collective-permute-done.4, bf16[4,160,1280]{2,1,0:T(8,128)(2,1)} %collective-permute-done.3, bf16[4,160,1280]{2,1,0:T(8,128)(2,1)} %collective-permute-done.2, bf16[4,160,1280]{2,1,0:T(8,128)(2,1)} %get-tuple-element.10.refs_1_), kind=kLoop, calls=%fused_computation | loop fusion | flops 5734400 | bytes 9830400 | tf_op jit(solution)/shard_map/add | solution.py:157
  117.0 1.1 fusion.8
  118.1 0.6 collective-permute-start.7
  118.7 0.8 collective-permute-start.5
  119.6 0.5 broadcast
  120.1 3.4 %reduce = f32[64,1600]{1,0:T(8,128)} reduce(f32[64,1,1600]{2,1,0:T(1,128)} %all-to-all-done, f32[]{:T(128)} %broadcast), dimensions={1}, to_apply=%all_to_all.3.reduce_sub_computation | reduce | bytes 819204 | tf_op jit(solution)/shard_map/all_to_all | solution.py:218
  123.5 2.6 %reshape.36.refs_0_ = f32[64,40,40]{2,1,0:T(8,128)} reshape(f32[64,1600]{1,0:T(8,128)} %reduce) | data formatting | bytes 819200
  126.2 1.5 %reduce-precision_convert_fusion = (bf16[2560,40]{1,0:T(8,128)(2,1)S(1)}, bf16[2560,40]{1,0:T(8,128)(2,1)S(1)}) fusion(f32[64,40,40]{2,1,0:T(8,128)} %gate.3), kind=kLoop, calls=%fused_computation.2 | loop fusion | flops 409600 | bytes 819200 | tf_op jit(solution)/shard_map/convert_element_type | solution.py:43
  127.7 4.3 %collective-permute-done.5 = bf16[160,1280]{1,0:T(8,128)(2,1)} collective-permute-done((bf16[160,1280]{1,0:T(8,128)(2,1)}, bf16[160,1280]{1,0:T(8,128)(2,1)}, u32[]{:S(2)}, u32[]{:S(2)}) %collective-permute-start.5) | collective-permute-done | bytes 409632 | tf_op jit(solution)/shard_map/ppermute | solution.py:34
  132.0 1.4 fusion.2
  133.5 1.5 %collective-permute-start.8 = (bf16[80,1280]{1,0:T(8,128)(2,1)S(1)}, bf16[80,1280]{1,0:T(8,128)(2,1)S(1)}, u32[]{:S(2)}, u32[]{:S(2)}) collective-permute-start(bf16[80,1280]{1,0:T(8,128)(2,1)S(1)} %fusion.18), channel_id=1, source_target_pairs={{0,4},{4,0},{1,5},{5,1},{2,6},{6,2},{3,7},{7,3},{8,12},{12,8},{9,1... | collective-permute-start | bytes 614408 | tf_op jit(solution)/shard_map/ppermute | solution.py:23
  135.0 4.0 %fusion.3 = f32[80,1280]{1,0:T(8,128)S(1)} fusion(bf16[2560,1280]{1,0:T(8,128)(2,1)} %param.7, bf16[2560,40]{1,0:T(8,128)(2,1)S(1)} %get-tuple-element.25, bf16[2560,40]{1,0:T(8,128)(2,1)S(1)} %get-tuple-element.24), kind=kOutput, calls=%fused_computation.11 | convolution fusion | flops 525107200 | bytes 7372800 | tf_op jit(solution)/shard_map/dot_general | solution.py:16
  139.2 7.0 %collective-permute-start.9 = (f32[40,1280]{1,0:T(8,128)S(1)}, f32[40,1280]{1,0:T(8,128)S(1)}, u32[]{:S(2)}, u32[]{:S(2)}) collective-permute-start(f32[40,1280]{1,0:T(8,128)S(1)} %dynamic-slice_bitcast_fusion.2), channel_id=1, source_target_pairs={{0,2},{2,0},{1,3},{3,1},{4,6},{6,4},{5,7},{7,5},{8,10},{10,8},{9,1... | collective-permute-start | bytes 614408 | tf_op jit(solution)/shard_map/ppermute | solution.py:23
  146.1 0.7 slice_add_fusion
  146.8 0.4 collective-permute-done.9
  147.3 0.8 maximum_bitcast_fusion
  (30 shorter events, 0.6 us)
Async XLA Ops:
  0.6 8.3 %collective-permute-start = (bf16[768,2560]{1,0:T(8,128)(2,1)}, bf16[768,2560]{1,0:T(8,128)(2,1)}, u32[]{:S(2)}, u32[]{:S(2)}) collective-permute-start(bf16[768,2560]{1,0:T(8,128)(2,1)} %b0.1), channel_id=1, source_target_pairs={{0,2},{2,0},{1,3},{3,1},{4,6},{6,4},{5,7},{7,5},{8,10},{10,8},{9,1... | collective-permute-start | bytes 11796488 | tf_op jit(solution)/shard_map/ppermute | solution.py:23
  2.1 12.4 %collective-permute-start.1 = (bf16[768,2560]{1,0:T(8,128)(2,1)}, bf16[768,2560]{1,0:T(8,128)(2,1)}, u32[]{:S(2)}, u32[]{:S(2)}) collective-permute-start(bf16[768,2560]{1,0:T(8,128)(2,1)} %a0.1), channel_id=1, source_target_pairs={{0,2},{2,0},{1,3},{3,1},{4,6},{6,4},{5,7},{7,5},{8,10},{10,8},{9,1... | collective-permute-start | bytes 11796488 | tf_op jit(solution)/shard_map/ppermute | solution.py:23
  2.3 24.0 %copy-start.1 = (s32[4]{0:T(128)}, s32[4]{0:T(128)S(1)}, u32[]{:S(2)}) copy-start(s32[4]{0:T(128)S(1)} %pad_add_fusion.place) | copy-start | bytes 52
  26.3 0.9 copy-start
  27.2 22.0 %collective-permute-start.12 = (bf16[4,80,1280]{2,1,0:T(8,128)(2,1)S(1)}, bf16[4,80,1280]{2,1,0:T(8,128)(2,1)S(1)}, u32[]{:S(2)}, u32[]{:S(2)}) collective-permute-start(bf16[4,80,1280]{2,1,0:T(8,128)(2,1)S(1)} %get-tuple-element.17), channel_id=1, source_target_pairs={{0,96},{2,26},{8,104},{10,2},{16,112},{18,10},{24,120},{26,18},{32... | collective-permute-start | bytes 2457608 | tf_op jit(solution)/shard_map/ppermute | solution.py:34
  30.1 19.2 %collective-permute-start.11 = (bf16[4,80,1280]{2,1,0:T(8,128)(2,1)S(1)}, bf16[4,80,1280]{2,1,0:T(8,128)(2,1)}, u32[]{:S(2)}, u32[]{:S(2)}) collective-permute-start(bf16[4,80,1280]{2,1,0:T(8,128)(2,1)S(1)} %get-tuple-element.16), channel_id=1, source_target_pairs={{0,64},{2,18},{8,72},{10,26},{16,80},{18,2},{24,88},{26,10},{32,96... | collective-permute-start | bytes 2457608 | tf_op jit(solution)/shard_map/ppermute | solution.py:34
  30.4 21.5 %collective-permute-start.10 = (bf16[4,80,1280]{2,1,0:T(8,128)(2,1)S(1)}, bf16[4,80,1280]{2,1,0:T(8,128)(2,1)}, u32[]{:S(2)}, u32[]{:S(2)}) collective-permute-start(bf16[4,80,1280]{2,1,0:T(8,128)(2,1)S(1)} %get-tuple-element.15), channel_id=1, source_target_pairs={{0,32},{2,10},{8,40},{10,18},{16,48},{18,26},{24,56},{26,2},{32,64... | collective-permute-start | bytes 2457608 | tf_op jit(solution)/shard_map/ppermute | solution.py:34
  54.0 8.4 %collective-permute-start.15 = (bf16[80,1280]{1,0:T(8,128)(2,1)S(1)}, bf16[80,1280]{1,0:T(8,128)(2,1)S(1)}, u32[]{:S(2)}, u32[]{:S(2)}) collective-permute-start(bf16[80,1280]{1,0:T(8,128)(2,1)S(1)} %get-tuple-element.22), channel_id=1, source_target_pairs={{0,24},{2,98},{8,0},{10,106},{16,8},{18,114},{24,16},{26,122},{32,... | collective-permute-start | bytes 614408 | tf_op jit(solution)/shard_map/ppermute | solution.py:34
  57.6 6.2 %collective-permute-start.14 = (bf16[80,1280]{1,0:T(8,128)(2,1)S(1)}, bf16[80,1280]{1,0:T(8,128)(2,1)S(1)}, u32[]{:S(2)}, u32[]{:S(2)}) collective-permute-start(bf16[80,1280]{1,0:T(8,128)(2,1)S(1)} %get-tuple-element.23), channel_id=1, source_target_pairs={{0,16},{2,66},{8,24},{10,74},{16,0},{18,82},{24,8},{26,90},{32,48}... | collective-permute-start | bytes 614408 | tf_op jit(solution)/shard_map/ppermute | solution.py:34
  57.6 8.3 %collective-permute-start.13 = (bf16[80,1280]{1,0:T(8,128)(2,1)S(1)}, bf16[80,1280]{1,0:T(8,128)(2,1)S(1)}, u32[]{:S(2)}, u32[]{:S(2)}) collective-permute-start(bf16[80,1280]{1,0:T(8,128)(2,1)S(1)} %get-tuple-element.21), channel_id=1, source_target_pairs={{0,8},{2,34},{8,16},{10,42},{16,24},{18,50},{24,0},{26,58},{32,40}... | collective-permute-start | bytes 614408 | tf_op jit(solution)/shard_map/ppermute | solution.py:34
  66.0 6.2 %collective-permute-start.17 = (f32[40,1280]{1,0:T(8,128)S(1)}, f32[40,1280]{1,0:T(8,128)S(1)}, u32[]{:S(2)}, u32[]{:S(2)}) collective-permute-start(f32[40,1280]{1,0:T(8,128)S(1)} %get-tuple-element.35), channel_id=1, source_target_pairs={{0,1},{1,0},{2,3},{3,2},{4,5},{5,4},{6,7},{7,6},{8,9},{9,8},{10,11... | collective-permute-start | bytes 614408 | tf_op jit(solution)/shard_map/ppermute | solution.py:23
  68.8 7.6 %collective-permute-start.18 = (f32[40,1280]{1,0:T(8,128)S(1)}, f32[40,1280]{1,0:T(8,128)S(1)}, u32[]{:S(2)}, u32[]{:S(2)}) collective-permute-start(f32[40,1280]{1,0:T(8,128)S(1)} %get-tuple-element.34), channel_id=1, source_target_pairs={{0,5},{1,4},{4,1},{5,0},{2,7},{3,6},{6,3},{7,2},{8,13},{9,12},{12,... | collective-permute-start | bytes 614408 | tf_op jit(solution)/shard_map/ppermute | solution.py:202
  69.7 6.7 %collective-permute-start.16 = (f32[40,1280]{1,0:T(8,128)S(1)}, f32[40,1280]{1,0:T(8,128)S(1)}, u32[]{:S(2)}, u32[]{:S(2)}) collective-permute-start(f32[40,1280]{1,0:T(8,128)S(1)} %get-tuple-element.34), channel_id=1, source_target_pairs={{0,4},{4,0},{1,5},{5,1},{2,6},{6,2},{3,7},{7,3},{8,12},{12,8},{9,1... | collective-permute-start | bytes 614408 | tf_op jit(solution)/shard_map/ppermute | solution.py:23
  69.7 31.7 %collective-permute-start.4 = (bf16[4,160,1280]{2,1,0:T(8,128)(2,1)}, bf16[4,160,1280]{2,1,0:T(8,128)(2,1)}, u32[]{:S(2)}, u32[]{:S(2)}) collective-permute-start(bf16[4,160,1280]{2,1,0:T(8,128)(2,1)} %get-tuple-element.13), channel_id=1, source_target_pairs={{0,96},{2,26},{8,104},{10,2},{16,112},{18,10},{24,120},{26,18},{32... | collective-permute-start | bytes 4915208 | tf_op jit(solution)/shard_map/ppermute | solution.py:34
  70.3 31.1 %collective-permute-start.3 = (bf16[4,160,1280]{2,1,0:T(8,128)(2,1)}, bf16[4,160,1280]{2,1,0:T(8,128)(2,1)}, u32[]{:S(2)}, u32[]{:S(2)}) collective-permute-start(bf16[4,160,1280]{2,1,0:T(8,128)(2,1)} %get-tuple-element.12), channel_id=1, source_target_pairs={{0,64},{2,18},{8,72},{10,26},{16,80},{18,2},{24,88},{26,10},{32,96... | collective-permute-start | bytes 4915208 | tf_op jit(solution)/shard_map/ppermute | solution.py:34
  72.2 41.2 %collective-permute-start.2 = (bf16[4,160,1280]{2,1,0:T(8,128)(2,1)}, bf16[4,160,1280]{2,1,0:T(8,128)(2,1)}, u32[]{:S(2)}, u32[]{:S(2)}) collective-permute-start(bf16[4,160,1280]{2,1,0:T(8,128)(2,1)} %get-tuple-element.11), channel_id=1, source_target_pairs={{0,32},{2,10},{8,40},{10,18},{16,48},{18,26},{24,56},{26,2},{32,64... | collective-permute-start | bytes 4915208 | tf_op jit(solution)/shard_map/ppermute | solution.py:34
  80.7 6.6 %collective-permute-start.19 = (f32[40,1280]{1,0:T(8,128)S(1)}, f32[40,1280]{1,0:T(8,128)S(1)}, u32[]{:S(2)}, u32[]{:S(2)}) collective-permute-start(f32[40,1280]{1,0:T(8,128)S(1)} %slice_add_fusion.1), channel_id=1, source_target_pairs={{0,1},{1,0},{2,3},{3,2},{4,5},{5,4},{6,7},{7,6},{8,9},{9,8},{10,11... | collective-permute-start | bytes 614408 | tf_op jit(solution)/shard_map/ppermute | solution.py:23
  92.3 27.3 %all-to-all-start = ((f32[64,1,1600]{2,1,0:T(1,128)}), f32[64,1,1600]{2,1,0:T(1,128)}, u32[]{:S(2)}, u32[]{:S(2)}) async-start(f32[64,1,1600]{2,1,0:T(1,128)} %reshape.35), calls=%async_computation | async-start | bytes 851968 | tf_op jit(solution)/shard_map/all_to_all | solution.py:218
  118.1 9.6 %collective-permute-start.7 = (bf16[160,1280]{1,0:T(8,128)(2,1)}, bf16[160,1280]{1,0:T(8,128)(2,1)}, u32[]{:S(2)}, u32[]{:S(2)}) collective-permute-start(bf16[160,1280]{1,0:T(8,128)(2,1)} %get-tuple-element.19), channel_id=1, source_target_pairs={{0,24},{2,98},{8,0},{10,106},{16,8},{18,114},{24,16},{26,122},{32,... | collective-permute-start | bytes 1228808 | tf_op jit(solution)/shard_map/ppermute | solution.py:34
  118.7 9.0 %collective-permute-start.6 = (bf16[160,1280]{1,0:T(8,128)(2,1)}, bf16[160,1280]{1,0:T(8,128)(2,1)}, u32[]{:S(2)}, u32[]{:S(2)}) collective-permute-start(bf16[160,1280]{1,0:T(8,128)(2,1)} %get-tuple-element.20), channel_id=1, source_target_pairs={{0,16},{2,66},{8,24},{10,74},{16,0},{18,82},{24,8},{26,90},{32,48}... | collective-permute-start | bytes 1228808 | tf_op jit(solution)/shard_map/ppermute | solution.py:34
  118.7 13.3 %collective-permute-start.5 = (bf16[160,1280]{1,0:T(8,128)(2,1)}, bf16[160,1280]{1,0:T(8,128)(2,1)}, u32[]{:S(2)}, u32[]{:S(2)}) collective-permute-start(bf16[160,1280]{1,0:T(8,128)(2,1)} %get-tuple-element.18.refs_1_), channel_id=1, source_target_pairs={{0,8},{2,34},{8,16},{10,42},{16,24},{18,50},{24,0},{26,58},{32,40}... | collective-permute-start | bytes 1228808 | tf_op jit(solution)/shard_map/ppermute | solution.py:34
  133.5 5.6 %collective-permute-start.8 = (bf16[80,1280]{1,0:T(8,128)(2,1)S(1)}, bf16[80,1280]{1,0:T(8,128)(2,1)S(1)}, u32[]{:S(2)}, u32[]{:S(2)}) collective-permute-start(bf16[80,1280]{1,0:T(8,128)(2,1)S(1)} %fusion.18), channel_id=1, source_target_pairs={{0,4},{4,0},{1,5},{5,1},{2,6},{6,2},{3,7},{7,3},{8,12},{12,8},{9,1... | collective-permute-start | bytes 614408 | tf_op jit(solution)/shard_map/ppermute | solution.py:23
  139.2 8.1 %collective-permute-start.9 = (f32[40,1280]{1,0:T(8,128)S(1)}, f32[40,1280]{1,0:T(8,128)S(1)}, u32[]{:S(2)}, u32[]{:S(2)}) collective-permute-start(f32[40,1280]{1,0:T(8,128)S(1)} %dynamic-slice_bitcast_fusion.2), channel_id=1, source_target_pairs={{0,2},{2,0},{1,3},{3,1},{4,6},{6,4},{5,7},{7,5},{8,10},{10,8},{9,1... | collective-permute-start | bytes 614408 | tf_op jit(solution)/shard_map/ppermute | solution.py:23

commit v3 on v2

--- a/solution.py
+++ b/solution.py
@@ -27,10 +27,11 @@
     pairs = []
     for z in range(4):
         for y in range(4):
-            for c in range(2):
-                along_z = (c == 0) == (stage == 0)
-                there = ((z + step) % 4, y) if along_z else (z, (y + step) % 4)
-                pairs.append(((z * 4 + y) * 2 + c, (there[0] * 4 + there[1]) * 2 + c))
+            for h in range(2):
+                along_z = (h == 0) == (stage == 0)
+                z2, y2 = ((z + step) % 4, y) if along_z else (z, (y + step) % 4)
+                core, core2 = h ^ ((z + y) & 1), h ^ ((z2 + y2) & 1)
+                pairs.append(((z * 4 + y) * 2 + core, (z2 * 4 + y2) * 2 + core2))
     return lax.ppermute(x, ("z", "y", "c"), pairs)
 
 
@@ -44,15 +45,15 @@
 
 
 def place_blocks(place, buffer, sems, outs, m, n, zs, finish):
-    core, z_me, y_me = place[1], place[2], place[3]
+    part_me, z_me, y_me = place[1], place[2], place[3]
     rows = TILE // (zs * 4)
     wide = buffer.shape[2] // sems.shape[1]
     lanes = pl.ds(pl.multiple_of(n * wide, wide), wide)
     for a in range(zs):
         for k in range(4):
             z = m * zs + a
-            ahead = jnp.where(core == 0, z - z_me + 4, k - y_me + 4) & 3
-            slot = jnp.where(core == 0, k, z)
+            ahead = jnp.where(part_me == 0, z - z_me + 4, k - y_me + 4) & 3
+            slot = jnp.where(part_me == 0, k, z)
             part = a * 4 + k
             block = buffer.at[m, pl.ds(part * rows, rows), lanes]
 
@@ -77,9 +78,13 @@
                 place_blocks(place, buffer, sems, outs, i, j, zs, True)
 
 
-def cross_kernel(place, a0, a1, b0, b1, own, ahead1, ahead2, ahead3, buffer, sems):
+def own_kernel(place, a, b, out):
+    out[...] = contract(a[...], b[...])
+
+
+def cross_kernel(place, a, b, partial, own, ahead1, ahead2, ahead3, buffer, sems):
     m, n = pl.program_id(0), pl.program_id(1)
-    tile = (contract(a0[...], b0[...]) + contract(a1[...], b1[...])).astype(BF)
+    tile = (partial[...] + contract(a[...], b[...])).astype(BF)
     for lane in range(2):
 
         @pl.when(n == lane)
@@ -94,6 +99,21 @@
     half = width // 2
     left = pl.BlockSpec((tokens, TILE), lambda m, n, p: (0, p[1] * 2 + m))
     right = pl.BlockSpec((tokens, TILE), lambda m, n, p: (0, (p[1] ^ p[0]) * 2 + n))
+    middle = pl.BlockSpec((TILE, TILE), lambda m, n, p: (m, n))
+    params = pltpu.CompilerParams(vmem_limit_bytes=48 * 2**20)
+    cost = pl.CostEstimate(
+        flops=2 * tokens * half * half, bytes_accessed=10 * tokens * half, transcendentals=0
+    )
+    partial = pl.pallas_call(
+        own_kernel,
+        out_shape=jax.ShapeDtypeStruct((half, half), F32),
+        grid_spec=pltpu.PrefetchScalarGridSpec(
+            num_scalar_prefetch=1, grid=(2, 2), in_specs=[left, right], out_specs=middle
+        ),
+        compiler_params=params,
+        cost_estimate=cost,
+        name="cross_own",
+    )(place, grads, acts)
     out = jax.ShapeDtypeStruct((4, half // 16, half), BF)
     return pl.pallas_call(
         cross_kernel,
@@ -101,16 +121,14 @@
         grid_spec=pltpu.PrefetchScalarGridSpec(
             num_scalar_prefetch=1,
             grid=(2, 2),
-            in_specs=[left, left, right, right],
+            in_specs=[left, right, middle],
             out_specs=[pl.BlockSpec(memory_space=pl.ANY)] * 4,
             scratch_shapes=[pltpu.VMEM((2, TILE, half), BF), pltpu.SemaphoreType.DMA((2, 2, 8))],
         ),
-        compiler_params=pltpu.CompilerParams(vmem_limit_bytes=48 * 2**20),
-        cost_estimate=pl.CostEstimate(
-            flops=4 * tokens * half * half, bytes_accessed=10 * tokens * half, transcendentals=0
-        ),
+        compiler_params=params,
+        cost_estimate=cost,
         name="cross_term",
-    )(place, grads, grads_next, acts, acts_next)
+    )(place, grads_next, acts_next, partial)
 
 
 def factor_kernel(
@@ -170,9 +188,37 @@
     )(x, *others)
 
 
-def send_second(x, me):
-    pieces = [pick(x, 0, (me + step) & 3).astype(BF) for step in (1, 2, 3)]
-    return pieces, [turn(piece, step, 1) for step, piece in zip((1, 2, 3), pieces)]
+def fold_kernel(me, a0, a1, a2, a3, own, ahead1, ahead2, ahead3):
+    step = pl.program_id(0)
+    total = add(a0[0], a1[0], a2[0], a3[0])
+
+    @pl.when(step == 0)
+    def _():
+        own[...] = total
+
+    for r, out in enumerate((ahead1, ahead2, ahead3)):
+
+        @pl.when(step == r + 1)
+        def _():
+            out[...] = total.astype(BF)
+
+
+def fold(me, parts):
+    _, rows, width = parts[0].shape
+    block = pl.BlockSpec((1, rows, width), lambda s, m: ((m[0] + s) & 3, 0, 0))
+    whole = pl.BlockSpec((rows, width), lambda s, m: (0, 0))
+    return pl.pallas_call(
+        fold_kernel,
+        out_shape=[jax.ShapeDtypeStruct((rows, width), t) for t in (F32, BF, BF, BF)],
+        grid_spec=pltpu.PrefetchScalarGridSpec(
+            num_scalar_prefetch=1, grid=(4,), in_specs=[block] * 4, out_specs=[whole] * 4
+        ),
+        compiler_params=pltpu.CompilerParams(vmem_limit_bytes=32 * 2**20),
+        cost_estimate=pl.CostEstimate(
+            flops=16 * rows * width, bytes_accessed=42 * rows * width, transcendentals=0
+        ),
+        name="fold",
+    )(me, *parts)
 
 
 def per_device(hidden, out_grad, left_inverse, right_inverse):
@@ -181,8 +227,9 @@
     half = width // 2
     token_total = tokens * 64
     first = o == 0
-    place = jnp.stack([o, c, z, y]).astype(jnp.int32)
-    second_me = jnp.where(c == 0, y, z)
+    h = c ^ ((z + y) & 1)
+    place = jnp.stack([o, h, z, y]).astype(jnp.int32)
+    second_me = jnp.where(h == 0, y, z).astype(jnp.int32)[None]
 
     grads_next = shift(out_grad, "c", 1)
     acts_next = shift(hidden, "c", 1)
@@ -191,18 +238,18 @@
     m_parts = [own, turn(m1, 1, 0), turn(m2, 2, 0), turn(m3, 3, 0)]
 
     own, f1, f2, f3 = factor_term(place, hidden, acts_next, out_grad, grads_next)
+    f_parts = [own, turn(f1, 1, 0), turn(f2, 2, 0), turn(f3, 3, 0)]
 
     m_parts[0] = gate(m_parts[0], own)
-    m = add(*m_parts)
-    _, received = send_second(m, second_me)
-    f_parts = [own, turn(f1, 1, 0), turn(f2, 2, 0), turn(f3, 3, 0)]
-    m = add(pick(m, 0, second_me), *received).reshape(2, half // 32, half)
+    m, *pieces = fold(second_me, m_parts)
+    m = add(m, *[turn(piece, s, 1) for s, piece in enumerate(pieces, 1)])
+    m = m.reshape(2, half // 32, half)
     mine, theirs = pick(m, 0, xl), pick(m, 0, 1 - xl)
     m_own = mine + shift(theirs, "xl", 1)
     partner = shift(mine, "o", 1) + lax.ppermute(
         theirs, ("xl", "o"), [(i, 3 - i) for i in range(4)]
     )
-    swap = (c ^ o) == 0
+    swap = (h ^ o) == 0
     mrow = jnp.concatenate(
         [jnp.where(swap, m_own, partner), jnp.where(swap, partner, m_own)], axis=1
     )
@@ -214,24 +261,28 @@
     pt = jnp.concatenate(
         [jnp.where(first, pt, pt_other), jnp.where(first, pt_other, pt)], axis=1
     )
-    blocks = pt.reshape(rows, 32, 2, rows).transpose(2, 1, 0, 3).reshape(64, rows, rows)
+    blocks = pt.reshape(rows, 32, 2, rows).transpose(2, 1, 0, 3).reshape(64, rows * rows)
+
+    f, *pieces = fold(second_me, f_parts)
+    f = add(f, *[turn(piece, s, 1) for s, piece in enumerate(pieces, 1)])
+
+    blocks = gate(blocks, pieces[0])
     blocks = lax.all_to_all(blocks, ("c", "z", "y", "xl"), 0, 0, tiled=True)
-
-    f = add(*f_parts)
-    pieces, received = send_second(f, second_me)
-    blocks = gate(blocks, pieces[0]).reshape(width, rows)
+    blocks = blocks.reshape(2, 4, 4, 2, rows, rows)
+    odd = ((jnp.arange(4)[:, None] + jnp.arange(4)) & 1).reshape(1, 4, 4, 1, 1, 1) == 1
+    blocks = jnp.where(odd, blocks[::-1], blocks).reshape(width, rows)
     stacked = jnp.concatenate(split_pair(blocks), axis=1)
     update = contract(stacked, right_inverse)
     update = update[:rows] + update[rows:]
 
-    f = add(pick(f, 0, second_me), *received).reshape(2, width // 32, half)
+    f = f.reshape(2, width // 32, half)
     f = pick(f, 0, xl) + shift(pick(f, 0, 1 - xl).astype(BF), "xl", 1).astype(F32)
     f = f * jnp.where(first, 1.0 / token_total, 1.0).astype(F32)
     f = f.reshape(2, width // 64, half)
     mine = pick(f, 0, c)
     theirs = shift(pick(f, 0, 1 - c), "c", 1)
     factors = jnp.concatenate(
-        [jnp.where(c == 0, mine, theirs), jnp.where(c == 0, theirs, mine)], axis=1
+        [jnp.where(h == 0, mine, theirs), jnp.where(h == 0, theirs, mine)], axis=1
     )[None]
     return factors, update
 

time: 149 us -> 152 us (1.020)
  Pallas kernels: 29.9 us -> 39.9 us
  waiting for transfers between devices: 49.5 us -> 39.7 us
  other arithmetic: 14 us -> 4.63 us
  local copies, waits for them, and re-layouts: 10.3 us -> 19.5 us
  starting transfers between devices: 35.4 us -> 38.6 us
    ppermute x12, starting transfers between devices: 10.4 us -> 23.6 us  [turn(): return lax.ppermute(x, ('z', 'y', 'c'), pairs)]
    pallas_call x0 -> x3, Pallas kernels: none -> 12.3 us  [the longest x1 8.04 us: cross_term(): pl.pallas_call(own_kernel, out_shape=jax.ShapeDtypeStruct((half, half), F...]
    ppermute x12, waiting for transfers between devices: 26.6 us -> 18.8 us  [turn(): return lax.ppermute(x, ('z', 'y', 'c'), pairs)]
    ppermute x7, starting transfers between devices: 15.1 us -> 7.41 us  [shift(): return lax.ppermute(x, axis, [(i, (i + step) % size) for i in range(size)])]
    reshape x2 -> x4, local copies, waits for them, and re-layouts: 3.06 us -> 9.69 us  [the longest x3 9.16 us: per_device(): pt.reshape(rows, 32, 2, rows).transpose(2, 1, 0, 3).reshape(64, rows * rows)]
    add x4 -> x2, other arithmetic: 7.16 us -> 1.4 us  [add(): total = total + x.astype(F32)]
    ppermute x7, waiting for transfers between devices: 18.7 us -> 13.4 us  [shift(): return lax.ppermute(x, axis, [(i, (i + step) % size) for i in range(size)])]
    all_to_all x1, waiting for transfers between devices: 0.01 us -> 5.27 us  [per_device(): blocks = lax.all_to_all(blocks, ('c', 'z', 'y', 'xl'), 0, 0, tiled=True)]
  transfers between devices with their start and end apart: 21 -> 21, of which waited for: 12 -> 14; matrix products, arithmetic and copies ran while one was open for 18% -> 13% of each run, Pallas kernels for 12% -> 17%
where the time goes in v3:
time: 152 us; the launch traced here: 151 us
  Pallas kernels  39.9 us (26%)
  waiting for transfers between devices  39.7 us (26%)
  starting transfers between devices  38.6 us (25%)
  local copies, waits for them, and re-layouts  19.5 us (13%)
  matrix products  8.13 us (5%)
  other arithmetic  4.63 us (3%)
    ppermute x12, starting transfers between devices, turn(): return lax.ppermute(x, ('z', 'y', 'c'), pairs)  23.6 us
    ppermute x12, waiting for transfers between devices, turn(): return lax.ppermute(x, ('z', 'y', 'c'), pairs)  18.8 us
    pallas_call x1, Pallas kernels, factor_term(): pl.pallas_call(factor_kernel, out_shape=[out] * 4, grid_spec=pltpu.Prefet...  18.1 us
    ppermute x7, waiting for transfers between devices, shift(): return lax.ppermute(x, axis, [(i, (i + step) % size) for i in range(size)])  13.4 us
    pallas_call x1, Pallas kernels, cross_term(): pl.pallas_call(cross_kernel, out_shape=[out] * 4, grid_spec=pltpu.Prefetc...  9.47 us
    reshape x3, local copies, waits for them, and re-layouts, per_device(): pt.reshape(rows, 32, 2, rows).transpose(2, 1, 0, 3).reshape(64, rows * rows)  9.16 us
    pallas_call x1, Pallas kernels, cross_term(): pl.pallas_call(own_kernel, out_shape=jax.ShapeDtypeStruct((half, half), F...  8.04 us
    ppermute x7, starting transfers between devices, shift(): return lax.ppermute(x, axis, [(i, (i + step) % size) for i in range(size)])  7.41 us
  transfers between devices with their start and end apart: 21, of which 14 were waited for; matrix products, arithmetic and copies ran while one was open for 13% of the time, Pallas kernels for 17%

profile of v3, /device:TPU:1, one launch (start us, length us, event | category | flops | bytes accessed | tf_op | source)
XLA Modules:
  0.0 151.4 jit_solution(5025731334784710942)
XLA Ops:
  0.6 1.5 collective-permute-start
  2.3 2.1 %copy-done.1 = bf16[768,2560]{1,0:T(8,128)(2,1)S(1)} copy-done((bf16[768,2560]{1,0:T(8,128)(2,1)S(1)}, bf16[768,2560]{1,0:T(8,128)(2,1)}, u32[]{:S(2)}) %copy-start.1) | copy-done | bytes 3932184
  4.4 8.0 %cross_own.1.partial = f32[1280,1280]{1,0:T(8,128)} custom-call(s32[4]{0:T(128)S(1)} %pad_add_fusion.place, bf16[768,2560]{1,0:T(8,128)(2,1)S(1)} %copy-done.1, bf16[768,2560]{1,0:T(8,128)(2,1)} %b.1), custom_call_target="tpu_custom_call" | custom-call | flops 2516582400 | bytes 9830400 | tf_op jit(solution)/shard_map/cross_own/pallas_call | solution.py:107
  12.5 2.0 %collective-permute-done.1.ga1.gb1.a = bf16[768,2560]{1,0:T(8,128)(2,1)} collective-permute-done((bf16[768,2560]{1,0:T(8,128)(2,1)}, bf16[768,2560]{1,0:T(8,128)(2,1)}, u32[]{:S(2)}, u32[]{:S(2)}) %collective-permute-start.1) | collective-permute-done | bytes 3932192 | tf_op jit(solution)/shard_map/ppermute | solution.py:23
  14.5 9.5 %cross_term.1 = (bf16[4,80,1280]{2,1,0:T(8,128)(2,1)S(1)}, bf16[4,80,1280]{2,1,0:T(8,128)(2,1)}, bf16[4,80,1280]{2,1,0:T(8,128)(2,1)}, bf16[4,80,1280]{2,1,0:T(8,128)(2,1)S(1)}) custom-call(s32[4]{0:T(128)S(1)} %pad_add_fusion.place, bf16[768,2560]{1,0:T(8,128)(2,1)} %collective-permute-done.1.ga1.gb1.a, bf16[768,2560]{1,0:T(8,128)(2,1)} %collective-permute-done.ha1.hb1.b, ...), custom_call_target="tpu_custom_call" | custom-call | flops 2516582400 | bytes 9830400 | tf_op jit(solution)/shard_map/cross_term/pallas_call | solution.py:118
  24.0 0.9 copy-done.2
  24.9 1.7 %collective-permute-start.10 = (bf16[4,80,1280]{2,1,0:T(8,128)(2,1)}, bf16[4,80,1280]{2,1,0:T(8,128)(2,1)S(1)}, u32[]{:S(2)}, u32[]{:S(2)}) collective-permute-start(bf16[4,80,1280]{2,1,0:T(8,128)(2,1)} %get-tuple-element.27), channel_id=1, source_target_pairs={{0,34},{2,8},{10,40},{8,18},{16,50},{18,24},{26,56},{24,2},{34,64}... | collective-permute-start | bytes 2457608 | tf_op jit(solution)/shard_map/ppermute | solution.py:35
  26.6 2.5 %collective-permute-start.11 = (bf16[4,80,1280]{2,1,0:T(8,128)(2,1)}, bf16[4,80,1280]{2,1,0:T(8,128)(2,1)S(1)}, u32[]{:S(2)}, u32[]{:S(2)}) collective-permute-start(bf16[4,80,1280]{2,1,0:T(8,128)(2,1)} %get-tuple-element.28), channel_id=1, source_target_pairs={{0,64},{2,18},{10,74},{8,24},{16,80},{18,2},{26,90},{24,8},{34,98}... | collective-permute-start | bytes 2457608 | tf_op jit(solution)/shard_map/ppermute | solution.py:35
  29.1 1.4 collective-permute-start.12
  30.5 18.1 %factor_term.1 = (bf16[4,160,1280]{2,1,0:T(8,128)(2,1)}, bf16[4,160,1280]{2,1,0:T(8,128)(2,1)}, bf16[4,160,1280]{2,1,0:T(8,128)(2,1)}, bf16[4,160,1280]{2,1,0:T(8,128)(2,1)}) custom-call(s32[4]{0:T(128)} %copy-done.8, bf16[768,2560]{1,0:T(8,128)(2,1)} %b.1, bf16[768,2560]{1,0:T(8,128)(2,1)} %collective-permute-done.ha1.hb1.b, bf16[768,2560]{1,0:T(8,128)(2,1)} %a.1, ...), custom_call_target="tpu_custom_call" | custom-call | flops 10066329600 | bytes 15728640 | tf_op jit(solution)/shard_map/factor_term/pallas_call | solution.py:154
  48.7 1.1 copy-done.3
  49.8 0.8 fold.3
  50.6 1.7 %collective-permute-start.13 = (bf16[80,1280]{1,0:T(8,128)(2,1)S(1)}, bf16[80,1280]{1,0:T(8,128)(2,1)S(1)}, u32[]{:S(2)}, u32[]{:S(2)}) collective-permute-start(bf16[80,1280]{1,0:T(8,128)(2,1)S(1)} %get-tuple-element.31), channel_id=1, source_target_pairs={{0,10},{2,32},{10,16},{8,42},{16,26},{18,48},{26,0},{24,58},{34,40... | collective-permute-start | bytes 614408 | tf_op jit(solution)/shard_map/ppermute | solution.py:35
  52.3 3.3 %collective-permute-start.14 = (bf16[80,1280]{1,0:T(8,128)(2,1)S(1)}, bf16[80,1280]{1,0:T(8,128)(2,1)S(1)}, u32[]{:S(2)}, u32[]{:S(2)}) collective-permute-start(bf16[80,1280]{1,0:T(8,128)(2,1)S(1)} %get-tuple-element.32), channel_id=1, source_target_pairs={{0,16},{2,66},{10,26},{8,72},{16,0},{18,82},{26,10},{24,88},{34,50... | collective-permute-start | bytes 614408 | tf_op jit(solution)/shard_map/ppermute | solution.py:35
  55.6 1.3 collective-permute-start.15
  56.9 1.0 collective-permute-done.13
  57.9 3.4 %collective-permute-done.14 = bf16[80,1280]{1,0:T(8,128)(2,1)S(1)} collective-permute-done((bf16[80,1280]{1,0:T(8,128)(2,1)S(1)}, bf16[80,1280]{1,0:T(8,128)(2,1)S(1)}, u32[]{:S(2)}, u32[]{:S(2)}) %collective-permute-start.14) | collective-permute-done | bytes 204832 | tf_op jit(solution)/shard_map/ppermute | solution.py:35
  61.5 1.3 collective-permute-start.16
  62.8 2.4 %collective-permute-start.17 = (f32[40,1280]{1,0:T(8,128)S(1)}, f32[40,1280]{1,0:T(8,128)S(1)}, u32[]{:S(2)}, u32[]{:S(2)}) collective-permute-start(f32[40,1280]{1,0:T(8,128)S(1)} %get-tuple-element.45), channel_id=1, source_target_pairs={{0,1},{1,0},{2,3},{3,2},{4,5},{5,4},{6,7},{7,6},{8,9},{9,8},{10,11... | collective-permute-start | bytes 614408 | tf_op jit(solution)/shard_map/ppermute | solution.py:23
  65.4 2.0 %collective-permute-start.2 = (bf16[4,160,1280]{2,1,0:T(8,128)(2,1)}, bf16[4,160,1280]{2,1,0:T(8,128)(2,1)S(1)}, u32[]{:S(2)}, u32[]{:S(2)}) collective-permute-start(bf16[4,160,1280]{2,1,0:T(8,128)(2,1)} %get-tuple-element.19), channel_id=1, source_target_pairs={{0,34},{2,8},{10,40},{8,18},{16,50},{18,24},{26,56},{24,2},{34,64}... | collective-permute-start | bytes 4915208 | tf_op jit(solution)/shard_map/ppermute | solution.py:35
  67.5 2.0 %collective-permute-start.3 = (bf16[4,160,1280]{2,1,0:T(8,128)(2,1)}, bf16[4,160,1280]{2,1,0:T(8,128)(2,1)}, u32[]{:S(2)}, u32[]{:S(2)}) collective-permute-start(bf16[4,160,1280]{2,1,0:T(8,128)(2,1)} %get-tuple-element.20), channel_id=1, source_target_pairs={{0,64},{2,18},{10,74},{8,24},{16,80},{18,2},{26,90},{24,8},{34,98}... | collective-permute-start | bytes 4915208 | tf_op jit(solution)/shard_map/ppermute | solution.py:35
  69.4 2.0 %collective-permute-start.4 = (bf16[4,160,1280]{2,1,0:T(8,128)(2,1)}, bf16[4,160,1280]{2,1,0:T(8,128)(2,1)}, u32[]{:S(2)}, u32[]{:S(2)}) collective-permute-start(bf16[4,160,1280]{2,1,0:T(8,128)(2,1)} %get-tuple-element.21), channel_id=1, source_target_pairs={{0,98},{2,24},{10,104},{8,2},{16,114},{18,8},{26,120},{24,18},{34,... | collective-permute-start | bytes 4915208 | tf_op jit(solution)/shard_map/ppermute | solution.py:35
  71.4 3.0 %collective-permute-done.17 = f32[40,1280]{1,0:T(8,128)S(1)} collective-permute-done((f32[40,1280]{1,0:T(8,128)S(1)}, f32[40,1280]{1,0:T(8,128)S(1)}, u32[]{:S(2)}, u32[]{:S(2)}) %collective-permute-start.17) | collective-permute-done | bytes 204832 | tf_op jit(solution)/shard_map/ppermute | solution.py:23
  74.4 2.3 %collective-permute-done.18 = f32[40,1280]{1,0:T(8,128)S(1)} collective-permute-done((f32[40,1280]{1,0:T(8,128)S(1)}, f32[40,1280]{1,0:T(8,128)S(1)}, u32[]{:S(2)}, u32[]{:S(2)}) %collective-permute-start.18) | collective-permute-done | bytes 204832 | tf_op jit(solution)/shard_map/ppermute | solution.py:249
  76.8 4.1 %fusion.6 = f32[80,1280]{1,0:T(8,128)S(1)} fusion(bf16[2560,1280]{1,0:T(8,128)(2,1)} %param.6, bf16[40,2560]{1,0:T(8,128)(2,1)S(1)} %get-tuple-element.43, bf16[40,2560]{1,0:T(8,128)(2,1)S(1)} %get-tuple-element.42), kind=kOutput, calls=%fused_computation.15 | convolution fusion | flops 525107200 | bytes 7372800 | tf_op jit(solution)/shard_map/dot_general | solution.py:258
  81.0 6.5 %collective-permute-done.19 = f32[40,1280]{1,0:T(8,128)S(1)} collective-permute-done((f32[40,1280]{1,0:T(8,128)S(1)}, f32[40,1280]{1,0:T(8,128)S(1)}, u32[]{:S(2)}, u32[]{:S(2)}) %collective-permute-start.19) | collective-permute-done | bytes 204832 | tf_op jit(solution)/shard_map/ppermute | solution.py:23
  87.5 3.4 %reshape.49 = f32[40,32,2,40]{3,2,1,0:T(2,128)} reshape(f32[40,2560]{1,0:T(8,128)S(1)} %pad_maximum_fusion.1) | data formatting | bytes 819200 | tf_op jit(solution)/shard_map/reshape | solution.py:264
  90.9 3.3 %copy.12 = f32[40,32,2,40]{3,0,1,2:T(8,128)} copy(f32[40,32,2,40]{3,2,1,0:T(2,128)} %reshape.49) | data formatting | bytes 819200 | tf_op jit(solution)/shard_map/reshape | solution.py:264
  94.2 2.5 %reshape.50.refs_0_ = f32[64,1600]{1,0:T(8,128)} reshape(f32[2,32,40,40]{3,2,1,0:T(8,128)} %bitcast.36) | data formatting | bytes 819200 | tf_op jit(solution)/shard_map/reshape | solution.py:264
  96.7 9.3 %collective-permute-done.3.a2 = bf16[4,160,1280]{2,1,0:T(8,128)(2,1)} collective-permute-done((bf16[4,160,1280]{2,1,0:T(8,128)(2,1)}, bf16[4,160,1280]{2,1,0:T(8,128)(2,1)}, u32[]{:S(2)}, u32[]{:S(2)}) %collective-permute-start.3) | collective-permute-done | bytes 1638432 | tf_op jit(solution)/shard_map/ppermute | solution.py:35
  106.2 3.5 %fold.2 = (f32[160,1280]{1,0:T(8,128)S(1)}, bf16[160,1280]{1,0:T(8,128)(2,1)S(1)}, bf16[160,1280]{1,0:T(8,128)(2,1)S(1)}, bf16[160,1280]{1,0:T(8,128)(2,1)S(1)}) custom-call(s32[1]{0:T(128)} %bitcast.me, bf16[4,160,1280]{2,1,0:T(8,128)(2,1)S(1)} %copy-done, bf16[4,160,1280]{2,1,0:T(8,128)(2,1)S(1)} %collective-permute-done.2.a1, ...), custom_call_target="tpu_custom_call" | custom-call | flops 3276800 | bytes 8601600 | tf_op jit(solution)/shard_map/fold/pallas_call | solution.py:210
  109.8 0.9 copy-done.4
  110.7 0.8 copy-done.6
  112.2 0.8 copy-done.11
  113.0 2.3 %copy.10 = f32[64,1,1600]{2,1,0:T(1,128)} copy(f32[64,1,1600]{2,0,1:T(8,128)} %bitcast.37) | data formatting | bytes 819200 | tf_op jit(solution)/shard_map/all_to_all | solution.py:270
  115.3 7.3 %all-to-all-start = ((f32[64,1,1600]{2,1,0:T(1,128)}), f32[64,1,1600]{2,1,0:T(1,128)S(1)}, u32[]{:S(2)}, u32[]{:S(2)}) async-start(f32[64,1,1600]{2,1,0:T(1,128)} %copy.10), calls=%async_computation | async-start | bytes 851968 | tf_op jit(solution)/shard_map/all_to_all | solution.py:270
  122.7 1.6 %collective-permute-start.5 = (bf16[160,1280]{1,0:T(8,128)(2,1)S(1)}, bf16[160,1280]{1,0:T(8,128)(2,1)S(1)}, u32[]{:S(2)}, u32[]{:S(2)}) collective-permute-start(bf16[160,1280]{1,0:T(8,128)(2,1)S(1)} %copy-done.7), channel_id=1, source_target_pairs={{0,10},{2,32},{10,16},{8,42},{16,26},{18,48},{26,0},{24,58},{34,40... | collective-permute-start | bytes 1228808 | tf_op jit(solution)/shard_map/ppermute | solution.py:35
  124.3 2.4 %collective-permute-start.6 = (bf16[160,1280]{1,0:T(8,128)(2,1)S(1)}, bf16[160,1280]{1,0:T(8,128)(2,1)}, u32[]{:S(2)}, u32[]{:S(2)}) collective-permute-start(bf16[160,1280]{1,0:T(8,128)(2,1)S(1)} %copy-done.12), channel_id=1, source_target_pairs={{0,16},{2,66},{10,26},{8,72},{16,0},{18,82},{26,10},{24,88},{34,50... | collective-permute-start | bytes 1228808 | tf_op jit(solution)/shard_map/ppermute | solution.py:35
  126.7 1.6 %collective-permute-start.7 = (bf16[160,1280]{1,0:T(8,128)(2,1)S(1)}, bf16[160,1280]{1,0:T(8,128)(2,1)}, u32[]{:S(2)}, u32[]{:S(2)}) collective-permute-start(bf16[160,1280]{1,0:T(8,128)(2,1)S(1)} %copy-done.10), channel_id=1, source_target_pairs={{0,26},{2,96},{10,0},{8,106},{16,10},{18,112},{26,16},{24,122},{34... | collective-permute-start | bytes 1228808 | tf_op jit(solution)/shard_map/ppermute | solution.py:35
  128.3 5.3 %all-to-all-done = f32[64,1,1600]{2,1,0:T(1,128)S(1)} async-done(((f32[64,1,1600]{2,1,0:T(1,128)}), f32[64,1,1600]{2,1,0:T(1,128)S(1)}, u32[]{:S(2)}, u32[]{:S(2)}) %all-to-all-start) | async-done | bytes 409632 | tf_op jit(solution)/shard_map/all_to_all | solution.py:270
  133.6 1.0 reduce
  135.8 4.6 %collective-permute-done.6 = bf16[160,1280]{1,0:T(8,128)(2,1)} collective-permute-done((bf16[160,1280]{1,0:T(8,128)(2,1)S(1)}, bf16[160,1280]{1,0:T(8,128)(2,1)}, u32[]{:S(2)}, u32[]{:S(2)}) %collective-permute-start.6) | collective-permute-done | bytes 409632 | tf_op jit(solution)/shard_map/ppermute | solution.py:35
  140.4 1.3 convert_add_fusion
  141.8 1.1 collective-permute-start.8
  142.9 4.0 %fusion.1 = f32[80,1280]{1,0:T(8,128)S(1)} fusion(bf16[2560,1280]{1,0:T(8,128)(2,1)} %param.7, bf16[2560,40]{1,0:T(8,128)(2,1)S(1)} %get-tuple-element.35, bf16[2560,40]{1,0:T(8,128)(2,1)S(1)} %get-tuple-element.34), kind=kOutput, calls=%fused_computation.6 | convolution fusion | flops 525107200 | bytes 7372800 | tf_op jit(solution)/shard_map/dot_general | solution.py:16
  146.9 1.6 %collective-permute-done.8 = bf16[80,1280]{1,0:T(8,128)(2,1)S(1)} collective-permute-done((bf16[80,1280]{1,0:T(8,128)(2,1)S(1)}, bf16[80,1280]{1,0:T(8,128)(2,1)S(1)}, u32[]{:S(2)}, u32[]{:S(2)}) %collective-permute-start.8) | collective-permute-done | bytes 204832 | tf_op jit(solution)/shard_map/ppermute | solution.py:23
  148.6 0.9 collective-permute-start.9
  150.6 0.8 maximum_bitcast_fusion
  (53 shorter events, 4.3 us)
Async XLA Ops:
  0.6 11.8 %collective-permute-start = (bf16[768,2560]{1,0:T(8,128)(2,1)}, bf16[768,2560]{1,0:T(8,128)(2,1)}, u32[]{:S(2)}, u32[]{:S(2)}) collective-permute-start(bf16[768,2560]{1,0:T(8,128)(2,1)} %b.1), channel_id=1, source_target_pairs={{0,2},{2,0},{1,3},{3,1},{4,6},{6,4},{5,7},{7,5},{8,10},{10,8},{9,1... | collective-permute-start | bytes 11796488 | tf_op jit(solution)/shard_map/ppermute | solution.py:23
  2.1 12.4 %collective-permute-start.1 = (bf16[768,2560]{1,0:T(8,128)(2,1)}, bf16[768,2560]{1,0:T(8,128)(2,1)}, u32[]{:S(2)}, u32[]{:S(2)}) collective-permute-start(bf16[768,2560]{1,0:T(8,128)(2,1)} %a.1), channel_id=1, source_target_pairs={{0,2},{2,0},{1,3},{3,1},{4,6},{6,4},{5,7},{7,5},{8,10},{10,8},{9,1... | collective-permute-start | bytes 11796488 | tf_op jit(solution)/shard_map/ppermute | solution.py:23
  2.3 2.1 %copy-start.1 = (bf16[768,2560]{1,0:T(8,128)(2,1)S(1)}, bf16[768,2560]{1,0:T(8,128)(2,1)}, u32[]{:S(2)}) copy-start(bf16[768,2560]{1,0:T(8,128)(2,1)} %a.1) | copy-start | bytes 11796484
  4.4 10.1 %copy-start.8 = (s32[4]{0:T(128)}, s32[4]{0:T(128)S(1)}, u32[]{:S(2)}) copy-start(s32[4]{0:T(128)S(1)} %pad_add_fusion.place) | copy-start | bytes 52
  24.0 0.9 copy-start.2
  24.9 23.8 %collective-permute-start.10 = (bf16[4,80,1280]{2,1,0:T(8,128)(2,1)}, bf16[4,80,1280]{2,1,0:T(8,128)(2,1)S(1)}, u32[]{:S(2)}, u32[]{:S(2)}) collective-permute-start(bf16[4,80,1280]{2,1,0:T(8,128)(2,1)} %get-tuple-element.27), channel_id=1, source_target_pairs={{0,34},{2,8},{10,40},{8,18},{16,50},{18,24},{26,56},{24,2},{34,64}... | collective-permute-start | bytes 2457608 | tf_op jit(solution)/shard_map/ppermute | solution.py:35
  26.6 22.1 %collective-permute-start.11 = (bf16[4,80,1280]{2,1,0:T(8,128)(2,1)}, bf16[4,80,1280]{2,1,0:T(8,128)(2,1)S(1)}, u32[]{:S(2)}, u32[]{:S(2)}) collective-permute-start(bf16[4,80,1280]{2,1,0:T(8,128)(2,1)} %get-tuple-element.28), channel_id=1, source_target_pairs={{0,64},{2,18},{10,74},{8,24},{16,80},{18,2},{26,90},{24,8},{34,98}... | collective-permute-start | bytes 2457608 | tf_op jit(solution)/shard_map/ppermute | solution.py:35
  29.1 19.6 %collective-permute-start.12 = (bf16[4,80,1280]{2,1,0:T(8,128)(2,1)S(1)}, bf16[4,80,1280]{2,1,0:T(8,128)(2,1)S(1)}, u32[]{:S(2)}, u32[]{:S(2)}) collective-permute-start(bf16[4,80,1280]{2,1,0:T(8,128)(2,1)S(1)} %get-tuple-element.29), channel_id=1, source_target_pairs={{0,98},{2,24},{10,104},{8,2},{16,114},{18,8},{26,120},{24,18},{34,... | collective-permute-start | bytes 2457608 | tf_op jit(solution)/shard_map/ppermute | solution.py:35
  48.7 1.1 copy-start.3
  50.6 7.3 %collective-permute-start.13 = (bf16[80,1280]{1,0:T(8,128)(2,1)S(1)}, bf16[80,1280]{1,0:T(8,128)(2,1)S(1)}, u32[]{:S(2)}, u32[]{:S(2)}) collective-permute-start(bf16[80,1280]{1,0:T(8,128)(2,1)S(1)} %get-tuple-element.31), channel_id=1, source_target_pairs={{0,10},{2,32},{10,16},{8,42},{16,26},{18,48},{26,0},{24,58},{34,40... | collective-permute-start | bytes 614408 | tf_op jit(solution)/shard_map/ppermute | solution.py:35
  52.3 8.9 %collective-permute-start.14 = (bf16[80,1280]{1,0:T(8,128)(2,1)S(1)}, bf16[80,1280]{1,0:T(8,128)(2,1)S(1)}, u32[]{:S(2)}, u32[]{:S(2)}) collective-permute-start(bf16[80,1280]{1,0:T(8,128)(2,1)S(1)} %get-tuple-element.32), channel_id=1, source_target_pairs={{0,16},{2,66},{10,26},{8,72},{16,0},{18,82},{26,10},{24,88},{34,50... | collective-permute-start | bytes 614408 | tf_op jit(solution)/shard_map/ppermute | solution.py:35
  55.6 5.7 %collective-permute-start.15 = (bf16[80,1280]{1,0:T(8,128)(2,1)S(1)}, bf16[80,1280]{1,0:T(8,128)(2,1)S(1)}, u32[]{:S(2)}, u32[]{:S(2)}) collective-permute-start(bf16[80,1280]{1,0:T(8,128)(2,1)S(1)} %get-tuple-element.33), channel_id=1, source_target_pairs={{0,26},{2,96},{10,0},{8,106},{16,10},{18,112},{26,16},{24,122},{34... | collective-permute-start | bytes 614408 | tf_op jit(solution)/shard_map/ppermute | solution.py:35
  61.5 7.9 %collective-permute-start.16 = (f32[40,1280]{1,0:T(8,128)S(1)}, f32[40,1280]{1,0:T(8,128)S(1)}, u32[]{:S(2)}, u32[]{:S(2)}) collective-permute-start(f32[40,1280]{1,0:T(8,128)S(1)} %get-tuple-element.44), channel_id=1, source_target_pairs={{0,4},{4,0},{1,5},{5,1},{2,6},{6,2},{3,7},{7,3},{8,12},{12,8},{9,1... | collective-permute-start | bytes 614408 | tf_op jit(solution)/shard_map/ppermute | solution.py:23
  62.8 11.6 %collective-permute-start.17 = (f32[40,1280]{1,0:T(8,128)S(1)}, f32[40,1280]{1,0:T(8,128)S(1)}, u32[]{:S(2)}, u32[]{:S(2)}) collective-permute-start(f32[40,1280]{1,0:T(8,128)S(1)} %get-tuple-element.45), channel_id=1, source_target_pairs={{0,1},{1,0},{2,3},{3,2},{4,5},{5,4},{6,7},{7,6},{8,9},{9,8},{10,11... | collective-permute-start | bytes 614408 | tf_op jit(solution)/shard_map/ppermute | solution.py:23
  65.2 11.5 %collective-permute-start.18 = (f32[40,1280]{1,0:T(8,128)S(1)}, f32[40,1280]{1,0:T(8,128)S(1)}, u32[]{:S(2)}, u32[]{:S(2)}) collective-permute-start(f32[40,1280]{1,0:T(8,128)S(1)} %get-tuple-element.44), channel_id=1, source_target_pairs={{0,5},{1,4},{4,1},{5,0},{2,7},{3,6},{6,3},{7,2},{8,13},{9,12},{12,... | collective-permute-start | bytes 614408 | tf_op jit(solution)/shard_map/ppermute | solution.py:249
  65.4 31.3 %collective-permute-start.2 = (bf16[4,160,1280]{2,1,0:T(8,128)(2,1)}, bf16[4,160,1280]{2,1,0:T(8,128)(2,1)S(1)}, u32[]{:S(2)}, u32[]{:S(2)}) collective-permute-start(bf16[4,160,1280]{2,1,0:T(8,128)(2,1)} %get-tuple-element.19), channel_id=1, source_target_pairs={{0,34},{2,8},{10,40},{8,18},{16,50},{18,24},{26,56},{24,2},{34,64}... | collective-permute-start | bytes 4915208 | tf_op jit(solution)/shard_map/ppermute | solution.py:35
  67.5 38.6 %collective-permute-start.3 = (bf16[4,160,1280]{2,1,0:T(8,128)(2,1)}, bf16[4,160,1280]{2,1,0:T(8,128)(2,1)}, u32[]{:S(2)}, u32[]{:S(2)}) collective-permute-start(bf16[4,160,1280]{2,1,0:T(8,128)(2,1)} %get-tuple-element.20), channel_id=1, source_target_pairs={{0,64},{2,18},{10,74},{8,24},{16,80},{18,2},{26,90},{24,8},{34,98}... | collective-permute-start | bytes 4915208 | tf_op jit(solution)/shard_map/ppermute | solution.py:35
  69.4 36.8 %collective-permute-start.4 = (bf16[4,160,1280]{2,1,0:T(8,128)(2,1)}, bf16[4,160,1280]{2,1,0:T(8,128)(2,1)}, u32[]{:S(2)}, u32[]{:S(2)}) collective-permute-start(bf16[4,160,1280]{2,1,0:T(8,128)(2,1)} %get-tuple-element.21), channel_id=1, source_target_pairs={{0,98},{2,24},{10,104},{8,2},{16,114},{18,8},{26,120},{24,18},{34,... | collective-permute-start | bytes 4915208 | tf_op jit(solution)/shard_map/ppermute | solution.py:35
  80.9 6.6 %collective-permute-start.19 = (f32[40,1280]{1,0:T(8,128)S(1)}, f32[40,1280]{1,0:T(8,128)S(1)}, u32[]{:S(2)}, u32[]{:S(2)}) collective-permute-start(f32[40,1280]{1,0:T(8,128)S(1)} %slice_add_fusion.1), channel_id=1, source_target_pairs={{0,1},{1,0},{2,3},{3,2},{4,5},{5,4},{6,7},{7,6},{8,9},{9,8},{10,11... | collective-permute-start | bytes 614408 | tf_op jit(solution)/shard_map/ppermute | solution.py:23
  90.9 15.3 %copy-start = (bf16[4,160,1280]{2,1,0:T(8,128)(2,1)S(1)}, bf16[4,160,1280]{2,1,0:T(8,128)(2,1)}, u32[]{:S(2)}) copy-start(bf16[4,160,1280]{2,1,0:T(8,128)(2,1)} %get-tuple-element.18.a0.refs_1_) | copy-start | bytes 4915204
  109.8 0.9 copy-start.4
  110.7 0.8 copy-start.6
  111.5 0.8 copy-start.9
  112.2 0.8 copy-start.11
  113.0 9.7 %copy-start.7 = (bf16[160,1280]{1,0:T(8,128)(2,1)S(1)}, bf16[160,1280]{1,0:T(8,128)(2,1)}, u32[]{:S(2)}) copy-start(bf16[160,1280]{1,0:T(8,128)(2,1)} %copy-done.6) | copy-start | bytes 1228804
  113.0 11.3 %copy-start.12 = (bf16[160,1280]{1,0:T(8,128)(2,1)S(1)}, bf16[160,1280]{1,0:T(8,128)(2,1)}, u32[]{:S(2)}) copy-start(bf16[160,1280]{1,0:T(8,128)(2,1)} %copy-done.11) | copy-start | bytes 1228804
  113.0 13.7 %copy-start.10 = (bf16[160,1280]{1,0:T(8,128)(2,1)S(1)}, bf16[160,1280]{1,0:T(8,128)(2,1)}, u32[]{:S(2)}) copy-start(bf16[160,1280]{1,0:T(8,128)(2,1)} %copy-done.9) | copy-start | bytes 1228804
  115.3 18.3 %all-to-all-start = ((f32[64,1,1600]{2,1,0:T(1,128)}), f32[64,1,1600]{2,1,0:T(1,128)S(1)}, u32[]{:S(2)}, u32[]{:S(2)}) async-start(f32[64,1,1600]{2,1,0:T(1,128)} %copy.10), calls=%async_computation | async-start | bytes 851968 | tf_op jit(solution)/shard_map/all_to_all | solution.py:270
  122.7 13.1 %collective-permute-start.5 = (bf16[160,1280]{1,0:T(8,128)(2,1)S(1)}, bf16[160,1280]{1,0:T(8,128)(2,1)S(1)}, u32[]{:S(2)}, u32[]{:S(2)}) collective-permute-start(bf16[160,1280]{1,0:T(8,128)(2,1)S(1)} %copy-done.7), channel_id=1, source_target_pairs={{0,10},{2,32},{10,16},{8,42},{16,26},{18,48},{26,0},{24,58},{34,40... | collective-permute-start | bytes 1228808 | tf_op jit(solution)/shard_map/ppermute | solution.py:35
  124.3 16.1 %collective-permute-start.6 = (bf16[160,1280]{1,0:T(8,128)(2,1)S(1)}, bf16[160,1280]{1,0:T(8,128)(2,1)}, u32[]{:S(2)}, u32[]{:S(2)}) collective-permute-start(bf16[160,1280]{1,0:T(8,128)(2,1)S(1)} %copy-done.12), channel_id=1, source_target_pairs={{0,16},{2,66},{10,26},{8,72},{16,0},{18,82},{26,10},{24,88},{34,50... | collective-permute-start | bytes 1228808 | tf_op jit(solution)/shard_map/ppermute | solution.py:35
  126.7 13.7 %collective-permute-start.7 = (bf16[160,1280]{1,0:T(8,128)(2,1)S(1)}, bf16[160,1280]{1,0:T(8,128)(2,1)}, u32[]{:S(2)}, u32[]{:S(2)}) collective-permute-start(bf16[160,1280]{1,0:T(8,128)(2,1)S(1)} %copy-done.10), channel_id=1, source_target_pairs={{0,26},{2,96},{10,0},{8,106},{16,10},{18,112},{26,16},{24,122},{34... | collective-permute-start | bytes 1228808 | tf_op jit(solution)/shard_map/ppermute | solution.py:35
  135.3 5.1 %copy-start.5 = (f32[160,1280]{1,0:T(8,128)S(1)}, f32[160,1280]{1,0:T(8,128)}, u32[]{:S(2)}) copy-start(f32[160,1280]{1,0:T(8,128)} %copy-done.4) | copy-start | bytes 2457604
  141.8 6.7 %collective-permute-start.8 = (bf16[80,1280]{1,0:T(8,128)(2,1)S(1)}, bf16[80,1280]{1,0:T(8,128)(2,1)S(1)}, u32[]{:S(2)}, u32[]{:S(2)}) collective-permute-start(bf16[80,1280]{1,0:T(8,128)(2,1)S(1)} %fusion.11), channel_id=1, source_target_pairs={{0,4},{4,0},{1,5},{5,1},{2,6},{6,2},{3,7},{7,3},{8,12},{12,8},{9,1... | collective-permute-start | bytes 614408 | tf_op jit(solution)/shard_map/ppermute | solution.py:23
  148.6 2.0 %collective-permute-start.9 = (f32[40,1280]{1,0:T(8,128)S(1)}, f32[40,1280]{1,0:T(8,128)S(1)}, u32[]{:S(2)}, u32[]{:S(2)}) collective-permute-start(f32[40,1280]{1,0:T(8,128)S(1)} %dynamic-slice_bitcast_fusion.2), channel_id=1, source_target_pairs={{0,2},{2,0},{1,3},{3,1},{4,6},{6,4},{5,7},{7,5},{8,10},{10,8},{9,1... | collective-permute-start | bytes 614408 | tf_op jit(solution)/shard_map/ppermute | solution.py:23

commit v4 on v3

--- a/solution.py
+++ b/solution.py
@@ -44,45 +44,38 @@
     return high.astype(BF), (x - high).astype(BF)
 
 
-def place_blocks(place, buffer, sems, outs, m, n, zs, finish):
-    part_me, z_me, y_me = place[1], place[2], place[3]
+def place_tile(place, buffer, sem, outs, m, zs, lanes):
     rows = TILE // (zs * 4)
-    wide = buffer.shape[2] // sems.shape[1]
-    lanes = pl.ds(pl.multiple_of(n * wide, wide), wide)
     for a in range(zs):
-        for k in range(4):
-            z = m * zs + a
-            ahead = jnp.where(part_me == 0, z - z_me + 4, k - y_me + 4) & 3
-            slot = jnp.where(part_me == 0, k, z)
-            part = a * 4 + k
-            block = buffer.at[m, pl.ds(part * rows, rows), lanes]
-
-            def move(out):
-                copy = pltpu.make_async_copy(block, out.at[slot, :, lanes], sems.at[m, n, part])
-                if finish:
-                    copy.wait()
-                else:
-                    copy.start()
-
+        z = m * zs + a
+
+        @pl.when(place[1] == 0)
+        def _():
             for r, out in enumerate(outs):
-                pl.when(ahead == r)(functools.partial(move, out))
-
-
-def store_tile(place, buffer, sems, outs, m, n, steps, lanes, zs):
-    place_blocks(place, buffer, sems, outs, m, n, zs, False)
-
-    @pl.when((m == steps - 1) & (n == lanes - 1))
-    def _():
-        for i in range(steps):
-            for j in range(lanes):
-                place_blocks(place, buffer, sems, outs, i, j, zs, True)
+
+                @pl.when(((z - place[2] + 4) & 3) == r)
+                def _():
+                    for k in range(4):
+                        block = buffer.at[m, pl.ds((a * 4 + k) * rows, rows), lanes]
+                        pltpu.make_async_copy(block, out.at[k], sem).start()
+
+        @pl.when(place[1] == 1)
+        def _():
+            for r, out in enumerate(outs):
+                at = pl.multiple_of((a * 4 + ((place[3] + r) & 3)) * rows, 16)
+                block = buffer.at[m, pl.ds(at, rows), lanes]
+                pltpu.make_async_copy(block, out.at[z], sem).start()
+
+
+def wait_tiles(buffer, sem):
+    pltpu.make_async_copy(buffer, buffer, sem).wait()
 
 
 def own_kernel(place, a, b, out):
     out[...] = contract(a[...], b[...])
 
 
-def cross_kernel(place, a, b, partial, own, ahead1, ahead2, ahead3, buffer, sems):
+def cross_kernel(place, a, b, partial, own, ahead1, ahead2, ahead3, buffer, sem):
     m, n = pl.program_id(0), pl.program_id(1)
     tile = (partial[...] + contract(a[...], b[...])).astype(BF)
     for lane in range(2):
@@ -91,7 +84,13 @@
         def _():
             buffer[m, :, lane * TILE : (lane + 1) * TILE] = tile
 
-    store_tile(place, buffer, sems, [own, ahead1, ahead2, ahead3], m, n, 2, 2, 2)
+    @pl.when(n == 1)
+    def _():
+        place_tile(place, buffer, sem, [own, ahead1, ahead2, ahead3], m, 2, slice(None))
+
+    @pl.when((m == 1) & (n == 1))
+    def _():
+        wait_tiles(buffer, sem)
 
 
 def cross_term(place, grads, grads_next, acts, acts_next):
@@ -123,7 +122,7 @@
             grid=(2, 2),
             in_specs=[left, right, middle],
             out_specs=[pl.BlockSpec(memory_space=pl.ANY)] * 4,
-            scratch_shapes=[pltpu.VMEM((2, TILE, half), BF), pltpu.SemaphoreType.DMA((2, 2, 8))],
+            scratch_shapes=[pltpu.VMEM((2, TILE, half), BF), pltpu.SemaphoreType.DMA],
         ),
         compiler_params=params,
         cost_estimate=cost,
@@ -131,42 +130,66 @@
     )(place, grads_next, acts_next, partial)
 
 
-def factor_kernel(
-    place, ha0, ha1, ga0, ga1, hb0, hb1, gb0, gb1, own, ahead1, ahead2, ahead3, buffer, sems
-):
+def factor_kernel(place, h0, h1, g0, g1, *rest):
+    outs, (lhs, rhs, buffer, lhs_sems, rhs_sem, sem) = rest[:8], rest[8:]
     m = pl.program_id(0)
-
-    def tile(a0, a1, b0, b1):
-        buffer[m] = (contract(a0[...], b0[...]) + contract(a1[...], b1[...])).astype(BF)
-
-    pl.when(place[0] == 0)(lambda: tile(ha0, ha1, hb0, hb1))
-    pl.when(place[0] == 1)(lambda: tile(ga0, ga1, gb0, gb1))
-    store_tile(place, buffer, sems, [own, ahead1, ahead2, ahead3], m, 0, 4, 1, 1)
+    half = rhs.shape[2]
+
+    def fetch(step, first):
+        at = pl.ds(pl.multiple_of(step * TILE, TILE), TILE)
+        right = pl.ds(pl.multiple_of(place[1] * half, half), half)
+        for owner, refs in enumerate(((h0, h1), (g0, g1))):
+
+            @pl.when(place[0] == owner)
+            def _():
+                for k, ref in enumerate(refs):
+                    if first:
+                        pltpu.make_async_copy(ref.at[:, right], rhs.at[k], rhs_sem).start()
+                    slot = step & 1
+                    pltpu.make_async_copy(ref.at[:, at], lhs.at[slot, k], lhs_sems.at[slot]).start()
+
+    pl.when(m == 0)(lambda: fetch(0, True))
+    pl.when(m < 3)(lambda: fetch(m + 1, False))
+    slot = m & 1
+    pltpu.make_async_copy(lhs.at[slot], lhs.at[slot], lhs_sems.at[slot]).wait()
+    pl.when(m == 0)(lambda: pltpu.make_async_copy(rhs, rhs, rhs_sem).wait())
+
+    buffer[m] = (contract(lhs[slot, 0], rhs[0]) + contract(lhs[slot, 1], rhs[1])).astype(BF)
+    for part in range(2):
+        lanes = slice(part * TILE, (part + 1) * TILE)
+        place_tile(place, buffer, sem, outs[part * 4 : part * 4 + 4], m, 1, lanes)
+    pl.when(m == 3)(lambda: wait_tiles(buffer, sem))
 
 
 def factor_term(place, acts, acts_next, grads, grads_next):
     tokens, width = acts.shape
     half = width // 2
-    a_acts = pl.BlockSpec((tokens, TILE), lambda m, p: (0, m * (1 - p[0])))
-    a_grads = pl.BlockSpec((tokens, TILE), lambda m, p: (0, m * p[0]))
-    b = pl.BlockSpec((tokens, half), lambda m, p: (0, p[1]))
-    out = jax.ShapeDtypeStruct((4, width // 16, half), BF)
-    return pl.pallas_call(
+    anywhere = pl.BlockSpec(memory_space=pl.ANY)
+    out = jax.ShapeDtypeStruct((4, width // 16, TILE), BF)
+    outs = pl.pallas_call(
         factor_kernel,
-        out_shape=[out] * 4,
+        out_shape=[out] * 8,
         grid_spec=pltpu.PrefetchScalarGridSpec(
             num_scalar_prefetch=1,
             grid=(4,),
-            in_specs=[a_acts, a_acts, a_grads, a_grads, b, b, b, b],
-            out_specs=[pl.BlockSpec(memory_space=pl.ANY)] * 4,
-            scratch_shapes=[pltpu.VMEM((4, TILE, half), BF), pltpu.SemaphoreType.DMA((4, 1, 4))],
-        ),
-        compiler_params=pltpu.CompilerParams(vmem_limit_bytes=56 * 2**20),
+            in_specs=[anywhere] * 4,
+            out_specs=[anywhere] * 8,
+            scratch_shapes=[
+                pltpu.VMEM((2, 2, tokens, TILE), BF),
+                pltpu.VMEM((2, tokens, half), BF),
+                pltpu.VMEM((4, TILE, half), BF),
+                pltpu.SemaphoreType.DMA((2,)),
+                pltpu.SemaphoreType.DMA,
+                pltpu.SemaphoreType.DMA,
+            ],
+        ),
+        compiler_params=pltpu.CompilerParams(vmem_limit_bytes=40 * 2**20),
         cost_estimate=pl.CostEstimate(
             flops=4 * tokens * width * half, bytes_accessed=16 * tokens * half, transcendentals=0
         ),
         name="factor_term",
-    )(place, acts, acts_next, grads, grads_next, acts, acts_next, grads, grads_next)
+    )(place, acts, acts_next, grads, grads_next)
+    return outs[:4], outs[4:]
 
 
 def add(first, *rest):
@@ -237,12 +260,16 @@
     own, m1, m2, m3 = cross_term(place, out_grad, grads_next, hidden, acts_next)
     m_parts = [own, turn(m1, 1, 0), turn(m2, 2, 0), turn(m3, 3, 0)]
 
-    own, f1, f2, f3 = factor_term(place, hidden, acts_next, out_grad, grads_next)
-    f_parts = [own, turn(f1, 1, 0), turn(f2, 2, 0), turn(f3, 3, 0)]
-
-    m_parts[0] = gate(m_parts[0], own)
-    m, *pieces = fold(second_me, m_parts)
-    m = add(m, *[turn(piece, s, 1) for s, piece in enumerate(pieces, 1)])
+    f_terms = factor_term(place, hidden, acts_next, out_grad, grads_next)
+    f_parts = [[term[0]] + [turn(term[s], s, 0) for s in (1, 2, 3)] for term in f_terms]
+
+    def second_round(parts):
+        total, *pieces = fold(second_me, parts)
+        return pieces[0], add(total, *[turn(piece, s, 1) for s, piece in enumerate(pieces, 1)])
+
+    m_parts[0] = gate(m_parts[0], f_terms[0][0])
+    _, m = second_round(m_parts)
+    early, f_early = second_round(f_parts[0])
     m = m.reshape(2, half // 32, half)
     mine, theirs = pick(m, 0, xl), pick(m, 0, 1 - xl)
     m_own = mine + shift(theirs, "xl", 1)
@@ -254,19 +281,17 @@
         [jnp.where(swap, m_own, partner), jnp.where(swap, partner, m_own)], axis=1
     )
     rows = mrow.shape[0]
-    stacked = jnp.concatenate(split_pair(mrow))
+    stacked = jnp.concatenate(split_pair(gate(mrow, early)))
     pt = jnp.dot(stacked, left_inverse, preferred_element_type=F32)
     pt = pt[:rows] + pt[rows:]
     pt_other = shift(pt, "o", 1)
     pt = jnp.concatenate(
         [jnp.where(first, pt, pt_other), jnp.where(first, pt_other, pt)], axis=1
     )
-    blocks = pt.reshape(rows, 32, 2, rows).transpose(2, 1, 0, 3).reshape(64, rows * rows)
-
-    f, *pieces = fold(second_me, f_parts)
-    f = add(f, *[turn(piece, s, 1) for s, piece in enumerate(pieces, 1)])
-
-    blocks = gate(blocks, pieces[0])
+    blocks = pt.reshape(rows, 32, 2, rows).transpose(2, 1, 0, 3).reshape(64, rows, rows)
+
+    late, f_late = second_round(f_parts[1])
+    blocks = gate(blocks, late)
     blocks = lax.all_to_all(blocks, ("c", "z", "y", "xl"), 0, 0, tiled=True)
     blocks = blocks.reshape(2, 4, 4, 2, rows, rows)
     odd = ((jnp.arange(4)[:, None] + jnp.arange(4)) & 1).reshape(1, 4, 4, 1, 1, 1) == 1
@@ -275,7 +300,7 @@
     update = contract(stacked, right_inverse)
     update = update[:rows] + update[rows:]
 
-    f = f.reshape(2, width // 32, half)
+    f = jnp.concatenate([f_early, f_late], axis=1).reshape(2, width // 32, half)
     f = pick(f, 0, xl) + shift(pick(f, 0, 1 - xl).astype(BF), "xl", 1).astype(F32)
     f = f * jnp.where(first, 1.0 / token_total, 1.0).astype(F32)
     f = f.reshape(2, width // 64, half)

time: 152 us -> 169 us (1.11)
  starting transfers between devices: 38.6 us -> 49.1 us
  other arithmetic: 4.63 us -> 7.04 us
  Pallas kernels: 39.9 us -> 42.3 us
    unnamed x26 -> x34, local copies, waits for them, and re-layouts: 7.36 us -> 15.8 us
    reshape x4 -> x2, local copies, waits for them, and re-layouts: 9.69 us -> 4.15 us  [per_device(): pt.reshape(rows, 32, 2, rows).transpose(2, 1, 0, 3).reshape(64, rows, rows)]
    all_to_all x1, waiting for transfers between devices: 5.27 us -> 10.1 us  [per_device(): blocks = lax.all_to_all(blocks, ('c', 'z', 'y', 'xl'), 0, 0, tiled=True)]
    ppermute x7, waiting for transfers between devices: 13.4 us -> 8.74 us  [shift(): return lax.ppermute(x, axis, [(i, (i + step) % size) for i in range(size)])]
    ppermute x7, starting transfers between devices: 7.41 us -> 10.8 us  [shift(): return lax.ppermute(x, axis, [(i, (i + step) % size) for i in range(size)])]
    pallas_call x1, Pallas kernels: 18.1 us -> 15.2 us  [factor_term(): pl.pallas_call(factor_kernel, out_shape=[out] * 8, grid_spec=pltpu.Prefet...]
    all_to_all x1, starting transfers between devices: 7.35 us -> 10.1 us  [per_device(): blocks = lax.all_to_all(blocks, ('c', 'z', 'y', 'xl'), 0, 0, tiled=True)]
    pallas_call x2 -> x3, Pallas kernels: 4.3 us -> 7.07 us  [fold(): pl.pallas_call(fold_kernel, out_shape=[jax.ShapeDtypeStruct((rows, width)...]
  transfers between devices with their start and end apart: 21 -> 27, of which waited for: 14 -> 7; matrix products, arithmetic and copies ran while one was open for 13% -> 9% of each run, Pallas kernels for 17% -> 18%
where the time goes in v4:
time: 169 us; the launch traced here: 168 us
  starting transfers between devices  49.1 us (29%)
  Pallas kernels  42.3 us (25%)
  waiting for transfers between devices  40.3 us (24%)
  local copies, waits for them, and re-layouts  20.5 us (12%)
  matrix products  8.13 us (5%)
  other arithmetic  7.04 us (4%)
    ppermute x18, starting transfers between devices, turn(): return lax.ppermute(x, ('z', 'y', 'c'), pairs)  25.8 us
    ppermute x18, waiting for transfers between devices, turn(): return lax.ppermute(x, ('z', 'y', 'c'), pairs)  21.5 us
    unnamed x34, local copies, waits for them, and re-layouts  15.8 us
    pallas_call x1, Pallas kernels, factor_term(): pl.pallas_call(factor_kernel, out_shape=[out] * 8, grid_spec=pltpu.Prefet...  15.2 us
    pallas_call x1, Pallas kernels, cross_term(): pl.pallas_call(cross_kernel, out_shape=[out] * 4, grid_spec=pltpu.Prefetc...  12 us
    ppermute x7, starting transfers between devices, shift(): return lax.ppermute(x, axis, [(i, (i + step) % size) for i in range(size)])  10.8 us
    all_to_all x1, starting transfers between devices, per_device(): blocks = lax.all_to_all(blocks, ('c', 'z', 'y', 'xl'), 0, 0, tiled=True)  10.1 us
    all_to_all x1, waiting for transfers between devices, per_device(): blocks = lax.all_to_all(blocks, ('c', 'z', 'y', 'xl'), 0, 0, tiled=True)  10.1 us
  transfers between devices with their start and end apart: 27, of which 7 were waited for; matrix products, arithmetic and copies ran while one was open for 9% of the time, Pallas kernels for 18%

profile of v4, /device:TPU:1, one launch (start us, length us, event | category | flops | bytes accessed | tf_op | source)
XLA Modules:
  0.0 168.3 jit_solution(337429197514282330)
XLA Ops:
  0.6 1.5 collective-permute-start
  2.3 2.1 %copy-done.1 = bf16[768,2560]{1,0:T(8,128)(2,1)S(1)} copy-done((bf16[768,2560]{1,0:T(8,128)(2,1)S(1)}, bf16[768,2560]{1,0:T(8,128)(2,1)}, u32[]{:S(2)}) %copy-start.1) | copy-done | bytes 3932184
  4.4 8.0 %cross_own.1.partial = f32[1280,1280]{1,0:T(8,128)} custom-call(s32[4]{0:T(128)S(1)} %pad_add_fusion.place, bf16[768,2560]{1,0:T(8,128)(2,1)S(1)} %copy-done.1, bf16[768,2560]{1,0:T(8,128)(2,1)} %b.1), custom_call_target="tpu_custom_call" | custom-call | flops 2516582400 | bytes 9830400 | tf_op jit(solution)/shard_map/cross_own/pallas_call | solution.py:106
  12.5 2.0 %collective-permute-done.1.g1.a = bf16[768,2560]{1,0:T(8,128)(2,1)} collective-permute-done((bf16[768,2560]{1,0:T(8,128)(2,1)}, bf16[768,2560]{1,0:T(8,128)(2,1)}, u32[]{:S(2)}, u32[]{:S(2)}) %collective-permute-start.1) | collective-permute-done | bytes 3932192 | tf_op jit(solution)/shard_map/ppermute | solution.py:23
  14.5 12.0 %cross_term.1 = (bf16[4,80,1280]{2,1,0:T(8,128)(2,1)S(1)}, bf16[4,80,1280]{2,1,0:T(8,128)(2,1)S(1)}, bf16[4,80,1280]{2,1,0:T(8,128)(2,1)S(1)}, bf16[4,80,1280]{2,1,0:T(8,128)(2,1)S(1)}) custom-call(s32[4]{0:T(128)S(1)} %pad_add_fusion.place, bf16[768,2560]{1,0:T(8,128)(2,1)} %collective-permute-done.1.g1.a, bf16[768,2560]{1,0:T(8,128)(2,1)} %collective-permute-done.h1.b, ...), custom_call_target="tpu_custom_call" | custom-call | flops 2516582400 | bytes 9830400 | tf_op jit(solution)/shard_map/cross_term/pallas_call | solution.py:117
  26.6 0.9 copy-done.4
  27.5 1.6 collective-permute-start.16
  29.1 2.6 %collective-permute-start.17 = (bf16[4,80,1280]{2,1,0:T(8,128)(2,1)S(1)}, bf16[4,80,1280]{2,1,0:T(8,128)(2,1)S(1)}, u32[]{:S(2)}, u32[]{:S(2)}) collective-permute-start(bf16[4,80,1280]{2,1,0:T(8,128)(2,1)S(1)} %get-tuple-element.44), channel_id=1, source_target_pairs={{0,64},{2,18},{10,74},{8,24},{16,80},{18,2},{26,90},{24,8},{34,98}... | collective-permute-start | bytes 2457608 | tf_op jit(solution)/shard_map/ppermute | solution.py:35
  31.7 1.4 collective-permute-start.18
  33.1 15.2 %factor_term.1 = (bf16[4,160,640]{2,1,0:T(8,128)(2,1)S(1)}, bf16[4,160,640]{2,1,0:T(8,128)(2,1)S(1)}, bf16[4,160,640]{2,1,0:T(8,128)(2,1)}, bf16[4,160,640]{2,1,...) custom-call(s32[4]{0:T(128)S(1)} %pad_add_fusion.place, ...), custom_call_target="tpu_custom_call" | custom-call | flops 10066329600 | bytes 15728640 | tf_op jit(solution)/shard_map/factor_term/pallas_call | solution.py:169
  48.3 0.9 copy-done.2
  50.4 1.0 copy-done.6
  51.4 1.9 %collective-permute-start.4 = (bf16[4,160,640]{2,1,0:T(8,128)(2,1)}, bf16[4,160,640]{2,1,0:T(8,128)(2,1)}, u32[]{:S(2)}, u32[]{:S(2)}) collective-permute-start(bf16[4,160,640]{2,1,0:T(8,128)(2,1)} %get-tuple-element.29), channel_id=1, source_target_pairs={{0,98},{2,24},{10,104},{8,2},{16,114},{18,8},{26,120},{24,18},{34,... | collective-permute-start | bytes 2457608 | tf_op jit(solution)/shard_map/ppermute | solution.py:35
  55.0 0.9 copy-done.10
  56.8 14.5 %collective-permute-done.2.a1 = bf16[4,160,640]{2,1,0:T(8,128)(2,1)S(1)} collective-permute-done((bf16[4,160,640]{2,1,0:T(8,128)(2,1)S(1)}, bf16[4,160,640]{2,1,0:T(8,128)(2,1)S(1)}, u32[]{:S(2)}, u32[]{:S(2)}) %collective-permute-start.2) | collective-permute-done | bytes 819232 | tf_op jit(solution)/shard_map/ppermute | solution.py:35
  71.3 1.1 copy-done.5
  72.4 1.1 copy-done.7
  73.6 1.1 copy-done.9
  74.7 1.1 copy-done.11
  75.9 1.6 fold.5
  78.2 1.3 collective-permute-start.19
  79.6 3.3 %collective-permute-start.20 = (bf16[80,1280]{1,0:T(8,128)(2,1)}, bf16[80,1280]{1,0:T(8,128)(2,1)}, u32[]{:S(2)}, u32[]{:S(2)}) collective-permute-start(bf16[80,1280]{1,0:T(8,128)(2,1)} %get-tuple-element.48), channel_id=1, source_target_pairs={{0,16},{2,66},{10,26},{8,72},{16,0},{18,82},{26,10},{24,88},{34,50... | collective-permute-start | bytes 614408 | tf_op jit(solution)/shard_map/ppermute | solution.py:35
  82.9 1.5 collective-permute-start.21
  84.3 2.7 %fold.3 = (f32[160,640]{1,0:T(8,128)S(1)}, bf16[160,640]{1,0:T(8,128)(2,1)S(1)}, bf16[160,640]{1,0:T(8,128)(2,1)S(1)}, bf16[160,640]{1,0:T(8,128)(2,1)S(1)}) custom-call(s32[1]{0:T(128)} %bitcast.me, bf16[4,160,640]{2,1,0:T(8,128)(2,1)S(1)} %copy-done.3, bf16[4,160,640]{2,1,0:T(8,128)(2,1)S(1)} %collective-permute-done.2.a1, ...), custom_call_target="tpu_custom_call" | custom-call | flops 1638400 | bytes 4300800 | tf_op jit(solution)/shard_map/fold/pallas_call | solution.py:233
  87.1 5.9 %collective-permute-done.8.a1 = bf16[4,160,640]{2,1,0:T(8,128)(2,1)} collective-permute-done((bf16[4,160,640]{2,1,0:T(8,128)(2,1)}, bf16[4,160,640]{2,1,0:T(8,128)(2,1)}, u32[]{:S(2)}, u32[]{:S(2)}) %collective-permute-start.8) | collective-permute-done | bytes 819232 | tf_op jit(solution)/shard_map/ppermute | solution.py:35
  93.0 3.5 %collective-permute-start.6 = (bf16[160,640]{1,0:T(8,128)(2,1)S(1)}, bf16[160,640]{1,0:T(8,128)(2,1)S(1)}, u32[]{:S(2)}, u32[]{:S(2)}) collective-permute-start(bf16[160,640]{1,0:T(8,128)(2,1)S(1)} %get-tuple-element.32), channel_id=1, source_target_pairs={{0,16},{2,66},{10,26},{8,72},{16,0},{18,82},{26,10},{24,88},{34,50... | collective-permute-start | bytes 614408 | tf_op jit(solution)/shard_map/ppermute | solution.py:35
  96.5 2.7 %fold.4 = (f32[160,640]{1,0:T(8,128)S(1)}, bf16[160,640]{1,0:T(8,128)(2,1)S(1)}, bf16[160,640]{1,0:T(8,128)(2,1)S(1)}, bf16[160,640]{1,0:T(8,128)(2,1)S(1)}) custom-call(s32[1]{0:T(128)} %bitcast.me, bf16[4,160,640]{2,1,0:T(8,128)(2,1)S(1)} %get-tuple-element.34.a0, bf16[4,160,640]{2,1,0:T(8,128)(2,1)} %collective-permute-done.8.a1, ...), custom_call_target="tpu_custom_call" | custom-call | flops 1638400 | bytes 4300800 | tf_op jit(solution)/shard_map/fold/pallas_call | solution.py:233
  99.3 2.7 %collective-permute-start.7 = (bf16[160,640]{1,0:T(8,128)(2,1)S(1)}, bf16[160,640]{1,0:T(8,128)(2,1)S(1)}, u32[]{:S(2)}, u32[]{:S(2)}) collective-permute-start(bf16[160,640]{1,0:T(8,128)(2,1)S(1)} %get-tuple-element.33), channel_id=1, source_target_pairs={{0,26},{2,96},{10,0},{8,106},{16,10},{18,112},{26,16},{24,122},{34... | collective-permute-start | bytes 614408 | tf_op jit(solution)/shard_map/ppermute | solution.py:35
  102.0 1.3 collective-permute-start.12
  103.3 1.1 convert_add_fusion
  104.5 1.8 %collective-permute-start.13 = (bf16[160,640]{1,0:T(8,128)(2,1)S(1)}, bf16[160,640]{1,0:T(8,128)(2,1)S(1)}, u32[]{:S(2)}, u32[]{:S(2)}) collective-permute-start(bf16[160,640]{1,0:T(8,128)(2,1)S(1)} %get-tuple-element.41), channel_id=1, source_target_pairs={{0,26},{2,96},{10,0},{8,106},{16,10},{18,112},{26,16},{24,122},{34... | collective-permute-start | bytes 614408 | tf_op jit(solution)/shard_map/ppermute | solution.py:35
  106.2 1.2 collective-permute-start.22
  107.4 2.3 %collective-permute-start.24 = (f32[40,1280]{1,0:T(8,128)S(1)}, f32[40,1280]{1,0:T(8,128)S(1)}, u32[]{:S(2)}, u32[]{:S(2)}) collective-permute-start(f32[40,1280]{1,0:T(8,128)S(1)} %get-tuple-element.60), channel_id=1, source_target_pairs={{0,5},{1,4},{4,1},{5,0},{2,7},{3,6},{6,3},{7,2},{8,13},{9,12},{12,... | collective-permute-start | bytes 614408 | tf_op jit(solution)/shard_map/ppermute | solution.py:276
  109.8 1.0 collective-permute-done.11
  110.9 3.2 %collective-permute-start.23 = (f32[40,1280]{1,0:T(8,128)S(1)}, f32[40,1280]{1,0:T(8,128)S(1)}, u32[]{:S(2)}, u32[]{:S(2)}) collective-permute-start(f32[40,1280]{1,0:T(8,128)S(1)} %get-tuple-element.61), channel_id=1, source_target_pairs={{0,1},{1,0},{2,3},{3,2},{4,5},{5,4},{6,7},{7,6},{8,9},{9,8},{10,11... | collective-permute-start | bytes 614408 | tf_op jit(solution)/shard_map/ppermute | solution.py:23
  114.7 5.0 %collective-permute-done.23 = f32[40,1280]{1,0:T(8,128)S(1)} collective-permute-done((f32[40,1280]{1,0:T(8,128)S(1)}, f32[40,1280]{1,0:T(8,128)S(1)}, u32[]{:S(2)}, u32[]{:S(2)}) %collective-permute-start.23) | collective-permute-done | bytes 204832 | tf_op jit(solution)/shard_map/ppermute | solution.py:23
  120.6 1.0 reduce-precision_convert_fusion.1
  121.6 4.1 %fusion.6 = f32[80,1280]{1,0:T(8,128)S(1)} fusion(bf16[2560,1280]{1,0:T(8,128)(2,1)} %param.6, bf16[40,2560]{1,0:T(8,128)(2,1)S(1)} %get-tuple-element.59, bf16[40,2560]{1,0:T(8,128)(2,1)S(1)} %get-tuple-element.58), kind=kOutput, calls=%fused_computation.14 | convolution fusion | flops 525107200 | bytes 7372800 | tf_op jit(solution)/shard_map/dot_general | solution.py:285
  125.8 2.9 %collective-permute-start.25 = (f32[40,1280]{1,0:T(8,128)S(1)}, f32[40,1280]{1,0:T(8,128)S(1)}, u32[]{:S(2)}, u32[]{:S(2)}) collective-permute-start(f32[40,1280]{1,0:T(8,128)S(1)} %slice_add_fusion.1), channel_id=1, source_target_pairs={{0,1},{1,0},{2,3},{3,2},{4,5},{5,4},{6,7},{7,6},{8,9},{9,8},{10,11... | collective-permute-start | bytes 614408 | tf_op jit(solution)/shard_map/ppermute | solution.py:23
  128.8 1.5 collective-permute-start.15
  130.3 1.7 collective-permute-done.25
  132.1 2.3 %reshape.46 = f32[40,32,2,40]{3,2,1,0:T(2,128)S(1)} reshape(f32[40,2560]{1,0:T(8,128)S(1)} %pad_maximum_fusion.2) | data formatting | bytes 819200 | tf_op jit(solution)/shard_map/reshape | solution.py:291
  134.4 1.9 %copy.9 = f32[40,32,2,40]{3,0,1,2:T(8,128)} copy(f32[40,32,2,40]{3,2,1,0:T(2,128)S(1)} %reshape.46) | data formatting | bytes 819200 | tf_op jit(solution)/shard_map/reshape | solution.py:291
  136.2 3.2 %reshape.50 = f32[64,1,1600]{2,1,0:T(1,128)} reshape(f32[64,40,40]{2,1,0:T(8,128)} %gate.5) | data formatting | bytes 819200
  139.4 10.1 %all-to-all-start = ((f32[64,1,1600]{2,1,0:T(1,128)}), f32[64,1,1600]{2,1,0:T(1,128)S(1)}, u32[]{:S(2)}, u32[]{:S(2)}) async-start(f32[64,1,1600]{2,1,0:T(1,128)} %reshape.50), calls=%async_computation | async-start | bytes 851968 | tf_op jit(solution)/shard_map/all_to_all | solution.py:295
  150.4 10.1 %all-to-all-done = f32[64,1,1600]{2,1,0:T(1,128)S(1)} async-done(((f32[64,1,1600]{2,1,0:T(1,128)}), f32[64,1,1600]{2,1,0:T(1,128)S(1)}, u32[]{:S(2)}, u32[]{:S(2)}) %all-to-all-start) | async-done | bytes 409632 | tf_op jit(solution)/shard_map/all_to_all | solution.py:295
  161.0 1.7 reduce
  163.6 4.0 %fusion.1 = f32[80,1280]{1,0:T(8,128)S(1)} fusion(bf16[2560,1280]{1,0:T(8,128)(2,1)} %param.7, bf16[2560,40]{1,0:T(8,128)(2,1)S(1)} %get-tuple-element.51, bf16[2560,40]{1,0:T(8,128)(2,1)S(1)} %get-tuple-element.50), kind=kOutput, calls=%fused_computation.5 | convolution fusion | flops 525107200 | bytes 7372800 | tf_op jit(solution)/shard_map/dot_general | solution.py:16
  (76 shorter events, 9.5 us)
Async XLA Ops:
  0.6 11.8 %collective-permute-start = (bf16[768,2560]{1,0:T(8,128)(2,1)}, bf16[768,2560]{1,0:T(8,128)(2,1)}, u32[]{:S(2)}, u32[]{:S(2)}) collective-permute-start(bf16[768,2560]{1,0:T(8,128)(2,1)} %b.1), channel_id=1, source_target_pairs={{0,2},{2,0},{1,3},{3,1},{4,6},{6,4},{5,7},{7,5},{8,10},{10,8},{9,1... | collective-permute-start | bytes 11796488 | tf_op jit(solution)/shard_map/ppermute | solution.py:23
  2.1 12.4 %collective-permute-start.1 = (bf16[768,2560]{1,0:T(8,128)(2,1)}, bf16[768,2560]{1,0:T(8,128)(2,1)}, u32[]{:S(2)}, u32[]{:S(2)}) collective-permute-start(bf16[768,2560]{1,0:T(8,128)(2,1)} %a.1), channel_id=1, source_target_pairs={{0,2},{2,0},{1,3},{3,1},{4,6},{6,4},{5,7},{7,5},{8,10},{10,8},{9,1... | collective-permute-start | bytes 11796488 | tf_op jit(solution)/shard_map/ppermute | solution.py:23
  2.3 2.1 %copy-start.1 = (bf16[768,2560]{1,0:T(8,128)(2,1)S(1)}, bf16[768,2560]{1,0:T(8,128)(2,1)}, u32[]{:S(2)}) copy-start(bf16[768,2560]{1,0:T(8,128)(2,1)} %a.1) | copy-start | bytes 11796484
  12.5 20.6 %copy-start = (bf16[768,2560]{1,0:T(8,128)(2,1)S(1)}, bf16[768,2560]{1,0:T(8,128)(2,1)}, u32[]{:S(2)}) copy-start(bf16[768,2560]{1,0:T(8,128)(2,1)} %b.1) | copy-start | bytes 11796484
  26.5 0.9 copy-start.4
  27.5 23.0 %collective-permute-start.16 = (bf16[4,80,1280]{2,1,0:T(8,128)(2,1)S(1)}, bf16[4,80,1280]{2,1,0:T(8,128)(2,1)S(1)}, u32[]{:S(2)}, u32[]{:S(2)}) collective-permute-start(bf16[4,80,1280]{2,1,0:T(8,128)(2,1)S(1)} %get-tuple-element.43), channel_id=1, source_target_pairs={{0,34},{2,8},{10,40},{8,18},{16,50},{18,24},{26,56},{24,2},{34,64}... | collective-permute-start | bytes 2457608 | tf_op jit(solution)/shard_map/ppermute | solution.py:35
  29.1 24.2 %collective-permute-start.17 = (bf16[4,80,1280]{2,1,0:T(8,128)(2,1)S(1)}, bf16[4,80,1280]{2,1,0:T(8,128)(2,1)S(1)}, u32[]{:S(2)}, u32[]{:S(2)}) collective-permute-start(bf16[4,80,1280]{2,1,0:T(8,128)(2,1)S(1)} %get-tuple-element.44), channel_id=1, source_target_pairs={{0,64},{2,18},{10,74},{8,24},{16,80},{18,2},{26,90},{24,8},{34,98}... | collective-permute-start | bytes 2457608 | tf_op jit(solution)/shard_map/ppermute | solution.py:35
  31.7 23.3 %collective-permute-start.18 = (bf16[4,80,1280]{2,1,0:T(8,128)(2,1)S(1)}, bf16[4,80,1280]{2,1,0:T(8,128)(2,1)S(1)}, u32[]{:S(2)}, u32[]{:S(2)}) collective-permute-start(bf16[4,80,1280]{2,1,0:T(8,128)(2,1)S(1)} %get-tuple-element.45), channel_id=1, source_target_pairs={{0,98},{2,24},{10,104},{8,2},{16,114},{18,8},{26,120},{24,18},{34,... | collective-permute-start | bytes 2457608 | tf_op jit(solution)/shard_map/ppermute | solution.py:35
  48.3 0.9 copy-start.2
  49.2 22.0 %collective-permute-start.2 = (bf16[4,160,640]{2,1,0:T(8,128)(2,1)S(1)}, bf16[4,160,640]{2,1,0:T(8,128)(2,1)S(1)}, u32[]{:S(2)}, u32[]{:S(2)}) collective-permute-start(bf16[4,160,640]{2,1,0:T(8,128)(2,1)S(1)} %get-tuple-element.27), channel_id=1, source_target_pairs={{0,34},{2,8},{10,40},{8,18},{16,50},{18,24},{26,56},{24,2},{34,64}... | collective-permute-start | bytes 2457608 | tf_op jit(solution)/shard_map/ppermute | solution.py:35
  49.6 28.6 %collective-permute-start.3 = (bf16[4,160,640]{2,1,0:T(8,128)(2,1)}, bf16[4,160,640]{2,1,0:T(8,128)(2,1)}, u32[]{:S(2)}, u32[]{:S(2)}) collective-permute-start(bf16[4,160,640]{2,1,0:T(8,128)(2,1)} %get-tuple-element.28), channel_id=1, source_target_pairs={{0,64},{2,18},{10,74},{8,24},{16,80},{18,2},{26,90},{24,8},{34,98}... | collective-permute-start | bytes 2457608 | tf_op jit(solution)/shard_map/ppermute | solution.py:35
  50.4 1.0 copy-start.6
  51.4 28.2 %collective-permute-start.4 = (bf16[4,160,640]{2,1,0:T(8,128)(2,1)}, bf16[4,160,640]{2,1,0:T(8,128)(2,1)}, u32[]{:S(2)}, u32[]{:S(2)}) collective-permute-start(bf16[4,160,640]{2,1,0:T(8,128)(2,1)} %get-tuple-element.29), channel_id=1, source_target_pairs={{0,98},{2,24},{10,104},{8,2},{16,114},{18,8},{26,120},{24,18},{34,... | collective-permute-start | bytes 2457608 | tf_op jit(solution)/shard_map/ppermute | solution.py:35
  53.3 0.9 copy-start.8
  54.1 28.7 %collective-permute-start.10 = (bf16[4,160,640]{2,1,0:T(8,128)(2,1)}, bf16[4,160,640]{2,1,0:T(8,128)(2,1)S(1)}, u32[]{:S(2)}, u32[]{:S(2)}) collective-permute-start(bf16[4,160,640]{2,1,0:T(8,128)(2,1)} %get-tuple-element.37), channel_id=1, source_target_pairs={{0,98},{2,24},{10,104},{8,2},{16,114},{18,8},{26,120},{24,18},{34,... | collective-permute-start | bytes 2457608 | tf_op jit(solution)/shard_map/ppermute | solution.py:35
  55.0 0.9 copy-start.10
  55.9 37.1 %collective-permute-start.8 = (bf16[4,160,640]{2,1,0:T(8,128)(2,1)}, bf16[4,160,640]{2,1,0:T(8,128)(2,1)}, u32[]{:S(2)}, u32[]{:S(2)}) collective-permute-start(bf16[4,160,640]{2,1,0:T(8,128)(2,1)} %get-tuple-element.35), channel_id=1, source_target_pairs={{0,34},{2,8},{10,40},{8,18},{16,50},{18,24},{26,56},{24,2},{34,64}... | collective-permute-start | bytes 2457608 | tf_op jit(solution)/shard_map/ppermute | solution.py:35
  71.3 21.7 %collective-permute-start.9 = (bf16[4,160,640]{2,1,0:T(8,128)(2,1)}, bf16[4,160,640]{2,1,0:T(8,128)(2,1)}, u32[]{:S(2)}, u32[]{:S(2)}) collective-permute-start(bf16[4,160,640]{2,1,0:T(8,128)(2,1)} %get-tuple-element.36), channel_id=1, source_target_pairs={{0,64},{2,18},{10,74},{8,24},{16,80},{18,2},{26,90},{24,8},{34,98}... | collective-permute-start | bytes 2457608 | tf_op jit(solution)/shard_map/ppermute | solution.py:35
  71.3 1.1 copy-start.5
  72.4 1.1 copy-start.7
  73.6 1.1 copy-start.9
  74.7 1.1 copy-start.11
  75.9 8.5 %copy-start.3 = (bf16[4,160,640]{2,1,0:T(8,128)(2,1)S(1)}, bf16[4,160,640]{2,1,0:T(8,128)(2,1)}, u32[]{:S(2)}) copy-start(bf16[4,160,640]{2,1,0:T(8,128)(2,1)} %copy-done.2) | copy-start | bytes 2457604
  77.5 0.8 copy-start.12
  78.2 21.1 %collective-permute-start.19 = (bf16[80,1280]{1,0:T(8,128)(2,1)}, bf16[80,1280]{1,0:T(8,128)(2,1)S(1)}, u32[]{:S(2)}, u32[]{:S(2)}) collective-permute-start(bf16[80,1280]{1,0:T(8,128)(2,1)} %get-tuple-element.47), channel_id=1, source_target_pairs={{0,10},{2,32},{10,16},{8,42},{16,26},{18,48},{26,0},{24,58},{34,40... | collective-permute-start | bytes 614408 | tf_op jit(solution)/shard_map/ppermute | solution.py:35
  79.6 22.4 %collective-permute-start.20 = (bf16[80,1280]{1,0:T(8,128)(2,1)}, bf16[80,1280]{1,0:T(8,128)(2,1)}, u32[]{:S(2)}, u32[]{:S(2)}) collective-permute-start(bf16[80,1280]{1,0:T(8,128)(2,1)} %get-tuple-element.48), channel_id=1, source_target_pairs={{0,16},{2,66},{10,26},{8,72},{16,0},{18,82},{26,10},{24,88},{34,50... | collective-permute-start | bytes 614408 | tf_op jit(solution)/shard_map/ppermute | solution.py:35
  82.9 19.1 %collective-permute-start.21 = (bf16[80,1280]{1,0:T(8,128)(2,1)}, bf16[80,1280]{1,0:T(8,128)(2,1)}, u32[]{:S(2)}, u32[]{:S(2)}) collective-permute-start(bf16[80,1280]{1,0:T(8,128)(2,1)} %get-tuple-element.49), channel_id=1, source_target_pairs={{0,26},{2,96},{10,0},{8,106},{16,10},{18,112},{26,16},{24,122},{34... | collective-permute-start | bytes 614408 | tf_op jit(solution)/shard_map/ppermute | solution.py:35
  87.1 12.2 %copy-start.14 = (bf16[160,640]{1,0:T(8,128)(2,1)}, bf16[160,640]{1,0:T(8,128)(2,1)S(1)}, u32[]{:S(2)}) copy-start(bf16[160,640]{1,0:T(8,128)(2,1)S(1)} %get-tuple-element.31.refs_1_) | copy-start | bytes 614404
  93.0 11.5 %collective-permute-start.5 = (bf16[160,640]{1,0:T(8,128)(2,1)S(1)}, bf16[160,640]{1,0:T(8,128)(2,1)S(1)}, u32[]{:S(2)}, u32[]{:S(2)}) collective-permute-start(bf16[160,640]{1,0:T(8,128)(2,1)S(1)} %get-tuple-element.31.refs_1_), channel_id=1, source_target_pairs={{0,10},{2,32},{10,16},{8,42},{16,26},{18,48},{26,0},{24,58},{34,40... | collective-permute-start | bytes 614408 | tf_op jit(solution)/shard_map/ppermute | solution.py:35
  93.0 13.2 %collective-permute-start.6 = (bf16[160,640]{1,0:T(8,128)(2,1)S(1)}, bf16[160,640]{1,0:T(8,128)(2,1)S(1)}, u32[]{:S(2)}, u32[]{:S(2)}) collective-permute-start(bf16[160,640]{1,0:T(8,128)(2,1)S(1)} %get-tuple-element.32), channel_id=1, source_target_pairs={{0,16},{2,66},{10,26},{8,72},{16,0},{18,82},{26,10},{24,88},{34,50... | collective-permute-start | bytes 614408 | tf_op jit(solution)/shard_map/ppermute | solution.py:35
  96.5 6.8 %copy-start.13 = (f32[80,1280]{1,0:T(8,128)S(1)}, f32[80,1280]{1,0:T(8,128)}, u32[]{:S(2)}) copy-start(f32[80,1280]{1,0:T(8,128)} %copy-done.12) | copy-start | bytes 1228804
  99.3 10.5 %copy-start.15 = (bf16[160,640]{1,0:T(8,128)(2,1)}, bf16[160,640]{1,0:T(8,128)(2,1)S(1)}, u32[]{:S(2)}) copy-start(bf16[160,640]{1,0:T(8,128)(2,1)S(1)} %get-tuple-element.39.refs_1_) | copy-start | bytes 614404
  99.3 8.1 %collective-permute-start.7 = (bf16[160,640]{1,0:T(8,128)(2,1)S(1)}, bf16[160,640]{1,0:T(8,128)(2,1)S(1)}, u32[]{:S(2)}, u32[]{:S(2)}) collective-permute-start(bf16[160,640]{1,0:T(8,128)(2,1)S(1)} %get-tuple-element.33), channel_id=1, source_target_pairs={{0,26},{2,96},{10,0},{8,106},{16,10},{18,112},{26,16},{24,122},{34... | collective-permute-start | bytes 614408 | tf_op jit(solution)/shard_map/ppermute | solution.py:35
  102.0 8.9 %collective-permute-start.11 = (bf16[160,640]{1,0:T(8,128)(2,1)S(1)}, bf16[160,640]{1,0:T(8,128)(2,1)S(1)}, u32[]{:S(2)}, u32[]{:S(2)}) collective-permute-start(bf16[160,640]{1,0:T(8,128)(2,1)S(1)} %get-tuple-element.39.refs_1_), channel_id=1, source_target_pairs={{0,10},{2,32},{10,16},{8,42},{16,26},{18,48},{26,0},{24,58},{34,40... | collective-permute-start | bytes 614408 | tf_op jit(solution)/shard_map/ppermute | solution.py:35
  102.0 12.1 %collective-permute-start.12 = (bf16[160,640]{1,0:T(8,128)(2,1)S(1)}, bf16[160,640]{1,0:T(8,128)(2,1)S(1)}, u32[]{:S(2)}, u32[]{:S(2)}) collective-permute-start(bf16[160,640]{1,0:T(8,128)(2,1)S(1)} %get-tuple-element.40), channel_id=1, source_target_pairs={{0,16},{2,66},{10,26},{8,72},{16,0},{18,82},{26,10},{24,88},{34,50... | collective-permute-start | bytes 614408 | tf_op jit(solution)/shard_map/ppermute | solution.py:35
  104.5 9.6 %collective-permute-start.13 = (bf16[160,640]{1,0:T(8,128)(2,1)S(1)}, bf16[160,640]{1,0:T(8,128)(2,1)S(1)}, u32[]{:S(2)}, u32[]{:S(2)}) collective-permute-start(bf16[160,640]{1,0:T(8,128)(2,1)S(1)} %get-tuple-element.41), channel_id=1, source_target_pairs={{0,26},{2,96},{10,0},{8,106},{16,10},{18,112},{26,16},{24,122},{34... | collective-permute-start | bytes 614408 | tf_op jit(solution)/shard_map/ppermute | solution.py:35
  106.2 8.5 %collective-permute-start.22 = (f32[40,1280]{1,0:T(8,128)S(1)}, f32[40,1280]{1,0:T(8,128)S(1)}, u32[]{:S(2)}, u32[]{:S(2)}) collective-permute-start(f32[40,1280]{1,0:T(8,128)S(1)} %get-tuple-element.60), channel_id=1, source_target_pairs={{0,4},{4,0},{1,5},{5,1},{2,6},{6,2},{3,7},{7,3},{8,12},{12,8},{9,1... | collective-permute-start | bytes 614408 | tf_op jit(solution)/shard_map/ppermute | solution.py:23
  107.4 12.3 %collective-permute-start.24 = (f32[40,1280]{1,0:T(8,128)S(1)}, f32[40,1280]{1,0:T(8,128)S(1)}, u32[]{:S(2)}, u32[]{:S(2)}) collective-permute-start(f32[40,1280]{1,0:T(8,128)S(1)} %get-tuple-element.60), channel_id=1, source_target_pairs={{0,5},{1,4},{4,1},{5,0},{2,7},{3,6},{6,3},{7,2},{8,13},{9,12},{12,... | collective-permute-start | bytes 614408 | tf_op jit(solution)/shard_map/ppermute | solution.py:276
  110.9 8.8 %collective-permute-start.23 = (f32[40,1280]{1,0:T(8,128)S(1)}, f32[40,1280]{1,0:T(8,128)S(1)}, u32[]{:S(2)}, u32[]{:S(2)}) collective-permute-start(f32[40,1280]{1,0:T(8,128)S(1)} %get-tuple-element.61), channel_id=1, source_target_pairs={{0,1},{1,0},{2,3},{3,2},{4,5},{5,4},{6,7},{7,6},{8,9},{9,8},{10,11... | collective-permute-start | bytes 614408 | tf_op jit(solution)/shard_map/ppermute | solution.py:23
  114.3 14.4 %collective-permute-start.14 = (bf16[80,1280]{1,0:T(8,128)(2,1)S(1)}, bf16[80,1280]{1,0:T(8,128)(2,1)S(1)}, u32[]{:S(2)}, u32[]{:S(2)}) collective-permute-start(bf16[80,1280]{1,0:T(8,128)(2,1)S(1)} %fusion.11), channel_id=1, source_target_pairs={{0,4},{4,0},{1,5},{5,1},{2,6},{6,2},{3,7},{7,3},{8,12},{12,8},{9,1... | collective-permute-start | bytes 614408 | tf_op jit(solution)/shard_map/ppermute | solution.py:23
  125.8 6.2 %collective-permute-start.25 = (f32[40,1280]{1,0:T(8,128)S(1)}, f32[40,1280]{1,0:T(8,128)S(1)}, u32[]{:S(2)}, u32[]{:S(2)}) collective-permute-start(f32[40,1280]{1,0:T(8,128)S(1)} %slice_add_fusion.1), channel_id=1, source_target_pairs={{0,1},{1,0},{2,3},{3,2},{4,5},{5,4},{6,7},{7,6},{8,9},{9,8},{10,11... | collective-permute-start | bytes 614408 | tf_op jit(solution)/shard_map/ppermute | solution.py:23
  128.8 20.8 %collective-permute-start.15 = (f32[40,1280]{1,0:T(8,128)S(1)}, f32[40,1280]{1,0:T(8,128)S(1)}, u32[]{:S(2)}, u32[]{:S(2)}) collective-permute-start(f32[40,1280]{1,0:T(8,128)S(1)} %dynamic-slice_bitcast_fusion.2), channel_id=1, source_target_pairs={{0,2},{2,0},{1,3},{3,1},{4,6},{6,4},{5,7},{7,5},{8,10},{10,8},{9,1... | collective-permute-start | bytes 614408 | tf_op jit(solution)/shard_map/ppermute | solution.py:23
  139.4 21.1 %all-to-all-start = ((f32[64,1,1600]{2,1,0:T(1,128)}), f32[64,1,1600]{2,1,0:T(1,128)S(1)}, u32[]{:S(2)}, u32[]{:S(2)}) async-start(f32[64,1,1600]{2,1,0:T(1,128)} %reshape.50), calls=%async_computation | async-start | bytes 851968 | tf_op jit(solution)/shard_map/all_to_all | solution.py:295

commit v5 on v4

v5 whole, which is shorter than its diff:
```python
import functools

import jax
import jax.numpy as jnp
from jax import lax
from jax.experimental import pallas as pl
from jax.experimental.pallas import tpu as pltpu
from jax.sharding import Mesh, PartitionSpec as P

BF = jnp.bfloat16
F32 = jnp.float32
TILE = 640


def contract(first_rows, second_rows):
    return lax.dot_general(
        first_rows, second_rows, (((0,), (0,)), ((), ())), preferred_element_type=F32
    )


def shift(x, axis, step):
    size = lax.axis_size(axis)
    return lax.ppermute(x, axis, [(i, (i + step) % size) for i in range(size)])


def turn(x, step, stage):
    pairs = []
    for z in range(4):
        for y in range(4):
            for h in range(2):
                along_z = (h == 0) == (stage == 0)
                z2, y2 = ((z + step) % 4, y) if along_z else (z, (y + step) % 4)
                core, core2 = h ^ ((z + y) & 1), h ^ ((z2 + y2) & 1)
                pairs.append(((z * 4 + y) * 2 + core, (z2 * 4 + y2) * 2 + core2))
    return lax.ppermute(x, ("z", "y", "c"), pairs)


def pick(x, dim, index):
    return lax.dynamic_index_in_dim(x, index, dim, keepdims=False)


def split_pair(x):
    high = lax.reduce_precision(x, 8, 7)
    return high.astype(BF), (x - high).astype(BF)


def place_tile(place, buffer, sem, outs, m, zs):
    rows = TILE // (zs * 4)

    def start(at, out, slot):
        block = buffer.at[m, pl.ds(at, rows)]
        pltpu.make_async_copy(block, out.at[slot], sem).start()

    for a in range(zs):
        z = m * zs + a

        @pl.when(place[1] == 0)
        def _():
            for r, out in enumerate(outs):

                @pl.when(((z - place[2] + 4) & 3) == r)
                def _():
                    for k in range(4):
                        if isinstance(out, tuple):
                            start((a * 4 + k) * rows, out[k // 2], k % 2)
                        else:
                            start((a * 4 + k) * rows, out, k)

        @pl.when(place[1] == 1)
        def _():
            for r, out in enumerate(outs):
                at = pl.multiple_of((a * 4 + ((place[3] + r) & 3)) * rows, 16)
                if isinstance(out, tuple):
                    pl.when(z < 2)(functools.partial(start, at, out[0], z & 1))
                    pl.when(z >= 2)(functools.partial(start, at, out[1], z & 1))
                else:
                    start(at, out, z)


def wait_all(buffer, sem):
    pltpu.make_async_copy(buffer, buffer, sem).wait()


def own_kernel(place, a, b, out):
    out[...] = contract(a[...], b[...])


def cross_kernel(place, a, b, partial, own, ahead1, ahead2, ahead3, held, buffer, held_sems, sem):
    m = pl.program_id(0)

    @pl.when(m == 0)
    def _():
        for k in range(2):
            rows = partial.at[pl.ds(k * TILE, TILE)]
            pltpu.make_async_copy(rows, held.at[k], held_sems.at[k]).start()

    tile = contract(a[...], b[...])
    wait_all(held.at[m], held_sems.at[m])
    buffer[m] = (held[m] + tile).astype(BF)
    place_tile(place, buffer, sem, [own, ahead1, ahead2, ahead3], m, 2)
    pl.when(m == 1)(lambda: wait_all(buffer, sem))


def cross_term(place, grads, grads_next, acts, acts_next):
    tokens, half = grads_next.shape
    anywhere = pl.BlockSpec(memory_space=pl.ANY)
    cost = pl.CostEstimate(
        flops=2 * tokens * half * half, bytes_accessed=10 * tokens * half, transcendentals=0
    )
    partial = pl.pallas_call(
        own_kernel,
        out_shape=jax.ShapeDtypeStruct((half, half), F32),
        grid_spec=pltpu.PrefetchScalarGridSpec(
            num_scalar_prefetch=1,
            grid=(2,),
            in_specs=[
                pl.BlockSpec((tokens, TILE), lambda m, p: (0, p[1] * 2 + m)),
                pl.BlockSpec((tokens, half), lambda m, p: (0, p[1] ^ p[0])),
            ],
            out_specs=pl.BlockSpec((TILE, half), lambda m, p: (m, 0)),
        ),
        compiler_params=pltpu.CompilerParams(vmem_limit_bytes=32 * 2**20),
        cost_estimate=cost,
        name="cross_own",
    )(place, grads, acts)
    out = jax.ShapeDtypeStruct((4, half // 16, half), BF)
    return pl.pallas_call(
        cross_kernel,
        out_shape=[out] * 4,
        grid_spec=pltpu.PrefetchScalarGridSpec(
            num_scalar_prefetch=1,
            grid=(2,),
            in_specs=[
                pl.BlockSpec((tokens, TILE), lambda m, p: (0, m)),
                pl.BlockSpec((tokens, half), lambda m, p: (0, 0)),
                anywhere,
            ],
            out_specs=[anywhere] * 4,
            scratch_shapes=[
                pltpu.VMEM((2, TILE, half), F32),
                pltpu.VMEM((2, TILE, half), BF),
                pltpu.SemaphoreType.DMA((2,)),
                pltpu.SemaphoreType.DMA,
            ],
        ),
        compiler_params=pltpu.CompilerParams(vmem_limit_bytes=32 * 2**20),
        cost_estimate=cost,
        name="cross_term",
    )(place, grads_next, acts_next, partial)


def factor_kernel(place, h_own, g_own, h_next, g_next, x_next, *rest):
    own, right, far_a, far_b, left, lhs, rhs, buffer, lhs_sems, rhs_sem, sem = rest
    m = pl.program_id(0)
    half = rhs.shape[2]

    def lanes(step, wide):
        return pl.ds(pl.multiple_of(step * wide, wide), wide)

    def fetch(step, with_rhs):
        slot = step & 1

        def left_block(ref, k, at):
            pltpu.make_async_copy(ref.at[:, lanes(at, TILE)], lhs.at[slot, k], lhs_sems.at[slot]).start()

        for owner, (mine, theirs) in enumerate(((h_own, h_next), (g_own, g_next))):

            @pl.when(place[0] == owner)
            def _():
                left_block(mine, 0, step)
                pl.when((step >> 1) == place[1])(lambda: left_block(theirs, 1, step & 1))
                if with_rhs:
                    at = lanes(place[1], half)
                    pltpu.make_async_copy(mine.at[:, at], rhs.at[0], rhs_sem).start()
                    pltpu.make_async_copy(theirs, rhs.at[1], rhs_sem).start()

        pl.when((step >> 1) != place[1])(lambda: left_block(x_next, 1, step & 1))

    pl.when(m == 0)(lambda: fetch(0, True))
    pl.when(m < 3)(lambda: fetch(m + 1, False))
    slot = m & 1
    wait_all(lhs.at[slot], lhs_sems.at[slot])
    pl.when(m == 0)(lambda: wait_all(rhs, rhs_sem))

    buffer[m] = (contract(lhs[slot, 0], rhs[0]) + contract(lhs[slot, 1], rhs[1])).astype(BF)
    place_tile(place, buffer, sem, [own, right, (far_a, far_b), left], m, 1)
    pl.when(m == 3)(lambda: wait_all(buffer, sem))


def factor_term(place, acts, grads, acts_next, grads_next, rest_next):
    tokens, width = acts.shape
    half = width // 2
    anywhere = pl.BlockSpec(memory_space=pl.ANY)
    out = jax.ShapeDtypeStruct((4, width // 16, half), BF)
    side = jax.ShapeDtypeStruct((2, width // 16, half), BF)
    return pl.pallas_call(
        factor_kernel,
        out_shape=[out, out, side, side, out],
        grid_spec=pltpu.PrefetchScalarGridSpec(
            num_scalar_prefetch=1,
            grid=(4,),
            in_specs=[anywhere] * 5,
            out_specs=[anywhere] * 5,
            scratch_shapes=[
                pltpu.VMEM((2, 2, tokens, TILE), BF),
                pltpu.VMEM((2, tokens, half), BF),
                pltpu.VMEM((4, TILE, half), BF),
                pltpu.SemaphoreType.DMA((2,)),
                pltpu.SemaphoreType.DMA,
                pltpu.SemaphoreType.DMA,
            ],
        ),
        compiler_params=pltpu.CompilerParams(vmem_limit_bytes=40 * 2**20),
        cost_estimate=pl.CostEstimate(
            flops=4 * tokens * width * half, bytes_accessed=16 * tokens * half, transcendentals=0
        ),
        name="factor_term",
    )(place, acts, grads, acts_next, grads_next, rest_next)


def add(first, *rest):
    total = first.astype(F32)
    for x in rest:
        total = total + x.astype(F32)
    return total


def gate(x, *others):
    anywhere = pl.BlockSpec(memory_space=pl.ANY)
    return pl.pallas_call(
        lambda *refs: None,
        out_shape=jax.ShapeDtypeStruct(x.shape, x.dtype),
        in_specs=[anywhere] * (1 + len(others)),
        out_specs=anywhere,
        input_output_aliases={0: 0},
        name="gate",
    )(x, *others)


def fold_kernel(me, *refs):
    parts, (own, *others) = refs[:-4], refs[-4:]
    step = pl.program_id(0)
    total = add(*[part[0] for part in parts])

    @pl.when(step == 0)
    def _():
        own[...] = total

    for r, out in enumerate(others):

        @pl.when(step == r + 1)
        def _():
            out[...] = total.astype(BF)


def fold(me, parts):
    _, rows, width = parts[0].shape
    block = pl.BlockSpec((1, rows, width), lambda s, m: ((m[0] + s) & 3, 0, 0))
    whole = pl.BlockSpec((rows, width), lambda s, m: (0, 0))
    return pl.pallas_call(
        fold_kernel,
        out_shape=[jax.ShapeDtypeStruct((rows, width), t) for t in (F32, BF, BF, BF)],
        grid_spec=pltpu.PrefetchScalarGridSpec(
            num_scalar_prefetch=1, grid=(4,), in_specs=[block] * len(parts), out_specs=[whole] * 4
        ),
        compiler_params=pltpu.CompilerParams(vmem_limit_bytes=32 * 2**20),
        cost_estimate=pl.CostEstimate(
            flops=16 * rows * width, bytes_accessed=42 * rows * width, transcendentals=0
        ),
        name="fold",
    )(me, *parts)


def per_device(hidden, out_grad, left_inverse, right_inverse):
    z, y, xl, c, o = (lax.axis_index(n) for n in ("z", "y", "xl", "c", "o"))
    tokens, width = hidden.shape
    half = width // 2
    token_total = tokens * 64
    first = o == 0
    h = c ^ ((z + y) & 1)
    place = jnp.stack([o, h, z, y]).astype(jnp.int32)
    second_me = jnp.where(h == 0, y, z).astype(jnp.int32)[None]

    def columns(x, index):
        return lax.dynamic_slice_in_dim(x, index * half, half, 1)

    grads_next = shift(columns(out_grad, 1 - h), "c", 1)
    acts_next = shift(columns(hidden, (1 - h) ^ o), "c", 1)
    rest_next = shift(jnp.where(first, columns(hidden, h), columns(out_grad, h)), "c", 1)

    own, m1, m2, m3 = cross_term(place, out_grad, grads_next, hidden, acts_next)
    m_parts = [own, turn(m1, 1, 0), turn(m2, 2, 0), turn(m3, 3, 0)]

    f_own, right, far_a, far_b, left = factor_term(
        place, hidden, out_grad, acts_next, grads_next, rest_next
    )

    def second_round(parts):
        total, *pieces = fold(second_me, parts)
        return pieces[0], add(total, *[turn(piece, s, 1) for s, piece in enumerate(pieces, 1)])

    m_parts[0] = gate(m_parts[0], f_own)
    from_left, from_right = turn(far_a, 1, 0), turn(far_b, -1, 0)
    right = jnp.concatenate([add(right[:2], from_left).astype(BF), right[2:]])
    left = jnp.concatenate([left[:2], add(left[2:], from_right).astype(BF)])
    f_parts = [f_own, turn(right, 1, 0), turn(left, -1, 0)]

    _, m = second_round(m_parts)
    m = m.reshape(2, half // 32, half)
    mine, theirs = pick(m, 0, xl), pick(m, 0, 1 - xl)
    m_own = mine + shift(theirs, "xl", 1)
    partner = shift(mine, "o", 1) + lax.ppermute(
        theirs, ("xl", "o"), [(i, 3 - i) for i in range(4)]
    )
    swap = (h ^ o) == 0
    mrow = jnp.concatenate(
        [jnp.where(swap, m_own, partner), jnp.where(swap, partner, m_own)], axis=1
    )
    rows = mrow.shape[0]
    stacked = jnp.concatenate(split_pair(mrow))
    pt = jnp.dot(stacked, left_inverse, preferred_element_type=F32)
    pt = pt[:rows] + pt[rows:]
    blocks = pt.reshape(rows, 2, 4, 2, 2, rows).transpose(4, 1, 2, 3, 0, 5)
    blocks = jnp.broadcast_to(blocks[None, :, None], (2, 2, 2, 2, 4, 2, rows, rows))
    blocks = lax.all_to_all(
        blocks.reshape(128, rows, rows), ("o", "c", "z", "y", "xl"), 0, 0, tiled=True
    )

    late, f = second_round(f_parts)
    blocks = pick(blocks.reshape(2, 64, rows, rows), 0, z >> 1)
    blocks = gate(blocks, late)
    blocks = blocks.reshape(2, 4, 4, 2, rows, rows)
    odd = ((jnp.arange(4)[:, None] + jnp.arange(4)) & 1).reshape(1, 4, 4, 1, 1, 1) == 1
    blocks = jnp.where(odd, blocks[::-1], blocks).reshape(width, rows)
    stacked = jnp.concatenate(split_pair(blocks), axis=1)
    update = contract(stacked, right_inverse)
    update = update[:rows] + update[rows:]

    f = f.reshape(2, width // 32, half)
    f = pick(f, 0, xl) + shift(pick(f, 0, 1 - xl).astype(BF), "xl", 1).astype(F32)
    f = f * jnp.where(first, 1.0 / token_total, 1.0).astype(F32)
    f = f.reshape(2, width // 64, half)
    mine = pick(f, 0, c)
    theirs = shift(pick(f, 0, 1 - c), "c", 1)
    factors = jnp.concatenate(
        [jnp.where(h == 0, mine, theirs), jnp.where(h == 0, theirs, mine)], axis=1
    )[None]
    return factors, update


def solution(mesh):
    fine = Mesh(mesh.devices.reshape(4, 4, 2, 2, 2), ("z", "y", "xl", "c", "o"))
    dp = ("z", "y", "xl", "c")
    in_specs = (P(dp, None), P(dp, None), P(None, "o"), P(None, "o"))
    out_specs = (P("o", dp, None), P(dp, "o"))
    return jax.shard_map(
        per_device, mesh=fine, in_specs=in_specs, out_specs=out_specs, check_vma=False
    )
```

time: 169 us -> 154 us (0.911)
  starting transfers between devices: 49.1 us -> 35.2 us
  other arithmetic: 7.04 us -> 18.2 us
  Pallas kernels: 42.3 us -> 32.8 us
  local copies, waits for them, and re-layouts: 20.5 us -> 23.9 us
  waiting for transfers between devices: 40.3 us -> 37.3 us
  matrix products: 8.13 us -> 5.27 us
    ppermute x18 -> x13, waiting for transfers between devices: 21.5 us -> 8.03 us  [turn(): return lax.ppermute(x, ('z', 'y', 'c'), pairs)]
    all_to_all x1, waiting for transfers between devices: 10.1 us -> 17 us  [per_device(): lax.all_to_all(blocks.reshape(128, rows, rows), ('o', 'c', 'z', 'y', 'xl'...]
    ppermute x18 -> x13, starting transfers between devices: 25.8 us -> 20.3 us  [turn(): return lax.ppermute(x, ('z', 'y', 'c'), pairs)]
    ppermute x7, starting transfers between devices: 10.8 us -> 5.45 us  [shift(): return lax.ppermute(x, axis, [(i, (i + step) % size) for i in range(size)])]
    pallas_call x1, Pallas kernels: 12 us -> 7.18 us  [cross_term(): pl.pallas_call(cross_kernel, out_shape=[out] * 4, grid_spec=pltpu.Prefetc...]
    pallas_call x1, Pallas kernels: 8.04 us -> 3.9 us  [cross_term(): pl.pallas_call(own_kernel, out_shape=jax.ShapeDtypeStruct((half, half), F...]
    select_n x1, other arithmetic: 0.06 us -> 3.92 us  [per_device(): jnp.where(first, columns(hidden, h), columns(out_grad, h))]
    all_to_all x1, other arithmetic: 1.65 us -> 4.73 us  [per_device(): lax.all_to_all(blocks.reshape(128, rows, rows), ('o', 'c', 'z', 'y', 'xl'...]
  transfers between devices with their start and end apart: 27 -> 22, of which waited for: 7 -> 10; matrix products, arithmetic and copies ran while one was open for 9% -> 24% of each run, Pallas kernels for 18% -> 20%
where the time goes in v5:
time: 154 us
  waiting for transfers between devices  37.3 us (24%)
  starting transfers between devices  35.2 us (23%)
  Pallas kernels  32.8 us (21%)
  local copies, waits for them, and re-layouts  23.9 us (16%)
  other arithmetic  18.2 us (12%)
  matrix products  5.27 us (3%)
    ppermute x13, starting transfers between devices, turn(): return lax.ppermute(x, ('z', 'y', 'c'), pairs)  20.3 us
    all_to_all x1, waiting for transfers between devices, per_device(): lax.all_to_all(blocks.reshape(128, rows, rows), ('o', 'c', 'z', 'y', 'xl'...  17 us
    pallas_call x1, Pallas kernels, factor_term(): pl.pallas_call(factor_kernel, out_shape=[out, out, side, side, out], grid...  16.8 us
    unnamed x34, local copies, waits for them, and re-layouts  13.4 us
    ppermute x7, waiting for transfers between devices, shift(): return lax.ppermute(x, axis, [(i, (i + step) % size) for i in range(size)])  11.6 us
    ppermute x13, waiting for transfers between devices, turn(): return lax.ppermute(x, ('z', 'y', 'c'), pairs)  8.03 us
    all_to_all x1, starting transfers between devices, per_device(): lax.all_to_all(blocks.reshape(128, rows, rows), ('o', 'c', 'z', 'y', 'xl'...  7.69 us
    pallas_call x1, Pallas kernels, cross_term(): pl.pallas_call(cross_kernel, out_shape=[out] * 4, grid_spec=pltpu.Prefetc...  7.18 us
  transfers between devices with their start and end apart: 22, of which 10 were waited for; matrix products, arithmetic and copies ran while one was open for 24% of the time, Pallas kernels for 20%

profile of v5, /device:TPU:1, one launch (start us, length us, event | category | flops | bytes accessed | tf_op | source)
XLA Modules:
  0.0 153.7 jit_solution(15505294930819320393)
XLA Ops:
  0.7 3.9 %dynamic-slice_select_fusion = (bf16[768,1280]{1,0:T(8,128)(2,1)S(1)}, bf16[768,1280]{1,0:T(8,128)(2,1)S(1)}, bf16[768,1280]{1,0:T(8,128)(2,1)S(1)}) fusion(bf16[768,2560]{1,0:T(8,128)(2,1)} %a.1, s32[]{:T(128)S(6)} %select_n.77, bf16[768,2560]{1,0:T(8,128)(2,1)} %b.1, pred[]{:T(512)S(6)} %eq.20, s32[]{:T(128)S(6)} %select_n.74, s32[]{:T(128)S(6)} %select_n.75), kind=kLoop, calls=%fused_computation.1 | loop fusion | flops 983040 | bytes 13762573 | tf_op jit(solution)/shard_map/jit(_where)/select_n | solution.py:289
  4.6 1.5 collective-permute-start
  6.7 3.9 %cross_own.1.partial = f32[1280,1280]{1,0:T(8,128)S(1)} custom-call(s32[4]{0:T(128)S(1)} %pad_add_fusion.place, bf16[768,2560]{1,0:T(8,128)(2,1)S(1)} %copy-done.1, bf16[768,2560]{1,0:T(8,128)(2,1)S(1)} %copy-done), custom_call_target="tpu_custom_call" | custom-call | flops 2516582400 | bytes 9830400 | tf_op jit(solution)/shard_map/cross_own/pallas_call | solution.py:110
  10.6 1.9 %collective-permute-done.1.g_next.a = bf16[768,1280]{1,0:T(8,128)(2,1)S(1)} collective-permute-done((bf16[768,1280]{1,0:T(8,128)(2,1)S(1)}, bf16[768,1280]{1,0:T(8,128)(2,1)S(1)}, u32[]{:S(2)}, u32[]{:S(2)}) %collective-permute-start.1) | collective-permute-done | bytes 1966112 | tf_op jit(solution)/shard_map/ppermute | solution.py:23
  12.5 7.2 %cross_term.1 = (bf16[4,80,1280]{2,1,0:T(8,128)(2,1)S(1)}, bf16[4,80,1280]{2,1,0:T(8,128)(2,1)}, bf16[4,80,1280]{2,1,0:T(8,128)(2,1)}, bf16[4,80,1280]{2,1,0:T(8,128)(2,1)}) custom-call(s32[4]{0:T(128)S(1)} %pad_add_fusion.place, bf16[768,1280]{1,0:T(8,128)(2,1)S(1)} %collective-permute-done.1.g_next.a, bf16[768,1280]{1,0:T(8,128)(2,1)S(1)} %collective-permute-done.h_next.b, ...), custom_call_target="tpu_custom_call" | custom-call | flops 2516582400 | bytes 9830400 | tf_op jit(solution)/shard_map/cross_term/pallas_call | solution.py:127
  19.7 0.9 copy-done.4
  20.6 1.6 %collective-permute-start.12 = (bf16[4,80,1280]{2,1,0:T(8,128)(2,1)}, bf16[4,80,1280]{2,1,0:T(8,128)(2,1)}, u32[]{:S(2)}, u32[]{:S(2)}) collective-permute-start(bf16[4,80,1280]{2,1,0:T(8,128)(2,1)} %get-tuple-element.29), channel_id=1, source_target_pairs={{0,34},{2,8},{10,40},{8,18},{16,50},{18,24},{26,56},{24,2},{34,64}... | collective-permute-start | bytes 2457608 | tf_op jit(solution)/shard_map/ppermute | solution.py:35
  22.3 2.6 %collective-permute-start.13 = (bf16[4,80,1280]{2,1,0:T(8,128)(2,1)}, bf16[4,80,1280]{2,1,0:T(8,128)(2,1)}, u32[]{:S(2)}, u32[]{:S(2)}) collective-permute-start(bf16[4,80,1280]{2,1,0:T(8,128)(2,1)} %get-tuple-element.30), channel_id=1, source_target_pairs={{0,64},{2,18},{10,74},{8,24},{16,80},{18,2},{26,90},{24,8},{34,98}... | collective-permute-start | bytes 2457608 | tf_op jit(solution)/shard_map/ppermute | solution.py:35
  24.9 1.4 collective-permute-start.14
  26.3 16.8 %factor_term.1 = (bf16[4,160,1280]{2,1,0:T(8,128)(2,1)S(1)}, bf16[4,160,1280]{2,1,0:T(8,128)(2,1)S(1)}, bf16[2,160,1280]{2,1,0:T(8,128)(2,1)}, bf16[2,160,1280]{2,1,0:T(8,128)(2,1)}, bf16[4,160,1280]{2,1,0:T(8,128)(2,1)S(1)}) custom-call(s32[4]{0:T(128)S(1)} %pad_add_fusion.place, bf16[768,2560]{1,0:T(8,128)(2,1)} %b.1, bf16[768,2560]{1,0:T(8,128)(2,1)} %a.1, ...), custom_call_target="tpu_custom_call" | custom-call | flops 10066329600 | bytes 15728640 | tf_op jit(solution)/shard_map/factor_term/pallas_call | solution.py:196
  43.1 1.2 copy-done.2
  44.3 1.0 slice.26
  45.3 1.7 %collective-permute-start.3 = (bf16[2,160,1280]{2,1,0:T(8,128)(2,1)}, bf16[2,160,1280]{2,1,0:T(8,128)(2,1)}, u32[]{:S(2)}, u32[]{:S(2)}) collective-permute-start(bf16[2,160,1280]{2,1,0:T(8,128)(2,1)} %get-tuple-element.21), channel_id=1, source_target_pairs={{0,34},{2,8},{10,40},{8,18},{16,50},{18,24},{26,56},{24,2},{34,64}... | collective-permute-start | bytes 2457608 | tf_op jit(solution)/shard_map/ppermute | solution.py:35
  47.0 1.0 slice.25
  48.0 1.1 copy-done.5
  49.1 2.9 %fold.3 = (f32[80,1280]{1,0:T(8,128)S(1)}, bf16[80,1280]{1,0:T(8,128)(2,1)S(1)}, bf16[80,1280]{1,0:T(8,128)(2,1)S(1)}, bf16[80,1280]{1,0:T(8,128)(2,1)S(1)}) custom-call(s32[1]{0:T(128)} %bitcast.me, bf16[4,80,1280]{2,1,0:T(8,128)(2,1)S(1)} %copy-done.5, bf16[4,80,1280]{2,1,0:T(8,128)(2,1)} %collective-permute-done.12.refs_1_, ...), custom_call_target="tpu_custom_call" | custom-call | flops 1638400 | bytes 4300800 | tf_op jit(solution)/shard_map/fold/pallas_call | solution.py:260
  52.0 1.7 %collective-permute-start.15 = (bf16[80,1280]{1,0:T(8,128)(2,1)S(1)}, bf16[80,1280]{1,0:T(8,128)(2,1)S(1)}, u32[]{:S(2)}, u32[]{:S(2)}) collective-permute-start(bf16[80,1280]{1,0:T(8,128)(2,1)S(1)} %get-tuple-element.33), channel_id=1, source_target_pairs={{0,10},{2,32},{10,16},{8,42},{16,26},{18,48},{26,0},{24,58},{34,40... | collective-permute-start | bytes 614408 | tf_op jit(solution)/shard_map/ppermute | solution.py:35
  53.7 3.3 %collective-permute-start.16 = (bf16[80,1280]{1,0:T(8,128)(2,1)S(1)}, bf16[80,1280]{1,0:T(8,128)(2,1)S(1)}, u32[]{:S(2)}, u32[]{:S(2)}) collective-permute-start(bf16[80,1280]{1,0:T(8,128)(2,1)S(1)} %get-tuple-element.34), channel_id=1, source_target_pairs={{0,16},{2,66},{10,26},{8,72},{16,0},{18,82},{26,10},{24,88},{34,50... | collective-permute-start | bytes 614408 | tf_op jit(solution)/shard_map/ppermute | solution.py:35
  57.0 1.3 collective-permute-start.17
  58.3 1.3 add_convert_fusion
  59.7 1.3 pad_maximum_fusion.1
  61.0 0.9 collective-permute-start.6
  61.9 1.0 collective-permute-done.3
  63.0 1.3 add_convert_fusion.1
  64.5 1.3 collective-permute-start.18
  65.8 1.8 %collective-permute-start.20 = (f32[40,1280]{1,0:T(8,128)S(1)}, f32[40,1280]{1,0:T(8,128)S(1)}, u32[]{:S(2)}, u32[]{:S(2)}) collective-permute-start(f32[40,1280]{1,0:T(8,128)S(1)} %get-tuple-element.47), channel_id=1, source_target_pairs={{0,5},{1,4},{4,1},{5,0},{2,7},{3,6},{6,3},{7,2},{8,13},{9,12},{12,... | collective-permute-start | bytes 614408 | tf_op jit(solution)/shard_map/ppermute | solution.py:312
  68.2 1.3 pad_maximum_fusion
  70.3 1.3 collective-permute-done.18
  71.6 5.9 %collective-permute-done.19 = f32[40,1280]{1,0:T(8,128)S(1)} collective-permute-done((f32[40,1280]{1,0:T(8,128)S(1)}, f32[40,1280]{1,0:T(8,128)S(1)}, u32[]{:S(2)}, u32[]{:S(2)}) %collective-permute-start.19) | collective-permute-done | bytes 204832 | tf_op jit(solution)/shard_map/ppermute | solution.py:23
  78.4 1.3 fusion.6
  79.7 2.0 %reshape.50 = f32[40,2,4,2,2,40]{5,4,3,2,1,0:T(2,128)} reshape(f32[40,1280]{1,0:T(8,128)S(1)} %slice_add_fusion.1) | data formatting | bytes 409600 | tf_op jit(solution)/shard_map/reshape | solution.py:323
  81.7 1.5 copy.8
  83.2 1.8 %broadcast_in_dim.25 = f32[2,2,2,2,4,2,40,40]{7,6,5,4,3,2,1,0:T(8,128)} broadcast(f32[2,2,4,2,40,40]{5,4,3,2,1,0:T(8,128)S(1)} %copy.8), dimensions={1,3,4,5,6,7} | broadcast | bytes 1024000 | tf_op jit(solution)/shard_map/broadcast_in_dim | solution.py:324
  85.0 4.4 %reshape.55 = f32[128,1,1600]{2,1,0:T(1,128)} reshape(f32[128,40,40]{2,1,0:T(8,128)} %bitcast.37) | data formatting | bytes 1638400
  89.4 7.7 %all-to-all-start = ((f32[128,1,1600]{2,1,0:T(1,128)}), f32[128,1,1600]{2,1,0:T(1,128)}, u32[]{:S(2)}, u32[]{:S(2)}) async-start(f32[128,1,1600]{2,1,0:T(1,128)} %reshape.55), calls=%async_computation | async-start | bytes 1703936 | tf_op jit(solution)/shard_map/all_to_all | solution.py:325
  97.2 17.0 %all-to-all-done = f32[128,1,1600]{2,1,0:T(1,128)} async-done(((f32[128,1,1600]{2,1,0:T(1,128)}), f32[128,1,1600]{2,1,0:T(1,128)}, u32[]{:S(2)}, u32[]{:S(2)}) %all-to-all-start) | async-done | bytes 819232 | tf_op jit(solution)/shard_map/all_to_all | solution.py:325
  114.6 4.7 %reduce = f32[128,1600]{1,0:T(8,128)} reduce(f32[128,1,1600]{2,1,0:T(1,128)} %all-to-all-done, f32[]{:T(128)} %broadcast.22), dimensions={1}, to_apply=%all_to_all.3.reduce_sub_computation | reduce | bytes 1638404 | tf_op jit(solution)/shard_map/all_to_all | solution.py:325
  119.4 3.3 %reshape.56 = f32[128,40,40]{2,1,0:T(8,128)} reshape(f32[128,1600]{1,0:T(8,128)} %reduce) | data formatting | bytes 1638400
  122.6 2.6 %dynamic-slice_bitcast_fusion.refs_0_ = f32[64,40,40]{2,1,0:T(8,128)} fusion(f32[2,64,40,40]{3,2,1,0:T(8,128)} %bitcast.40, s32[]{:T(128)S(6)} %select_n.89), kind=kLoop, calls=%fused_computation.9 | loop fusion | bytes 819204 | tf_op jit(solution)/shard_map/jit(dynamic_index_in_dim)/squeeze | solution.py:39
  125.2 2.0 %fold.2 = (f32[160,1280]{1,0:T(8,128)S(1)}, bf16[160,1280]{1,0:T(8,128)(2,1)}, bf16[160,1280]{1,0:T(8,128)(2,1)S(1)}, bf16[160,1280]{1,0:T(8,128)(2,1)S(1)}) custom-call(s32[1]{0:T(128)} %bitcast.me, bf16[4,160,1280]{2,1,0:T(8,128)(2,1)S(1)} %copy-done.3, bf16[4,160,1280]{2,1,0:T(8,128)(2,1)S(1)} %collective-permute-done.4.refs_1_, ...), custom_call_target="tpu_custom_call" | custom-call | flops 3276800 | bytes 8601600 | tf_op jit(solution)/shard_map/fold/pallas_call | solution.py:260
  127.2 0.9 copy-done.6
  129.7 1.3 collective-permute-start.7
  131.8 2.9 %collective-permute-start.9 = (bf16[160,1280]{1,0:T(8,128)(2,1)S(1)}, bf16[160,1280]{1,0:T(8,128)(2,1)S(1)}, u32[]{:S(2)}, u32[]{:S(2)}) collective-permute-start(bf16[160,1280]{1,0:T(8,128)(2,1)S(1)} %copy-done.9), channel_id=1, source_target_pairs={{0,26},{2,96},{10,0},{8,106},{16,10},{18,112},{26,16},{24,122},{34... | collective-permute-start | bytes 1228808 | tf_op jit(solution)/shard_map/ppermute | solution.py:35
  134.7 1.9 %reverse_select_fusion = f32[2,4,4,2,40,40]{5,4,3,2,1,0:T(8,128)S(1)} fusion(f32[2,4,4,2,40,40]{5,4,3,2,1,0:T(8,128)} %bitcast.36, pred[4,4]{1,0:T(4,128)(4,1)S(1)} %and_compare_fusion), kind=kLoop, calls=%fused_computation | loop fusion | flops 102400 | bytes 819216 | tf_op jit(solution)/shard_map/jit(_where)/select_n | solution.py:334
  136.8 6.3 %collective-permute-done.7 = bf16[160,1280]{1,0:T(8,128)(2,1)S(1)} collective-permute-done((bf16[160,1280]{1,0:T(8,128)(2,1)}, bf16[160,1280]{1,0:T(8,128)(2,1)S(1)}, u32[]{:S(2)}, u32[]{:S(2)}) %collective-permute-start.7) | collective-permute-done | bytes 409632 | tf_op jit(solution)/shard_map/ppermute | solution.py:35
  144.2 4.0 %fusion.1 = f32[80,1280]{1,0:T(8,128)S(1)} fusion(bf16[2560,1280]{1,0:T(8,128)(2,1)} %param.7, bf16[2560,40]{1,0:T(8,128)(2,1)S(1)} %get-tuple-element.40, bf16[2560,40]{1,0:T(8,128)(2,1)S(1)} %get-tuple-element.39), kind=kOutput, calls=%fused_computation.11 | convolution fusion | flops 525107200 | bytes 7372800 | tf_op jit(solution)/shard_map/dot_general | solution.py:16
  148.3 2.1 %collective-permute-done.10 = bf16[80,1280]{1,0:T(8,128)(2,1)S(1)} collective-permute-done((bf16[80,1280]{1,0:T(8,128)(2,1)S(1)}, bf16[80,1280]{1,0:T(8,128)(2,1)S(1)}, u32[]{:S(2)}, u32[]{:S(2)}) %collective-permute-start.10) | collective-permute-done | bytes 204832 | tf_op jit(solution)/shard_map/ppermute | solution.py:23
  150.5 1.3 collective-permute-start.11
  (69 shorter events, 9.2 us)
Async XLA Ops:
  0.7 6.0 %copy-start = (bf16[768,2560]{1,0:T(8,128)(2,1)S(1)}, bf16[768,2560]{1,0:T(8,128)(2,1)}, u32[]{:S(2)}) copy-start(bf16[768,2560]{1,0:T(8,128)(2,1)} %b.1) | copy-start | bytes 11796484
  0.7 6.0 %copy-start.1 = (bf16[768,2560]{1,0:T(8,128)(2,1)S(1)}, bf16[768,2560]{1,0:T(8,128)(2,1)}, u32[]{:S(2)}) copy-start(bf16[768,2560]{1,0:T(8,128)(2,1)} %a.1) | copy-start | bytes 11796484
  4.6 6.0 %collective-permute-start = (bf16[768,1280]{1,0:T(8,128)(2,1)S(1)}, bf16[768,1280]{1,0:T(8,128)(2,1)S(1)}, u32[]{:S(2)}, u32[]{:S(2)}) collective-permute-start(bf16[768,1280]{1,0:T(8,128)(2,1)S(1)} %get-tuple-element.37), channel_id=1, source_target_pairs={{0,2},{2,0},{1,3},{3,1},{4,6},{6,4},{5,7},{7,5},{8,10},{10,8},{9,1... | collective-permute-start | bytes 5898248 | tf_op jit(solution)/shard_map/ppermute | solution.py:23
  6.1 6.4 %collective-permute-start.1 = (bf16[768,1280]{1,0:T(8,128)(2,1)S(1)}, bf16[768,1280]{1,0:T(8,128)(2,1)S(1)}, u32[]{:S(2)}, u32[]{:S(2)}) collective-permute-start(bf16[768,1280]{1,0:T(8,128)(2,1)S(1)} %get-tuple-element.38), channel_id=1, source_target_pairs={{0,2},{2,0},{1,3},{3,1},{4,6},{6,4},{5,7},{7,5},{8,10},{10,8},{9,1... | collective-permute-start | bytes 5898248 | tf_op jit(solution)/shard_map/ppermute | solution.py:23
  6.2 20.1 %collective-permute-start.2 = (bf16[768,1280]{1,0:T(8,128)(2,1)S(1)}, bf16[768,1280]{1,0:T(8,128)(2,1)S(1)}, u32[]{:S(2)}, u32[]{:S(2)}) collective-permute-start(bf16[768,1280]{1,0:T(8,128)(2,1)S(1)} %get-tuple-element.36), channel_id=1, source_target_pairs={{0,2},{2,0},{1,3},{3,1},{4,6},{6,4},{5,7},{7,5},{8,10},{10,8},{9,1... | collective-permute-start | bytes 5898248 | tf_op jit(solution)/shard_map/ppermute | solution.py:23
  19.7 0.9 copy-start.4
  20.6 27.3 %collective-permute-start.12 = (bf16[4,80,1280]{2,1,0:T(8,128)(2,1)}, bf16[4,80,1280]{2,1,0:T(8,128)(2,1)}, u32[]{:S(2)}, u32[]{:S(2)}) collective-permute-start(bf16[4,80,1280]{2,1,0:T(8,128)(2,1)} %get-tuple-element.29), channel_id=1, source_target_pairs={{0,34},{2,8},{10,40},{8,18},{16,50},{18,24},{26,56},{24,2},{34,64}... | collective-permute-start | bytes 2457608 | tf_op jit(solution)/shard_map/ppermute | solution.py:35
  22.3 25.7 %collective-permute-start.13 = (bf16[4,80,1280]{2,1,0:T(8,128)(2,1)}, bf16[4,80,1280]{2,1,0:T(8,128)(2,1)}, u32[]{:S(2)}, u32[]{:S(2)}) collective-permute-start(bf16[4,80,1280]{2,1,0:T(8,128)(2,1)} %get-tuple-element.30), channel_id=1, source_target_pairs={{0,64},{2,18},{10,74},{8,24},{16,80},{18,2},{26,90},{24,8},{34,98}... | collective-permute-start | bytes 2457608 | tf_op jit(solution)/shard_map/ppermute | solution.py:35
  24.9 23.1 %collective-permute-start.14 = (bf16[4,80,1280]{2,1,0:T(8,128)(2,1)}, bf16[4,80,1280]{2,1,0:T(8,128)(2,1)}, u32[]{:S(2)}, u32[]{:S(2)}) collective-permute-start(bf16[4,80,1280]{2,1,0:T(8,128)(2,1)} %get-tuple-element.31), channel_id=1, source_target_pairs={{0,98},{2,24},{10,104},{8,2},{16,114},{18,8},{26,120},{24,18},{34,... | collective-permute-start | bytes 2457608 | tf_op jit(solution)/shard_map/ppermute | solution.py:35
  43.1 1.2 copy-start.2
  44.3 14.0 %collective-permute-start.5 = (bf16[2,160,1280]{2,1,0:T(8,128)(2,1)}, bf16[2,160,1280]{2,1,0:T(8,128)(2,1)}, u32[]{:S(2)}, u32[]{:S(2)}) collective-permute-start(bf16[2,160,1280]{2,1,0:T(8,128)(2,1)} %get-tuple-element.23), channel_id=1, source_target_pairs={{0,98},{2,24},{10,104},{8,2},{16,114},{18,8},{26,120},{24,18},{34,... | collective-permute-start | bytes 2457608 | tf_op jit(solution)/shard_map/ppermute | solution.py:35
  45.3 17.7 %collective-permute-start.3 = (bf16[2,160,1280]{2,1,0:T(8,128)(2,1)}, bf16[2,160,1280]{2,1,0:T(8,128)(2,1)}, u32[]{:S(2)}, u32[]{:S(2)}) collective-permute-start(bf16[2,160,1280]{2,1,0:T(8,128)(2,1)} %get-tuple-element.21), channel_id=1, source_target_pairs={{0,34},{2,8},{10,40},{8,18},{16,50},{18,24},{26,56},{24,2},{34,64}... | collective-permute-start | bytes 2457608 | tf_op jit(solution)/shard_map/ppermute | solution.py:35
  48.0 1.1 copy-start.5
  52.0 7.6 %copy-start.13 = (bf16[2,160,1280]{2,1,0:T(8,128)(2,1)S(1)}, bf16[2,160,1280]{2,1,0:T(8,128)(2,1)}, u32[]{:S(2)}) copy-start(bf16[2,160,1280]{2,1,0:T(8,128)(2,1)} %slice.26) | copy-start | bytes 2457604
  52.0 12.3 %collective-permute-start.15 = (bf16[80,1280]{1,0:T(8,128)(2,1)S(1)}, bf16[80,1280]{1,0:T(8,128)(2,1)S(1)}, u32[]{:S(2)}, u32[]{:S(2)}) collective-permute-start(bf16[80,1280]{1,0:T(8,128)(2,1)S(1)} %get-tuple-element.33), channel_id=1, source_target_pairs={{0,10},{2,32},{10,16},{8,42},{16,26},{18,48},{26,0},{24,58},{34,40... | collective-permute-start | bytes 614408 | tf_op jit(solution)/shard_map/ppermute | solution.py:35
  53.7 10.6 %collective-permute-start.16 = (bf16[80,1280]{1,0:T(8,128)(2,1)S(1)}, bf16[80,1280]{1,0:T(8,128)(2,1)S(1)}, u32[]{:S(2)}, u32[]{:S(2)}) collective-permute-start(bf16[80,1280]{1,0:T(8,128)(2,1)S(1)} %get-tuple-element.34), channel_id=1, source_target_pairs={{0,16},{2,66},{10,26},{8,72},{16,0},{18,82},{26,10},{24,88},{34,50... | collective-permute-start | bytes 614408 | tf_op jit(solution)/shard_map/ppermute | solution.py:35
  57.0 7.3 %collective-permute-start.17 = (bf16[80,1280]{1,0:T(8,128)(2,1)S(1)}, bf16[80,1280]{1,0:T(8,128)(2,1)S(1)}, u32[]{:S(2)}, u32[]{:S(2)}) collective-permute-start(bf16[80,1280]{1,0:T(8,128)(2,1)S(1)} %get-tuple-element.35), channel_id=1, source_target_pairs={{0,26},{2,96},{10,0},{8,106},{16,10},{18,112},{26,16},{24,122},{34... | collective-permute-start | bytes 614408 | tf_op jit(solution)/shard_map/ppermute | solution.py:35
  59.7 18.7 %slice-start = ((s8[6553600]{0:T(1024)(128)(4,1)}), s8[4194304]{0:T(1024)(128)(4,1)S(1)}, s32[]{:S(2)}) async-start(s8[6553600]{0:T(1024)(128)(4,1)} %bitcast.38), calls=%async_computation.1 | async-start | bytes 8388608
  61.0 64.2 %collective-permute-start.6 = (bf16[4,160,1280]{2,1,0:T(8,128)(2,1)}, bf16[4,160,1280]{2,1,0:T(8,128)(2,1)S(1)}, u32[]{:S(2)}, u32[]{:S(2)}) collective-permute-start(bf16[4,160,1280]{2,1,0:T(8,128)(2,1)} %pad_maximum_fusion.1), channel_id=1, source_target_pairs={{0,98},{2,24},{10,104},{8,2},{16,114},{18,8},{26,120},{24,18},{34,... | collective-permute-start | bytes 4915208 | tf_op jit(solution)/shard_map/ppermute | solution.py:35
  64.3 3.9 %copy-start.12 = (bf16[2,160,1280]{2,1,0:T(8,128)(2,1)S(1)}, bf16[2,160,1280]{2,1,0:T(8,128)(2,1)}, u32[]{:S(2)}) copy-start(bf16[2,160,1280]{2,1,0:T(8,128)(2,1)} %slice.25) | copy-start | bytes 2457604
  64.4 14.0 %slice-start.1 = ((s8[6553600]{0:T(1024)(128)(4,1)}), s8[2359296]{0:T(1024)(128)(4,1)S(1)}, s32[]{:S(2)}) async-start(s8[6553600]{0:T(1024)(128)(4,1)} %bitcast.38), calls=%async_computation.2 | async-start | bytes 4718592
  64.5 7.1 %collective-permute-start.18 = (f32[40,1280]{1,0:T(8,128)S(1)}, f32[40,1280]{1,0:T(8,128)S(1)}, u32[]{:S(2)}, u32[]{:S(2)}) collective-permute-start(f32[40,1280]{1,0:T(8,128)S(1)} %get-tuple-element.47), channel_id=1, source_target_pairs={{0,4},{4,0},{1,5},{5,1},{2,6},{6,2},{3,7},{7,3},{8,12},{12,8},{9,1... | collective-permute-start | bytes 614408 | tf_op jit(solution)/shard_map/ppermute | solution.py:23
  65.8 12.5 %collective-permute-start.20 = (f32[40,1280]{1,0:T(8,128)S(1)}, f32[40,1280]{1,0:T(8,128)S(1)}, u32[]{:S(2)}, u32[]{:S(2)}) collective-permute-start(f32[40,1280]{1,0:T(8,128)S(1)} %get-tuple-element.47), channel_id=1, source_target_pairs={{0,5},{1,4},{4,1},{5,0},{2,7},{3,6},{6,3},{7,2},{8,13},{9,12},{12,... | collective-permute-start | bytes 614408 | tf_op jit(solution)/shard_map/ppermute | solution.py:312
  67.6 9.9 %collective-permute-start.19 = (f32[40,1280]{1,0:T(8,128)S(1)}, f32[40,1280]{1,0:T(8,128)S(1)}, u32[]{:S(2)}, u32[]{:S(2)}) collective-permute-start(f32[40,1280]{1,0:T(8,128)S(1)} %get-tuple-element.48), channel_id=1, source_target_pairs={{0,1},{1,0},{2,3},{3,2},{4,5},{5,4},{6,7},{7,6},{8,9},{9,8},{10,11... | collective-permute-start | bytes 614408 | tf_op jit(solution)/shard_map/ppermute | solution.py:23
  69.6 55.6 %collective-permute-start.4 = (bf16[4,160,1280]{2,1,0:T(8,128)(2,1)}, bf16[4,160,1280]{2,1,0:T(8,128)(2,1)S(1)}, u32[]{:S(2)}, u32[]{:S(2)}) collective-permute-start(bf16[4,160,1280]{2,1,0:T(8,128)(2,1)} %pad_maximum_fusion), channel_id=1, source_target_pairs={{0,34},{2,8},{10,40},{8,18},{16,50},{18,24},{26,56},{24,2},{34,64}... | collective-permute-start | bytes 4915208 | tf_op jit(solution)/shard_map/ppermute | solution.py:35
  89.4 24.7 %all-to-all-start = ((f32[128,1,1600]{2,1,0:T(1,128)}), f32[128,1,1600]{2,1,0:T(1,128)}, u32[]{:S(2)}, u32[]{:S(2)}) async-start(f32[128,1,1600]{2,1,0:T(1,128)} %reshape.55), calls=%async_computation | async-start | bytes 1703936 | tf_op jit(solution)/shard_map/all_to_all | solution.py:325
  122.6 2.6 %copy-start.3 = (bf16[4,160,1280]{2,1,0:T(8,128)(2,1)S(1)}, bf16[4,160,1280]{2,1,0:T(8,128)(2,1)}, u32[]{:S(2)}) copy-start(bf16[4,160,1280]{2,1,0:T(8,128)(2,1)} %copy-done.2) | copy-start | bytes 4915204
  127.2 0.9 copy-start.6
  128.1 0.8 copy-start.8
  128.9 0.8 copy-start.10
  129.7 1.3 copy-start.11
  129.7 2.1 %copy-start.9 = (bf16[160,1280]{1,0:T(8,128)(2,1)S(1)}, bf16[160,1280]{1,0:T(8,128)(2,1)}, u32[]{:S(2)}) copy-start(bf16[160,1280]{1,0:T(8,128)(2,1)} %copy-done.8) | copy-start | bytes 1228804
  129.7 13.5 %collective-permute-start.7 = (bf16[160,1280]{1,0:T(8,128)(2,1)}, bf16[160,1280]{1,0:T(8,128)(2,1)S(1)}, u32[]{:S(2)}, u32[]{:S(2)}) collective-permute-start(bf16[160,1280]{1,0:T(8,128)(2,1)} %get-tuple-element.25.refs_1_), channel_id=1, source_target_pairs={{0,10},{2,32},{10,16},{8,42},{16,26},{18,48},{26,0},{24,58},{34,40... | collective-permute-start | bytes 1228808 | tf_op jit(solution)/shard_map/ppermute | solution.py:35
  131.0 12.2 %collective-permute-start.8 = (bf16[160,1280]{1,0:T(8,128)(2,1)S(1)}, bf16[160,1280]{1,0:T(8,128)(2,1)S(1)}, u32[]{:S(2)}, u32[]{:S(2)}) collective-permute-start(bf16[160,1280]{1,0:T(8,128)(2,1)S(1)} %copy-done.11), channel_id=1, source_target_pairs={{0,16},{2,66},{10,26},{8,72},{16,0},{18,82},{26,10},{24,88},{34,50... | collective-permute-start | bytes 1228808 | tf_op jit(solution)/shard_map/ppermute | solution.py:35
  131.8 12.0 %collective-permute-start.9 = (bf16[160,1280]{1,0:T(8,128)(2,1)S(1)}, bf16[160,1280]{1,0:T(8,128)(2,1)S(1)}, u32[]{:S(2)}, u32[]{:S(2)}) collective-permute-start(bf16[160,1280]{1,0:T(8,128)(2,1)S(1)} %copy-done.9), channel_id=1, source_target_pairs={{0,26},{2,96},{10,0},{8,106},{16,10},{18,112},{26,16},{24,122},{34... | collective-permute-start | bytes 1228808 | tf_op jit(solution)/shard_map/ppermute | solution.py:35
  136.6 7.2 %copy-start.7 = (f32[160,1280]{1,0:T(8,128)S(1)}, f32[160,1280]{1,0:T(8,128)}, u32[]{:S(2)}) copy-start(f32[160,1280]{1,0:T(8,128)} %copy-done.6) | copy-start | bytes 2457604
  144.0 6.3 %collective-permute-start.10 = (bf16[80,1280]{1,0:T(8,128)(2,1)S(1)}, bf16[80,1280]{1,0:T(8,128)(2,1)S(1)}, u32[]{:S(2)}, u32[]{:S(2)}) collective-permute-start(bf16[80,1280]{1,0:T(8,128)(2,1)S(1)} %fusion.11), channel_id=1, source_target_pairs={{0,4},{4,0},{1,5},{5,1},{2,6},{6,2},{3,7},{7,3},{8,12},{12,8},{9,1... | collective-permute-start | bytes 614408 | tf_op jit(solution)/shard_map/ppermute | solution.py:23
  150.5 2.4 %collective-permute-start.11 = (f32[40,1280]{1,0:T(8,128)S(1)}, f32[40,1280]{1,0:T(8,128)S(1)}, u32[]{:S(2)}, u32[]{:S(2)}) collective-permute-start(f32[40,1280]{1,0:T(8,128)S(1)} %dynamic-slice_bitcast_fusion.3), channel_id=1, source_target_pairs={{0,2},{2,0},{1,3},{3,1},{4,6},{6,4},{5,7},{7,5},{8,10},{10,8},{9,1... | collective-permute-start | bytes 614408 | tf_op jit(solution)/shard_map/ppermute | solution.py:23

commit v6 on v5

--- a/solution.py
+++ b/solution.py
@@ -40,8 +40,8 @@
 
 
 def split_pair(x):
-    high = lax.reduce_precision(x, 8, 7)
-    return high.astype(BF), (x - high).astype(BF)
+    high = x.astype(BF)
+    return high, (x - high.astype(F32)).astype(BF)
 
 
 def place_tile(place, buffer, sem, outs, m, zs):
@@ -119,7 +119,7 @@
             ],
             out_specs=pl.BlockSpec((TILE, half), lambda m, p: (m, 0)),
         ),
-        compiler_params=pltpu.CompilerParams(vmem_limit_bytes=32 * 2**20),
+        compiler_params=pltpu.CompilerParams(vmem_limit_bytes=28 * 2**20),
         cost_estimate=cost,
         name="cross_own",
     )(place, grads, acts)
@@ -143,13 +143,14 @@
                 pltpu.SemaphoreType.DMA,
             ],
         ),
-        compiler_params=pltpu.CompilerParams(vmem_limit_bytes=32 * 2**20),
+        compiler_params=pltpu.CompilerParams(vmem_limit_bytes=28 * 2**20),
         cost_estimate=cost,
         name="cross_term",
     )(place, grads_next, acts_next, partial)
 
 
-def factor_kernel(place, h_own, g_own, h_next, g_next, x_next, *rest):
+def factor_kernel(place, h_own, g_own, h_next, g_next, x_next, after, *rest):
+    del after
     own, right, far_a, far_b, left, lhs, rhs, buffer, lhs_sems, rhs_sem, sem = rest
     m = pl.program_id(0)
     half = rhs.shape[2]
@@ -187,7 +188,7 @@
     pl.when(m == 3)(lambda: wait_all(buffer, sem))
 
 
-def factor_term(place, acts, grads, acts_next, grads_next, rest_next):
+def factor_term(place, acts, grads, acts_next, grads_next, rest_next, after):
     tokens, width = acts.shape
     half = width // 2
     anywhere = pl.BlockSpec(memory_space=pl.ANY)
@@ -199,7 +200,7 @@
         grid_spec=pltpu.PrefetchScalarGridSpec(
             num_scalar_prefetch=1,
             grid=(4,),
-            in_specs=[anywhere] * 5,
+            in_specs=[anywhere] * 6,
             out_specs=[anywhere] * 5,
             scratch_shapes=[
                 pltpu.VMEM((2, 2, tokens, TILE), BF),
@@ -210,12 +211,12 @@
                 pltpu.SemaphoreType.DMA,
             ],
         ),
-        compiler_params=pltpu.CompilerParams(vmem_limit_bytes=40 * 2**20),
+        compiler_params=pltpu.CompilerParams(vmem_limit_bytes=30 * 2**20),
         cost_estimate=pl.CostEstimate(
             flops=4 * tokens * width * half, bytes_accessed=16 * tokens * half, transcendentals=0
         ),
         name="factor_term",
-    )(place, acts, grads, acts_next, grads_next, rest_next)
+    )(place, acts, grads, acts_next, grads_next, rest_next, after)
 
 
 def add(first, *rest):
@@ -233,6 +234,8 @@
         in_specs=[anywhere] * (1 + len(others)),
         out_specs=anywhere,
         input_output_aliases={0: 0},
+        compiler_params=pltpu.CompilerParams(vmem_limit_bytes=2**20),
+        cost_estimate=pl.CostEstimate(flops=0, bytes_accessed=0, transcendentals=0),
         name="gate",
     )(x, *others)
 
@@ -263,12 +266,153 @@
         grid_spec=pltpu.PrefetchScalarGridSpec(
             num_scalar_prefetch=1, grid=(4,), in_specs=[block] * len(parts), out_specs=[whole] * 4
         ),
-        compiler_params=pltpu.CompilerParams(vmem_limit_bytes=32 * 2**20),
+        compiler_params=pltpu.CompilerParams(vmem_limit_bytes=14 * 2**20),
         cost_estimate=pl.CostEstimate(
             flops=16 * rows * width, bytes_accessed=42 * rows * width, transcendentals=0
         ),
         name="fold",
     )(me, *parts)
+
+
+def cut_kernel(place, a, b, out):
+    pl.when(place[0] == 0)(lambda: out.__setitem__(..., a[...]))
+    pl.when(place[0] == 1)(lambda: out.__setitem__(..., b[...]))
+
+
+def cut(place, a, b, index):
+    tokens, width = a.shape
+    block = (tokens // 4, width // 2)
+    return pl.pallas_call(
+        cut_kernel,
+        out_shape=jax.ShapeDtypeStruct((tokens, width // 2), a.dtype),
+        grid_spec=pltpu.PrefetchScalarGridSpec(
+            num_scalar_prefetch=1,
+            grid=(4,),
+            in_specs=[
+                pl.BlockSpec(block, lambda m, p: (m * (1 - p[0]), index(p))),
+                pl.BlockSpec(block, lambda m, p: (m * p[0], index(p))),
+            ],
+            out_specs=pl.BlockSpec(block, lambda m, p: (m, 0)),
+        ),
+        compiler_params=pltpu.CompilerParams(vmem_limit_bytes=8 * 2**20),
+        cost_estimate=pl.CostEstimate(flops=0, bytes_accessed=2 * tokens * width, transcendentals=0),
+        name="cut",
+    )(place, a, b)
+
+
+def grow_kernel(x, received, out):
+    out[...] = add(x[...], received[...]).astype(BF)
+
+
+def grow(x, received, side):
+    block = pl.BlockSpec((1,) + x.shape[1:], lambda s: (side * 2 + s, 0, 0))
+    return pl.pallas_call(
+        grow_kernel,
+        out_shape=jax.ShapeDtypeStruct(x.shape, x.dtype),
+        grid=(2,),
+        in_specs=[block, pl.BlockSpec((1,) + x.shape[1:], lambda s: (s, 0, 0))],
+        out_specs=block,
+        input_output_aliases={0: 0},
+        compiler_params=pltpu.CompilerParams(vmem_limit_bytes=8 * 2**20),
+        cost_estimate=pl.CostEstimate(flops=x.size // 2, bytes_accessed=3 * x.size, transcendentals=0),
+        name="grow",
+    )(x, received)
+
+
+def left_kernel(place, mine, other, partner, partner_other, left, out, total):
+    step = pl.program_id(0)
+    at = pl.ds(pl.multiple_of((step & 1) * TILE, TILE), TILE)
+    rows = mine.shape[0]
+
+    def term(a, b):
+        stacked = jnp.concatenate(split_pair(a[:, at] + b[:, at]), axis=0)
+        value = jnp.dot(stacked, left[...], preferred_element_type=F32)
+        total[...] = jnp.where(step == 0, value, total[...] + value)
+
+    own = (step >> 1) == (place[1] ^ place[0])
+    pl.when(own)(lambda: term(mine, other))
+    pl.when(jnp.logical_not(own))(lambda: term(partner, partner_other))
+
+    @pl.when(step == 3)
+    def _():
+        value = total[:rows] + total[rows:]
+        for z in range(2):
+            for y in range(4):
+                for xl in range(2):
+                    for c in range(2):
+                        at = (((z * 4 + y) * 2 + xl) * 2 + c) * rows
+                        block = value[:, at : at + rows]
+                        for there in (0, 2):
+                            d = c * 32 + (there + z) * 8 + y * 2 + xl
+                            for owner in (0, 64):
+                                out[owner + d, 0:16, 0:rows] = block[0:16]
+                                out[owner + d, 0:16, rows : 2 * rows] = block[16:32]
+                                out[owner + d, 0:8, 2 * rows : 3 * rows] = block[32:40]
+
+
+def left_product(place, mine, other, partner, partner_other, left):
+    rows, half = mine.shape
+    whole = pl.BlockSpec((rows, half), lambda k, p: (0, 0))
+    return pl.pallas_call(
+        left_kernel,
+        out_shape=jax.ShapeDtypeStruct((128, 16, 128), F32),
+        grid_spec=pltpu.PrefetchScalarGridSpec(
+            num_scalar_prefetch=1,
+            grid=(4,),
+            in_specs=[whole] * 4 + [pl.BlockSpec((TILE, half), lambda k, p: (k, 0))],
+            out_specs=pl.BlockSpec((128, 16, 128), lambda k, p: (0, 0, 0)),
+            scratch_shapes=[pltpu.VMEM((2 * rows, half), F32)],
+        ),
+        compiler_params=pltpu.CompilerParams(vmem_limit_bytes=16 * 2**20),
+        cost_estimate=pl.CostEstimate(
+            flops=8 * rows * half * half, bytes_accessed=4 * half * half, transcendentals=0
+        ),
+        name="left_product",
+    )(place, mine, other, partner, partner_other, left)
+
+
+def right_kernel(place, blocks, right, late, out, rows_in):
+    del late
+    step = pl.program_id(0)
+    rows = out.shape[0]
+    for near in range(2):
+        for y in range(4):
+            core = (step >> 1) ^ ((near + y) & 1)
+            for xl in range(2):
+                block = blocks[core * 32 + ((step & 1) * 2 + near) * 8 + y * 2 + xl]
+                at = ((near * 4 + y) * 2 + xl) * rows
+                rows_in[at : at + 16, :] = block[:, 0:rows]
+                rows_in[at + 16 : at + 32, :] = block[:, rows : 2 * rows]
+                rows_in[at + 32 : at + 40, :] = block[0:8, 2 * rows : 3 * rows]
+    high, low = split_pair(rows_in[...])
+    value = contract(high, right[...]) + contract(low, right[...])
+    pl.when(step == 0)(lambda: out.__setitem__(..., value))
+    pl.when(step > 0)(lambda: out.__setitem__(..., out[...] + value))
+
+
+def right_product(place, blocks, right, late):
+    width, half = right.shape
+    rows = width // 64
+    return pl.pallas_call(
+        right_kernel,
+        out_shape=jax.ShapeDtypeStruct((rows, half), F32),
+        grid_spec=pltpu.PrefetchScalarGridSpec(
+            num_scalar_prefetch=1,
+            grid=(4,),
+            in_specs=[
+                pl.BlockSpec((64, 16, 128), lambda k, p: (p[2] >> 1, 0, 0)),
+                pl.BlockSpec((TILE, half), lambda k, p: (k, 0)),
+                pl.BlockSpec(memory_space=pl.ANY),
+            ],
+            out_specs=pl.BlockSpec((rows, half), lambda k, p: (0, 0)),
+            scratch_shapes=[pltpu.VMEM((TILE, rows), F32)],
+        ),
+        compiler_params=pltpu.CompilerParams(vmem_limit_bytes=16 * 2**20),
+        cost_estimate=pl.CostEstimate(
+            flops=8 * rows * half * half, bytes_accessed=4 * half * half, transcendentals=0
+        ),
+        name="right_product",
+    )(place, blocks, right, late)
 
 
 def per_device(hidden, out_grad, left_inverse, right_inverse):
@@ -281,18 +425,15 @@
     place = jnp.stack([o, h, z, y]).astype(jnp.int32)
     second_me = jnp.where(h == 0, y, z).astype(jnp.int32)[None]
 
-    def columns(x, index):
-        return lax.dynamic_slice_in_dim(x, index * half, half, 1)
-
-    grads_next = shift(columns(out_grad, 1 - h), "c", 1)
-    acts_next = shift(columns(hidden, (1 - h) ^ o), "c", 1)
-    rest_next = shift(jnp.where(first, columns(hidden, h), columns(out_grad, h)), "c", 1)
+    grads_next = shift(cut(place, out_grad, out_grad, lambda p: 1 - p[1]), "c", 1)
+    acts_next = shift(cut(place, hidden, hidden, lambda p: (1 - p[1]) ^ p[0]), "c", 1)
+    rest_next = shift(cut(place, hidden, out_grad, lambda p: p[1]), "c", 1)
 
     own, m1, m2, m3 = cross_term(place, out_grad, grads_next, hidden, acts_next)
     m_parts = [own, turn(m1, 1, 0), turn(m2, 2, 0), turn(m3, 3, 0)]
 
     f_own, right, far_a, far_b, left = factor_term(
-        place, hidden, out_grad, acts_next, grads_next, rest_next
+        place, hidden, out_grad, acts_next, grads_next, rest_next, m1
     )
 
     def second_round(parts):
@@ -301,40 +442,19 @@
 
     m_parts[0] = gate(m_parts[0], f_own)
     from_left, from_right = turn(far_a, 1, 0), turn(far_b, -1, 0)
-    right = jnp.concatenate([add(right[:2], from_left).astype(BF), right[2:]])
-    left = jnp.concatenate([left[:2], add(left[2:], from_right).astype(BF)])
+    right, left = grow(right, from_left, 0), grow(left, from_right, 1)
     f_parts = [f_own, turn(right, 1, 0), turn(left, -1, 0)]
 
     _, m = second_round(m_parts)
-    m = m.reshape(2, half // 32, half)
+    m = gate(m, right, left).reshape(2, half // 32, half)
     mine, theirs = pick(m, 0, xl), pick(m, 0, 1 - xl)
-    m_own = mine + shift(theirs, "xl", 1)
-    partner = shift(mine, "o", 1) + lax.ppermute(
-        theirs, ("xl", "o"), [(i, 3 - i) for i in range(4)]
+    across = lax.ppermute(theirs, ("xl", "o"), [(i, 3 - i) for i in range(4)])
+    blocks = left_product(
+        place, mine, shift(theirs, "xl", 1), shift(mine, "o", 1), across, left_inverse
     )
-    swap = (h ^ o) == 0
-    mrow = jnp.concatenate(
-        [jnp.where(swap, m_own, partner), jnp.where(swap, partner, m_own)], axis=1
-    )
-    rows = mrow.shape[0]
-    stacked = jnp.concatenate(split_pair(mrow))
-    pt = jnp.dot(stacked, left_inverse, preferred_element_type=F32)
-    pt = pt[:rows] + pt[rows:]
-    blocks = pt.reshape(rows, 2, 4, 2, 2, rows).transpose(4, 1, 2, 3, 0, 5)
-    blocks = jnp.broadcast_to(blocks[None, :, None], (2, 2, 2, 2, 4, 2, rows, rows))
-    blocks = lax.all_to_all(
-        blocks.reshape(128, rows, rows), ("o", "c", "z", "y", "xl"), 0, 0, tiled=True
-    )
-
+    blocks = lax.all_to_all(blocks, ("o", "c", "z", "y", "xl"), 0, 0, tiled=True)
     late, f = second_round(f_parts)
-    blocks = pick(blocks.reshape(2, 64, rows, rows), 0, z >> 1)
-    blocks = gate(blocks, late)
-    blocks = blocks.reshape(2, 4, 4, 2, rows, rows)
-    odd = ((jnp.arange(4)[:, None] + jnp.arange(4)) & 1).reshape(1, 4, 4, 1, 1, 1) == 1
-    blocks = jnp.where(odd, blocks[::-1], blocks).reshape(width, rows)
-    stacked = jnp.concatenate(split_pair(blocks), axis=1)
-    update = contract(stacked, right_inverse)
-    update = update[:rows] + update[rows:]
+    update = right_product(place, blocks, right_inverse, late)
 
     f = f.reshape(2, width // 32, half)
     f = pick(f, 0, xl) + shift(pick(f, 0, 1 - xl).astype(BF), "xl", 1).astype(F32)

time: 154 us -> 172 us (1.12)
  waiting for transfers between devices: 37.3 us -> 64.7 us
  other arithmetic: 18.2 us -> 2.38 us
  Pallas kernels: 32.8 us -> 47.4 us
  local copies, waits for them, and re-layouts: 23.9 us -> 14.5 us
  starting transfers between devices: 35.2 us -> 41.8 us
  matrix products: 5.27 us -> 0 us
    ppermute x13, waiting for transfers between devices: 8.03 us -> 45.7 us  [turn(): return lax.ppermute(x, ('z', 'y', 'c'), pairs)]
    pallas_call x0 -> x7, Pallas kernels: none -> 13.5 us  [the longest x1 4.7 us: right_product(): pl.pallas_call(right_kernel, out_shape=jax.ShapeDtypeStruct((rows, half),...]
    ppermute x7, waiting for transfers between devices: 11.6 us -> 0.95 us  [shift(): return lax.ppermute(x, axis, [(i, (i + step) % size) for i in range(size)])]
    select_n x3 -> x0, other arithmetic: 5.94 us -> none  [the longest x1 3.92 us: per_device(): jnp.where(first, columns(hidden, h), columns(out_grad, h))]
    dot_general x2 -> x0, matrix products: 5.27 us -> none  [the longest x1 4.02 us: contract(): lax.dot_general(first_rows, second_rows, (((0,), (0,)), ((), ())), prefer...]
    all_to_all x1 -> x0, other arithmetic: 4.73 us -> none  [per_device(): lax.all_to_all(blocks.reshape(128, rows, rows), ('o', 'c', 'z', 'y', 'xl'...]
    all_to_all x1, starting transfers between devices: 7.69 us -> 12 us  [per_device(): lax.all_to_all(blocks, ('o', 'c', 'z', 'y', 'xl'), 0, 0, tiled=True)]
    ppermute x7, starting transfers between devices: 5.45 us -> 9.41 us  [shift(): return lax.ppermute(x, axis, [(i, (i + step) % size) for i in range(size)])]
  transfers between devices with their start and end apart: 22 -> 22, of which waited for: 10 -> 6; matrix products, arithmetic and copies ran while one was open for 24% -> 1% of each run, Pallas kernels for 20% -> 18%
where the time goes in v6:
time: 172 us
  waiting for transfers between devices  64.7 us (38%)
  Pallas kernels  47.4 us (28%)
  starting transfers between devices  41.8 us (24%)
  local copies, waits for them, and re-layouts  14.5 us (8%)
  other arithmetic  2.38 us (1%)
    ppermute x13, waiting for transfers between devices, turn(): return lax.ppermute(x, ('z', 'y', 'c'), pairs)  45.7 us
    ppermute x13, starting transfers between devices, turn(): return lax.ppermute(x, ('z', 'y', 'c'), pairs)  18.5 us
    all_to_all x1, waiting for transfers between devices, per_device(): lax.all_to_all(blocks, ('o', 'c', 'z', 'y', 'xl'), 0, 0, tiled=True)  18 us
    pallas_call x1, Pallas kernels, factor_term(): pl.pallas_call(factor_kernel, out_shape=[out, out, side, side, out], grid...  15.8 us
    unnamed x36, local copies, waits for them, and re-layouts  14.4 us
    all_to_all x1, starting transfers between devices, per_device(): lax.all_to_all(blocks, ('o', 'c', 'z', 'y', 'xl'), 0, 0, tiled=True)  12 us
    ppermute x7, starting transfers between devices, shift(): return lax.ppermute(x, axis, [(i, (i + step) % size) for i in range(size)])  9.41 us
    pallas_call x1, Pallas kernels, cross_term(): pl.pallas_call(cross_kernel, out_shape=[out] * 4, grid_spec=pltpu.Prefetc...  7.19 us
  transfers between devices with their start and end apart: 22, of which 6 were waited for; matrix products, arithmetic and copies ran while one was open for 1% of the time, Pallas kernels for 18%

profile of v6, /device:TPU:1, one launch (start us, length us, event | category | flops | bytes accessed | tf_op | source)
XLA Modules:
  0.0 171.7 jit_solution(1026314074394177865)
XLA Ops:
  0.7 2.1 %copy-done = bf16[768,2560]{1,0:T(8,128)(2,1)S(1)} copy-done((bf16[768,2560]{1,0:T(8,128)(2,1)S(1)}, bf16[768,2560]{1,0:T(8,128)(2,1)}, u32[]{:S(2)}) %copy-start) | copy-done | bytes 3932184
  2.8 1.0 cut.3
  3.9 1.5 collective-permute-start
  5.4 1.0 cut.4
  6.4 1.1 collective-permute-start.1
  7.5 1.0 cut.5
  8.5 1.1 collective-permute-start.2
  9.6 3.9 %cross_own.1.partial = f32[1280,1280]{1,0:T(8,128)S(1)} custom-call(s32[4]{0:T(128)S(1)} %pad_add_fusion.place, bf16[768,2560]{1,0:T(8,128)(2,1)S(1)} %copy-done.2, bf16[768,2560]{1,0:T(8,128)(2,1)S(1)} %copy-done.1), custom_call_target="tpu_custom_call" | custom-call | flops 2516582400 | bytes 9830400 | tf_op jit(solution)/shard_map/cross_own/pallas_call | solution.py:110
  13.5 7.2 %cross_term.1 = (bf16[4,80,1280]{2,1,0:T(8,128)(2,1)S(1)}, bf16[4,80,1280]{2,1,0:T(8,128)(2,1)}, bf16[4,80,1280]{2,1,0:T(8,128)(2,1)}, bf16[4,80,1280]{2,1,0:T(8,128)(2,1)}) custom-call(s32[4]{0:T(128)S(1)} %pad_add_fusion.place, bf16[768,1280]{1,0:T(8,128)(2,1)S(1)} %collective-permute-done.1.a.g_next, bf16[768,1280]{1,0:T(8,128)(2,1)S(1)} %collective-permute-done.b.h_next, ...), custom_call_target="tpu_custom_call" | custom-call | flops 2516582400 | bytes 9830400 | tf_op jit(solution)/shard_map/cross_term/pallas_call | solution.py:127
  20.8 1.0 copy-done.4
  21.7 1.3 copy-done.14
  23.0 1.5 copy-done.9
  24.6 1.5 copy-done.15
  26.1 15.8 %factor_term.1 = (bf16[4,160,1280]{2,1,0:T(8,128)(2,1)S(1)}, bf16[4,160,1280]{2,1,0:T(8,128)(2,1)}, bf16[2,160,1280]{2,1,0:T(8,128)(2,1)S(1)}, bf16[2,160,1280]{...) custom-call(s32[4]{0:T(128)S(1)} %pad_add_fusion.place, bf16[768,2560]{1,0:T(8,128)(2,1)S(1)} %copy-done.1, ...), custom_call_target="tpu_custom_call" | custom-call | flops 10066329600 | bytes 15728640 | tf_op jit(solution)/shard_map/factor_term/pallas_call | solution.py:197
  41.9 1.3 collective-permute-start.3
  43.2 1.7 collective-permute-start.5
  44.9 10.0 %collective-permute-done.3.received = bf16[2,160,1280]{2,1,0:T(8,128)(2,1)S(1)} collective-permute-done((bf16[2,160,1280]{2,1,0:T(8,128)(2,1)S(1)}, bf16[2,160,1280]{2,1,0:T(8,128)(2,1)S(1)}, u32[]{:S(2)}, u32[]{:S(2)}) %collective-permute-start.3) | collective-permute-done | bytes 819232 | tf_op jit(solution)/shard_map/ppermute | solution.py:35
  54.9 2.0 %grow.2.refs_1_ = bf16[4,160,1280]{2,1,0:T(8,128)(2,1)} custom-call(bf16[4,160,1280]{2,1,0:T(8,128)(2,1)} %get-tuple-element.21.x, bf16[2,160,1280]{2,1,0:T(8,128)(2,1)S(1)} %collective-permute-done.3.received), custom_call_target="tpu_custom_call", output_to_operand_aliasing={{}: (0, {})} | custom-call | flops 409600 | bytes 2457600 | tf_op jit(solution)/shard_map/grow/pallas_call | solution.py:309
  57.0 0.3 grow.3.refs_2_
  57.3 3.0 %collective-permute-start.6 = (bf16[4,160,1280]{2,1,0:T(8,128)(2,1)S(1)}, bf16[4,160,1280]{2,1,0:T(8,128)(2,1)}, u32[]{:S(2)}, u32[]{:S(2)}) collective-permute-start(bf16[4,160,1280]{2,1,0:T(8,128)(2,1)S(1)} %grow.3.refs_2_), channel_id=1, source_target_pairs={{0,98},{2,24},{10,104},{8,2},{16,114},{18,8},{26,120},{24,18},{34,... | collective-permute-start | bytes 4915208 | tf_op jit(solution)/shard_map/ppermute | solution.py:35
  60.2 1.5 collective-permute-start.13
  61.7 2.0 %collective-permute-start.14 = (bf16[4,80,1280]{2,1,0:T(8,128)(2,1)}, bf16[4,80,1280]{2,1,0:T(8,128)(2,1)}, u32[]{:S(2)}, u32[]{:S(2)}) collective-permute-start(bf16[4,80,1280]{2,1,0:T(8,128)(2,1)} %get-tuple-element.31), channel_id=1, source_target_pairs={{0,98},{2,24},{10,104},{8,2},{16,114},{18,8},{26,120},{24,18},{34,... | collective-permute-start | bytes 2457608 | tf_op jit(solution)/shard_map/ppermute | solution.py:35
  63.7 1.1 copy-done.5
  64.9 1.0 copy-done.6
  65.8 31.0 %collective-permute-done.12.refs_1_ = bf16[4,80,1280]{2,1,0:T(8,128)(2,1)} collective-permute-done((bf16[4,80,1280]{2,1,0:T(8,128)(2,1)}, bf16[4,80,1280]{2,1,0:T(8,128)(2,1)}, u32[]{:S(2)}, u32[]{:S(2)}) %collective-permute-start.12) | collective-permute-done | bytes 819232 | tf_op jit(solution)/shard_map/ppermute | solution.py:35
  96.9 1.1 copy-done.7
  98.0 3.6 %fold.3 = (f32[80,1280]{1,0:T(8,128)S(1)}, bf16[80,1280]{1,0:T(8,128)(2,1)S(1)}, bf16[80,1280]{1,0:T(8,128)(2,1)}, bf16[80,1280]{1,0:T(8,128)(2,1)}) custom-call(s32[1]{0:T(128)} %bitcast.me, bf16[4,80,1280]{2,1,0:T(8,128)(2,1)S(1)} %copy-done.7, bf16[4,80,1280]{2,1,0:T(8,128)(2,1)} %collective-permute-done.12.refs_1_, ...), custom_call_target="tpu_custom_call" | custom-call | flops 1638400 | bytes 4300800 | tf_op jit(solution)/shard_map/fold/pallas_call | solution.py:263
  101.6 0.7 copy-done.10
  102.4 4.2 %collective-permute-start.17 = (bf16[80,1280]{1,0:T(8,128)(2,1)}, bf16[80,1280]{1,0:T(8,128)(2,1)}, u32[]{:S(2)}, u32[]{:S(2)}) collective-permute-start(bf16[80,1280]{1,0:T(8,128)(2,1)} %get-tuple-element.35), channel_id=1, source_target_pairs={{0,26},{2,96},{10,0},{8,106},{16,10},{18,112},{26,16},{24,122},{34... | collective-permute-start | bytes 614408 | tf_op jit(solution)/shard_map/ppermute | solution.py:35
  106.6 0.9 collective-permute-start.15
  107.5 3.4 %fold.2 = (f32[160,1280]{1,0:T(8,128)S(1)}, bf16[160,1280]{1,0:T(8,128)(2,1)S(1)}, bf16[160,1280]{1,0:T(8,128)(2,1)S(1)}, bf16[160,1280]{1,0:T(8,128)(2,1)S(1)}) custom-call(s32[1]{0:T(128)} %bitcast.me, bf16[4,160,1280]{2,1,0:T(8,128)(2,1)S(1)} %get-tuple-element.20.refs_0_.refs_1_, bf16[4,160,1280]{2,1,0:T(8,128)(2,1)} %collective-permute-done.4.refs_1_, ...), custom_call_target="tpu_custom_call" | custom-call | flops 3276800 | bytes 8601600 | tf_op jit(solution)/shard_map/fold/pallas_call | solution.py:263
  110.9 2.2 %collective-permute-start.9 = (bf16[160,1280]{1,0:T(8,128)(2,1)S(1)}, bf16[160,1280]{1,0:T(8,128)(2,1)S(1)}, u32[]{:S(2)}, u32[]{:S(2)}) collective-permute-start(bf16[160,1280]{1,0:T(8,128)(2,1)S(1)} %get-tuple-element.28), channel_id=1, source_target_pairs={{0,26},{2,96},{10,0},{8,106},{16,10},{18,112},{26,16},{24,122},{34... | collective-permute-start | bytes 1228808 | tf_op jit(solution)/shard_map/ppermute | solution.py:35
  113.1 1.8 %collective-permute-start.8 = (bf16[160,1280]{1,0:T(8,128)(2,1)S(1)}, bf16[160,1280]{1,0:T(8,128)(2,1)S(1)}, u32[]{:S(2)}, u32[]{:S(2)}) collective-permute-start(bf16[160,1280]{1,0:T(8,128)(2,1)S(1)} %get-tuple-element.27), channel_id=1, source_target_pairs={{0,16},{2,66},{10,26},{8,72},{16,0},{18,82},{26,10},{24,88},{34,50... | collective-permute-start | bytes 1228808 | tf_op jit(solution)/shard_map/ppermute | solution.py:35
  114.9 0.4 collective-permute-done.15
  115.2 1.2 convert_add_fusion.1.refs_0_
  116.5 1.3 collective-permute-start.18
  117.8 1.8 %collective-permute-start.20 = (f32[40,1280]{1,0:T(8,128)S(1)}, f32[40,1280]{1,0:T(8,128)S(1)}, u32[]{:S(2)}, u32[]{:S(2)}) collective-permute-start(f32[40,1280]{1,0:T(8,128)S(1)} %get-tuple-element.38), channel_id=1, source_target_pairs={{0,5},{1,4},{4,1},{5,0},{2,7},{3,6},{6,3},{7,2},{8,13},{9,12},{12,... | collective-permute-start | bytes 614408 | tf_op jit(solution)/shard_map/ppermute | solution.py:451
  119.7 2.1 %collective-permute-start.19 = (f32[40,1280]{1,0:T(8,128)S(1)}, f32[40,1280]{1,0:T(8,128)S(1)}, u32[]{:S(2)}, u32[]{:S(2)}) collective-permute-start(f32[40,1280]{1,0:T(8,128)S(1)} %get-tuple-element.39.mine), channel_id=1, source_target_pairs={{0,1},{1,0},{2,3},{3,2},{4,5},{5,4},{6,7},{7,6},{8,9},{9,8},{10,11... | collective-permute-start | bytes 614408 | tf_op jit(solution)/shard_map/ppermute | solution.py:23
  121.7 4.3 %collective-permute-done.7 = bf16[160,1280]{1,0:T(8,128)(2,1)S(1)} collective-permute-done((bf16[160,1280]{1,0:T(8,128)(2,1)S(1)}, bf16[160,1280]{1,0:T(8,128)(2,1)S(1)}, u32[]{:S(2)}, u32[]{:S(2)}) %collective-permute-start.7) | collective-permute-done | bytes 409632 | tf_op jit(solution)/shard_map/ppermute | solution.py:35
  126.3 1.3 collective-permute-start.10
  127.6 0.9 collective-permute-done.19.partner
  128.6 3.4 %left_product.1 = f32[128,16,128]{2,1,0:T(8,128)} custom-call(s32[4]{0:T(128)S(1)} %pad_add_fusion.place, f32[40,1280]{1,0:T(8,128)S(1)} %get-tuple-element.39.mine, f32[40,1280]{1,0:T(8,128)S(1)} %collective-permute-done.18.other, f32[40,1280]{1,0:T(8,128)S(1)} %collective-permute-done.19.partner, f32[40,1280]{1,0:T(8,128)S(1)} %collective-permute-done.20.partner_other, ...), custom_call_target="tpu_custom_call" | custom-call | flops 524288000 | bytes 6553600 | tf_op jit(solution)/shard_map/left_product/pallas_call | solution.py:356
  132.0 12.0 %all-to-all-start = ((f32[128,16,128]{2,1,0:T(8,128)}), f32[128,16,128]{2,1,0:T(8,128)S(1)}, u32[]{:S(2)}, u32[]{:S(2)}) async-start(f32[128,16,128]{2,1,0:T(8,128)} %left_product.1), calls=%async_computation | async-start | bytes 2097152 | tf_op jit(solution)/shard_map/all_to_all | solution.py:455
  144.2 1.1 collective-permute-start.11
  145.3 18.0 %all-to-all-done.blocks = f32[128,16,128]{2,1,0:T(8,128)S(1)} async-done(((f32[128,16,128]{2,1,0:T(8,128)}), f32[128,16,128]{2,1,0:T(8,128)S(1)}, u32[]{:S(2)}, u32[]{:S(2)}) %all-to-all-start) | async-done | bytes 1048608 | tf_op jit(solution)/shard_map/all_to_all | solution.py:455
  163.3 2.9 %copy-done.3 = bf16[2560,1280]{1,0:T(8,128)(2,1)S(1)} copy-done((bf16[2560,1280]{1,0:T(8,128)(2,1)S(1)}, bf16[2560,1280]{1,0:T(8,128)(2,1)}, u32[]{:S(2)}) %copy-start.3) | copy-done | bytes 6553624
  166.2 4.7 %right_product.1 = f32[40,1280]{1,0:T(8,128)} custom-call(s32[4]{0:T(128)S(1)} %pad_add_fusion.place, f32[128,16,128]{2,1,0:T(8,128)S(1)} %all-to-all-done.blocks, bf16[2560,1280]{1,0:T(8,128)(2,1)S(1)} %copy-done.3, bf16[160,1280]{1,0:T(8,128)(2,1)S(1)} %copy-done.13), custom_call_target="tpu_custom_call" | custom-call | flops 524288000 | bytes 6553600 | tf_op jit(solution)/shard_map/right_product/pallas_call | solution.py:396
  170.9 0.8 maximum_bitcast_fusion
  (56 shorter events, 0.7 us)
Async XLA Ops:
  0.7 2.1 %copy-start = (bf16[768,2560]{1,0:T(8,128)(2,1)S(1)}, bf16[768,2560]{1,0:T(8,128)(2,1)}, u32[]{:S(2)}) copy-start(bf16[768,2560]{1,0:T(8,128)(2,1)} %h_own.1) | copy-start | bytes 11796484
  2.8 2.5 %copy-start.2 = (bf16[768,2560]{1,0:T(8,128)(2,1)S(1)}, bf16[768,2560]{1,0:T(8,128)(2,1)}, u32[]{:S(2)}) copy-start(bf16[768,2560]{1,0:T(8,128)(2,1)} %g_own.1) | copy-start | bytes 11796484
  3.9 9.6 %collective-permute-start = (bf16[768,1280]{1,0:T(8,128)(2,1)S(1)}, bf16[768,1280]{1,0:T(8,128)(2,1)S(1)}, u32[]{:S(2)}, u32[]{:S(2)}) collective-permute-start(bf16[768,1280]{1,0:T(8,128)(2,1)S(1)} %cut.3), channel_id=1, source_target_pairs={{0,2},{2,0},{1,3},{3,1},{4,6},{6,4},{5,7},{7,5},{8,10},{10,8},{9,1... | collective-permute-start | bytes 5898248 | tf_op jit(solution)/shard_map/ppermute | solution.py:23
  5.4 2.1 %copy-start.1 = (bf16[768,2560]{1,0:T(8,128)(2,1)S(1)}, bf16[768,2560]{1,0:T(8,128)(2,1)}, u32[]{:S(2)}) copy-start(bf16[768,2560]{1,0:T(8,128)(2,1)} %h_own.1) | copy-start | bytes 11796484
  6.4 7.1 %collective-permute-start.1 = (bf16[768,1280]{1,0:T(8,128)(2,1)S(1)}, bf16[768,1280]{1,0:T(8,128)(2,1)S(1)}, u32[]{:S(2)}, u32[]{:S(2)}) collective-permute-start(bf16[768,1280]{1,0:T(8,128)(2,1)S(1)} %cut.4), channel_id=1, source_target_pairs={{0,2},{2,0},{1,3},{3,1},{4,6},{6,4},{5,7},{7,5},{8,10},{10,8},{9,1... | collective-permute-start | bytes 5898248 | tf_op jit(solution)/shard_map/ppermute | solution.py:23
  8.5 13.2 %collective-permute-start.2 = (bf16[768,1280]{1,0:T(8,128)(2,1)S(1)}, bf16[768,1280]{1,0:T(8,128)(2,1)S(1)}, u32[]{:S(2)}, u32[]{:S(2)}) collective-permute-start(bf16[768,1280]{1,0:T(8,128)(2,1)S(1)} %cut.5), channel_id=1, source_target_pairs={{0,2},{2,0},{1,3},{3,1},{4,6},{6,4},{5,7},{7,5},{8,10},{10,8},{9,1... | collective-permute-start | bytes 5898248 | tf_op jit(solution)/shard_map/ppermute | solution.py:23
  13.5 7.2 %copy-start.8 = (bf16[768,1280]{1,0:T(8,128)(2,1)}, bf16[768,1280]{1,0:T(8,128)(2,1)S(1)}, u32[]{:S(2)}) copy-start(bf16[768,1280]{1,0:T(8,128)(2,1)S(1)} %collective-permute-done.1.a.g_next) | copy-start | bytes 5898244
  20.7 1.0 copy-start.4
  21.7 1.3 copy-start.14
  23.0 1.5 copy-start.9
  24.6 1.5 copy-start.15
  41.9 13.0 %collective-permute-start.3 = (bf16[2,160,1280]{2,1,0:T(8,128)(2,1)S(1)}, bf16[2,160,1280]{2,1,0:T(8,128)(2,1)S(1)}, u32[]{:S(2)}, u32[]{:S(2)}) collective-permute-start(bf16[2,160,1280]{2,1,0:T(8,128)(2,1)S(1)} %get-tuple-element.22), channel_id=1, source_target_pairs={{0,34},{2,8},{10,40},{8,18},{16,50},{18,24},{26,56},{24,2},{34,64}... | collective-permute-start | bytes 2457608 | tf_op jit(solution)/shard_map/ppermute | solution.py:35
  43.2 13.8 %collective-permute-start.5 = (bf16[2,160,1280]{2,1,0:T(8,128)(2,1)S(1)}, bf16[2,160,1280]{2,1,0:T(8,128)(2,1)S(1)}, u32[]{:S(2)}, u32[]{:S(2)}) collective-permute-start(bf16[2,160,1280]{2,1,0:T(8,128)(2,1)S(1)} %get-tuple-element.24), channel_id=1, source_target_pairs={{0,98},{2,24},{10,104},{8,2},{16,114},{18,8},{26,120},{24,18},{34,... | collective-permute-start | bytes 2457608 | tf_op jit(solution)/shard_map/ppermute | solution.py:35
  56.9 50.5 %collective-permute-start.4 = (bf16[4,160,1280]{2,1,0:T(8,128)(2,1)}, bf16[4,160,1280]{2,1,0:T(8,128)(2,1)}, u32[]{:S(2)}, u32[]{:S(2)}) collective-permute-start(bf16[4,160,1280]{2,1,0:T(8,128)(2,1)} %grow.2.refs_1_), channel_id=1, source_target_pairs={{0,34},{2,8},{10,40},{8,18},{16,50},{18,24},{26,56},{24,2},{34,64}... | collective-permute-start | bytes 4915208 | tf_op jit(solution)/shard_map/ppermute | solution.py:35
  57.3 50.2 %collective-permute-start.6 = (bf16[4,160,1280]{2,1,0:T(8,128)(2,1)S(1)}, bf16[4,160,1280]{2,1,0:T(8,128)(2,1)}, u32[]{:S(2)}, u32[]{:S(2)}) collective-permute-start(bf16[4,160,1280]{2,1,0:T(8,128)(2,1)S(1)} %grow.3.refs_2_), channel_id=1, source_target_pairs={{0,98},{2,24},{10,104},{8,2},{16,114},{18,8},{26,120},{24,18},{34,... | collective-permute-start | bytes 4915208 | tf_op jit(solution)/shard_map/ppermute | solution.py:35
  60.2 36.6 %collective-permute-start.12 = (bf16[4,80,1280]{2,1,0:T(8,128)(2,1)}, bf16[4,80,1280]{2,1,0:T(8,128)(2,1)}, u32[]{:S(2)}, u32[]{:S(2)}) collective-permute-start(bf16[4,80,1280]{2,1,0:T(8,128)(2,1)} %get-tuple-element.19.after), channel_id=1, source_target_pairs={{0,34},{2,8},{10,40},{8,18},{16,50},{18,24},{26,56},{24,2},{34,64}... | collective-permute-start | bytes 2457608 | tf_op jit(solution)/shard_map/ppermute | solution.py:35
  60.2 36.6 %collective-permute-start.13 = (bf16[4,80,1280]{2,1,0:T(8,128)(2,1)}, bf16[4,80,1280]{2,1,0:T(8,128)(2,1)}, u32[]{:S(2)}, u32[]{:S(2)}) collective-permute-start(bf16[4,80,1280]{2,1,0:T(8,128)(2,1)} %get-tuple-element.30), channel_id=1, source_target_pairs={{0,64},{2,18},{10,74},{8,24},{16,80},{18,2},{26,90},{24,8},{34,98}... | collective-permute-start | bytes 2457608 | tf_op jit(solution)/shard_map/ppermute | solution.py:35
  61.7 35.2 %collective-permute-start.14 = (bf16[4,80,1280]{2,1,0:T(8,128)(2,1)}, bf16[4,80,1280]{2,1,0:T(8,128)(2,1)}, u32[]{:S(2)}, u32[]{:S(2)}) collective-permute-start(bf16[4,80,1280]{2,1,0:T(8,128)(2,1)} %get-tuple-element.31), channel_id=1, source_target_pairs={{0,98},{2,24},{10,104},{8,2},{16,114},{18,8},{26,120},{24,18},{34,... | collective-permute-start | bytes 2457608 | tf_op jit(solution)/shard_map/ppermute | solution.py:35
  63.7 1.1 copy-start.5
  64.9 1.0 copy-start.6
  96.9 1.1 copy-start.7
  101.6 0.8 copy-start.10
  102.4 12.5 %collective-permute-start.17 = (bf16[80,1280]{1,0:T(8,128)(2,1)}, bf16[80,1280]{1,0:T(8,128)(2,1)}, u32[]{:S(2)}, u32[]{:S(2)}) collective-permute-start(bf16[80,1280]{1,0:T(8,128)(2,1)} %get-tuple-element.35), channel_id=1, source_target_pairs={{0,26},{2,96},{10,0},{8,106},{16,10},{18,112},{26,16},{24,122},{34... | collective-permute-start | bytes 614408 | tf_op jit(solution)/shard_map/ppermute | solution.py:35
  106.6 8.3 %collective-permute-start.16 = (bf16[80,1280]{1,0:T(8,128)(2,1)}, bf16[80,1280]{1,0:T(8,128)(2,1)}, u32[]{:S(2)}, u32[]{:S(2)}) collective-permute-start(bf16[80,1280]{1,0:T(8,128)(2,1)} %get-tuple-element.34), channel_id=1, source_target_pairs={{0,16},{2,66},{10,26},{8,72},{16,0},{18,82},{26,10},{24,88},{34,50... | collective-permute-start | bytes 614408 | tf_op jit(solution)/shard_map/ppermute | solution.py:35
  106.6 8.6 %collective-permute-start.15 = (bf16[80,1280]{1,0:T(8,128)(2,1)S(1)}, bf16[80,1280]{1,0:T(8,128)(2,1)}, u32[]{:S(2)}, u32[]{:S(2)}) collective-permute-start(bf16[80,1280]{1,0:T(8,128)(2,1)S(1)} %get-tuple-element.33), channel_id=1, source_target_pairs={{0,10},{2,32},{10,16},{8,42},{16,26},{18,48},{26,0},{24,58},{34,40... | collective-permute-start | bytes 614408 | tf_op jit(solution)/shard_map/ppermute | solution.py:35
  107.4 7.8 %copy-start.11 = (f32[80,1280]{1,0:T(8,128)S(1)}, f32[80,1280]{1,0:T(8,128)}, u32[]{:S(2)}) copy-start(f32[80,1280]{1,0:T(8,128)} %copy-done.10) | copy-start | bytes 1228804
  107.5 21.1 %slice-start = ((s8[6553600]{0:T(1024)(128)(4,1)}), s8[2359296]{0:T(1024)(128)(4,1)S(1)}, s32[]{:S(2)}) async-start(s8[6553600]{0:T(1024)(128)(4,1)} %bitcast.25), calls=%async_computation.1 | async-start | bytes 4718592
  110.9 5.6 %copy-start.12 = (bf16[160,1280]{1,0:T(8,128)(2,1)}, bf16[160,1280]{1,0:T(8,128)(2,1)S(1)}, u32[]{:S(2)}) copy-start(bf16[160,1280]{1,0:T(8,128)(2,1)S(1)} %get-tuple-element.26.late) | copy-start | bytes 1228804
  110.9 8.7 %collective-permute-start.9 = (bf16[160,1280]{1,0:T(8,128)(2,1)S(1)}, bf16[160,1280]{1,0:T(8,128)(2,1)S(1)}, u32[]{:S(2)}, u32[]{:S(2)}) collective-permute-start(bf16[160,1280]{1,0:T(8,128)(2,1)S(1)} %get-tuple-element.28), channel_id=1, source_target_pairs={{0,26},{2,96},{10,0},{8,106},{16,10},{18,112},{26,16},{24,122},{34... | collective-permute-start | bytes 1228808 | tf_op jit(solution)/shard_map/ppermute | solution.py:35
  113.1 8.6 %collective-permute-start.8 = (bf16[160,1280]{1,0:T(8,128)(2,1)S(1)}, bf16[160,1280]{1,0:T(8,128)(2,1)S(1)}, u32[]{:S(2)}, u32[]{:S(2)}) collective-permute-start(bf16[160,1280]{1,0:T(8,128)(2,1)S(1)} %get-tuple-element.27), channel_id=1, source_target_pairs={{0,16},{2,66},{10,26},{8,72},{16,0},{18,82},{26,10},{24,88},{34,50... | collective-permute-start | bytes 1228808 | tf_op jit(solution)/shard_map/ppermute | solution.py:35
  114.8 11.2 %collective-permute-start.7 = (bf16[160,1280]{1,0:T(8,128)(2,1)S(1)}, bf16[160,1280]{1,0:T(8,128)(2,1)S(1)}, u32[]{:S(2)}, u32[]{:S(2)}) collective-permute-start(bf16[160,1280]{1,0:T(8,128)(2,1)S(1)} %get-tuple-element.26.late), channel_id=1, source_target_pairs={{0,10},{2,32},{10,16},{8,42},{16,26},{18,48},{26,0},{24,58},{34,40... | collective-permute-start | bytes 1228808 | tf_op jit(solution)/shard_map/ppermute | solution.py:35
  116.4 12.1 %slice-start.1 = ((s8[6553600]{0:T(1024)(128)(4,1)}), s8[4194304]{0:T(1024)(128)(4,1)S(1)}, s32[]{:S(2)}) async-start(s8[6553600]{0:T(1024)(128)(4,1)} %bitcast.25), calls=%async_computation.2 | async-start | bytes 8388608
  116.5 11.1 %collective-permute-start.18 = (f32[40,1280]{1,0:T(8,128)S(1)}, f32[40,1280]{1,0:T(8,128)S(1)}, u32[]{:S(2)}, u32[]{:S(2)}) collective-permute-start(f32[40,1280]{1,0:T(8,128)S(1)} %get-tuple-element.38), channel_id=1, source_target_pairs={{0,4},{4,0},{1,5},{5,1},{2,6},{6,2},{3,7},{7,3},{8,12},{12,8},{9,1... | collective-permute-start | bytes 614408 | tf_op jit(solution)/shard_map/ppermute | solution.py:23
  117.8 10.8 %collective-permute-start.20 = (f32[40,1280]{1,0:T(8,128)S(1)}, f32[40,1280]{1,0:T(8,128)S(1)}, u32[]{:S(2)}, u32[]{:S(2)}) collective-permute-start(f32[40,1280]{1,0:T(8,128)S(1)} %get-tuple-element.38), channel_id=1, source_target_pairs={{0,5},{1,4},{4,1},{5,0},{2,7},{3,6},{6,3},{7,2},{8,13},{9,12},{12,... | collective-permute-start | bytes 614408 | tf_op jit(solution)/shard_map/ppermute | solution.py:451
  119.7 8.9 %collective-permute-start.19 = (f32[40,1280]{1,0:T(8,128)S(1)}, f32[40,1280]{1,0:T(8,128)S(1)}, u32[]{:S(2)}, u32[]{:S(2)}) collective-permute-start(f32[40,1280]{1,0:T(8,128)S(1)} %get-tuple-element.39.mine), channel_id=1, source_target_pairs={{0,1},{1,0},{2,3},{3,2},{4,5},{5,4},{6,7},{7,6},{8,9},{9,8},{10,11... | collective-permute-start | bytes 614408 | tf_op jit(solution)/shard_map/ppermute | solution.py:23
  126.3 17.7 %collective-permute-start.10 = (bf16[80,1280]{1,0:T(8,128)(2,1)S(1)}, bf16[80,1280]{1,0:T(8,128)(2,1)S(1)}, u32[]{:S(2)}, u32[]{:S(2)}) collective-permute-start(bf16[80,1280]{1,0:T(8,128)(2,1)S(1)} %fusion.1), channel_id=1, source_target_pairs={{0,4},{4,0},{1,5},{5,1},{2,6},{6,2},{3,7},{7,3},{8,12},{12,8},{9,1... | collective-permute-start | bytes 614408 | tf_op jit(solution)/shard_map/ppermute | solution.py:23
  132.0 31.3 %copy-start.13 = (bf16[160,1280]{1,0:T(8,128)(2,1)S(1)}, bf16[160,1280]{1,0:T(8,128)(2,1)}, u32[]{:S(2)}) copy-start(bf16[160,1280]{1,0:T(8,128)(2,1)} %copy-done.12) | copy-start | bytes 1228804
  132.0 31.3 %all-to-all-start = ((f32[128,16,128]{2,1,0:T(8,128)}), f32[128,16,128]{2,1,0:T(8,128)S(1)}, u32[]{:S(2)}, u32[]{:S(2)}) async-start(f32[128,16,128]{2,1,0:T(8,128)} %left_product.1), calls=%async_computation | async-start | bytes 2097152 | tf_op jit(solution)/shard_map/all_to_all | solution.py:455
  144.2 26.7 %collective-permute-start.11 = (f32[40,1280]{1,0:T(8,128)S(1)}, f32[40,1280]{1,0:T(8,128)S(1)}, u32[]{:S(2)}, u32[]{:S(2)}) collective-permute-start(f32[40,1280]{1,0:T(8,128)S(1)} %dynamic-slice_bitcast_fusion.2), channel_id=1, source_target_pairs={{0,2},{2,0},{1,3},{3,1},{4,6},{6,4},{5,7},{7,5},{8,10},{10,8},{9,1... | collective-permute-start | bytes 614408 | tf_op jit(solution)/shard_map/ppermute | solution.py:23
  163.3 2.9 %copy-start.3 = (bf16[2560,1280]{1,0:T(8,128)(2,1)S(1)}, bf16[2560,1280]{1,0:T(8,128)(2,1)}, u32[]{:S(2)}) copy-start(bf16[2560,1280]{1,0:T(8,128)(2,1)} %right.1) | copy-start | bytes 19660804

commit v7 on v6

--- a/solution.py
+++ b/solution.py
@@ -103,7 +103,7 @@
 
 def cross_term(place, grads, grads_next, acts, acts_next):
     tokens, half = grads_next.shape
-    anywhere = pl.BlockSpec(memory_space=pl.ANY)
+    anywhere = pl.BlockSpec(memory_space=pltpu.HBM)
     cost = pl.CostEstimate(
         flops=2 * tokens * half * half, bytes_accessed=10 * tokens * half, transcendentals=0
     )
@@ -191,7 +191,7 @@
 def factor_term(place, acts, grads, acts_next, grads_next, rest_next, after):
     tokens, width = acts.shape
     half = width // 2
-    anywhere = pl.BlockSpec(memory_space=pl.ANY)
+    anywhere = pl.BlockSpec(memory_space=pltpu.HBM)
     out = jax.ShapeDtypeStruct((4, width // 16, half), BF)
     side = jax.ShapeDtypeStruct((2, width // 16, half), BF)
     return pl.pallas_call(
@@ -226,24 +226,10 @@
     return total
 
 
-def gate(x, *others):
-    anywhere = pl.BlockSpec(memory_space=pl.ANY)
-    return pl.pallas_call(
-        lambda *refs: None,
-        out_shape=jax.ShapeDtypeStruct(x.shape, x.dtype),
-        in_specs=[anywhere] * (1 + len(others)),
-        out_specs=anywhere,
-        input_output_aliases={0: 0},
-        compiler_params=pltpu.CompilerParams(vmem_limit_bytes=2**20),
-        cost_estimate=pl.CostEstimate(flops=0, bytes_accessed=0, transcendentals=0),
-        name="gate",
-    )(x, *others)
-
-
-def fold_kernel(me, *refs):
-    parts, (own, *others) = refs[:-4], refs[-4:]
+def fold_kernel(count, me, *refs):
     step = pl.program_id(0)
-    total = add(*[part[0] for part in parts])
+    own, *others = refs[-4:]
+    total = add(*[part[0] for part in refs[:count]])
 
     @pl.when(step == 0)
     def _():
@@ -256,67 +242,120 @@
             out[...] = total.astype(BF)
 
 
-def fold(me, parts):
+def fold(me, parts, *after):
     _, rows, width = parts[0].shape
     block = pl.BlockSpec((1, rows, width), lambda s, m: ((m[0] + s) & 3, 0, 0))
     whole = pl.BlockSpec((rows, width), lambda s, m: (0, 0))
     return pl.pallas_call(
-        fold_kernel,
+        functools.partial(fold_kernel, len(parts)),
         out_shape=[jax.ShapeDtypeStruct((rows, width), t) for t in (F32, BF, BF, BF)],
         grid_spec=pltpu.PrefetchScalarGridSpec(
-            num_scalar_prefetch=1, grid=(4,), in_specs=[block] * len(parts), out_specs=[whole] * 4
+            num_scalar_prefetch=1,
+            grid=(4,),
+            in_specs=[block] * len(parts) + [pl.BlockSpec(memory_space=pltpu.HBM)] * len(after),
+            out_specs=[whole] * 4,
         ),
         compiler_params=pltpu.CompilerParams(vmem_limit_bytes=14 * 2**20),
         cost_estimate=pl.CostEstimate(
             flops=16 * rows * width, bytes_accessed=42 * rows * width, transcendentals=0
         ),
         name="fold",
-    )(me, *parts)
-
-
-def cut_kernel(place, a, b, out):
-    pl.when(place[0] == 0)(lambda: out.__setitem__(..., a[...]))
-    pl.when(place[0] == 1)(lambda: out.__setitem__(..., b[...]))
+    )(me, *parts, *after)
+
+
+def settle_kernel(xl, total, r1, r2, r3, *refs):
+    mine, theirs = refs[-2:]
+    rows = mine.shape[0]
+    for out, index in ((mine, xl[0]), (theirs, 1 - xl[0])):
+        at = pl.ds(pl.multiple_of(index * rows, 8), rows)
+        value = add(total[at], r1[at], r2[at], r3[at])
+        out[...] = value.astype(out.dtype)
+
+
+def settle(xl, total, received, dtype, *after):
+    rows, width = total.shape
+    whole = pl.BlockSpec((rows, width), lambda s, x: (0, 0))
+    part = pl.BlockSpec((rows // 2, width), lambda s, x: (0, 0))
+    return pl.pallas_call(
+        settle_kernel,
+        out_shape=[jax.ShapeDtypeStruct((rows // 2, width), t) for t in (F32, dtype)],
+        grid_spec=pltpu.PrefetchScalarGridSpec(
+            num_scalar_prefetch=1,
+            grid=(1,),
+            in_specs=[whole] * 4 + [pl.BlockSpec(memory_space=pltpu.HBM)] * len(after),
+            out_specs=[part] * 2,
+        ),
+        compiler_params=pltpu.CompilerParams(vmem_limit_bytes=10 * 2**20),
+        cost_estimate=pl.CostEstimate(
+            flops=4 * rows * width, bytes_accessed=14 * rows * width, transcendentals=0
+        ),
+        name="settle",
+    )(xl, total, *received, *after)
+
+
+def cut_kernel(index, place, a, b, out, held, sems, out_sem):
+    rows = held.shape[1]
+    width = held.shape[2]
+    at = pl.ds(pl.multiple_of(index(place) * width, width), width)
+    for owner, ref in enumerate((a, b)):
+
+        @pl.when(place[0] == owner)
+        def _():
+            for k in range(4):
+                part = ref.at[pl.ds(k * rows, rows), at]
+                pltpu.make_async_copy(part, held.at[k], sems.at[k]).start()
+
+    for k in range(4):
+        wait_all(held.at[k], sems.at[k])
+        pltpu.make_async_copy(held.at[k], out.at[pl.ds(k * rows, rows)], out_sem).start()
+    wait_all(held, out_sem)
 
 
 def cut(place, a, b, index):
     tokens, width = a.shape
-    block = (tokens // 4, width // 2)
-    return pl.pallas_call(
-        cut_kernel,
+    hbm = pl.BlockSpec(memory_space=pltpu.HBM)
+    return pl.pallas_call(
+        functools.partial(cut_kernel, index),
         out_shape=jax.ShapeDtypeStruct((tokens, width // 2), a.dtype),
         grid_spec=pltpu.PrefetchScalarGridSpec(
             num_scalar_prefetch=1,
-            grid=(4,),
-            in_specs=[
-                pl.BlockSpec(block, lambda m, p: (m * (1 - p[0]), index(p))),
-                pl.BlockSpec(block, lambda m, p: (m * p[0], index(p))),
+            grid=(1,),
+            in_specs=[hbm, hbm],
+            out_specs=hbm,
+            scratch_shapes=[
+                pltpu.VMEM((4, tokens // 4, width // 2), a.dtype),
+                pltpu.SemaphoreType.DMA((4,)),
+                pltpu.SemaphoreType.DMA,
             ],
-            out_specs=pl.BlockSpec(block, lambda m, p: (m, 0)),
-        ),
-        compiler_params=pltpu.CompilerParams(vmem_limit_bytes=8 * 2**20),
+        ),
+        compiler_params=pltpu.CompilerParams(vmem_limit_bytes=4 * 2**20),
         cost_estimate=pl.CostEstimate(flops=0, bytes_accessed=2 * tokens * width, transcendentals=0),
         name="cut",
     )(place, a, b)
 
 
-def grow_kernel(x, received, out):
+def grow_kernel(x, received, after, out):
+    del after
     out[...] = add(x[...], received[...]).astype(BF)
 
 
-def grow(x, received, side):
+def grow(x, received, side, after):
     block = pl.BlockSpec((1,) + x.shape[1:], lambda s: (side * 2 + s, 0, 0))
     return pl.pallas_call(
         grow_kernel,
         out_shape=jax.ShapeDtypeStruct(x.shape, x.dtype),
         grid=(2,),
-        in_specs=[block, pl.BlockSpec((1,) + x.shape[1:], lambda s: (s, 0, 0))],
+        in_specs=[
+            block,
+            pl.BlockSpec((1,) + x.shape[1:], lambda s: (s, 0, 0)),
+            pl.BlockSpec(memory_space=pltpu.HBM),
+        ],
         out_specs=block,
         input_output_aliases={0: 0},
         compiler_params=pltpu.CompilerParams(vmem_limit_bytes=8 * 2**20),
         cost_estimate=pl.CostEstimate(flops=x.size // 2, bytes_accessed=3 * x.size, transcendentals=0),
         name="grow",
-    )(x, received)
+    )(x, received, after)
 
 
 def left_kernel(place, mine, other, partner, partner_other, left, out, total):
@@ -365,7 +404,7 @@
         ),
         compiler_params=pltpu.CompilerParams(vmem_limit_bytes=16 * 2**20),
         cost_estimate=pl.CostEstimate(
-            flops=8 * rows * half * half, bytes_accessed=4 * half * half, transcendentals=0
+            flops=256 * rows * half * half, bytes_accessed=4 * half * half, transcendentals=0
         ),
         name="left_product",
     )(place, mine, other, partner, partner_other, left)
@@ -402,14 +441,14 @@
             in_specs=[
                 pl.BlockSpec((64, 16, 128), lambda k, p: (p[2] >> 1, 0, 0)),
                 pl.BlockSpec((TILE, half), lambda k, p: (k, 0)),
-                pl.BlockSpec(memory_space=pl.ANY),
+                pl.BlockSpec(memory_space=pltpu.HBM),
             ],
             out_specs=pl.BlockSpec((rows, half), lambda k, p: (0, 0)),
             scratch_shapes=[pltpu.VMEM((TILE, rows), F32)],
         ),
         compiler_params=pltpu.CompilerParams(vmem_limit_bytes=16 * 2**20),
         cost_estimate=pl.CostEstimate(
-            flops=8 * rows * half * half, bytes_accessed=4 * half * half, transcendentals=0
+            flops=640 * rows * half * half, bytes_accessed=4 * half * half, transcendentals=0
         ),
         name="right_product",
     )(place, blocks, right, late)
@@ -436,28 +475,29 @@
         place, hidden, out_grad, acts_next, grads_next, rest_next, m1
     )
 
-    def second_round(parts):
-        total, *pieces = fold(second_me, parts)
-        return pieces[0], add(total, *[turn(piece, s, 1) for s, piece in enumerate(pieces, 1)])
-
-    m_parts[0] = gate(m_parts[0], f_own)
+    my_xl = xl.astype(jnp.int32)[None]
+
+    def second_sends(pieces):
+        return [turn(piece, s, 1) for s, piece in enumerate(pieces, 1)]
+
     from_left, from_right = turn(far_a, 1, 0), turn(far_b, -1, 0)
-    right, left = grow(right, from_left, 0), grow(left, from_right, 1)
+    m, *m_pieces = fold(second_me, m_parts, f_own)
+    m_received = second_sends(m_pieces)
+    right = grow(right, from_left, 0, m_received[1])
+    left = grow(left, from_right, 1, m_received[1])
     f_parts = [f_own, turn(right, 1, 0), turn(left, -1, 0)]
 
-    _, m = second_round(m_parts)
-    m = gate(m, right, left).reshape(2, half // 32, half)
-    mine, theirs = pick(m, 0, xl), pick(m, 0, 1 - xl)
+    mine, theirs = settle(my_xl, m, m_received, F32)
     across = lax.ppermute(theirs, ("xl", "o"), [(i, 3 - i) for i in range(4)])
     blocks = left_product(
         place, mine, shift(theirs, "xl", 1), shift(mine, "o", 1), across, left_inverse
     )
     blocks = lax.all_to_all(blocks, ("o", "c", "z", "y", "xl"), 0, 0, tiled=True)
-    late, f = second_round(f_parts)
-    update = right_product(place, blocks, right_inverse, late)
-
-    f = f.reshape(2, width // 32, half)
-    f = pick(f, 0, xl) + shift(pick(f, 0, 1 - xl).astype(BF), "xl", 1).astype(F32)
+    f, *f_pieces = fold(second_me, f_parts)
+    f_mine, f_theirs = settle(my_xl, f, second_sends(f_pieces), BF)
+    update = right_product(place, blocks, right_inverse, f_pieces[0])
+
+    f = add(f_mine, shift(f_theirs, "xl", 1))
     f = f * jnp.where(first, 1.0 / token_total, 1.0).astype(F32)
     f = f.reshape(2, width // 64, half)
     mine = pick(f, 0, c)

time: 172 us -> 143 us (0.83)
  waiting for transfers between devices: 64.7 us -> 31.9 us
  Pallas kernels: 47.4 us -> 53.8 us
    ppermute x13, waiting for transfers between devices: 45.7 us -> 15.9 us  [turn(): return lax.ppermute(x, ('z', 'y', 'c'), pairs)]
    all_to_all x1, waiting for transfers between devices: 18 us -> 1.12 us  [per_device(): lax.all_to_all(blocks, ('o', 'c', 'z', 'y', 'xl'), 0, 0, tiled=True)]
    ppermute x7, waiting for transfers between devices: 0.95 us -> 14.9 us  [shift(): return lax.ppermute(x, axis, [(i, (i + step) % size) for i in range(size)])]
    ppermute x13, starting transfers between devices: 18.5 us -> 24.3 us  [turn(): return lax.ppermute(x, ('z', 'y', 'c'), pairs)]
    pallas_call x7, Pallas kernels: 10.1 us -> 15.5 us  [the longest x2 7.64 us: fold(): pl.pallas_call(functools.partial(fold_kernel, len(parts)), out_shape=[jax...]
    all_to_all x1, starting transfers between devices: 12 us -> 7.55 us  [per_device(): lax.all_to_all(blocks, ('o', 'c', 'z', 'y', 'xl'), 0, 0, tiled=True)]
    unnamed x36 -> x28, local copies, waits for them, and re-layouts: 14.4 us -> 14.5 us
  transfers between devices with their start and end apart: 22 -> 22, of which waited for: 6 -> 7; matrix products, arithmetic and copies ran while one was open for 1% -> 0% of each run, Pallas kernels for 18% -> 36%
where the time goes in v7:
time: 143 us; the launch traced here: 142 us
  Pallas kernels  53.8 us (38%)
  starting transfers between devices  40.2 us (28%)
  waiting for transfers between devices  31.9 us (22%)
  local copies, waits for them, and re-layouts  14.5 us (10%)
    ppermute x13, starting transfers between devices, turn(): return lax.ppermute(x, ('z', 'y', 'c'), pairs)  24.3 us
    ppermute x13, waiting for transfers between devices, turn(): return lax.ppermute(x, ('z', 'y', 'c'), pairs)  15.9 us
    pallas_call x1, Pallas kernels, factor_term(): pl.pallas_call(factor_kernel, out_shape=[out, out, side, side, out], grid...  15.5 us
    ppermute x7, waiting for transfers between devices, shift(): return lax.ppermute(x, axis, [(i, (i + step) % size) for i in range(size)])  14.9 us
    unnamed x28, local copies, waits for them, and re-layouts  14.5 us
    ppermute x7, starting transfers between devices, shift(): return lax.ppermute(x, axis, [(i, (i + step) % size) for i in range(size)])  8.25 us
    pallas_call x2, Pallas kernels, fold(): pl.pallas_call(functools.partial(fold_kernel, len(parts)), out_shape=[jax...  7.64 us
    all_to_all x1, starting transfers between devices, per_device(): lax.all_to_all(blocks, ('o', 'c', 'z', 'y', 'xl'), 0, 0, tiled=True)  7.55 us
  transfers between devices with their start and end apart: 22, of which 7 were waited for; matrix products, arithmetic and copies ran while one was open for 0% of the time, Pallas kernels for 36%

profile of v7, /device:TPU:1, one launch (start us, length us, event | category | flops | bytes accessed | tf_op | source)
XLA Modules:
  0.0 142.2 jit_solution(2441276065862866876)
XLA Ops:
  0.7 2.1 %copy-done = bf16[768,2560]{1,0:T(8,128)(2,1)S(1)} copy-done((bf16[768,2560]{1,0:T(8,128)(2,1)S(1)}, bf16[768,2560]{1,0:T(8,128)(2,1)}, u32[]{:S(2)}) %copy-start) | copy-done | bytes 3932184
  2.8 2.0 %cut.3 = bf16[768,1280]{1,0:T(8,128)(2,1)S(1)} custom-call(s32[4]{0:T(128)S(1)} %pad_add_fusion.place, bf16[768,2560]{1,0:T(8,128)(2,1)S(1)} %copy-done, bf16[768,2560]{1,0:T(8,128)(2,1)S(1)} %copy-done), custom_call_target="tpu_custom_call" | custom-call | bytes 3932160 | tf_op jit(solution)/shard_map/cut/pallas_call | solution.py:317
  4.8 1.5 %collective-permute-start = (bf16[768,1280]{1,0:T(8,128)(2,1)S(1)}, bf16[768,1280]{1,0:T(8,128)(2,1)S(1)}, u32[]{:S(2)}, u32[]{:S(2)}) collective-permute-start(bf16[768,1280]{1,0:T(8,128)(2,1)S(1)} %cut.3), channel_id=1, source_target_pairs={{0,2},{2,0},{1,3},{3,1},{4,6},{6,4},{5,7},{7,5},{8,10},{10,8},{9,1... | collective-permute-start | bytes 5898248 | tf_op jit(solution)/shard_map/ppermute | solution.py:23
  6.3 2.0 %cut.4 = bf16[768,1280]{1,0:T(8,128)(2,1)S(1)} custom-call(s32[4]{0:T(128)S(1)} %pad_add_fusion.place, bf16[768,2560]{1,0:T(8,128)(2,1)S(1)} %copy-done.2, bf16[768,2560]{1,0:T(8,128)(2,1)S(1)} %copy-done.2), custom_call_target="tpu_custom_call" | custom-call | bytes 3932160 | tf_op jit(solution)/shard_map/cut/pallas_call | solution.py:317
  8.5 2.0 %cut.5 = bf16[768,1280]{1,0:T(8,128)(2,1)S(1)} custom-call(s32[4]{0:T(128)S(1)} %pad_add_fusion.place, bf16[768,2560]{1,0:T(8,128)(2,1)S(1)} %copy-done.1, bf16[768,2560]{1,0:T(8,128)(2,1)S(1)} %copy-done.2), custom_call_target="tpu_custom_call" | custom-call | bytes 3932160 | tf_op jit(solution)/shard_map/cut/pallas_call | solution.py:317
  10.5 0.6 collective-permute-start.2
  11.0 3.9 %cross_own.1.partial = f32[1280,1280]{1,0:T(8,128)S(1)} custom-call(s32[4]{0:T(128)S(1)} %pad_add_fusion.place, bf16[768,2560]{1,0:T(8,128)(2,1)S(1)} %copy-done.2, bf16[768,2560]{1,0:T(8,128)(2,1)S(1)} %copy-done.1), custom_call_target="tpu_custom_call" | custom-call | flops 2516582400 | bytes 9830400 | tf_op jit(solution)/shard_map/cross_own/pallas_call | solution.py:110
  15.0 7.2 %cross_term.1 = (bf16[4,80,1280]{2,1,0:T(8,128)(2,1)S(1)}, bf16[4,80,1280]{2,1,0:T(8,128)(2,1)}, bf16[4,80,1280]{2,1,0:T(8,128)(2,1)}, bf16[4,80,1280]{2,1,0:T(8,128)(2,1)}) custom-call(s32[4]{0:T(128)S(1)} %pad_add_fusion.place, bf16[768,1280]{1,0:T(8,128)(2,1)S(1)} %collective-permute-done.1.a.g_next, bf16[768,1280]{1,0:T(8,128)(2,1)S(1)} %collective-permute-done.b.h_next, ...), custom_call_target="tpu_custom_call" | custom-call | flops 2516582400 | bytes 9830400 | tf_op jit(solution)/shard_map/cross_term/pallas_call | solution.py:127
  22.1 0.9 copy-done.6
  23.0 1.3 collective-permute-start.4
  24.3 2.6 %collective-permute-start.5 = (bf16[4,80,1280]{2,1,0:T(8,128)(2,1)}, bf16[4,80,1280]{2,1,0:T(8,128)(2,1)}, u32[]{:S(2)}, u32[]{:S(2)}) collective-permute-start(bf16[4,80,1280]{2,1,0:T(8,128)(2,1)} %get-tuple-element.28), channel_id=1, source_target_pairs={{0,64},{2,18},{10,74},{8,24},{16,80},{18,2},{26,90},{24,8},{34,98}... | collective-permute-start | bytes 2457608 | tf_op jit(solution)/shard_map/ppermute | solution.py:35
  26.9 1.7 %collective-permute-start.6 = (bf16[4,80,1280]{2,1,0:T(8,128)(2,1)}, bf16[4,80,1280]{2,1,0:T(8,128)(2,1)}, u32[]{:S(2)}, u32[]{:S(2)}) collective-permute-start(bf16[4,80,1280]{2,1,0:T(8,128)(2,1)} %get-tuple-element.29), channel_id=1, source_target_pairs={{0,98},{2,24},{10,104},{8,2},{16,114},{18,8},{26,120},{24,18},{34,... | collective-permute-start | bytes 2457608 | tf_op jit(solution)/shard_map/ppermute | solution.py:35
  28.7 1.5 %copy-done.4 = bf16[768,1280]{1,0:T(8,128)(2,1)S(1)} copy-done((bf16[768,1280]{1,0:T(8,128)(2,1)S(1)}, bf16[768,1280]{1,0:T(8,128)(2,1)}, u32[]{:S(2)}) %copy-start.4) | copy-done | bytes 1966104
  30.2 15.5 %factor_term.1 = (bf16[4,160,1280]{2,1,0:T(8,128)(2,1)S(1)}, bf16[4,160,1280]{2,1,0:T(8,128)(2,1)S(1)}, bf16[2,160,1280]{2,1,0:T(8,128)(2,1)}, bf16[2,160,1280]{2,1,0:T(8,128)(2,1)}, bf16[4,160,1280]{2,1,0:T(8,128)(2,1)}) custom-call(s32[4]{0:T(128)S(1)} %pad_add_fusion.place, bf16[768,2560]{1,0:T(8,128)(2,1)S(1)} %copy-done.1, ...), custom_call_target="tpu_custom_call" | custom-call | flops 10066329600 | bytes 15728640 | tf_op jit(solution)/shard_map/factor_term/pallas_call | solution.py:197
  45.9 2.9 %collective-permute-start.9 = (bf16[2,160,1280]{2,1,0:T(8,128)(2,1)}, bf16[2,160,1280]{2,1,0:T(8,128)(2,1)}, u32[]{:S(2)}, u32[]{:S(2)}) collective-permute-start(bf16[2,160,1280]{2,1,0:T(8,128)(2,1)} %get-tuple-element.32), channel_id=1, source_target_pairs={{0,98},{2,24},{10,104},{8,2},{16,114},{18,8},{26,120},{24,18},{34,... | collective-permute-start | bytes 2457608 | tf_op jit(solution)/shard_map/ppermute | solution.py:35
  48.8 1.1 copy-done.7
  49.9 3.6 %fold.2 = (f32[80,1280]{1,0:T(8,128)S(1)}, bf16[80,1280]{1,0:T(8,128)(2,1)}, bf16[80,1280]{1,0:T(8,128)(2,1)S(1)}, bf16[80,1280]{1,0:T(8,128)(2,1)}) custom-call(s32[1]{0:T(128)} %bitcast.1.me, bf16[4,80,1280]{2,1,0:T(8,128)(2,1)S(1)} %copy-done.7, bf16[4,80,1280]{2,1,0:T(8,128)(2,1)} %collective-permute-done.4.refs_1_, ...), custom_call_target="tpu_custom_call" | custom-call | flops 1638400 | bytes 4300800 | tf_op jit(solution)/shard_map/fold/pallas_call | solution.py:249
  53.6 3.6 %collective-permute-start.7 = (bf16[80,1280]{1,0:T(8,128)(2,1)S(1)}, bf16[80,1280]{1,0:T(8,128)(2,1)S(1)}, u32[]{:S(2)}, u32[]{:S(2)}) collective-permute-start(bf16[80,1280]{1,0:T(8,128)(2,1)S(1)} %get-tuple-element.30), channel_id=1, source_target_pairs={{0,16},{2,66},{10,26},{8,72},{16,0},{18,82},{26,10},{24,88},{34,50... | collective-permute-start | bytes 614408 | tf_op jit(solution)/shard_map/ppermute | solution.py:35
  57.2 4.4 %collective-permute-done.3.received = bf16[2,160,1280]{2,1,0:T(8,128)(2,1)} collective-permute-done((bf16[2,160,1280]{2,1,0:T(8,128)(2,1)}, bf16[2,160,1280]{2,1,0:T(8,128)(2,1)}, u32[]{:S(2)}, u32[]{:S(2)}) %collective-permute-start.3) | collective-permute-done | bytes 819232 | tf_op jit(solution)/shard_map/ppermute | solution.py:35
  61.6 1.3 grow.2
  62.9 1.2 copy-done.5
  64.1 2.3 %grow.3 = bf16[4,160,1280]{2,1,0:T(8,128)(2,1)} custom-call(bf16[4,160,1280]{2,1,0:T(8,128)(2,1)} %get-tuple-element.31.x, bf16[2,160,1280]{2,1,0:T(8,128)(2,1)} %collective-permute-done.9.received, bf16[80,1280]{1,0:T(8,128)(2,1)S(1)} %collective-permute-done.7.after.r2), custom_call_target="tpu_custom_call", output_to_operand_aliasing={{}: (0, {})} | custom-call | flops 409600 | bytes 2457600 | tf_op jit(solution)/shard_map/grow/pallas_call | solution.py:344
  66.3 2.9 %collective-permute-start.10 = (bf16[4,160,1280]{2,1,0:T(8,128)(2,1)}, bf16[4,160,1280]{2,1,0:T(8,128)(2,1)}, u32[]{:S(2)}, u32[]{:S(2)}) collective-permute-start(bf16[4,160,1280]{2,1,0:T(8,128)(2,1)} %grow.3), channel_id=1, source_target_pairs={{0,98},{2,24},{10,104},{8,2},{16,114},{18,8},{26,120},{24,18},{34,... | collective-permute-start | bytes 4915208 | tf_op jit(solution)/shard_map/ppermute | solution.py:35
  69.3 1.0 collective-permute-start.16
  70.2 2.1 %collective-permute-start.17 = (bf16[80,1280]{1,0:T(8,128)(2,1)}, bf16[80,1280]{1,0:T(8,128)(2,1)}, u32[]{:S(2)}, u32[]{:S(2)}) collective-permute-start(bf16[80,1280]{1,0:T(8,128)(2,1)} %get-tuple-element.41), channel_id=1, source_target_pairs={{0,26},{2,96},{10,0},{8,106},{16,10},{18,112},{26,16},{24,122},{34... | collective-permute-start | bytes 614408 | tf_op jit(solution)/shard_map/ppermute | solution.py:35
  72.4 6.3 %collective-permute-done.16.r1 = bf16[80,1280]{1,0:T(8,128)(2,1)} collective-permute-done((bf16[80,1280]{1,0:T(8,128)(2,1)}, bf16[80,1280]{1,0:T(8,128)(2,1)}, u32[]{:S(2)}, u32[]{:S(2)}) %collective-permute-start.16) | collective-permute-done | bytes 204832 | tf_op jit(solution)/shard_map/ppermute | solution.py:35
  78.8 1.0 copy-done.11
  79.8 1.1 settle.3
  81.0 1.3 collective-permute-start.18
  82.3 2.5 %collective-permute-start.19 = (f32[40,1280]{1,0:T(8,128)S(1)}, f32[40,1280]{1,0:T(8,128)S(1)}, u32[]{:S(2)}, u32[]{:S(2)}) collective-permute-start(f32[40,1280]{1,0:T(8,128)S(1)} %get-tuple-element.42.mine), channel_id=1, source_target_pairs={{0,1},{1,0},{2,3},{3,2},{4,5},{5,4},{6,7},{7,6},{8,9},{9,8},{10,11... | collective-permute-start | bytes 614408 | tf_op jit(solution)/shard_map/ppermute | solution.py:23
  84.9 3.4 %collective-permute-done.8.refs_1_ = bf16[4,160,1280]{2,1,0:T(8,128)(2,1)S(1)} collective-permute-done((bf16[4,160,1280]{2,1,0:T(8,128)(2,1)}, bf16[4,160,1280]{2,1,0:T(8,128)(2,1)S(1)}, u32[]{:S(2)}, u32[]{:S(2)}) %collective-permute-start.8) | collective-permute-done | bytes 1638432 | tf_op jit(solution)/shard_map/ppermute | solution.py:35
  88.3 1.6 %collective-permute-done.10.refs_2_ = bf16[4,160,1280]{2,1,0:T(8,128)(2,1)} collective-permute-done((bf16[4,160,1280]{2,1,0:T(8,128)(2,1)}, bf16[4,160,1280]{2,1,0:T(8,128)(2,1)}, u32[]{:S(2)}, u32[]{:S(2)}) %collective-permute-start.10) | collective-permute-done | bytes 1638432 | tf_op jit(solution)/shard_map/ppermute | solution.py:35
  89.8 4.0 %fold.3 = (f32[160,1280]{1,0:T(8,128)S(1)}, bf16[160,1280]{1,0:T(8,128)(2,1)}, bf16[160,1280]{1,0:T(8,128)(2,1)}, bf16[160,1280]{1,0:T(8,128)(2,1)}) custom-call(s32[1]{0:T(128)} %bitcast.1.me, bf16[4,160,1280]{2,1,0:T(8,128)(2,1)S(1)} %get-tuple-element.24.refs_4_.refs_0_, bf16[4,160,1280]{2,1,0:T(8,128)(2,1)S(1)} %collective-permute-done.8.refs_1_, ...), custom_call_target="tpu_custom_call" | custom-call | flops 3276800 | bytes 8601600 | tf_op jit(solution)/shard_map/fold/pallas_call | solution.py:249
  93.8 0.9 copy-done.8
  94.7 1.6 %collective-permute-start.11 = (bf16[160,1280]{1,0:T(8,128)(2,1)}, bf16[160,1280]{1,0:T(8,128)(2,1)S(1)}, u32[]{:S(2)}, u32[]{:S(2)}) collective-permute-start(bf16[160,1280]{1,0:T(8,128)(2,1)} %get-tuple-element.34.late), channel_id=1, source_target_pairs={{0,10},{2,32},{10,16},{8,42},{16,26},{18,48},{26,0},{24,58},{34,40... | collective-permute-start | bytes 1228808 | tf_op jit(solution)/shard_map/ppermute | solution.py:35
  96.3 3.3 %collective-permute-start.12 = (bf16[160,1280]{1,0:T(8,128)(2,1)}, bf16[160,1280]{1,0:T(8,128)(2,1)S(1)}, u32[]{:S(2)}, u32[]{:S(2)}) collective-permute-start(bf16[160,1280]{1,0:T(8,128)(2,1)} %get-tuple-element.35), channel_id=1, source_target_pairs={{0,16},{2,66},{10,26},{8,72},{16,0},{18,82},{26,10},{24,88},{34,50... | collective-permute-start | bytes 1228808 | tf_op jit(solution)/shard_map/ppermute | solution.py:35
  99.6 1.1 collective-permute-start.13
  100.7 2.9 %copy-done.12 = bf16[2560,1280]{1,0:T(8,128)(2,1)S(1)} copy-done((bf16[2560,1280]{1,0:T(8,128)(2,1)S(1)}, bf16[2560,1280]{1,0:T(8,128)(2,1)}, u32[]{:S(2)}) %copy-start.12) | copy-done | bytes 6553624
  103.5 3.4 %left_product.1 = f32[128,16,128]{2,1,0:T(8,128)} custom-call(s32[4]{0:T(128)S(1)} %pad_add_fusion.place, f32[40,1280]{1,0:T(8,128)S(1)} %get-tuple-element.42.mine, f32[40,1280]{1,0:T(8,128)S(1)} %collective-permute-done.18.other, f32[40,1280]{1,0:T(8,128)S(1)} %collective-permute-done.19.partner, f32[40,1280]{1,0:T(8,128)S(1)} %collective-permute-done.20.partner_other, ...), custom_call_target="tpu_custom_call" | custom-call | flops 16777216000 | bytes 6553600 | tf_op jit(solution)/shard_map/left_product/pallas_call | solution.py:395
  107.0 7.6 %all-to-all-start = ((f32[128,16,128]{2,1,0:T(8,128)}), f32[128,16,128]{2,1,0:T(8,128)S(1)}, u32[]{:S(2)}, u32[]{:S(2)}) async-start(f32[128,16,128]{2,1,0:T(8,128)} %left_product.1), calls=%async_computation | async-start | bytes 2097152 | tf_op jit(solution)/shard_map/all_to_all | solution.py:495
  114.6 0.8 settle.2
  115.4 1.4 collective-permute-start.14
  116.7 14.9 %collective-permute-done.14 = bf16[80,1280]{1,0:T(8,128)(2,1)S(1)} collective-permute-done((bf16[80,1280]{1,0:T(8,128)(2,1)}, bf16[80,1280]{1,0:T(8,128)(2,1)S(1)}, u32[]{:S(2)}, u32[]{:S(2)}) %collective-permute-start.14) | collective-permute-done | bytes 204832 | tf_op jit(solution)/shard_map/ppermute | solution.py:23
  131.7 1.0 collective-permute-start.15
  132.7 1.1 all-to-all-done.blocks
  133.8 2.9 %copy-done.13 = bf16[2560,1280]{1,0:T(8,128)(2,1)S(1)} copy-done((bf16[2560,1280]{1,0:T(8,128)(2,1)S(1)}, bf16[2560,1280]{1,0:T(8,128)(2,1)}, u32[]{:S(2)}) %copy-start.13) | copy-done | bytes 6553624
  136.7 4.7 %right_product.1 = f32[40,1280]{1,0:T(8,128)} custom-call(s32[4]{0:T(128)S(1)} %pad_add_fusion.place, f32[128,16,128]{2,1,0:T(8,128)S(1)} %all-to-all-done.blocks, bf16[2560,1280]{1,0:T(8,128)(2,1)S(1)} %copy-done.13, bf16[160,1280]{1,0:T(8,128)(2,1)} %get-tuple-element.34.late), custom_call_target="tpu_custom_call" | custom-call | flops 41943040000 | bytes 6553600 | tf_op jit(solution)/shard_map/right_product/pallas_call | solution.py:435
  141.4 0.8 maximum_bitcast_fusion
  (43 shorter events, 0.8 us)
Async XLA Ops:
  0.7 2.1 %copy-start = (bf16[768,2560]{1,0:T(8,128)(2,1)S(1)}, bf16[768,2560]{1,0:T(8,128)(2,1)}, u32[]{:S(2)}) copy-start(bf16[768,2560]{1,0:T(8,128)(2,1)} %h_own.1) | copy-start | bytes 11796484
  2.8 3.5 %copy-start.2 = (bf16[768,2560]{1,0:T(8,128)(2,1)S(1)}, bf16[768,2560]{1,0:T(8,128)(2,1)}, u32[]{:S(2)}) copy-start(bf16[768,2560]{1,0:T(8,128)(2,1)} %g_own.1) | copy-start | bytes 11796484
  4.8 10.1 %collective-permute-start = (bf16[768,1280]{1,0:T(8,128)(2,1)S(1)}, bf16[768,1280]{1,0:T(8,128)(2,1)S(1)}, u32[]{:S(2)}, u32[]{:S(2)}) collective-permute-start(bf16[768,1280]{1,0:T(8,128)(2,1)S(1)} %cut.3), channel_id=1, source_target_pairs={{0,2},{2,0},{1,3},{3,1},{4,6},{6,4},{5,7},{7,5},{8,10},{10,8},{9,1... | collective-permute-start | bytes 5898248 | tf_op jit(solution)/shard_map/ppermute | solution.py:23
  6.3 2.1 %copy-start.1 = (bf16[768,2560]{1,0:T(8,128)(2,1)S(1)}, bf16[768,2560]{1,0:T(8,128)(2,1)}, u32[]{:S(2)}) copy-start(bf16[768,2560]{1,0:T(8,128)(2,1)} %h_own.1) | copy-start | bytes 11796484
  8.4 6.6 %collective-permute-start.1 = (bf16[768,1280]{1,0:T(8,128)(2,1)S(1)}, bf16[768,1280]{1,0:T(8,128)(2,1)S(1)}, u32[]{:S(2)}, u32[]{:S(2)}) collective-permute-start(bf16[768,1280]{1,0:T(8,128)(2,1)S(1)} %cut.4), channel_id=1, source_target_pairs={{0,2},{2,0},{1,3},{3,1},{4,6},{6,4},{5,7},{7,5},{8,10},{10,8},{9,1... | collective-permute-start | bytes 5898248 | tf_op jit(solution)/shard_map/ppermute | solution.py:23
  10.5 18.2 %collective-permute-start.2 = (bf16[768,1280]{1,0:T(8,128)(2,1)S(1)}, bf16[768,1280]{1,0:T(8,128)(2,1)S(1)}, u32[]{:S(2)}, u32[]{:S(2)}) collective-permute-start(bf16[768,1280]{1,0:T(8,128)(2,1)S(1)} %cut.5), channel_id=1, source_target_pairs={{0,2},{2,0},{1,3},{3,1},{4,6},{6,4},{5,7},{7,5},{8,10},{10,8},{9,1... | collective-permute-start | bytes 5898248 | tf_op jit(solution)/shard_map/ppermute | solution.py:23
  14.9 7.2 %copy-start.3 = (bf16[768,1280]{1,0:T(8,128)(2,1)}, bf16[768,1280]{1,0:T(8,128)(2,1)S(1)}, u32[]{:S(2)}) copy-start(bf16[768,1280]{1,0:T(8,128)(2,1)S(1)} %collective-permute-done.1.a.g_next) | copy-start | bytes 5898244
  22.1 0.9 copy-start.6
  23.0 25.8 %collective-permute-start.4 = (bf16[4,80,1280]{2,1,0:T(8,128)(2,1)}, bf16[4,80,1280]{2,1,0:T(8,128)(2,1)}, u32[]{:S(2)}, u32[]{:S(2)}) collective-permute-start(bf16[4,80,1280]{2,1,0:T(8,128)(2,1)} %get-tuple-element.23.after), channel_id=1, source_target_pairs={{0,34},{2,8},{10,40},{8,18},{16,50},{18,24},{26,56},{24,2},{34,64}... | collective-permute-start | bytes 2457608 | tf_op jit(solution)/shard_map/ppermute | solution.py:35
  24.3 24.5 %collective-permute-start.5 = (bf16[4,80,1280]{2,1,0:T(8,128)(2,1)}, bf16[4,80,1280]{2,1,0:T(8,128)(2,1)}, u32[]{:S(2)}, u32[]{:S(2)}) collective-permute-start(bf16[4,80,1280]{2,1,0:T(8,128)(2,1)} %get-tuple-element.28), channel_id=1, source_target_pairs={{0,64},{2,18},{10,74},{8,24},{16,80},{18,2},{26,90},{24,8},{34,98}... | collective-permute-start | bytes 2457608 | tf_op jit(solution)/shard_map/ppermute | solution.py:35
  26.9 21.8 %collective-permute-start.6 = (bf16[4,80,1280]{2,1,0:T(8,128)(2,1)}, bf16[4,80,1280]{2,1,0:T(8,128)(2,1)}, u32[]{:S(2)}, u32[]{:S(2)}) collective-permute-start(bf16[4,80,1280]{2,1,0:T(8,128)(2,1)} %get-tuple-element.29), channel_id=1, source_target_pairs={{0,98},{2,24},{10,104},{8,2},{16,114},{18,8},{26,120},{24,18},{34,... | collective-permute-start | bytes 2457608 | tf_op jit(solution)/shard_map/ppermute | solution.py:35
  28.7 1.5 %copy-start.4 = (bf16[768,1280]{1,0:T(8,128)(2,1)S(1)}, bf16[768,1280]{1,0:T(8,128)(2,1)}, u32[]{:S(2)}) copy-start(bf16[768,1280]{1,0:T(8,128)(2,1)} %copy-done.3) | copy-start | bytes 5898244
  45.7 15.9 %collective-permute-start.3 = (bf16[2,160,1280]{2,1,0:T(8,128)(2,1)}, bf16[2,160,1280]{2,1,0:T(8,128)(2,1)}, u32[]{:S(2)}, u32[]{:S(2)}) collective-permute-start(bf16[2,160,1280]{2,1,0:T(8,128)(2,1)} %get-tuple-element.26), channel_id=1, source_target_pairs={{0,34},{2,8},{10,40},{8,18},{16,50},{18,24},{26,56},{24,2},{34,64}... | collective-permute-start | bytes 2457608 | tf_op jit(solution)/shard_map/ppermute | solution.py:35
  45.9 18.2 %collective-permute-start.9 = (bf16[2,160,1280]{2,1,0:T(8,128)(2,1)}, bf16[2,160,1280]{2,1,0:T(8,128)(2,1)}, u32[]{:S(2)}, u32[]{:S(2)}) collective-permute-start(bf16[2,160,1280]{2,1,0:T(8,128)(2,1)} %get-tuple-element.32), channel_id=1, source_target_pairs={{0,98},{2,24},{10,104},{8,2},{16,114},{18,8},{26,120},{24,18},{34,... | collective-permute-start | bytes 2457608 | tf_op jit(solution)/shard_map/ppermute | solution.py:35
  48.8 1.1 copy-start.7
  53.6 9.3 %copy-start.10 = (f32[80,1280]{1,0:T(8,128)}, f32[80,1280]{1,0:T(8,128)S(1)}, u32[]{:S(2)}) copy-start(f32[80,1280]{1,0:T(8,128)S(1)} %get-tuple-element.39.total) | copy-start | bytes 1228804
  53.6 8.0 %collective-permute-start.7 = (bf16[80,1280]{1,0:T(8,128)(2,1)S(1)}, bf16[80,1280]{1,0:T(8,128)(2,1)S(1)}, u32[]{:S(2)}, u32[]{:S(2)}) collective-permute-start(bf16[80,1280]{1,0:T(8,128)(2,1)S(1)} %get-tuple-element.30), channel_id=1, source_target_pairs={{0,16},{2,66},{10,26},{8,72},{16,0},{18,82},{26,10},{24,88},{34,50... | collective-permute-start | bytes 614408 | tf_op jit(solution)/shard_map/ppermute | solution.py:35
  62.9 1.2 copy-start.5
  64.0 24.2 %collective-permute-start.8 = (bf16[4,160,1280]{2,1,0:T(8,128)(2,1)}, bf16[4,160,1280]{2,1,0:T(8,128)(2,1)S(1)}, u32[]{:S(2)}, u32[]{:S(2)}) collective-permute-start(bf16[4,160,1280]{2,1,0:T(8,128)(2,1)} %copy-done.5), channel_id=1, source_target_pairs={{0,34},{2,8},{10,40},{8,18},{16,50},{18,24},{26,56},{24,2},{34,64}... | collective-permute-start | bytes 4915208 | tf_op jit(solution)/shard_map/ppermute | solution.py:35
  66.3 23.5 %collective-permute-start.10 = (bf16[4,160,1280]{2,1,0:T(8,128)(2,1)}, bf16[4,160,1280]{2,1,0:T(8,128)(2,1)}, u32[]{:S(2)}, u32[]{:S(2)}) collective-permute-start(bf16[4,160,1280]{2,1,0:T(8,128)(2,1)} %grow.3), channel_id=1, source_target_pairs={{0,98},{2,24},{10,104},{8,2},{16,114},{18,8},{26,120},{24,18},{34,... | collective-permute-start | bytes 4915208 | tf_op jit(solution)/shard_map/ppermute | solution.py:35
  69.3 9.4 %collective-permute-start.16 = (bf16[80,1280]{1,0:T(8,128)(2,1)}, bf16[80,1280]{1,0:T(8,128)(2,1)}, u32[]{:S(2)}, u32[]{:S(2)}) collective-permute-start(bf16[80,1280]{1,0:T(8,128)(2,1)} %get-tuple-element.40), channel_id=1, source_target_pairs={{0,10},{2,32},{10,16},{8,42},{16,26},{18,48},{26,0},{24,58},{34,40... | collective-permute-start | bytes 614408 | tf_op jit(solution)/shard_map/ppermute | solution.py:35
  70.2 8.6 %collective-permute-start.17 = (bf16[80,1280]{1,0:T(8,128)(2,1)}, bf16[80,1280]{1,0:T(8,128)(2,1)}, u32[]{:S(2)}, u32[]{:S(2)}) collective-permute-start(bf16[80,1280]{1,0:T(8,128)(2,1)} %get-tuple-element.41), channel_id=1, source_target_pairs={{0,26},{2,96},{10,0},{8,106},{16,10},{18,112},{26,16},{24,122},{34... | collective-permute-start | bytes 614408 | tf_op jit(solution)/shard_map/ppermute | solution.py:35
  78.8 1.0 copy-start.11
  81.0 18.6 %collective-permute-start.18 = (f32[40,1280]{1,0:T(8,128)S(1)}, f32[40,1280]{1,0:T(8,128)S(1)}, u32[]{:S(2)}, u32[]{:S(2)}) collective-permute-start(f32[40,1280]{1,0:T(8,128)S(1)} %get-tuple-element.43), channel_id=1, source_target_pairs={{0,4},{4,0},{1,5},{5,1},{2,6},{6,2},{3,7},{7,3},{8,12},{12,8},{9,1... | collective-permute-start | bytes 614408 | tf_op jit(solution)/shard_map/ppermute | solution.py:23
  82.3 18.4 %collective-permute-start.19 = (f32[40,1280]{1,0:T(8,128)S(1)}, f32[40,1280]{1,0:T(8,128)S(1)}, u32[]{:S(2)}, u32[]{:S(2)}) collective-permute-start(f32[40,1280]{1,0:T(8,128)S(1)} %get-tuple-element.42.mine), channel_id=1, source_target_pairs={{0,1},{1,0},{2,3},{3,2},{4,5},{5,4},{6,7},{7,6},{8,9},{9,8},{10,11... | collective-permute-start | bytes 614408 | tf_op jit(solution)/shard_map/ppermute | solution.py:23
  84.7 16.0 %collective-permute-start.20 = (f32[40,1280]{1,0:T(8,128)S(1)}, f32[40,1280]{1,0:T(8,128)S(1)}, u32[]{:S(2)}, u32[]{:S(2)}) collective-permute-start(f32[40,1280]{1,0:T(8,128)S(1)} %get-tuple-element.43), channel_id=1, source_target_pairs={{0,5},{1,4},{4,1},{5,0},{2,7},{3,6},{6,3},{7,2},{8,13},{9,12},{12,... | collective-permute-start | bytes 614408 | tf_op jit(solution)/shard_map/ppermute | solution.py:491
  93.8 0.9 copy-start.8
  94.7 19.8 %collective-permute-start.11 = (bf16[160,1280]{1,0:T(8,128)(2,1)}, bf16[160,1280]{1,0:T(8,128)(2,1)S(1)}, u32[]{:S(2)}, u32[]{:S(2)}) collective-permute-start(bf16[160,1280]{1,0:T(8,128)(2,1)} %get-tuple-element.34.late), channel_id=1, source_target_pairs={{0,10},{2,32},{10,16},{8,42},{16,26},{18,48},{26,0},{24,58},{34,40... | collective-permute-start | bytes 1228808 | tf_op jit(solution)/shard_map/ppermute | solution.py:35
  96.3 18.3 %collective-permute-start.12 = (bf16[160,1280]{1,0:T(8,128)(2,1)}, bf16[160,1280]{1,0:T(8,128)(2,1)S(1)}, u32[]{:S(2)}, u32[]{:S(2)}) collective-permute-start(bf16[160,1280]{1,0:T(8,128)(2,1)} %get-tuple-element.35), channel_id=1, source_target_pairs={{0,16},{2,66},{10,26},{8,72},{16,0},{18,82},{26,10},{24,88},{34,50... | collective-permute-start | bytes 1228808 | tf_op jit(solution)/shard_map/ppermute | solution.py:35
  99.6 15.0 %collective-permute-start.13 = (bf16[160,1280]{1,0:T(8,128)(2,1)}, bf16[160,1280]{1,0:T(8,128)(2,1)S(1)}, u32[]{:S(2)}, u32[]{:S(2)}) collective-permute-start(bf16[160,1280]{1,0:T(8,128)(2,1)} %get-tuple-element.36), channel_id=1, source_target_pairs={{0,26},{2,96},{10,0},{8,106},{16,10},{18,112},{26,16},{24,122},{34... | collective-permute-start | bytes 1228808 | tf_op jit(solution)/shard_map/ppermute | solution.py:35
  100.7 2.9 %copy-start.12 = (bf16[2560,1280]{1,0:T(8,128)(2,1)S(1)}, bf16[2560,1280]{1,0:T(8,128)(2,1)}, u32[]{:S(2)}) copy-start(bf16[2560,1280]{1,0:T(8,128)(2,1)} %left.1) | copy-start | bytes 19660804
  107.0 7.6 %copy-start.9 = (f32[160,1280]{1,0:T(8,128)S(1)}, f32[160,1280]{1,0:T(8,128)}, u32[]{:S(2)}) copy-start(f32[160,1280]{1,0:T(8,128)} %copy-done.8) | copy-start | bytes 2457604
  107.0 26.8 %all-to-all-start = ((f32[128,16,128]{2,1,0:T(8,128)}), f32[128,16,128]{2,1,0:T(8,128)S(1)}, u32[]{:S(2)}, u32[]{:S(2)}) async-start(f32[128,16,128]{2,1,0:T(8,128)} %left_product.1), calls=%async_computation | async-start | bytes 2097152 | tf_op jit(solution)/shard_map/all_to_all | solution.py:495
  115.4 16.3 %collective-permute-start.14 = (bf16[80,1280]{1,0:T(8,128)(2,1)}, bf16[80,1280]{1,0:T(8,128)(2,1)S(1)}, u32[]{:S(2)}, u32[]{:S(2)}) collective-permute-start(bf16[80,1280]{1,0:T(8,128)(2,1)} %get-tuple-element.38), channel_id=1, source_target_pairs={{0,4},{4,0},{1,5},{5,1},{2,6},{6,2},{3,7},{7,3},{8,12},{12,8},{9,1... | collective-permute-start | bytes 614408 | tf_op jit(solution)/shard_map/ppermute | solution.py:23
  131.7 9.6 %collective-permute-start.15 = (f32[40,1280]{1,0:T(8,128)S(1)}, f32[40,1280]{1,0:T(8,128)S(1)}, u32[]{:S(2)}, u32[]{:S(2)}) collective-permute-start(f32[40,1280]{1,0:T(8,128)S(1)} %dynamic-slice_bitcast_fusion), channel_id=1, source_target_pairs={{0,2},{2,0},{1,3},{3,1},{4,6},{6,4},{5,7},{7,5},{8,10},{10,8},{9,1... | collective-permute-start | bytes 614408 | tf_op jit(solution)/shard_map/ppermute | solution.py:23
  133.8 2.9 %copy-start.13 = (bf16[2560,1280]{1,0:T(8,128)(2,1)S(1)}, bf16[2560,1280]{1,0:T(8,128)(2,1)}, u32[]{:S(2)}) copy-start(bf16[2560,1280]{1,0:T(8,128)(2,1)} %right.1) | copy-start | bytes 19660804

commit v8 on v7

--- a/solution.py
+++ b/solution.py
@@ -10,6 +10,7 @@
 BF = jnp.bfloat16
 F32 = jnp.float32
 TILE = 640
+ANY = pl.BlockSpec(memory_space=pl.ANY)
 
 
 def contract(first_rows, second_rows):
@@ -81,8 +82,21 @@
     pltpu.make_async_copy(buffer, buffer, sem).wait()
 
 
-def own_kernel(place, a, b, out):
-    out[...] = contract(a[...], b[...])
+def own_kernel(place, a, b, out, lhs, rhs, lhs_sems, rhs_sem):
+    m = pl.program_id(0)
+    half = rhs.shape[1]
+
+    @pl.when(m == 0)
+    def _():
+        at = pl.ds(pl.multiple_of((place[1] ^ place[0]) * half, half), half)
+        pltpu.make_async_copy(b.at[:, at], rhs, rhs_sem).start()
+        for k in range(2):
+            at = pl.ds(pl.multiple_of(place[1] * half + k * TILE, TILE), TILE)
+            pltpu.make_async_copy(a.at[:, at], lhs.at[k], lhs_sems.at[k]).start()
+        wait_all(rhs, rhs_sem)
+
+    wait_all(lhs.at[m], lhs_sems.at[m])
+    out[...] = contract(lhs[m], rhs[...])
 
 
 def cross_kernel(place, a, b, partial, own, ahead1, ahead2, ahead3, held, buffer, held_sems, sem):
@@ -101,28 +115,33 @@
     pl.when(m == 1)(lambda: wait_all(buffer, sem))
 
 
-def cross_term(place, grads, grads_next, acts, acts_next):
-    tokens, half = grads_next.shape
-    anywhere = pl.BlockSpec(memory_space=pltpu.HBM)
-    cost = pl.CostEstimate(
-        flops=2 * tokens * half * half, bytes_accessed=10 * tokens * half, transcendentals=0
-    )
-    partial = pl.pallas_call(
+def cross_own(place, grads, acts):
+    tokens, half = grads.shape[0], grads.shape[1] // 2
+    return pl.pallas_call(
         own_kernel,
         out_shape=jax.ShapeDtypeStruct((half, half), F32),
         grid_spec=pltpu.PrefetchScalarGridSpec(
             num_scalar_prefetch=1,
             grid=(2,),
-            in_specs=[
-                pl.BlockSpec((tokens, TILE), lambda m, p: (0, p[1] * 2 + m)),
-                pl.BlockSpec((tokens, half), lambda m, p: (0, p[1] ^ p[0])),
-            ],
+            in_specs=[pl.BlockSpec(memory_space=pltpu.HBM)] * 2,
             out_specs=pl.BlockSpec((TILE, half), lambda m, p: (m, 0)),
+            scratch_shapes=[
+                pltpu.VMEM((2, tokens, TILE), BF),
+                pltpu.VMEM((tokens, half), BF),
+                pltpu.SemaphoreType.DMA((2,)),
+                pltpu.SemaphoreType.DMA,
+            ],
         ),
         compiler_params=pltpu.CompilerParams(vmem_limit_bytes=28 * 2**20),
-        cost_estimate=cost,
+        cost_estimate=pl.CostEstimate(
+            flops=2 * tokens * half * half, bytes_accessed=8 * tokens * half, transcendentals=0
+        ),
         name="cross_own",
     )(place, grads, acts)
+
+
+def cross_term(place, grads_next, acts_next, partial):
+    tokens, half = grads_next.shape
     out = jax.ShapeDtypeStruct((4, half // 16, half), BF)
     return pl.pallas_call(
         cross_kernel,
@@ -133,9 +152,9 @@
             in_specs=[
                 pl.BlockSpec((tokens, TILE), lambda m, p: (0, m)),
                 pl.BlockSpec((tokens, half), lambda m, p: (0, 0)),
-                anywhere,
-            ],
-            out_specs=[anywhere] * 4,
+                ANY,
+            ],
+            out_specs=[pl.BlockSpec(memory_space=pltpu.HBM)] * 4,
             scratch_shapes=[
                 pltpu.VMEM((2, TILE, half), F32),
                 pltpu.VMEM((2, TILE, half), BF),
@@ -144,7 +163,9 @@
             ],
         ),
         compiler_params=pltpu.CompilerParams(vmem_limit_bytes=28 * 2**20),
-        cost_estimate=cost,
+        cost_estimate=pl.CostEstimate(
+            flops=2 * tokens * half * half, bytes_accessed=10 * tokens * half, transcendentals=0
+        ),
         name="cross_term",
     )(place, grads_next, acts_next, partial)
 
@@ -191,7 +212,7 @@
 def factor_term(place, acts, grads, acts_next, grads_next, rest_next, after):
     tokens, width = acts.shape
     half = width // 2
-    anywhere = pl.BlockSpec(memory_space=pltpu.HBM)
+    hbm = pl.BlockSpec(memory_space=pltpu.HBM)
     out = jax.ShapeDtypeStruct((4, width // 16, half), BF)
     side = jax.ShapeDtypeStruct((2, width // 16, half), BF)
     return pl.pallas_call(
@@ -200,8 +221,8 @@
         grid_spec=pltpu.PrefetchScalarGridSpec(
             num_scalar_prefetch=1,
             grid=(4,),
-            in_specs=[anywhere] * 6,
-            out_specs=[anywhere] * 5,
+            in_specs=[hbm] * 2 + [ANY] * 4,
+            out_specs=[hbm] * 5,
             scratch_shapes=[
                 pltpu.VMEM((2, 2, tokens, TILE), BF),
                 pltpu.VMEM((2, tokens, half), BF),
@@ -228,8 +249,16 @@
 
 def fold_kernel(count, me, *refs):
     step = pl.program_id(0)
-    own, *others = refs[-4:]
-    total = add(*[part[0] for part in refs[:count]])
+    own, *others = refs[-6:-2]
+    held, sems = refs[-2:]
+
+    @pl.when(step == 0)
+    def _():
+        for k in range(4):
+            pltpu.make_async_copy(refs[0].at[(me[0] + k) & 3], held.at[k], sems.at[k]).start()
+
+    wait_all(held.at[step], sems.at[step])
+    total = add(held[step], *[part[0] for part in refs[1:count]])
 
     @pl.when(step == 0)
     def _():
@@ -252,10 +281,13 @@
         grid_spec=pltpu.PrefetchScalarGridSpec(
             num_scalar_prefetch=1,
             grid=(4,),
-            in_specs=[block] * len(parts) + [pl.BlockSpec(memory_space=pltpu.HBM)] * len(after),
+            in_specs=[pl.BlockSpec(memory_space=pltpu.HBM)]
+            + [block] * (len(parts) - 1)
+            + [ANY] * len(after),
             out_specs=[whole] * 4,
-        ),
-        compiler_params=pltpu.CompilerParams(vmem_limit_bytes=14 * 2**20),
+            scratch_shapes=[pltpu.VMEM((4, rows, width), BF), pltpu.SemaphoreType.DMA((4,))],
+        ),
+        compiler_params=pltpu.CompilerParams(vmem_limit_bytes=16 * 2**20),
         cost_estimate=pl.CostEstimate(
             flops=16 * rows * width, bytes_accessed=42 * rows * width, transcendentals=0
         ),
@@ -263,8 +295,7 @@
     )(me, *parts, *after)
 
 
-def settle_kernel(xl, total, r1, r2, r3, *refs):
-    mine, theirs = refs[-2:]
+def settle_kernel(xl, total, r1, r2, r3, mine, theirs):
     rows = mine.shape[0]
     for out, index in ((mine, xl[0]), (theirs, 1 - xl[0])):
         at = pl.ds(pl.multiple_of(index * rows, 8), rows)
@@ -272,7 +303,7 @@
         out[...] = value.astype(out.dtype)
 
 
-def settle(xl, total, received, dtype, *after):
+def settle(xl, total, received, dtype):
     rows, width = total.shape
     whole = pl.BlockSpec((rows, width), lambda s, x: (0, 0))
     part = pl.BlockSpec((rows // 2, width), lambda s, x: (0, 0))
@@ -282,7 +313,7 @@
         grid_spec=pltpu.PrefetchScalarGridSpec(
             num_scalar_prefetch=1,
             grid=(1,),
-            in_specs=[whole] * 4 + [pl.BlockSpec(memory_space=pltpu.HBM)] * len(after),
+            in_specs=[whole] * 4,
             out_specs=[part] * 2,
         ),
         compiler_params=pltpu.CompilerParams(vmem_limit_bytes=10 * 2**20),
@@ -290,82 +321,109 @@
             flops=4 * rows * width, bytes_accessed=14 * rows * width, transcendentals=0
         ),
         name="settle",
-    )(xl, total, *received, *after)
-
-
-def cut_kernel(index, place, a, b, out, held, sems, out_sem):
-    rows = held.shape[1]
-    width = held.shape[2]
-    at = pl.ds(pl.multiple_of(index(place) * width, width), width)
-    for owner, ref in enumerate((a, b)):
-
-        @pl.when(place[0] == owner)
-        def _():
-            for k in range(4):
-                part = ref.at[pl.ds(k * rows, rows), at]
-                pltpu.make_async_copy(part, held.at[k], sems.at[k]).start()
-
-    for k in range(4):
+    )(xl, total, *received)
+
+
+def cut_kernel(pairs, indices, place, *refs):
+    sources, outs = refs[: 2 * pairs], refs[-3 - pairs : -3]
+    held, sems, out_sem = refs[-3:]
+    rows, width = held.shape[2:]
+
+    for i in range(pairs):
+        at = pl.ds(pl.multiple_of(indices[i](place) * width, width), width)
+        for owner in range(2):
+
+            @pl.when(place[0] == owner)
+            def _():
+                for k in range(4):
+                    part = sources[2 * i + owner].at[pl.ds(k * rows, rows), at]
+                    pltpu.make_async_copy(part, held.at[i, k], sems.at[i, k]).start()
+
+    for i in range(pairs):
+        for k in range(4):
+            wait_all(held.at[i, k], sems.at[i, k])
+            target = outs[i].at[pl.ds(k * rows, rows)]
+            pltpu.make_async_copy(held.at[i, k], target, out_sem).start()
+    wait_all(held, out_sem)
+
+
+def cut(place, sources, indices, *after):
+    tokens, width = sources[0][0].shape
+    pairs = len(sources)
+    hbm = pl.BlockSpec(memory_space=pltpu.HBM)
+    dtype = sources[0][0].dtype
+    return pl.pallas_call(
+        functools.partial(cut_kernel, pairs, indices),
+        out_shape=[jax.ShapeDtypeStruct((tokens, width // 2), dtype)] * pairs,
+        grid_spec=pltpu.PrefetchScalarGridSpec(
+            num_scalar_prefetch=1,
+            grid=(1,),
+            in_specs=[hbm] * (2 * pairs) + [ANY] * len(after),
+            out_specs=[hbm] * pairs,
+            scratch_shapes=[
+                pltpu.VMEM((pairs, 4, tokens // 4, width // 2), dtype),
+                pltpu.SemaphoreType.DMA((pairs, 4)),
+                pltpu.SemaphoreType.DMA,
+            ],
+        ),
+        compiler_params=pltpu.CompilerParams(vmem_limit_bytes=8 * 2**20),
+        cost_estimate=pl.CostEstimate(
+            flops=0, bytes_accessed=2 * pairs * tokens * width, transcendentals=0
+        ),
+        name="cut",
+    )(place, *[x for pair in sources for x in pair], *after)
+
+
+def grow_kernel(side, x, received, *refs):
+    out, held, sems, out_sem = refs[-4:]
+    for k in range(2):
+        pltpu.make_async_copy(x.at[side * 2 + k], held.at[k], sems.at[k]).start()
+    for k in range(2):
         wait_all(held.at[k], sems.at[k])
-        pltpu.make_async_copy(held.at[k], out.at[pl.ds(k * rows, rows)], out_sem).start()
+        held[k] = add(held[k], received[k]).astype(BF)
+        pltpu.make_async_copy(held.at[k], out.at[side * 2 + k], out_sem).start()
     wait_all(held, out_sem)
 
 
-def cut(place, a, b, index):
-    tokens, width = a.shape
+def grow(x, received, side, *after):
     hbm = pl.BlockSpec(memory_space=pltpu.HBM)
     return pl.pallas_call(
-        functools.partial(cut_kernel, index),
-        out_shape=jax.ShapeDtypeStruct((tokens, width // 2), a.dtype),
-        grid_spec=pltpu.PrefetchScalarGridSpec(
-            num_scalar_prefetch=1,
-            grid=(1,),
-            in_specs=[hbm, hbm],
-            out_specs=hbm,
-            scratch_shapes=[
-                pltpu.VMEM((4, tokens // 4, width // 2), a.dtype),
-                pltpu.SemaphoreType.DMA((4,)),
-                pltpu.SemaphoreType.DMA,
-            ],
-        ),
-        compiler_params=pltpu.CompilerParams(vmem_limit_bytes=4 * 2**20),
-        cost_estimate=pl.CostEstimate(flops=0, bytes_accessed=2 * tokens * width, transcendentals=0),
-        name="cut",
-    )(place, a, b)
-
-
-def grow_kernel(x, received, after, out):
-    del after
-    out[...] = add(x[...], received[...]).astype(BF)
-
-
-def grow(x, received, side, after):
-    block = pl.BlockSpec((1,) + x.shape[1:], lambda s: (side * 2 + s, 0, 0))
-    return pl.pallas_call(
-        grow_kernel,
+        functools.partial(grow_kernel, side),
         out_shape=jax.ShapeDtypeStruct(x.shape, x.dtype),
-        grid=(2,),
-        in_specs=[
-            block,
-            pl.BlockSpec((1,) + x.shape[1:], lambda s: (s, 0, 0)),
-            pl.BlockSpec(memory_space=pltpu.HBM),
+        grid=(1,),
+        in_specs=[hbm, pl.BlockSpec(received.shape, lambda s: (0, 0, 0))] + [ANY] * len(after),
+        out_specs=hbm,
+        scratch_shapes=[
+            pltpu.VMEM(received.shape, x.dtype),
+            pltpu.SemaphoreType.DMA((2,)),
+            pltpu.SemaphoreType.DMA,
         ],
-        out_specs=block,
         input_output_aliases={0: 0},
         compiler_params=pltpu.CompilerParams(vmem_limit_bytes=8 * 2**20),
         cost_estimate=pl.CostEstimate(flops=x.size // 2, bytes_accessed=3 * x.size, transcendentals=0),
         name="grow",
-    )(x, received, after)
-
-
-def left_kernel(place, mine, other, partner, partner_other, left, out, total):
+    )(x, received, *after)
+
+
+def fetch_tiles(step, source, held, sems):
+    @pl.when(step == 0)
+    def _():
+        for k in range(4):
+            rows = source.at[pl.ds(k * TILE, TILE)]
+            pltpu.make_async_copy(rows, held.at[k], sems.at[k]).start()
+
+    wait_all(held.at[step], sems.at[step])
+
+
+def left_kernel(place, mine, other, partner, partner_other, left, out, total, held, sems):
     step = pl.program_id(0)
+    fetch_tiles(step, left, held, sems)
     at = pl.ds(pl.multiple_of((step & 1) * TILE, TILE), TILE)
     rows = mine.shape[0]
 
     def term(a, b):
         stacked = jnp.concatenate(split_pair(a[:, at] + b[:, at]), axis=0)
-        value = jnp.dot(stacked, left[...], preferred_element_type=F32)
+        value = jnp.dot(stacked, held[step], preferred_element_type=F32)
         total[...] = jnp.where(step == 0, value, total[...] + value)
 
     own = (step >> 1) == (place[1] ^ place[0])
@@ -398,11 +456,15 @@
         grid_spec=pltpu.PrefetchScalarGridSpec(
             num_scalar_prefetch=1,
             grid=(4,),
-            in_specs=[whole] * 4 + [pl.BlockSpec((TILE, half), lambda k, p: (k, 0))],
+            in_specs=[whole] * 4 + [pl.BlockSpec(memory_space=pltpu.HBM)],
             out_specs=pl.BlockSpec((128, 16, 128), lambda k, p: (0, 0, 0)),
-            scratch_shapes=[pltpu.VMEM((2 * rows, half), F32)],
-        ),
-        compiler_params=pltpu.CompilerParams(vmem_limit_bytes=16 * 2**20),
+            scratch_shapes=[
+                pltpu.VMEM((2 * rows, half), F32),
+                pltpu.VMEM((4, TILE, half), BF),
+                pltpu.SemaphoreType.DMA((4,)),
+            ],
+        ),
+        compiler_params=pltpu.CompilerParams(vmem_limit_bytes=20 * 2**20),
         cost_estimate=pl.CostEstimate(
             flops=256 * rows * half * half, bytes_accessed=4 * half * half, transcendentals=0
         ),
@@ -410,9 +472,10 @@
     )(place, mine, other, partner, partner_other, left)
 
 
-def right_kernel(place, blocks, right, late, out, rows_in):
+def right_kernel(place, blocks, right, late, out, rows_in, held, sems):
     del late
     step = pl.program_id(0)
+    fetch_tiles(step, right, held, sems)
     rows = out.shape[0]
     for near in range(2):
         for y in range(4):
@@ -424,7 +487,7 @@
                 rows_in[at + 16 : at + 32, :] = block[:, rows : 2 * rows]
                 rows_in[at + 32 : at + 40, :] = block[0:8, 2 * rows : 3 * rows]
     high, low = split_pair(rows_in[...])
-    value = contract(high, right[...]) + contract(low, right[...])
+    value = contract(high, held[step]) + contract(low, held[step])
     pl.when(step == 0)(lambda: out.__setitem__(..., value))
     pl.when(step > 0)(lambda: out.__setitem__(..., out[...] + value))
 
@@ -440,13 +503,17 @@
             grid=(4,),
             in_specs=[
                 pl.BlockSpec((64, 16, 128), lambda k, p: (p[2] >> 1, 0, 0)),
-                pl.BlockSpec((TILE, half), lambda k, p: (k, 0)),
                 pl.BlockSpec(memory_space=pltpu.HBM),
+                ANY,
             ],
             out_specs=pl.BlockSpec((rows, half), lambda k, p: (0, 0)),
-            scratch_shapes=[pltpu.VMEM((TILE, rows), F32)],
-        ),
-        compiler_params=pltpu.CompilerParams(vmem_limit_bytes=16 * 2**20),
+            scratch_shapes=[
+                pltpu.VMEM((TILE, rows), F32),
+                pltpu.VMEM((4, TILE, half), BF),
+                pltpu.SemaphoreType.DMA((4,)),
+            ],
+        ),
+        compiler_params=pltpu.CompilerParams(vmem_limit_bytes=20 * 2**20),
         cost_estimate=pl.CostEstimate(
             flops=640 * rows * half * half, bytes_accessed=4 * half * half, transcendentals=0
         ),
@@ -461,14 +528,24 @@
     token_total = tokens * 64
     first = o == 0
     h = c ^ ((z + y) & 1)
+    hidden, out_grad, left_inverse, right_inverse = (
+        pltpu.with_memory_space_constraint(x, pltpu.HBM)
+        for x in (hidden, out_grad, left_inverse, right_inverse)
+    )
     place = jnp.stack([o, h, z, y]).astype(jnp.int32)
     second_me = jnp.where(h == 0, y, z).astype(jnp.int32)[None]
 
-    grads_next = shift(cut(place, out_grad, out_grad, lambda p: 1 - p[1]), "c", 1)
-    acts_next = shift(cut(place, hidden, hidden, lambda p: (1 - p[1]) ^ p[0]), "c", 1)
-    rest_next = shift(cut(place, hidden, out_grad, lambda p: p[1]), "c", 1)
-
-    own, m1, m2, m3 = cross_term(place, out_grad, grads_next, hidden, acts_next)
+    grads_cut, acts_cut = cut(
+        place,
+        [(out_grad, out_grad), (hidden, hidden)],
+        [lambda p: 1 - p[1], lambda p: (1 - p[1]) ^ p[0]],
+    )
+    grads_next, acts_next = shift(grads_cut, "c", 1), shift(acts_cut, "c", 1)
+    partial = cross_own(place, out_grad, hidden)
+    (rest_cut,) = cut(place, [(hidden, out_grad)], [lambda p: p[1]], partial)
+    rest_next = shift(rest_cut, "c", 1)
+
+    own, m1, m2, m3 = cross_term(place, grads_next, acts_next, partial)
     m_parts = [own, turn(m1, 1, 0), turn(m2, 2, 0), turn(m3, 3, 0)]
 
     f_own, right, far_a, far_b, left = factor_term(
@@ -483,17 +560,17 @@
     from_left, from_right = turn(far_a, 1, 0), turn(far_b, -1, 0)
     m, *m_pieces = fold(second_me, m_parts, f_own)
     m_received = second_sends(m_pieces)
-    right = grow(right, from_left, 0, m_received[1])
-    left = grow(left, from_right, 1, m_received[1])
+    right = grow(right, from_left, 0, *m_received)
+    left = grow(left, from_right, 1, *m_received)
     f_parts = [f_own, turn(right, 1, 0), turn(left, -1, 0)]
 
     mine, theirs = settle(my_xl, m, m_received, F32)
     across = lax.ppermute(theirs, ("xl", "o"), [(i, 3 - i) for i in range(4)])
-    blocks = left_product(
+    products = left_product(
         place, mine, shift(theirs, "xl", 1), shift(mine, "o", 1), across, left_inverse
     )
-    blocks = lax.all_to_all(blocks, ("o", "c", "z", "y", "xl"), 0, 0, tiled=True)
-    f, *f_pieces = fold(second_me, f_parts)
+    blocks = lax.all_to_all(products, ("o", "c", "z", "y", "xl"), 0, 0, tiled=True)
+    f, *f_pieces = fold(second_me, f_parts, products)
     f_mine, f_theirs = settle(my_xl, f, second_sends(f_pieces), BF)
     update = right_product(place, blocks, right_inverse, f_pieces[0])
 

time: 143 us -> 139 us (0.972)
  local copies, waits for them, and re-layouts: 14.5 us -> 5 us
  Pallas kernels: 53.8 us -> 59.7 us
  starting transfers between devices: 40.2 us -> 38 us
  waiting for transfers between devices: 31.9 us -> 34 us
    unnamed x28 -> x12, local copies, waits for them, and re-layouts: 14.5 us -> 4.98 us
    pallas_call x6 -> x5, Pallas kernels: 13.4 us -> 16.8 us  [the longest x2 7.03 us: cut(): pl.pallas_call(functools.partial(cut_kernel, pairs, indices), out_shape=[...]
    ppermute x1, waiting for transfers between devices: 0.01 us -> 2.27 us  [per_device(): across = lax.ppermute(theirs, ('xl', 'o'), [(i, 3 - i) for i in range(4)])]
    pallas_call x1, Pallas kernels: 3.43 us -> 5.16 us  [left_product(): pl.pallas_call(left_kernel, out_shape=jax.ShapeDtypeStruct((128, 16, 128)...]
    pallas_call x2, Pallas kernels: 1.91 us -> 0.31 us  [settle(): pl.pallas_call(settle_kernel, out_shape=[jax.ShapeDtypeStruct((rows // 2,...]
    pallas_call x1, Pallas kernels: 4.68 us -> 6.16 us  [right_product(): pl.pallas_call(right_kernel, out_shape=jax.ShapeDtypeStruct((rows, half),...]
  transfers between devices with their start and end apart: 22 -> 22, of which waited for: 7 -> 10; matrix products, arithmetic and copies ran while one was open for 0% -> 0% of each run, Pallas kernels for 36% -> 38%
where the time goes in v8:
time: 139 us; the launch traced here: 138 us
  Pallas kernels  59.7 us (43%)
  starting transfers between devices  38 us (27%)
  waiting for transfers between devices  34 us (24%)
  local copies, waits for them, and re-layouts  5 us (4%)
    ppermute x13, starting transfers between devices, turn(): return lax.ppermute(x, ('z', 'y', 'c'), pairs)  23.2 us
    ppermute x13, waiting for transfers between devices, turn(): return lax.ppermute(x, ('z', 'y', 'c'), pairs)  16.2 us
    pallas_call x1, Pallas kernels, factor_term(): pl.pallas_call(factor_kernel, out_shape=[out, out, side, side, out], grid...  16.1 us
    ppermute x7, waiting for transfers between devices, shift(): return lax.ppermute(x, axis, [(i, (i + step) % size) for i in range(size)])  14.4 us
    pallas_call x2, Pallas kernels, fold(): pl.pallas_call(functools.partial(fold_kernel, len(parts)), out_shape=[jax...  7.98 us
    all_to_all x1, starting transfers between devices, per_device(): lax.all_to_all(products, ('o', 'c', 'z', 'y', 'xl'), 0, 0, tiled=True)  7.68 us
    pallas_call x1, Pallas kernels, cross_term(): pl.pallas_call(cross_kernel, out_shape=[out] * 4, grid_spec=pltpu.Prefetc...  7.19 us
    pallas_call x2, Pallas kernels, cut(): pl.pallas_call(functools.partial(cut_kernel, pairs, indices), out_shape=[...  7.03 us
  transfers between devices with their start and end apart: 22, of which 10 were waited for; matrix products, arithmetic and copies ran while one was open for 0% of the time, Pallas kernels for 38%

profile of v8, /device:TPU:1, one launch (start us, length us, event | category | flops | bytes accessed | tf_op | source)
XLA Modules:
  0.0 138.5 jit_solution(8011094345027867542)
XLA Ops:
  0.7 4.2 %cut.2 = (bf16[768,1280]{1,0:T(8,128)(2,1)S(1)}, bf16[768,1280]{1,0:T(8,128)(2,1)S(1)}) custom-call(s32[4]{0:T(128)S(1)} %pad_add_fusion.place, bf16[768,2560]{1,0:T(8,128)(2,1)} %g_own.1, bf16[768,2560]{1,0:T(8,128)(2,1)} %g_own.1, bf16[768,2560]{1,0:T(8,128)(2,1)} %h_own.1, bf16[768,2560]{1,0:T(8,128)(2,1)} %h_own.1), custom_call_target="tpu_custom_call" | custom-call | bytes 7864320 | tf_op jit(solution)/shard_map/cut/pallas_call | solution.py:355
  4.9 1.5 %collective-permute-start = (bf16[768,1280]{1,0:T(8,128)(2,1)S(1)}, bf16[768,1280]{1,0:T(8,128)(2,1)S(1)}, u32[]{:S(2)}, u32[]{:S(2)}) collective-permute-start(bf16[768,1280]{1,0:T(8,128)(2,1)S(1)} %get-tuple-element.25), channel_id=1, source_target_pairs={{0,2},{2,0},{1,3},{3,1},{4,6},{6,4},{5,7},{7,5},{8,10},{10,8},{9,1... | collective-permute-start | bytes 5898248 | tf_op jit(solution)/shard_map/ppermute | solution.py:24
  6.5 5.4 %cross_own.1.refs_2_.partial = f32[1280,1280]{1,0:T(8,128)S(1)} custom-call(s32[4]{0:T(128)S(1)} %pad_add_fusion.place, bf16[768,2560]{1,0:T(8,128)(2,1)} %g_own.1, bf16[768,2560]{1,0:T(8,128)(2,1)} %h_own.1), custom_call_target="tpu_custom_call" | custom-call | flops 2516582400 | bytes 7864320 | tf_op jit(solution)/shard_map/cross_own/pallas_call | solution.py:120
  11.9 2.9 %cut.3 = bf16[768,1280]{1,0:T(8,128)(2,1)S(1)} custom-call(s32[4]{0:T(128)S(1)} %pad_add_fusion.place, bf16[768,2560]{1,0:T(8,128)(2,1)} %h_own.1, bf16[768,2560]{1,0:T(8,128)(2,1)} %g_own.1, f32[1280,1280]{1,0:T(8,128)S(1)} %cross_own.1.refs_2_.partial), custom_call_target="tpu_custom_call" | custom-call | bytes 3932160 | tf_op jit(solution)/shard_map/cut/pallas_call | solution.py:355
  14.8 0.5 collective-permute-start.2
  15.3 7.2 %cross_term.1 = (bf16[4,80,1280]{2,1,0:T(8,128)(2,1)S(1)}, bf16[4,80,1280]{2,1,0:T(8,128)(2,1)}, bf16[4,80,1280]{2,1,0:T(8,128)(2,1)}, bf16[4,80,1280]{2,1,0:T(8,128)(2,1)}) custom-call(s32[4]{0:T(128)S(1)} %pad_add_fusion.place, bf16[768,1280]{1,0:T(8,128)(2,1)S(1)} %collective-permute-done.1.a.g_next, bf16[768,1280]{1,0:T(8,128)(2,1)S(1)} %collective-permute-done.b.h_next, ...), custom_call_target="tpu_custom_call" | custom-call | flops 2516582400 | bytes 9830400 | tf_op jit(solution)/shard_map/cross_term/pallas_call | solution.py:146
  22.5 0.9 copy-done.2
  23.4 1.4 collective-permute-start.4
  24.7 2.6 %collective-permute-start.5 = (bf16[4,80,1280]{2,1,0:T(8,128)(2,1)}, bf16[4,80,1280]{2,1,0:T(8,128)(2,1)}, u32[]{:S(2)}, u32[]{:S(2)}) collective-permute-start(bf16[4,80,1280]{2,1,0:T(8,128)(2,1)} %get-tuple-element.32), channel_id=1, source_target_pairs={{0,64},{2,18},{10,74},{8,24},{16,80},{18,2},{26,90},{24,8},{34,98}... | collective-permute-start | bytes 2457608 | tf_op jit(solution)/shard_map/ppermute | solution.py:36
  27.4 1.7 %collective-permute-start.6 = (bf16[4,80,1280]{2,1,0:T(8,128)(2,1)}, bf16[4,80,1280]{2,1,0:T(8,128)(2,1)}, u32[]{:S(2)}, u32[]{:S(2)}) collective-permute-start(bf16[4,80,1280]{2,1,0:T(8,128)(2,1)} %get-tuple-element.33), channel_id=1, source_target_pairs={{0,98},{2,24},{10,104},{8,2},{16,114},{18,8},{26,120},{24,18},{34,... | collective-permute-start | bytes 2457608 | tf_op jit(solution)/shard_map/ppermute | solution.py:36
  29.0 16.1 %factor_term.1 = (bf16[4,160,1280]{2,1,0:T(8,128)(2,1)S(1)}, bf16[4,160,1280]{2,1,0:T(8,128)(2,1)}, bf16[2,160,1280]{2,1,0:T(8,128)(2,1)}, bf16[2,160,1280]{2,1,0:T(8,128)(2,1)}, bf16[4,160,1280]{2,1,0:T(8,128)(2,1)S(1)}) custom-call(s32[4]{0:T(128)S(1)} %pad_add_fusion.place, bf16[768,2560]{1,0:T(8,128)(2,1)} %h_own.1, bf16[768,2560]{1,0:T(8,128)(2,1)} %g_own.1, ...), custom_call_target="tpu_custom_call" | custom-call | flops 10066329600 | bytes 15728640 | tf_op jit(solution)/shard_map/factor_term/pallas_call | solution.py:218
  45.1 1.2 copy-done
  46.4 2.9 %collective-permute-start.11 = (bf16[2,160,1280]{2,1,0:T(8,128)(2,1)}, bf16[2,160,1280]{2,1,0:T(8,128)(2,1)S(1)}, u32[]{:S(2)}, u32[]{:S(2)}) collective-permute-start(bf16[2,160,1280]{2,1,0:T(8,128)(2,1)} %get-tuple-element.38), channel_id=1, source_target_pairs={{0,98},{2,24},{10,104},{8,2},{16,114},{18,8},{26,120},{24,18},{34,... | collective-permute-start | bytes 2457608 | tf_op jit(solution)/shard_map/ppermute | solution.py:36
  49.3 1.1 copy-done.3
  50.5 4.8 %fold.2 = (f32[80,1280]{1,0:T(8,128)S(1)}, bf16[80,1280]{1,0:T(8,128)(2,1)}, bf16[80,1280]{1,0:T(8,128)(2,1)}, bf16[80,1280]{1,0:T(8,128)(2,1)}) custom-call(s32[1]{0:T(128)} %bitcast.1.me, bf16[4,80,1280]{2,1,0:T(8,128)(2,1)S(1)} %copy-done.3, bf16[4,80,1280]{2,1,0:T(8,128)(2,1)} %collective-permute-done.4.refs_1_, ...), custom_call_target="tpu_custom_call" | custom-call | flops 1638400 | bytes 4300800 | tf_op jit(solution)/shard_map/fold/pallas_call | solution.py:278
  55.3 1.4 %collective-permute-start.7 = (bf16[80,1280]{1,0:T(8,128)(2,1)}, bf16[80,1280]{1,0:T(8,128)(2,1)S(1)}, u32[]{:S(2)}, u32[]{:S(2)}) collective-permute-start(bf16[80,1280]{1,0:T(8,128)(2,1)} %get-tuple-element.34), channel_id=1, source_target_pairs={{0,10},{2,32},{10,16},{8,42},{16,26},{18,48},{26,0},{24,58},{34,40... | collective-permute-start | bytes 614408 | tf_op jit(solution)/shard_map/ppermute | solution.py:36
  56.7 3.3 %collective-permute-start.8 = (bf16[80,1280]{1,0:T(8,128)(2,1)}, bf16[80,1280]{1,0:T(8,128)(2,1)S(1)}, u32[]{:S(2)}, u32[]{:S(2)}) collective-permute-start(bf16[80,1280]{1,0:T(8,128)(2,1)} %get-tuple-element.35), channel_id=1, source_target_pairs={{0,16},{2,66},{10,26},{8,72},{16,0},{18,82},{26,10},{24,88},{34,50... | collective-permute-start | bytes 614408 | tf_op jit(solution)/shard_map/ppermute | solution.py:36
  60.0 1.6 %collective-permute-start.9 = (bf16[80,1280]{1,0:T(8,128)(2,1)}, bf16[80,1280]{1,0:T(8,128)(2,1)S(1)}, u32[]{:S(2)}, u32[]{:S(2)}) collective-permute-start(bf16[80,1280]{1,0:T(8,128)(2,1)} %get-tuple-element.36), channel_id=1, source_target_pairs={{0,26},{2,96},{10,0},{8,106},{16,10},{18,112},{26,16},{24,122},{34... | collective-permute-start | bytes 614408 | tf_op jit(solution)/shard_map/ppermute | solution.py:36
  61.6 0.9 collective-permute-done.7.refs_0_.r1
  62.4 3.4 %collective-permute-done.8.refs_1_.r2 = bf16[80,1280]{1,0:T(8,128)(2,1)S(1)} collective-permute-done((bf16[80,1280]{1,0:T(8,128)(2,1)}, bf16[80,1280]{1,0:T(8,128)(2,1)S(1)}, u32[]{:S(2)}, u32[]{:S(2)}) %collective-permute-start.8) | collective-permute-done | bytes 204832 | tf_op jit(solution)/shard_map/ppermute | solution.py:36
  65.8 0.1 settle.2
  65.9 1.3 collective-permute-start.13
  67.2 2.5 %collective-permute-start.14 = (f32[40,1280]{1,0:T(8,128)S(1)}, f32[40,1280]{1,0:T(8,128)S(1)}, u32[]{:S(2)}, u32[]{:S(2)}) collective-permute-start(f32[40,1280]{1,0:T(8,128)S(1)} %get-tuple-element.40.mine), channel_id=1, source_target_pairs={{0,1},{1,0},{2,3},{3,2},{4,5},{5,4},{6,7},{7,6},{8,9},{9,8},{10,11... | collective-permute-start | bytes 614408 | tf_op jit(solution)/shard_map/ppermute | solution.py:24
  69.7 0.1 collective-permute-start.15
  69.9 3.3 %grow.2 = bf16[4,160,1280]{2,1,0:T(8,128)(2,1)} custom-call(bf16[4,160,1280]{2,1,0:T(8,128)(2,1)} %get-tuple-element.29.x, bf16[2,160,1280]{2,1,0:T(8,128)(2,1)} %collective-permute-done.3.received, bf16[80,1280]{1,0:T(8,128)(2,1)S(1)} %collective-permute-done.7.refs_0_.r1, ...), custom_call_target="tpu_custom_call", output_to_operand_aliasing={{}: (0, {})} | custom-call | flops 409600 | bytes 2457600 | tf_op jit(solution)/shard_map/grow/pallas_call | solution.py:390
  73.1 1.3 collective-permute-start.10
  74.4 1.0 grow.3
  75.5 2.0 %collective-permute-start.12 = (bf16[4,160,1280]{2,1,0:T(8,128)(2,1)S(1)}, bf16[4,160,1280]{2,1,0:T(8,128)(2,1)S(1)}, u32[]{:S(2)}, u32[]{:S(2)}) collective-permute-start(bf16[4,160,1280]{2,1,0:T(8,128)(2,1)S(1)} %grow.3), channel_id=1, source_target_pairs={{0,98},{2,24},{10,104},{8,2},{16,114},{18,8},{26,120},{24,18},{34,... | collective-permute-start | bytes 4915208 | tf_op jit(solution)/shard_map/ppermute | solution.py:36
  77.5 1.5 %collective-permute-done.14.partner = f32[40,1280]{1,0:T(8,128)S(1)} collective-permute-done((f32[40,1280]{1,0:T(8,128)S(1)}, f32[40,1280]{1,0:T(8,128)S(1)}, u32[]{:S(2)}, u32[]{:S(2)}) %collective-permute-start.14) | collective-permute-done | bytes 204832 | tf_op jit(solution)/shard_map/ppermute | solution.py:24
  78.9 2.3 %collective-permute-done.15.partner_other = f32[40,1280]{1,0:T(8,128)S(1)} collective-permute-done((f32[40,1280]{1,0:T(8,128)S(1)}, f32[40,1280]{1,0:T(8,128)S(1)}, u32[]{:S(2)}, u32[]{:S(2)}) %collective-permute-start.15) | collective-permute-done | bytes 204832 | tf_op jit(solution)/shard_map/ppermute | solution.py:568
  81.2 5.2 %left_product.1.refs_3_ = f32[128,16,128]{2,1,0:T(8,128)} custom-call(s32[4]{0:T(128)S(1)} %pad_add_fusion.place, f32[40,1280]{1,0:T(8,128)S(1)} %get-tuple-element.40.mine, f32[40,1280]{1,0:T(8,128)S(1)} %collective-permute-done.13.other, f32[40,1280]{1,0:T(8,128)S(1)} %collective-permute-done.14.partner, ...), custom_call_target="tpu_custom_call" | custom-call | flops 16777216000 | bytes 6553600 | tf_op jit(solution)/shard_map/left_product/pallas_call | solution.py:453
  86.4 9.1 %collective-permute-done.10.refs_1_ = bf16[4,160,1280]{2,1,0:T(8,128)(2,1)S(1)} collective-permute-done((bf16[4,160,1280]{2,1,0:T(8,128)(2,1)}, bf16[4,160,1280]{2,1,0:T(8,128)(2,1)S(1)}, u32[]{:S(2)}, u32[]{:S(2)}) %collective-permute-start.10) | collective-permute-done | bytes 1638432 | tf_op jit(solution)/shard_map/ppermute | solution.py:36
  95.5 0.8 collective-permute-done.12.refs_2_
  96.3 3.2 %fold.3 = (f32[160,1280]{1,0:T(8,128)S(1)}, bf16[160,1280]{1,0:T(8,128)(2,1)}, bf16[160,1280]{1,0:T(8,128)(2,1)}, bf16[160,1280]{1,0:T(8,128)(2,1)}) custom-call(s32[1]{0:T(128)} %bitcast.1.me, bf16[4,160,1280]{2,1,0:T(8,128)(2,1)S(1)} %get-tuple-element.28.refs_4_.refs_0_, bf16[4,160,1280]{2,1,0:T(8,128)(2,1)S(1)} %collective-permute-done.10.refs_1_, ...), custom_call_target="tpu_custom_call" | custom-call | flops 3276800 | bytes 8601600 | tf_op jit(solution)/shard_map/fold/pallas_call | solution.py:278
  99.5 2.3 %collective-permute-start.16 = (bf16[160,1280]{1,0:T(8,128)(2,1)}, bf16[160,1280]{1,0:T(8,128)(2,1)S(1)}, u32[]{:S(2)}, u32[]{:S(2)}) collective-permute-start(bf16[160,1280]{1,0:T(8,128)(2,1)} %get-tuple-element.43.late), channel_id=1, source_target_pairs={{0,10},{2,32},{10,16},{8,42},{16,26},{18,48},{26,0},{24,58},{34,40... | collective-permute-start | bytes 1228808 | tf_op jit(solution)/shard_map/ppermute | solution.py:36
  101.7 2.4 %collective-permute-start.17 = (bf16[160,1280]{1,0:T(8,128)(2,1)}, bf16[160,1280]{1,0:T(8,128)(2,1)S(1)}, u32[]{:S(2)}, u32[]{:S(2)}) collective-permute-start(bf16[160,1280]{1,0:T(8,128)(2,1)} %get-tuple-element.44), channel_id=1, source_target_pairs={{0,16},{2,66},{10,26},{8,72},{16,0},{18,82},{26,10},{24,88},{34,50... | collective-permute-start | bytes 1228808 | tf_op jit(solution)/shard_map/ppermute | solution.py:36
  104.1 0.4 collective-permute-start.18
  104.5 7.7 %all-to-all-start = ((f32[128,16,128]{2,1,0:T(8,128)}), f32[128,16,128]{2,1,0:T(8,128)S(1)}, u32[]{:S(2)}, u32[]{:S(2)}) async-start(f32[128,16,128]{2,1,0:T(8,128)} %left_product.1.refs_3_), calls=%async_computation | async-start | bytes 2097152 | tf_op jit(solution)/shard_map/all_to_all | solution.py:572
  112.2 1.9 %collective-permute-done.17.r2 = bf16[160,1280]{1,0:T(8,128)(2,1)S(1)} collective-permute-done((bf16[160,1280]{1,0:T(8,128)(2,1)}, bf16[160,1280]{1,0:T(8,128)(2,1)S(1)}, u32[]{:S(2)}, u32[]{:S(2)}) %collective-permute-start.17) | collective-permute-done | bytes 409632 | tf_op jit(solution)/shard_map/ppermute | solution.py:36
  114.1 0.1 collective-permute-done.18.r3
  114.3 0.8 copy-done.4
  115.0 1.0 copy-done.5
  116.0 0.2 settle.3
  116.3 13.0 %collective-permute-done.19 = bf16[80,1280]{1,0:T(8,128)(2,1)S(1)} collective-permute-done((bf16[80,1280]{1,0:T(8,128)(2,1)S(1)}, bf16[80,1280]{1,0:T(8,128)(2,1)S(1)}, u32[]{:S(2)}, u32[]{:S(2)}) %collective-permute-start.19) | collective-permute-done | bytes 204832 | tf_op jit(solution)/shard_map/ppermute | solution.py:24
  129.4 1.0 collective-permute-start.20
  130.3 1.1 all-to-all-done.blocks
  131.5 6.2 %right_product.1 = f32[40,1280]{1,0:T(8,128)} custom-call(s32[4]{0:T(128)S(1)} %pad_add_fusion.place, f32[128,16,128]{2,1,0:T(8,128)S(1)} %all-to-all-done.blocks, bf16[2560,1280]{1,0:T(8,128)(2,1)} %right.1, bf16[160,1280]{1,0:T(8,128)(2,1)} %get-tuple-element.43.late), custom_call_target="tpu_custom_call" | custom-call | flops 41943040000 | bytes 6553600 | tf_op jit(solution)/shard_map/right_product/pallas_call | solution.py:498
  137.7 0.8 maximum_bitcast_fusion
  (26 shorter events, 0.5 us)
Async XLA Ops:
  4.9 10.4 %collective-permute-start = (bf16[768,1280]{1,0:T(8,128)(2,1)S(1)}, bf16[768,1280]{1,0:T(8,128)(2,1)S(1)}, u32[]{:S(2)}, u32[]{:S(2)}) collective-permute-start(bf16[768,1280]{1,0:T(8,128)(2,1)S(1)} %get-tuple-element.25), channel_id=1, source_target_pairs={{0,2},{2,0},{1,3},{3,1},{4,6},{6,4},{5,7},{7,5},{8,10},{10,8},{9,1... | collective-permute-start | bytes 5898248 | tf_op jit(solution)/shard_map/ppermute | solution.py:24
  6.4 8.9 %collective-permute-start.1 = (bf16[768,1280]{1,0:T(8,128)(2,1)S(1)}, bf16[768,1280]{1,0:T(8,128)(2,1)S(1)}, u32[]{:S(2)}, u32[]{:S(2)}) collective-permute-start(bf16[768,1280]{1,0:T(8,128)(2,1)S(1)} %get-tuple-element.26), channel_id=1, source_target_pairs={{0,2},{2,0},{1,3},{3,1},{4,6},{6,4},{5,7},{7,5},{8,10},{10,8},{9,1... | collective-permute-start | bytes 5898248 | tf_op jit(solution)/shard_map/ppermute | solution.py:24
  14.8 14.2 %collective-permute-start.2 = (bf16[768,1280]{1,0:T(8,128)(2,1)S(1)}, bf16[768,1280]{1,0:T(8,128)(2,1)S(1)}, u32[]{:S(2)}, u32[]{:S(2)}) collective-permute-start(bf16[768,1280]{1,0:T(8,128)(2,1)S(1)} %cut.3), channel_id=1, source_target_pairs={{0,2},{2,0},{1,3},{3,1},{4,6},{6,4},{5,7},{7,5},{8,10},{10,8},{9,1... | collective-permute-start | bytes 5898248 | tf_op jit(solution)/shard_map/ppermute | solution.py:24
  22.5 0.9 copy-start.2
  23.4 25.9 %collective-permute-start.4 = (bf16[4,80,1280]{2,1,0:T(8,128)(2,1)}, bf16[4,80,1280]{2,1,0:T(8,128)(2,1)}, u32[]{:S(2)}, u32[]{:S(2)}) collective-permute-start(bf16[4,80,1280]{2,1,0:T(8,128)(2,1)} %get-tuple-element.27.after), channel_id=1, source_target_pairs={{0,34},{2,8},{10,40},{8,18},{16,50},{18,24},{26,56},{24,2},{34,64}... | collective-permute-start | bytes 2457608 | tf_op jit(solution)/shard_map/ppermute | solution.py:36
  24.7 24.6 %collective-permute-start.5 = (bf16[4,80,1280]{2,1,0:T(8,128)(2,1)}, bf16[4,80,1280]{2,1,0:T(8,128)(2,1)}, u32[]{:S(2)}, u32[]{:S(2)}) collective-permute-start(bf16[4,80,1280]{2,1,0:T(8,128)(2,1)} %get-tuple-element.32), channel_id=1, source_target_pairs={{0,64},{2,18},{10,74},{8,24},{16,80},{18,2},{26,90},{24,8},{34,98}... | collective-permute-start | bytes 2457608 | tf_op jit(solution)/shard_map/ppermute | solution.py:36
  27.4 21.9 %collective-permute-start.6 = (bf16[4,80,1280]{2,1,0:T(8,128)(2,1)}, bf16[4,80,1280]{2,1,0:T(8,128)(2,1)}, u32[]{:S(2)}, u32[]{:S(2)}) collective-permute-start(bf16[4,80,1280]{2,1,0:T(8,128)(2,1)} %get-tuple-element.33), channel_id=1, source_target_pairs={{0,98},{2,24},{10,104},{8,2},{16,114},{18,8},{26,120},{24,18},{34,... | collective-permute-start | bytes 2457608 | tf_op jit(solution)/shard_map/ppermute | solution.py:36
  45.1 1.2 copy-start
  46.3 23.5 %collective-permute-start.3 = (bf16[2,160,1280]{2,1,0:T(8,128)(2,1)}, bf16[2,160,1280]{2,1,0:T(8,128)(2,1)}, u32[]{:S(2)}, u32[]{:S(2)}) collective-permute-start(bf16[2,160,1280]{2,1,0:T(8,128)(2,1)} %get-tuple-element.30), channel_id=1, source_target_pairs={{0,34},{2,8},{10,40},{8,18},{16,50},{18,24},{26,56},{24,2},{34,64}... | collective-permute-start | bytes 2457608 | tf_op jit(solution)/shard_map/ppermute | solution.py:36
  46.4 28.0 %collective-permute-start.11 = (bf16[2,160,1280]{2,1,0:T(8,128)(2,1)}, bf16[2,160,1280]{2,1,0:T(8,128)(2,1)S(1)}, u32[]{:S(2)}, u32[]{:S(2)}) collective-permute-start(bf16[2,160,1280]{2,1,0:T(8,128)(2,1)} %get-tuple-element.38), channel_id=1, source_target_pairs={{0,98},{2,24},{10,104},{8,2},{16,114},{18,8},{26,120},{24,18},{34,... | collective-permute-start | bytes 2457608 | tf_op jit(solution)/shard_map/ppermute | solution.py:36
  49.3 1.1 copy-start.3
  55.3 7.2 %collective-permute-start.7 = (bf16[80,1280]{1,0:T(8,128)(2,1)}, bf16[80,1280]{1,0:T(8,128)(2,1)S(1)}, u32[]{:S(2)}, u32[]{:S(2)}) collective-permute-start(bf16[80,1280]{1,0:T(8,128)(2,1)} %get-tuple-element.34), channel_id=1, source_target_pairs={{0,10},{2,32},{10,16},{8,42},{16,26},{18,48},{26,0},{24,58},{34,40... | collective-permute-start | bytes 614408 | tf_op jit(solution)/shard_map/ppermute | solution.py:36
  56.7 9.1 %collective-permute-start.8 = (bf16[80,1280]{1,0:T(8,128)(2,1)}, bf16[80,1280]{1,0:T(8,128)(2,1)S(1)}, u32[]{:S(2)}, u32[]{:S(2)}) collective-permute-start(bf16[80,1280]{1,0:T(8,128)(2,1)} %get-tuple-element.35), channel_id=1, source_target_pairs={{0,16},{2,66},{10,26},{8,72},{16,0},{18,82},{26,10},{24,88},{34,50... | collective-permute-start | bytes 614408 | tf_op jit(solution)/shard_map/ppermute | solution.py:36
  60.0 5.8 %collective-permute-start.9 = (bf16[80,1280]{1,0:T(8,128)(2,1)}, bf16[80,1280]{1,0:T(8,128)(2,1)S(1)}, u32[]{:S(2)}, u32[]{:S(2)}) collective-permute-start(bf16[80,1280]{1,0:T(8,128)(2,1)} %get-tuple-element.36), channel_id=1, source_target_pairs={{0,26},{2,96},{10,0},{8,106},{16,10},{18,112},{26,16},{24,122},{34... | collective-permute-start | bytes 614408 | tf_op jit(solution)/shard_map/ppermute | solution.py:36
  65.9 11.6 %collective-permute-start.13 = (f32[40,1280]{1,0:T(8,128)S(1)}, f32[40,1280]{1,0:T(8,128)S(1)}, u32[]{:S(2)}, u32[]{:S(2)}) collective-permute-start(f32[40,1280]{1,0:T(8,128)S(1)} %get-tuple-element.41), channel_id=1, source_target_pairs={{0,4},{4,0},{1,5},{5,1},{2,6},{6,2},{3,7},{7,3},{8,12},{12,8},{9,1... | collective-permute-start | bytes 614408 | tf_op jit(solution)/shard_map/ppermute | solution.py:24
  67.2 11.7 %collective-permute-start.14 = (f32[40,1280]{1,0:T(8,128)S(1)}, f32[40,1280]{1,0:T(8,128)S(1)}, u32[]{:S(2)}, u32[]{:S(2)}) collective-permute-start(f32[40,1280]{1,0:T(8,128)S(1)} %get-tuple-element.40.mine), channel_id=1, source_target_pairs={{0,1},{1,0},{2,3},{3,2},{4,5},{5,4},{6,7},{7,6},{8,9},{9,8},{10,11... | collective-permute-start | bytes 614408 | tf_op jit(solution)/shard_map/ppermute | solution.py:24
  69.7 11.5 %collective-permute-start.15 = (f32[40,1280]{1,0:T(8,128)S(1)}, f32[40,1280]{1,0:T(8,128)S(1)}, u32[]{:S(2)}, u32[]{:S(2)}) collective-permute-start(f32[40,1280]{1,0:T(8,128)S(1)} %get-tuple-element.41), channel_id=1, source_target_pairs={{0,5},{1,4},{4,1},{5,0},{2,7},{3,6},{6,3},{7,2},{8,13},{9,12},{12,... | collective-permute-start | bytes 614408 | tf_op jit(solution)/shard_map/ppermute | solution.py:568
  69.8 4.6 %copy-start.1 = (bf16[4,160,1280]{2,1,0:T(8,128)(2,1)S(1)}, bf16[4,160,1280]{2,1,0:T(8,128)(2,1)}, u32[]{:S(2)}) copy-start(bf16[4,160,1280]{2,1,0:T(8,128)(2,1)} %copy-done) | copy-start | bytes 4915204
  73.1 22.3 %collective-permute-start.10 = (bf16[4,160,1280]{2,1,0:T(8,128)(2,1)}, bf16[4,160,1280]{2,1,0:T(8,128)(2,1)S(1)}, u32[]{:S(2)}, u32[]{:S(2)}) collective-permute-start(bf16[4,160,1280]{2,1,0:T(8,128)(2,1)} %grow.2), channel_id=1, source_target_pairs={{0,34},{2,8},{10,40},{8,18},{16,50},{18,24},{26,56},{24,2},{34,64}... | collective-permute-start | bytes 4915208 | tf_op jit(solution)/shard_map/ppermute | solution.py:36
  75.5 20.8 %collective-permute-start.12 = (bf16[4,160,1280]{2,1,0:T(8,128)(2,1)S(1)}, bf16[4,160,1280]{2,1,0:T(8,128)(2,1)S(1)}, u32[]{:S(2)}, u32[]{:S(2)}) collective-permute-start(bf16[4,160,1280]{2,1,0:T(8,128)(2,1)S(1)} %grow.3), channel_id=1, source_target_pairs={{0,98},{2,24},{10,104},{8,2},{16,114},{18,8},{26,120},{24,18},{34,... | collective-permute-start | bytes 4915208 | tf_op jit(solution)/shard_map/ppermute | solution.py:36
  99.5 12.7 %collective-permute-start.16 = (bf16[160,1280]{1,0:T(8,128)(2,1)}, bf16[160,1280]{1,0:T(8,128)(2,1)S(1)}, u32[]{:S(2)}, u32[]{:S(2)}) collective-permute-start(bf16[160,1280]{1,0:T(8,128)(2,1)} %get-tuple-element.43.late), channel_id=1, source_target_pairs={{0,10},{2,32},{10,16},{8,42},{16,26},{18,48},{26,0},{24,58},{34,40... | collective-permute-start | bytes 1228808 | tf_op jit(solution)/shard_map/ppermute | solution.py:36
  101.7 12.4 %collective-permute-start.17 = (bf16[160,1280]{1,0:T(8,128)(2,1)}, bf16[160,1280]{1,0:T(8,128)(2,1)S(1)}, u32[]{:S(2)}, u32[]{:S(2)}) collective-permute-start(bf16[160,1280]{1,0:T(8,128)(2,1)} %get-tuple-element.44), channel_id=1, source_target_pairs={{0,16},{2,66},{10,26},{8,72},{16,0},{18,82},{26,10},{24,88},{34,50... | collective-permute-start | bytes 1228808 | tf_op jit(solution)/shard_map/ppermute | solution.py:36
  104.1 10.1 %collective-permute-start.18 = (bf16[160,1280]{1,0:T(8,128)(2,1)}, bf16[160,1280]{1,0:T(8,128)(2,1)S(1)}, u32[]{:S(2)}, u32[]{:S(2)}) collective-permute-start(bf16[160,1280]{1,0:T(8,128)(2,1)} %get-tuple-element.45), channel_id=1, source_target_pairs={{0,26},{2,96},{10,0},{8,106},{16,10},{18,112},{26,16},{24,122},{34... | collective-permute-start | bytes 1228808 | tf_op jit(solution)/shard_map/ppermute | solution.py:36
  104.5 27.0 %all-to-all-start = ((f32[128,16,128]{2,1,0:T(8,128)}), f32[128,16,128]{2,1,0:T(8,128)S(1)}, u32[]{:S(2)}, u32[]{:S(2)}) async-start(f32[128,16,128]{2,1,0:T(8,128)} %left_product.1.refs_3_), calls=%async_computation | async-start | bytes 2097152 | tf_op jit(solution)/shard_map/all_to_all | solution.py:572
  114.3 0.8 copy-start.4
  115.0 1.0 copy-start.5
  116.2 13.1 %collective-permute-start.19 = (bf16[80,1280]{1,0:T(8,128)(2,1)S(1)}, bf16[80,1280]{1,0:T(8,128)(2,1)S(1)}, u32[]{:S(2)}, u32[]{:S(2)}) collective-permute-start(bf16[80,1280]{1,0:T(8,128)(2,1)S(1)} %get-tuple-element.47), channel_id=1, source_target_pairs={{0,4},{4,0},{1,5},{5,1},{2,6},{6,2},{3,7},{7,3},{8,12},{12,8},{9,1... | collective-permute-start | bytes 614408 | tf_op jit(solution)/shard_map/ppermute | solution.py:24
  129.4 8.2 %collective-permute-start.20 = (f32[40,1280]{1,0:T(8,128)S(1)}, f32[40,1280]{1,0:T(8,128)S(1)}, u32[]{:S(2)}, u32[]{:S(2)}) collective-permute-start(f32[40,1280]{1,0:T(8,128)S(1)} %dynamic-slice_bitcast_fusion), channel_id=1, source_target_pairs={{0,2},{2,0},{1,3},{3,1},{4,6},{6,4},{5,7},{7,5},{8,10},{10,8},{9,1... | collective-permute-start | bytes 614408 | tf_op jit(solution)/shard_map/ppermute | solution.py:24

commit v9 on v8

--- a/solution.py
+++ b/solution.py
@@ -36,6 +36,10 @@
     return lax.ppermute(x, ("z", "y", "c"), pairs)
 
 
+def in_hbm(x):
+    return pltpu.with_memory_space_constraint(x, pltpu.HBM)
+
+
 def pick(x, dim, index):
     return lax.dynamic_index_in_dim(x, index, dim, keepdims=False)
 
@@ -142,7 +146,7 @@
 
 def cross_term(place, grads_next, acts_next, partial):
     tokens, half = grads_next.shape
-    out = jax.ShapeDtypeStruct((4, half // 16, half), BF)
+    out = pltpu.HBM((4, half // 16, half), BF)
     return pl.pallas_call(
         cross_kernel,
         out_shape=[out] * 4,
@@ -213,8 +217,8 @@
     tokens, width = acts.shape
     half = width // 2
     hbm = pl.BlockSpec(memory_space=pltpu.HBM)
-    out = jax.ShapeDtypeStruct((4, width // 16, half), BF)
-    side = jax.ShapeDtypeStruct((2, width // 16, half), BF)
+    out = pltpu.HBM((4, width // 16, half), BF)
+    side = pltpu.HBM((2, width // 16, half), BF)
     return pl.pallas_call(
         factor_kernel,
         out_shape=[out, out, side, side, out],
@@ -248,54 +252,40 @@
 
 
 def fold_kernel(count, me, *refs):
-    step = pl.program_id(0)
     own, *others = refs[-6:-2]
-    held, sems = refs[-2:]
-
-    @pl.when(step == 0)
-    def _():
-        for k in range(4):
-            pltpu.make_async_copy(refs[0].at[(me[0] + k) & 3], held.at[k], sems.at[k]).start()
-
-    wait_all(held.at[step], sems.at[step])
-    total = add(held[step], *[part[0] for part in refs[1:count]])
-
-    @pl.when(step == 0)
-    def _():
-        own[...] = total
-
-    for r, out in enumerate(others):
-
-        @pl.when(step == r + 1)
-        def _():
-            out[...] = total.astype(BF)
+    held, sem = refs[-2:]
+    copy = pltpu.make_async_copy(refs[0], held, sem)
+    copy.start()
+    copy.wait()
+    for r, out in enumerate([own, *others]):
+        at = (me[0] + r) & 3
+        out[...] = add(held[at], *[part[at] for part in refs[1:count]]).astype(out.dtype)
 
 
 def fold(me, parts, *after):
     _, rows, width = parts[0].shape
-    block = pl.BlockSpec((1, rows, width), lambda s, m: ((m[0] + s) & 3, 0, 0))
+    block = pl.BlockSpec((4, rows, width), lambda s, m: (0, 0, 0))
     whole = pl.BlockSpec((rows, width), lambda s, m: (0, 0))
     return pl.pallas_call(
         functools.partial(fold_kernel, len(parts)),
         out_shape=[jax.ShapeDtypeStruct((rows, width), t) for t in (F32, BF, BF, BF)],
         grid_spec=pltpu.PrefetchScalarGridSpec(
             num_scalar_prefetch=1,
-            grid=(4,),
+            grid=(1,),
             in_specs=[pl.BlockSpec(memory_space=pltpu.HBM)]
             + [block] * (len(parts) - 1)
             + [ANY] * len(after),
             out_specs=[whole] * 4,
-            scratch_shapes=[pltpu.VMEM((4, rows, width), BF), pltpu.SemaphoreType.DMA((4,))],
-        ),
-        compiler_params=pltpu.CompilerParams(vmem_limit_bytes=16 * 2**20),
-        cost_estimate=pl.CostEstimate(
-            flops=16 * rows * width, bytes_accessed=42 * rows * width, transcendentals=0
-        ),
+            scratch_shapes=[pltpu.VMEM((4, rows, width), BF), pltpu.SemaphoreType.DMA],
+        ),
+        compiler_params=pltpu.CompilerParams(vmem_limit_bytes=20 * 2**20),
+        cost_estimate=pl.CostEstimate(flops=0, bytes_accessed=0, transcendentals=0),
         name="fold",
-    )(me, *parts, *after)
-
-
-def settle_kernel(xl, total, r1, r2, r3, mine, theirs):
+    )(me, in_hbm(parts[0]), *parts[1:], *after)
+
+
+def settle_kernel(xl, total, r1, r2, r3, *refs):
+    mine, theirs = refs[-2:]
     rows = mine.shape[0]
     for out, index in ((mine, xl[0]), (theirs, 1 - xl[0])):
         at = pl.ds(pl.multiple_of(index * rows, 8), rows)
@@ -303,7 +293,7 @@
         out[...] = value.astype(out.dtype)
 
 
-def settle(xl, total, received, dtype):
+def settle(xl, total, received, dtype, *after):
     rows, width = total.shape
     whole = pl.BlockSpec((rows, width), lambda s, x: (0, 0))
     part = pl.BlockSpec((rows // 2, width), lambda s, x: (0, 0))
@@ -313,22 +303,19 @@
         grid_spec=pltpu.PrefetchScalarGridSpec(
             num_scalar_prefetch=1,
             grid=(1,),
-            in_specs=[whole] * 4,
+            in_specs=[whole] * 4 + [ANY] * len(after),
             out_specs=[part] * 2,
         ),
         compiler_params=pltpu.CompilerParams(vmem_limit_bytes=10 * 2**20),
-        cost_estimate=pl.CostEstimate(
-            flops=4 * rows * width, bytes_accessed=14 * rows * width, transcendentals=0
-        ),
+        cost_estimate=pl.CostEstimate(flops=0, bytes_accessed=0, transcendentals=0),
         name="settle",
-    )(xl, total, *received)
+    )(xl, total, *received, *after)
 
 
 def cut_kernel(pairs, indices, place, *refs):
-    sources, outs = refs[: 2 * pairs], refs[-3 - pairs : -3]
-    held, sems, out_sem = refs[-3:]
-    rows, width = held.shape[2:]
-
+    sources, outs, sem = refs[: 2 * pairs], refs[-1 - pairs : -1], refs[-1]
+    tokens, width = outs[0].shape
+    rows = tokens // 4
     for i in range(pairs):
         at = pl.ds(pl.multiple_of(indices[i](place) * width, width), width)
         for owner in range(2):
@@ -336,15 +323,12 @@
             @pl.when(place[0] == owner)
             def _():
                 for k in range(4):
-                    part = sources[2 * i + owner].at[pl.ds(k * rows, rows), at]
-                    pltpu.make_async_copy(part, held.at[i, k], sems.at[i, k]).start()
-
-    for i in range(pairs):
-        for k in range(4):
-            wait_all(held.at[i, k], sems.at[i, k])
-            target = outs[i].at[pl.ds(k * rows, rows)]
-            pltpu.make_async_copy(held.at[i, k], target, out_sem).start()
-    wait_all(held, out_sem)
+                    part = pl.ds(k * rows, rows)
+                    source = sources[2 * i + owner].at[part, at]
+                    pltpu.make_async_copy(source, outs[i].at[part], sem).start()
+
+    for out in outs:
+        wait_all(out, sem)
 
 
 def cut(place, sources, indices, *after):
@@ -354,17 +338,13 @@
     dtype = sources[0][0].dtype
     return pl.pallas_call(
         functools.partial(cut_kernel, pairs, indices),
-        out_shape=[jax.ShapeDtypeStruct((tokens, width // 2), dtype)] * pairs,
+        out_shape=[pltpu.HBM((tokens, width // 2), dtype)] * pairs,
         grid_spec=pltpu.PrefetchScalarGridSpec(
             num_scalar_prefetch=1,
             grid=(1,),
             in_specs=[hbm] * (2 * pairs) + [ANY] * len(after),
             out_specs=[hbm] * pairs,
-            scratch_shapes=[
-                pltpu.VMEM((pairs, 4, tokens // 4, width // 2), dtype),
-                pltpu.SemaphoreType.DMA((pairs, 4)),
-                pltpu.SemaphoreType.DMA,
-            ],
+            scratch_shapes=[pltpu.SemaphoreType.DMA],
         ),
         compiler_params=pltpu.CompilerParams(vmem_limit_bytes=8 * 2**20),
         cost_estimate=pl.CostEstimate(
@@ -389,7 +369,7 @@
     hbm = pl.BlockSpec(memory_space=pltpu.HBM)
     return pl.pallas_call(
         functools.partial(grow_kernel, side),
-        out_shape=jax.ShapeDtypeStruct(x.shape, x.dtype),
+        out_shape=pltpu.HBM(x.shape, x.dtype),
         grid=(1,),
         in_specs=[hbm, pl.BlockSpec(received.shape, lambda s: (0, 0, 0))] + [ANY] * len(after),
         out_specs=hbm,
@@ -400,9 +380,9 @@
         ],
         input_output_aliases={0: 0},
         compiler_params=pltpu.CompilerParams(vmem_limit_bytes=8 * 2**20),
-        cost_estimate=pl.CostEstimate(flops=x.size // 2, bytes_accessed=3 * x.size, transcendentals=0),
+        cost_estimate=pl.CostEstimate(flops=0, bytes_accessed=0, transcendentals=0),
         name="grow",
-    )(x, received, *after)
+    )(in_hbm(x), received, *after)
 
 
 def fetch_tiles(step, source, held, sems):
@@ -528,10 +508,8 @@
     token_total = tokens * 64
     first = o == 0
     h = c ^ ((z + y) & 1)
-    hidden, out_grad, left_inverse, right_inverse = (
-        pltpu.with_memory_space_constraint(x, pltpu.HBM)
-        for x in (hidden, out_grad, left_inverse, right_inverse)
-    )
+    hidden, out_grad = in_hbm(hidden), in_hbm(out_grad)
+    left_inverse, right_inverse = in_hbm(left_inverse), in_hbm(right_inverse)
     place = jnp.stack([o, h, z, y]).astype(jnp.int32)
     second_me = jnp.where(h == 0, y, z).astype(jnp.int32)[None]
 
@@ -549,7 +527,7 @@
     m_parts = [own, turn(m1, 1, 0), turn(m2, 2, 0), turn(m3, 3, 0)]
 
     f_own, right, far_a, far_b, left = factor_term(
-        place, hidden, out_grad, acts_next, grads_next, rest_next, m1
+        place, hidden, out_grad, acts_next, grads_next, rest_next, in_hbm(m1)
     )
 
     my_xl = xl.astype(jnp.int32)[None]
@@ -558,7 +536,7 @@
         return [turn(piece, s, 1) for s, piece in enumerate(pieces, 1)]
 
     from_left, from_right = turn(far_a, 1, 0), turn(far_b, -1, 0)
-    m, *m_pieces = fold(second_me, m_parts, f_own)
+    m, *m_pieces = fold(second_me, m_parts, in_hbm(f_own))
     m_received = second_sends(m_pieces)
     right = grow(right, from_left, 0, *m_received)
     left = grow(left, from_right, 1, *m_received)
@@ -571,7 +549,7 @@
     )
     blocks = lax.all_to_all(products, ("o", "c", "z", "y", "xl"), 0, 0, tiled=True)
     f, *f_pieces = fold(second_me, f_parts, products)
-    f_mine, f_theirs = settle(my_xl, f, second_sends(f_pieces), BF)
+    f_mine, f_theirs = settle(my_xl, f, second_sends(f_pieces), BF, blocks)
     update = right_product(place, blocks, right_inverse, f_pieces[0])
 
     f = add(f_mine, shift(f_theirs, "xl", 1))

time: 139 us -> 311 us (2.24)
  Pallas kernels: 59.7 us -> 233 us
  local copies, waits for them, and re-layouts: 5 us -> 0.02 us
  starting transfers between devices: 38 us -> 42.9 us
    pallas_call x2, Pallas kernels: 7.03 us -> 182 us  [cut(): pl.pallas_call(functools.partial(cut_kernel, pairs, indices), out_shape=[...]
    ppermute x7, waiting for transfers between devices: 14.4 us -> 6.12 us  [shift(): return lax.ppermute(x, axis, [(i, (i + step) % size) for i in range(size)])]
    ppermute x13, waiting for transfers between devices: 16.2 us -> 22.6 us  [turn(): return lax.ppermute(x, ('z', 'y', 'c'), pairs)]
    unnamed x12 -> x0, local copies, waits for them, and re-layouts: 4.98 us -> none
  transfers between devices with their start and end apart: 22 -> 22, of which waited for: 10 -> 12; matrix products, arithmetic and copies ran while one was open for 0% -> 0% of each run, Pallas kernels for 38% -> 36%
where the time goes in v9:
time: 311 us; the launch traced here: 309 us
  Pallas kernels  233 us (75%)
  starting transfers between devices  42.9 us (14%)
  waiting for transfers between devices  31.4 us (10%)
    pallas_call x2, Pallas kernels, cut(): pl.pallas_call(functools.partial(cut_kernel, pairs, indices), out_shape=[...  182 us
    ppermute x13, starting transfers between devices, turn(): return lax.ppermute(x, ('z', 'y', 'c'), pairs)  26.1 us
    ppermute x13, waiting for transfers between devices, turn(): return lax.ppermute(x, ('z', 'y', 'c'), pairs)  22.6 us
    pallas_call x1, Pallas kernels, factor_term(): pl.pallas_call(factor_kernel, out_shape=[out, out, side, side, out], grid...  14.9 us
    ppermute x7, starting transfers between devices, shift(): return lax.ppermute(x, axis, [(i, (i + step) % size) for i in range(size)])  8.43 us
    all_to_all x1, starting transfers between devices, per_device(): lax.all_to_all(products, ('o', 'c', 'z', 'y', 'xl'), 0, 0, tiled=True)  8.26 us
    pallas_call x2, Pallas kernels, fold(): pl.pallas_call(functools.partial(fold_kernel, len(parts)), out_shape=[jax...  7.79 us
    pallas_call x1, Pallas kernels, cross_term(): pl.pallas_call(cross_kernel, out_shape=[out] * 4, grid_spec=pltpu.Prefetc...  6.42 us
  transfers between devices with their start and end apart: 22, of which 12 were waited for; matrix products, arithmetic and copies ran while one was open for 0% of the time, Pallas kernels for 36%

profile of v9, /device:TPU:1, one launch (start us, length us, event | category | flops | bytes accessed | tf_op | source)
XLA Modules:
  0.0 308.9 jit_solution(4200021218564402421)
XLA Ops:
  0.6 0.1 pad_add_fusion.place
  0.7 120.8 %cut.2 = (bf16[768,1280]{1,0:T(8,128)(2,1)}, bf16[768,1280]{1,0:T(8,128)(2,1)}) custom-call(s32[4]{0:T(128)S(1)} %pad_add_fusion.place, bf16[768,2560]{1,0:T(8,128)(2,1)} %g_own.1, bf16[768,2560]{1,0:T(8,128)(2,1)} %g_own.1, bf16[768,2560]{1,0:T(8,128)(2,1)} %h_own.1, bf16[768,2560]{1,0:T(8,128)(2,1)} %h_own.1), custom_call_target="tpu_custom_call" | custom-call | bytes 7864320 | tf_op jit(solution)/shard_map/cut/pallas_call | solution.py:339
  121.5 1.5 collective-permute-start
  123.0 0.1 collective-permute-start.1
  123.1 5.4 %cross_own.1.refs_2_.partial = f32[1280,1280]{1,0:T(8,128)S(1)} custom-call(s32[4]{0:T(128)S(1)} %pad_add_fusion.place, bf16[768,2560]{1,0:T(8,128)(2,1)} %g_own.1, bf16[768,2560]{1,0:T(8,128)(2,1)} %h_own.1), custom_call_target="tpu_custom_call" | custom-call | flops 2516582400 | bytes 7864320 | tf_op jit(solution)/shard_map/cross_own/pallas_call | solution.py:124
  128.5 61.2 %cut.3 = bf16[768,1280]{1,0:T(8,128)(2,1)} custom-call(s32[4]{0:T(128)S(1)} %pad_add_fusion.place, bf16[768,2560]{1,0:T(8,128)(2,1)} %h_own.1, bf16[768,2560]{1,0:T(8,128)(2,1)} %g_own.1, f32[1280,1280]{1,0:T(8,128)S(1)} %cross_own.1.refs_2_.partial), custom_call_target="tpu_custom_call" | custom-call | bytes 3932160 | tf_op jit(solution)/shard_map/cut/pallas_call | solution.py:339
  189.7 0.5 collective-permute-start.2
  190.2 0.0 collective-permute-done.b.h_next
  190.2 6.4 %cross_term.1 = (bf16[4,80,1280]{2,1,0:T(8,128)(2,1)}, bf16[4,80,1280]{2,1,0:T(8,128)(2,1)}, bf16[4,80,1280]{2,1,0:T(8,128)(2,1)}, bf16[4,80,1280]{2,1,0:T(8,128)(2,1)}) custom-call(s32[4]{0:T(128)S(1)} %pad_add_fusion.place, bf16[768,1280]{1,0:T(8,128)(2,1)S(1)} %collective-permute-done.1.a.g_next, bf16[768,1280]{1,0:T(8,128)(2,1)S(1)} %collective-permute-done.b.h_next, ...), custom_call_target="tpu_custom_call" | custom-call | flops 2516582400 | bytes 9830400 | tf_op jit(solution)/shard_map/cross_term/pallas_call | solution.py:150
  196.7 1.4 collective-permute-start.4
  198.1 2.6 collective-permute-start.5
  200.7 1.6 collective-permute-start.6
  202.4 14.9 %factor_term.1 = (bf16[4,160,1280]{2,1,0:T(8,128)(2,1)}, bf16[4,160,1280]{2,1,0:T(8,128)(2,1)}, bf16[2,160,1280]{2,1,0:T(8,128)(2,1)}, bf16[2,160,1280]{2,1,0:T(8,128)(2,1)}, bf16[4,160,1280]{2,1,0:T(8,128)(2,1)}) custom-call(s32[4]{0:T(128)S(1)} %pad_add_fusion.place, bf16[768,2560]{1,0:T(8,128)(2,1)} %h_own.1, bf16[768,2560]{1,0:T(8,128)(2,1)} %g_own.1, ...), custom_call_target="tpu_custom_call" | custom-call | flops 10066329600 | bytes 15728640 | tf_op jit(solution)/shard_map/factor_term/pallas_call | solution.py:222
  217.3 0.2 collective-permute-start.3
  217.4 2.8 collective-permute-start.11
  220.3 3.5 %fold.2 = (f32[80,1280]{1,0:T(8,128)S(1)}, bf16[80,1280]{1,0:T(8,128)(2,1)}, bf16[80,1280]{1,0:T(8,128)(2,1)}, bf16[80,1280]{1,0:T(8,128)(2,1)}) custom-call(s32[1]{0:T(128)} %bitcast.1.me, bf16[4,80,1280]{2,1,0:T(8,128)(2,1)} %get-tuple-element.31.refs_0_, bf16[4,80,1280]{2,1,0:T(8,128)(2,1)S(1)} %collective-permute-done.4.refs_1_, ...), custom_call_target="tpu_custom_call" | custom-call | tf_op jit(solution)/shard_map/fold/pallas_call | solution.py:269
  223.9 2.1 collective-permute-start.7
  226.0 3.3 %collective-permute-start.8 = (bf16[80,1280]{1,0:T(8,128)(2,1)}, bf16[80,1280]{1,0:T(8,128)(2,1)S(1)}, u32[]{:S(2)}, u32[]{:S(2)}) collective-permute-start(bf16[80,1280]{1,0:T(8,128)(2,1)} %get-tuple-element.35), channel_id=1, source_target_pairs={{0,16},{2,66},{10,26},{8,72},{16,0},{18,82},{26,10},{24,88},{34,50... | collective-permute-start | bytes 614408 | tf_op jit(solution)/shard_map/ppermute | solution.py:36
  229.3 0.9 collective-permute-start.9
  230.2 2.6 collective-permute-done.7.refs_0_.r1
  232.8 2.2 collective-permute-done.8.refs_1_.r2
  234.9 0.3 collective-permute-done.9.refs_2_.r3
  235.2 0.1 settle.2
  235.3 1.3 collective-permute-start.13
  236.6 2.5 collective-permute-start.14
  239.1 0.2 collective-permute-start.15
  239.3 2.0 grow.2
  241.3 2.8 collective-permute-start.10
  244.0 2.0 grow.3
  246.1 1.4 collective-permute-start.12
  247.4 0.9 collective-permute-done.14.partner
  248.3 2.3 collective-permute-done.15.partner_other
  250.6 5.1 %left_product.1.refs_3_ = f32[128,16,128]{2,1,0:T(8,128)} custom-call(s32[4]{0:T(128)S(1)} %pad_add_fusion.place, f32[40,1280]{1,0:T(8,128)S(1)} %get-tuple-element.40.mine, f32[40,1280]{1,0:T(8,128)S(1)} %collective-permute-done.13.other, f32[40,1280]{1,0:T(8,128)S(1)} %collective-permute-done.14.partner, ...), custom_call_target="tpu_custom_call" | custom-call | flops 16777216000 | bytes 6553600 | tf_op jit(solution)/shard_map/left_product/pallas_call | solution.py:433
  255.7 8.3 %all-to-all-start = ((f32[128,16,128]{2,1,0:T(8,128)}), f32[128,16,128]{2,1,0:T(8,128)S(1)}, u32[]{:S(2)}, u32[]{:S(2)}) async-start(f32[128,16,128]{2,1,0:T(8,128)} %left_product.1.refs_3_), calls=%async_computation | async-start | bytes 2097152 | tf_op jit(solution)/shard_map/all_to_all | solution.py:550
  264.0 0.2 collective-permute-done.10.refs_1_
  264.2 7.5 %collective-permute-done.12.refs_2_ = bf16[4,160,1280]{2,1,0:T(8,128)(2,1)} collective-permute-done((bf16[4,160,1280]{2,1,0:T(8,128)(2,1)}, bf16[4,160,1280]{2,1,0:T(8,128)(2,1)}, u32[]{:S(2)}, u32[]{:S(2)}) %collective-permute-start.12) | collective-permute-done | bytes 1638432 | tf_op jit(solution)/shard_map/ppermute | solution.py:36
  271.7 4.2 %fold.3 = (f32[160,1280]{1,0:T(8,128)S(1)}, bf16[160,1280]{1,0:T(8,128)(2,1)}, bf16[160,1280]{1,0:T(8,128)(2,1)}, bf16[160,1280]{1,0:T(8,128)(2,1)}) custom-call(s32[1]{0:T(128)} %bitcast.1.me, bf16[4,160,1280]{2,1,0:T(8,128)(2,1)} %get-tuple-element.28.refs_4_.refs_0_, bf16[4,160,1280]{2,1,0:T(8,128)(2,1)S(1)} %collective-permute-done.10.refs_1_, ...), custom_call_target="tpu_custom_call" | custom-call | tf_op jit(solution)/shard_map/fold/pallas_call | solution.py:269
  275.9 3.6 %collective-permute-start.16 = (bf16[160,1280]{1,0:T(8,128)(2,1)}, bf16[160,1280]{1,0:T(8,128)(2,1)S(1)}, u32[]{:S(2)}, u32[]{:S(2)}) collective-permute-start(bf16[160,1280]{1,0:T(8,128)(2,1)} %get-tuple-element.43.late), channel_id=1, source_target_pairs={{0,10},{2,32},{10,16},{8,42},{16,26},{18,48},{26,0},{24,58},{34,40... | collective-permute-start | bytes 1228808 | tf_op jit(solution)/shard_map/ppermute | solution.py:36
  279.5 3.3 %collective-permute-start.17 = (bf16[160,1280]{1,0:T(8,128)(2,1)}, bf16[160,1280]{1,0:T(8,128)(2,1)S(1)}, u32[]{:S(2)}, u32[]{:S(2)}) collective-permute-start(bf16[160,1280]{1,0:T(8,128)(2,1)} %get-tuple-element.44), channel_id=1, source_target_pairs={{0,16},{2,66},{10,26},{8,72},{16,0},{18,82},{26,10},{24,88},{34,50... | collective-permute-start | bytes 1228808 | tf_op jit(solution)/shard_map/ppermute | solution.py:36
  282.9 0.4 all-to-all-done.refs_0_.blocks
  283.3 4.7 %collective-permute-done.16.r1 = bf16[160,1280]{1,0:T(8,128)(2,1)S(1)} collective-permute-done((bf16[160,1280]{1,0:T(8,128)(2,1)}, bf16[160,1280]{1,0:T(8,128)(2,1)S(1)}, u32[]{:S(2)}, u32[]{:S(2)}) %collective-permute-start.16) | collective-permute-done | bytes 409632 | tf_op jit(solution)/shard_map/ppermute | solution.py:36
  288.0 5.1 %collective-permute-done.17.r2 = bf16[160,1280]{1,0:T(8,128)(2,1)S(1)} collective-permute-done((bf16[160,1280]{1,0:T(8,128)(2,1)}, bf16[160,1280]{1,0:T(8,128)(2,1)S(1)}, u32[]{:S(2)}, u32[]{:S(2)}) %collective-permute-start.17) | collective-permute-done | bytes 409632 | tf_op jit(solution)/shard_map/ppermute | solution.py:36
  293.1 0.1 collective-permute-done.18.r3
  293.2 0.8 settle.3
  294.0 5.2 %collective-permute-done.19 = bf16[80,1280]{1,0:T(8,128)(2,1)S(1)} collective-permute-done((bf16[80,1280]{1,0:T(8,128)(2,1)}, bf16[80,1280]{1,0:T(8,128)(2,1)S(1)}, u32[]{:S(2)}, u32[]{:S(2)}) %collective-permute-start.19) | collective-permute-done | bytes 204832 | tf_op jit(solution)/shard_map/ppermute | solution.py:24
  299.3 2.6 collective-permute-start.20
  301.8 6.2 %right_product.1 = f32[40,1280]{1,0:T(8,128)} custom-call(s32[4]{0:T(128)S(1)} %pad_add_fusion.place, f32[128,16,128]{2,1,0:T(8,128)S(1)} %all-to-all-done.refs_0_.blocks, bf16[2560,1280]{1,0:T(8,128)(2,1)} %right.1, bf16[160,1280]{1,0:T(8,128)(2,1)} %get-tuple-element.43.late), custom_call_target="tpu_custom_call" | custom-call | flops 41943040000 | bytes 6553600 | tf_op jit(solution)/shard_map/right_product/pallas_call | solution.py:478
  308.1 0.8 maximum_bitcast_fusion
  (14 shorter events, 0.1 us)
Async XLA Ops:
  121.5 68.7 %collective-permute-start = (bf16[768,1280]{1,0:T(8,128)(2,1)}, bf16[768,1280]{1,0:T(8,128)(2,1)S(1)}, u32[]{:S(2)}, u32[]{:S(2)}) collective-permute-start(bf16[768,1280]{1,0:T(8,128)(2,1)} %get-tuple-element.25), channel_id=1, source_target_pairs={{0,2},{2,0},{1,3},{3,1},{4,6},{6,4},{5,7},{7,5},{8,10},{10,8},{9,1... | collective-permute-start | bytes 5898248 | tf_op jit(solution)/shard_map/ppermute | solution.py:24
  123.0 67.2 %collective-permute-start.1 = (bf16[768,1280]{1,0:T(8,128)(2,1)}, bf16[768,1280]{1,0:T(8,128)(2,1)S(1)}, u32[]{:S(2)}, u32[]{:S(2)}) collective-permute-start(bf16[768,1280]{1,0:T(8,128)(2,1)} %get-tuple-element.26), channel_id=1, source_target_pairs={{0,2},{2,0},{1,3},{3,1},{4,6},{6,4},{5,7},{7,5},{8,10},{10,8},{9,1... | collective-permute-start | bytes 5898248 | tf_op jit(solution)/shard_map/ppermute | solution.py:24
  189.7 12.6 %collective-permute-start.2 = (bf16[768,1280]{1,0:T(8,128)(2,1)}, bf16[768,1280]{1,0:T(8,128)(2,1)S(1)}, u32[]{:S(2)}, u32[]{:S(2)}) collective-permute-start(bf16[768,1280]{1,0:T(8,128)(2,1)} %cut.3), channel_id=1, source_target_pairs={{0,2},{2,0},{1,3},{3,1},{4,6},{6,4},{5,7},{7,5},{8,10},{10,8},{9,1... | collective-permute-start | bytes 5898248 | tf_op jit(solution)/shard_map/ppermute | solution.py:24
  196.7 23.6 %collective-permute-start.4 = (bf16[4,80,1280]{2,1,0:T(8,128)(2,1)}, bf16[4,80,1280]{2,1,0:T(8,128)(2,1)S(1)}, u32[]{:S(2)}, u32[]{:S(2)}) collective-permute-start(bf16[4,80,1280]{2,1,0:T(8,128)(2,1)} %get-tuple-element.27.after), channel_id=1, source_target_pairs={{0,34},{2,8},{10,40},{8,18},{16,50},{18,24},{26,56},{24,2},{34,64}... | collective-permute-start | bytes 2457608 | tf_op jit(solution)/shard_map/ppermute | solution.py:36
  198.1 22.2 %collective-permute-start.5 = (bf16[4,80,1280]{2,1,0:T(8,128)(2,1)}, bf16[4,80,1280]{2,1,0:T(8,128)(2,1)}, u32[]{:S(2)}, u32[]{:S(2)}) collective-permute-start(bf16[4,80,1280]{2,1,0:T(8,128)(2,1)} %get-tuple-element.32), channel_id=1, source_target_pairs={{0,64},{2,18},{10,74},{8,24},{16,80},{18,2},{26,90},{24,8},{34,98}... | collective-permute-start | bytes 2457608 | tf_op jit(solution)/shard_map/ppermute | solution.py:36
  200.7 19.6 %collective-permute-start.6 = (bf16[4,80,1280]{2,1,0:T(8,128)(2,1)}, bf16[4,80,1280]{2,1,0:T(8,128)(2,1)}, u32[]{:S(2)}, u32[]{:S(2)}) collective-permute-start(bf16[4,80,1280]{2,1,0:T(8,128)(2,1)} %get-tuple-element.33), channel_id=1, source_target_pairs={{0,98},{2,24},{10,104},{8,2},{16,114},{18,8},{26,120},{24,18},{34,... | collective-permute-start | bytes 2457608 | tf_op jit(solution)/shard_map/ppermute | solution.py:36
  217.3 22.0 %collective-permute-start.3 = (bf16[2,160,1280]{2,1,0:T(8,128)(2,1)}, bf16[2,160,1280]{2,1,0:T(8,128)(2,1)S(1)}, u32[]{:S(2)}, u32[]{:S(2)}) collective-permute-start(bf16[2,160,1280]{2,1,0:T(8,128)(2,1)} %get-tuple-element.30), channel_id=1, source_target_pairs={{0,34},{2,8},{10,40},{8,18},{16,50},{18,24},{26,56},{24,2},{34,64}... | collective-permute-start | bytes 2457608 | tf_op jit(solution)/shard_map/ppermute | solution.py:36
  217.4 26.6 %collective-permute-start.11 = (bf16[2,160,1280]{2,1,0:T(8,128)(2,1)}, bf16[2,160,1280]{2,1,0:T(8,128)(2,1)S(1)}, u32[]{:S(2)}, u32[]{:S(2)}) collective-permute-start(bf16[2,160,1280]{2,1,0:T(8,128)(2,1)} %get-tuple-element.38), channel_id=1, source_target_pairs={{0,98},{2,24},{10,104},{8,2},{16,114},{18,8},{26,120},{24,18},{34,... | collective-permute-start | bytes 2457608 | tf_op jit(solution)/shard_map/ppermute | solution.py:36
  223.9 8.9 %collective-permute-start.7 = (bf16[80,1280]{1,0:T(8,128)(2,1)}, bf16[80,1280]{1,0:T(8,128)(2,1)S(1)}, u32[]{:S(2)}, u32[]{:S(2)}) collective-permute-start(bf16[80,1280]{1,0:T(8,128)(2,1)} %get-tuple-element.34), channel_id=1, source_target_pairs={{0,10},{2,32},{10,16},{8,42},{16,26},{18,48},{26,0},{24,58},{34,40... | collective-permute-start | bytes 614408 | tf_op jit(solution)/shard_map/ppermute | solution.py:36
  226.0 9.0 %collective-permute-start.8 = (bf16[80,1280]{1,0:T(8,128)(2,1)}, bf16[80,1280]{1,0:T(8,128)(2,1)S(1)}, u32[]{:S(2)}, u32[]{:S(2)}) collective-permute-start(bf16[80,1280]{1,0:T(8,128)(2,1)} %get-tuple-element.35), channel_id=1, source_target_pairs={{0,16},{2,66},{10,26},{8,72},{16,0},{18,82},{26,10},{24,88},{34,50... | collective-permute-start | bytes 614408 | tf_op jit(solution)/shard_map/ppermute | solution.py:36
  229.3 5.9 %collective-permute-start.9 = (bf16[80,1280]{1,0:T(8,128)(2,1)}, bf16[80,1280]{1,0:T(8,128)(2,1)S(1)}, u32[]{:S(2)}, u32[]{:S(2)}) collective-permute-start(bf16[80,1280]{1,0:T(8,128)(2,1)} %get-tuple-element.36), channel_id=1, source_target_pairs={{0,26},{2,96},{10,0},{8,106},{16,10},{18,112},{26,16},{24,122},{34... | collective-permute-start | bytes 614408 | tf_op jit(solution)/shard_map/ppermute | solution.py:36
  235.3 12.1 %collective-permute-start.13 = (f32[40,1280]{1,0:T(8,128)S(1)}, f32[40,1280]{1,0:T(8,128)S(1)}, u32[]{:S(2)}, u32[]{:S(2)}) collective-permute-start(f32[40,1280]{1,0:T(8,128)S(1)} %get-tuple-element.41), channel_id=1, source_target_pairs={{0,4},{4,0},{1,5},{5,1},{2,6},{6,2},{3,7},{7,3},{8,12},{12,8},{9,1... | collective-permute-start | bytes 614408 | tf_op jit(solution)/shard_map/ppermute | solution.py:24
  236.6 11.7 %collective-permute-start.14 = (f32[40,1280]{1,0:T(8,128)S(1)}, f32[40,1280]{1,0:T(8,128)S(1)}, u32[]{:S(2)}, u32[]{:S(2)}) collective-permute-start(f32[40,1280]{1,0:T(8,128)S(1)} %get-tuple-element.40.mine), channel_id=1, source_target_pairs={{0,1},{1,0},{2,3},{3,2},{4,5},{5,4},{6,7},{7,6},{8,9},{9,8},{10,11... | collective-permute-start | bytes 614408 | tf_op jit(solution)/shard_map/ppermute | solution.py:24
  239.1 11.5 %collective-permute-start.15 = (f32[40,1280]{1,0:T(8,128)S(1)}, f32[40,1280]{1,0:T(8,128)S(1)}, u32[]{:S(2)}, u32[]{:S(2)}) collective-permute-start(f32[40,1280]{1,0:T(8,128)S(1)} %get-tuple-element.41), channel_id=1, source_target_pairs={{0,5},{1,4},{4,1},{5,0},{2,7},{3,6},{6,3},{7,2},{8,13},{9,12},{12,... | collective-permute-start | bytes 614408 | tf_op jit(solution)/shard_map/ppermute | solution.py:546
  241.3 22.9 %collective-permute-start.10 = (bf16[4,160,1280]{2,1,0:T(8,128)(2,1)}, bf16[4,160,1280]{2,1,0:T(8,128)(2,1)S(1)}, u32[]{:S(2)}, u32[]{:S(2)}) collective-permute-start(bf16[4,160,1280]{2,1,0:T(8,128)(2,1)} %grow.2), channel_id=1, source_target_pairs={{0,34},{2,8},{10,40},{8,18},{16,50},{18,24},{26,56},{24,2},{34,64}... | collective-permute-start | bytes 4915208 | tf_op jit(solution)/shard_map/ppermute | solution.py:36
  246.1 25.6 %collective-permute-start.12 = (bf16[4,160,1280]{2,1,0:T(8,128)(2,1)}, bf16[4,160,1280]{2,1,0:T(8,128)(2,1)}, u32[]{:S(2)}, u32[]{:S(2)}) collective-permute-start(bf16[4,160,1280]{2,1,0:T(8,128)(2,1)} %grow.3), channel_id=1, source_target_pairs={{0,98},{2,24},{10,104},{8,2},{16,114},{18,8},{26,120},{24,18},{34,... | collective-permute-start | bytes 4915208 | tf_op jit(solution)/shard_map/ppermute | solution.py:36
  255.7 27.5 %all-to-all-start = ((f32[128,16,128]{2,1,0:T(8,128)}), f32[128,16,128]{2,1,0:T(8,128)S(1)}, u32[]{:S(2)}, u32[]{:S(2)}) async-start(f32[128,16,128]{2,1,0:T(8,128)} %left_product.1.refs_3_), calls=%async_computation | async-start | bytes 2097152 | tf_op jit(solution)/shard_map/all_to_all | solution.py:550
  275.9 12.1 %collective-permute-start.16 = (bf16[160,1280]{1,0:T(8,128)(2,1)}, bf16[160,1280]{1,0:T(8,128)(2,1)S(1)}, u32[]{:S(2)}, u32[]{:S(2)}) collective-permute-start(bf16[160,1280]{1,0:T(8,128)(2,1)} %get-tuple-element.43.late), channel_id=1, source_target_pairs={{0,10},{2,32},{10,16},{8,42},{16,26},{18,48},{26,0},{24,58},{34,40... | collective-permute-start | bytes 1228808 | tf_op jit(solution)/shard_map/ppermute | solution.py:36
  279.5 13.6 %collective-permute-start.17 = (bf16[160,1280]{1,0:T(8,128)(2,1)}, bf16[160,1280]{1,0:T(8,128)(2,1)S(1)}, u32[]{:S(2)}, u32[]{:S(2)}) collective-permute-start(bf16[160,1280]{1,0:T(8,128)(2,1)} %get-tuple-element.44), channel_id=1, source_target_pairs={{0,16},{2,66},{10,26},{8,72},{16,0},{18,82},{26,10},{24,88},{34,50... | collective-permute-start | bytes 1228808 | tf_op jit(solution)/shard_map/ppermute | solution.py:36
  282.9 10.3 %collective-permute-start.18 = (bf16[160,1280]{1,0:T(8,128)(2,1)}, bf16[160,1280]{1,0:T(8,128)(2,1)S(1)}, u32[]{:S(2)}, u32[]{:S(2)}) collective-permute-start(bf16[160,1280]{1,0:T(8,128)(2,1)} %get-tuple-element.45), channel_id=1, source_target_pairs={{0,26},{2,96},{10,0},{8,106},{16,10},{18,112},{26,16},{24,122},{34... | collective-permute-start | bytes 1228808 | tf_op jit(solution)/shard_map/ppermute | solution.py:36
  294.0 5.2 %collective-permute-start.19 = (bf16[80,1280]{1,0:T(8,128)(2,1)}, bf16[80,1280]{1,0:T(8,128)(2,1)S(1)}, u32[]{:S(2)}, u32[]{:S(2)}) collective-permute-start(bf16[80,1280]{1,0:T(8,128)(2,1)} %get-tuple-element.47), channel_id=1, source_target_pairs={{0,4},{4,0},{1,5},{5,1},{2,6},{6,2},{3,7},{7,3},{8,12},{12,8},{9,1... | collective-permute-start | bytes 614408 | tf_op jit(solution)/shard_map/ppermute | solution.py:24
  299.3 8.7 %collective-permute-start.20 = (f32[40,1280]{1,0:T(8,128)S(1)}, f32[40,1280]{1,0:T(8,128)S(1)}, u32[]{:S(2)}, u32[]{:S(2)}) collective-permute-start(f32[40,1280]{1,0:T(8,128)S(1)} %dynamic-slice_bitcast_fusion), channel_id=1, source_target_pairs={{0,2},{2,0},{1,3},{3,1},{4,6},{6,4},{5,7},{7,5},{8,10},{10,8},{9,1... | collective-permute-start | bytes 614408 | tf_op jit(solution)/shard_map/ppermute | solution.py:24

commit v10 on v9

--- a/solution.py
+++ b/solution.py
@@ -10,6 +10,7 @@
 BF = jnp.bfloat16
 F32 = jnp.float32
 TILE = 640
+NO_COST = pl.CostEstimate(flops=0, bytes_accessed=0, transcendentals=0)
 ANY = pl.BlockSpec(memory_space=pl.ANY)
 
 
@@ -66,20 +67,13 @@
                 @pl.when(((z - place[2] + 4) & 3) == r)
                 def _():
                     for k in range(4):
-                        if isinstance(out, tuple):
-                            start((a * 4 + k) * rows, out[k // 2], k % 2)
-                        else:
-                            start((a * 4 + k) * rows, out, k)
+                        start((a * 4 + k) * rows, out, k)
 
         @pl.when(place[1] == 1)
         def _():
             for r, out in enumerate(outs):
                 at = pl.multiple_of((a * 4 + ((place[3] + r) & 3)) * rows, 16)
-                if isinstance(out, tuple):
-                    pl.when(z < 2)(functools.partial(start, at, out[0], z & 1))
-                    pl.when(z >= 2)(functools.partial(start, at, out[1], z & 1))
-                else:
-                    start(at, out, z)
+                start(at, out, z)
 
 
 def wait_all(buffer, sem):
@@ -137,15 +131,13 @@
             ],
         ),
         compiler_params=pltpu.CompilerParams(vmem_limit_bytes=28 * 2**20),
-        cost_estimate=pl.CostEstimate(
-            flops=2 * tokens * half * half, bytes_accessed=8 * tokens * half, transcendentals=0
-        ),
+        cost_estimate=NO_COST,
         name="cross_own",
     )(place, grads, acts)
 
 
 def cross_term(place, grads_next, acts_next, partial):
-    tokens, half = grads_next.shape
+    tokens, half = grads_next.shape[0], grads_next.shape[1] // 2
     out = pltpu.HBM((4, half // 16, half), BF)
     return pl.pallas_call(
         cross_kernel,
@@ -154,8 +146,8 @@
             num_scalar_prefetch=1,
             grid=(2,),
             in_specs=[
-                pl.BlockSpec((tokens, TILE), lambda m, p: (0, m)),
-                pl.BlockSpec((tokens, half), lambda m, p: (0, 0)),
+                pl.BlockSpec((tokens, TILE), lambda m, p: (0, p[1] * 2 + m)),
+                pl.BlockSpec((tokens, half), lambda m, p: (0, p[1] ^ p[0])),
                 ANY,
             ],
             out_specs=[pl.BlockSpec(memory_space=pltpu.HBM)] * 4,
@@ -167,40 +159,29 @@
             ],
         ),
         compiler_params=pltpu.CompilerParams(vmem_limit_bytes=28 * 2**20),
-        cost_estimate=pl.CostEstimate(
-            flops=2 * tokens * half * half, bytes_accessed=10 * tokens * half, transcendentals=0
-        ),
+        cost_estimate=NO_COST,
         name="cross_term",
     )(place, grads_next, acts_next, partial)
 
 
-def factor_kernel(place, h_own, g_own, h_next, g_next, x_next, after, *rest):
+def factor_kernel(place, h_own, g_own, h_next, g_next, after, *rest):
     del after
-    own, right, far_a, far_b, left, lhs, rhs, buffer, lhs_sems, rhs_sem, sem = rest
+    outs, (lhs, rhs, buffer, lhs_sems, rhs_sem, sem) = rest[:4], rest[4:]
     m = pl.program_id(0)
     half = rhs.shape[2]
 
-    def lanes(step, wide):
-        return pl.ds(pl.multiple_of(step * wide, wide), wide)
-
     def fetch(step, with_rhs):
         slot = step & 1
-
-        def left_block(ref, k, at):
-            pltpu.make_async_copy(ref.at[:, lanes(at, TILE)], lhs.at[slot, k], lhs_sems.at[slot]).start()
-
-        for owner, (mine, theirs) in enumerate(((h_own, h_next), (g_own, g_next))):
+        at = pl.ds(pl.multiple_of(step * TILE, TILE), TILE)
+        right = pl.ds(pl.multiple_of(place[1] * half, half), half)
+        for owner, refs in enumerate(((h_own, h_next), (g_own, g_next))):
 
             @pl.when(place[0] == owner)
             def _():
-                left_block(mine, 0, step)
-                pl.when((step >> 1) == place[1])(lambda: left_block(theirs, 1, step & 1))
-                if with_rhs:
-                    at = lanes(place[1], half)
-                    pltpu.make_async_copy(mine.at[:, at], rhs.at[0], rhs_sem).start()
-                    pltpu.make_async_copy(theirs, rhs.at[1], rhs_sem).start()
-
-        pl.when((step >> 1) != place[1])(lambda: left_block(x_next, 1, step & 1))
+                for k, ref in enumerate(refs):
+                    pltpu.make_async_copy(ref.at[:, at], lhs.at[slot, k], lhs_sems.at[slot]).start()
+                    if with_rhs:
+                        pltpu.make_async_copy(ref.at[:, right], rhs.at[k], rhs_sem).start()
 
     pl.when(m == 0)(lambda: fetch(0, True))
     pl.when(m < 3)(lambda: fetch(m + 1, False))
@@ -209,24 +190,23 @@
     pl.when(m == 0)(lambda: wait_all(rhs, rhs_sem))
 
     buffer[m] = (contract(lhs[slot, 0], rhs[0]) + contract(lhs[slot, 1], rhs[1])).astype(BF)
-    place_tile(place, buffer, sem, [own, right, (far_a, far_b), left], m, 1)
+    place_tile(place, buffer, sem, outs, m, 1)
     pl.when(m == 3)(lambda: wait_all(buffer, sem))
 
 
-def factor_term(place, acts, grads, acts_next, grads_next, rest_next, after):
+def factor_term(place, acts, grads, acts_next, grads_next, after):
     tokens, width = acts.shape
     half = width // 2
     hbm = pl.BlockSpec(memory_space=pltpu.HBM)
     out = pltpu.HBM((4, width // 16, half), BF)
-    side = pltpu.HBM((2, width // 16, half), BF)
     return pl.pallas_call(
         factor_kernel,
-        out_shape=[out, out, side, side, out],
+        out_shape=[out] * 4,
         grid_spec=pltpu.PrefetchScalarGridSpec(
             num_scalar_prefetch=1,
             grid=(4,),
-            in_specs=[hbm] * 2 + [ANY] * 4,
-            out_specs=[hbm] * 5,
+            in_specs=[hbm] * 2 + [ANY] * 3,
+            out_specs=[hbm] * 4,
             scratch_shapes=[
                 pltpu.VMEM((2, 2, tokens, TILE), BF),
                 pltpu.VMEM((2, tokens, half), BF),
@@ -237,11 +217,9 @@
             ],
         ),
         compiler_params=pltpu.CompilerParams(vmem_limit_bytes=30 * 2**20),
-        cost_estimate=pl.CostEstimate(
-            flops=4 * tokens * width * half, bytes_accessed=16 * tokens * half, transcendentals=0
-        ),
+        cost_estimate=NO_COST,
         name="factor_term",
-    )(place, acts, grads, acts_next, grads_next, rest_next, after)
+    )(place, acts, grads, acts_next, grads_next, after)
 
 
 def add(first, *rest):
@@ -278,8 +256,8 @@
             out_specs=[whole] * 4,
             scratch_shapes=[pltpu.VMEM((4, rows, width), BF), pltpu.SemaphoreType.DMA],
         ),
-        compiler_params=pltpu.CompilerParams(vmem_limit_bytes=20 * 2**20),
-        cost_estimate=pl.CostEstimate(flops=0, bytes_accessed=0, transcendentals=0),
+        compiler_params=pltpu.CompilerParams(vmem_limit_bytes=26 * 2**20),
+        cost_estimate=NO_COST,
         name="fold",
     )(me, in_hbm(parts[0]), *parts[1:], *after)
 
@@ -307,82 +285,9 @@
             out_specs=[part] * 2,
         ),
         compiler_params=pltpu.CompilerParams(vmem_limit_bytes=10 * 2**20),
-        cost_estimate=pl.CostEstimate(flops=0, bytes_accessed=0, transcendentals=0),
+        cost_estimate=NO_COST,
         name="settle",
     )(xl, total, *received, *after)
-
-
-def cut_kernel(pairs, indices, place, *refs):
-    sources, outs, sem = refs[: 2 * pairs], refs[-1 - pairs : -1], refs[-1]
-    tokens, width = outs[0].shape
-    rows = tokens // 4
-    for i in range(pairs):
-        at = pl.ds(pl.multiple_of(indices[i](place) * width, width), width)
-        for owner in range(2):
-
-            @pl.when(place[0] == owner)
-            def _():
-                for k in range(4):
-                    part = pl.ds(k * rows, rows)
-                    source = sources[2 * i + owner].at[part, at]
-                    pltpu.make_async_copy(source, outs[i].at[part], sem).start()
-
-    for out in outs:
-        wait_all(out, sem)
-
-
-def cut(place, sources, indices, *after):
-    tokens, width = sources[0][0].shape
-    pairs = len(sources)
-    hbm = pl.BlockSpec(memory_space=pltpu.HBM)
-    dtype = sources[0][0].dtype
-    return pl.pallas_call(
-        functools.partial(cut_kernel, pairs, indices),
-        out_shape=[pltpu.HBM((tokens, width // 2), dtype)] * pairs,
-        grid_spec=pltpu.PrefetchScalarGridSpec(
-            num_scalar_prefetch=1,
-            grid=(1,),
-            in_specs=[hbm] * (2 * pairs) + [ANY] * len(after),
-            out_specs=[hbm] * pairs,
-            scratch_shapes=[pltpu.SemaphoreType.DMA],
-        ),
-        compiler_params=pltpu.CompilerParams(vmem_limit_bytes=8 * 2**20),
-        cost_estimate=pl.CostEstimate(
-            flops=0, bytes_accessed=2 * pairs * tokens * width, transcendentals=0
-        ),
-        name="cut",
-    )(place, *[x for pair in sources for x in pair], *after)
-
-
-def grow_kernel(side, x, received, *refs):
-    out, held, sems, out_sem = refs[-4:]
-    for k in range(2):
-        pltpu.make_async_copy(x.at[side * 2 + k], held.at[k], sems.at[k]).start()
-    for k in range(2):
-        wait_all(held.at[k], sems.at[k])
-        held[k] = add(held[k], received[k]).astype(BF)
-        pltpu.make_async_copy(held.at[k], out.at[side * 2 + k], out_sem).start()
-    wait_all(held, out_sem)
-
-
-def grow(x, received, side, *after):
-    hbm = pl.BlockSpec(memory_space=pltpu.HBM)
-    return pl.pallas_call(
-        functools.partial(grow_kernel, side),
-        out_shape=pltpu.HBM(x.shape, x.dtype),
-        grid=(1,),
-        in_specs=[hbm, pl.BlockSpec(received.shape, lambda s: (0, 0, 0))] + [ANY] * len(after),
-        out_specs=hbm,
-        scratch_shapes=[
-            pltpu.VMEM(received.shape, x.dtype),
-            pltpu.SemaphoreType.DMA((2,)),
-            pltpu.SemaphoreType.DMA,
-        ],
-        input_output_aliases={0: 0},
-        compiler_params=pltpu.CompilerParams(vmem_limit_bytes=8 * 2**20),
-        cost_estimate=pl.CostEstimate(flops=0, bytes_accessed=0, transcendentals=0),
-        name="grow",
-    )(in_hbm(x), received, *after)
 
 
 def fetch_tiles(step, source, held, sems):
@@ -445,9 +350,7 @@
             ],
         ),
         compiler_params=pltpu.CompilerParams(vmem_limit_bytes=20 * 2**20),
-        cost_estimate=pl.CostEstimate(
-            flops=256 * rows * half * half, bytes_accessed=4 * half * half, transcendentals=0
-        ),
+        cost_estimate=NO_COST,
         name="left_product",
     )(place, mine, other, partner, partner_other, left)
 
@@ -494,9 +397,7 @@
             ],
         ),
         compiler_params=pltpu.CompilerParams(vmem_limit_bytes=20 * 2**20),
-        cost_estimate=pl.CostEstimate(
-            flops=640 * rows * half * half, bytes_accessed=4 * half * half, transcendentals=0
-        ),
+        cost_estimate=NO_COST,
         name="right_product",
     )(place, blocks, right, late)
 
@@ -513,35 +414,22 @@
     place = jnp.stack([o, h, z, y]).astype(jnp.int32)
     second_me = jnp.where(h == 0, y, z).astype(jnp.int32)[None]
 
-    grads_cut, acts_cut = cut(
-        place,
-        [(out_grad, out_grad), (hidden, hidden)],
-        [lambda p: 1 - p[1], lambda p: (1 - p[1]) ^ p[0]],
-    )
-    grads_next, acts_next = shift(grads_cut, "c", 1), shift(acts_cut, "c", 1)
+    grads_next, acts_next = in_hbm(shift(out_grad, "c", 1)), in_hbm(shift(hidden, "c", 1))
     partial = cross_own(place, out_grad, hidden)
-    (rest_cut,) = cut(place, [(hidden, out_grad)], [lambda p: p[1]], partial)
-    rest_next = shift(rest_cut, "c", 1)
 
     own, m1, m2, m3 = cross_term(place, grads_next, acts_next, partial)
     m_parts = [own, turn(m1, 1, 0), turn(m2, 2, 0), turn(m3, 3, 0)]
 
-    f_own, right, far_a, far_b, left = factor_term(
-        place, hidden, out_grad, acts_next, grads_next, rest_next, in_hbm(m1)
-    )
+    f_own, f1, f2, f3 = factor_term(place, hidden, out_grad, acts_next, grads_next, in_hbm(m1))
+    f_parts = [f_own, turn(f1, 1, 0), turn(f2, 2, 0), turn(f3, 3, 0)]
 
     my_xl = xl.astype(jnp.int32)[None]
 
     def second_sends(pieces):
         return [turn(piece, s, 1) for s, piece in enumerate(pieces, 1)]
 
-    from_left, from_right = turn(far_a, 1, 0), turn(far_b, -1, 0)
     m, *m_pieces = fold(second_me, m_parts, in_hbm(f_own))
     m_received = second_sends(m_pieces)
-    right = grow(right, from_left, 0, *m_received)
-    left = grow(left, from_right, 1, *m_received)
-    f_parts = [f_own, turn(right, 1, 0), turn(left, -1, 0)]
-
     mine, theirs = settle(my_xl, m, m_received, F32)
     across = lax.ppermute(theirs, ("xl", "o"), [(i, 3 - i) for i in range(4)])
     products = left_product(

time: 311 us -> 147 us (0.47)
  Pallas kernels: 233 us -> 48.8 us
  waiting for transfers between devices: 31.4 us -> 52.4 us
  local copies, waits for them, and re-layouts: 0.02 us -> 3.52 us
    pallas_call x5 -> x1, Pallas kernels: 201 us -> 15.9 us  [factor_term(): pl.pallas_call(factor_kernel, out_shape=[out] * 4, grid_spec=pltpu.Prefet...]
    ppermute x7 -> x6, waiting for transfers between devices: 6.12 us -> 18.3 us  [shift(): return lax.ppermute(x, axis, [(i, (i + step) % size) for i in range(size)])]
    ppermute x13 -> x12, waiting for transfers between devices: 22.6 us -> 29.7 us  [turn(): return lax.ppermute(x, ('z', 'y', 'c'), pairs)]
    ppermute x13 -> x12, starting transfers between devices: 26.1 us -> 21.3 us  [turn(): return lax.ppermute(x, ('z', 'y', 'c'), pairs)]
    unnamed x0 -> x8, local copies, waits for them, and re-layouts: none -> 3.49 us
    ppermute x7 -> x6, starting transfers between devices: 8.43 us -> 6.21 us  [shift(): return lax.ppermute(x, axis, [(i, (i + step) % size) for i in range(size)])]
  transfers between devices with their start and end apart: 22 -> 20, of which waited for: 12 -> 11; matrix products, arithmetic and copies ran while one was open for 0% -> 0% of each run, Pallas kernels for 36% -> 27%
where the time goes in v10:
time: 147 us; the launch traced here: 146 us
  waiting for transfers between devices  52.4 us (36%)
  Pallas kernels  48.8 us (33%)
  starting transfers between devices  39.9 us (27%)
  local copies, waits for them, and re-layouts  3.52 us (2%)
    ppermute x12, waiting for transfers between devices, turn(): return lax.ppermute(x, ('z', 'y', 'c'), pairs)  29.7 us
    ppermute x12, starting transfers between devices, turn(): return lax.ppermute(x, ('z', 'y', 'c'), pairs)  21.3 us
    ppermute x6, waiting for transfers between devices, shift(): return lax.ppermute(x, axis, [(i, (i + step) % size) for i in range(size)])  18.3 us
    pallas_call x1, Pallas kernels, factor_term(): pl.pallas_call(factor_kernel, out_shape=[out] * 4, grid_spec=pltpu.Prefet...  15.9 us
    all_to_all x1, starting transfers between devices, per_device(): lax.all_to_all(products, ('o', 'c', 'z', 'y', 'xl'), 0, 0, tiled=True)  10.2 us
    pallas_call x1, Pallas kernels, cross_term(): pl.pallas_call(cross_kernel, out_shape=[out] * 4, grid_spec=pltpu.Prefetc...  8.03 us
    pallas_call x2, Pallas kernels, fold(): pl.pallas_call(functools.partial(fold_kernel, len(parts)), out_shape=[jax...  7.31 us
    ppermute x6, starting transfers between devices, shift(): return lax.ppermute(x, axis, [(i, (i + step) % size) for i in range(size)])  6.21 us
  transfers between devices with their start and end apart: 20, of which 11 were waited for; matrix products, arithmetic and copies ran while one was open for 0% of the time, Pallas kernels for 27%

profile of v10, /device:TPU:1, one launch (start us, length us, event | category | flops | bytes accessed | tf_op | source)
XLA Modules:
  0.0 146.5 jit_solution(5262856812272231557)
XLA Ops:
  0.6 1.5 %collective-permute-start = (bf16[768,2560]{1,0:T(8,128)(2,1)}, bf16[768,2560]{1,0:T(8,128)(2,1)}, u32[]{:S(2)}, u32[]{:S(2)}) collective-permute-start(bf16[768,2560]{1,0:T(8,128)(2,1)} %h_own.1), channel_id=1, source_target_pairs={{0,2},{2,0},{1,3},{3,1},{4,6},{6,4},{5,7},{7,5},{8,10},{10,8},{9,1... | collective-permute-start | bytes 11796488 | tf_op jit(solution)/shard_map/ppermute | solution.py:25
  2.1 0.1 collective-permute-start.1
  2.2 0.1 pad_add_fusion.place
  2.3 5.4 %cross_own.1.partial = f32[1280,1280]{1,0:T(8,128)S(1)} custom-call(s32[4]{0:T(128)S(1)} %pad_add_fusion.place, bf16[768,2560]{1,0:T(8,128)(2,1)} %g_own.1, bf16[768,2560]{1,0:T(8,128)(2,1)} %h_own.1), custom_call_target="tpu_custom_call" | custom-call | tf_op jit(solution)/shard_map/cross_own/pallas_call | solution.py:118
  7.7 1.1 collective-permute-done.b.h_next
  8.9 5.6 %collective-permute-done.1.a.g_next = bf16[768,2560]{1,0:T(8,128)(2,1)} collective-permute-done((bf16[768,2560]{1,0:T(8,128)(2,1)}, bf16[768,2560]{1,0:T(8,128)(2,1)}, u32[]{:S(2)}, u32[]{:S(2)}) %collective-permute-start.1) | collective-permute-done | bytes 3932192 | tf_op jit(solution)/shard_map/ppermute | solution.py:25
  14.5 8.0 %cross_term.1 = (bf16[4,80,1280]{2,1,0:T(8,128)(2,1)}, bf16[4,80,1280]{2,1,0:T(8,128)(2,1)}, bf16[4,80,1280]{2,1,0:T(8,128)(2,1)}, bf16[4,80,1280]{2,1,0:T(8,128)(2,1)}) custom-call(s32[4]{0:T(128)S(1)} %pad_add_fusion.place, bf16[768,2560]{1,0:T(8,128)(2,1)} %collective-permute-done.1.a.g_next, bf16[768,2560]{1,0:T(8,128)(2,1)} %collective-permute-done.b.h_next, ...), custom_call_target="tpu_custom_call" | custom-call | tf_op jit(solution)/shard_map/cross_term/pallas_call | solution.py:142
  22.5 1.7 %collective-permute-start.5 = (bf16[4,80,1280]{2,1,0:T(8,128)(2,1)}, bf16[4,80,1280]{2,1,0:T(8,128)(2,1)S(1)}, u32[]{:S(2)}, u32[]{:S(2)}) collective-permute-start(bf16[4,80,1280]{2,1,0:T(8,128)(2,1)} %get-tuple-element.22.after), channel_id=1, source_target_pairs={{0,34},{2,8},{10,40},{8,18},{16,50},{18,24},{26,56},{24,2},{34,64}... | collective-permute-start | bytes 2457608 | tf_op jit(solution)/shard_map/ppermute | solution.py:37
  24.2 2.6 %collective-permute-start.6 = (bf16[4,80,1280]{2,1,0:T(8,128)(2,1)}, bf16[4,80,1280]{2,1,0:T(8,128)(2,1)S(1)}, u32[]{:S(2)}, u32[]{:S(2)}) collective-permute-start(bf16[4,80,1280]{2,1,0:T(8,128)(2,1)} %get-tuple-element.28), channel_id=1, source_target_pairs={{0,64},{2,18},{10,74},{8,24},{16,80},{18,2},{26,90},{24,8},{34,98}... | collective-permute-start | bytes 2457608 | tf_op jit(solution)/shard_map/ppermute | solution.py:37
  26.9 1.4 collective-permute-start.7
  28.2 15.9 %factor_term.1 = (bf16[4,160,1280]{2,1,0:T(8,128)(2,1)}, bf16[4,160,1280]{2,1,0:T(8,128)(2,1)}, bf16[4,160,1280]{2,1,0:T(8,128)(2,1)}, bf16[4,160,1280]{2,1,0:T(8,128)(2,1)}) custom-call(s32[4]{0:T(128)S(1)} %pad_add_fusion.place, bf16[768,2560]{1,0:T(8,128)(2,1)} %h_own.1, bf16[768,2560]{1,0:T(8,128)(2,1)} %g_own.1, ...), custom_call_target="tpu_custom_call" | custom-call | tf_op jit(solution)/shard_map/factor_term/pallas_call | solution.py:202
  44.1 0.5 collective-permute-start.2
  44.6 0.8 collective-permute-start.3
  45.4 2.0 %collective-permute-start.4 = (bf16[4,160,1280]{2,1,0:T(8,128)(2,1)}, bf16[4,160,1280]{2,1,0:T(8,128)(2,1)}, u32[]{:S(2)}, u32[]{:S(2)}) collective-permute-start(bf16[4,160,1280]{2,1,0:T(8,128)(2,1)} %get-tuple-element.26), channel_id=1, source_target_pairs={{0,98},{2,24},{10,104},{8,2},{16,114},{18,8},{26,120},{24,18},{34,... | collective-permute-start | bytes 4915208 | tf_op jit(solution)/shard_map/ppermute | solution.py:37
  47.3 3.2 %fold.2 = (f32[80,1280]{1,0:T(8,128)S(1)}, bf16[80,1280]{1,0:T(8,128)(2,1)S(1)}, bf16[80,1280]{1,0:T(8,128)(2,1)}, bf16[80,1280]{1,0:T(8,128)(2,1)S(1)}) custom-call(s32[1]{0:T(128)} %bitcast.1.me, bf16[4,80,1280]{2,1,0:T(8,128)(2,1)} %get-tuple-element.27.refs_0_, bf16[4,80,1280]{2,1,0:T(8,128)(2,1)S(1)} %collective-permute-done.5.refs_1_, ...), custom_call_target="tpu_custom_call" | custom-call | tf_op jit(solution)/shard_map/fold/pallas_call | solution.py:247
  50.5 0.0 copy-start
  50.5 0.7 copy-done
  51.3 1.7 %collective-permute-start.8 = (bf16[80,1280]{1,0:T(8,128)(2,1)S(1)}, bf16[80,1280]{1,0:T(8,128)(2,1)S(1)}, u32[]{:S(2)}, u32[]{:S(2)}) collective-permute-start(bf16[80,1280]{1,0:T(8,128)(2,1)S(1)} %get-tuple-element.31), channel_id=1, source_target_pairs={{0,10},{2,32},{10,16},{8,42},{16,26},{18,48},{26,0},{24,58},{34,40... | collective-permute-start | bytes 614408 | tf_op jit(solution)/shard_map/ppermute | solution.py:37
  52.9 3.3 %collective-permute-start.9 = (bf16[80,1280]{1,0:T(8,128)(2,1)}, bf16[80,1280]{1,0:T(8,128)(2,1)S(1)}, u32[]{:S(2)}, u32[]{:S(2)}) collective-permute-start(bf16[80,1280]{1,0:T(8,128)(2,1)} %get-tuple-element.32), channel_id=1, source_target_pairs={{0,16},{2,66},{10,26},{8,72},{16,0},{18,82},{26,10},{24,88},{34,50... | collective-permute-start | bytes 614408 | tf_op jit(solution)/shard_map/ppermute | solution.py:37
  56.2 4.8 %collective-permute-done.8.r1 = bf16[80,1280]{1,0:T(8,128)(2,1)S(1)} collective-permute-done((bf16[80,1280]{1,0:T(8,128)(2,1)S(1)}, bf16[80,1280]{1,0:T(8,128)(2,1)S(1)}, u32[]{:S(2)}, u32[]{:S(2)}) %collective-permute-start.8) | collective-permute-done | bytes 204832 | tf_op jit(solution)/shard_map/ppermute | solution.py:37
  61.0 1.4 collective-permute-start.10
  62.5 3.8 %collective-permute-done.9.r2 = bf16[80,1280]{1,0:T(8,128)(2,1)S(1)} collective-permute-done((bf16[80,1280]{1,0:T(8,128)(2,1)}, bf16[80,1280]{1,0:T(8,128)(2,1)S(1)}, u32[]{:S(2)}, u32[]{:S(2)}) %collective-permute-start.9) | collective-permute-done | bytes 204832 | tf_op jit(solution)/shard_map/ppermute | solution.py:37
  66.3 6.6 %collective-permute-done.10.r3 = bf16[80,1280]{1,0:T(8,128)(2,1)S(1)} collective-permute-done((bf16[80,1280]{1,0:T(8,128)(2,1)S(1)}, bf16[80,1280]{1,0:T(8,128)(2,1)S(1)}, u32[]{:S(2)}, u32[]{:S(2)}) %collective-permute-start.10) | collective-permute-done | bytes 204832 | tf_op jit(solution)/shard_map/ppermute | solution.py:37
  72.9 1.0 copy-done.1
  73.9 0.1 settle.2
  74.0 1.3 collective-permute-start.11
  75.3 2.3 %collective-permute-start.12 = (f32[40,1280]{1,0:T(8,128)S(1)}, f32[40,1280]{1,0:T(8,128)S(1)}, u32[]{:S(2)}, u32[]{:S(2)}) collective-permute-start(f32[40,1280]{1,0:T(8,128)S(1)} %get-tuple-element.34.mine), channel_id=1, source_target_pairs={{0,1},{1,0},{2,3},{3,2},{4,5},{5,4},{6,7},{7,6},{8,9},{9,8},{10,11... | collective-permute-start | bytes 614408 | tf_op jit(solution)/shard_map/ppermute | solution.py:25
  77.6 2.1 %collective-permute-done.11.other = f32[40,1280]{1,0:T(8,128)S(1)} collective-permute-done((f32[40,1280]{1,0:T(8,128)S(1)}, f32[40,1280]{1,0:T(8,128)S(1)}, u32[]{:S(2)}, u32[]{:S(2)}) %collective-permute-start.11) | collective-permute-done | bytes 204832 | tf_op jit(solution)/shard_map/ppermute | solution.py:25
  79.8 2.2 %collective-permute-start.13 = (f32[40,1280]{1,0:T(8,128)S(1)}, f32[40,1280]{1,0:T(8,128)S(1)}, u32[]{:S(2)}, u32[]{:S(2)}) collective-permute-start(f32[40,1280]{1,0:T(8,128)S(1)} %get-tuple-element.35), channel_id=1, source_target_pairs={{0,5},{1,4},{4,1},{5,0},{2,7},{3,6},{6,3},{7,2},{8,13},{9,12},{12,... | collective-permute-start | bytes 614408 | tf_op jit(solution)/shard_map/ppermute | solution.py:434
  82.0 4.2 %collective-permute-done.12.partner = f32[40,1280]{1,0:T(8,128)S(1)} collective-permute-done((f32[40,1280]{1,0:T(8,128)S(1)}, f32[40,1280]{1,0:T(8,128)S(1)}, u32[]{:S(2)}, u32[]{:S(2)}) %collective-permute-start.12) | collective-permute-done | bytes 204832 | tf_op jit(solution)/shard_map/ppermute | solution.py:25
  86.1 4.5 %collective-permute-done.13.partner_other = f32[40,1280]{1,0:T(8,128)S(1)} collective-permute-done((f32[40,1280]{1,0:T(8,128)S(1)}, f32[40,1280]{1,0:T(8,128)S(1)}, u32[]{:S(2)}, u32[]{:S(2)}) %collective-permute-start.13) | collective-permute-done | bytes 204832 | tf_op jit(solution)/shard_map/ppermute | solution.py:434
  90.6 5.2 %left_product.1.refs_4_ = f32[128,16,128]{2,1,0:T(8,128)} custom-call(s32[4]{0:T(128)S(1)} %pad_add_fusion.place, f32[40,1280]{1,0:T(8,128)S(1)} %get-tuple-element.34.mine, f32[40,1280]{1,0:T(8,128)S(1)} %collective-permute-done.11.other, f32[40,1280]{1,0:T(8,128)S(1)} %collective-permute-done.12.partner, ...), custom_call_target="tpu_custom_call" | custom-call | tf_op jit(solution)/shard_map/left_product/pallas_call | solution.py:338
  95.8 10.2 %all-to-all-start = ((f32[128,16,128]{2,1,0:T(8,128)}), f32[128,16,128]{2,1,0:T(8,128)S(1)}, u32[]{:S(2)}, u32[]{:S(2)}) async-start(f32[128,16,128]{2,1,0:T(8,128)} %left_product.1.refs_4_), calls=%async_computation | async-start | bytes 2097152 | tf_op jit(solution)/shard_map/all_to_all | solution.py:438
  106.1 4.1 %fold.3 = (f32[160,1280]{1,0:T(8,128)S(1)}, bf16[160,1280]{1,0:T(8,128)(2,1)S(1)}, bf16[160,1280]{1,0:T(8,128)(2,1)S(1)}, bf16[160,1280]{1,0:T(8,128)(2,1)S(1)}) custom-call(s32[1]{0:T(128)} %bitcast.1.me, bf16[4,160,1280]{2,1,0:T(8,128)(2,1)} %get-tuple-element.23.refs_4_.refs_0_, bf16[4,160,1280]{2,1,0:T(8,128)(2,1)S(1)} %collective-permute-done.2.refs_1_, ...), custom_call_target="tpu_custom_call" | custom-call | tf_op jit(solution)/shard_map/fold/pallas_call | solution.py:247
  110.2 1.8 %collective-permute-start.14 = (bf16[160,1280]{1,0:T(8,128)(2,1)S(1)}, bf16[160,1280]{1,0:T(8,128)(2,1)S(1)}, u32[]{:S(2)}, u32[]{:S(2)}) collective-permute-start(bf16[160,1280]{1,0:T(8,128)(2,1)S(1)} %get-tuple-element.37.late), channel_id=1, source_target_pairs={{0,10},{2,32},{10,16},{8,42},{16,26},{18,48},{26,0},{24,58},{34,40... | collective-permute-start | bytes 1228808 | tf_op jit(solution)/shard_map/ppermute | solution.py:37
  112.0 0.7 copy-done.2
  112.8 2.9 %collective-permute-start.15 = (bf16[160,1280]{1,0:T(8,128)(2,1)S(1)}, bf16[160,1280]{1,0:T(8,128)(2,1)S(1)}, u32[]{:S(2)}, u32[]{:S(2)}) collective-permute-start(bf16[160,1280]{1,0:T(8,128)(2,1)S(1)} %get-tuple-element.38), channel_id=1, source_target_pairs={{0,16},{2,66},{10,26},{8,72},{16,0},{18,82},{26,10},{24,88},{34,50... | collective-permute-start | bytes 1228808 | tf_op jit(solution)/shard_map/ppermute | solution.py:37
  115.7 1.2 collective-permute-start.16
  117.0 10.3 %collective-permute-done.14.r1 = bf16[160,1280]{1,0:T(8,128)(2,1)S(1)} collective-permute-done((bf16[160,1280]{1,0:T(8,128)(2,1)S(1)}, bf16[160,1280]{1,0:T(8,128)(2,1)S(1)}, u32[]{:S(2)}, u32[]{:S(2)}) %collective-permute-start.14) | collective-permute-done | bytes 409632 | tf_op jit(solution)/shard_map/ppermute | solution.py:37
  127.2 4.1 %collective-permute-done.15.r2 = bf16[160,1280]{1,0:T(8,128)(2,1)S(1)} collective-permute-done((bf16[160,1280]{1,0:T(8,128)(2,1)S(1)}, bf16[160,1280]{1,0:T(8,128)(2,1)S(1)}, u32[]{:S(2)}, u32[]{:S(2)}) %collective-permute-start.15) | collective-permute-done | bytes 409632 | tf_op jit(solution)/shard_map/ppermute | solution.py:37
  131.4 0.8 settle.3
  132.2 0.9 collective-permute-start.17
  133.1 5.2 %collective-permute-done.17 = bf16[80,1280]{1,0:T(8,128)(2,1)S(1)} collective-permute-done((bf16[80,1280]{1,0:T(8,128)(2,1)}, bf16[80,1280]{1,0:T(8,128)(2,1)S(1)}, u32[]{:S(2)}, u32[]{:S(2)}) %collective-permute-start.17) | collective-permute-done | bytes 204832 | tf_op jit(solution)/shard_map/ppermute | solution.py:25
  138.4 0.1 collective-permute-start.18
  138.4 0.0 copy-start.3
  138.5 1.0 copy-done.3
  139.5 6.2 %right_product.1 = f32[40,1280]{1,0:T(8,128)} custom-call(s32[4]{0:T(128)S(1)} %pad_add_fusion.place, f32[128,16,128]{2,1,0:T(8,128)S(1)} %all-to-all-done.refs_0_.blocks, bf16[2560,1280]{1,0:T(8,128)(2,1)} %right.1, bf16[160,1280]{1,0:T(8,128)(2,1)S(1)} %copy-done.3), custom_call_target="tpu_custom_call" | custom-call | tf_op jit(solution)/shard_map/right_product/pallas_call | solution.py:381
  145.7 0.8 maximum_bitcast_fusion
  (14 shorter events, 0.1 us)
Async XLA Ops:
  0.6 8.3 %collective-permute-start = (bf16[768,2560]{1,0:T(8,128)(2,1)}, bf16[768,2560]{1,0:T(8,128)(2,1)}, u32[]{:S(2)}, u32[]{:S(2)}) collective-permute-start(bf16[768,2560]{1,0:T(8,128)(2,1)} %h_own.1), channel_id=1, source_target_pairs={{0,2},{2,0},{1,3},{3,1},{4,6},{6,4},{5,7},{7,5},{8,10},{10,8},{9,1... | collective-permute-start | bytes 11796488 | tf_op jit(solution)/shard_map/ppermute | solution.py:25
  2.1 12.4 %collective-permute-start.1 = (bf16[768,2560]{1,0:T(8,128)(2,1)}, bf16[768,2560]{1,0:T(8,128)(2,1)}, u32[]{:S(2)}, u32[]{:S(2)}) collective-permute-start(bf16[768,2560]{1,0:T(8,128)(2,1)} %g_own.1), channel_id=1, source_target_pairs={{0,2},{2,0},{1,3},{3,1},{4,6},{6,4},{5,7},{7,5},{8,10},{10,8},{9,1... | collective-permute-start | bytes 11796488 | tf_op jit(solution)/shard_map/ppermute | solution.py:25
  22.5 22.8 %collective-permute-start.5 = (bf16[4,80,1280]{2,1,0:T(8,128)(2,1)}, bf16[4,80,1280]{2,1,0:T(8,128)(2,1)S(1)}, u32[]{:S(2)}, u32[]{:S(2)}) collective-permute-start(bf16[4,80,1280]{2,1,0:T(8,128)(2,1)} %get-tuple-element.22.after), channel_id=1, source_target_pairs={{0,34},{2,8},{10,40},{8,18},{16,50},{18,24},{26,56},{24,2},{34,64}... | collective-permute-start | bytes 2457608 | tf_op jit(solution)/shard_map/ppermute | solution.py:37
  24.2 23.1 %collective-permute-start.6 = (bf16[4,80,1280]{2,1,0:T(8,128)(2,1)}, bf16[4,80,1280]{2,1,0:T(8,128)(2,1)S(1)}, u32[]{:S(2)}, u32[]{:S(2)}) collective-permute-start(bf16[4,80,1280]{2,1,0:T(8,128)(2,1)} %get-tuple-element.28), channel_id=1, source_target_pairs={{0,64},{2,18},{10,74},{8,24},{16,80},{18,2},{26,90},{24,8},{34,98}... | collective-permute-start | bytes 2457608 | tf_op jit(solution)/shard_map/ppermute | solution.py:37
  26.9 20.5 %collective-permute-start.7 = (bf16[4,80,1280]{2,1,0:T(8,128)(2,1)}, bf16[4,80,1280]{2,1,0:T(8,128)(2,1)}, u32[]{:S(2)}, u32[]{:S(2)}) collective-permute-start(bf16[4,80,1280]{2,1,0:T(8,128)(2,1)} %get-tuple-element.29), channel_id=1, source_target_pairs={{0,98},{2,24},{10,104},{8,2},{16,114},{18,8},{26,120},{24,18},{34,... | collective-permute-start | bytes 2457608 | tf_op jit(solution)/shard_map/ppermute | solution.py:37
  44.1 61.9 %collective-permute-start.2 = (bf16[4,160,1280]{2,1,0:T(8,128)(2,1)}, bf16[4,160,1280]{2,1,0:T(8,128)(2,1)S(1)}, u32[]{:S(2)}, u32[]{:S(2)}) collective-permute-start(bf16[4,160,1280]{2,1,0:T(8,128)(2,1)} %get-tuple-element.24), channel_id=1, source_target_pairs={{0,34},{2,8},{10,40},{8,18},{16,50},{18,24},{26,56},{24,2},{34,64}... | collective-permute-start | bytes 4915208 | tf_op jit(solution)/shard_map/ppermute | solution.py:37
  44.6 61.5 %collective-permute-start.3 = (bf16[4,160,1280]{2,1,0:T(8,128)(2,1)}, bf16[4,160,1280]{2,1,0:T(8,128)(2,1)}, u32[]{:S(2)}, u32[]{:S(2)}) collective-permute-start(bf16[4,160,1280]{2,1,0:T(8,128)(2,1)} %get-tuple-element.25), channel_id=1, source_target_pairs={{0,64},{2,18},{10,74},{8,24},{16,80},{18,2},{26,90},{24,8},{34,98}... | collective-permute-start | bytes 4915208 | tf_op jit(solution)/shard_map/ppermute | solution.py:37
  45.4 60.7 %collective-permute-start.4 = (bf16[4,160,1280]{2,1,0:T(8,128)(2,1)}, bf16[4,160,1280]{2,1,0:T(8,128)(2,1)}, u32[]{:S(2)}, u32[]{:S(2)}) collective-permute-start(bf16[4,160,1280]{2,1,0:T(8,128)(2,1)} %get-tuple-element.26), channel_id=1, source_target_pairs={{0,98},{2,24},{10,104},{8,2},{16,114},{18,8},{26,120},{24,18},{34,... | collective-permute-start | bytes 4915208 | tf_op jit(solution)/shard_map/ppermute | solution.py:37
  50.5 0.8 copy-start
  51.3 9.8 %collective-permute-start.8 = (bf16[80,1280]{1,0:T(8,128)(2,1)S(1)}, bf16[80,1280]{1,0:T(8,128)(2,1)S(1)}, u32[]{:S(2)}, u32[]{:S(2)}) collective-permute-start(bf16[80,1280]{1,0:T(8,128)(2,1)S(1)} %get-tuple-element.31), channel_id=1, source_target_pairs={{0,10},{2,32},{10,16},{8,42},{16,26},{18,48},{26,0},{24,58},{34,40... | collective-permute-start | bytes 614408 | tf_op jit(solution)/shard_map/ppermute | solution.py:37
  52.9 13.4 %collective-permute-start.9 = (bf16[80,1280]{1,0:T(8,128)(2,1)}, bf16[80,1280]{1,0:T(8,128)(2,1)S(1)}, u32[]{:S(2)}, u32[]{:S(2)}) collective-permute-start(bf16[80,1280]{1,0:T(8,128)(2,1)} %get-tuple-element.32), channel_id=1, source_target_pairs={{0,16},{2,66},{10,26},{8,72},{16,0},{18,82},{26,10},{24,88},{34,50... | collective-permute-start | bytes 614408 | tf_op jit(solution)/shard_map/ppermute | solution.py:37
  61.0 11.9 %collective-permute-start.10 = (bf16[80,1280]{1,0:T(8,128)(2,1)S(1)}, bf16[80,1280]{1,0:T(8,128)(2,1)S(1)}, u32[]{:S(2)}, u32[]{:S(2)}) collective-permute-start(bf16[80,1280]{1,0:T(8,128)(2,1)S(1)} %get-tuple-element.33), channel_id=1, source_target_pairs={{0,26},{2,96},{10,0},{8,106},{16,10},{18,112},{26,16},{24,122},{34... | collective-permute-start | bytes 614408 | tf_op jit(solution)/shard_map/ppermute | solution.py:37
  72.9 1.0 copy-start.1
  74.0 5.7 %collective-permute-start.11 = (f32[40,1280]{1,0:T(8,128)S(1)}, f32[40,1280]{1,0:T(8,128)S(1)}, u32[]{:S(2)}, u32[]{:S(2)}) collective-permute-start(f32[40,1280]{1,0:T(8,128)S(1)} %get-tuple-element.35), channel_id=1, source_target_pairs={{0,4},{4,0},{1,5},{5,1},{2,6},{6,2},{3,7},{7,3},{8,12},{12,8},{9,1... | collective-permute-start | bytes 614408 | tf_op jit(solution)/shard_map/ppermute | solution.py:25
  75.3 10.8 %collective-permute-start.12 = (f32[40,1280]{1,0:T(8,128)S(1)}, f32[40,1280]{1,0:T(8,128)S(1)}, u32[]{:S(2)}, u32[]{:S(2)}) collective-permute-start(f32[40,1280]{1,0:T(8,128)S(1)} %get-tuple-element.34.mine), channel_id=1, source_target_pairs={{0,1},{1,0},{2,3},{3,2},{4,5},{5,4},{6,7},{7,6},{8,9},{9,8},{10,11... | collective-permute-start | bytes 614408 | tf_op jit(solution)/shard_map/ppermute | solution.py:25
  79.8 10.8 %collective-permute-start.13 = (f32[40,1280]{1,0:T(8,128)S(1)}, f32[40,1280]{1,0:T(8,128)S(1)}, u32[]{:S(2)}, u32[]{:S(2)}) collective-permute-start(f32[40,1280]{1,0:T(8,128)S(1)} %get-tuple-element.35), channel_id=1, source_target_pairs={{0,5},{1,4},{4,1},{5,0},{2,7},{3,6},{6,3},{7,2},{8,13},{9,12},{12,... | collective-permute-start | bytes 614408 | tf_op jit(solution)/shard_map/ppermute | solution.py:434
  95.8 35.6 %all-to-all-start = ((f32[128,16,128]{2,1,0:T(8,128)}), f32[128,16,128]{2,1,0:T(8,128)S(1)}, u32[]{:S(2)}, u32[]{:S(2)}) async-start(f32[128,16,128]{2,1,0:T(8,128)} %left_product.1.refs_4_), calls=%async_computation | async-start | bytes 2097152 | tf_op jit(solution)/shard_map/all_to_all | solution.py:438
  110.2 17.0 %collective-permute-start.14 = (bf16[160,1280]{1,0:T(8,128)(2,1)S(1)}, bf16[160,1280]{1,0:T(8,128)(2,1)S(1)}, u32[]{:S(2)}, u32[]{:S(2)}) collective-permute-start(bf16[160,1280]{1,0:T(8,128)(2,1)S(1)} %get-tuple-element.37.late), channel_id=1, source_target_pairs={{0,10},{2,32},{10,16},{8,42},{16,26},{18,48},{26,0},{24,58},{34,40... | collective-permute-start | bytes 1228808 | tf_op jit(solution)/shard_map/ppermute | solution.py:37
  112.0 0.8 copy-start.2
  112.8 18.6 %collective-permute-start.15 = (bf16[160,1280]{1,0:T(8,128)(2,1)S(1)}, bf16[160,1280]{1,0:T(8,128)(2,1)S(1)}, u32[]{:S(2)}, u32[]{:S(2)}) collective-permute-start(bf16[160,1280]{1,0:T(8,128)(2,1)S(1)} %get-tuple-element.38), channel_id=1, source_target_pairs={{0,16},{2,66},{10,26},{8,72},{16,0},{18,82},{26,10},{24,88},{34,50... | collective-permute-start | bytes 1228808 | tf_op jit(solution)/shard_map/ppermute | solution.py:37
  115.7 15.6 %collective-permute-start.16 = (bf16[160,1280]{1,0:T(8,128)(2,1)S(1)}, bf16[160,1280]{1,0:T(8,128)(2,1)S(1)}, u32[]{:S(2)}, u32[]{:S(2)}) collective-permute-start(bf16[160,1280]{1,0:T(8,128)(2,1)S(1)} %get-tuple-element.39), channel_id=1, source_target_pairs={{0,26},{2,96},{10,0},{8,106},{16,10},{18,112},{26,16},{24,122},{34... | collective-permute-start | bytes 1228808 | tf_op jit(solution)/shard_map/ppermute | solution.py:37
  132.2 6.1 %collective-permute-start.17 = (bf16[80,1280]{1,0:T(8,128)(2,1)}, bf16[80,1280]{1,0:T(8,128)(2,1)S(1)}, u32[]{:S(2)}, u32[]{:S(2)}) collective-permute-start(bf16[80,1280]{1,0:T(8,128)(2,1)} %get-tuple-element.41), channel_id=1, source_target_pairs={{0,4},{4,0},{1,5},{5,1},{2,6},{6,2},{3,7},{7,3},{8,12},{12,8},{9,1... | collective-permute-start | bytes 614408 | tf_op jit(solution)/shard_map/ppermute | solution.py:25
  138.4 7.3 %collective-permute-start.18 = (f32[40,1280]{1,0:T(8,128)S(1)}, f32[40,1280]{1,0:T(8,128)S(1)}, u32[]{:S(2)}, u32[]{:S(2)}) collective-permute-start(f32[40,1280]{1,0:T(8,128)S(1)} %dynamic-slice_bitcast_fusion), channel_id=1, source_target_pairs={{0,2},{2,0},{1,3},{3,1},{4,6},{6,4},{5,7},{7,5},{8,10},{10,8},{9,1... | collective-permute-start | bytes 614408 | tf_op jit(solution)/shard_map/ppermute | solution.py:25
  138.4 1.0 copy-start.3

commit v11 on v10

--- a/solution.py
+++ b/solution.py
@@ -50,29 +50,33 @@
     return high, (x - high.astype(F32)).astype(BF)
 
 
-def place_tile(place, buffer, sem, outs, m, zs):
-    rows = TILE // (zs * 4)
+def place_tile(place, buffer, sem, outs, z):
+    rows = TILE // 4
 
     def start(at, out, slot):
-        block = buffer.at[m, pl.ds(at, rows)]
+        block = buffer.at[z, pl.ds(at, rows)]
         pltpu.make_async_copy(block, out.at[slot], sem).start()
 
-    for a in range(zs):
-        z = m * zs + a
-
-        @pl.when(place[1] == 0)
-        def _():
-            for r, out in enumerate(outs):
-
-                @pl.when(((z - place[2] + 4) & 3) == r)
-                def _():
-                    for k in range(4):
-                        start((a * 4 + k) * rows, out, k)
-
-        @pl.when(place[1] == 1)
-        def _():
-            for r, out in enumerate(outs):
-                at = pl.multiple_of((a * 4 + ((place[3] + r) & 3)) * rows, 16)
+    @pl.when(place[1] == 0)
+    def _():
+        for r, out in enumerate(outs):
+
+            @pl.when(((z - place[2] + 4) & 3) == r)
+            def _():
+                for k in range(4):
+                    if isinstance(out, tuple):
+                        start(k * rows, out[k // 2], k % 2)
+                    else:
+                        start(k * rows, out, k)
+
+    @pl.when(place[1] == 1)
+    def _():
+        for r, out in enumerate(outs):
+            at = pl.multiple_of(((place[3] + r) & 3) * rows, 16)
+            if isinstance(out, tuple):
+                pl.when(z < 2)(functools.partial(start, at, out[0], z & 1))
+                pl.when(z >= 2)(functools.partial(start, at, out[1], z & 1))
+            else:
                 start(at, out, z)
 
 
@@ -97,7 +101,7 @@
     out[...] = contract(lhs[m], rhs[...])
 
 
-def cross_kernel(place, a, b, partial, own, ahead1, ahead2, ahead3, held, buffer, held_sems, sem):
+def cross_kernel(place, a, b, partial, out, held, held_sems):
     m = pl.program_id(0)
 
     @pl.when(m == 0)
@@ -108,9 +112,7 @@
 
     tile = contract(a[...], b[...])
     wait_all(held.at[m], held_sems.at[m])
-    buffer[m] = (held[m] + tile).astype(BF)
-    place_tile(place, buffer, sem, [own, ahead1, ahead2, ahead3], m, 2)
-    pl.when(m == 1)(lambda: wait_all(buffer, sem))
+    out[...] = (held[m] + tile).astype(BF).reshape(out.shape)
 
 
 def cross_own(place, grads, acts):
@@ -138,10 +140,9 @@
 
 def cross_term(place, grads_next, acts_next, partial):
     tokens, half = grads_next.shape[0], grads_next.shape[1] // 2
-    out = pltpu.HBM((4, half // 16, half), BF)
     return pl.pallas_call(
         cross_kernel,
-        out_shape=[out] * 4,
+        out_shape=pltpu.HBM((16, half // 16, half), BF),
         grid_spec=pltpu.PrefetchScalarGridSpec(
             num_scalar_prefetch=1,
             grid=(2,),
@@ -150,13 +151,8 @@
                 pl.BlockSpec((tokens, half), lambda m, p: (0, p[1] ^ p[0])),
                 ANY,
             ],
-            out_specs=[pl.BlockSpec(memory_space=pltpu.HBM)] * 4,
-            scratch_shapes=[
-                pltpu.VMEM((2, TILE, half), F32),
-                pltpu.VMEM((2, TILE, half), BF),
-                pltpu.SemaphoreType.DMA((2,)),
-                pltpu.SemaphoreType.DMA,
-            ],
+            out_specs=pl.BlockSpec((8, half // 16, half), lambda m, p: (m, 0, 0)),
+            scratch_shapes=[pltpu.VMEM((2, TILE, half), F32), pltpu.SemaphoreType.DMA((2,))],
         ),
         compiler_params=pltpu.CompilerParams(vmem_limit_bytes=28 * 2**20),
         cost_estimate=NO_COST,
@@ -166,14 +162,14 @@
 
 def factor_kernel(place, h_own, g_own, h_next, g_next, after, *rest):
     del after
-    outs, (lhs, rhs, buffer, lhs_sems, rhs_sem, sem) = rest[:4], rest[4:]
+    own, right, far_a, far_b, left, lhs, rhs, buffer, lhs_sems, rhs_sem, sem = rest
     m = pl.program_id(0)
     half = rhs.shape[2]
 
     def fetch(step, with_rhs):
         slot = step & 1
         at = pl.ds(pl.multiple_of(step * TILE, TILE), TILE)
-        right = pl.ds(pl.multiple_of(place[1] * half, half), half)
+        columns = pl.ds(pl.multiple_of(place[1] * half, half), half)
         for owner, refs in enumerate(((h_own, h_next), (g_own, g_next))):
 
             @pl.when(place[0] == owner)
@@ -181,7 +177,7 @@
                 for k, ref in enumerate(refs):
                     pltpu.make_async_copy(ref.at[:, at], lhs.at[slot, k], lhs_sems.at[slot]).start()
                     if with_rhs:
-                        pltpu.make_async_copy(ref.at[:, right], rhs.at[k], rhs_sem).start()
+                        pltpu.make_async_copy(ref.at[:, columns], rhs.at[k], rhs_sem).start()
 
     pl.when(m == 0)(lambda: fetch(0, True))
     pl.when(m < 3)(lambda: fetch(m + 1, False))
@@ -190,7 +186,7 @@
     pl.when(m == 0)(lambda: wait_all(rhs, rhs_sem))
 
     buffer[m] = (contract(lhs[slot, 0], rhs[0]) + contract(lhs[slot, 1], rhs[1])).astype(BF)
-    place_tile(place, buffer, sem, outs, m, 1)
+    place_tile(place, buffer, sem, [own, right, (far_a, far_b), left], m)
     pl.when(m == 3)(lambda: wait_all(buffer, sem))
 
 
@@ -199,14 +195,15 @@
     half = width // 2
     hbm = pl.BlockSpec(memory_space=pltpu.HBM)
     out = pltpu.HBM((4, width // 16, half), BF)
+    side = pltpu.HBM((2, width // 16, half), BF)
     return pl.pallas_call(
         factor_kernel,
-        out_shape=[out] * 4,
+        out_shape=[out, out, side, side, out],
         grid_spec=pltpu.PrefetchScalarGridSpec(
             num_scalar_prefetch=1,
             grid=(4,),
             in_specs=[hbm] * 2 + [ANY] * 3,
-            out_specs=[hbm] * 4,
+            out_specs=[hbm] * 5,
             scratch_shapes=[
                 pltpu.VMEM((2, 2, tokens, TILE), BF),
                 pltpu.VMEM((2, tokens, half), BF),
@@ -262,32 +259,67 @@
     )(me, in_hbm(parts[0]), *parts[1:], *after)
 
 
-def settle_kernel(xl, total, r1, r2, r3, *refs):
-    mine, theirs = refs[-2:]
+def settle_kernel(count, xl, *refs):
+    mine, theirs, total = refs[-3:]
     rows = mine.shape[0]
+    value = None
+    for ref in refs[:count]:
+        for part in [ref[...]] if len(ref.shape) == 2 else [ref[k] for k in range(ref.shape[0])]:
+            value = part.astype(F32) if value is None else value + part.astype(F32)
+    total[...] = value
     for out, index in ((mine, xl[0]), (theirs, 1 - xl[0])):
-        at = pl.ds(pl.multiple_of(index * rows, 8), rows)
-        value = add(total[at], r1[at], r2[at], r3[at])
-        out[...] = value.astype(out.dtype)
-
-
-def settle(xl, total, received, dtype, *after):
-    rows, width = total.shape
-    whole = pl.BlockSpec((rows, width), lambda s, x: (0, 0))
-    part = pl.BlockSpec((rows // 2, width), lambda s, x: (0, 0))
-    return pl.pallas_call(
-        settle_kernel,
+        out[...] = total[pl.ds(pl.multiple_of(index * rows, 8), rows)].astype(out.dtype)
+
+
+def settle(xl, parts, dtype, *after):
+    rows, width = parts[0].shape[-2:]
+    half = pl.BlockSpec((rows // 2, width), lambda s, x: (0, 0))
+    return pl.pallas_call(
+        functools.partial(settle_kernel, len(parts)),
         out_shape=[jax.ShapeDtypeStruct((rows // 2, width), t) for t in (F32, dtype)],
         grid_spec=pltpu.PrefetchScalarGridSpec(
             num_scalar_prefetch=1,
             grid=(1,),
-            in_specs=[whole] * 4 + [ANY] * len(after),
-            out_specs=[part] * 2,
-        ),
-        compiler_params=pltpu.CompilerParams(vmem_limit_bytes=10 * 2**20),
+            in_specs=[pl.BlockSpec(p.shape, lambda s, x, n=p.ndim: (0,) * n) for p in parts]
+            + [ANY] * len(after),
+            out_specs=[half] * 2,
+            scratch_shapes=[pltpu.VMEM((rows, width), F32)],
+        ),
+        compiler_params=pltpu.CompilerParams(vmem_limit_bytes=16 * 2**20),
         cost_estimate=NO_COST,
         name="settle",
-    )(xl, total, *received, *after)
+    )(xl, *parts, *after)
+
+
+def grow_kernel(side, x, received, *refs):
+    out, held, sems, out_sem = refs[-4:]
+    for k in range(2):
+        pltpu.make_async_copy(x.at[side * 2 + k], held.at[k], sems.at[k]).start()
+    for k in range(2):
+        wait_all(held.at[k], sems.at[k])
+        held[k] = add(held[k], received[k]).astype(BF)
+        pltpu.make_async_copy(held.at[k], out.at[side * 2 + k], out_sem).start()
+    wait_all(held, out_sem)
+
+
+def grow(x, received, side, *after):
+    hbm = pl.BlockSpec(memory_space=pltpu.HBM)
+    return pl.pallas_call(
+        functools.partial(grow_kernel, side),
+        out_shape=pltpu.HBM(x.shape, x.dtype),
+        grid=(1,),
+        in_specs=[hbm, pl.BlockSpec(received.shape, lambda s: (0, 0, 0))] + [ANY] * len(after),
+        out_specs=hbm,
+        scratch_shapes=[
+            pltpu.VMEM(received.shape, x.dtype),
+            pltpu.SemaphoreType.DMA((2,)),
+            pltpu.SemaphoreType.DMA,
+        ],
+        input_output_aliases={0: 0},
+        compiler_params=pltpu.CompilerParams(vmem_limit_bytes=8 * 2**20),
+        cost_estimate=NO_COST,
+        name="grow",
+    )(in_hbm(x), received, *after)
 
 
 def fetch_tiles(step, source, held, sems):
@@ -300,7 +332,7 @@
     wait_all(held.at[step], sems.at[step])
 
 
-def left_kernel(place, mine, other, partner, partner_other, left, out, total, held, sems):
+def left_kernel(place, mine, other, partner, partner_other, left, out, total, packed, held, sems):
     step = pl.program_id(0)
     fetch_tiles(step, left, held, sems)
     at = pl.ds(pl.multiple_of((step & 1) * TILE, TILE), TILE)
@@ -322,14 +354,16 @@
             for y in range(4):
                 for xl in range(2):
                     for c in range(2):
-                        at = (((z * 4 + y) * 2 + xl) * 2 + c) * rows
-                        block = value[:, at : at + rows]
+                        n = ((z * 4 + y) * 2 + xl) * 2 + c
+                        block = value[:, n * rows : (n + 1) * rows]
+                        packed[n, 0:16, 0:rows] = block[0:16]
+                        packed[n, 0:16, rows : 2 * rows] = block[16:32]
+                        packed[n, 0:8, 2 * rows : 3 * rows] = block[32:40]
+                        ready = packed[n].astype(BF)
                         for there in (0, 2):
                             d = c * 32 + (there + z) * 8 + y * 2 + xl
-                            for owner in (0, 64):
-                                out[owner + d, 0:16, 0:rows] = block[0:16]
-                                out[owner + d, 0:16, rows : 2 * rows] = block[16:32]
-                                out[owner + d, 0:8, 2 * rows : 3 * rows] = block[32:40]
+                            out[d] = ready
+                            out[64 + d] = ready
 
 
 def left_product(place, mine, other, partner, partner_other, left):
@@ -337,7 +371,7 @@
     whole = pl.BlockSpec((rows, half), lambda k, p: (0, 0))
     return pl.pallas_call(
         left_kernel,
-        out_shape=jax.ShapeDtypeStruct((128, 16, 128), F32),
+        out_shape=jax.ShapeDtypeStruct((128, 16, 128), BF),
         grid_spec=pltpu.PrefetchScalarGridSpec(
             num_scalar_prefetch=1,
             grid=(4,),
@@ -345,6 +379,7 @@
             out_specs=pl.BlockSpec((128, 16, 128), lambda k, p: (0, 0, 0)),
             scratch_shapes=[
                 pltpu.VMEM((2 * rows, half), F32),
+                pltpu.VMEM((32, 16, 128), F32),
                 pltpu.VMEM((4, TILE, half), BF),
                 pltpu.SemaphoreType.DMA((4,)),
             ],
@@ -362,15 +397,13 @@
     rows = out.shape[0]
     for near in range(2):
         for y in range(4):
-            core = (step >> 1) ^ ((near + y) & 1)
             for xl in range(2):
-                block = blocks[core * 32 + ((step & 1) * 2 + near) * 8 + y * 2 + xl]
+                block = blocks[(step >> 1) * 32 + ((step & 1) * 2 + near) * 8 + y * 2 + xl].astype(F32)
                 at = ((near * 4 + y) * 2 + xl) * rows
                 rows_in[at : at + 16, :] = block[:, 0:rows]
                 rows_in[at + 16 : at + 32, :] = block[:, rows : 2 * rows]
                 rows_in[at + 32 : at + 40, :] = block[0:8, 2 * rows : 3 * rows]
-    high, low = split_pair(rows_in[...])
-    value = contract(high, held[step]) + contract(low, held[step])
+    value = contract(rows_in[...].astype(BF), held[step])
     pl.when(step == 0)(lambda: out.__setitem__(..., value))
     pl.when(step > 0)(lambda: out.__setitem__(..., out[...] + value))
 
@@ -411,33 +444,37 @@
     h = c ^ ((z + y) & 1)
     hidden, out_grad = in_hbm(hidden), in_hbm(out_grad)
     left_inverse, right_inverse = in_hbm(left_inverse), in_hbm(right_inverse)
-    place = jnp.stack([o, h, z, y]).astype(jnp.int32)
+    place = jnp.stack([o, c, z, y]).astype(jnp.int32)
+    place_h = jnp.stack([o, h, z, y]).astype(jnp.int32)
     second_me = jnp.where(h == 0, y, z).astype(jnp.int32)[None]
 
     grads_next, acts_next = in_hbm(shift(out_grad, "c", 1)), in_hbm(shift(hidden, "c", 1))
     partial = cross_own(place, out_grad, hidden)
 
-    own, m1, m2, m3 = cross_term(place, grads_next, acts_next, partial)
-    m_parts = [own, turn(m1, 1, 0), turn(m2, 2, 0), turn(m3, 3, 0)]
-
-    f_own, f1, f2, f3 = factor_term(place, hidden, out_grad, acts_next, grads_next, in_hbm(m1))
-    f_parts = [f_own, turn(f1, 1, 0), turn(f2, 2, 0), turn(f3, 3, 0)]
+    m = cross_term(place, grads_next, acts_next, partial)
+    m_blocks = lax.all_to_all(m, ("z", "y"), 0, 0, tiled=True)
+
+    f_own, right, far_a, far_b, left = factor_term(
+        place_h, hidden, out_grad, acts_next, grads_next, in_hbm(m)
+    )
+    from_left, from_right = turn(far_a, 1, 0), turn(far_b, -1, 0)
 
     my_xl = xl.astype(jnp.int32)[None]
 
     def second_sends(pieces):
         return [turn(piece, s, 1) for s, piece in enumerate(pieces, 1)]
 
-    m, *m_pieces = fold(second_me, m_parts, in_hbm(f_own))
-    m_received = second_sends(m_pieces)
-    mine, theirs = settle(my_xl, m, m_received, F32)
+    right, left = grow(right, from_left, 0), grow(left, from_right, 1)
+    f_parts = [f_own, turn(right, 1, 0), turn(left, -1, 0)]
+
+    mine, theirs = settle(my_xl, [m_blocks], F32, in_hbm(right), in_hbm(left))
     across = lax.ppermute(theirs, ("xl", "o"), [(i, 3 - i) for i in range(4)])
     products = left_product(
         place, mine, shift(theirs, "xl", 1), shift(mine, "o", 1), across, left_inverse
     )
     blocks = lax.all_to_all(products, ("o", "c", "z", "y", "xl"), 0, 0, tiled=True)
     f, *f_pieces = fold(second_me, f_parts, products)
-    f_mine, f_theirs = settle(my_xl, f, second_sends(f_pieces), BF, blocks)
+    f_mine, f_theirs = settle(my_xl, [f, *second_sends(f_pieces)], BF)
     update = right_product(place, blocks, right_inverse, f_pieces[0])
 
     f = add(f_mine, shift(f_theirs, "xl", 1))

time: 147 us -> 166 us (1.13)
  waiting for transfers between devices: 52.4 us -> 74 us
  local copies, waits for them, and re-layouts: 3.52 us -> 0.02 us
    ppermute x12 -> x7, waiting for transfers between devices: 29.7 us -> 47.1 us  [turn(): return lax.ppermute(x, ('z', 'y', 'c'), pairs)]
    all_to_all x1, waiting for transfers between devices: 0.01 us -> 12.6 us  [per_device(): lax.all_to_all(products, ('o', 'c', 'z', 'y', 'xl'), 0, 0, tiled=True)]
    all_to_all x0 -> x1, starting transfers between devices: none -> 7.86 us  [per_device(): m_blocks = lax.all_to_all(m, ('z', 'y'), 0, 0, tiled=True)]
    ppermute x6, waiting for transfers between devices: 18.3 us -> 12.2 us  [shift(): return lax.ppermute(x, axis, [(i, (i + step) % size) for i in range(size)])]
    ppermute x12 -> x7, starting transfers between devices: 21.3 us -> 15.3 us  [turn(): return lax.ppermute(x, ('z', 'y', 'c'), pairs)]
    pallas_call x4 -> x6, Pallas kernels: 24.8 us -> 29.9 us  [the longest x1 15.9 us: factor_term(): pl.pallas_call(factor_kernel, out_shape=[out, out, side, side, out], grid...]
    unnamed x8 -> x0, local copies, waits for them, and re-layouts: 3.49 us -> none
    pallas_call x2 -> x1, Pallas kernels: 7.31 us -> 3.93 us  [fold(): pl.pallas_call(functools.partial(fold_kernel, len(parts)), out_shape=[jax...]
  transfers between devices with their start and end apart: 20 -> 16, of which waited for: 11 -> 11; matrix products, arithmetic and copies ran while one was open for 0% -> 0% of each run, Pallas kernels for 27% -> 22%
where the time goes in v11:
time: 166 us
  waiting for transfers between devices  74 us (45%)
  Pallas kernels  49 us (30%)
  starting transfers between devices  40.9 us (25%)
    ppermute x7, waiting for transfers between devices, turn(): return lax.ppermute(x, ('z', 'y', 'c'), pairs)  47.1 us
    pallas_call x1, Pallas kernels, factor_term(): pl.pallas_call(factor_kernel, out_shape=[out, out, side, side, out], grid...  15.9 us
    ppermute x7, starting transfers between devices, turn(): return lax.ppermute(x, ('z', 'y', 'c'), pairs)  15.3 us
    all_to_all x1, waiting for transfers between devices, per_device(): lax.all_to_all(products, ('o', 'c', 'z', 'y', 'xl'), 0, 0, tiled=True)  12.6 us
    ppermute x6, waiting for transfers between devices, shift(): return lax.ppermute(x, axis, [(i, (i + step) % size) for i in range(size)])  12.2 us
    all_to_all x1, starting transfers between devices, per_device(): lax.all_to_all(products, ('o', 'c', 'z', 'y', 'xl'), 0, 0, tiled=True)  9.89 us
    pallas_call x1, Pallas kernels, cross_term(): pl.pallas_call(cross_kernel, out_shape=pltpu.HBM((16, half // 16, half),...  8.22 us
    all_to_all x1, starting transfers between devices, per_device(): m_blocks = lax.all_to_all(m, ('z', 'y'), 0, 0, tiled=True)  7.86 us
  transfers between devices with their start and end apart: 16, of which 11 were waited for; matrix products, arithmetic and copies ran while one was open for 0% of the time, Pallas kernels for 22%

profile of v11, /device:TPU:1, one launch (start us, length us, event | category | flops | bytes accessed | tf_op | source)
XLA Modules:
  0.0 165.7 jit_solution(6728423214052086125)
XLA Ops:
  0.6 1.5 collective-permute-start
  2.1 0.1 collective-permute-start.1
  2.2 0.1 add_add_fusion.1.place
  2.3 5.4 %cross_own.1.partial = f32[1280,1280]{1,0:T(8,128)S(1)} custom-call(s32[4]{0:T(128)S(1)} %add_add_fusion.1.place, bf16[768,2560]{1,0:T(8,128)(2,1)} %g_own.1, bf16[768,2560]{1,0:T(8,128)(2,1)} %h_own.1), custom_call_target="tpu_custom_call" | custom-call | tf_op jit(solution)/shard_map/cross_own/pallas_call | solution.py:120
  7.7 1.1 collective-permute-done.b.h_next
  8.9 5.6 %collective-permute-done.1.a.g_next = bf16[768,2560]{1,0:T(8,128)(2,1)} collective-permute-done((bf16[768,2560]{1,0:T(8,128)(2,1)}, bf16[768,2560]{1,0:T(8,128)(2,1)}, u32[]{:S(2)}, u32[]{:S(2)}) %collective-permute-start.1) | collective-permute-done | bytes 3932192 | tf_op jit(solution)/shard_map/ppermute | solution.py:25
  14.5 8.2 %cross_term.1.after = bf16[16,80,1280]{2,1,0:T(8,128)(2,1)} custom-call(s32[4]{0:T(128)S(1)} %add_add_fusion.1.place, bf16[768,2560]{1,0:T(8,128)(2,1)} %collective-permute-done.1.a.g_next, bf16[768,2560]{1,0:T(8,128)(2,1)} %collective-permute-done.b.h_next, f32[1280,1280]{1,0:T(8,128)S(1)} %cross_own.1.partial), custom_call_target="tpu_custom_call" | custom-call | tf_op jit(solution)/shard_map/cross_term/pallas_call | solution.py:143
  22.7 7.9 %all-to-all-start = ((bf16[16,80,1280]{2,1,0:T(8,128)(2,1)}), bf16[16,80,1280]{2,1,0:T(8,128)(2,1)S(1)}, u32[]{:S(2)}, u32[]{:S(2)}) async-start(bf16[16,80,1280]{2,1,0:T(8,128)(2,1)} %cross_term.1.after), calls=%async_computation | async-start | bytes 6553600 | tf_op jit(solution)/shard_map/all_to_all | solution.py:455
  30.6 0.1 add_add_fusion.place
  30.7 15.9 %factor_term.1 = (bf16[4,160,1280]{2,1,0:T(8,128)(2,1)}, bf16[4,160,1280]{2,1,0:T(8,128)(2,1)}, bf16[2,160,1280]{2,1,0:T(8,128)(2,1)}, bf16[2,160,1280]{2,1,0:T(8,128)(2,1)}, bf16[4,160,1280]{2,1,0:T(8,128)(2,1)}) custom-call(s32[4]{0:T(128)S(1)} %add_add_fusion.place, bf16[768,2560]{1,0:T(8,128)(2,1)} %h_own.1, bf16[768,2560]{1,0:T(8,128)(2,1)} %g_own.1, ...), custom_call_target="tpu_custom_call" | custom-call | tf_op jit(solution)/shard_map/factor_term/pallas_call | solution.py:199
  46.6 2.2 %collective-permute-start.2 = (bf16[2,160,1280]{2,1,0:T(8,128)(2,1)}, bf16[2,160,1280]{2,1,0:T(8,128)(2,1)S(1)}, u32[]{:S(2)}, u32[]{:S(2)}) collective-permute-start(bf16[2,160,1280]{2,1,0:T(8,128)(2,1)} %get-tuple-element.17), channel_id=1, source_target_pairs={{0,34},{2,8},{10,40},{8,18},{16,50},{18,24},{26,56},{24,2},{34,64}... | collective-permute-start | bytes 2457608 | tf_op jit(solution)/shard_map/ppermute | solution.py:37
  48.8 1.3 collective-permute-start.4
  50.1 33.4 %collective-permute-done.2.received = bf16[2,160,1280]{2,1,0:T(8,128)(2,1)S(1)} collective-permute-done((bf16[2,160,1280]{2,1,0:T(8,128)(2,1)}, bf16[2,160,1280]{2,1,0:T(8,128)(2,1)S(1)}, u32[]{:S(2)}, u32[]{:S(2)}) %collective-permute-start.2) | collective-permute-done | bytes 819232 | tf_op jit(solution)/shard_map/ppermute | solution.py:37
  83.5 2.1 %grow.2.refs_1_ = bf16[4,160,1280]{2,1,0:T(8,128)(2,1)} custom-call(bf16[4,160,1280]{2,1,0:T(8,128)(2,1)} %get-tuple-element.16.x, bf16[2,160,1280]{2,1,0:T(8,128)(2,1)S(1)} %collective-permute-done.2.received), custom_call_target="tpu_custom_call", output_to_operand_aliasing={{}: (0, {})} | custom-call | tf_op jit(solution)/shard_map/grow/pallas_call | solution.py:307
  85.6 2.2 %collective-permute-start.3 = (bf16[4,160,1280]{2,1,0:T(8,128)(2,1)}, bf16[4,160,1280]{2,1,0:T(8,128)(2,1)}, u32[]{:S(2)}, u32[]{:S(2)}) collective-permute-start(bf16[4,160,1280]{2,1,0:T(8,128)(2,1)} %grow.2.refs_1_), channel_id=1, source_target_pairs={{0,34},{2,8},{10,40},{8,18},{16,50},{18,24},{26,56},{24,2},{34,64}... | collective-permute-start | bytes 4915208 | tf_op jit(solution)/shard_map/ppermute | solution.py:37
  87.8 0.4 collective-permute-done.4.received
  88.2 2.1 %grow.3.refs_2_ = bf16[4,160,1280]{2,1,0:T(8,128)(2,1)} custom-call(bf16[4,160,1280]{2,1,0:T(8,128)(2,1)} %get-tuple-element.18.x, bf16[2,160,1280]{2,1,0:T(8,128)(2,1)S(1)} %collective-permute-done.4.received), custom_call_target="tpu_custom_call", output_to_operand_aliasing={{}: (0, {})} | custom-call | tf_op jit(solution)/shard_map/grow/pallas_call | solution.py:307
  90.2 3.7 %collective-permute-start.5 = (bf16[4,160,1280]{2,1,0:T(8,128)(2,1)}, bf16[4,160,1280]{2,1,0:T(8,128)(2,1)}, u32[]{:S(2)}, u32[]{:S(2)}) collective-permute-start(bf16[4,160,1280]{2,1,0:T(8,128)(2,1)} %grow.3.refs_2_), channel_id=1, source_target_pairs={{0,98},{2,24},{10,104},{8,2},{16,114},{18,8},{26,120},{24,18},{34,... | collective-permute-start | bytes 4915208 | tf_op jit(solution)/shard_map/ppermute | solution.py:37
  93.9 0.0 all-to-all-done.refs_0_
  93.9 1.4 settle.2
  95.3 1.2 collective-permute-start.6
  96.6 2.4 %collective-permute-start.7 = (f32[40,1280]{1,0:T(8,128)S(1)}, f32[40,1280]{1,0:T(8,128)S(1)}, u32[]{:S(2)}, u32[]{:S(2)}) collective-permute-start(f32[40,1280]{1,0:T(8,128)S(1)} %get-tuple-element.20.mine), channel_id=1, source_target_pairs={{0,1},{1,0},{2,3},{3,2},{4,5},{5,4},{6,7},{7,6},{8,9},{9,8},{10,11... | collective-permute-start | bytes 614408 | tf_op jit(solution)/shard_map/ppermute | solution.py:25
  99.0 0.2 collective-permute-start.8
  99.2 1.4 collective-permute-done.6.other
  100.6 4.1 %collective-permute-done.7.partner = f32[40,1280]{1,0:T(8,128)S(1)} collective-permute-done((f32[40,1280]{1,0:T(8,128)S(1)}, f32[40,1280]{1,0:T(8,128)S(1)}, u32[]{:S(2)}, u32[]{:S(2)}) %collective-permute-start.7) | collective-permute-done | bytes 204832 | tf_op jit(solution)/shard_map/ppermute | solution.py:25
  104.6 2.1 %collective-permute-done.8.partner_other = f32[40,1280]{1,0:T(8,128)S(1)} collective-permute-done((f32[40,1280]{1,0:T(8,128)}, f32[40,1280]{1,0:T(8,128)S(1)}, u32[]{:S(2)}, u32[]{:S(2)}) %collective-permute-start.8) | collective-permute-done | bytes 204832 | tf_op jit(solution)/shard_map/ppermute | solution.py:471
  106.7 5.0 %left_product.1.refs_3_ = bf16[128,16,128]{2,1,0:T(8,128)(2,1)} custom-call(s32[4]{0:T(128)S(1)} %add_add_fusion.1.place, f32[40,1280]{1,0:T(8,128)S(1)} %get-tuple-element.20.mine, f32[40,1280]{1,0:T(8,128)S(1)} %collective-permute-done.6.other, f32[40,1280]{1,0:T(8,128)S(1)} %collective-permute-done.7.partner, ...), custom_call_target="tpu_custom_call" | custom-call | tf_op jit(solution)/shard_map/left_product/pallas_call | solution.py:372
  111.8 0.0 collective-permute-done.3.refs_1_
  111.8 5.1 %collective-permute-done.5.refs_2_ = bf16[4,160,1280]{2,1,0:T(8,128)(2,1)} collective-permute-done((bf16[4,160,1280]{2,1,0:T(8,128)(2,1)}, bf16[4,160,1280]{2,1,0:T(8,128)(2,1)}, u32[]{:S(2)}, u32[]{:S(2)}) %collective-permute-start.5) | collective-permute-done | bytes 1638432 | tf_op jit(solution)/shard_map/ppermute | solution.py:37
  116.9 3.9 %fold.1 = (f32[160,1280]{1,0:T(8,128)S(1)}, bf16[160,1280]{1,0:T(8,128)(2,1)S(1)}, bf16[160,1280]{1,0:T(8,128)(2,1)S(1)}, bf16[160,1280]{1,0:T(8,128)(2,1)S(1)}) custom-call(s32[1]{0:T(128)} %bitcast.1.me, bf16[4,160,1280]{2,1,0:T(8,128)(2,1)} %get-tuple-element.15.refs_0_, bf16[4,160,1280]{2,1,0:T(8,128)(2,1)} %collective-permute-done.3.refs_1_, ...), custom_call_target="tpu_custom_call" | custom-call | tf_op jit(solution)/shard_map/fold/pallas_call | solution.py:244
  120.8 0.6 collective-permute-start.9
  121.4 2.7 %collective-permute-start.10 = (bf16[160,1280]{1,0:T(8,128)(2,1)S(1)}, bf16[160,1280]{1,0:T(8,128)(2,1)S(1)}, u32[]{:S(2)}, u32[]{:S(2)}) collective-permute-start(bf16[160,1280]{1,0:T(8,128)(2,1)S(1)} %get-tuple-element.24), channel_id=1, source_target_pairs={{0,16},{2,66},{10,26},{8,72},{16,0},{18,82},{26,10},{24,88},{34,50... | collective-permute-start | bytes 1228808 | tf_op jit(solution)/shard_map/ppermute | solution.py:37
  124.1 2.5 %collective-permute-start.11 = (bf16[160,1280]{1,0:T(8,128)(2,1)S(1)}, bf16[160,1280]{1,0:T(8,128)(2,1)S(1)}, u32[]{:S(2)}, u32[]{:S(2)}) collective-permute-start(bf16[160,1280]{1,0:T(8,128)(2,1)S(1)} %get-tuple-element.25), channel_id=1, source_target_pairs={{0,26},{2,96},{10,0},{8,106},{16,10},{18,112},{26,16},{24,122},{34... | collective-permute-start | bytes 1228808 | tf_op jit(solution)/shard_map/ppermute | solution.py:37
  126.6 7.2 %collective-permute-done.9.refs_1_ = bf16[160,1280]{1,0:T(8,128)(2,1)S(1)} collective-permute-done((bf16[160,1280]{1,0:T(8,128)(2,1)S(1)}, bf16[160,1280]{1,0:T(8,128)(2,1)S(1)}, u32[]{:S(2)}, u32[]{:S(2)}) %collective-permute-start.9) | collective-permute-done | bytes 409632 | tf_op jit(solution)/shard_map/ppermute | solution.py:37
  133.9 0.0 collective-permute-done.10.refs_2_
  133.9 0.9 collective-permute-done.11.refs_3_
  134.8 0.3 settle.3
  135.1 1.3 collective-permute-start.12
  136.4 9.9 %all-to-all-start.1 = ((bf16[128,16,128]{2,1,0:T(8,128)(2,1)}), bf16[128,16,128]{2,1,0:T(8,128)(2,1)S(1)}, u32[]{:S(2)}, u32[]{:S(2)}) async-start(bf16[128,16,128]{2,1,0:T(8,128)(2,1)} %left_product.1.refs_3_), calls=%async_computation.1 | async-start | bytes 1048576 | tf_op jit(solution)/shard_map/all_to_all | solution.py:475
  146.3 0.0 collective-permute-done.12
  146.3 0.1 add_multiply_fusion
  146.4 1.1 collective-permute-start.13
  147.6 12.6 %all-to-all-done.1.blocks = bf16[128,16,128]{2,1,0:T(8,128)(2,1)S(1)} async-done(((bf16[128,16,128]{2,1,0:T(8,128)(2,1)}), bf16[128,16,128]{2,1,0:T(8,128)(2,1)S(1)}, u32[]{:S(2)}, u32[]{:S(2)}) %all-to-all-start.1) | async-done | bytes 524320 | tf_op jit(solution)/shard_map/all_to_all | solution.py:475
  160.2 4.7 %right_product.1 = f32[40,1280]{1,0:T(8,128)} custom-call(s32[4]{0:T(128)S(1)} %add_add_fusion.1.place, bf16[128,16,128]{2,1,0:T(8,128)(2,1)S(1)} %all-to-all-done.1.blocks, bf16[2560,1280]{1,0:T(8,128)(2,1)} %right.1, bf16[160,1280]{1,0:T(8,128)(2,1)S(1)} %get-tuple-element.23.late), custom_call_target="tpu_custom_call" | custom-call | tf_op jit(solution)/shard_map/right_product/pallas_call | solution.py:414
  164.9 0.0 collective-permute-done.13
  165.0 0.8 maximum_bitcast_fusion
  (2 shorter events, 0.1 us)
Async XLA Ops:
  0.6 8.3 %collective-permute-start = (bf16[768,2560]{1,0:T(8,128)(2,1)}, bf16[768,2560]{1,0:T(8,128)(2,1)}, u32[]{:S(2)}, u32[]{:S(2)}) collective-permute-start(bf16[768,2560]{1,0:T(8,128)(2,1)} %h_own.1), channel_id=1, source_target_pairs={{0,2},{2,0},{1,3},{3,1},{4,6},{6,4},{5,7},{7,5},{8,10},{10,8},{9,1... | collective-permute-start | bytes 11796488 | tf_op jit(solution)/shard_map/ppermute | solution.py:25
  2.1 12.4 %collective-permute-start.1 = (bf16[768,2560]{1,0:T(8,128)(2,1)}, bf16[768,2560]{1,0:T(8,128)(2,1)}, u32[]{:S(2)}, u32[]{:S(2)}) collective-permute-start(bf16[768,2560]{1,0:T(8,128)(2,1)} %g_own.1), channel_id=1, source_target_pairs={{0,2},{2,0},{1,3},{3,1},{4,6},{6,4},{5,7},{7,5},{8,10},{10,8},{9,1... | collective-permute-start | bytes 11796488 | tf_op jit(solution)/shard_map/ppermute | solution.py:25
  22.7 71.2 %all-to-all-start = ((bf16[16,80,1280]{2,1,0:T(8,128)(2,1)}), bf16[16,80,1280]{2,1,0:T(8,128)(2,1)S(1)}, u32[]{:S(2)}, u32[]{:S(2)}) async-start(bf16[16,80,1280]{2,1,0:T(8,128)(2,1)} %cross_term.1.after), calls=%async_computation | async-start | bytes 6553600 | tf_op jit(solution)/shard_map/all_to_all | solution.py:455
  46.6 36.9 %collective-permute-start.2 = (bf16[2,160,1280]{2,1,0:T(8,128)(2,1)}, bf16[2,160,1280]{2,1,0:T(8,128)(2,1)S(1)}, u32[]{:S(2)}, u32[]{:S(2)}) collective-permute-start(bf16[2,160,1280]{2,1,0:T(8,128)(2,1)} %get-tuple-element.17), channel_id=1, source_target_pairs={{0,34},{2,8},{10,40},{8,18},{16,50},{18,24},{26,56},{24,2},{34,64}... | collective-permute-start | bytes 2457608 | tf_op jit(solution)/shard_map/ppermute | solution.py:37
  48.8 39.4 %collective-permute-start.4 = (bf16[2,160,1280]{2,1,0:T(8,128)(2,1)}, bf16[2,160,1280]{2,1,0:T(8,128)(2,1)S(1)}, u32[]{:S(2)}, u32[]{:S(2)}) collective-permute-start(bf16[2,160,1280]{2,1,0:T(8,128)(2,1)} %get-tuple-element.19), channel_id=1, source_target_pairs={{0,98},{2,24},{10,104},{8,2},{16,114},{18,8},{26,120},{24,18},{34,... | collective-permute-start | bytes 2457608 | tf_op jit(solution)/shard_map/ppermute | solution.py:37
  85.6 26.2 %collective-permute-start.3 = (bf16[4,160,1280]{2,1,0:T(8,128)(2,1)}, bf16[4,160,1280]{2,1,0:T(8,128)(2,1)}, u32[]{:S(2)}, u32[]{:S(2)}) collective-permute-start(bf16[4,160,1280]{2,1,0:T(8,128)(2,1)} %grow.2.refs_1_), channel_id=1, source_target_pairs={{0,34},{2,8},{10,40},{8,18},{16,50},{18,24},{26,56},{24,2},{34,64}... | collective-permute-start | bytes 4915208 | tf_op jit(solution)/shard_map/ppermute | solution.py:37
  90.2 26.6 %collective-permute-start.5 = (bf16[4,160,1280]{2,1,0:T(8,128)(2,1)}, bf16[4,160,1280]{2,1,0:T(8,128)(2,1)}, u32[]{:S(2)}, u32[]{:S(2)}) collective-permute-start(bf16[4,160,1280]{2,1,0:T(8,128)(2,1)} %grow.3.refs_2_), channel_id=1, source_target_pairs={{0,98},{2,24},{10,104},{8,2},{16,114},{18,8},{26,120},{24,18},{34,... | collective-permute-start | bytes 4915208 | tf_op jit(solution)/shard_map/ppermute | solution.py:37
  95.3 5.2 %collective-permute-start.6 = (f32[40,1280]{1,0:T(8,128)}, f32[40,1280]{1,0:T(8,128)S(1)}, u32[]{:S(2)}, u32[]{:S(2)}) collective-permute-start(f32[40,1280]{1,0:T(8,128)} %get-tuple-element.21), channel_id=1, source_target_pairs={{0,4},{4,0},{1,5},{5,1},{2,6},{6,2},{3,7},{7,3},{8,12},{12,8},{9,1... | collective-permute-start | bytes 614408 | tf_op jit(solution)/shard_map/ppermute | solution.py:25
  96.6 8.1 %collective-permute-start.7 = (f32[40,1280]{1,0:T(8,128)S(1)}, f32[40,1280]{1,0:T(8,128)S(1)}, u32[]{:S(2)}, u32[]{:S(2)}) collective-permute-start(f32[40,1280]{1,0:T(8,128)S(1)} %get-tuple-element.20.mine), channel_id=1, source_target_pairs={{0,1},{1,0},{2,3},{3,2},{4,5},{5,4},{6,7},{7,6},{8,9},{9,8},{10,11... | collective-permute-start | bytes 614408 | tf_op jit(solution)/shard_map/ppermute | solution.py:25
  99.0 7.7 %collective-permute-start.8 = (f32[40,1280]{1,0:T(8,128)}, f32[40,1280]{1,0:T(8,128)S(1)}, u32[]{:S(2)}, u32[]{:S(2)}) collective-permute-start(f32[40,1280]{1,0:T(8,128)} %get-tuple-element.21), channel_id=1, source_target_pairs={{0,5},{1,4},{4,1},{5,0},{2,7},{3,6},{6,3},{7,2},{8,13},{9,12},{12,... | collective-permute-start | bytes 614408 | tf_op jit(solution)/shard_map/ppermute | solution.py:471
  120.8 13.0 %collective-permute-start.9 = (bf16[160,1280]{1,0:T(8,128)(2,1)S(1)}, bf16[160,1280]{1,0:T(8,128)(2,1)S(1)}, u32[]{:S(2)}, u32[]{:S(2)}) collective-permute-start(bf16[160,1280]{1,0:T(8,128)(2,1)S(1)} %get-tuple-element.23.late), channel_id=1, source_target_pairs={{0,10},{2,32},{10,16},{8,42},{16,26},{18,48},{26,0},{24,58},{34,40... | collective-permute-start | bytes 1228808 | tf_op jit(solution)/shard_map/ppermute | solution.py:37
  121.4 12.5 %collective-permute-start.10 = (bf16[160,1280]{1,0:T(8,128)(2,1)S(1)}, bf16[160,1280]{1,0:T(8,128)(2,1)S(1)}, u32[]{:S(2)}, u32[]{:S(2)}) collective-permute-start(bf16[160,1280]{1,0:T(8,128)(2,1)S(1)} %get-tuple-element.24), channel_id=1, source_target_pairs={{0,16},{2,66},{10,26},{8,72},{16,0},{18,82},{26,10},{24,88},{34,50... | collective-permute-start | bytes 1228808 | tf_op jit(solution)/shard_map/ppermute | solution.py:37
  124.1 10.7 %collective-permute-start.11 = (bf16[160,1280]{1,0:T(8,128)(2,1)S(1)}, bf16[160,1280]{1,0:T(8,128)(2,1)S(1)}, u32[]{:S(2)}, u32[]{:S(2)}) collective-permute-start(bf16[160,1280]{1,0:T(8,128)(2,1)S(1)} %get-tuple-element.25), channel_id=1, source_target_pairs={{0,26},{2,96},{10,0},{8,106},{16,10},{18,112},{26,16},{24,122},{34... | collective-permute-start | bytes 1228808 | tf_op jit(solution)/shard_map/ppermute | solution.py:37
  135.1 11.2 %collective-permute-start.12 = (bf16[80,1280]{1,0:T(8,128)(2,1)S(1)}, bf16[80,1280]{1,0:T(8,128)(2,1)S(1)}, u32[]{:S(2)}, u32[]{:S(2)}) collective-permute-start(bf16[80,1280]{1,0:T(8,128)(2,1)S(1)} %get-tuple-element.27), channel_id=1, source_target_pairs={{0,4},{4,0},{1,5},{5,1},{2,6},{6,2},{3,7},{7,3},{8,12},{12,8},{9,1... | collective-permute-start | bytes 614408 | tf_op jit(solution)/shard_map/ppermute | solution.py:25
  136.4 23.8 %all-to-all-start.1 = ((bf16[128,16,128]{2,1,0:T(8,128)(2,1)}), bf16[128,16,128]{2,1,0:T(8,128)(2,1)S(1)}, u32[]{:S(2)}, u32[]{:S(2)}) async-start(bf16[128,16,128]{2,1,0:T(8,128)(2,1)} %left_product.1.refs_3_), calls=%async_computation.1 | async-start | bytes 1048576 | tf_op jit(solution)/shard_map/all_to_all | solution.py:475
  146.4 18.5 %collective-permute-start.13 = (f32[40,1280]{1,0:T(8,128)S(1)}, f32[40,1280]{1,0:T(8,128)S(1)}, u32[]{:S(2)}, u32[]{:S(2)}) collective-permute-start(f32[40,1280]{1,0:T(8,128)S(1)} %dynamic-slice_bitcast_fusion), channel_id=1, source_target_pairs={{0,2},{2,0},{1,3},{3,1},{4,6},{6,4},{5,7},{7,5},{8,10},{10,8},{9,1... | collective-permute-start | bytes 614408 | tf_op jit(solution)/shard_map/ppermute | solution.py:25

commit v12 on v11

--- a/solution.py
+++ b/solution.py
@@ -50,34 +50,37 @@
     return high, (x - high.astype(F32)).astype(BF)
 
 
-def place_tile(place, buffer, sem, outs, z):
-    rows = TILE // 4
+def place_tile(place, buffer, sem, outs, m, zs):
+    rows = TILE // (zs * 4)
 
     def start(at, out, slot):
-        block = buffer.at[z, pl.ds(at, rows)]
+        block = buffer.at[m, pl.ds(at, rows)]
         pltpu.make_async_copy(block, out.at[slot], sem).start()
 
-    @pl.when(place[1] == 0)
-    def _():
-        for r, out in enumerate(outs):
-
-            @pl.when(((z - place[2] + 4) & 3) == r)
-            def _():
-                for k in range(4):
-                    if isinstance(out, tuple):
-                        start(k * rows, out[k // 2], k % 2)
-                    else:
-                        start(k * rows, out, k)
-
-    @pl.when(place[1] == 1)
-    def _():
-        for r, out in enumerate(outs):
-            at = pl.multiple_of(((place[3] + r) & 3) * rows, 16)
-            if isinstance(out, tuple):
-                pl.when(z < 2)(functools.partial(start, at, out[0], z & 1))
-                pl.when(z >= 2)(functools.partial(start, at, out[1], z & 1))
-            else:
-                start(at, out, z)
+    for a in range(zs):
+        z = m * zs + a
+
+        @pl.when(place[1] == 0)
+        def _():
+            for r, out in enumerate(outs):
+
+                @pl.when(((z - place[2] + 4) & 3) == r)
+                def _():
+                    for k in range(4):
+                        if isinstance(out, tuple):
+                            start((a * 4 + k) * rows, out[k // 2], k % 2)
+                        else:
+                            start((a * 4 + k) * rows, out, k)
+
+        @pl.when(place[1] == 1)
+        def _():
+            for r, out in enumerate(outs):
+                at = pl.multiple_of((a * 4 + ((place[3] + r) & 3)) * rows, 16)
+                if isinstance(out, tuple):
+                    pl.when(z < 2)(functools.partial(start, at, out[0], z & 1))
+                    pl.when(z >= 2)(functools.partial(start, at, out[1], z & 1))
+                else:
+                    start(at, out, z)
 
 
 def wait_all(buffer, sem):
@@ -101,7 +104,7 @@
     out[...] = contract(lhs[m], rhs[...])
 
 
-def cross_kernel(place, a, b, partial, out, held, held_sems):
+def cross_kernel(place, a, b, partial, own, ahead1, ahead2, ahead3, held, buffer, held_sems, sem):
     m = pl.program_id(0)
 
     @pl.when(m == 0)
@@ -112,7 +115,9 @@
 
     tile = contract(a[...], b[...])
     wait_all(held.at[m], held_sems.at[m])
-    out[...] = (held[m] + tile).astype(BF).reshape(out.shape)
+    buffer[m] = (held[m] + tile).astype(BF)
+    place_tile(place, buffer, sem, [own, ahead1, ahead2, ahead3], m, 2)
+    pl.when(m == 1)(lambda: wait_all(buffer, sem))
 
 
 def cross_own(place, grads, acts):
@@ -140,9 +145,10 @@
 
 def cross_term(place, grads_next, acts_next, partial):
     tokens, half = grads_next.shape[0], grads_next.shape[1] // 2
+    out = pltpu.HBM((4, half // 16, half), BF)
     return pl.pallas_call(
         cross_kernel,
-        out_shape=pltpu.HBM((16, half // 16, half), BF),
+        out_shape=[out] * 4,
         grid_spec=pltpu.PrefetchScalarGridSpec(
             num_scalar_prefetch=1,
             grid=(2,),
@@ -151,8 +157,13 @@
                 pl.BlockSpec((tokens, half), lambda m, p: (0, p[1] ^ p[0])),
                 ANY,
             ],
-            out_specs=pl.BlockSpec((8, half // 16, half), lambda m, p: (m, 0, 0)),
-            scratch_shapes=[pltpu.VMEM((2, TILE, half), F32), pltpu.SemaphoreType.DMA((2,))],
+            out_specs=[pl.BlockSpec(memory_space=pltpu.HBM)] * 4,
+            scratch_shapes=[
+                pltpu.VMEM((2, TILE, half), F32),
+                pltpu.VMEM((2, TILE, half), BF),
+                pltpu.SemaphoreType.DMA((2,)),
+                pltpu.SemaphoreType.DMA,
+            ],
         ),
         compiler_params=pltpu.CompilerParams(vmem_limit_bytes=28 * 2**20),
         cost_estimate=NO_COST,
@@ -186,7 +197,7 @@
     pl.when(m == 0)(lambda: wait_all(rhs, rhs_sem))
 
     buffer[m] = (contract(lhs[slot, 0], rhs[0]) + contract(lhs[slot, 1], rhs[1])).astype(BF)
-    place_tile(place, buffer, sem, [own, right, (far_a, far_b), left], m)
+    place_tile(place, buffer, sem, [own, right, (far_a, far_b), left], m, 1)
     pl.when(m == 3)(lambda: wait_all(buffer, sem))
 
 
@@ -286,7 +297,7 @@
             scratch_shapes=[pltpu.VMEM((rows, width), F32)],
         ),
         compiler_params=pltpu.CompilerParams(vmem_limit_bytes=16 * 2**20),
-        cost_estimate=NO_COST,
+        cost_estimate=pl.CostEstimate(flops=0, bytes_accessed=0, transcendentals=0),
         name="settle",
     )(xl, *parts, *after)
 
@@ -398,7 +409,8 @@
     for near in range(2):
         for y in range(4):
             for xl in range(2):
-                block = blocks[(step >> 1) * 32 + ((step & 1) * 2 + near) * 8 + y * 2 + xl].astype(F32)
+                core = (step >> 1) ^ ((near + y) & 1)
+                block = blocks[core * 32 + ((step & 1) * 2 + near) * 8 + y * 2 + xl].astype(F32)
                 at = ((near * 4 + y) * 2 + xl) * rows
                 rows_in[at : at + 16, :] = block[:, 0:rows]
                 rows_in[at + 16 : at + 32, :] = block[:, rows : 2 * rows]
@@ -444,18 +456,17 @@
     h = c ^ ((z + y) & 1)
     hidden, out_grad = in_hbm(hidden), in_hbm(out_grad)
     left_inverse, right_inverse = in_hbm(left_inverse), in_hbm(right_inverse)
-    place = jnp.stack([o, c, z, y]).astype(jnp.int32)
-    place_h = jnp.stack([o, h, z, y]).astype(jnp.int32)
+    place = jnp.stack([o, h, z, y]).astype(jnp.int32)
     second_me = jnp.where(h == 0, y, z).astype(jnp.int32)[None]
 
     grads_next, acts_next = in_hbm(shift(out_grad, "c", 1)), in_hbm(shift(hidden, "c", 1))
     partial = cross_own(place, out_grad, hidden)
 
-    m = cross_term(place, grads_next, acts_next, partial)
-    m_blocks = lax.all_to_all(m, ("z", "y"), 0, 0, tiled=True)
+    own, m1, m2, m3 = cross_term(place, grads_next, acts_next, partial)
+    m_parts = [own, turn(m1, 1, 0), turn(m2, 2, 0), turn(m3, 3, 0)]
 
     f_own, right, far_a, far_b, left = factor_term(
-        place_h, hidden, out_grad, acts_next, grads_next, in_hbm(m)
+        place, hidden, out_grad, acts_next, grads_next, in_hbm(m1)
     )
     from_left, from_right = turn(far_a, 1, 0), turn(far_b, -1, 0)
 
@@ -464,17 +475,20 @@
     def second_sends(pieces):
         return [turn(piece, s, 1) for s, piece in enumerate(pieces, 1)]
 
-    right, left = grow(right, from_left, 0), grow(left, from_right, 1)
+    m, *m_pieces = fold(second_me, m_parts, in_hbm(f_own))
+    m_received = second_sends(m_pieces)
+    right = grow(right, from_left, 0, m_received[0])
+    left = grow(left, from_right, 1, m_received[1], m_received[2])
     f_parts = [f_own, turn(right, 1, 0), turn(left, -1, 0)]
 
-    mine, theirs = settle(my_xl, [m_blocks], F32, in_hbm(right), in_hbm(left))
+    mine, theirs = settle(my_xl, [m, *m_received], F32)
     across = lax.ppermute(theirs, ("xl", "o"), [(i, 3 - i) for i in range(4)])
     products = left_product(
         place, mine, shift(theirs, "xl", 1), shift(mine, "o", 1), across, left_inverse
     )
     blocks = lax.all_to_all(products, ("o", "c", "z", "y", "xl"), 0, 0, tiled=True)
     f, *f_pieces = fold(second_me, f_parts, products)
-    f_mine, f_theirs = settle(my_xl, [f, *second_sends(f_pieces)], BF)
+    f_mine, f_theirs = settle(my_xl, [f, *second_sends(f_pieces)], BF, blocks)
     update = right_product(place, blocks, right_inverse, f_pieces[0])
 
     f = add(f_mine, shift(f_theirs, "xl", 1))

time: 166 us -> 133 us (0.80)
  waiting for transfers between devices: 74 us -> 41.8 us
  starting transfers between devices: 40.9 us -> 36.2 us
  Pallas kernels: 49 us -> 51.5 us
    ppermute x7 -> x13, waiting for transfers between devices: 47.1 us -> 13.9 us  [turn(): return lax.ppermute(x, ('z', 'y', 'c'), pairs)]
    ppermute x6, waiting for transfers between devices: 12.2 us -> 21.9 us  [shift(): return lax.ppermute(x, axis, [(i, (i + step) % size) for i in range(size)])]
    all_to_all x1, waiting for transfers between devices: 12.6 us -> 3.64 us  [per_device(): lax.all_to_all(products, ('o', 'c', 'z', 'y', 'xl'), 0, 0, tiled=True)]
    ppermute x7 -> x13, starting transfers between devices: 15.3 us -> 24.1 us  [turn(): return lax.ppermute(x, ('z', 'y', 'c'), pairs)]
    all_to_all x1 -> x0, starting transfers between devices: 7.86 us -> none  [per_device(): m_blocks = lax.all_to_all(m, ('z', 'y'), 0, 0, tiled=True)]
    all_to_all x1, starting transfers between devices: 9.89 us -> 5.66 us  [per_device(): lax.all_to_all(products, ('o', 'c', 'z', 'y', 'xl'), 0, 0, tiled=True)]
    pallas_call x1 -> x2, Pallas kernels: 3.93 us -> 5.74 us  [fold(): pl.pallas_call(functools.partial(fold_kernel, len(parts)), out_shape=[jax...]
  transfers between devices with their start and end apart: 16 -> 21, of which waited for: 11 -> 10; matrix products, arithmetic and copies ran while one was open for 0% -> 0% of each run, Pallas kernels for 22% -> 32%
where the time goes in v12:
time: 133 us; the launch traced here: 132 us
  Pallas kernels  51.5 us (39%)
  waiting for transfers between devices  41.8 us (31%)
  starting transfers between devices  36.2 us (27%)
    ppermute x13, starting transfers between devices, turn(): return lax.ppermute(x, ('z', 'y', 'c'), pairs)  24.1 us
    ppermute x6, waiting for transfers between devices, shift(): return lax.ppermute(x, axis, [(i, (i + step) % size) for i in range(size)])  21.9 us
    pallas_call x1, Pallas kernels, factor_term(): pl.pallas_call(factor_kernel, out_shape=[out, out, side, side, out], grid...  15.9 us
    ppermute x13, waiting for transfers between devices, turn(): return lax.ppermute(x, ('z', 'y', 'c'), pairs)  13.9 us
    pallas_call x1, Pallas kernels, cross_term(): pl.pallas_call(cross_kernel, out_shape=[out] * 4, grid_spec=pltpu.Prefetc...  8.29 us
    ppermute x6, starting transfers between devices, shift(): return lax.ppermute(x, axis, [(i, (i + step) % size) for i in range(size)])  6.26 us
    pallas_call x2, Pallas kernels, fold(): pl.pallas_call(functools.partial(fold_kernel, len(parts)), out_shape=[jax...  5.74 us
    all_to_all x1, starting transfers between devices, per_device(): lax.all_to_all(products, ('o', 'c', 'z', 'y', 'xl'), 0, 0, tiled=True)  5.66 us
  transfers between devices with their start and end apart: 21, of which 10 were waited for; matrix products, arithmetic and copies ran while one was open for 0% of the time, Pallas kernels for 32%

profile of v12, /device:TPU:1, one launch (start us, length us, event | category | flops | bytes accessed | tf_op | source)
XLA Modules:
  0.0 132.2 jit_solution(2961873218902418279)
XLA Ops:
  0.6 1.5 %collective-permute-start = (bf16[768,2560]{1,0:T(8,128)(2,1)}, bf16[768,2560]{1,0:T(8,128)(2,1)}, u32[]{:S(2)}, u32[]{:S(2)}) collective-permute-start(bf16[768,2560]{1,0:T(8,128)(2,1)} %h_own.1), channel_id=1, source_target_pairs={{0,2},{2,0},{1,3},{3,1},{4,6},{6,4},{5,7},{7,5},{8,10},{10,8},{9,1... | collective-permute-start | bytes 11796488 | tf_op jit(solution)/shard_map/ppermute | solution.py:25
  2.1 0.1 collective-permute-start.1
  2.2 0.1 pad_add_fusion.place
  2.3 5.4 %cross_own.1.partial = f32[1280,1280]{1,0:T(8,128)S(1)} custom-call(s32[4]{0:T(128)S(1)} %pad_add_fusion.place, bf16[768,2560]{1,0:T(8,128)(2,1)} %g_own.1, bf16[768,2560]{1,0:T(8,128)(2,1)} %h_own.1), custom_call_target="tpu_custom_call" | custom-call | tf_op jit(solution)/shard_map/cross_own/pallas_call | solution.py:125
  7.7 1.1 collective-permute-done.b.h_next
  8.9 5.6 %collective-permute-done.1.a.g_next = bf16[768,2560]{1,0:T(8,128)(2,1)} collective-permute-done((bf16[768,2560]{1,0:T(8,128)(2,1)}, bf16[768,2560]{1,0:T(8,128)(2,1)}, u32[]{:S(2)}, u32[]{:S(2)}) %collective-permute-start.1) | collective-permute-done | bytes 3932192 | tf_op jit(solution)/shard_map/ppermute | solution.py:25
  14.5 8.3 %cross_term.1 = (bf16[4,80,1280]{2,1,0:T(8,128)(2,1)}, bf16[4,80,1280]{2,1,0:T(8,128)(2,1)}, bf16[4,80,1280]{2,1,0:T(8,128)(2,1)}, bf16[4,80,1280]{2,1,0:T(8,128)(2,1)}) custom-call(s32[4]{0:T(128)S(1)} %pad_add_fusion.place, bf16[768,2560]{1,0:T(8,128)(2,1)} %collective-permute-done.1.a.g_next, bf16[768,2560]{1,0:T(8,128)(2,1)} %collective-permute-done.b.h_next, ...), custom_call_target="tpu_custom_call" | custom-call | tf_op jit(solution)/shard_map/cross_term/pallas_call | solution.py:149
  22.8 1.7 %collective-permute-start.3 = (bf16[4,80,1280]{2,1,0:T(8,128)(2,1)}, bf16[4,80,1280]{2,1,0:T(8,128)(2,1)S(1)}, u32[]{:S(2)}, u32[]{:S(2)}) collective-permute-start(bf16[4,80,1280]{2,1,0:T(8,128)(2,1)} %get-tuple-element.23.after), channel_id=1, source_target_pairs={{0,34},{2,8},{10,40},{8,18},{16,50},{18,24},{26,56},{24,2},{34,64}... | collective-permute-start | bytes 2457608 | tf_op jit(solution)/shard_map/ppermute | solution.py:37
  24.5 2.6 %collective-permute-start.4 = (bf16[4,80,1280]{2,1,0:T(8,128)(2,1)}, bf16[4,80,1280]{2,1,0:T(8,128)(2,1)S(1)}, u32[]{:S(2)}, u32[]{:S(2)}) collective-permute-start(bf16[4,80,1280]{2,1,0:T(8,128)(2,1)} %get-tuple-element.28), channel_id=1, source_target_pairs={{0,64},{2,18},{10,74},{8,24},{16,80},{18,2},{26,90},{24,8},{34,98}... | collective-permute-start | bytes 2457608 | tf_op jit(solution)/shard_map/ppermute | solution.py:37
  27.1 1.4 %collective-permute-start.5 = (bf16[4,80,1280]{2,1,0:T(8,128)(2,1)}, bf16[4,80,1280]{2,1,0:T(8,128)(2,1)S(1)}, u32[]{:S(2)}, u32[]{:S(2)}) collective-permute-start(bf16[4,80,1280]{2,1,0:T(8,128)(2,1)} %get-tuple-element.29), channel_id=1, source_target_pairs={{0,98},{2,24},{10,104},{8,2},{16,114},{18,8},{26,120},{24,18},{34,... | collective-permute-start | bytes 2457608 | tf_op jit(solution)/shard_map/ppermute | solution.py:37
  28.5 15.9 %factor_term.1 = (bf16[4,160,1280]{2,1,0:T(8,128)(2,1)}, bf16[4,160,1280]{2,1,0:T(8,128)(2,1)}, bf16[2,160,1280]{2,1,0:T(8,128)(2,1)}, bf16[2,160,1280]{2,1,0:T(8,128)(2,1)}, bf16[4,160,1280]{2,1,0:T(8,128)(2,1)}) custom-call(s32[4]{0:T(128)S(1)} %pad_add_fusion.place, bf16[768,2560]{1,0:T(8,128)(2,1)} %h_own.1, bf16[768,2560]{1,0:T(8,128)(2,1)} %g_own.1, ...), custom_call_target="tpu_custom_call" | custom-call | tf_op jit(solution)/shard_map/factor_term/pallas_call | solution.py:210
  44.4 0.4 collective-permute-start.2
  44.8 2.6 %collective-permute-start.8 = (bf16[2,160,1280]{2,1,0:T(8,128)(2,1)}, bf16[2,160,1280]{2,1,0:T(8,128)(2,1)S(1)}, u32[]{:S(2)}, u32[]{:S(2)}) collective-permute-start(bf16[2,160,1280]{2,1,0:T(8,128)(2,1)} %get-tuple-element.32), channel_id=1, source_target_pairs={{0,98},{2,24},{10,104},{8,2},{16,114},{18,8},{26,120},{24,18},{34,... | collective-permute-start | bytes 2457608 | tf_op jit(solution)/shard_map/ppermute | solution.py:37
  47.4 0.0 collective-permute-done.4.refs_2_
  47.4 0.0 collective-permute-done.5.refs_3_
  47.4 1.5 %fold.2 = (f32[80,1280]{1,0:T(8,128)S(1)}, bf16[80,1280]{1,0:T(8,128)(2,1)S(1)}, bf16[80,1280]{1,0:T(8,128)(2,1)S(1)}, bf16[80,1280]{1,0:T(8,128)(2,1)S(1)}) custom-call(s32[1]{0:T(128)} %bitcast.1.me, bf16[4,80,1280]{2,1,0:T(8,128)(2,1)} %get-tuple-element.27.refs_0_, bf16[4,80,1280]{2,1,0:T(8,128)(2,1)S(1)} %collective-permute-done.3.refs_1_, ...), custom_call_target="tpu_custom_call" | custom-call | tf_op jit(solution)/shard_map/fold/pallas_call | solution.py:255
  49.0 0.0 copy-start
  49.0 1.7 %collective-permute-start.6 = (bf16[80,1280]{1,0:T(8,128)(2,1)S(1)}, bf16[80,1280]{1,0:T(8,128)(2,1)S(1)}, u32[]{:S(2)}, u32[]{:S(2)}) collective-permute-start(bf16[80,1280]{1,0:T(8,128)(2,1)S(1)} %get-tuple-element.30), channel_id=1, source_target_pairs={{0,10},{2,32},{10,16},{8,42},{16,26},{18,48},{26,0},{24,58},{34,40... | collective-permute-start | bytes 614408 | tf_op jit(solution)/shard_map/ppermute | solution.py:37
  50.7 3.3 %collective-permute-start.9 = (bf16[80,1280]{1,0:T(8,128)(2,1)S(1)}, bf16[80,1280]{1,0:T(8,128)(2,1)S(1)}, u32[]{:S(2)}, u32[]{:S(2)}) collective-permute-start(bf16[80,1280]{1,0:T(8,128)(2,1)S(1)} %get-tuple-element.33), channel_id=1, source_target_pairs={{0,16},{2,66},{10,26},{8,72},{16,0},{18,82},{26,10},{24,88},{34,50... | collective-permute-start | bytes 614408 | tf_op jit(solution)/shard_map/ppermute | solution.py:37
  54.0 1.3 collective-permute-start.10
  55.3 7.1 %collective-permute-done.2.received = bf16[2,160,1280]{2,1,0:T(8,128)(2,1)} collective-permute-done((bf16[2,160,1280]{2,1,0:T(8,128)(2,1)}, bf16[2,160,1280]{2,1,0:T(8,128)(2,1)}, u32[]{:S(2)}, u32[]{:S(2)}) %collective-permute-start.2) | collective-permute-done | bytes 819232 | tf_op jit(solution)/shard_map/ppermute | solution.py:37
  62.4 3.2 %grow.2 = bf16[4,160,1280]{2,1,0:T(8,128)(2,1)} custom-call(bf16[4,160,1280]{2,1,0:T(8,128)(2,1)} %get-tuple-element.25.x, bf16[2,160,1280]{2,1,0:T(8,128)(2,1)} %collective-permute-done.2.received, bf16[80,1280]{1,0:T(8,128)(2,1)S(1)} %collective-permute-done.6.refs_0_.refs_1_), custom_call_target="tpu_custom_call", output_to_operand_aliasing={{}: (0, {})} | custom-call | tf_op jit(solution)/shard_map/grow/pallas_call | solution.py:318
  65.6 0.1 collective-permute-start.7
  65.7 2.1 %grow.3 = bf16[4,160,1280]{2,1,0:T(8,128)(2,1)} custom-call(bf16[4,160,1280]{2,1,0:T(8,128)(2,1)} %get-tuple-element.31.x, bf16[2,160,1280]{2,1,0:T(8,128)(2,1)S(1)} %collective-permute-done.8.received, bf16[80,1280]{1,0:T(8,128)(2,1)S(1)} %collective-permute-done.9.refs_0_.refs_2_, ...), custom_call_target="tpu_custom_call", output_to_operand_aliasing={{}: (0, {})} | custom-call | tf_op jit(solution)/shard_map/grow/pallas_call | solution.py:318
  67.8 3.0 %collective-permute-start.11 = (bf16[4,160,1280]{2,1,0:T(8,128)(2,1)}, bf16[4,160,1280]{2,1,0:T(8,128)(2,1)}, u32[]{:S(2)}, u32[]{:S(2)}) collective-permute-start(bf16[4,160,1280]{2,1,0:T(8,128)(2,1)} %grow.3), channel_id=1, source_target_pairs={{0,98},{2,24},{10,104},{8,2},{16,114},{18,8},{26,120},{24,18},{34,... | collective-permute-start | bytes 4915208 | tf_op jit(solution)/shard_map/ppermute | solution.py:37
  70.8 1.0 copy-done.1
  71.8 0.2 settle.2
  72.0 1.3 collective-permute-start.12
  73.3 2.5 %collective-permute-start.13 = (f32[40,1280]{1,0:T(8,128)S(1)}, f32[40,1280]{1,0:T(8,128)S(1)}, u32[]{:S(2)}, u32[]{:S(2)}) collective-permute-start(f32[40,1280]{1,0:T(8,128)S(1)} %get-tuple-element.36.mine), channel_id=1, source_target_pairs={{0,1},{1,0},{2,3},{3,2},{4,5},{5,4},{6,7},{7,6},{8,9},{9,8},{10,11... | collective-permute-start | bytes 614408 | tf_op jit(solution)/shard_map/ppermute | solution.py:25
  75.7 0.2 collective-permute-start.14
  75.9 2.2 %collective-permute-done.12.other = f32[40,1280]{1,0:T(8,128)S(1)} collective-permute-done((f32[40,1280]{1,0:T(8,128)S(1)}, f32[40,1280]{1,0:T(8,128)S(1)}, u32[]{:S(2)}, u32[]{:S(2)}) %collective-permute-start.12) | collective-permute-done | bytes 204832 | tf_op jit(solution)/shard_map/ppermute | solution.py:25
  78.1 6.8 %collective-permute-done.13.partner = f32[40,1280]{1,0:T(8,128)S(1)} collective-permute-done((f32[40,1280]{1,0:T(8,128)S(1)}, f32[40,1280]{1,0:T(8,128)S(1)}, u32[]{:S(2)}, u32[]{:S(2)}) %collective-permute-start.13) | collective-permute-done | bytes 204832 | tf_op jit(solution)/shard_map/ppermute | solution.py:25
  84.8 2.4 %collective-permute-done.14.partner_other = f32[40,1280]{1,0:T(8,128)S(1)} collective-permute-done((f32[40,1280]{1,0:T(8,128)S(1)}, f32[40,1280]{1,0:T(8,128)S(1)}, u32[]{:S(2)}, u32[]{:S(2)}) %collective-permute-start.14) | collective-permute-done | bytes 204832 | tf_op jit(solution)/shard_map/ppermute | solution.py:485
  87.2 5.0 %left_product.1.refs_3_ = bf16[128,16,128]{2,1,0:T(8,128)(2,1)} custom-call(s32[4]{0:T(128)S(1)} %pad_add_fusion.place, f32[40,1280]{1,0:T(8,128)S(1)} %get-tuple-element.36.mine, f32[40,1280]{1,0:T(8,128)S(1)} %collective-permute-done.12.other, f32[40,1280]{1,0:T(8,128)S(1)} %collective-permute-done.13.partner, ...), custom_call_target="tpu_custom_call" | custom-call | tf_op jit(solution)/shard_map/left_product/pallas_call | solution.py:383
  92.2 5.7 %all-to-all-start = ((bf16[128,16,128]{2,1,0:T(8,128)(2,1)}), bf16[128,16,128]{2,1,0:T(8,128)(2,1)S(1)}, u32[]{:S(2)}, u32[]{:S(2)}) async-start(bf16[128,16,128]{2,1,0:T(8,128)(2,1)} %left_product.1.refs_3_), calls=%async_computation | async-start | bytes 1048576 | tf_op jit(solution)/shard_map/all_to_all | solution.py:489
  97.9 4.2 %fold.3 = (f32[160,1280]{1,0:T(8,128)S(1)}, bf16[160,1280]{1,0:T(8,128)(2,1)S(1)}, bf16[160,1280]{1,0:T(8,128)(2,1)}, bf16[160,1280]{1,0:T(8,128)(2,1)}) custom-call(s32[1]{0:T(128)} %bitcast.1.me, bf16[4,160,1280]{2,1,0:T(8,128)(2,1)} %get-tuple-element.24.refs_4_.refs_0_, bf16[4,160,1280]{2,1,0:T(8,128)(2,1)S(1)} %collective-permute-done.7.refs_1_, ...), custom_call_target="tpu_custom_call" | custom-call | tf_op jit(solution)/shard_map/fold/pallas_call | solution.py:255
  102.1 1.8 %collective-permute-start.15 = (bf16[160,1280]{1,0:T(8,128)(2,1)S(1)}, bf16[160,1280]{1,0:T(8,128)(2,1)S(1)}, u32[]{:S(2)}, u32[]{:S(2)}) collective-permute-start(bf16[160,1280]{1,0:T(8,128)(2,1)S(1)} %get-tuple-element.39.late), channel_id=1, source_target_pairs={{0,10},{2,32},{10,16},{8,42},{16,26},{18,48},{26,0},{24,58},{34,40... | collective-permute-start | bytes 1228808 | tf_op jit(solution)/shard_map/ppermute | solution.py:37
  103.9 2.9 %collective-permute-start.16 = (bf16[160,1280]{1,0:T(8,128)(2,1)}, bf16[160,1280]{1,0:T(8,128)(2,1)S(1)}, u32[]{:S(2)}, u32[]{:S(2)}) collective-permute-start(bf16[160,1280]{1,0:T(8,128)(2,1)} %get-tuple-element.40), channel_id=1, source_target_pairs={{0,16},{2,66},{10,26},{8,72},{16,0},{18,82},{26,10},{24,88},{34,50... | collective-permute-start | bytes 1228808 | tf_op jit(solution)/shard_map/ppermute | solution.py:37
  106.8 1.2 collective-permute-start.17
  108.1 3.6 %all-to-all-done.refs_4_.blocks = bf16[128,16,128]{2,1,0:T(8,128)(2,1)S(1)} async-done(((bf16[128,16,128]{2,1,0:T(8,128)(2,1)}), bf16[128,16,128]{2,1,0:T(8,128)(2,1)S(1)}, u32[]{:S(2)}, u32[]{:S(2)}) %all-to-all-start) | async-done | bytes 524320 | tf_op jit(solution)/shard_map/all_to_all | solution.py:489
  111.7 2.6 %collective-permute-done.15.refs_1_ = bf16[160,1280]{1,0:T(8,128)(2,1)S(1)} collective-permute-done((bf16[160,1280]{1,0:T(8,128)(2,1)S(1)}, bf16[160,1280]{1,0:T(8,128)(2,1)S(1)}, u32[]{:S(2)}, u32[]{:S(2)}) %collective-permute-start.15) | collective-permute-done | bytes 409632 | tf_op jit(solution)/shard_map/ppermute | solution.py:37
  114.3 4.2 %collective-permute-done.16.refs_2_ = bf16[160,1280]{1,0:T(8,128)(2,1)S(1)} collective-permute-done((bf16[160,1280]{1,0:T(8,128)(2,1)}, bf16[160,1280]{1,0:T(8,128)(2,1)S(1)}, u32[]{:S(2)}, u32[]{:S(2)}) %collective-permute-start.16) | collective-permute-done | bytes 409632 | tf_op jit(solution)/shard_map/ppermute | solution.py:37
  118.5 1.0 settle.3
  119.5 0.5 collective-permute-start.18
  120.0 6.2 %collective-permute-done.18 = bf16[80,1280]{1,0:T(8,128)(2,1)S(1)} collective-permute-done((bf16[80,1280]{1,0:T(8,128)(2,1)}, bf16[80,1280]{1,0:T(8,128)(2,1)S(1)}, u32[]{:S(2)}, u32[]{:S(2)}) %collective-permute-start.18) | collective-permute-done | bytes 204832 | tf_op jit(solution)/shard_map/ppermute | solution.py:25
  126.2 0.5 collective-permute-start.19
  126.7 4.7 %right_product.1 = f32[40,1280]{1,0:T(8,128)} custom-call(s32[4]{0:T(128)S(1)} %pad_add_fusion.place, bf16[128,16,128]{2,1,0:T(8,128)(2,1)S(1)} %all-to-all-done.refs_4_.blocks, bf16[2560,1280]{1,0:T(8,128)(2,1)} %right.1, bf16[160,1280]{1,0:T(8,128)(2,1)S(1)} %get-tuple-element.39.late), custom_call_target="tpu_custom_call" | custom-call | tf_op jit(solution)/shard_map/right_product/pallas_call | solution.py:426
  131.4 0.8 maximum_bitcast_fusion
  (14 shorter events, 0.1 us)
Async XLA Ops:
  0.6 8.3 %collective-permute-start = (bf16[768,2560]{1,0:T(8,128)(2,1)}, bf16[768,2560]{1,0:T(8,128)(2,1)}, u32[]{:S(2)}, u32[]{:S(2)}) collective-permute-start(bf16[768,2560]{1,0:T(8,128)(2,1)} %h_own.1), channel_id=1, source_target_pairs={{0,2},{2,0},{1,3},{3,1},{4,6},{6,4},{5,7},{7,5},{8,10},{10,8},{9,1... | collective-permute-start | bytes 11796488 | tf_op jit(solution)/shard_map/ppermute | solution.py:25
  2.1 12.4 %collective-permute-start.1 = (bf16[768,2560]{1,0:T(8,128)(2,1)}, bf16[768,2560]{1,0:T(8,128)(2,1)}, u32[]{:S(2)}, u32[]{:S(2)}) collective-permute-start(bf16[768,2560]{1,0:T(8,128)(2,1)} %g_own.1), channel_id=1, source_target_pairs={{0,2},{2,0},{1,3},{3,1},{4,6},{6,4},{5,7},{7,5},{8,10},{10,8},{9,1... | collective-permute-start | bytes 11796488 | tf_op jit(solution)/shard_map/ppermute | solution.py:25
  22.8 24.6 %collective-permute-start.3 = (bf16[4,80,1280]{2,1,0:T(8,128)(2,1)}, bf16[4,80,1280]{2,1,0:T(8,128)(2,1)S(1)}, u32[]{:S(2)}, u32[]{:S(2)}) collective-permute-start(bf16[4,80,1280]{2,1,0:T(8,128)(2,1)} %get-tuple-element.23.after), channel_id=1, source_target_pairs={{0,34},{2,8},{10,40},{8,18},{16,50},{18,24},{26,56},{24,2},{34,64}... | collective-permute-start | bytes 2457608 | tf_op jit(solution)/shard_map/ppermute | solution.py:37
  24.5 22.9 %collective-permute-start.4 = (bf16[4,80,1280]{2,1,0:T(8,128)(2,1)}, bf16[4,80,1280]{2,1,0:T(8,128)(2,1)S(1)}, u32[]{:S(2)}, u32[]{:S(2)}) collective-permute-start(bf16[4,80,1280]{2,1,0:T(8,128)(2,1)} %get-tuple-element.28), channel_id=1, source_target_pairs={{0,64},{2,18},{10,74},{8,24},{16,80},{18,2},{26,90},{24,8},{34,98}... | collective-permute-start | bytes 2457608 | tf_op jit(solution)/shard_map/ppermute | solution.py:37
  27.1 20.3 %collective-permute-start.5 = (bf16[4,80,1280]{2,1,0:T(8,128)(2,1)}, bf16[4,80,1280]{2,1,0:T(8,128)(2,1)S(1)}, u32[]{:S(2)}, u32[]{:S(2)}) collective-permute-start(bf16[4,80,1280]{2,1,0:T(8,128)(2,1)} %get-tuple-element.29), channel_id=1, source_target_pairs={{0,98},{2,24},{10,104},{8,2},{16,114},{18,8},{26,120},{24,18},{34,... | collective-permute-start | bytes 2457608 | tf_op jit(solution)/shard_map/ppermute | solution.py:37
  44.4 18.0 %collective-permute-start.2 = (bf16[2,160,1280]{2,1,0:T(8,128)(2,1)}, bf16[2,160,1280]{2,1,0:T(8,128)(2,1)}, u32[]{:S(2)}, u32[]{:S(2)}) collective-permute-start(bf16[2,160,1280]{2,1,0:T(8,128)(2,1)} %get-tuple-element.26), channel_id=1, source_target_pairs={{0,34},{2,8},{10,40},{8,18},{16,50},{18,24},{26,56},{24,2},{34,64}... | collective-permute-start | bytes 2457608 | tf_op jit(solution)/shard_map/ppermute | solution.py:37
  44.8 20.9 %collective-permute-start.8 = (bf16[2,160,1280]{2,1,0:T(8,128)(2,1)}, bf16[2,160,1280]{2,1,0:T(8,128)(2,1)S(1)}, u32[]{:S(2)}, u32[]{:S(2)}) collective-permute-start(bf16[2,160,1280]{2,1,0:T(8,128)(2,1)} %get-tuple-element.32), channel_id=1, source_target_pairs={{0,98},{2,24},{10,104},{8,2},{16,114},{18,8},{26,120},{24,18},{34,... | collective-permute-start | bytes 2457608 | tf_op jit(solution)/shard_map/ppermute | solution.py:37
  49.0 18.8 %copy-start = (f32[80,1280]{1,0:T(8,128)}, f32[80,1280]{1,0:T(8,128)S(1)}, u32[]{:S(2)}) copy-start(f32[80,1280]{1,0:T(8,128)S(1)} %get-tuple-element.35.refs_0_) | copy-start | bytes 1228804
  49.0 13.4 %collective-permute-start.6 = (bf16[80,1280]{1,0:T(8,128)(2,1)S(1)}, bf16[80,1280]{1,0:T(8,128)(2,1)S(1)}, u32[]{:S(2)}, u32[]{:S(2)}) collective-permute-start(bf16[80,1280]{1,0:T(8,128)(2,1)S(1)} %get-tuple-element.30), channel_id=1, source_target_pairs={{0,10},{2,32},{10,16},{8,42},{16,26},{18,48},{26,0},{24,58},{34,40... | collective-permute-start | bytes 614408 | tf_op jit(solution)/shard_map/ppermute | solution.py:37
  50.7 15.0 %collective-permute-start.9 = (bf16[80,1280]{1,0:T(8,128)(2,1)S(1)}, bf16[80,1280]{1,0:T(8,128)(2,1)S(1)}, u32[]{:S(2)}, u32[]{:S(2)}) collective-permute-start(bf16[80,1280]{1,0:T(8,128)(2,1)S(1)} %get-tuple-element.33), channel_id=1, source_target_pairs={{0,16},{2,66},{10,26},{8,72},{16,0},{18,82},{26,10},{24,88},{34,50... | collective-permute-start | bytes 614408 | tf_op jit(solution)/shard_map/ppermute | solution.py:37
  54.0 11.7 %collective-permute-start.10 = (bf16[80,1280]{1,0:T(8,128)(2,1)S(1)}, bf16[80,1280]{1,0:T(8,128)(2,1)S(1)}, u32[]{:S(2)}, u32[]{:S(2)}) collective-permute-start(bf16[80,1280]{1,0:T(8,128)(2,1)S(1)} %get-tuple-element.34), channel_id=1, source_target_pairs={{0,26},{2,96},{10,0},{8,106},{16,10},{18,112},{26,16},{24,122},{34... | collective-permute-start | bytes 614408 | tf_op jit(solution)/shard_map/ppermute | solution.py:37
  65.6 32.3 %collective-permute-start.7 = (bf16[4,160,1280]{2,1,0:T(8,128)(2,1)}, bf16[4,160,1280]{2,1,0:T(8,128)(2,1)S(1)}, u32[]{:S(2)}, u32[]{:S(2)}) collective-permute-start(bf16[4,160,1280]{2,1,0:T(8,128)(2,1)} %grow.2), channel_id=1, source_target_pairs={{0,34},{2,8},{10,40},{8,18},{16,50},{18,24},{26,56},{24,2},{34,64}... | collective-permute-start | bytes 4915208 | tf_op jit(solution)/shard_map/ppermute | solution.py:37
  67.8 30.1 %collective-permute-start.11 = (bf16[4,160,1280]{2,1,0:T(8,128)(2,1)}, bf16[4,160,1280]{2,1,0:T(8,128)(2,1)}, u32[]{:S(2)}, u32[]{:S(2)}) collective-permute-start(bf16[4,160,1280]{2,1,0:T(8,128)(2,1)} %grow.3), channel_id=1, source_target_pairs={{0,98},{2,24},{10,104},{8,2},{16,114},{18,8},{26,120},{24,18},{34,... | collective-permute-start | bytes 4915208 | tf_op jit(solution)/shard_map/ppermute | solution.py:37
  70.8 1.0 copy-start.1
  72.0 6.1 %collective-permute-start.12 = (f32[40,1280]{1,0:T(8,128)S(1)}, f32[40,1280]{1,0:T(8,128)S(1)}, u32[]{:S(2)}, u32[]{:S(2)}) collective-permute-start(f32[40,1280]{1,0:T(8,128)S(1)} %get-tuple-element.37), channel_id=1, source_target_pairs={{0,4},{4,0},{1,5},{5,1},{2,6},{6,2},{3,7},{7,3},{8,12},{12,8},{9,1... | collective-permute-start | bytes 614408 | tf_op jit(solution)/shard_map/ppermute | solution.py:25
  73.3 11.6 %collective-permute-start.13 = (f32[40,1280]{1,0:T(8,128)S(1)}, f32[40,1280]{1,0:T(8,128)S(1)}, u32[]{:S(2)}, u32[]{:S(2)}) collective-permute-start(f32[40,1280]{1,0:T(8,128)S(1)} %get-tuple-element.36.mine), channel_id=1, source_target_pairs={{0,1},{1,0},{2,3},{3,2},{4,5},{5,4},{6,7},{7,6},{8,9},{9,8},{10,11... | collective-permute-start | bytes 614408 | tf_op jit(solution)/shard_map/ppermute | solution.py:25
  75.7 11.5 %collective-permute-start.14 = (f32[40,1280]{1,0:T(8,128)S(1)}, f32[40,1280]{1,0:T(8,128)S(1)}, u32[]{:S(2)}, u32[]{:S(2)}) collective-permute-start(f32[40,1280]{1,0:T(8,128)S(1)} %get-tuple-element.37), channel_id=1, source_target_pairs={{0,5},{1,4},{4,1},{5,0},{2,7},{3,6},{6,3},{7,2},{8,13},{9,12},{12,... | collective-permute-start | bytes 614408 | tf_op jit(solution)/shard_map/ppermute | solution.py:485
  92.2 19.5 %all-to-all-start = ((bf16[128,16,128]{2,1,0:T(8,128)(2,1)}), bf16[128,16,128]{2,1,0:T(8,128)(2,1)S(1)}, u32[]{:S(2)}, u32[]{:S(2)}) async-start(bf16[128,16,128]{2,1,0:T(8,128)(2,1)} %left_product.1.refs_3_), calls=%async_computation | async-start | bytes 1048576 | tf_op jit(solution)/shard_map/all_to_all | solution.py:489
  102.1 12.2 %collective-permute-start.15 = (bf16[160,1280]{1,0:T(8,128)(2,1)S(1)}, bf16[160,1280]{1,0:T(8,128)(2,1)S(1)}, u32[]{:S(2)}, u32[]{:S(2)}) collective-permute-start(bf16[160,1280]{1,0:T(8,128)(2,1)S(1)} %get-tuple-element.39.late), channel_id=1, source_target_pairs={{0,10},{2,32},{10,16},{8,42},{16,26},{18,48},{26,0},{24,58},{34,40... | collective-permute-start | bytes 1228808 | tf_op jit(solution)/shard_map/ppermute | solution.py:37
  103.9 14.6 %collective-permute-start.16 = (bf16[160,1280]{1,0:T(8,128)(2,1)}, bf16[160,1280]{1,0:T(8,128)(2,1)S(1)}, u32[]{:S(2)}, u32[]{:S(2)}) collective-permute-start(bf16[160,1280]{1,0:T(8,128)(2,1)} %get-tuple-element.40), channel_id=1, source_target_pairs={{0,16},{2,66},{10,26},{8,72},{16,0},{18,82},{26,10},{24,88},{34,50... | collective-permute-start | bytes 1228808 | tf_op jit(solution)/shard_map/ppermute | solution.py:37
  106.8 11.6 %collective-permute-start.17 = (bf16[160,1280]{1,0:T(8,128)(2,1)}, bf16[160,1280]{1,0:T(8,128)(2,1)S(1)}, u32[]{:S(2)}, u32[]{:S(2)}) collective-permute-start(bf16[160,1280]{1,0:T(8,128)(2,1)} %get-tuple-element.41), channel_id=1, source_target_pairs={{0,26},{2,96},{10,0},{8,106},{16,10},{18,112},{26,16},{24,122},{34... | collective-permute-start | bytes 1228808 | tf_op jit(solution)/shard_map/ppermute | solution.py:37
  119.5 6.6 %collective-permute-start.18 = (bf16[80,1280]{1,0:T(8,128)(2,1)}, bf16[80,1280]{1,0:T(8,128)(2,1)S(1)}, u32[]{:S(2)}, u32[]{:S(2)}) collective-permute-start(bf16[80,1280]{1,0:T(8,128)(2,1)} %get-tuple-element.43), channel_id=1, source_target_pairs={{0,4},{4,0},{1,5},{5,1},{2,6},{6,2},{3,7},{7,3},{8,12},{12,8},{9,1... | collective-permute-start | bytes 614408 | tf_op jit(solution)/shard_map/ppermute | solution.py:25
  126.2 5.2 %collective-permute-start.19 = (f32[40,1280]{1,0:T(8,128)S(1)}, f32[40,1280]{1,0:T(8,128)S(1)}, u32[]{:S(2)}, u32[]{:S(2)}) collective-permute-start(f32[40,1280]{1,0:T(8,128)S(1)} %dynamic-slice_bitcast_fusion), channel_id=1, source_target_pairs={{0,2},{2,0},{1,3},{3,1},{4,6},{6,4},{5,7},{7,5},{8,10},{10,8},{9,1... | collective-permute-start | bytes 614408 | tf_op jit(solution)/shard_map/ppermute | solution.py:25

commit v13 on v12

--- a/solution.py
+++ b/solution.py
@@ -10,7 +10,6 @@
 BF = jnp.bfloat16
 F32 = jnp.float32
 TILE = 640
-NO_COST = pl.CostEstimate(flops=0, bytes_accessed=0, transcendentals=0)
 ANY = pl.BlockSpec(memory_space=pl.ANY)
 
 
@@ -138,7 +137,9 @@
             ],
         ),
         compiler_params=pltpu.CompilerParams(vmem_limit_bytes=28 * 2**20),
-        cost_estimate=NO_COST,
+        cost_estimate=pl.CostEstimate(
+            flops=2 * tokens * half * half, bytes_accessed=8 * tokens * half, transcendentals=0
+        ),
         name="cross_own",
     )(place, grads, acts)
 
@@ -166,7 +167,9 @@
             ],
         ),
         compiler_params=pltpu.CompilerParams(vmem_limit_bytes=28 * 2**20),
-        cost_estimate=NO_COST,
+        cost_estimate=pl.CostEstimate(
+            flops=2 * tokens * half * half, bytes_accessed=10 * tokens * half, transcendentals=0
+        ),
         name="cross_term",
     )(place, grads_next, acts_next, partial)
 
@@ -225,7 +228,9 @@
             ],
         ),
         compiler_params=pltpu.CompilerParams(vmem_limit_bytes=30 * 2**20),
-        cost_estimate=NO_COST,
+        cost_estimate=pl.CostEstimate(
+            flops=4 * tokens * width * half, bytes_accessed=16 * tokens * half, transcendentals=0
+        ),
         name="factor_term",
     )(place, acts, grads, acts_next, grads_next, after)
 
@@ -254,7 +259,8 @@
     whole = pl.BlockSpec((rows, width), lambda s, m: (0, 0))
     return pl.pallas_call(
         functools.partial(fold_kernel, len(parts)),
-        out_shape=[jax.ShapeDtypeStruct((rows, width), t) for t in (F32, BF, BF, BF)],
+        out_shape=[pltpu.HBM((rows, width), F32)]
+        + [jax.ShapeDtypeStruct((rows, width), BF)] * 3,
         grid_spec=pltpu.PrefetchScalarGridSpec(
             num_scalar_prefetch=1,
             grid=(1,),
@@ -265,7 +271,7 @@
             scratch_shapes=[pltpu.VMEM((4, rows, width), BF), pltpu.SemaphoreType.DMA],
         ),
         compiler_params=pltpu.CompilerParams(vmem_limit_bytes=26 * 2**20),
-        cost_estimate=NO_COST,
+        cost_estimate=pl.CostEstimate(flops=0, bytes_accessed=0, transcendentals=0),
         name="fold",
     )(me, in_hbm(parts[0]), *parts[1:], *after)
 
@@ -328,7 +334,7 @@
         ],
         input_output_aliases={0: 0},
         compiler_params=pltpu.CompilerParams(vmem_limit_bytes=8 * 2**20),
-        cost_estimate=NO_COST,
+        cost_estimate=pl.CostEstimate(flops=0, bytes_accessed=0, transcendentals=0),
         name="grow",
     )(in_hbm(x), received, *after)
 
@@ -396,7 +402,9 @@
             ],
         ),
         compiler_params=pltpu.CompilerParams(vmem_limit_bytes=20 * 2**20),
-        cost_estimate=NO_COST,
+        cost_estimate=pl.CostEstimate(
+            flops=256 * rows * half * half, bytes_accessed=4 * half * half, transcendentals=0
+        ),
         name="left_product",
     )(place, mine, other, partner, partner_other, left)
 
@@ -442,7 +450,9 @@
             ],
         ),
         compiler_params=pltpu.CompilerParams(vmem_limit_bytes=20 * 2**20),
-        cost_estimate=NO_COST,
+        cost_estimate=pl.CostEstimate(
+            flops=640 * rows * half * half, bytes_accessed=4 * half * half, transcendentals=0
+        ),
         name="right_product",
     )(place, blocks, right, late)
 
@@ -477,19 +487,19 @@
 
     m, *m_pieces = fold(second_me, m_parts, in_hbm(f_own))
     m_received = second_sends(m_pieces)
-    right = grow(right, from_left, 0, m_received[0])
-    left = grow(left, from_right, 1, m_received[1], m_received[2])
+    right = grow(right, from_left, 0, *m_received)
+    left = grow(left, from_right, 1, *m_received)
     f_parts = [f_own, turn(right, 1, 0), turn(left, -1, 0)]
 
-    mine, theirs = settle(my_xl, [m, *m_received], F32)
+    mine, theirs = settle(my_xl, [in_hbm(m), *m_received], F32)
     across = lax.ppermute(theirs, ("xl", "o"), [(i, 3 - i) for i in range(4)])
     products = left_product(
         place, mine, shift(theirs, "xl", 1), shift(mine, "o", 1), across, left_inverse
     )
     blocks = lax.all_to_all(products, ("o", "c", "z", "y", "xl"), 0, 0, tiled=True)
     f, *f_pieces = fold(second_me, f_parts, products)
-    f_mine, f_theirs = settle(my_xl, [f, *second_sends(f_pieces)], BF, blocks)
     update = right_product(place, blocks, right_inverse, f_pieces[0])
+    f_mine, f_theirs = settle(my_xl, [in_hbm(f), *second_sends(f_pieces)], BF, in_hbm(update))
 
     f = add(f_mine, shift(f_theirs, "xl", 1))
     f = f * jnp.where(first, 1.0 / token_total, 1.0).astype(F32)

time: 133 us -> 129 us (0.970)
  waiting for transfers between devices: 41.8 us -> 31.7 us
  starting transfers between devices: 36.2 us -> 41.3 us
  Pallas kernels: 51.5 us -> 53.6 us
    ppermute x6, waiting for transfers between devices: 21.9 us -> 14.8 us  [shift(): return lax.ppermute(x, axis, [(i, (i + step) % size) for i in range(size)])]
    all_to_all x1, waiting for transfers between devices: 3.64 us -> 0.01 us  [per_device(): lax.all_to_all(products, ('o', 'c', 'z', 'y', 'xl'), 0, 0, tiled=True)]
    all_to_all x1, starting transfers between devices: 5.66 us -> 8.29 us  [per_device(): lax.all_to_all(products, ('o', 'c', 'z', 'y', 'xl'), 0, 0, tiled=True)]
    pallas_call x2, Pallas kernels: 5.74 us -> 7.87 us  [fold(): pl.pallas_call(functools.partial(fold_kernel, len(parts)), out_shape=[plt...]
    ppermute x13, starting transfers between devices: 24.1 us -> 26 us  [turn(): return lax.ppermute(x, ('z', 'y', 'c'), pairs)]
    pallas_call x2, Pallas kernels: 1.17 us -> 2.61 us  [settle(): pl.pallas_call(functools.partial(settle_kernel, len(parts)), out_shape=[j...]
  transfers between devices with their start and end apart: 21 -> 21, of which waited for: 10 -> 11; matrix products, arithmetic and copies ran while one was open for 0% -> 0% of each run, Pallas kernels for 32% -> 34%
where the time goes in v13:
time: 129 us; the launch traced here: 128 us
  Pallas kernels  53.6 us (42%)
  starting transfers between devices  41.3 us (32%)
  waiting for transfers between devices  31.7 us (25%)
    ppermute x13, starting transfers between devices, turn(): return lax.ppermute(x, ('z', 'y', 'c'), pairs)  26 us
    pallas_call x1, Pallas kernels, factor_term(): pl.pallas_call(factor_kernel, out_shape=[out, out, side, side, out], grid...  15.9 us
    ppermute x6, waiting for transfers between devices, shift(): return lax.ppermute(x, axis, [(i, (i + step) % size) for i in range(size)])  14.8 us
    ppermute x13, waiting for transfers between devices, turn(): return lax.ppermute(x, ('z', 'y', 'c'), pairs)  14.6 us
    all_to_all x1, starting transfers between devices, per_device(): lax.all_to_all(products, ('o', 'c', 'z', 'y', 'xl'), 0, 0, tiled=True)  8.29 us
    pallas_call x1, Pallas kernels, cross_term(): pl.pallas_call(cross_kernel, out_shape=[out] * 4, grid_spec=pltpu.Prefetc...  8.05 us
    pallas_call x2, Pallas kernels, fold(): pl.pallas_call(functools.partial(fold_kernel, len(parts)), out_shape=[plt...  7.87 us
    ppermute x6, starting transfers between devices, shift(): return lax.ppermute(x, axis, [(i, (i + step) % size) for i in range(size)])  6.85 us
  transfers between devices with their start and end apart: 21, of which 11 were waited for; matrix products, arithmetic and copies ran while one was open for 0% of the time, Pallas kernels for 34%

profile of v13, /device:TPU:1, one launch (start us, length us, event | category | flops | bytes accessed | tf_op | source)
XLA Modules:
  0.0 128.4 jit_solution(14999387465590101720)
XLA Ops:
  0.6 1.5 %collective-permute-start = (bf16[768,2560]{1,0:T(8,128)(2,1)}, bf16[768,2560]{1,0:T(8,128)(2,1)}, u32[]{:S(2)}, u32[]{:S(2)}) collective-permute-start(bf16[768,2560]{1,0:T(8,128)(2,1)} %h_own.1), channel_id=1, source_target_pairs={{0,2},{2,0},{1,3},{3,1},{4,6},{6,4},{5,7},{7,5},{8,10},{10,8},{9,1... | collective-permute-start | bytes 11796488 | tf_op jit(solution)/shard_map/ppermute | solution.py:24
  2.1 0.1 collective-permute-start.1
  2.2 0.1 pad_add_fusion.place
  2.3 5.4 %cross_own.1.partial = f32[1280,1280]{1,0:T(8,128)S(1)} custom-call(s32[4]{0:T(128)S(1)} %pad_add_fusion.place, bf16[768,2560]{1,0:T(8,128)(2,1)} %g_own.1, bf16[768,2560]{1,0:T(8,128)(2,1)} %h_own.1), custom_call_target="tpu_custom_call" | custom-call | flops 2516582400 | bytes 7864320 | tf_op jit(solution)/shard_map/cross_own/pallas_call | solution.py:124
  7.7 1.1 collective-permute-done.b.h_next
  8.9 5.6 %collective-permute-done.1.a.g_next = bf16[768,2560]{1,0:T(8,128)(2,1)} collective-permute-done((bf16[768,2560]{1,0:T(8,128)(2,1)}, bf16[768,2560]{1,0:T(8,128)(2,1)}, u32[]{:S(2)}, u32[]{:S(2)}) %collective-permute-start.1) | collective-permute-done | bytes 3932192 | tf_op jit(solution)/shard_map/ppermute | solution.py:24
  14.5 8.1 %cross_term.1 = (bf16[4,80,1280]{2,1,0:T(8,128)(2,1)}, bf16[4,80,1280]{2,1,0:T(8,128)(2,1)}, bf16[4,80,1280]{2,1,0:T(8,128)(2,1)}, bf16[4,80,1280]{2,1,0:T(8,128)(2,1)}) custom-call(s32[4]{0:T(128)S(1)} %pad_add_fusion.place, bf16[768,2560]{1,0:T(8,128)(2,1)} %collective-permute-done.1.a.g_next, bf16[768,2560]{1,0:T(8,128)(2,1)} %collective-permute-done.b.h_next, ...), custom_call_target="tpu_custom_call" | custom-call | flops 2516582400 | bytes 9830400 | tf_op jit(solution)/shard_map/cross_term/pallas_call | solution.py:150
  22.6 1.7 %collective-permute-start.3 = (bf16[4,80,1280]{2,1,0:T(8,128)(2,1)}, bf16[4,80,1280]{2,1,0:T(8,128)(2,1)S(1)}, u32[]{:S(2)}, u32[]{:S(2)}) collective-permute-start(bf16[4,80,1280]{2,1,0:T(8,128)(2,1)} %get-tuple-element.23.after), channel_id=1, source_target_pairs={{0,34},{2,8},{10,40},{8,18},{16,50},{18,24},{26,56},{24,2},{34,64}... | collective-permute-start | bytes 2457608 | tf_op jit(solution)/shard_map/ppermute | solution.py:36
  24.3 2.6 %collective-permute-start.4 = (bf16[4,80,1280]{2,1,0:T(8,128)(2,1)}, bf16[4,80,1280]{2,1,0:T(8,128)(2,1)}, u32[]{:S(2)}, u32[]{:S(2)}) collective-permute-start(bf16[4,80,1280]{2,1,0:T(8,128)(2,1)} %get-tuple-element.28), channel_id=1, source_target_pairs={{0,64},{2,18},{10,74},{8,24},{16,80},{18,2},{26,90},{24,8},{34,98}... | collective-permute-start | bytes 2457608 | tf_op jit(solution)/shard_map/ppermute | solution.py:36
  26.9 1.4 %collective-permute-start.5 = (bf16[4,80,1280]{2,1,0:T(8,128)(2,1)}, bf16[4,80,1280]{2,1,0:T(8,128)(2,1)}, u32[]{:S(2)}, u32[]{:S(2)}) collective-permute-start(bf16[4,80,1280]{2,1,0:T(8,128)(2,1)} %get-tuple-element.29), channel_id=1, source_target_pairs={{0,98},{2,24},{10,104},{8,2},{16,114},{18,8},{26,120},{24,18},{34,... | collective-permute-start | bytes 2457608 | tf_op jit(solution)/shard_map/ppermute | solution.py:36
  28.3 15.9 %factor_term.1 = (bf16[4,160,1280]{2,1,0:T(8,128)(2,1)}, bf16[4,160,1280]{2,1,0:T(8,128)(2,1)}, bf16[2,160,1280]{2,1,0:T(8,128)(2,1)}, bf16[2,160,1280]{2,1,0:T(8,128)(2,1)}, bf16[4,160,1280]{2,1,0:T(8,128)(2,1)}) custom-call(s32[4]{0:T(128)S(1)} %pad_add_fusion.place, bf16[768,2560]{1,0:T(8,128)(2,1)} %h_own.1, bf16[768,2560]{1,0:T(8,128)(2,1)} %g_own.1, ...), custom_call_target="tpu_custom_call" | custom-call | flops 10066329600 | bytes 15728640 | tf_op jit(solution)/shard_map/factor_term/pallas_call | solution.py:213
  44.2 0.4 collective-permute-start.2
  44.6 2.6 %collective-permute-start.10 = (bf16[2,160,1280]{2,1,0:T(8,128)(2,1)}, bf16[2,160,1280]{2,1,0:T(8,128)(2,1)S(1)}, u32[]{:S(2)}, u32[]{:S(2)}) collective-permute-start(bf16[2,160,1280]{2,1,0:T(8,128)(2,1)} %get-tuple-element.34), channel_id=1, source_target_pairs={{0,98},{2,24},{10,104},{8,2},{16,114},{18,8},{26,120},{24,18},{34,... | collective-permute-start | bytes 2457608 | tf_op jit(solution)/shard_map/ppermute | solution.py:36
  47.2 0.0 collective-permute-done.3.refs_1_
  47.2 0.0 collective-permute-done.4.refs_2_
  47.2 0.0 collective-permute-done.5.refs_3_
  47.2 3.6 %fold.2 = (f32[80,1280]{1,0:T(8,128)}, bf16[80,1280]{1,0:T(8,128)(2,1)}, bf16[80,1280]{1,0:T(8,128)(2,1)S(1)}, bf16[80,1280]{1,0:T(8,128)(2,1)S(1)}) custom-call(s32[1]{0:T(128)} %bitcast.1.me, bf16[4,80,1280]{2,1,0:T(8,128)(2,1)} %get-tuple-element.27.refs_0_, bf16[4,80,1280]{2,1,0:T(8,128)(2,1)S(1)} %collective-permute-done.3.refs_1_, ...), custom_call_target="tpu_custom_call" | custom-call | tf_op jit(solution)/shard_map/fold/pallas_call | solution.py:260
  50.8 1.7 %collective-permute-start.6 = (bf16[80,1280]{1,0:T(8,128)(2,1)}, bf16[80,1280]{1,0:T(8,128)(2,1)S(1)}, u32[]{:S(2)}, u32[]{:S(2)}) collective-permute-start(bf16[80,1280]{1,0:T(8,128)(2,1)} %get-tuple-element.30), channel_id=1, source_target_pairs={{0,10},{2,32},{10,16},{8,42},{16,26},{18,48},{26,0},{24,58},{34,40... | collective-permute-start | bytes 614408 | tf_op jit(solution)/shard_map/ppermute | solution.py:36
  52.5 3.3 %collective-permute-start.7 = (bf16[80,1280]{1,0:T(8,128)(2,1)S(1)}, bf16[80,1280]{1,0:T(8,128)(2,1)S(1)}, u32[]{:S(2)}, u32[]{:S(2)}) collective-permute-start(bf16[80,1280]{1,0:T(8,128)(2,1)S(1)} %get-tuple-element.31), channel_id=1, source_target_pairs={{0,16},{2,66},{10,26},{8,72},{16,0},{18,82},{26,10},{24,88},{34,50... | collective-permute-start | bytes 614408 | tf_op jit(solution)/shard_map/ppermute | solution.py:36
  55.8 1.3 %collective-permute-start.8 = (bf16[80,1280]{1,0:T(8,128)(2,1)S(1)}, bf16[80,1280]{1,0:T(8,128)(2,1)S(1)}, u32[]{:S(2)}, u32[]{:S(2)}) collective-permute-start(bf16[80,1280]{1,0:T(8,128)(2,1)S(1)} %get-tuple-element.32), channel_id=1, source_target_pairs={{0,26},{2,96},{10,0},{8,106},{16,10},{18,112},{26,16},{24,122},{34... | collective-permute-start | bytes 614408 | tf_op jit(solution)/shard_map/ppermute | solution.py:36
  57.1 5.0 %collective-permute-done.6.refs_0_.refs_1_ = bf16[80,1280]{1,0:T(8,128)(2,1)S(1)} collective-permute-done((bf16[80,1280]{1,0:T(8,128)(2,1)}, bf16[80,1280]{1,0:T(8,128)(2,1)S(1)}, u32[]{:S(2)}, u32[]{:S(2)}) %collective-permute-start.6) | collective-permute-done | bytes 204832 | tf_op jit(solution)/shard_map/ppermute | solution.py:36
  62.1 1.2 settle.2
  63.3 1.3 %collective-permute-start.12 = (f32[40,1280]{1,0:T(8,128)S(1)}, f32[40,1280]{1,0:T(8,128)S(1)}, u32[]{:S(2)}, u32[]{:S(2)}) collective-permute-start(f32[40,1280]{1,0:T(8,128)S(1)} %get-tuple-element.37), channel_id=1, source_target_pairs={{0,4},{4,0},{1,5},{5,1},{2,6},{6,2},{3,7},{7,3},{8,12},{12,8},{9,1... | collective-permute-start | bytes 614408 | tf_op jit(solution)/shard_map/ppermute | solution.py:24
  64.6 2.5 %collective-permute-start.13 = (f32[40,1280]{1,0:T(8,128)S(1)}, f32[40,1280]{1,0:T(8,128)S(1)}, u32[]{:S(2)}, u32[]{:S(2)}) collective-permute-start(f32[40,1280]{1,0:T(8,128)S(1)} %get-tuple-element.36.mine), channel_id=1, source_target_pairs={{0,1},{1,0},{2,3},{3,2},{4,5},{5,4},{6,7},{7,6},{8,9},{9,8},{10,11... | collective-permute-start | bytes 614408 | tf_op jit(solution)/shard_map/ppermute | solution.py:24
  67.0 0.2 collective-permute-start.14
  67.2 0.0 collective-permute-done.2.received
  67.2 2.0 %grow.2 = bf16[4,160,1280]{2,1,0:T(8,128)(2,1)} custom-call(bf16[4,160,1280]{2,1,0:T(8,128)(2,1)} %get-tuple-element.25.x, bf16[2,160,1280]{2,1,0:T(8,128)(2,1)S(1)} %collective-permute-done.2.received, bf16[80,1280]{1,0:T(8,128)(2,1)S(1)} %collective-permute-done.6.refs_0_.refs_1_, ...), custom_call_target="tpu_custom_call", output_to_operand_aliasing={{}: (0, {})} | custom-call | tf_op jit(solution)/shard_map/grow/pallas_call | solution.py:324
  69.2 2.7 %collective-permute-start.9 = (bf16[4,160,1280]{2,1,0:T(8,128)(2,1)}, bf16[4,160,1280]{2,1,0:T(8,128)(2,1)S(1)}, u32[]{:S(2)}, u32[]{:S(2)}) collective-permute-start(bf16[4,160,1280]{2,1,0:T(8,128)(2,1)} %grow.2), channel_id=1, source_target_pairs={{0,34},{2,8},{10,40},{8,18},{16,50},{18,24},{26,56},{24,2},{34,64}... | collective-permute-start | bytes 4915208 | tf_op jit(solution)/shard_map/ppermute | solution.py:36
  71.9 2.0 %grow.3 = bf16[4,160,1280]{2,1,0:T(8,128)(2,1)} custom-call(bf16[4,160,1280]{2,1,0:T(8,128)(2,1)} %get-tuple-element.33.x, bf16[2,160,1280]{2,1,0:T(8,128)(2,1)S(1)} %collective-permute-done.10.received, bf16[80,1280]{1,0:T(8,128)(2,1)S(1)} %collective-permute-done.6.refs_0_.refs_1_, ...), custom_call_target="tpu_custom_call", output_to_operand_aliasing={{}: (0, {})} | custom-call | tf_op jit(solution)/shard_map/grow/pallas_call | solution.py:324
  73.9 1.5 %collective-permute-start.11 = (bf16[4,160,1280]{2,1,0:T(8,128)(2,1)}, bf16[4,160,1280]{2,1,0:T(8,128)(2,1)}, u32[]{:S(2)}, u32[]{:S(2)}) collective-permute-start(bf16[4,160,1280]{2,1,0:T(8,128)(2,1)} %grow.3), channel_id=1, source_target_pairs={{0,98},{2,24},{10,104},{8,2},{16,114},{18,8},{26,120},{24,18},{34,... | collective-permute-start | bytes 4915208 | tf_op jit(solution)/shard_map/ppermute | solution.py:36
  75.5 0.8 collective-permute-done.13.partner
  76.2 2.3 %collective-permute-done.14.partner_other = f32[40,1280]{1,0:T(8,128)S(1)} collective-permute-done((f32[40,1280]{1,0:T(8,128)S(1)}, f32[40,1280]{1,0:T(8,128)S(1)}, u32[]{:S(2)}, u32[]{:S(2)}) %collective-permute-start.14) | collective-permute-done | bytes 204832 | tf_op jit(solution)/shard_map/ppermute | solution.py:495
  78.5 5.0 %left_product.1.refs_3_ = bf16[128,16,128]{2,1,0:T(8,128)(2,1)} custom-call(s32[4]{0:T(128)S(1)} %pad_add_fusion.place, f32[40,1280]{1,0:T(8,128)S(1)} %get-tuple-element.36.mine, f32[40,1280]{1,0:T(8,128)S(1)} %collective-permute-done.12.other, f32[40,1280]{1,0:T(8,128)S(1)} %collective-permute-done.13.partner, ...), custom_call_target="tpu_custom_call" | custom-call | flops 16777216000 | bytes 6553600 | tf_op jit(solution)/shard_map/left_product/pallas_call | solution.py:389
  83.5 8.3 %all-to-all-start = ((bf16[128,16,128]{2,1,0:T(8,128)(2,1)}), bf16[128,16,128]{2,1,0:T(8,128)(2,1)S(1)}, u32[]{:S(2)}, u32[]{:S(2)}) async-start(bf16[128,16,128]{2,1,0:T(8,128)(2,1)} %left_product.1.refs_3_), calls=%async_computation | async-start | bytes 1048576 | tf_op jit(solution)/shard_map/all_to_all | solution.py:499
  91.8 0.5 collective-permute-done.9.refs_1_
  92.3 4.0 %collective-permute-done.11.refs_2_ = bf16[4,160,1280]{2,1,0:T(8,128)(2,1)} collective-permute-done((bf16[4,160,1280]{2,1,0:T(8,128)(2,1)}, bf16[4,160,1280]{2,1,0:T(8,128)(2,1)}, u32[]{:S(2)}, u32[]{:S(2)}) %collective-permute-start.11) | collective-permute-done | bytes 1638432 | tf_op jit(solution)/shard_map/ppermute | solution.py:36
  96.3 4.3 %fold.3 = (f32[160,1280]{1,0:T(8,128)}, bf16[160,1280]{1,0:T(8,128)(2,1)S(1)}, bf16[160,1280]{1,0:T(8,128)(2,1)S(1)}, bf16[160,1280]{1,0:T(8,128)(2,1)S(1)}) custom-call(s32[1]{0:T(128)} %bitcast.1.me, bf16[4,160,1280]{2,1,0:T(8,128)(2,1)} %get-tuple-element.24.refs_4_.refs_0_, bf16[4,160,1280]{2,1,0:T(8,128)(2,1)S(1)} %collective-permute-done.9.refs_1_, ...), custom_call_target="tpu_custom_call" | custom-call | tf_op jit(solution)/shard_map/fold/pallas_call | solution.py:260
  100.6 0.3 collective-permute-start.15
  100.9 6.5 %collective-permute-start.16 = (bf16[160,1280]{1,0:T(8,128)(2,1)S(1)}, bf16[160,1280]{1,0:T(8,128)(2,1)S(1)}, u32[]{:S(2)}, u32[]{:S(2)}) collective-permute-start(bf16[160,1280]{1,0:T(8,128)(2,1)S(1)} %get-tuple-element.40), channel_id=1, source_target_pairs={{0,16},{2,66},{10,26},{8,72},{16,0},{18,82},{26,10},{24,88},{34,50... | collective-permute-start | bytes 1228808 | tf_op jit(solution)/shard_map/ppermute | solution.py:36
  107.4 4.7 %right_product.1.refs_4_ = f32[40,1280]{1,0:T(8,128)} custom-call(s32[4]{0:T(128)S(1)} %pad_add_fusion.place, bf16[128,16,128]{2,1,0:T(8,128)(2,1)S(1)} %all-to-all-done.blocks, bf16[2560,1280]{1,0:T(8,128)(2,1)} %right.1, bf16[160,1280]{1,0:T(8,128)(2,1)S(1)} %get-tuple-element.39.late), custom_call_target="tpu_custom_call" | custom-call | flops 41943040000 | bytes 6553600 | tf_op jit(solution)/shard_map/right_product/pallas_call | solution.py:434
  112.2 5.0 %collective-permute-done.16.refs_2_ = bf16[160,1280]{1,0:T(8,128)(2,1)S(1)} collective-permute-done((bf16[160,1280]{1,0:T(8,128)(2,1)S(1)}, bf16[160,1280]{1,0:T(8,128)(2,1)S(1)}, u32[]{:S(2)}, u32[]{:S(2)}) %collective-permute-start.16) | collective-permute-done | bytes 409632 | tf_op jit(solution)/shard_map/ppermute | solution.py:36
  117.2 0.1 collective-permute-done.17.refs_3_
  117.3 1.5 %settle.3 = (f32[80,1280]{1,0:T(8,128)S(1)}, bf16[80,1280]{1,0:T(8,128)(2,1)S(1)}) custom-call(s32[1]{0:T(128)} %bitcast.xl, f32[160,1280]{1,0:T(8,128)} %get-tuple-element.38.refs_0_, bf16[160,1280]{1,0:T(8,128)(2,1)S(1)} %collective-permute-done.15.refs_1_, bf16[160,1280]{1,0:T(8,128)(2,1)S(1)} %collective-permute-done.16.refs_2_, ...), custom_call_target="tpu_custom_call" | custom-call | tf_op jit(solution)/shard_map/settle/pallas_call | solution.py:294
  118.7 0.4 collective-permute-start.18
  119.1 6.1 %collective-permute-done.18 = bf16[80,1280]{1,0:T(8,128)(2,1)S(1)} collective-permute-done((bf16[80,1280]{1,0:T(8,128)(2,1)S(1)}, bf16[80,1280]{1,0:T(8,128)(2,1)S(1)}, u32[]{:S(2)}, u32[]{:S(2)}) %collective-permute-start.18) | collective-permute-done | bytes 204832 | tf_op jit(solution)/shard_map/ppermute | solution.py:24
  125.3 1.2 collective-permute-start.19
  126.5 1.1 collective-permute-done.19
  127.6 0.8 maximum_bitcast_fusion
  (10 shorter events, 0.1 us)
Async XLA Ops:
  0.6 8.3 %collective-permute-start = (bf16[768,2560]{1,0:T(8,128)(2,1)}, bf16[768,2560]{1,0:T(8,128)(2,1)}, u32[]{:S(2)}, u32[]{:S(2)}) collective-permute-start(bf16[768,2560]{1,0:T(8,128)(2,1)} %h_own.1), channel_id=1, source_target_pairs={{0,2},{2,0},{1,3},{3,1},{4,6},{6,4},{5,7},{7,5},{8,10},{10,8},{9,1... | collective-permute-start | bytes 11796488 | tf_op jit(solution)/shard_map/ppermute | solution.py:24
  2.1 12.4 %collective-permute-start.1 = (bf16[768,2560]{1,0:T(8,128)(2,1)}, bf16[768,2560]{1,0:T(8,128)(2,1)}, u32[]{:S(2)}, u32[]{:S(2)}) collective-permute-start(bf16[768,2560]{1,0:T(8,128)(2,1)} %g_own.1), channel_id=1, source_target_pairs={{0,2},{2,0},{1,3},{3,1},{4,6},{6,4},{5,7},{7,5},{8,10},{10,8},{9,1... | collective-permute-start | bytes 11796488 | tf_op jit(solution)/shard_map/ppermute | solution.py:24
  22.6 24.6 %collective-permute-start.3 = (bf16[4,80,1280]{2,1,0:T(8,128)(2,1)}, bf16[4,80,1280]{2,1,0:T(8,128)(2,1)S(1)}, u32[]{:S(2)}, u32[]{:S(2)}) collective-permute-start(bf16[4,80,1280]{2,1,0:T(8,128)(2,1)} %get-tuple-element.23.after), channel_id=1, source_target_pairs={{0,34},{2,8},{10,40},{8,18},{16,50},{18,24},{26,56},{24,2},{34,64}... | collective-permute-start | bytes 2457608 | tf_op jit(solution)/shard_map/ppermute | solution.py:36
  24.3 22.9 %collective-permute-start.4 = (bf16[4,80,1280]{2,1,0:T(8,128)(2,1)}, bf16[4,80,1280]{2,1,0:T(8,128)(2,1)}, u32[]{:S(2)}, u32[]{:S(2)}) collective-permute-start(bf16[4,80,1280]{2,1,0:T(8,128)(2,1)} %get-tuple-element.28), channel_id=1, source_target_pairs={{0,64},{2,18},{10,74},{8,24},{16,80},{18,2},{26,90},{24,8},{34,98}... | collective-permute-start | bytes 2457608 | tf_op jit(solution)/shard_map/ppermute | solution.py:36
  26.9 20.3 %collective-permute-start.5 = (bf16[4,80,1280]{2,1,0:T(8,128)(2,1)}, bf16[4,80,1280]{2,1,0:T(8,128)(2,1)}, u32[]{:S(2)}, u32[]{:S(2)}) collective-permute-start(bf16[4,80,1280]{2,1,0:T(8,128)(2,1)} %get-tuple-element.29), channel_id=1, source_target_pairs={{0,98},{2,24},{10,104},{8,2},{16,114},{18,8},{26,120},{24,18},{34,... | collective-permute-start | bytes 2457608 | tf_op jit(solution)/shard_map/ppermute | solution.py:36
  44.2 23.0 %collective-permute-start.2 = (bf16[2,160,1280]{2,1,0:T(8,128)(2,1)}, bf16[2,160,1280]{2,1,0:T(8,128)(2,1)S(1)}, u32[]{:S(2)}, u32[]{:S(2)}) collective-permute-start(bf16[2,160,1280]{2,1,0:T(8,128)(2,1)} %get-tuple-element.26), channel_id=1, source_target_pairs={{0,34},{2,8},{10,40},{8,18},{16,50},{18,24},{26,56},{24,2},{34,64}... | collective-permute-start | bytes 2457608 | tf_op jit(solution)/shard_map/ppermute | solution.py:36
  44.6 27.3 %collective-permute-start.10 = (bf16[2,160,1280]{2,1,0:T(8,128)(2,1)}, bf16[2,160,1280]{2,1,0:T(8,128)(2,1)S(1)}, u32[]{:S(2)}, u32[]{:S(2)}) collective-permute-start(bf16[2,160,1280]{2,1,0:T(8,128)(2,1)} %get-tuple-element.34), channel_id=1, source_target_pairs={{0,98},{2,24},{10,104},{8,2},{16,114},{18,8},{26,120},{24,18},{34,... | collective-permute-start | bytes 2457608 | tf_op jit(solution)/shard_map/ppermute | solution.py:36
  50.8 11.3 %collective-permute-start.6 = (bf16[80,1280]{1,0:T(8,128)(2,1)}, bf16[80,1280]{1,0:T(8,128)(2,1)S(1)}, u32[]{:S(2)}, u32[]{:S(2)}) collective-permute-start(bf16[80,1280]{1,0:T(8,128)(2,1)} %get-tuple-element.30), channel_id=1, source_target_pairs={{0,10},{2,32},{10,16},{8,42},{16,26},{18,48},{26,0},{24,58},{34,40... | collective-permute-start | bytes 614408 | tf_op jit(solution)/shard_map/ppermute | solution.py:36
  52.5 9.6 %collective-permute-start.7 = (bf16[80,1280]{1,0:T(8,128)(2,1)S(1)}, bf16[80,1280]{1,0:T(8,128)(2,1)S(1)}, u32[]{:S(2)}, u32[]{:S(2)}) collective-permute-start(bf16[80,1280]{1,0:T(8,128)(2,1)S(1)} %get-tuple-element.31), channel_id=1, source_target_pairs={{0,16},{2,66},{10,26},{8,72},{16,0},{18,82},{26,10},{24,88},{34,50... | collective-permute-start | bytes 614408 | tf_op jit(solution)/shard_map/ppermute | solution.py:36
  55.8 6.3 %collective-permute-start.8 = (bf16[80,1280]{1,0:T(8,128)(2,1)S(1)}, bf16[80,1280]{1,0:T(8,128)(2,1)S(1)}, u32[]{:S(2)}, u32[]{:S(2)}) collective-permute-start(bf16[80,1280]{1,0:T(8,128)(2,1)S(1)} %get-tuple-element.32), channel_id=1, source_target_pairs={{0,26},{2,96},{10,0},{8,106},{16,10},{18,112},{26,16},{24,122},{34... | collective-permute-start | bytes 614408 | tf_op jit(solution)/shard_map/ppermute | solution.py:36
  63.3 12.2 %collective-permute-start.12 = (f32[40,1280]{1,0:T(8,128)S(1)}, f32[40,1280]{1,0:T(8,128)S(1)}, u32[]{:S(2)}, u32[]{:S(2)}) collective-permute-start(f32[40,1280]{1,0:T(8,128)S(1)} %get-tuple-element.37), channel_id=1, source_target_pairs={{0,4},{4,0},{1,5},{5,1},{2,6},{6,2},{3,7},{7,3},{8,12},{12,8},{9,1... | collective-permute-start | bytes 614408 | tf_op jit(solution)/shard_map/ppermute | solution.py:24
  64.6 11.7 %collective-permute-start.13 = (f32[40,1280]{1,0:T(8,128)S(1)}, f32[40,1280]{1,0:T(8,128)S(1)}, u32[]{:S(2)}, u32[]{:S(2)}) collective-permute-start(f32[40,1280]{1,0:T(8,128)S(1)} %get-tuple-element.36.mine), channel_id=1, source_target_pairs={{0,1},{1,0},{2,3},{3,2},{4,5},{5,4},{6,7},{7,6},{8,9},{9,8},{10,11... | collective-permute-start | bytes 614408 | tf_op jit(solution)/shard_map/ppermute | solution.py:24
  67.0 11.5 %collective-permute-start.14 = (f32[40,1280]{1,0:T(8,128)S(1)}, f32[40,1280]{1,0:T(8,128)S(1)}, u32[]{:S(2)}, u32[]{:S(2)}) collective-permute-start(f32[40,1280]{1,0:T(8,128)S(1)} %get-tuple-element.37), channel_id=1, source_target_pairs={{0,5},{1,4},{4,1},{5,0},{2,7},{3,6},{6,3},{7,2},{8,13},{9,12},{12,... | collective-permute-start | bytes 614408 | tf_op jit(solution)/shard_map/ppermute | solution.py:495
  69.2 23.1 %collective-permute-start.9 = (bf16[4,160,1280]{2,1,0:T(8,128)(2,1)}, bf16[4,160,1280]{2,1,0:T(8,128)(2,1)S(1)}, u32[]{:S(2)}, u32[]{:S(2)}) collective-permute-start(bf16[4,160,1280]{2,1,0:T(8,128)(2,1)} %grow.2), channel_id=1, source_target_pairs={{0,34},{2,8},{10,40},{8,18},{16,50},{18,24},{26,56},{24,2},{34,64}... | collective-permute-start | bytes 4915208 | tf_op jit(solution)/shard_map/ppermute | solution.py:36
  73.9 22.4 %collective-permute-start.11 = (bf16[4,160,1280]{2,1,0:T(8,128)(2,1)}, bf16[4,160,1280]{2,1,0:T(8,128)(2,1)}, u32[]{:S(2)}, u32[]{:S(2)}) collective-permute-start(bf16[4,160,1280]{2,1,0:T(8,128)(2,1)} %grow.3), channel_id=1, source_target_pairs={{0,98},{2,24},{10,104},{8,2},{16,114},{18,8},{26,120},{24,18},{34,... | collective-permute-start | bytes 4915208 | tf_op jit(solution)/shard_map/ppermute | solution.py:36
  83.5 23.9 %all-to-all-start = ((bf16[128,16,128]{2,1,0:T(8,128)(2,1)}), bf16[128,16,128]{2,1,0:T(8,128)(2,1)S(1)}, u32[]{:S(2)}, u32[]{:S(2)}) async-start(bf16[128,16,128]{2,1,0:T(8,128)(2,1)} %left_product.1.refs_3_), calls=%async_computation | async-start | bytes 1048576 | tf_op jit(solution)/shard_map/all_to_all | solution.py:499
  100.6 11.5 %collective-permute-start.15 = (bf16[160,1280]{1,0:T(8,128)(2,1)S(1)}, bf16[160,1280]{1,0:T(8,128)(2,1)S(1)}, u32[]{:S(2)}, u32[]{:S(2)}) collective-permute-start(bf16[160,1280]{1,0:T(8,128)(2,1)S(1)} %get-tuple-element.39.late), channel_id=1, source_target_pairs={{0,10},{2,32},{10,16},{8,42},{16,26},{18,48},{26,0},{24,58},{34,40... | collective-permute-start | bytes 1228808 | tf_op jit(solution)/shard_map/ppermute | solution.py:36
  100.9 16.2 %collective-permute-start.16 = (bf16[160,1280]{1,0:T(8,128)(2,1)S(1)}, bf16[160,1280]{1,0:T(8,128)(2,1)S(1)}, u32[]{:S(2)}, u32[]{:S(2)}) collective-permute-start(bf16[160,1280]{1,0:T(8,128)(2,1)S(1)} %get-tuple-element.40), channel_id=1, source_target_pairs={{0,16},{2,66},{10,26},{8,72},{16,0},{18,82},{26,10},{24,88},{34,50... | collective-permute-start | bytes 1228808 | tf_op jit(solution)/shard_map/ppermute | solution.py:36
  107.4 9.8 %collective-permute-start.17 = (bf16[160,1280]{1,0:T(8,128)(2,1)S(1)}, bf16[160,1280]{1,0:T(8,128)(2,1)S(1)}, u32[]{:S(2)}, u32[]{:S(2)}) collective-permute-start(bf16[160,1280]{1,0:T(8,128)(2,1)S(1)} %get-tuple-element.41), channel_id=1, source_target_pairs={{0,26},{2,96},{10,0},{8,106},{16,10},{18,112},{26,16},{24,122},{34... | collective-permute-start | bytes 1228808 | tf_op jit(solution)/shard_map/ppermute | solution.py:36
  118.7 6.5 %collective-permute-start.18 = (bf16[80,1280]{1,0:T(8,128)(2,1)S(1)}, bf16[80,1280]{1,0:T(8,128)(2,1)S(1)}, u32[]{:S(2)}, u32[]{:S(2)}) collective-permute-start(bf16[80,1280]{1,0:T(8,128)(2,1)S(1)} %get-tuple-element.43), channel_id=1, source_target_pairs={{0,4},{4,0},{1,5},{5,1},{2,6},{6,2},{3,7},{7,3},{8,12},{12,8},{9,1... | collective-permute-start | bytes 614408 | tf_op jit(solution)/shard_map/ppermute | solution.py:24
  125.3 2.2 %collective-permute-start.19 = (f32[40,1280]{1,0:T(8,128)S(1)}, f32[40,1280]{1,0:T(8,128)S(1)}, u32[]{:S(2)}, u32[]{:S(2)}) collective-permute-start(f32[40,1280]{1,0:T(8,128)S(1)} %dynamic-slice_bitcast_fusion), channel_id=1, source_target_pairs={{0,2},{2,0},{1,3},{3,1},{4,6},{6,4},{5,7},{7,5},{8,10},{10,8},{9,1... | collective-permute-start | bytes 614408 | tf_op jit(solution)/shard_map/ppermute | solution.py:24

commit v14 on v12

--- a/solution.py
+++ b/solution.py
@@ -104,7 +104,9 @@
     out[...] = contract(lhs[m], rhs[...])
 
 
-def cross_kernel(place, a, b, partial, own, ahead1, ahead2, ahead3, held, buffer, held_sems, sem):
+def cross_kernel(place, a, b, partial, after, *rest):
+    del after
+    own, ahead1, ahead2, ahead3, held, buffer, held_sems, sem = rest
     m = pl.program_id(0)
 
     @pl.when(m == 0)
@@ -143,7 +145,7 @@
     )(place, grads, acts)
 
 
-def cross_term(place, grads_next, acts_next, partial):
+def cross_term(place, grads_next, acts_next, partial, after):
     tokens, half = grads_next.shape[0], grads_next.shape[1] // 2
     out = pltpu.HBM((4, half // 16, half), BF)
     return pl.pallas_call(
@@ -155,6 +157,7 @@
             in_specs=[
                 pl.BlockSpec((tokens, TILE), lambda m, p: (0, p[1] * 2 + m)),
                 pl.BlockSpec((tokens, half), lambda m, p: (0, p[1] ^ p[0])),
+                ANY,
                 ANY,
             ],
             out_specs=[pl.BlockSpec(memory_space=pltpu.HBM)] * 4,
@@ -168,41 +171,85 @@
         compiler_params=pltpu.CompilerParams(vmem_limit_bytes=28 * 2**20),
         cost_estimate=NO_COST,
         name="cross_term",
-    )(place, grads_next, acts_next, partial)
-
-
-def factor_kernel(place, h_own, g_own, h_next, g_next, after, *rest):
+    )(place, grads_next, acts_next, partial, after)
+
+
+def factor_fetch(place, refs, step, lhs, rhs, lhs_sems, rhs_sem):
+    half = rhs.shape[1]
+    at = pl.ds(pl.multiple_of(step * TILE, TILE), TILE)
+    columns = pl.ds(pl.multiple_of(place[1] * half, half), half)
+    for owner, ref in enumerate(refs):
+
+        @pl.when(place[0] == owner)
+        def _():
+            slot = step & 1
+            pltpu.make_async_copy(ref.at[:, at], lhs.at[slot], lhs_sems.at[slot]).start()
+            if isinstance(step, int):
+                pltpu.make_async_copy(ref.at[:, columns], rhs, rhs_sem).start()
+
+
+def factor_tile(place, refs, lhs, rhs, lhs_sems, rhs_sem):
+    m = pl.program_id(0)
+    pl.when(m == 0)(lambda: factor_fetch(place, refs, 0, lhs, rhs, lhs_sems, rhs_sem))
+    pl.when(m < 3)(lambda: factor_fetch(place, refs, m + 1, lhs, rhs, lhs_sems, rhs_sem))
+    wait_all(lhs.at[m & 1], lhs_sems.at[m & 1])
+    pl.when(m == 0)(lambda: wait_all(rhs, rhs_sem))
+    return contract(lhs[m & 1], rhs[...])
+
+
+def factor_own_kernel(place, acts, grads, after, out, *scratch):
     del after
-    own, right, far_a, far_b, left, lhs, rhs, buffer, lhs_sems, rhs_sem, sem = rest
+    out[...] = factor_tile(place, (acts, grads), *scratch)
+
+
+def factor_scratch(tokens, half):
+    return [
+        pltpu.VMEM((2, tokens, TILE), BF),
+        pltpu.VMEM((tokens, half), BF),
+        pltpu.SemaphoreType.DMA((2,)),
+        pltpu.SemaphoreType.DMA,
+    ]
+
+
+def factor_own(place, acts, grads, after):
+    tokens, width = acts.shape
+    half = width // 2
+    return pl.pallas_call(
+        factor_own_kernel,
+        out_shape=pltpu.HBM((width, half), F32),
+        grid_spec=pltpu.PrefetchScalarGridSpec(
+            num_scalar_prefetch=1,
+            grid=(4,),
+            in_specs=[pl.BlockSpec(memory_space=pltpu.HBM)] * 2 + [ANY],
+            out_specs=pl.BlockSpec((TILE, half), lambda m, p: (m, 0)),
+            scratch_shapes=factor_scratch(tokens, half),
+        ),
+        compiler_params=pltpu.CompilerParams(vmem_limit_bytes=24 * 2**20),
+        cost_estimate=NO_COST,
+        name="factor_own",
+    )(place, acts, grads, after)
+
+
+def factor_kernel(place, acts, grads, partial, after, *rest):
+    del after
+    own, right, far_a, far_b, left, held, buffer, held_sems, sem = rest[:9]
     m = pl.program_id(0)
-    half = rhs.shape[2]
-
-    def fetch(step, with_rhs):
-        slot = step & 1
-        at = pl.ds(pl.multiple_of(step * TILE, TILE), TILE)
-        columns = pl.ds(pl.multiple_of(place[1] * half, half), half)
-        for owner, refs in enumerate(((h_own, h_next), (g_own, g_next))):
-
-            @pl.when(place[0] == owner)
-            def _():
-                for k, ref in enumerate(refs):
-                    pltpu.make_async_copy(ref.at[:, at], lhs.at[slot, k], lhs_sems.at[slot]).start()
-                    if with_rhs:
-                        pltpu.make_async_copy(ref.at[:, columns], rhs.at[k], rhs_sem).start()
-
-    pl.when(m == 0)(lambda: fetch(0, True))
-    pl.when(m < 3)(lambda: fetch(m + 1, False))
-    slot = m & 1
-    wait_all(lhs.at[slot], lhs_sems.at[slot])
-    pl.when(m == 0)(lambda: wait_all(rhs, rhs_sem))
-
-    buffer[m] = (contract(lhs[slot, 0], rhs[0]) + contract(lhs[slot, 1], rhs[1])).astype(BF)
+
+    def fetch_partial(step):
+        rows = partial.at[pl.ds(pl.multiple_of(step * TILE, TILE), TILE)]
+        pltpu.make_async_copy(rows, held.at[step & 1], held_sems.at[step & 1]).start()
+
+    pl.when(m == 0)(lambda: fetch_partial(0))
+    pl.when(m < 3)(lambda: fetch_partial(m + 1))
+    tile = factor_tile(place, (acts, grads), *rest[9:])
+    wait_all(held.at[m & 1], held_sems.at[m & 1])
+    buffer[m] = (held[m & 1] + tile).astype(BF)
     place_tile(place, buffer, sem, [own, right, (far_a, far_b), left], m, 1)
     pl.when(m == 3)(lambda: wait_all(buffer, sem))
 
 
-def factor_term(place, acts, grads, acts_next, grads_next, after):
-    tokens, width = acts.shape
+def factor_term(place, acts_next, grads_next, partial, after):
+    tokens, width = acts_next.shape
     half = width // 2
     hbm = pl.BlockSpec(memory_space=pltpu.HBM)
     out = pltpu.HBM((4, width // 16, half), BF)
@@ -213,21 +260,20 @@
         grid_spec=pltpu.PrefetchScalarGridSpec(
             num_scalar_prefetch=1,
             grid=(4,),
-            in_specs=[hbm] * 2 + [ANY] * 3,
+            in_specs=[hbm] * 4,
             out_specs=[hbm] * 5,
             scratch_shapes=[
-                pltpu.VMEM((2, 2, tokens, TILE), BF),
-                pltpu.VMEM((2, tokens, half), BF),
+                pltpu.VMEM((2, TILE, half), F32),
                 pltpu.VMEM((4, TILE, half), BF),
                 pltpu.SemaphoreType.DMA((2,)),
                 pltpu.SemaphoreType.DMA,
-                pltpu.SemaphoreType.DMA,
-            ],
+            ]
+            + factor_scratch(tokens, half),
         ),
         compiler_params=pltpu.CompilerParams(vmem_limit_bytes=30 * 2**20),
         cost_estimate=NO_COST,
         name="factor_term",
-    )(place, acts, grads, acts_next, grads_next, after)
+    )(place, acts_next, grads_next, partial, after)
 
 
 def add(first, *rest):
@@ -254,7 +300,8 @@
     whole = pl.BlockSpec((rows, width), lambda s, m: (0, 0))
     return pl.pallas_call(
         functools.partial(fold_kernel, len(parts)),
-        out_shape=[jax.ShapeDtypeStruct((rows, width), t) for t in (F32, BF, BF, BF)],
+        out_shape=[pltpu.HBM((rows, width), F32)]
+        + [jax.ShapeDtypeStruct((rows, width), BF)] * 3,
         grid_spec=pltpu.PrefetchScalarGridSpec(
             num_scalar_prefetch=1,
             grid=(1,),
@@ -461,12 +508,15 @@
 
     grads_next, acts_next = in_hbm(shift(out_grad, "c", 1)), in_hbm(shift(hidden, "c", 1))
     partial = cross_own(place, out_grad, hidden)
-
-    own, m1, m2, m3 = cross_term(place, grads_next, acts_next, partial)
+    factor_partial = factor_own(place, hidden, out_grad, partial)
+
+    own, m1, m2, m3 = cross_term(
+        place, grads_next, acts_next, partial, in_hbm(factor_partial)
+    )
     m_parts = [own, turn(m1, 1, 0), turn(m2, 2, 0), turn(m3, 3, 0)]
 
     f_own, right, far_a, far_b, left = factor_term(
-        place, hidden, out_grad, acts_next, grads_next, in_hbm(m1)
+        place, acts_next, grads_next, in_hbm(factor_partial), in_hbm(m1)
     )
     from_left, from_right = turn(far_a, 1, 0), turn(far_b, -1, 0)
 
@@ -481,15 +531,15 @@
     left = grow(left, from_right, 1, m_received[1], m_received[2])
     f_parts = [f_own, turn(right, 1, 0), turn(left, -1, 0)]
 
-    mine, theirs = settle(my_xl, [m, *m_received], F32)
+    mine, theirs = settle(my_xl, [in_hbm(m), *m_received], F32)
     across = lax.ppermute(theirs, ("xl", "o"), [(i, 3 - i) for i in range(4)])
     products = left_product(
         place, mine, shift(theirs, "xl", 1), shift(mine, "o", 1), across, left_inverse
     )
     blocks = lax.all_to_all(products, ("o", "c", "z", "y", "xl"), 0, 0, tiled=True)
     f, *f_pieces = fold(second_me, f_parts, products)
-    f_mine, f_theirs = settle(my_xl, [f, *second_sends(f_pieces)], BF, blocks)
     update = right_product(place, blocks, right_inverse, f_pieces[0])
+    f_mine, f_theirs = settle(my_xl, [in_hbm(f), *second_sends(f_pieces)], BF, in_hbm(update))
 
     f = add(f_mine, shift(f_theirs, "xl", 1))
     f = f * jnp.where(first, 1.0 / token_total, 1.0).astype(F32)

time: 133 us -> 130 us (0.977)
  waiting for transfers between devices: 41.8 us -> 30.5 us
  Pallas kernels: 51.5 us -> 60.8 us
    pallas_call x2 -> x3, Pallas kernels: 5.74 us -> 17.4 us  [the longest x1 10.9 us: factor_own(): pl.pallas_call(factor_own_kernel, out_shape=pltpu.HBM((width, half), F32)...]
    ppermute x6, waiting for transfers between devices: 21.9 us -> 16.3 us  [shift(): return lax.ppermute(x, axis, [(i, (i + step) % size) for i in range(size)])]
    ppermute x13, waiting for transfers between devices: 13.9 us -> 8.65 us  [turn(): return lax.ppermute(x, ('z', 'y', 'c'), pairs)]
    pallas_call x1, Pallas kernels: 15.9 us -> 12 us  [factor_term(): pl.pallas_call(factor_kernel, out_shape=[out, out, side, side, out], grid...]
    pallas_call x2, Pallas kernels: 1.17 us -> 2.62 us  [settle(): pl.pallas_call(functools.partial(settle_kernel, len(parts)), out_shape=[j...]
  transfers between devices with their start and end apart: 21 -> 21, of which waited for: 10 -> 11; matrix products, arithmetic and copies ran while one was open for 0% -> 0% of each run, Pallas kernels for 32% -> 39%
where the time goes in v14:
time: 130 us
  Pallas kernels  60.8 us (47%)
  starting transfers between devices  36.9 us (28%)
  waiting for transfers between devices  30.5 us (23%)
    ppermute x13, starting transfers between devices, turn(): return lax.ppermute(x, ('z', 'y', 'c'), pairs)  24.1 us
    ppermute x6, waiting for transfers between devices, shift(): return lax.ppermute(x, axis, [(i, (i + step) % size) for i in range(size)])  16.3 us
    pallas_call x1, Pallas kernels, factor_term(): pl.pallas_call(factor_kernel, out_shape=[out, out, side, side, out], grid...  12 us
    pallas_call x1, Pallas kernels, factor_own(): pl.pallas_call(factor_own_kernel, out_shape=pltpu.HBM((width, half), F32)...  10.9 us
    ppermute x13, waiting for transfers between devices, turn(): return lax.ppermute(x, ('z', 'y', 'c'), pairs)  8.65 us
    pallas_call x1, Pallas kernels, cross_term(): pl.pallas_call(cross_kernel, out_shape=[out] * 4, grid_spec=pltpu.Prefetc...  8.33 us
    pallas_call x2, Pallas kernels, fold(): pl.pallas_call(functools.partial(fold_kernel, len(parts)), out_shape=[plt...  6.48 us
    all_to_all x1, starting transfers between devices, per_device(): lax.all_to_all(products, ('o', 'c', 'z', 'y', 'xl'), 0, 0, tiled=True)  6.32 us
  transfers between devices with their start and end apart: 21, of which 11 were waited for; matrix products, arithmetic and copies ran while one was open for 0% of the time, Pallas kernels for 39%

profile of v14, /device:TPU:1, one launch (start us, length us, event | category | flops | bytes accessed | tf_op | source)
XLA Modules:
  0.0 129.9 jit_solution(1754520510046329820)
XLA Ops:
  0.6 1.5 %collective-permute-start = (bf16[768,2560]{1,0:T(8,128)(2,1)}, bf16[768,2560]{1,0:T(8,128)(2,1)}, u32[]{:S(2)}, u32[]{:S(2)}) collective-permute-start(bf16[768,2560]{1,0:T(8,128)(2,1)} %acts.1), channel_id=1, source_target_pairs={{0,2},{2,0},{1,3},{3,1},{4,6},{6,4},{5,7},{7,5},{8,10},{10,8},{9,1... | collective-permute-start | bytes 11796488 | tf_op jit(solution)/shard_map/ppermute | solution.py:25
  2.1 0.1 collective-permute-start.1
  2.2 0.1 pad_add_fusion.place
  2.3 5.4 %cross_own.1.after.partial = f32[1280,1280]{1,0:T(8,128)S(1)} custom-call(s32[4]{0:T(128)S(1)} %pad_add_fusion.place, bf16[768,2560]{1,0:T(8,128)(2,1)} %grads.1, bf16[768,2560]{1,0:T(8,128)(2,1)} %acts.1), custom_call_target="tpu_custom_call" | custom-call | tf_op jit(solution)/shard_map/cross_own/pallas_call | solution.py:127
  7.7 10.9 %factor_own.1.after.partial = f32[2560,1280]{1,0:T(8,128)} custom-call(s32[4]{0:T(128)S(1)} %pad_add_fusion.place, bf16[768,2560]{1,0:T(8,128)(2,1)} %acts.1, bf16[768,2560]{1,0:T(8,128)(2,1)} %grads.1, f32[1280,1280]{1,0:T(8,128)S(1)} %cross_own.1.after.partial), custom_call_target="tpu_custom_call" | custom-call | tf_op jit(solution)/shard_map/factor_own/pallas_call | solution.py:217
  18.7 8.3 %cross_term.1 = (bf16[4,80,1280]{2,1,0:T(8,128)(2,1)}, bf16[4,80,1280]{2,1,0:T(8,128)(2,1)}, bf16[4,80,1280]{2,1,0:T(8,128)(2,1)}, bf16[4,80,1280]{2,1,0:T(8,128)(2,1)}) custom-call(s32[4]{0:T(128)S(1)} %pad_add_fusion.place, bf16[768,2560]{1,0:T(8,128)(2,1)} %collective-permute-done.1.a.grads, bf16[768,2560]{1,0:T(8,128)(2,1)} %collective-permute-done.b.acts, ...), custom_call_target="tpu_custom_call" | custom-call | tf_op jit(solution)/shard_map/cross_term/pallas_call | solution.py:151
  27.0 1.7 %collective-permute-start.3 = (bf16[4,80,1280]{2,1,0:T(8,128)(2,1)}, bf16[4,80,1280]{2,1,0:T(8,128)(2,1)S(1)}, u32[]{:S(2)}, u32[]{:S(2)}) collective-permute-start(bf16[4,80,1280]{2,1,0:T(8,128)(2,1)} %get-tuple-element.23.after), channel_id=1, source_target_pairs={{0,34},{2,8},{10,40},{8,18},{16,50},{18,24},{26,56},{24,2},{34,64}... | collective-permute-start | bytes 2457608 | tf_op jit(solution)/shard_map/ppermute | solution.py:37
  28.7 2.6 %collective-permute-start.4 = (bf16[4,80,1280]{2,1,0:T(8,128)(2,1)}, bf16[4,80,1280]{2,1,0:T(8,128)(2,1)S(1)}, u32[]{:S(2)}, u32[]{:S(2)}) collective-permute-start(bf16[4,80,1280]{2,1,0:T(8,128)(2,1)} %get-tuple-element.28), channel_id=1, source_target_pairs={{0,64},{2,18},{10,74},{8,24},{16,80},{18,2},{26,90},{24,8},{34,98}... | collective-permute-start | bytes 2457608 | tf_op jit(solution)/shard_map/ppermute | solution.py:37
  31.4 1.3 %collective-permute-start.5 = (bf16[4,80,1280]{2,1,0:T(8,128)(2,1)}, bf16[4,80,1280]{2,1,0:T(8,128)(2,1)S(1)}, u32[]{:S(2)}, u32[]{:S(2)}) collective-permute-start(bf16[4,80,1280]{2,1,0:T(8,128)(2,1)} %get-tuple-element.29), channel_id=1, source_target_pairs={{0,98},{2,24},{10,104},{8,2},{16,114},{18,8},{26,120},{24,18},{34,... | collective-permute-start | bytes 2457608 | tf_op jit(solution)/shard_map/ppermute | solution.py:37
  32.7 12.0 %factor_term.1 = (bf16[4,160,1280]{2,1,0:T(8,128)(2,1)}, bf16[4,160,1280]{2,1,0:T(8,128)(2,1)}, bf16[2,160,1280]{2,1,0:T(8,128)(2,1)}, bf16[2,160,1280]{2,1,0:T(8,128)(2,1)}, bf16[4,160,1280]{2,1,0:T(8,128)(2,1)}) custom-call(s32[4]{0:T(128)S(1)} %pad_add_fusion.place, bf16[768,2560]{1,0:T(8,128)(2,1)} %collective-permute-done.b.acts, ...), custom_call_target="tpu_custom_call" | custom-call | tf_op jit(solution)/shard_map/factor_term/pallas_call | solution.py:257
  44.7 0.5 collective-permute-start.2
  45.2 2.6 %collective-permute-start.8 = (bf16[2,160,1280]{2,1,0:T(8,128)(2,1)}, bf16[2,160,1280]{2,1,0:T(8,128)(2,1)S(1)}, u32[]{:S(2)}, u32[]{:S(2)}) collective-permute-start(bf16[2,160,1280]{2,1,0:T(8,128)(2,1)} %get-tuple-element.32), channel_id=1, source_target_pairs={{0,98},{2,24},{10,104},{8,2},{16,114},{18,8},{26,120},{24,18},{34,... | collective-permute-start | bytes 2457608 | tf_op jit(solution)/shard_map/ppermute | solution.py:37
  47.8 2.6 %collective-permute-done.4.refs_2_ = bf16[4,80,1280]{2,1,0:T(8,128)(2,1)S(1)} collective-permute-done((bf16[4,80,1280]{2,1,0:T(8,128)(2,1)}, bf16[4,80,1280]{2,1,0:T(8,128)(2,1)S(1)}, u32[]{:S(2)}, u32[]{:S(2)}) %collective-permute-start.4) | collective-permute-done | bytes 819232 | tf_op jit(solution)/shard_map/ppermute | solution.py:37
  50.4 0.2 collective-permute-done.5.refs_3_
  50.6 2.1 %fold.2 = (f32[80,1280]{1,0:T(8,128)}, bf16[80,1280]{1,0:T(8,128)(2,1)S(1)}, bf16[80,1280]{1,0:T(8,128)(2,1)S(1)}, bf16[80,1280]{1,0:T(8,128)(2,1)S(1)}) custom-call(s32[1]{0:T(128)} %bitcast.1.me, bf16[4,80,1280]{2,1,0:T(8,128)(2,1)} %get-tuple-element.27.refs_0_, bf16[4,80,1280]{2,1,0:T(8,128)(2,1)S(1)} %collective-permute-done.3.refs_1_, ...), custom_call_target="tpu_custom_call" | custom-call | tf_op jit(solution)/shard_map/fold/pallas_call | solution.py:301
  52.7 2.2 %collective-permute-start.6 = (bf16[80,1280]{1,0:T(8,128)(2,1)S(1)}, bf16[80,1280]{1,0:T(8,128)(2,1)S(1)}, u32[]{:S(2)}, u32[]{:S(2)}) collective-permute-start(bf16[80,1280]{1,0:T(8,128)(2,1)S(1)} %get-tuple-element.30), channel_id=1, source_target_pairs={{0,10},{2,32},{10,16},{8,42},{16,26},{18,48},{26,0},{24,58},{34,40... | collective-permute-start | bytes 614408 | tf_op jit(solution)/shard_map/ppermute | solution.py:37
  54.8 3.3 %collective-permute-start.9 = (bf16[80,1280]{1,0:T(8,128)(2,1)S(1)}, bf16[80,1280]{1,0:T(8,128)(2,1)S(1)}, u32[]{:S(2)}, u32[]{:S(2)}) collective-permute-start(bf16[80,1280]{1,0:T(8,128)(2,1)S(1)} %get-tuple-element.33), channel_id=1, source_target_pairs={{0,16},{2,66},{10,26},{8,72},{16,0},{18,82},{26,10},{24,88},{34,50... | collective-permute-start | bytes 614408 | tf_op jit(solution)/shard_map/ppermute | solution.py:37
  58.1 0.8 collective-permute-start.10
  59.0 1.2 collective-permute-done.2.received
  60.1 2.5 %collective-permute-done.6.refs_0_.refs_1_ = bf16[80,1280]{1,0:T(8,128)(2,1)S(1)} collective-permute-done((bf16[80,1280]{1,0:T(8,128)(2,1)S(1)}, bf16[80,1280]{1,0:T(8,128)(2,1)S(1)}, u32[]{:S(2)}, u32[]{:S(2)}) %collective-permute-start.6) | collective-permute-done | bytes 204832 | tf_op jit(solution)/shard_map/ppermute | solution.py:37
  62.7 3.2 %grow.2 = bf16[4,160,1280]{2,1,0:T(8,128)(2,1)} custom-call(bf16[4,160,1280]{2,1,0:T(8,128)(2,1)} %get-tuple-element.25.x, bf16[2,160,1280]{2,1,0:T(8,128)(2,1)} %collective-permute-done.2.received, bf16[80,1280]{1,0:T(8,128)(2,1)S(1)} %collective-permute-done.6.refs_0_.refs_1_), custom_call_target="tpu_custom_call", output_to_operand_aliasing={{}: (0, {})} | custom-call | tf_op jit(solution)/shard_map/grow/pallas_call | solution.py:365
  65.9 1.1 collective-permute-start.7
  67.1 2.1 %grow.3 = bf16[4,160,1280]{2,1,0:T(8,128)(2,1)} custom-call(bf16[4,160,1280]{2,1,0:T(8,128)(2,1)} %get-tuple-element.31.x, bf16[2,160,1280]{2,1,0:T(8,128)(2,1)S(1)} %collective-permute-done.8.received, bf16[80,1280]{1,0:T(8,128)(2,1)S(1)} %collective-permute-done.9.refs_0_.refs_2_, ...), custom_call_target="tpu_custom_call", output_to_operand_aliasing={{}: (0, {})} | custom-call | tf_op jit(solution)/shard_map/grow/pallas_call | solution.py:365
  69.2 1.9 %collective-permute-start.11 = (bf16[4,160,1280]{2,1,0:T(8,128)(2,1)}, bf16[4,160,1280]{2,1,0:T(8,128)(2,1)}, u32[]{:S(2)}, u32[]{:S(2)}) collective-permute-start(bf16[4,160,1280]{2,1,0:T(8,128)(2,1)} %grow.3), channel_id=1, source_target_pairs={{0,98},{2,24},{10,104},{8,2},{16,114},{18,8},{26,120},{24,18},{34,... | collective-permute-start | bytes 4915208 | tf_op jit(solution)/shard_map/ppermute | solution.py:37
  71.1 1.2 settle.2
  72.3 1.3 collective-permute-start.12
  73.6 2.4 %collective-permute-start.13 = (f32[40,1280]{1,0:T(8,128)S(1)}, f32[40,1280]{1,0:T(8,128)S(1)}, u32[]{:S(2)}, u32[]{:S(2)}) collective-permute-start(f32[40,1280]{1,0:T(8,128)S(1)} %get-tuple-element.36.mine), channel_id=1, source_target_pairs={{0,1},{1,0},{2,3},{3,2},{4,5},{5,4},{6,7},{7,6},{8,9},{9,8},{10,11... | collective-permute-start | bytes 614408 | tf_op jit(solution)/shard_map/ppermute | solution.py:25
  76.0 0.3 collective-permute-start.14
  76.2 2.7 %collective-permute-done.12.other = f32[40,1280]{1,0:T(8,128)S(1)} collective-permute-done((f32[40,1280]{1,0:T(8,128)S(1)}, f32[40,1280]{1,0:T(8,128)S(1)}, u32[]{:S(2)}, u32[]{:S(2)}) %collective-permute-start.12) | collective-permute-done | bytes 204832 | tf_op jit(solution)/shard_map/ppermute | solution.py:25
  78.9 6.5 %collective-permute-done.13.partner = f32[40,1280]{1,0:T(8,128)S(1)} collective-permute-done((f32[40,1280]{1,0:T(8,128)S(1)}, f32[40,1280]{1,0:T(8,128)S(1)}, u32[]{:S(2)}, u32[]{:S(2)}) %collective-permute-start.13) | collective-permute-done | bytes 204832 | tf_op jit(solution)/shard_map/ppermute | solution.py:25
  85.4 2.0 %collective-permute-done.14.partner_other = f32[40,1280]{1,0:T(8,128)S(1)} collective-permute-done((f32[40,1280]{1,0:T(8,128)S(1)}, f32[40,1280]{1,0:T(8,128)S(1)}, u32[]{:S(2)}, u32[]{:S(2)}) %collective-permute-start.14) | collective-permute-done | bytes 204832 | tf_op jit(solution)/shard_map/ppermute | solution.py:535
  87.5 5.0 %left_product.1.refs_3_ = bf16[128,16,128]{2,1,0:T(8,128)(2,1)} custom-call(s32[4]{0:T(128)S(1)} %pad_add_fusion.place, f32[40,1280]{1,0:T(8,128)S(1)} %get-tuple-element.36.mine, f32[40,1280]{1,0:T(8,128)S(1)} %collective-permute-done.12.other, f32[40,1280]{1,0:T(8,128)S(1)} %collective-permute-done.13.partner, ...), custom_call_target="tpu_custom_call" | custom-call | tf_op jit(solution)/shard_map/left_product/pallas_call | solution.py:430
  92.5 6.3 %all-to-all-start = ((bf16[128,16,128]{2,1,0:T(8,128)(2,1)}), bf16[128,16,128]{2,1,0:T(8,128)(2,1)S(1)}, u32[]{:S(2)}, u32[]{:S(2)}) async-start(bf16[128,16,128]{2,1,0:T(8,128)(2,1)} %left_product.1.refs_3_), calls=%async_computation | async-start | bytes 1048576 | tf_op jit(solution)/shard_map/all_to_all | solution.py:539
  98.8 0.0 collective-permute-done.7.refs_1_
  98.8 0.0 collective-permute-done.11.refs_2_
  98.8 4.4 %fold.3 = (f32[160,1280]{1,0:T(8,128)}, bf16[160,1280]{1,0:T(8,128)(2,1)S(1)}, bf16[160,1280]{1,0:T(8,128)(2,1)}, bf16[160,1280]{1,0:T(8,128)(2,1)S(1)}) custom-call(s32[1]{0:T(128)} %bitcast.1.me, bf16[4,160,1280]{2,1,0:T(8,128)(2,1)} %get-tuple-element.24.refs_4_.refs_0_, bf16[4,160,1280]{2,1,0:T(8,128)(2,1)S(1)} %collective-permute-done.7.refs_1_, ...), custom_call_target="tpu_custom_call" | custom-call | tf_op jit(solution)/shard_map/fold/pallas_call | solution.py:301
  103.2 1.8 %collective-permute-start.15 = (bf16[160,1280]{1,0:T(8,128)(2,1)S(1)}, bf16[160,1280]{1,0:T(8,128)(2,1)S(1)}, u32[]{:S(2)}, u32[]{:S(2)}) collective-permute-start(bf16[160,1280]{1,0:T(8,128)(2,1)S(1)} %get-tuple-element.39.late), channel_id=1, source_target_pairs={{0,10},{2,32},{10,16},{8,42},{16,26},{18,48},{26,0},{24,58},{34,40... | collective-permute-start | bytes 1228808 | tf_op jit(solution)/shard_map/ppermute | solution.py:37
  105.0 2.9 %collective-permute-start.16 = (bf16[160,1280]{1,0:T(8,128)(2,1)}, bf16[160,1280]{1,0:T(8,128)(2,1)S(1)}, u32[]{:S(2)}, u32[]{:S(2)}) collective-permute-start(bf16[160,1280]{1,0:T(8,128)(2,1)} %get-tuple-element.40), channel_id=1, source_target_pairs={{0,16},{2,66},{10,26},{8,72},{16,0},{18,82},{26,10},{24,88},{34,50... | collective-permute-start | bytes 1228808 | tf_op jit(solution)/shard_map/ppermute | solution.py:37
  108.0 1.2 collective-permute-start.17
  109.2 3.4 %all-to-all-done.blocks = bf16[128,16,128]{2,1,0:T(8,128)(2,1)S(1)} async-done(((bf16[128,16,128]{2,1,0:T(8,128)(2,1)}), bf16[128,16,128]{2,1,0:T(8,128)(2,1)S(1)}, u32[]{:S(2)}, u32[]{:S(2)}) %all-to-all-start) | async-done | bytes 524320 | tf_op jit(solution)/shard_map/all_to_all | solution.py:539
  112.6 4.7 %right_product.1.refs_4_ = f32[40,1280]{1,0:T(8,128)} custom-call(s32[4]{0:T(128)S(1)} %pad_add_fusion.place, bf16[128,16,128]{2,1,0:T(8,128)(2,1)S(1)} %all-to-all-done.blocks, bf16[2560,1280]{1,0:T(8,128)(2,1)} %right.1, bf16[160,1280]{1,0:T(8,128)(2,1)S(1)} %get-tuple-element.39.late), custom_call_target="tpu_custom_call" | custom-call | tf_op jit(solution)/shard_map/right_product/pallas_call | solution.py:473
  117.4 2.1 %collective-permute-done.16.refs_2_ = bf16[160,1280]{1,0:T(8,128)(2,1)S(1)} collective-permute-done((bf16[160,1280]{1,0:T(8,128)(2,1)}, bf16[160,1280]{1,0:T(8,128)(2,1)S(1)}, u32[]{:S(2)}, u32[]{:S(2)}) %collective-permute-start.16) | collective-permute-done | bytes 409632 | tf_op jit(solution)/shard_map/ppermute | solution.py:37
  119.5 1.5 %settle.3 = (f32[80,1280]{1,0:T(8,128)S(1)}, bf16[80,1280]{1,0:T(8,128)(2,1)S(1)}) custom-call(s32[1]{0:T(128)} %bitcast.xl, f32[160,1280]{1,0:T(8,128)} %get-tuple-element.38.refs_0_, bf16[160,1280]{1,0:T(8,128)(2,1)S(1)} %collective-permute-done.15.refs_1_, bf16[160,1280]{1,0:T(8,128)(2,1)S(1)} %collective-permute-done.16.refs_2_, ...), custom_call_target="tpu_custom_call" | custom-call | tf_op jit(solution)/shard_map/settle/pallas_call | solution.py:335
  121.0 0.5 collective-permute-start.18
  121.4 6.0 %collective-permute-done.18 = bf16[80,1280]{1,0:T(8,128)(2,1)S(1)} collective-permute-done((bf16[80,1280]{1,0:T(8,128)(2,1)S(1)}, bf16[80,1280]{1,0:T(8,128)(2,1)S(1)}, u32[]{:S(2)}, u32[]{:S(2)}) %collective-permute-start.18) | collective-permute-done | bytes 204832 | tf_op jit(solution)/shard_map/ppermute | solution.py:25
  127.5 0.4 collective-permute-start.19
  128.0 1.1 collective-permute-done.19
  129.1 0.8 maximum_bitcast_fusion
  (11 shorter events, 0.1 us)
Async XLA Ops:
  0.6 18.0 %collective-permute-start = (bf16[768,2560]{1,0:T(8,128)(2,1)}, bf16[768,2560]{1,0:T(8,128)(2,1)}, u32[]{:S(2)}, u32[]{:S(2)}) collective-permute-start(bf16[768,2560]{1,0:T(8,128)(2,1)} %acts.1), channel_id=1, source_target_pairs={{0,2},{2,0},{1,3},{3,1},{4,6},{6,4},{5,7},{7,5},{8,10},{10,8},{9,1... | collective-permute-start | bytes 11796488 | tf_op jit(solution)/shard_map/ppermute | solution.py:25
  2.1 16.5 %collective-permute-start.1 = (bf16[768,2560]{1,0:T(8,128)(2,1)}, bf16[768,2560]{1,0:T(8,128)(2,1)}, u32[]{:S(2)}, u32[]{:S(2)}) collective-permute-start(bf16[768,2560]{1,0:T(8,128)(2,1)} %grads.1), channel_id=1, source_target_pairs={{0,2},{2,0},{1,3},{3,1},{4,6},{6,4},{5,7},{7,5},{8,10},{10,8},{9,1... | collective-permute-start | bytes 11796488 | tf_op jit(solution)/shard_map/ppermute | solution.py:25
  27.0 20.8 %collective-permute-start.3 = (bf16[4,80,1280]{2,1,0:T(8,128)(2,1)}, bf16[4,80,1280]{2,1,0:T(8,128)(2,1)S(1)}, u32[]{:S(2)}, u32[]{:S(2)}) collective-permute-start(bf16[4,80,1280]{2,1,0:T(8,128)(2,1)} %get-tuple-element.23.after), channel_id=1, source_target_pairs={{0,34},{2,8},{10,40},{8,18},{16,50},{18,24},{26,56},{24,2},{34,64}... | collective-permute-start | bytes 2457608 | tf_op jit(solution)/shard_map/ppermute | solution.py:37
  28.7 21.6 %collective-permute-start.4 = (bf16[4,80,1280]{2,1,0:T(8,128)(2,1)}, bf16[4,80,1280]{2,1,0:T(8,128)(2,1)S(1)}, u32[]{:S(2)}, u32[]{:S(2)}) collective-permute-start(bf16[4,80,1280]{2,1,0:T(8,128)(2,1)} %get-tuple-element.28), channel_id=1, source_target_pairs={{0,64},{2,18},{10,74},{8,24},{16,80},{18,2},{26,90},{24,8},{34,98}... | collective-permute-start | bytes 2457608 | tf_op jit(solution)/shard_map/ppermute | solution.py:37
  31.4 19.2 %collective-permute-start.5 = (bf16[4,80,1280]{2,1,0:T(8,128)(2,1)}, bf16[4,80,1280]{2,1,0:T(8,128)(2,1)S(1)}, u32[]{:S(2)}, u32[]{:S(2)}) collective-permute-start(bf16[4,80,1280]{2,1,0:T(8,128)(2,1)} %get-tuple-element.29), channel_id=1, source_target_pairs={{0,98},{2,24},{10,104},{8,2},{16,114},{18,8},{26,120},{24,18},{34,... | collective-permute-start | bytes 2457608 | tf_op jit(solution)/shard_map/ppermute | solution.py:37
  44.7 15.4 %collective-permute-start.2 = (bf16[2,160,1280]{2,1,0:T(8,128)(2,1)}, bf16[2,160,1280]{2,1,0:T(8,128)(2,1)}, u32[]{:S(2)}, u32[]{:S(2)}) collective-permute-start(bf16[2,160,1280]{2,1,0:T(8,128)(2,1)} %get-tuple-element.26), channel_id=1, source_target_pairs={{0,34},{2,8},{10,40},{8,18},{16,50},{18,24},{26,56},{24,2},{34,64}... | collective-permute-start | bytes 2457608 | tf_op jit(solution)/shard_map/ppermute | solution.py:37
  45.2 21.9 %collective-permute-start.8 = (bf16[2,160,1280]{2,1,0:T(8,128)(2,1)}, bf16[2,160,1280]{2,1,0:T(8,128)(2,1)S(1)}, u32[]{:S(2)}, u32[]{:S(2)}) collective-permute-start(bf16[2,160,1280]{2,1,0:T(8,128)(2,1)} %get-tuple-element.32), channel_id=1, source_target_pairs={{0,98},{2,24},{10,104},{8,2},{16,114},{18,8},{26,120},{24,18},{34,... | collective-permute-start | bytes 2457608 | tf_op jit(solution)/shard_map/ppermute | solution.py:37
  52.7 10.0 %collective-permute-start.6 = (bf16[80,1280]{1,0:T(8,128)(2,1)S(1)}, bf16[80,1280]{1,0:T(8,128)(2,1)S(1)}, u32[]{:S(2)}, u32[]{:S(2)}) collective-permute-start(bf16[80,1280]{1,0:T(8,128)(2,1)S(1)} %get-tuple-element.30), channel_id=1, source_target_pairs={{0,10},{2,32},{10,16},{8,42},{16,26},{18,48},{26,0},{24,58},{34,40... | collective-permute-start | bytes 614408 | tf_op jit(solution)/shard_map/ppermute | solution.py:37
  54.8 12.3 %collective-permute-start.9 = (bf16[80,1280]{1,0:T(8,128)(2,1)S(1)}, bf16[80,1280]{1,0:T(8,128)(2,1)S(1)}, u32[]{:S(2)}, u32[]{:S(2)}) collective-permute-start(bf16[80,1280]{1,0:T(8,128)(2,1)S(1)} %get-tuple-element.33), channel_id=1, source_target_pairs={{0,16},{2,66},{10,26},{8,72},{16,0},{18,82},{26,10},{24,88},{34,50... | collective-permute-start | bytes 614408 | tf_op jit(solution)/shard_map/ppermute | solution.py:37
  58.1 9.0 %collective-permute-start.10 = (bf16[80,1280]{1,0:T(8,128)(2,1)S(1)}, bf16[80,1280]{1,0:T(8,128)(2,1)S(1)}, u32[]{:S(2)}, u32[]{:S(2)}) collective-permute-start(bf16[80,1280]{1,0:T(8,128)(2,1)S(1)} %get-tuple-element.34), channel_id=1, source_target_pairs={{0,26},{2,96},{10,0},{8,106},{16,10},{18,112},{26,16},{24,122},{34... | collective-permute-start | bytes 614408 | tf_op jit(solution)/shard_map/ppermute | solution.py:37
  65.9 32.9 %collective-permute-start.7 = (bf16[4,160,1280]{2,1,0:T(8,128)(2,1)}, bf16[4,160,1280]{2,1,0:T(8,128)(2,1)S(1)}, u32[]{:S(2)}, u32[]{:S(2)}) collective-permute-start(bf16[4,160,1280]{2,1,0:T(8,128)(2,1)} %grow.2), channel_id=1, source_target_pairs={{0,34},{2,8},{10,40},{8,18},{16,50},{18,24},{26,56},{24,2},{34,64}... | collective-permute-start | bytes 4915208 | tf_op jit(solution)/shard_map/ppermute | solution.py:37
  69.2 29.6 %collective-permute-start.11 = (bf16[4,160,1280]{2,1,0:T(8,128)(2,1)}, bf16[4,160,1280]{2,1,0:T(8,128)(2,1)}, u32[]{:S(2)}, u32[]{:S(2)}) collective-permute-start(bf16[4,160,1280]{2,1,0:T(8,128)(2,1)} %grow.3), channel_id=1, source_target_pairs={{0,98},{2,24},{10,104},{8,2},{16,114},{18,8},{26,120},{24,18},{34,... | collective-permute-start | bytes 4915208 | tf_op jit(solution)/shard_map/ppermute | solution.py:37
  72.3 6.6 %collective-permute-start.12 = (f32[40,1280]{1,0:T(8,128)S(1)}, f32[40,1280]{1,0:T(8,128)S(1)}, u32[]{:S(2)}, u32[]{:S(2)}) collective-permute-start(f32[40,1280]{1,0:T(8,128)S(1)} %get-tuple-element.37), channel_id=1, source_target_pairs={{0,4},{4,0},{1,5},{5,1},{2,6},{6,2},{3,7},{7,3},{8,12},{12,8},{9,1... | collective-permute-start | bytes 614408 | tf_op jit(solution)/shard_map/ppermute | solution.py:25
  73.6 11.9 %collective-permute-start.13 = (f32[40,1280]{1,0:T(8,128)S(1)}, f32[40,1280]{1,0:T(8,128)S(1)}, u32[]{:S(2)}, u32[]{:S(2)}) collective-permute-start(f32[40,1280]{1,0:T(8,128)S(1)} %get-tuple-element.36.mine), channel_id=1, source_target_pairs={{0,1},{1,0},{2,3},{3,2},{4,5},{5,4},{6,7},{7,6},{8,9},{9,8},{10,11... | collective-permute-start | bytes 614408 | tf_op jit(solution)/shard_map/ppermute | solution.py:25
  76.0 11.5 %collective-permute-start.14 = (f32[40,1280]{1,0:T(8,128)S(1)}, f32[40,1280]{1,0:T(8,128)S(1)}, u32[]{:S(2)}, u32[]{:S(2)}) collective-permute-start(f32[40,1280]{1,0:T(8,128)S(1)} %get-tuple-element.37), channel_id=1, source_target_pairs={{0,5},{1,4},{4,1},{5,0},{2,7},{3,6},{6,3},{7,2},{8,13},{9,12},{12,... | collective-permute-start | bytes 614408 | tf_op jit(solution)/shard_map/ppermute | solution.py:535
  92.5 20.2 %all-to-all-start = ((bf16[128,16,128]{2,1,0:T(8,128)(2,1)}), bf16[128,16,128]{2,1,0:T(8,128)(2,1)S(1)}, u32[]{:S(2)}, u32[]{:S(2)}) async-start(bf16[128,16,128]{2,1,0:T(8,128)(2,1)} %left_product.1.refs_3_), calls=%async_computation | async-start | bytes 1048576 | tf_op jit(solution)/shard_map/all_to_all | solution.py:539
  103.2 14.2 %collective-permute-start.15 = (bf16[160,1280]{1,0:T(8,128)(2,1)S(1)}, bf16[160,1280]{1,0:T(8,128)(2,1)S(1)}, u32[]{:S(2)}, u32[]{:S(2)}) collective-permute-start(bf16[160,1280]{1,0:T(8,128)(2,1)S(1)} %get-tuple-element.39.late), channel_id=1, source_target_pairs={{0,10},{2,32},{10,16},{8,42},{16,26},{18,48},{26,0},{24,58},{34,40... | collective-permute-start | bytes 1228808 | tf_op jit(solution)/shard_map/ppermute | solution.py:37
  105.0 14.5 %collective-permute-start.16 = (bf16[160,1280]{1,0:T(8,128)(2,1)}, bf16[160,1280]{1,0:T(8,128)(2,1)S(1)}, u32[]{:S(2)}, u32[]{:S(2)}) collective-permute-start(bf16[160,1280]{1,0:T(8,128)(2,1)} %get-tuple-element.40), channel_id=1, source_target_pairs={{0,16},{2,66},{10,26},{8,72},{16,0},{18,82},{26,10},{24,88},{34,50... | collective-permute-start | bytes 1228808 | tf_op jit(solution)/shard_map/ppermute | solution.py:37
  108.0 11.5 %collective-permute-start.17 = (bf16[160,1280]{1,0:T(8,128)(2,1)S(1)}, bf16[160,1280]{1,0:T(8,128)(2,1)S(1)}, u32[]{:S(2)}, u32[]{:S(2)}) collective-permute-start(bf16[160,1280]{1,0:T(8,128)(2,1)S(1)} %get-tuple-element.41), channel_id=1, source_target_pairs={{0,26},{2,96},{10,0},{8,106},{16,10},{18,112},{26,16},{24,122},{34... | collective-permute-start | bytes 1228808 | tf_op jit(solution)/shard_map/ppermute | solution.py:37
  121.0 6.5 %collective-permute-start.18 = (bf16[80,1280]{1,0:T(8,128)(2,1)S(1)}, bf16[80,1280]{1,0:T(8,128)(2,1)S(1)}, u32[]{:S(2)}, u32[]{:S(2)}) collective-permute-start(bf16[80,1280]{1,0:T(8,128)(2,1)S(1)} %get-tuple-element.43), channel_id=1, source_target_pairs={{0,4},{4,0},{1,5},{5,1},{2,6},{6,2},{3,7},{7,3},{8,12},{12,8},{9,1... | collective-permute-start | bytes 614408 | tf_op jit(solution)/shard_map/ppermute | solution.py:25
  127.5 1.5 %collective-permute-start.19 = (f32[40,1280]{1,0:T(8,128)S(1)}, f32[40,1280]{1,0:T(8,128)S(1)}, u32[]{:S(2)}, u32[]{:S(2)}) collective-permute-start(f32[40,1280]{1,0:T(8,128)S(1)} %dynamic-slice_bitcast_fusion), channel_id=1, source_target_pairs={{0,2},{2,0},{1,3},{3,1},{4,6},{6,4},{5,7},{7,5},{8,10},{10,8},{9,1... | collective-permute-start | bytes 614408 | tf_op jit(solution)/shard_map/ppermute | solution.py:25

commit v15 on v13

--- a/solution.py
+++ b/solution.py
@@ -11,6 +11,7 @@
 F32 = jnp.float32
 TILE = 640
 ANY = pl.BlockSpec(memory_space=pl.ANY)
+VMEM = pl.BlockSpec(memory_space=pltpu.VMEM)
 
 
 def contract(first_rows, second_rows):
@@ -255,22 +256,21 @@
 
 def fold(me, parts, *after):
     _, rows, width = parts[0].shape
-    block = pl.BlockSpec((4, rows, width), lambda s, m: (0, 0, 0))
     whole = pl.BlockSpec((rows, width), lambda s, m: (0, 0))
     return pl.pallas_call(
         functools.partial(fold_kernel, len(parts)),
         out_shape=[pltpu.HBM((rows, width), F32)]
-        + [jax.ShapeDtypeStruct((rows, width), BF)] * 3,
+        + [pltpu.VMEM((rows, width), BF)] * 3,
         grid_spec=pltpu.PrefetchScalarGridSpec(
             num_scalar_prefetch=1,
             grid=(1,),
             in_specs=[pl.BlockSpec(memory_space=pltpu.HBM)]
-            + [block] * (len(parts) - 1)
+            + [VMEM] * (len(parts) - 1)
             + [ANY] * len(after),
-            out_specs=[whole] * 4,
+            out_specs=[whole] + [VMEM] * 3,
             scratch_shapes=[pltpu.VMEM((4, rows, width), BF), pltpu.SemaphoreType.DMA],
         ),
-        compiler_params=pltpu.CompilerParams(vmem_limit_bytes=26 * 2**20),
+        compiler_params=pltpu.CompilerParams(vmem_limit_bytes=12 * 2**20),
         cost_estimate=pl.CostEstimate(flops=0, bytes_accessed=0, transcendentals=0),
         name="fold",
     )(me, in_hbm(parts[0]), *parts[1:], *after)
@@ -297,12 +297,13 @@
         grid_spec=pltpu.PrefetchScalarGridSpec(
             num_scalar_prefetch=1,
             grid=(1,),
-            in_specs=[pl.BlockSpec(p.shape, lambda s, x, n=p.ndim: (0,) * n) for p in parts]
+            in_specs=[pl.BlockSpec((rows, width), lambda s, x: (0, 0))]
+            + [VMEM] * (len(parts) - 1)
             + [ANY] * len(after),
             out_specs=[half] * 2,
             scratch_shapes=[pltpu.VMEM((rows, width), F32)],
         ),
-        compiler_params=pltpu.CompilerParams(vmem_limit_bytes=16 * 2**20),
+        compiler_params=pltpu.CompilerParams(vmem_limit_bytes=8 * 2**20),
         cost_estimate=pl.CostEstimate(flops=0, bytes_accessed=0, transcendentals=0),
         name="settle",
     )(xl, *parts, *after)
@@ -325,7 +326,7 @@
         functools.partial(grow_kernel, side),
         out_shape=pltpu.HBM(x.shape, x.dtype),
         grid=(1,),
-        in_specs=[hbm, pl.BlockSpec(received.shape, lambda s: (0, 0, 0))] + [ANY] * len(after),
+        in_specs=[hbm, VMEM] + [ANY] * len(after),
         out_specs=hbm,
         scratch_shapes=[
             pltpu.VMEM(received.shape, x.dtype),
@@ -349,30 +350,39 @@
     wait_all(held.at[step], sems.at[step])
 
 
-def left_kernel(place, mine, other, partner, partner_other, left, out, total, packed, held, sems):
+def left_kernel(own, place, a, b, left, *rest):
+    before = None if own else rest[0]
+    out, total, held, sems = rest[-4:] if own else (rest[1], rest[2], *rest[4:])
     step = pl.program_id(0)
-    fetch_tiles(step, left, held, sems)
-    at = pl.ds(pl.multiple_of((step & 1) * TILE, TILE), TILE)
-    rows = mine.shape[0]
-
-    def term(a, b):
-        stacked = jnp.concatenate(split_pair(a[:, at] + b[:, at]), axis=0)
-        value = jnp.dot(stacked, held[step], preferred_element_type=F32)
-        total[...] = jnp.where(step == 0, value, total[...] + value)
-
-    own = (step >> 1) == (place[1] ^ place[0])
-    pl.when(own)(lambda: term(mine, other))
-    pl.when(jnp.logical_not(own))(lambda: term(partner, partner_other))
-
-    @pl.when(step == 3)
+    rows = a.shape[0]
+    at = pl.ds(pl.multiple_of(step * TILE, TILE), TILE)
+    part = place[1] ^ place[0] if own else 1 - (place[1] ^ place[0])
+
+    @pl.when(step == 0)
     def _():
-        value = total[:rows] + total[rows:]
+        for k in range(2):
+            tile = left.at[pl.ds(pl.multiple_of((part * 2 + k) * TILE, TILE), TILE)]
+            pltpu.make_async_copy(tile, held.at[k], sems.at[k]).start()
+
+    stacked = jnp.concatenate(split_pair(a[:, at] + b[:, at]), axis=0)
+    wait_all(held.at[step], sems.at[step])
+    value = jnp.dot(stacked, held[step], preferred_element_type=F32)
+    pl.when(step == 0)(lambda: total.__setitem__(..., value if own else before[...] + value))
+    pl.when(step == 1)(lambda: total.__setitem__(..., total[...] + value))
+    if own:
+        pl.when(step == 1)(lambda: out.__setitem__(..., total[...]))
+        return
+    packed = rest[3]
+
+    @pl.when(step == 1)
+    def _():
+        result = total[:rows] + total[rows:]
         for z in range(2):
             for y in range(4):
                 for xl in range(2):
                     for c in range(2):
                         n = ((z * 4 + y) * 2 + xl) * 2 + c
-                        block = value[:, n * rows : (n + 1) * rows]
+                        block = result[:, n * rows : (n + 1) * rows]
                         packed[n, 0:16, 0:rows] = block[0:16]
                         packed[n, 0:16, rows : 2 * rows] = block[16:32]
                         packed[n, 0:8, 2 * rows : 3 * rows] = block[32:40]
@@ -383,30 +393,28 @@
                             out[64 + d] = ready
 
 
-def left_product(place, mine, other, partner, partner_other, left):
-    rows, half = mine.shape
-    whole = pl.BlockSpec((rows, half), lambda k, p: (0, 0))
-    return pl.pallas_call(
-        left_kernel,
-        out_shape=jax.ShapeDtypeStruct((128, 16, 128), BF),
-        grid_spec=pltpu.PrefetchScalarGridSpec(
-            num_scalar_prefetch=1,
-            grid=(4,),
-            in_specs=[whole] * 4 + [pl.BlockSpec(memory_space=pltpu.HBM)],
-            out_specs=pl.BlockSpec((128, 16, 128), lambda k, p: (0, 0, 0)),
-            scratch_shapes=[
-                pltpu.VMEM((2 * rows, half), F32),
-                pltpu.VMEM((32, 16, 128), F32),
-                pltpu.VMEM((4, TILE, half), BF),
-                pltpu.SemaphoreType.DMA((4,)),
-            ],
-        ),
-        compiler_params=pltpu.CompilerParams(vmem_limit_bytes=20 * 2**20),
+def left_product(place, a, b, left, before=None):
+    rows, half = a.shape
+    own = before is None
+    total = pltpu.VMEM((2 * rows, half), F32)
+    return pl.pallas_call(
+        functools.partial(left_kernel, own),
+        out_shape=total if own else pltpu.VMEM((128, 16, 128), BF),
+        grid_spec=pltpu.PrefetchScalarGridSpec(
+            num_scalar_prefetch=1,
+            grid=(2,),
+            in_specs=[VMEM, VMEM, pl.BlockSpec(memory_space=pltpu.HBM)] + [VMEM] * (not own),
+            out_specs=VMEM,
+            scratch_shapes=[total]
+            + [pltpu.VMEM((32, 16, 128), F32)] * (not own)
+            + [pltpu.VMEM((2, TILE, half), BF), pltpu.SemaphoreType.DMA((2,))],
+        ),
+        compiler_params=pltpu.CompilerParams(vmem_limit_bytes=16 * 2**20),
         cost_estimate=pl.CostEstimate(
-            flops=256 * rows * half * half, bytes_accessed=4 * half * half, transcendentals=0
-        ),
-        name="left_product",
-    )(place, mine, other, partner, partner_other, left)
+            flops=0 if own else 256 * rows * half * half, bytes_accessed=0, transcendentals=0
+        ),
+        name="left_own" if own else "left_product",
+    )(place, a, b, left, *([] if own else [before]))
 
 
 def right_kernel(place, blocks, right, late, out, rows_in, held, sems):
@@ -493,9 +501,8 @@
 
     mine, theirs = settle(my_xl, [in_hbm(m), *m_received], F32)
     across = lax.ppermute(theirs, ("xl", "o"), [(i, 3 - i) for i in range(4)])
-    products = left_product(
-        place, mine, shift(theirs, "xl", 1), shift(mine, "o", 1), across, left_inverse
-    )
+    products = left_product(place, mine, shift(theirs, "xl", 1), left_inverse)
+    products = left_product(place, shift(mine, "o", 1), across, left_inverse, products)
     blocks = lax.all_to_all(products, ("o", "c", "z", "y", "xl"), 0, 0, tiled=True)
     f, *f_pieces = fold(second_me, f_parts, products)
     update = right_product(place, blocks, right_inverse, f_pieces[0])

time: 129 us -> 130 us (level)
  Pallas kernels: 53.6 us -> 55.6 us
  starting transfers between devices: 41.3 us -> 39.7 us
    ppermute x13, waiting for transfers between devices: 14.6 us -> 19 us  [turn(): return lax.ppermute(x, ('z', 'y', 'c'), pairs)]
    ppermute x1, waiting for transfers between devices: 2.27 us -> 0.1 us  [per_device(): across = lax.ppermute(theirs, ('xl', 'o'), [(i, 3 - i) for i in range(4)])]
    ppermute x13, starting transfers between devices: 26 us -> 24 us  [turn(): return lax.ppermute(x, ('z', 'y', 'c'), pairs)]
    pallas_call x1 -> x2, Pallas kernels: 5 us -> 6.94 us  [left_product(): pl.pallas_call(functools.partial(left_kernel, own), out_shape=total if ow...]
  transfers between devices with their start and end apart: 21 -> 21, of which waited for: 11 -> 10; matrix products, arithmetic and copies ran while one was open for 0% -> 0% of each run, Pallas kernels for 34% -> 35%
where the time goes in v15:
time: 130 us
  Pallas kernels  55.6 us (43%)
  starting transfers between devices  39.7 us (31%)
  waiting for transfers between devices  32.8 us (25%)
    ppermute x13, starting transfers between devices, turn(): return lax.ppermute(x, ('z', 'y', 'c'), pairs)  24 us
    ppermute x13, waiting for transfers between devices, turn(): return lax.ppermute(x, ('z', 'y', 'c'), pairs)  19 us
    pallas_call x1, Pallas kernels, factor_term(): pl.pallas_call(factor_kernel, out_shape=[out, out, side, side, out], grid...  15.9 us
    ppermute x6, waiting for transfers between devices, shift(): return lax.ppermute(x, axis, [(i, (i + step) % size) for i in range(size)])  13.7 us
    all_to_all x1, starting transfers between devices, per_device(): lax.all_to_all(products, ('o', 'c', 'z', 'y', 'xl'), 0, 0, tiled=True)  8.29 us
    pallas_call x1, Pallas kernels, cross_term(): pl.pallas_call(cross_kernel, out_shape=[out] * 4, grid_spec=pltpu.Prefetc...  8.05 us
    pallas_call x2, Pallas kernels, fold(): pl.pallas_call(functools.partial(fold_kernel, len(parts)), out_shape=[plt...  7.87 us
    ppermute x6, starting transfers between devices, shift(): return lax.ppermute(x, axis, [(i, (i + step) % size) for i in range(size)])  7.15 us
  transfers between devices with their start and end apart: 21, of which 10 were waited for; matrix products, arithmetic and copies ran while one was open for 0% of the time, Pallas kernels for 35%

profile of v15, /device:TPU:1, one launch (start us, length us, event | category | flops | bytes accessed | tf_op | source)
XLA Modules:
  0.0 129.8 jit_solution(6583598799597247197)
XLA Ops:
  0.6 1.5 %collective-permute-start = (bf16[768,2560]{1,0:T(8,128)(2,1)}, bf16[768,2560]{1,0:T(8,128)(2,1)}, u32[]{:S(2)}, u32[]{:S(2)}) collective-permute-start(bf16[768,2560]{1,0:T(8,128)(2,1)} %h_own.1), channel_id=1, source_target_pairs={{0,2},{2,0},{1,3},{3,1},{4,6},{6,4},{5,7},{7,5},{8,10},{10,8},{9,1... | collective-permute-start | bytes 11796488 | tf_op jit(solution)/shard_map/ppermute | solution.py:25
  2.1 0.1 collective-permute-start.1
  2.2 0.1 pad_add_fusion.place
  2.3 5.4 %cross_own.1.partial = f32[1280,1280]{1,0:T(8,128)S(1)} custom-call(s32[4]{0:T(128)S(1)} %pad_add_fusion.place, bf16[768,2560]{1,0:T(8,128)(2,1)} %g_own.1, bf16[768,2560]{1,0:T(8,128)(2,1)} %h_own.1), custom_call_target="tpu_custom_call" | custom-call | flops 2516582400 | bytes 7864320 | tf_op jit(solution)/shard_map/cross_own/pallas_call | solution.py:125
  7.7 1.1 collective-permute-done.b.h_next
  8.9 5.6 %collective-permute-done.1.a.g_next = bf16[768,2560]{1,0:T(8,128)(2,1)} collective-permute-done((bf16[768,2560]{1,0:T(8,128)(2,1)}, bf16[768,2560]{1,0:T(8,128)(2,1)}, u32[]{:S(2)}, u32[]{:S(2)}) %collective-permute-start.1) | collective-permute-done | bytes 3932192 | tf_op jit(solution)/shard_map/ppermute | solution.py:25
  14.5 8.1 %cross_term.1 = (bf16[4,80,1280]{2,1,0:T(8,128)(2,1)}, bf16[4,80,1280]{2,1,0:T(8,128)(2,1)}, bf16[4,80,1280]{2,1,0:T(8,128)(2,1)}, bf16[4,80,1280]{2,1,0:T(8,128)(2,1)}) custom-call(s32[4]{0:T(128)S(1)} %pad_add_fusion.place, bf16[768,2560]{1,0:T(8,128)(2,1)} %collective-permute-done.1.a.g_next, bf16[768,2560]{1,0:T(8,128)(2,1)} %collective-permute-done.b.h_next, ...), custom_call_target="tpu_custom_call" | custom-call | flops 2516582400 | bytes 9830400 | tf_op jit(solution)/shard_map/cross_term/pallas_call | solution.py:151
  22.6 1.7 %collective-permute-start.3 = (bf16[4,80,1280]{2,1,0:T(8,128)(2,1)}, bf16[4,80,1280]{2,1,0:T(8,128)(2,1)S(1)}, u32[]{:S(2)}, u32[]{:S(2)}) collective-permute-start(bf16[4,80,1280]{2,1,0:T(8,128)(2,1)} %get-tuple-element.23.after), channel_id=1, source_target_pairs={{0,34},{2,8},{10,40},{8,18},{16,50},{18,24},{26,56},{24,2},{34,64}... | collective-permute-start | bytes 2457608 | tf_op jit(solution)/shard_map/ppermute | solution.py:37
  24.3 2.6 %collective-permute-start.4 = (bf16[4,80,1280]{2,1,0:T(8,128)(2,1)}, bf16[4,80,1280]{2,1,0:T(8,128)(2,1)}, u32[]{:S(2)}, u32[]{:S(2)}) collective-permute-start(bf16[4,80,1280]{2,1,0:T(8,128)(2,1)} %get-tuple-element.28), channel_id=1, source_target_pairs={{0,64},{2,18},{10,74},{8,24},{16,80},{18,2},{26,90},{24,8},{34,98}... | collective-permute-start | bytes 2457608 | tf_op jit(solution)/shard_map/ppermute | solution.py:37
  26.9 1.4 %collective-permute-start.5 = (bf16[4,80,1280]{2,1,0:T(8,128)(2,1)}, bf16[4,80,1280]{2,1,0:T(8,128)(2,1)}, u32[]{:S(2)}, u32[]{:S(2)}) collective-permute-start(bf16[4,80,1280]{2,1,0:T(8,128)(2,1)} %get-tuple-element.29), channel_id=1, source_target_pairs={{0,98},{2,24},{10,104},{8,2},{16,114},{18,8},{26,120},{24,18},{34,... | collective-permute-start | bytes 2457608 | tf_op jit(solution)/shard_map/ppermute | solution.py:37
  28.3 15.9 %factor_term.1 = (bf16[4,160,1280]{2,1,0:T(8,128)(2,1)}, bf16[4,160,1280]{2,1,0:T(8,128)(2,1)}, bf16[2,160,1280]{2,1,0:T(8,128)(2,1)}, bf16[2,160,1280]{2,1,0:T(8,128)(2,1)}, bf16[4,160,1280]{2,1,0:T(8,128)(2,1)}) custom-call(s32[4]{0:T(128)S(1)} %pad_add_fusion.place, bf16[768,2560]{1,0:T(8,128)(2,1)} %h_own.1, bf16[768,2560]{1,0:T(8,128)(2,1)} %g_own.1, ...), custom_call_target="tpu_custom_call" | custom-call | flops 10066329600 | bytes 15728640 | tf_op jit(solution)/shard_map/factor_term/pallas_call | solution.py:214
  44.2 0.4 collective-permute-start.2
  44.6 2.6 %collective-permute-start.10 = (bf16[2,160,1280]{2,1,0:T(8,128)(2,1)}, bf16[2,160,1280]{2,1,0:T(8,128)(2,1)S(1)}, u32[]{:S(2)}, u32[]{:S(2)}) collective-permute-start(bf16[2,160,1280]{2,1,0:T(8,128)(2,1)} %get-tuple-element.34), channel_id=1, source_target_pairs={{0,98},{2,24},{10,104},{8,2},{16,114},{18,8},{26,120},{24,18},{34,... | collective-permute-start | bytes 2457608 | tf_op jit(solution)/shard_map/ppermute | solution.py:37
  47.2 0.0 collective-permute-done.3.refs_1_
  47.2 0.0 collective-permute-done.4.refs_2_
  47.2 0.0 collective-permute-done.5.refs_3_
  47.2 3.6 %fold.2 = (f32[80,1280]{1,0:T(8,128)}, bf16[80,1280]{1,0:T(8,128)(2,1)}, bf16[80,1280]{1,0:T(8,128)(2,1)S(1)}, bf16[80,1280]{1,0:T(8,128)(2,1)S(1)}) custom-call(s32[1]{0:T(128)} %bitcast.1.me, bf16[4,80,1280]{2,1,0:T(8,128)(2,1)} %get-tuple-element.27.refs_0_, bf16[4,80,1280]{2,1,0:T(8,128)(2,1)S(1)} %collective-permute-done.3.refs_1_, ...), custom_call_target="tpu_custom_call" | custom-call | tf_op jit(solution)/shard_map/fold/pallas_call | solution.py:260
  50.8 1.7 %collective-permute-start.6 = (bf16[80,1280]{1,0:T(8,128)(2,1)}, bf16[80,1280]{1,0:T(8,128)(2,1)S(1)}, u32[]{:S(2)}, u32[]{:S(2)}) collective-permute-start(bf16[80,1280]{1,0:T(8,128)(2,1)} %get-tuple-element.30), channel_id=1, source_target_pairs={{0,10},{2,32},{10,16},{8,42},{16,26},{18,48},{26,0},{24,58},{34,40... | collective-permute-start | bytes 614408 | tf_op jit(solution)/shard_map/ppermute | solution.py:37
  52.5 3.3 %collective-permute-start.7 = (bf16[80,1280]{1,0:T(8,128)(2,1)S(1)}, bf16[80,1280]{1,0:T(8,128)(2,1)S(1)}, u32[]{:S(2)}, u32[]{:S(2)}) collective-permute-start(bf16[80,1280]{1,0:T(8,128)(2,1)S(1)} %get-tuple-element.31), channel_id=1, source_target_pairs={{0,16},{2,66},{10,26},{8,72},{16,0},{18,82},{26,10},{24,88},{34,50... | collective-permute-start | bytes 614408 | tf_op jit(solution)/shard_map/ppermute | solution.py:37
  55.8 1.3 %collective-permute-start.8 = (bf16[80,1280]{1,0:T(8,128)(2,1)S(1)}, bf16[80,1280]{1,0:T(8,128)(2,1)S(1)}, u32[]{:S(2)}, u32[]{:S(2)}) collective-permute-start(bf16[80,1280]{1,0:T(8,128)(2,1)S(1)} %get-tuple-element.32), channel_id=1, source_target_pairs={{0,26},{2,96},{10,0},{8,106},{16,10},{18,112},{26,16},{24,122},{34... | collective-permute-start | bytes 614408 | tf_op jit(solution)/shard_map/ppermute | solution.py:37
  57.1 5.0 %collective-permute-done.6.refs_0_.refs_1_ = bf16[80,1280]{1,0:T(8,128)(2,1)S(1)} collective-permute-done((bf16[80,1280]{1,0:T(8,128)(2,1)}, bf16[80,1280]{1,0:T(8,128)(2,1)S(1)}, u32[]{:S(2)}, u32[]{:S(2)}) %collective-permute-start.6) | collective-permute-done | bytes 204832 | tf_op jit(solution)/shard_map/ppermute | solution.py:37
  62.1 1.2 settle.2
  63.3 1.3 collective-permute-start.14
  64.6 2.5 %collective-permute-start.12 = (f32[40,1280]{1,0:T(8,128)S(1)}, f32[40,1280]{1,0:T(8,128)S(1)}, u32[]{:S(2)}, u32[]{:S(2)}) collective-permute-start(f32[40,1280]{1,0:T(8,128)S(1)} %get-tuple-element.36.a), channel_id=1, source_target_pairs={{0,1},{1,0},{2,3},{3,2},{4,5},{5,4},{6,7},{7,6},{8,9},{9,8},{10,11... | collective-permute-start | bytes 614408 | tf_op jit(solution)/shard_map/ppermute | solution.py:25
  67.0 0.2 collective-permute-start.13
  67.2 0.0 collective-permute-done.2.received
  67.2 2.0 %grow.2 = bf16[4,160,1280]{2,1,0:T(8,128)(2,1)} custom-call(bf16[4,160,1280]{2,1,0:T(8,128)(2,1)} %get-tuple-element.25.x, bf16[2,160,1280]{2,1,0:T(8,128)(2,1)S(1)} %collective-permute-done.2.received, bf16[80,1280]{1,0:T(8,128)(2,1)S(1)} %collective-permute-done.6.refs_0_.refs_1_, ...), custom_call_target="tpu_custom_call", output_to_operand_aliasing={{}: (0, {})} | custom-call | tf_op jit(solution)/shard_map/grow/pallas_call | solution.py:325
  69.2 2.7 %collective-permute-start.9 = (bf16[4,160,1280]{2,1,0:T(8,128)(2,1)}, bf16[4,160,1280]{2,1,0:T(8,128)(2,1)S(1)}, u32[]{:S(2)}, u32[]{:S(2)}) collective-permute-start(bf16[4,160,1280]{2,1,0:T(8,128)(2,1)} %grow.2), channel_id=1, source_target_pairs={{0,34},{2,8},{10,40},{8,18},{16,50},{18,24},{26,56},{24,2},{34,64}... | collective-permute-start | bytes 4915208 | tf_op jit(solution)/shard_map/ppermute | solution.py:37
  71.9 2.0 %grow.3 = bf16[4,160,1280]{2,1,0:T(8,128)(2,1)} custom-call(bf16[4,160,1280]{2,1,0:T(8,128)(2,1)} %get-tuple-element.33.x, bf16[2,160,1280]{2,1,0:T(8,128)(2,1)S(1)} %collective-permute-done.10.received, bf16[80,1280]{1,0:T(8,128)(2,1)S(1)} %collective-permute-done.6.refs_0_.refs_1_, ...), custom_call_target="tpu_custom_call", output_to_operand_aliasing={{}: (0, {})} | custom-call | tf_op jit(solution)/shard_map/grow/pallas_call | solution.py:325
  73.9 1.5 %collective-permute-start.11 = (bf16[4,160,1280]{2,1,0:T(8,128)(2,1)}, bf16[4,160,1280]{2,1,0:T(8,128)(2,1)}, u32[]{:S(2)}, u32[]{:S(2)}) collective-permute-start(bf16[4,160,1280]{2,1,0:T(8,128)(2,1)} %grow.3), channel_id=1, source_target_pairs={{0,98},{2,24},{10,104},{8,2},{16,114},{18,8},{26,120},{24,18},{34,... | collective-permute-start | bytes 4915208 | tf_op jit(solution)/shard_map/ppermute | solution.py:37
  75.5 2.9 %left_own.1.rest_0_ = f32[80,1280]{1,0:T(8,128)S(1)} custom-call(s32[4]{0:T(128)S(1)} %pad_add_fusion.place, f32[40,1280]{1,0:T(8,128)S(1)} %get-tuple-element.36.a, f32[40,1280]{1,0:T(8,128)S(1)} %collective-permute-done.14.b, bf16[2560,1280]{1,0:T(8,128)(2,1)} %left.3), custom_call_target="tpu_custom_call" | custom-call | tf_op jit(solution)/shard_map/left_own/pallas_call | solution.py:400
  78.4 0.1 collective-permute-done.13.b
  78.5 4.0 %left_product.1.refs_3_ = bf16[128,16,128]{2,1,0:T(8,128)(2,1)} custom-call(s32[4]{0:T(128)S(1)} %pad_add_fusion.place, f32[40,1280]{1,0:T(8,128)S(1)} %collective-permute-done.12.a, f32[40,1280]{1,0:T(8,128)S(1)} %collective-permute-done.13.b, bf16[2560,1280]{1,0:T(8,128)(2,1)} %left.3, f32[80,1280]{1,0:T(8,128)S(1)} %left_own.1.rest_0_), custom_call_target="tpu_custom_call" | custom-call | flops 16777216000 | tf_op jit(solution)/shard_map/left_product/pallas_call | solution.py:400
  82.5 8.3 %all-to-all-start = ((bf16[128,16,128]{2,1,0:T(8,128)(2,1)}), bf16[128,16,128]{2,1,0:T(8,128)(2,1)S(1)}, u32[]{:S(2)}, u32[]{:S(2)}) async-start(bf16[128,16,128]{2,1,0:T(8,128)(2,1)} %left_product.1.refs_3_), calls=%async_computation | async-start | bytes 1048576 | tf_op jit(solution)/shard_map/all_to_all | solution.py:506
  90.8 1.5 %collective-permute-done.9.refs_1_ = bf16[4,160,1280]{2,1,0:T(8,128)(2,1)S(1)} collective-permute-done((bf16[4,160,1280]{2,1,0:T(8,128)(2,1)}, bf16[4,160,1280]{2,1,0:T(8,128)(2,1)S(1)}, u32[]{:S(2)}, u32[]{:S(2)}) %collective-permute-start.9) | collective-permute-done | bytes 1638432 | tf_op jit(solution)/shard_map/ppermute | solution.py:37
  92.3 7.0 %collective-permute-done.11.refs_2_ = bf16[4,160,1280]{2,1,0:T(8,128)(2,1)} collective-permute-done((bf16[4,160,1280]{2,1,0:T(8,128)(2,1)}, bf16[4,160,1280]{2,1,0:T(8,128)(2,1)}, u32[]{:S(2)}, u32[]{:S(2)}) %collective-permute-start.11) | collective-permute-done | bytes 1638432 | tf_op jit(solution)/shard_map/ppermute | solution.py:37
  99.4 4.3 %fold.3 = (f32[160,1280]{1,0:T(8,128)}, bf16[160,1280]{1,0:T(8,128)(2,1)S(1)}, bf16[160,1280]{1,0:T(8,128)(2,1)S(1)}, bf16[160,1280]{1,0:T(8,128)(2,1)S(1)}) custom-call(s32[1]{0:T(128)} %bitcast.1.me, bf16[4,160,1280]{2,1,0:T(8,128)(2,1)} %get-tuple-element.24.refs_4_.refs_0_, bf16[4,160,1280]{2,1,0:T(8,128)(2,1)S(1)} %collective-permute-done.9.refs_1_, ...), custom_call_target="tpu_custom_call" | custom-call | tf_op jit(solution)/shard_map/fold/pallas_call | solution.py:260
  103.7 0.1 collective-permute-start.15
  103.8 4.8 %collective-permute-start.16 = (bf16[160,1280]{1,0:T(8,128)(2,1)S(1)}, bf16[160,1280]{1,0:T(8,128)(2,1)S(1)}, u32[]{:S(2)}, u32[]{:S(2)}) collective-permute-start(bf16[160,1280]{1,0:T(8,128)(2,1)S(1)} %get-tuple-element.40), channel_id=1, source_target_pairs={{0,16},{2,66},{10,26},{8,72},{16,0},{18,82},{26,10},{24,88},{34,50... | collective-permute-start | bytes 1228808 | tf_op jit(solution)/shard_map/ppermute | solution.py:37
  108.5 4.7 %right_product.1.refs_4_ = f32[40,1280]{1,0:T(8,128)} custom-call(s32[4]{0:T(128)S(1)} %pad_add_fusion.place, bf16[128,16,128]{2,1,0:T(8,128)(2,1)S(1)} %all-to-all-done.blocks, bf16[2560,1280]{1,0:T(8,128)(2,1)} %right.1, bf16[160,1280]{1,0:T(8,128)(2,1)S(1)} %get-tuple-element.39.late), custom_call_target="tpu_custom_call" | custom-call | flops 41943040000 | bytes 6553600 | tf_op jit(solution)/shard_map/right_product/pallas_call | solution.py:442
  113.3 5.3 %collective-permute-done.16.refs_2_ = bf16[160,1280]{1,0:T(8,128)(2,1)S(1)} collective-permute-done((bf16[160,1280]{1,0:T(8,128)(2,1)S(1)}, bf16[160,1280]{1,0:T(8,128)(2,1)S(1)}, u32[]{:S(2)}, u32[]{:S(2)}) %collective-permute-start.16) | collective-permute-done | bytes 409632 | tf_op jit(solution)/shard_map/ppermute | solution.py:37
  118.5 0.1 collective-permute-done.17.refs_3_
  118.7 1.5 %settle.3 = (f32[80,1280]{1,0:T(8,128)S(1)}, bf16[80,1280]{1,0:T(8,128)(2,1)S(1)}) custom-call(s32[1]{0:T(128)} %bitcast.xl, f32[160,1280]{1,0:T(8,128)} %get-tuple-element.38.refs_0_, bf16[160,1280]{1,0:T(8,128)(2,1)S(1)} %collective-permute-done.15.refs_1_, bf16[160,1280]{1,0:T(8,128)(2,1)S(1)} %collective-permute-done.16.refs_2_, ...), custom_call_target="tpu_custom_call" | custom-call | tf_op jit(solution)/shard_map/settle/pallas_call | solution.py:294
  120.1 0.1 collective-permute-start.18
  120.2 5.8 %collective-permute-done.18 = bf16[80,1280]{1,0:T(8,128)(2,1)S(1)} collective-permute-done((bf16[80,1280]{1,0:T(8,128)(2,1)S(1)}, bf16[80,1280]{1,0:T(8,128)(2,1)S(1)}, u32[]{:S(2)}, u32[]{:S(2)}) %collective-permute-start.18) | collective-permute-done | bytes 204832 | tf_op jit(solution)/shard_map/ppermute | solution.py:25
  126.1 1.7 %collective-permute-start.19 = (f32[40,1280]{1,0:T(8,128)S(1)}, f32[40,1280]{1,0:T(8,128)S(1)}, u32[]{:S(2)}, u32[]{:S(2)}) collective-permute-start(f32[40,1280]{1,0:T(8,128)S(1)} %dynamic-slice_bitcast_fusion), channel_id=1, source_target_pairs={{0,2},{2,0},{1,3},{3,1},{4,6},{6,4},{5,7},{7,5},{8,10},{10,8},{9,1... | collective-permute-start | bytes 614408 | tf_op jit(solution)/shard_map/ppermute | solution.py:25
  127.8 1.1 collective-permute-done.19
  129.0 0.8 maximum_bitcast_fusion
  (11 shorter events, 0.1 us)
Async XLA Ops:
  0.6 8.3 %collective-permute-start = (bf16[768,2560]{1,0:T(8,128)(2,1)}, bf16[768,2560]{1,0:T(8,128)(2,1)}, u32[]{:S(2)}, u32[]{:S(2)}) collective-permute-start(bf16[768,2560]{1,0:T(8,128)(2,1)} %h_own.1), channel_id=1, source_target_pairs={{0,2},{2,0},{1,3},{3,1},{4,6},{6,4},{5,7},{7,5},{8,10},{10,8},{9,1... | collective-permute-start | bytes 11796488 | tf_op jit(solution)/shard_map/ppermute | solution.py:25
  2.1 12.4 %collective-permute-start.1 = (bf16[768,2560]{1,0:T(8,128)(2,1)}, bf16[768,2560]{1,0:T(8,128)(2,1)}, u32[]{:S(2)}, u32[]{:S(2)}) collective-permute-start(bf16[768,2560]{1,0:T(8,128)(2,1)} %g_own.1), channel_id=1, source_target_pairs={{0,2},{2,0},{1,3},{3,1},{4,6},{6,4},{5,7},{7,5},{8,10},{10,8},{9,1... | collective-permute-start | bytes 11796488 | tf_op jit(solution)/shard_map/ppermute | solution.py:25
  22.6 24.6 %collective-permute-start.3 = (bf16[4,80,1280]{2,1,0:T(8,128)(2,1)}, bf16[4,80,1280]{2,1,0:T(8,128)(2,1)S(1)}, u32[]{:S(2)}, u32[]{:S(2)}) collective-permute-start(bf16[4,80,1280]{2,1,0:T(8,128)(2,1)} %get-tuple-element.23.after), channel_id=1, source_target_pairs={{0,34},{2,8},{10,40},{8,18},{16,50},{18,24},{26,56},{24,2},{34,64}... | collective-permute-start | bytes 2457608 | tf_op jit(solution)/shard_map/ppermute | solution.py:37
  24.3 22.9 %collective-permute-start.4 = (bf16[4,80,1280]{2,1,0:T(8,128)(2,1)}, bf16[4,80,1280]{2,1,0:T(8,128)(2,1)}, u32[]{:S(2)}, u32[]{:S(2)}) collective-permute-start(bf16[4,80,1280]{2,1,0:T(8,128)(2,1)} %get-tuple-element.28), channel_id=1, source_target_pairs={{0,64},{2,18},{10,74},{8,24},{16,80},{18,2},{26,90},{24,8},{34,98}... | collective-permute-start | bytes 2457608 | tf_op jit(solution)/shard_map/ppermute | solution.py:37
  26.9 20.3 %collective-permute-start.5 = (bf16[4,80,1280]{2,1,0:T(8,128)(2,1)}, bf16[4,80,1280]{2,1,0:T(8,128)(2,1)}, u32[]{:S(2)}, u32[]{:S(2)}) collective-permute-start(bf16[4,80,1280]{2,1,0:T(8,128)(2,1)} %get-tuple-element.29), channel_id=1, source_target_pairs={{0,98},{2,24},{10,104},{8,2},{16,114},{18,8},{26,120},{24,18},{34,... | collective-permute-start | bytes 2457608 | tf_op jit(solution)/shard_map/ppermute | solution.py:37
  44.2 23.0 %collective-permute-start.2 = (bf16[2,160,1280]{2,1,0:T(8,128)(2,1)}, bf16[2,160,1280]{2,1,0:T(8,128)(2,1)S(1)}, u32[]{:S(2)}, u32[]{:S(2)}) collective-permute-start(bf16[2,160,1280]{2,1,0:T(8,128)(2,1)} %get-tuple-element.26), channel_id=1, source_target_pairs={{0,34},{2,8},{10,40},{8,18},{16,50},{18,24},{26,56},{24,2},{34,64}... | collective-permute-start | bytes 2457608 | tf_op jit(solution)/shard_map/ppermute | solution.py:37
  44.6 27.3 %collective-permute-start.10 = (bf16[2,160,1280]{2,1,0:T(8,128)(2,1)}, bf16[2,160,1280]{2,1,0:T(8,128)(2,1)S(1)}, u32[]{:S(2)}, u32[]{:S(2)}) collective-permute-start(bf16[2,160,1280]{2,1,0:T(8,128)(2,1)} %get-tuple-element.34), channel_id=1, source_target_pairs={{0,98},{2,24},{10,104},{8,2},{16,114},{18,8},{26,120},{24,18},{34,... | collective-permute-start | bytes 2457608 | tf_op jit(solution)/shard_map/ppermute | solution.py:37
  50.8 11.3 %collective-permute-start.6 = (bf16[80,1280]{1,0:T(8,128)(2,1)}, bf16[80,1280]{1,0:T(8,128)(2,1)S(1)}, u32[]{:S(2)}, u32[]{:S(2)}) collective-permute-start(bf16[80,1280]{1,0:T(8,128)(2,1)} %get-tuple-element.30), channel_id=1, source_target_pairs={{0,10},{2,32},{10,16},{8,42},{16,26},{18,48},{26,0},{24,58},{34,40... | collective-permute-start | bytes 614408 | tf_op jit(solution)/shard_map/ppermute | solution.py:37
  52.5 9.6 %collective-permute-start.7 = (bf16[80,1280]{1,0:T(8,128)(2,1)S(1)}, bf16[80,1280]{1,0:T(8,128)(2,1)S(1)}, u32[]{:S(2)}, u32[]{:S(2)}) collective-permute-start(bf16[80,1280]{1,0:T(8,128)(2,1)S(1)} %get-tuple-element.31), channel_id=1, source_target_pairs={{0,16},{2,66},{10,26},{8,72},{16,0},{18,82},{26,10},{24,88},{34,50... | collective-permute-start | bytes 614408 | tf_op jit(solution)/shard_map/ppermute | solution.py:37
  55.8 6.3 %collective-permute-start.8 = (bf16[80,1280]{1,0:T(8,128)(2,1)S(1)}, bf16[80,1280]{1,0:T(8,128)(2,1)S(1)}, u32[]{:S(2)}, u32[]{:S(2)}) collective-permute-start(bf16[80,1280]{1,0:T(8,128)(2,1)S(1)} %get-tuple-element.32), channel_id=1, source_target_pairs={{0,26},{2,96},{10,0},{8,106},{16,10},{18,112},{26,16},{24,122},{34... | collective-permute-start | bytes 614408 | tf_op jit(solution)/shard_map/ppermute | solution.py:37
  63.3 12.2 %collective-permute-start.14 = (f32[40,1280]{1,0:T(8,128)S(1)}, f32[40,1280]{1,0:T(8,128)S(1)}, u32[]{:S(2)}, u32[]{:S(2)}) collective-permute-start(f32[40,1280]{1,0:T(8,128)S(1)} %get-tuple-element.37), channel_id=1, source_target_pairs={{0,4},{4,0},{1,5},{5,1},{2,6},{6,2},{3,7},{7,3},{8,12},{12,8},{9,1... | collective-permute-start | bytes 614408 | tf_op jit(solution)/shard_map/ppermute | solution.py:25
  64.6 13.8 %collective-permute-start.12 = (f32[40,1280]{1,0:T(8,128)S(1)}, f32[40,1280]{1,0:T(8,128)S(1)}, u32[]{:S(2)}, u32[]{:S(2)}) collective-permute-start(f32[40,1280]{1,0:T(8,128)S(1)} %get-tuple-element.36.a), channel_id=1, source_target_pairs={{0,1},{1,0},{2,3},{3,2},{4,5},{5,4},{6,7},{7,6},{8,9},{9,8},{10,11... | collective-permute-start | bytes 614408 | tf_op jit(solution)/shard_map/ppermute | solution.py:25
  67.0 11.5 %collective-permute-start.13 = (f32[40,1280]{1,0:T(8,128)S(1)}, f32[40,1280]{1,0:T(8,128)S(1)}, u32[]{:S(2)}, u32[]{:S(2)}) collective-permute-start(f32[40,1280]{1,0:T(8,128)S(1)} %get-tuple-element.37), channel_id=1, source_target_pairs={{0,5},{1,4},{4,1},{5,0},{2,7},{3,6},{6,3},{7,2},{8,13},{9,12},{12,... | collective-permute-start | bytes 614408 | tf_op jit(solution)/shard_map/ppermute | solution.py:503
  69.2 23.1 %collective-permute-start.9 = (bf16[4,160,1280]{2,1,0:T(8,128)(2,1)}, bf16[4,160,1280]{2,1,0:T(8,128)(2,1)S(1)}, u32[]{:S(2)}, u32[]{:S(2)}) collective-permute-start(bf16[4,160,1280]{2,1,0:T(8,128)(2,1)} %grow.2), channel_id=1, source_target_pairs={{0,34},{2,8},{10,40},{8,18},{16,50},{18,24},{26,56},{24,2},{34,64}... | collective-permute-start | bytes 4915208 | tf_op jit(solution)/shard_map/ppermute | solution.py:37
  73.9 25.5 %collective-permute-start.11 = (bf16[4,160,1280]{2,1,0:T(8,128)(2,1)}, bf16[4,160,1280]{2,1,0:T(8,128)(2,1)}, u32[]{:S(2)}, u32[]{:S(2)}) collective-permute-start(bf16[4,160,1280]{2,1,0:T(8,128)(2,1)} %grow.3), channel_id=1, source_target_pairs={{0,98},{2,24},{10,104},{8,2},{16,114},{18,8},{26,120},{24,18},{34,... | collective-permute-start | bytes 4915208 | tf_op jit(solution)/shard_map/ppermute | solution.py:37
  82.5 26.0 %all-to-all-start = ((bf16[128,16,128]{2,1,0:T(8,128)(2,1)}), bf16[128,16,128]{2,1,0:T(8,128)(2,1)S(1)}, u32[]{:S(2)}, u32[]{:S(2)}) async-start(bf16[128,16,128]{2,1,0:T(8,128)(2,1)} %left_product.1.refs_3_), calls=%async_computation | async-start | bytes 1048576 | tf_op jit(solution)/shard_map/all_to_all | solution.py:506
  103.7 9.6 %collective-permute-start.15 = (bf16[160,1280]{1,0:T(8,128)(2,1)S(1)}, bf16[160,1280]{1,0:T(8,128)(2,1)S(1)}, u32[]{:S(2)}, u32[]{:S(2)}) collective-permute-start(bf16[160,1280]{1,0:T(8,128)(2,1)S(1)} %get-tuple-element.39.late), channel_id=1, source_target_pairs={{0,10},{2,32},{10,16},{8,42},{16,26},{18,48},{26,0},{24,58},{34,40... | collective-permute-start | bytes 1228808 | tf_op jit(solution)/shard_map/ppermute | solution.py:37
  103.8 14.8 %collective-permute-start.16 = (bf16[160,1280]{1,0:T(8,128)(2,1)S(1)}, bf16[160,1280]{1,0:T(8,128)(2,1)S(1)}, u32[]{:S(2)}, u32[]{:S(2)}) collective-permute-start(bf16[160,1280]{1,0:T(8,128)(2,1)S(1)} %get-tuple-element.40), channel_id=1, source_target_pairs={{0,16},{2,66},{10,26},{8,72},{16,0},{18,82},{26,10},{24,88},{34,50... | collective-permute-start | bytes 1228808 | tf_op jit(solution)/shard_map/ppermute | solution.py:37
  108.5 10.1 %collective-permute-start.17 = (bf16[160,1280]{1,0:T(8,128)(2,1)S(1)}, bf16[160,1280]{1,0:T(8,128)(2,1)S(1)}, u32[]{:S(2)}, u32[]{:S(2)}) collective-permute-start(bf16[160,1280]{1,0:T(8,128)(2,1)S(1)} %get-tuple-element.41), channel_id=1, source_target_pairs={{0,26},{2,96},{10,0},{8,106},{16,10},{18,112},{26,16},{24,122},{34... | collective-permute-start | bytes 1228808 | tf_op jit(solution)/shard_map/ppermute | solution.py:37
  120.1 5.9 %collective-permute-start.18 = (bf16[80,1280]{1,0:T(8,128)(2,1)S(1)}, bf16[80,1280]{1,0:T(8,128)(2,1)S(1)}, u32[]{:S(2)}, u32[]{:S(2)}) collective-permute-start(bf16[80,1280]{1,0:T(8,128)(2,1)S(1)} %get-tuple-element.43), channel_id=1, source_target_pairs={{0,4},{4,0},{1,5},{5,1},{2,6},{6,2},{3,7},{7,3},{8,12},{12,8},{9,1... | collective-permute-start | bytes 614408 | tf_op jit(solution)/shard_map/ppermute | solution.py:25
  126.1 2.8 %collective-permute-start.19 = (f32[40,1280]{1,0:T(8,128)S(1)}, f32[40,1280]{1,0:T(8,128)S(1)}, u32[]{:S(2)}, u32[]{:S(2)}) collective-permute-start(f32[40,1280]{1,0:T(8,128)S(1)} %dynamic-slice_bitcast_fusion), channel_id=1, source_target_pairs={{0,2},{2,0},{1,3},{3,1},{4,6},{6,4},{5,7},{7,5},{8,10},{10,8},{9,1... | collective-permute-start | bytes 614408 | tf_op jit(solution)/shard_map/ppermute | solution.py:25

commit v16 on v15

--- a/solution.py
+++ b/solution.py
@@ -245,13 +245,14 @@
 
 def fold_kernel(count, me, *refs):
     own, *others = refs[-6:-2]
-    held, sem = refs[-2:]
-    copy = pltpu.make_async_copy(refs[0], held, sem)
-    copy.start()
-    copy.wait()
-    for r, out in enumerate([own, *others]):
+    held, sems = refs[-2:]
+    steps = [(1, others[0]), (2, others[1]), (3, others[2]), (0, own)]
+    for r, _ in steps:
+        pltpu.make_async_copy(refs[0].at[(me[0] + r) & 3], held.at[r], sems.at[r]).start()
+    for r, out in steps:
+        wait_all(held.at[r], sems.at[r])
         at = (me[0] + r) & 3
-        out[...] = add(held[at], *[part[at] for part in refs[1:count]]).astype(out.dtype)
+        out[...] = add(held[r], *[part[at] for part in refs[1:count]]).astype(out.dtype)
 
 
 def fold(me, parts, *after):
@@ -268,7 +269,7 @@
             + [VMEM] * (len(parts) - 1)
             + [ANY] * len(after),
             out_specs=[whole] + [VMEM] * 3,
-            scratch_shapes=[pltpu.VMEM((4, rows, width), BF), pltpu.SemaphoreType.DMA],
+            scratch_shapes=[pltpu.VMEM((4, rows, width), BF), pltpu.SemaphoreType.DMA((4,))],
         ),
         compiler_params=pltpu.CompilerParams(vmem_limit_bytes=12 * 2**20),
         cost_estimate=pl.CostEstimate(flops=0, bytes_accessed=0, transcendentals=0),
@@ -309,35 +310,54 @@
     )(xl, *parts, *after)
 
 
-def grow_kernel(side, x, received, *refs):
-    out, held, sems, out_sem = refs[-4:]
-    for k in range(2):
-        pltpu.make_async_copy(x.at[side * 2 + k], held.at[k], sems.at[k]).start()
-    for k in range(2):
-        wait_all(held.at[k], sems.at[k])
-        held[k] = add(held[k], received[k]).astype(BF)
-        pltpu.make_async_copy(held.at[k], out.at[side * 2 + k], out_sem).start()
+def grow_kernel(right, left, from_left, from_right, *refs):
+    out_right, out_left, held, sems, out_sem = refs[-5:]
+    jobs = [(right, 0, from_left, 0, out_right), (left, 2, from_right, 0, out_left)]
+    jobs += [(right, 1, from_left, 1, out_right), (left, 3, from_right, 1, out_left)]
+    for n, (x, at, _, _, _) in enumerate(jobs):
+        pltpu.make_async_copy(x.at[at], held.at[n], sems.at[n]).start()
+    for n, (_, at, received, k, out) in enumerate(jobs):
+        wait_all(held.at[n], sems.at[n])
+        held[n] = add(held[n], received[k]).astype(BF)
+        pltpu.make_async_copy(held.at[n], out.at[at], out_sem).start()
     wait_all(held, out_sem)
 
 
-def grow(x, received, side, *after):
+def grow(right, left, from_left, from_right, *after):
     hbm = pl.BlockSpec(memory_space=pltpu.HBM)
     return pl.pallas_call(
-        functools.partial(grow_kernel, side),
-        out_shape=pltpu.HBM(x.shape, x.dtype),
+        grow_kernel,
+        out_shape=[pltpu.HBM(x.shape, x.dtype) for x in (right, left)],
         grid=(1,),
-        in_specs=[hbm, VMEM] + [ANY] * len(after),
-        out_specs=hbm,
+        in_specs=[hbm, hbm, VMEM, VMEM] + [ANY] * len(after),
+        out_specs=[hbm, hbm],
         scratch_shapes=[
-            pltpu.VMEM(received.shape, x.dtype),
-            pltpu.SemaphoreType.DMA((2,)),
+            pltpu.VMEM(right.shape, right.dtype),
+            pltpu.SemaphoreType.DMA((4,)),
             pltpu.SemaphoreType.DMA,
         ],
-        input_output_aliases={0: 0},
+        input_output_aliases={0: 0, 1: 1},
         compiler_params=pltpu.CompilerParams(vmem_limit_bytes=8 * 2**20),
         cost_estimate=pl.CostEstimate(flops=0, bytes_accessed=0, transcendentals=0),
         name="grow",
-    )(in_hbm(x), received, *after)
+    )(in_hbm(right), in_hbm(left), from_left, from_right, *after)
+
+
+def gate_kernel(x, after, out):
+    del x, after, out
+
+
+def gate(x, after):
+    return pl.pallas_call(
+        gate_kernel,
+        out_shape=pltpu.HBM(x.shape, x.dtype),
+        in_specs=[pl.BlockSpec(memory_space=pltpu.HBM), ANY],
+        out_specs=pl.BlockSpec(memory_space=pltpu.HBM),
+        input_output_aliases={0: 0},
+        compiler_params=pltpu.CompilerParams(vmem_limit_bytes=2**20),
+        cost_estimate=pl.CostEstimate(flops=0, bytes_accessed=0, transcendentals=0),
+        name="gate",
+    )(in_hbm(x), after)
 
 
 def fetch_tiles(step, source, held, sems):
@@ -399,12 +419,12 @@
     total = pltpu.VMEM((2 * rows, half), F32)
     return pl.pallas_call(
         functools.partial(left_kernel, own),
-        out_shape=total if own else pltpu.VMEM((128, 16, 128), BF),
+        out_shape=total if own else pltpu.HBM((128, 16, 128), BF),
         grid_spec=pltpu.PrefetchScalarGridSpec(
             num_scalar_prefetch=1,
             grid=(2,),
             in_specs=[VMEM, VMEM, pl.BlockSpec(memory_space=pltpu.HBM)] + [VMEM] * (not own),
-            out_specs=VMEM,
+            out_specs=VMEM if own else pl.BlockSpec((128, 16, 128), lambda k, p: (0, 0, 0)),
             scratch_shapes=[total]
             + [pltpu.VMEM((32, 16, 128), F32)] * (not own)
             + [pltpu.VMEM((2, TILE, half), BF), pltpu.SemaphoreType.DMA((2,))],
@@ -495,18 +515,18 @@
 
     m, *m_pieces = fold(second_me, m_parts, in_hbm(f_own))
     m_received = second_sends(m_pieces)
-    right = grow(right, from_left, 0, *m_received)
-    left = grow(left, from_right, 1, *m_received)
+    right, left = grow(right, left, from_left, from_right, *m_received)
     f_parts = [f_own, turn(right, 1, 0), turn(left, -1, 0)]
 
     mine, theirs = settle(my_xl, [in_hbm(m), *m_received], F32)
     across = lax.ppermute(theirs, ("xl", "o"), [(i, 3 - i) for i in range(4)])
     products = left_product(place, mine, shift(theirs, "xl", 1), left_inverse)
     products = left_product(place, shift(mine, "o", 1), across, left_inverse, products)
+    f, *f_pieces = fold(second_me, f_parts, in_hbm(products))
+    products = gate(products, f_pieces[0])
     blocks = lax.all_to_all(products, ("o", "c", "z", "y", "xl"), 0, 0, tiled=True)
-    f, *f_pieces = fold(second_me, f_parts, products)
-    update = right_product(place, blocks, right_inverse, f_pieces[0])
-    f_mine, f_theirs = settle(my_xl, [in_hbm(f), *second_sends(f_pieces)], BF, in_hbm(update))
+    f_mine, f_theirs = settle(my_xl, [in_hbm(f), *second_sends(f_pieces)], BF)
+    update = right_product(place, blocks, right_inverse, f_theirs)
 
     f = add(f_mine, shift(f_theirs, "xl", 1))
     f = f * jnp.where(first, 1.0 / token_total, 1.0).astype(F32)

time: 130 us -> 142 us (1.092)
  waiting for transfers between devices: 32.8 us -> 48.1 us
  Pallas kernels: 55.6 us -> 52.2 us
    all_to_all x1, waiting for transfers between devices: 0.01 us -> 12.6 us  [per_device(): lax.all_to_all(products, ('o', 'c', 'z', 'y', 'xl'), 0, 0, tiled=True)]
    ppermute x13, waiting for transfers between devices: 19 us -> 26.9 us  [turn(): return lax.ppermute(x, ('z', 'y', 'c'), pairs)]
    ppermute x6, waiting for transfers between devices: 13.7 us -> 6.77 us  [shift(): return lax.ppermute(x, axis, [(i, (i + step) % size) for i in range(size)])]
    pallas_call x2, Pallas kernels: 7.87 us -> 4.74 us  [fold(): pl.pallas_call(functools.partial(fold_kernel, len(parts)), out_shape=[plt...]
    ppermute x1, waiting for transfers between devices: 0.1 us -> 1.78 us  [per_device(): across = lax.ppermute(theirs, ('xl', 'o'), [(i, 3 - i) for i in range(4)])]
  transfers between devices with their start and end apart: 21 -> 21, of which waited for: 10 -> 10; matrix products, arithmetic and copies ran while one was open for 0% -> 0% of each run, Pallas kernels for 35% -> 28%
where the time goes in v16:
time: 142 us
  Pallas kernels  52.2 us (37%)
  waiting for transfers between devices  48.1 us (34%)
  starting transfers between devices  39.6 us (28%)
    ppermute x13, waiting for transfers between devices, turn(): return lax.ppermute(x, ('z', 'y', 'c'), pairs)  26.9 us
    ppermute x13, starting transfers between devices, turn(): return lax.ppermute(x, ('z', 'y', 'c'), pairs)  23.4 us
    pallas_call x1, Pallas kernels, factor_term(): pl.pallas_call(factor_kernel, out_shape=[out, out, side, side, out], grid...  15.9 us
    all_to_all x1, waiting for transfers between devices, per_device(): lax.all_to_all(products, ('o', 'c', 'z', 'y', 'xl'), 0, 0, tiled=True)  12.6 us
    all_to_all x1, starting transfers between devices, per_device(): lax.all_to_all(products, ('o', 'c', 'z', 'y', 'xl'), 0, 0, tiled=True)  9.48 us
    pallas_call x1, Pallas kernels, cross_term(): pl.pallas_call(cross_kernel, out_shape=[out] * 4, grid_spec=pltpu.Prefetc...  8.31 us
    pallas_call x2, Pallas kernels, left_product(): pl.pallas_call(functools.partial(left_kernel, own), out_shape=total if ow...  6.97 us
    ppermute x6, waiting for transfers between devices, shift(): return lax.ppermute(x, axis, [(i, (i + step) % size) for i in range(size)])  6.77 us
  transfers between devices with their start and end apart: 21, of which 10 were waited for; matrix products, arithmetic and copies ran while one was open for 0% of the time, Pallas kernels for 28%

profile of v16, /device:TPU:1, one launch (start us, length us, event | category | flops | bytes accessed | tf_op | source)
XLA Modules:
  0.0 141.6 jit_solution(17507388709064440409)
XLA Ops:
  0.6 1.5 %collective-permute-start = (bf16[768,2560]{1,0:T(8,128)(2,1)}, bf16[768,2560]{1,0:T(8,128)(2,1)}, u32[]{:S(2)}, u32[]{:S(2)}) collective-permute-start(bf16[768,2560]{1,0:T(8,128)(2,1)} %h_own.1), channel_id=1, source_target_pairs={{0,2},{2,0},{1,3},{3,1},{4,6},{6,4},{5,7},{7,5},{8,10},{10,8},{9,1... | collective-permute-start | bytes 11796488 | tf_op jit(solution)/shard_map/ppermute | solution.py:25
  2.1 0.1 collective-permute-start.1
  2.2 0.1 pad_add_fusion.place
  2.3 5.4 %cross_own.1.partial = f32[1280,1280]{1,0:T(8,128)S(1)} custom-call(s32[4]{0:T(128)S(1)} %pad_add_fusion.place, bf16[768,2560]{1,0:T(8,128)(2,1)} %g_own.1, bf16[768,2560]{1,0:T(8,128)(2,1)} %h_own.1), custom_call_target="tpu_custom_call" | custom-call | flops 2516582400 | bytes 7864320 | tf_op jit(solution)/shard_map/cross_own/pallas_call | solution.py:125
  7.7 1.1 collective-permute-done.b.h_next
  8.9 5.6 %collective-permute-done.1.a.g_next = bf16[768,2560]{1,0:T(8,128)(2,1)} collective-permute-done((bf16[768,2560]{1,0:T(8,128)(2,1)}, bf16[768,2560]{1,0:T(8,128)(2,1)}, u32[]{:S(2)}, u32[]{:S(2)}) %collective-permute-start.1) | collective-permute-done | bytes 3932192 | tf_op jit(solution)/shard_map/ppermute | solution.py:25
  14.5 8.3 %cross_term.1 = (bf16[4,80,1280]{2,1,0:T(8,128)(2,1)}, bf16[4,80,1280]{2,1,0:T(8,128)(2,1)}, bf16[4,80,1280]{2,1,0:T(8,128)(2,1)}, bf16[4,80,1280]{2,1,0:T(8,128)(2,1)}) custom-call(s32[4]{0:T(128)S(1)} %pad_add_fusion.place, bf16[768,2560]{1,0:T(8,128)(2,1)} %collective-permute-done.1.a.g_next, bf16[768,2560]{1,0:T(8,128)(2,1)} %collective-permute-done.b.h_next, ...), custom_call_target="tpu_custom_call" | custom-call | flops 2516582400 | bytes 9830400 | tf_op jit(solution)/shard_map/cross_term/pallas_call | solution.py:151
  22.8 1.7 %collective-permute-start.4 = (bf16[4,80,1280]{2,1,0:T(8,128)(2,1)}, bf16[4,80,1280]{2,1,0:T(8,128)(2,1)S(1)}, u32[]{:S(2)}, u32[]{:S(2)}) collective-permute-start(bf16[4,80,1280]{2,1,0:T(8,128)(2,1)} %get-tuple-element.25.after), channel_id=1, source_target_pairs={{0,34},{2,8},{10,40},{8,18},{16,50},{18,24},{26,56},{24,2},{34,64}... | collective-permute-start | bytes 2457608 | tf_op jit(solution)/shard_map/ppermute | solution.py:37
  24.5 2.6 %collective-permute-start.5 = (bf16[4,80,1280]{2,1,0:T(8,128)(2,1)}, bf16[4,80,1280]{2,1,0:T(8,128)(2,1)S(1)}, u32[]{:S(2)}, u32[]{:S(2)}) collective-permute-start(bf16[4,80,1280]{2,1,0:T(8,128)(2,1)} %get-tuple-element.32), channel_id=1, source_target_pairs={{0,64},{2,18},{10,74},{8,24},{16,80},{18,2},{26,90},{24,8},{34,98}... | collective-permute-start | bytes 2457608 | tf_op jit(solution)/shard_map/ppermute | solution.py:37
  27.2 1.4 collective-permute-start.6
  28.5 15.9 %factor_term.1 = (bf16[4,160,1280]{2,1,0:T(8,128)(2,1)}, bf16[4,160,1280]{2,1,0:T(8,128)(2,1)}, bf16[2,160,1280]{2,1,0:T(8,128)(2,1)}, bf16[2,160,1280]{2,1,0:T(8,128)(2,1)}, bf16[4,160,1280]{2,1,0:T(8,128)(2,1)}) custom-call(s32[4]{0:T(128)S(1)} %pad_add_fusion.place, bf16[768,2560]{1,0:T(8,128)(2,1)} %h_own.1, bf16[768,2560]{1,0:T(8,128)(2,1)} %g_own.1, ...), custom_call_target="tpu_custom_call" | custom-call | flops 10066329600 | bytes 15728640 | tf_op jit(solution)/shard_map/factor_term/pallas_call | solution.py:214
  44.4 0.4 collective-permute-start.2
  44.8 2.6 %collective-permute-start.3 = (bf16[2,160,1280]{2,1,0:T(8,128)(2,1)}, bf16[2,160,1280]{2,1,0:T(8,128)(2,1)}, u32[]{:S(2)}, u32[]{:S(2)}) collective-permute-start(bf16[2,160,1280]{2,1,0:T(8,128)(2,1)} %get-tuple-element.30), channel_id=1, source_target_pairs={{0,98},{2,24},{10,104},{8,2},{16,114},{18,8},{26,120},{24,18},{34,... | collective-permute-start | bytes 2457608 | tf_op jit(solution)/shard_map/ppermute | solution.py:37
  47.4 0.0 collective-permute-done.4.refs_1_
  47.4 0.0 collective-permute-done.5.refs_2_
  47.4 0.0 collective-permute-done.6.refs_3_
  47.4 2.2 %fold.2 = (f32[80,1280]{1,0:T(8,128)}, bf16[80,1280]{1,0:T(8,128)(2,1)}, bf16[80,1280]{1,0:T(8,128)(2,1)}, bf16[80,1280]{1,0:T(8,128)(2,1)S(1)}) custom-call(s32[1]{0:T(128)} %bitcast.1.me, bf16[4,80,1280]{2,1,0:T(8,128)(2,1)} %get-tuple-element.31.refs_0_, bf16[4,80,1280]{2,1,0:T(8,128)(2,1)S(1)} %collective-permute-done.4.refs_1_, ...), custom_call_target="tpu_custom_call" | custom-call | tf_op jit(solution)/shard_map/fold/pallas_call | solution.py:261
  49.7 1.7 %collective-permute-start.7 = (bf16[80,1280]{1,0:T(8,128)(2,1)}, bf16[80,1280]{1,0:T(8,128)(2,1)S(1)}, u32[]{:S(2)}, u32[]{:S(2)}) collective-permute-start(bf16[80,1280]{1,0:T(8,128)(2,1)} %get-tuple-element.34), channel_id=1, source_target_pairs={{0,10},{2,32},{10,16},{8,42},{16,26},{18,48},{26,0},{24,58},{34,40... | collective-permute-start | bytes 614408 | tf_op jit(solution)/shard_map/ppermute | solution.py:37
  51.3 3.3 %collective-permute-start.8 = (bf16[80,1280]{1,0:T(8,128)(2,1)}, bf16[80,1280]{1,0:T(8,128)(2,1)S(1)}, u32[]{:S(2)}, u32[]{:S(2)}) collective-permute-start(bf16[80,1280]{1,0:T(8,128)(2,1)} %get-tuple-element.35), channel_id=1, source_target_pairs={{0,16},{2,66},{10,26},{8,72},{16,0},{18,82},{26,10},{24,88},{34,50... | collective-permute-start | bytes 614408 | tf_op jit(solution)/shard_map/ppermute | solution.py:37
  54.6 1.4 collective-permute-start.9
  56.0 5.9 %collective-permute-done.7.refs_0_.refs_1_ = bf16[80,1280]{1,0:T(8,128)(2,1)S(1)} collective-permute-done((bf16[80,1280]{1,0:T(8,128)(2,1)}, bf16[80,1280]{1,0:T(8,128)(2,1)S(1)}, u32[]{:S(2)}, u32[]{:S(2)}) %collective-permute-start.7) | collective-permute-done | bytes 204832 | tf_op jit(solution)/shard_map/ppermute | solution.py:37
  61.8 0.6 collective-permute-done.9.refs_2_.refs_3_
  62.4 1.2 settle.2
  63.6 1.3 collective-permute-start.14
  64.8 2.5 %collective-permute-start.12 = (f32[40,1280]{1,0:T(8,128)S(1)}, f32[40,1280]{1,0:T(8,128)S(1)}, u32[]{:S(2)}, u32[]{:S(2)}) collective-permute-start(f32[40,1280]{1,0:T(8,128)S(1)} %get-tuple-element.40.a), channel_id=1, source_target_pairs={{0,1},{1,0},{2,3},{3,2},{4,5},{5,4},{6,7},{7,6},{8,9},{9,8},{10,11... | collective-permute-start | bytes 614408 | tf_op jit(solution)/shard_map/ppermute | solution.py:25
  67.4 0.1 collective-permute-start.13
  67.5 3.5 %grow.1 = (bf16[4,160,1280]{2,1,0:T(8,128)(2,1)}, bf16[4,160,1280]{2,1,0:T(8,128)(2,1)}) custom-call(bf16[4,160,1280]{2,1,0:T(8,128)(2,1)} %get-tuple-element.27.right, bf16[4,160,1280]{2,1,0:T(8,128)(2,1)} %get-tuple-element.28.left, bf16[2,160,1280]{2,1,0:T(8,128)(2,1)S(1)} %collective-permute-done.2.from_left, ...), custom_call_target="tpu_custom_call", output_to_operand_aliasing={{0}: (0, {}), {1}: (1, {})} | custom-call | tf_op jit(solution)/shard_map/grow/pallas_call | solution.py:328
  71.0 2.6 %collective-permute-start.10 = (bf16[4,160,1280]{2,1,0:T(8,128)(2,1)}, bf16[4,160,1280]{2,1,0:T(8,128)(2,1)S(1)}, u32[]{:S(2)}, u32[]{:S(2)}) collective-permute-start(bf16[4,160,1280]{2,1,0:T(8,128)(2,1)} %get-tuple-element.37), channel_id=1, source_target_pairs={{0,34},{2,8},{10,40},{8,18},{16,50},{18,24},{26,56},{24,2},{34,64}... | collective-permute-start | bytes 4915208 | tf_op jit(solution)/shard_map/ppermute | solution.py:37
  73.7 1.3 collective-permute-start.11
  74.9 2.9 %left_own.1.rest_0_ = f32[80,1280]{1,0:T(8,128)S(1)} custom-call(s32[4]{0:T(128)S(1)} %pad_add_fusion.place, f32[40,1280]{1,0:T(8,128)S(1)} %get-tuple-element.40.a, f32[40,1280]{1,0:T(8,128)S(1)} %collective-permute-done.14.b, bf16[2560,1280]{1,0:T(8,128)(2,1)} %left.3), custom_call_target="tpu_custom_call" | custom-call | tf_op jit(solution)/shard_map/left_own/pallas_call | solution.py:420
  77.9 1.8 %collective-permute-done.13.b = f32[40,1280]{1,0:T(8,128)S(1)} collective-permute-done((f32[40,1280]{1,0:T(8,128)S(1)}, f32[40,1280]{1,0:T(8,128)S(1)}, u32[]{:S(2)}, u32[]{:S(2)}) %collective-permute-start.13) | collective-permute-done | bytes 204832 | tf_op jit(solution)/shard_map/ppermute | solution.py:522
  79.7 4.0 %left_product.1.refs_3_.x = bf16[128,16,128]{2,1,0:T(8,128)(2,1)} custom-call(s32[4]{0:T(128)S(1)} %pad_add_fusion.place, f32[40,1280]{1,0:T(8,128)S(1)} %collective-permute-done.12.a, f32[40,1280]{1,0:T(8,128)S(1)} %collective-permute-done.13.b, bf16[2560,1280]{1,0:T(8,128)(2,1)} %left.3, f32[80,1280]{1,0:T(8,128)S(1)} %left_own.1.rest_0_), custom_call_target="tpu_custom_call" | custom-call | flops 16777216000 | tf_op jit(solution)/shard_map/left_product/pallas_call | solution.py:420
  83.7 10.0 %collective-permute-done.10.refs_1_ = bf16[4,160,1280]{2,1,0:T(8,128)(2,1)S(1)} collective-permute-done((bf16[4,160,1280]{2,1,0:T(8,128)(2,1)}, bf16[4,160,1280]{2,1,0:T(8,128)(2,1)S(1)}, u32[]{:S(2)}, u32[]{:S(2)}) %collective-permute-start.10) | collective-permute-done | bytes 1638432 | tf_op jit(solution)/shard_map/ppermute | solution.py:37
  93.7 0.7 collective-permute-done.11.refs_2_
  94.4 2.5 %fold.3 = (f32[160,1280]{1,0:T(8,128)}, bf16[160,1280]{1,0:T(8,128)(2,1)S(1)}, bf16[160,1280]{1,0:T(8,128)(2,1)S(1)}, bf16[160,1280]{1,0:T(8,128)(2,1)S(1)}) custom-call(s32[1]{0:T(128)} %bitcast.1.me, bf16[4,160,1280]{2,1,0:T(8,128)(2,1)} %get-tuple-element.26.refs_4_.refs_0_, bf16[4,160,1280]{2,1,0:T(8,128)(2,1)S(1)} %collective-permute-done.10.refs_1_, ...), custom_call_target="tpu_custom_call" | custom-call | tf_op jit(solution)/shard_map/fold/pallas_call | solution.py:261
  97.0 0.1 collective-permute-start.15
  97.0 4.3 %collective-permute-start.16 = (bf16[160,1280]{1,0:T(8,128)(2,1)S(1)}, bf16[160,1280]{1,0:T(8,128)(2,1)S(1)}, u32[]{:S(2)}, u32[]{:S(2)}) collective-permute-start(bf16[160,1280]{1,0:T(8,128)(2,1)S(1)} %get-tuple-element.44), channel_id=1, source_target_pairs={{0,16},{2,66},{10,26},{8,72},{16,0},{18,82},{26,10},{24,88},{34,50... | collective-permute-start | bytes 1228808 | tf_op jit(solution)/shard_map/ppermute | solution.py:37
  101.3 0.1 collective-permute-start.17
  101.4 4.4 %collective-permute-done.15.refs_1_ = bf16[160,1280]{1,0:T(8,128)(2,1)S(1)} collective-permute-done((bf16[160,1280]{1,0:T(8,128)(2,1)S(1)}, bf16[160,1280]{1,0:T(8,128)(2,1)S(1)}, u32[]{:S(2)}, u32[]{:S(2)}) %collective-permute-start.15) | collective-permute-done | bytes 409632 | tf_op jit(solution)/shard_map/ppermute | solution.py:37
  105.8 5.3 %collective-permute-done.16.refs_2_ = bf16[160,1280]{1,0:T(8,128)(2,1)S(1)} collective-permute-done((bf16[160,1280]{1,0:T(8,128)(2,1)S(1)}, bf16[160,1280]{1,0:T(8,128)(2,1)S(1)}, u32[]{:S(2)}, u32[]{:S(2)}) %collective-permute-start.16) | collective-permute-done | bytes 409632 | tf_op jit(solution)/shard_map/ppermute | solution.py:37
  111.1 0.0 collective-permute-done.17.refs_3_
  111.2 1.5 %settle.3 = (f32[80,1280]{1,0:T(8,128)S(1)}, bf16[80,1280]{1,0:T(8,128)(2,1)S(1)}) custom-call(s32[1]{0:T(128)} %bitcast.xl, f32[160,1280]{1,0:T(8,128)} %get-tuple-element.42.refs_0_, bf16[160,1280]{1,0:T(8,128)(2,1)S(1)} %collective-permute-done.15.refs_1_, bf16[160,1280]{1,0:T(8,128)(2,1)S(1)} %collective-permute-done.16.refs_2_, ...), custom_call_target="tpu_custom_call" | custom-call | tf_op jit(solution)/shard_map/settle/pallas_call | solution.py:295
  112.6 0.1 collective-permute-start.18
  112.7 9.5 %all-to-all-start = ((bf16[128,16,128]{2,1,0:T(8,128)(2,1)}), bf16[128,16,128]{2,1,0:T(8,128)(2,1)S(1)}, u32[]{:S(2)}, u32[]{:S(2)}) async-start(bf16[128,16,128]{2,1,0:T(8,128)(2,1)} %gate.1), calls=%async_computation | async-start | bytes 1048576 | tf_op jit(solution)/shard_map/all_to_all | solution.py:527
  122.3 1.1 collective-permute-start.19
  123.5 12.6 %all-to-all-done.blocks = bf16[128,16,128]{2,1,0:T(8,128)(2,1)S(1)} async-done(((bf16[128,16,128]{2,1,0:T(8,128)(2,1)}), bf16[128,16,128]{2,1,0:T(8,128)(2,1)S(1)}, u32[]{:S(2)}, u32[]{:S(2)}) %all-to-all-start) | async-done | bytes 524320 | tf_op jit(solution)/shard_map/all_to_all | solution.py:527
  136.1 4.7 %right_product.1 = f32[40,1280]{1,0:T(8,128)} custom-call(s32[4]{0:T(128)S(1)} %pad_add_fusion.place, bf16[128,16,128]{2,1,0:T(8,128)(2,1)S(1)} %all-to-all-done.blocks, bf16[2560,1280]{1,0:T(8,128)(2,1)} %right.1, bf16[80,1280]{1,0:T(8,128)(2,1)S(1)} %get-tuple-element.47.late), custom_call_target="tpu_custom_call" | custom-call | flops 41943040000 | bytes 6553600 | tf_op jit(solution)/shard_map/right_product/pallas_call | solution.py:462
  140.9 0.8 maximum_bitcast_fusion
  (11 shorter events, 0.1 us)
Async XLA Ops:
  0.6 8.3 %collective-permute-start = (bf16[768,2560]{1,0:T(8,128)(2,1)}, bf16[768,2560]{1,0:T(8,128)(2,1)}, u32[]{:S(2)}, u32[]{:S(2)}) collective-permute-start(bf16[768,2560]{1,0:T(8,128)(2,1)} %h_own.1), channel_id=1, source_target_pairs={{0,2},{2,0},{1,3},{3,1},{4,6},{6,4},{5,7},{7,5},{8,10},{10,8},{9,1... | collective-permute-start | bytes 11796488 | tf_op jit(solution)/shard_map/ppermute | solution.py:25
  2.1 12.4 %collective-permute-start.1 = (bf16[768,2560]{1,0:T(8,128)(2,1)}, bf16[768,2560]{1,0:T(8,128)(2,1)}, u32[]{:S(2)}, u32[]{:S(2)}) collective-permute-start(bf16[768,2560]{1,0:T(8,128)(2,1)} %g_own.1), channel_id=1, source_target_pairs={{0,2},{2,0},{1,3},{3,1},{4,6},{6,4},{5,7},{7,5},{8,10},{10,8},{9,1... | collective-permute-start | bytes 11796488 | tf_op jit(solution)/shard_map/ppermute | solution.py:25
  22.8 24.6 %collective-permute-start.4 = (bf16[4,80,1280]{2,1,0:T(8,128)(2,1)}, bf16[4,80,1280]{2,1,0:T(8,128)(2,1)S(1)}, u32[]{:S(2)}, u32[]{:S(2)}) collective-permute-start(bf16[4,80,1280]{2,1,0:T(8,128)(2,1)} %get-tuple-element.25.after), channel_id=1, source_target_pairs={{0,34},{2,8},{10,40},{8,18},{16,50},{18,24},{26,56},{24,2},{34,64}... | collective-permute-start | bytes 2457608 | tf_op jit(solution)/shard_map/ppermute | solution.py:37
  24.5 22.9 %collective-permute-start.5 = (bf16[4,80,1280]{2,1,0:T(8,128)(2,1)}, bf16[4,80,1280]{2,1,0:T(8,128)(2,1)S(1)}, u32[]{:S(2)}, u32[]{:S(2)}) collective-permute-start(bf16[4,80,1280]{2,1,0:T(8,128)(2,1)} %get-tuple-element.32), channel_id=1, source_target_pairs={{0,64},{2,18},{10,74},{8,24},{16,80},{18,2},{26,90},{24,8},{34,98}... | collective-permute-start | bytes 2457608 | tf_op jit(solution)/shard_map/ppermute | solution.py:37
  27.2 20.3 %collective-permute-start.6 = (bf16[4,80,1280]{2,1,0:T(8,128)(2,1)}, bf16[4,80,1280]{2,1,0:T(8,128)(2,1)S(1)}, u32[]{:S(2)}, u32[]{:S(2)}) collective-permute-start(bf16[4,80,1280]{2,1,0:T(8,128)(2,1)} %get-tuple-element.33), channel_id=1, source_target_pairs={{0,98},{2,24},{10,104},{8,2},{16,114},{18,8},{26,120},{24,18},{34,... | collective-permute-start | bytes 2457608 | tf_op jit(solution)/shard_map/ppermute | solution.py:37
  44.4 23.1 %collective-permute-start.2 = (bf16[2,160,1280]{2,1,0:T(8,128)(2,1)}, bf16[2,160,1280]{2,1,0:T(8,128)(2,1)S(1)}, u32[]{:S(2)}, u32[]{:S(2)}) collective-permute-start(bf16[2,160,1280]{2,1,0:T(8,128)(2,1)} %get-tuple-element.29), channel_id=1, source_target_pairs={{0,34},{2,8},{10,40},{8,18},{16,50},{18,24},{26,56},{24,2},{34,64}... | collective-permute-start | bytes 2457608 | tf_op jit(solution)/shard_map/ppermute | solution.py:37
  44.8 22.7 %collective-permute-start.3 = (bf16[2,160,1280]{2,1,0:T(8,128)(2,1)}, bf16[2,160,1280]{2,1,0:T(8,128)(2,1)}, u32[]{:S(2)}, u32[]{:S(2)}) collective-permute-start(bf16[2,160,1280]{2,1,0:T(8,128)(2,1)} %get-tuple-element.30), channel_id=1, source_target_pairs={{0,98},{2,24},{10,104},{8,2},{16,114},{18,8},{26,120},{24,18},{34,... | collective-permute-start | bytes 2457608 | tf_op jit(solution)/shard_map/ppermute | solution.py:37
  49.7 12.2 %collective-permute-start.7 = (bf16[80,1280]{1,0:T(8,128)(2,1)}, bf16[80,1280]{1,0:T(8,128)(2,1)S(1)}, u32[]{:S(2)}, u32[]{:S(2)}) collective-permute-start(bf16[80,1280]{1,0:T(8,128)(2,1)} %get-tuple-element.34), channel_id=1, source_target_pairs={{0,10},{2,32},{10,16},{8,42},{16,26},{18,48},{26,0},{24,58},{34,40... | collective-permute-start | bytes 614408 | tf_op jit(solution)/shard_map/ppermute | solution.py:37
  51.3 10.5 %collective-permute-start.8 = (bf16[80,1280]{1,0:T(8,128)(2,1)}, bf16[80,1280]{1,0:T(8,128)(2,1)S(1)}, u32[]{:S(2)}, u32[]{:S(2)}) collective-permute-start(bf16[80,1280]{1,0:T(8,128)(2,1)} %get-tuple-element.35), channel_id=1, source_target_pairs={{0,16},{2,66},{10,26},{8,72},{16,0},{18,82},{26,10},{24,88},{34,50... | collective-permute-start | bytes 614408 | tf_op jit(solution)/shard_map/ppermute | solution.py:37
  54.6 7.8 %collective-permute-start.9 = (bf16[80,1280]{1,0:T(8,128)(2,1)S(1)}, bf16[80,1280]{1,0:T(8,128)(2,1)S(1)}, u32[]{:S(2)}, u32[]{:S(2)}) collective-permute-start(bf16[80,1280]{1,0:T(8,128)(2,1)S(1)} %get-tuple-element.36), channel_id=1, source_target_pairs={{0,26},{2,96},{10,0},{8,106},{16,10},{18,112},{26,16},{24,122},{34... | collective-permute-start | bytes 614408 | tf_op jit(solution)/shard_map/ppermute | solution.py:37
  63.6 11.4 %collective-permute-start.14 = (f32[40,1280]{1,0:T(8,128)S(1)}, f32[40,1280]{1,0:T(8,128)S(1)}, u32[]{:S(2)}, u32[]{:S(2)}) collective-permute-start(f32[40,1280]{1,0:T(8,128)S(1)} %get-tuple-element.41), channel_id=1, source_target_pairs={{0,4},{4,0},{1,5},{5,1},{2,6},{6,2},{3,7},{7,3},{8,12},{12,8},{9,1... | collective-permute-start | bytes 614408 | tf_op jit(solution)/shard_map/ppermute | solution.py:25
  64.8 13.1 %collective-permute-start.12 = (f32[40,1280]{1,0:T(8,128)S(1)}, f32[40,1280]{1,0:T(8,128)S(1)}, u32[]{:S(2)}, u32[]{:S(2)}) collective-permute-start(f32[40,1280]{1,0:T(8,128)S(1)} %get-tuple-element.40.a), channel_id=1, source_target_pairs={{0,1},{1,0},{2,3},{3,2},{4,5},{5,4},{6,7},{7,6},{8,9},{9,8},{10,11... | collective-permute-start | bytes 614408 | tf_op jit(solution)/shard_map/ppermute | solution.py:25
  67.4 12.3 %collective-permute-start.13 = (f32[40,1280]{1,0:T(8,128)S(1)}, f32[40,1280]{1,0:T(8,128)S(1)}, u32[]{:S(2)}, u32[]{:S(2)}) collective-permute-start(f32[40,1280]{1,0:T(8,128)S(1)} %get-tuple-element.41), channel_id=1, source_target_pairs={{0,5},{1,4},{4,1},{5,0},{2,7},{3,6},{6,3},{7,2},{8,13},{9,12},{12,... | collective-permute-start | bytes 614408 | tf_op jit(solution)/shard_map/ppermute | solution.py:522
  71.0 22.7 %collective-permute-start.10 = (bf16[4,160,1280]{2,1,0:T(8,128)(2,1)}, bf16[4,160,1280]{2,1,0:T(8,128)(2,1)S(1)}, u32[]{:S(2)}, u32[]{:S(2)}) collective-permute-start(bf16[4,160,1280]{2,1,0:T(8,128)(2,1)} %get-tuple-element.37), channel_id=1, source_target_pairs={{0,34},{2,8},{10,40},{8,18},{16,50},{18,24},{26,56},{24,2},{34,64}... | collective-permute-start | bytes 4915208 | tf_op jit(solution)/shard_map/ppermute | solution.py:37
  73.7 20.8 %collective-permute-start.11 = (bf16[4,160,1280]{2,1,0:T(8,128)(2,1)}, bf16[4,160,1280]{2,1,0:T(8,128)(2,1)S(1)}, u32[]{:S(2)}, u32[]{:S(2)}) collective-permute-start(bf16[4,160,1280]{2,1,0:T(8,128)(2,1)} %get-tuple-element.38), channel_id=1, source_target_pairs={{0,98},{2,24},{10,104},{8,2},{16,114},{18,8},{26,120},{24,18},{34,... | collective-permute-start | bytes 4915208 | tf_op jit(solution)/shard_map/ppermute | solution.py:37
  97.0 8.8 %collective-permute-start.15 = (bf16[160,1280]{1,0:T(8,128)(2,1)S(1)}, bf16[160,1280]{1,0:T(8,128)(2,1)S(1)}, u32[]{:S(2)}, u32[]{:S(2)}) collective-permute-start(bf16[160,1280]{1,0:T(8,128)(2,1)S(1)} %get-tuple-element.43.after), channel_id=1, source_target_pairs={{0,10},{2,32},{10,16},{8,42},{16,26},{18,48},{26,0},{24,58},{34,40... | collective-permute-start | bytes 1228808 | tf_op jit(solution)/shard_map/ppermute | solution.py:37
  97.0 14.1 %collective-permute-start.16 = (bf16[160,1280]{1,0:T(8,128)(2,1)S(1)}, bf16[160,1280]{1,0:T(8,128)(2,1)S(1)}, u32[]{:S(2)}, u32[]{:S(2)}) collective-permute-start(bf16[160,1280]{1,0:T(8,128)(2,1)S(1)} %get-tuple-element.44), channel_id=1, source_target_pairs={{0,16},{2,66},{10,26},{8,72},{16,0},{18,82},{26,10},{24,88},{34,50... | collective-permute-start | bytes 1228808 | tf_op jit(solution)/shard_map/ppermute | solution.py:37
  101.3 9.8 %collective-permute-start.17 = (bf16[160,1280]{1,0:T(8,128)(2,1)S(1)}, bf16[160,1280]{1,0:T(8,128)(2,1)S(1)}, u32[]{:S(2)}, u32[]{:S(2)}) collective-permute-start(bf16[160,1280]{1,0:T(8,128)(2,1)S(1)} %get-tuple-element.45), channel_id=1, source_target_pairs={{0,26},{2,96},{10,0},{8,106},{16,10},{18,112},{26,16},{24,122},{34... | collective-permute-start | bytes 1228808 | tf_op jit(solution)/shard_map/ppermute | solution.py:37
  112.6 9.6 %collective-permute-start.18 = (bf16[80,1280]{1,0:T(8,128)(2,1)S(1)}, bf16[80,1280]{1,0:T(8,128)(2,1)S(1)}, u32[]{:S(2)}, u32[]{:S(2)}) collective-permute-start(bf16[80,1280]{1,0:T(8,128)(2,1)S(1)} %get-tuple-element.47.late), channel_id=1, source_target_pairs={{0,4},{4,0},{1,5},{5,1},{2,6},{6,2},{3,7},{7,3},{8,12},{12,8},{9,1... | collective-permute-start | bytes 614408 | tf_op jit(solution)/shard_map/ppermute | solution.py:25
  112.7 23.3 %all-to-all-start = ((bf16[128,16,128]{2,1,0:T(8,128)(2,1)}), bf16[128,16,128]{2,1,0:T(8,128)(2,1)S(1)}, u32[]{:S(2)}, u32[]{:S(2)}) async-start(bf16[128,16,128]{2,1,0:T(8,128)(2,1)} %gate.1), calls=%async_computation | async-start | bytes 1048576 | tf_op jit(solution)/shard_map/all_to_all | solution.py:527
  122.3 18.5 %collective-permute-start.19 = (f32[40,1280]{1,0:T(8,128)S(1)}, f32[40,1280]{1,0:T(8,128)S(1)}, u32[]{:S(2)}, u32[]{:S(2)}) collective-permute-start(f32[40,1280]{1,0:T(8,128)S(1)} %dynamic-slice_bitcast_fusion), channel_id=1, source_target_pairs={{0,2},{2,0},{1,3},{3,1},{4,6},{6,4},{5,7},{7,5},{8,10},{10,8},{9,1... | collective-permute-start | bytes 614408 | tf_op jit(solution)/shard_map/ppermute | solution.py:25

commit v17 on v16

--- a/solution.py
+++ b/solution.py
@@ -341,23 +341,6 @@
         cost_estimate=pl.CostEstimate(flops=0, bytes_accessed=0, transcendentals=0),
         name="grow",
     )(in_hbm(right), in_hbm(left), from_left, from_right, *after)
-
-
-def gate_kernel(x, after, out):
-    del x, after, out
-
-
-def gate(x, after):
-    return pl.pallas_call(
-        gate_kernel,
-        out_shape=pltpu.HBM(x.shape, x.dtype),
-        in_specs=[pl.BlockSpec(memory_space=pltpu.HBM), ANY],
-        out_specs=pl.BlockSpec(memory_space=pltpu.HBM),
-        input_output_aliases={0: 0},
-        compiler_params=pltpu.CompilerParams(vmem_limit_bytes=2**20),
-        cost_estimate=pl.CostEstimate(flops=0, bytes_accessed=0, transcendentals=0),
-        name="gate",
-    )(in_hbm(x), after)
 
 
 def fetch_tiles(step, source, held, sems):
@@ -522,11 +505,10 @@
     across = lax.ppermute(theirs, ("xl", "o"), [(i, 3 - i) for i in range(4)])
     products = left_product(place, mine, shift(theirs, "xl", 1), left_inverse)
     products = left_product(place, shift(mine, "o", 1), across, left_inverse, products)
+    blocks = lax.all_to_all(products, ("o", "c", "z", "y", "xl"), 0, 0, tiled=True)
     f, *f_pieces = fold(second_me, f_parts, in_hbm(products))
-    products = gate(products, f_pieces[0])
-    blocks = lax.all_to_all(products, ("o", "c", "z", "y", "xl"), 0, 0, tiled=True)
-    f_mine, f_theirs = settle(my_xl, [in_hbm(f), *second_sends(f_pieces)], BF)
-    update = right_product(place, blocks, right_inverse, f_theirs)
+    update = right_product(place, blocks, right_inverse, f_pieces[0])
+    f_mine, f_theirs = settle(my_xl, [in_hbm(f), *second_sends(f_pieces)], BF, in_hbm(update))
 
     f = add(f_mine, shift(f_theirs, "xl", 1))
     f = f * jnp.where(first, 1.0 / token_total, 1.0).astype(F32)

time: 142 us -> 128 us (0.901)
  waiting for transfers between devices: 48.1 us -> 36.2 us
  starting transfers between devices: 39.6 us -> 36.7 us
    all_to_all x1, waiting for transfers between devices: 12.6 us -> 0.01 us  [per_device(): lax.all_to_all(products, ('o', 'c', 'z', 'y', 'xl'), 0, 0, tiled=True)]
    ppermute x6, waiting for transfers between devices: 6.77 us -> 14.1 us  [shift(): return lax.ppermute(x, axis, [(i, (i + step) % size) for i in range(size)])]
    ppermute x13, waiting for transfers between devices: 26.9 us -> 20.1 us  [turn(): return lax.ppermute(x, ('z', 'y', 'c'), pairs)]
    all_to_all x1, starting transfers between devices: 9.48 us -> 6.62 us  [per_device(): lax.all_to_all(products, ('o', 'c', 'z', 'y', 'xl'), 0, 0, tiled=True)]
  transfers between devices with their start and end apart: 21 -> 21, of which waited for: 10 -> 10; matrix products, arithmetic and copies ran while one was open for 0% -> 0% of each run, Pallas kernels for 28% -> 34%
where the time goes in v17:
time: 128 us
  Pallas kernels  53.4 us (42%)
  starting transfers between devices  36.7 us (29%)
  waiting for transfers between devices  36.2 us (28%)
    ppermute x13, starting transfers between devices, turn(): return lax.ppermute(x, ('z', 'y', 'c'), pairs)  23.1 us
    ppermute x13, waiting for transfers between devices, turn(): return lax.ppermute(x, ('z', 'y', 'c'), pairs)  20.1 us
    pallas_call x1, Pallas kernels, factor_term(): pl.pallas_call(factor_kernel, out_shape=[out, out, side, side, out], grid...  15.9 us
    ppermute x6, waiting for transfers between devices, shift(): return lax.ppermute(x, axis, [(i, (i + step) % size) for i in range(size)])  14.1 us
    pallas_call x1, Pallas kernels, cross_term(): pl.pallas_call(cross_kernel, out_shape=[out] * 4, grid_spec=pltpu.Prefetc...  8.31 us
    pallas_call x2, Pallas kernels, left_product(): pl.pallas_call(functools.partial(left_kernel, own), out_shape=total if ow...  6.95 us
    ppermute x6, starting transfers between devices, shift(): return lax.ppermute(x, axis, [(i, (i + step) % size) for i in range(size)])  6.8 us
    all_to_all x1, starting transfers between devices, per_device(): lax.all_to_all(products, ('o', 'c', 'z', 'y', 'xl'), 0, 0, tiled=True)  6.62 us
  transfers between devices with their start and end apart: 21, of which 10 were waited for; matrix products, arithmetic and copies ran while one was open for 0% of the time, Pallas kernels for 34%

profile of v17, /device:TPU:1, one launch (start us, length us, event | category | flops | bytes accessed | tf_op | source)
XLA Modules:
  0.0 128.0 jit_solution(16729631458435901933)
XLA Ops:
  0.6 1.5 %collective-permute-start = (bf16[768,2560]{1,0:T(8,128)(2,1)}, bf16[768,2560]{1,0:T(8,128)(2,1)}, u32[]{:S(2)}, u32[]{:S(2)}) collective-permute-start(bf16[768,2560]{1,0:T(8,128)(2,1)} %h_own.1), channel_id=1, source_target_pairs={{0,2},{2,0},{1,3},{3,1},{4,6},{6,4},{5,7},{7,5},{8,10},{10,8},{9,1... | collective-permute-start | bytes 11796488 | tf_op jit(solution)/shard_map/ppermute | solution.py:25
  2.1 0.1 collective-permute-start.1
  2.2 0.1 pad_add_fusion.place
  2.3 5.4 %cross_own.1.partial = f32[1280,1280]{1,0:T(8,128)S(1)} custom-call(s32[4]{0:T(128)S(1)} %pad_add_fusion.place, bf16[768,2560]{1,0:T(8,128)(2,1)} %g_own.1, bf16[768,2560]{1,0:T(8,128)(2,1)} %h_own.1), custom_call_target="tpu_custom_call" | custom-call | flops 2516582400 | bytes 7864320 | tf_op jit(solution)/shard_map/cross_own/pallas_call | solution.py:125
  7.7 1.1 collective-permute-done.b.h_next
  8.9 5.6 %collective-permute-done.1.a.g_next = bf16[768,2560]{1,0:T(8,128)(2,1)} collective-permute-done((bf16[768,2560]{1,0:T(8,128)(2,1)}, bf16[768,2560]{1,0:T(8,128)(2,1)}, u32[]{:S(2)}, u32[]{:S(2)}) %collective-permute-start.1) | collective-permute-done | bytes 3932192 | tf_op jit(solution)/shard_map/ppermute | solution.py:25
  14.5 8.3 %cross_term.1 = (bf16[4,80,1280]{2,1,0:T(8,128)(2,1)}, bf16[4,80,1280]{2,1,0:T(8,128)(2,1)}, bf16[4,80,1280]{2,1,0:T(8,128)(2,1)}, bf16[4,80,1280]{2,1,0:T(8,128)(2,1)}) custom-call(s32[4]{0:T(128)S(1)} %pad_add_fusion.place, bf16[768,2560]{1,0:T(8,128)(2,1)} %collective-permute-done.1.a.g_next, bf16[768,2560]{1,0:T(8,128)(2,1)} %collective-permute-done.b.h_next, ...), custom_call_target="tpu_custom_call" | custom-call | flops 2516582400 | bytes 9830400 | tf_op jit(solution)/shard_map/cross_term/pallas_call | solution.py:151
  22.8 1.7 %collective-permute-start.4 = (bf16[4,80,1280]{2,1,0:T(8,128)(2,1)}, bf16[4,80,1280]{2,1,0:T(8,128)(2,1)S(1)}, u32[]{:S(2)}, u32[]{:S(2)}) collective-permute-start(bf16[4,80,1280]{2,1,0:T(8,128)(2,1)} %get-tuple-element.25.after), channel_id=1, source_target_pairs={{0,34},{2,8},{10,40},{8,18},{16,50},{18,24},{26,56},{24,2},{34,64}... | collective-permute-start | bytes 2457608 | tf_op jit(solution)/shard_map/ppermute | solution.py:37
  24.5 2.6 %collective-permute-start.5 = (bf16[4,80,1280]{2,1,0:T(8,128)(2,1)}, bf16[4,80,1280]{2,1,0:T(8,128)(2,1)S(1)}, u32[]{:S(2)}, u32[]{:S(2)}) collective-permute-start(bf16[4,80,1280]{2,1,0:T(8,128)(2,1)} %get-tuple-element.32), channel_id=1, source_target_pairs={{0,64},{2,18},{10,74},{8,24},{16,80},{18,2},{26,90},{24,8},{34,98}... | collective-permute-start | bytes 2457608 | tf_op jit(solution)/shard_map/ppermute | solution.py:37
  27.2 1.4 %collective-permute-start.6 = (bf16[4,80,1280]{2,1,0:T(8,128)(2,1)}, bf16[4,80,1280]{2,1,0:T(8,128)(2,1)S(1)}, u32[]{:S(2)}, u32[]{:S(2)}) collective-permute-start(bf16[4,80,1280]{2,1,0:T(8,128)(2,1)} %get-tuple-element.33), channel_id=1, source_target_pairs={{0,98},{2,24},{10,104},{8,2},{16,114},{18,8},{26,120},{24,18},{34,... | collective-permute-start | bytes 2457608 | tf_op jit(solution)/shard_map/ppermute | solution.py:37
  28.5 15.9 %factor_term.1 = (bf16[4,160,1280]{2,1,0:T(8,128)(2,1)}, bf16[4,160,1280]{2,1,0:T(8,128)(2,1)}, bf16[2,160,1280]{2,1,0:T(8,128)(2,1)}, bf16[2,160,1280]{2,1,0:T(8,128)(2,1)}, bf16[4,160,1280]{2,1,0:T(8,128)(2,1)}) custom-call(s32[4]{0:T(128)S(1)} %pad_add_fusion.place, bf16[768,2560]{1,0:T(8,128)(2,1)} %h_own.1, bf16[768,2560]{1,0:T(8,128)(2,1)} %g_own.1, ...), custom_call_target="tpu_custom_call" | custom-call | flops 10066329600 | bytes 15728640 | tf_op jit(solution)/shard_map/factor_term/pallas_call | solution.py:214
  44.4 0.4 collective-permute-start.2
  44.8 2.6 %collective-permute-start.3 = (bf16[2,160,1280]{2,1,0:T(8,128)(2,1)}, bf16[2,160,1280]{2,1,0:T(8,128)(2,1)}, u32[]{:S(2)}, u32[]{:S(2)}) collective-permute-start(bf16[2,160,1280]{2,1,0:T(8,128)(2,1)} %get-tuple-element.30), channel_id=1, source_target_pairs={{0,98},{2,24},{10,104},{8,2},{16,114},{18,8},{26,120},{24,18},{34,... | collective-permute-start | bytes 2457608 | tf_op jit(solution)/shard_map/ppermute | solution.py:37
  47.4 0.0 collective-permute-done.5.refs_2_
  47.4 0.0 collective-permute-done.6.refs_3_
  47.4 2.2 %fold.2 = (f32[80,1280]{1,0:T(8,128)}, bf16[80,1280]{1,0:T(8,128)(2,1)}, bf16[80,1280]{1,0:T(8,128)(2,1)}, bf16[80,1280]{1,0:T(8,128)(2,1)S(1)}) custom-call(s32[1]{0:T(128)} %bitcast.1.me, bf16[4,80,1280]{2,1,0:T(8,128)(2,1)} %get-tuple-element.31.refs_0_, bf16[4,80,1280]{2,1,0:T(8,128)(2,1)S(1)} %collective-permute-done.4.refs_1_, ...), custom_call_target="tpu_custom_call" | custom-call | tf_op jit(solution)/shard_map/fold/pallas_call | solution.py:261
  49.7 1.7 %collective-permute-start.7 = (bf16[80,1280]{1,0:T(8,128)(2,1)}, bf16[80,1280]{1,0:T(8,128)(2,1)S(1)}, u32[]{:S(2)}, u32[]{:S(2)}) collective-permute-start(bf16[80,1280]{1,0:T(8,128)(2,1)} %get-tuple-element.34), channel_id=1, source_target_pairs={{0,10},{2,32},{10,16},{8,42},{16,26},{18,48},{26,0},{24,58},{34,40... | collective-permute-start | bytes 614408 | tf_op jit(solution)/shard_map/ppermute | solution.py:37
  51.3 3.3 %collective-permute-start.8 = (bf16[80,1280]{1,0:T(8,128)(2,1)}, bf16[80,1280]{1,0:T(8,128)(2,1)S(1)}, u32[]{:S(2)}, u32[]{:S(2)}) collective-permute-start(bf16[80,1280]{1,0:T(8,128)(2,1)} %get-tuple-element.35), channel_id=1, source_target_pairs={{0,16},{2,66},{10,26},{8,72},{16,0},{18,82},{26,10},{24,88},{34,50... | collective-permute-start | bytes 614408 | tf_op jit(solution)/shard_map/ppermute | solution.py:37
  54.6 1.4 %collective-permute-start.9 = (bf16[80,1280]{1,0:T(8,128)(2,1)S(1)}, bf16[80,1280]{1,0:T(8,128)(2,1)S(1)}, u32[]{:S(2)}, u32[]{:S(2)}) collective-permute-start(bf16[80,1280]{1,0:T(8,128)(2,1)S(1)} %get-tuple-element.36), channel_id=1, source_target_pairs={{0,26},{2,96},{10,0},{8,106},{16,10},{18,112},{26,16},{24,122},{34... | collective-permute-start | bytes 614408 | tf_op jit(solution)/shard_map/ppermute | solution.py:37
  56.0 5.9 %collective-permute-done.7.refs_0_.refs_1_ = bf16[80,1280]{1,0:T(8,128)(2,1)S(1)} collective-permute-done((bf16[80,1280]{1,0:T(8,128)(2,1)}, bf16[80,1280]{1,0:T(8,128)(2,1)S(1)}, u32[]{:S(2)}, u32[]{:S(2)}) %collective-permute-start.7) | collective-permute-done | bytes 204832 | tf_op jit(solution)/shard_map/ppermute | solution.py:37
  61.8 0.6 collective-permute-done.9.refs_2_.refs_3_
  62.4 1.2 settle.2
  63.6 1.3 %collective-permute-start.14 = (f32[40,1280]{1,0:T(8,128)S(1)}, f32[40,1280]{1,0:T(8,128)S(1)}, u32[]{:S(2)}, u32[]{:S(2)}) collective-permute-start(f32[40,1280]{1,0:T(8,128)S(1)} %get-tuple-element.41), channel_id=1, source_target_pairs={{0,4},{4,0},{1,5},{5,1},{2,6},{6,2},{3,7},{7,3},{8,12},{12,8},{9,1... | collective-permute-start | bytes 614408 | tf_op jit(solution)/shard_map/ppermute | solution.py:25
  64.8 2.5 %collective-permute-start.12 = (f32[40,1280]{1,0:T(8,128)S(1)}, f32[40,1280]{1,0:T(8,128)S(1)}, u32[]{:S(2)}, u32[]{:S(2)}) collective-permute-start(f32[40,1280]{1,0:T(8,128)S(1)} %get-tuple-element.40.a), channel_id=1, source_target_pairs={{0,1},{1,0},{2,3},{3,2},{4,5},{5,4},{6,7},{7,6},{8,9},{9,8},{10,11... | collective-permute-start | bytes 614408 | tf_op jit(solution)/shard_map/ppermute | solution.py:25
  67.4 0.1 collective-permute-start.13
  67.5 0.0 collective-permute-done.2.from_left
  67.5 0.0 collective-permute-done.3.from_right
  67.5 3.5 %grow.1 = (bf16[4,160,1280]{2,1,0:T(8,128)(2,1)}, bf16[4,160,1280]{2,1,0:T(8,128)(2,1)}) custom-call(bf16[4,160,1280]{2,1,0:T(8,128)(2,1)} %get-tuple-element.27.right, bf16[4,160,1280]{2,1,0:T(8,128)(2,1)} %get-tuple-element.28.left, bf16[2,160,1280]{2,1,0:T(8,128)(2,1)S(1)} %collective-permute-done.2.from_left, ...), custom_call_target="tpu_custom_call", output_to_operand_aliasing={{0}: (0, {}), {1}: (1, {})} | custom-call | tf_op jit(solution)/shard_map/grow/pallas_call | solution.py:328
  71.0 2.6 %collective-permute-start.10 = (bf16[4,160,1280]{2,1,0:T(8,128)(2,1)}, bf16[4,160,1280]{2,1,0:T(8,128)(2,1)S(1)}, u32[]{:S(2)}, u32[]{:S(2)}) collective-permute-start(bf16[4,160,1280]{2,1,0:T(8,128)(2,1)} %get-tuple-element.37), channel_id=1, source_target_pairs={{0,34},{2,8},{10,40},{8,18},{16,50},{18,24},{26,56},{24,2},{34,64}... | collective-permute-start | bytes 4915208 | tf_op jit(solution)/shard_map/ppermute | solution.py:37
  73.7 1.1 collective-permute-start.11
  74.8 2.9 %left_own.1.rest_0_ = f32[80,1280]{1,0:T(8,128)S(1)} custom-call(s32[4]{0:T(128)S(1)} %pad_add_fusion.place, f32[40,1280]{1,0:T(8,128)S(1)} %get-tuple-element.40.a, f32[40,1280]{1,0:T(8,128)S(1)} %collective-permute-done.14.b, bf16[2560,1280]{1,0:T(8,128)(2,1)} %left.3), custom_call_target="tpu_custom_call" | custom-call | tf_op jit(solution)/shard_map/left_own/pallas_call | solution.py:403
  77.7 0.0 collective-permute-done.12.a
  77.7 2.0 %collective-permute-done.13.b = f32[40,1280]{1,0:T(8,128)S(1)} collective-permute-done((f32[40,1280]{1,0:T(8,128)S(1)}, f32[40,1280]{1,0:T(8,128)S(1)}, u32[]{:S(2)}, u32[]{:S(2)}) %collective-permute-start.13) | collective-permute-done | bytes 204832 | tf_op jit(solution)/shard_map/ppermute | solution.py:505
  79.7 4.0 %left_product.1.refs_3_ = bf16[128,16,128]{2,1,0:T(8,128)(2,1)} custom-call(s32[4]{0:T(128)S(1)} %pad_add_fusion.place, f32[40,1280]{1,0:T(8,128)S(1)} %collective-permute-done.12.a, f32[40,1280]{1,0:T(8,128)S(1)} %collective-permute-done.13.b, bf16[2560,1280]{1,0:T(8,128)(2,1)} %left.3, f32[80,1280]{1,0:T(8,128)S(1)} %left_own.1.rest_0_), custom_call_target="tpu_custom_call" | custom-call | flops 16777216000 | tf_op jit(solution)/shard_map/left_product/pallas_call | solution.py:403
  83.7 6.6 %all-to-all-start = ((bf16[128,16,128]{2,1,0:T(8,128)(2,1)}), bf16[128,16,128]{2,1,0:T(8,128)(2,1)}, u32[]{:S(2)}, u32[]{:S(2)}) async-start(bf16[128,16,128]{2,1,0:T(8,128)(2,1)} %left_product.1.refs_3_), calls=%async_computation | async-start | bytes 1048576 | tf_op jit(solution)/shard_map/all_to_all | solution.py:508
  90.3 5.0 %collective-permute-done.10.refs_1_ = bf16[4,160,1280]{2,1,0:T(8,128)(2,1)S(1)} collective-permute-done((bf16[4,160,1280]{2,1,0:T(8,128)(2,1)}, bf16[4,160,1280]{2,1,0:T(8,128)(2,1)S(1)}, u32[]{:S(2)}, u32[]{:S(2)}) %collective-permute-start.10) | collective-permute-done | bytes 1638432 | tf_op jit(solution)/shard_map/ppermute | solution.py:37
  95.3 4.3 %collective-permute-done.11.refs_2_ = bf16[4,160,1280]{2,1,0:T(8,128)(2,1)S(1)} collective-permute-done((bf16[4,160,1280]{2,1,0:T(8,128)(2,1)}, bf16[4,160,1280]{2,1,0:T(8,128)(2,1)S(1)}, u32[]{:S(2)}, u32[]{:S(2)}) %collective-permute-start.11) | collective-permute-done | bytes 1638432 | tf_op jit(solution)/shard_map/ppermute | solution.py:37
  99.6 2.8 %fold.3 = (f32[160,1280]{1,0:T(8,128)}, bf16[160,1280]{1,0:T(8,128)(2,1)}, bf16[160,1280]{1,0:T(8,128)(2,1)}, bf16[160,1280]{1,0:T(8,128)(2,1)}) custom-call(s32[1]{0:T(128)} %bitcast.1.me, bf16[4,160,1280]{2,1,0:T(8,128)(2,1)} %get-tuple-element.26.refs_4_.refs_0_, bf16[4,160,1280]{2,1,0:T(8,128)(2,1)S(1)} %collective-permute-done.10.refs_1_, ...), custom_call_target="tpu_custom_call" | custom-call | tf_op jit(solution)/shard_map/fold/pallas_call | solution.py:261
  102.5 0.1 collective-permute-start.15
  102.5 4.3 %collective-permute-start.16 = (bf16[160,1280]{1,0:T(8,128)(2,1)}, bf16[160,1280]{1,0:T(8,128)(2,1)S(1)}, u32[]{:S(2)}, u32[]{:S(2)}) collective-permute-start(bf16[160,1280]{1,0:T(8,128)(2,1)} %get-tuple-element.44), channel_id=1, source_target_pairs={{0,16},{2,66},{10,26},{8,72},{16,0},{18,82},{26,10},{24,88},{34,50... | collective-permute-start | bytes 1228808 | tf_op jit(solution)/shard_map/ppermute | solution.py:37
  106.9 5.7 %right_product.1.refs_4_ = f32[40,1280]{1,0:T(8,128)} custom-call(s32[4]{0:T(128)S(1)} %pad_add_fusion.place, bf16[128,16,128]{2,1,0:T(8,128)(2,1)} %all-to-all-done.blocks, bf16[2560,1280]{1,0:T(8,128)(2,1)} %right.1, bf16[160,1280]{1,0:T(8,128)(2,1)} %get-tuple-element.43.late), custom_call_target="tpu_custom_call" | custom-call | flops 41943040000 | bytes 6553600 | tf_op jit(solution)/shard_map/right_product/pallas_call | solution.py:445
  112.6 4.3 %collective-permute-done.16.refs_2_ = bf16[160,1280]{1,0:T(8,128)(2,1)S(1)} collective-permute-done((bf16[160,1280]{1,0:T(8,128)(2,1)}, bf16[160,1280]{1,0:T(8,128)(2,1)S(1)}, u32[]{:S(2)}, u32[]{:S(2)}) %collective-permute-start.16) | collective-permute-done | bytes 409632 | tf_op jit(solution)/shard_map/ppermute | solution.py:37
  116.9 1.5 %settle.3 = (f32[80,1280]{1,0:T(8,128)S(1)}, bf16[80,1280]{1,0:T(8,128)(2,1)S(1)}) custom-call(s32[1]{0:T(128)} %bitcast.xl, f32[160,1280]{1,0:T(8,128)} %get-tuple-element.42.refs_0_, bf16[160,1280]{1,0:T(8,128)(2,1)S(1)} %collective-permute-done.15.refs_1_, bf16[160,1280]{1,0:T(8,128)(2,1)S(1)} %collective-permute-done.16.refs_2_, ...), custom_call_target="tpu_custom_call" | custom-call | tf_op jit(solution)/shard_map/settle/pallas_call | solution.py:295
  118.4 0.1 collective-permute-start.18
  118.5 6.2 %collective-permute-done.18 = bf16[80,1280]{1,0:T(8,128)(2,1)S(1)} collective-permute-done((bf16[80,1280]{1,0:T(8,128)(2,1)S(1)}, bf16[80,1280]{1,0:T(8,128)(2,1)S(1)}, u32[]{:S(2)}, u32[]{:S(2)}) %collective-permute-start.18) | collective-permute-done | bytes 204832 | tf_op jit(solution)/shard_map/ppermute | solution.py:25
  124.8 1.3 %collective-permute-start.19 = (f32[40,1280]{1,0:T(8,128)S(1)}, f32[40,1280]{1,0:T(8,128)S(1)}, u32[]{:S(2)}, u32[]{:S(2)}) collective-permute-start(f32[40,1280]{1,0:T(8,128)S(1)} %dynamic-slice_bitcast_fusion), channel_id=1, source_target_pairs={{0,2},{2,0},{1,3},{3,1},{4,6},{6,4},{5,7},{7,5},{8,10},{10,8},{9,1... | collective-permute-start | bytes 614408 | tf_op jit(solution)/shard_map/ppermute | solution.py:25
  126.1 1.1 collective-permute-done.19
  127.2 0.8 maximum_bitcast_fusion
  (10 shorter events, 0.1 us)
Async XLA Ops:
  0.6 8.3 %collective-permute-start = (bf16[768,2560]{1,0:T(8,128)(2,1)}, bf16[768,2560]{1,0:T(8,128)(2,1)}, u32[]{:S(2)}, u32[]{:S(2)}) collective-permute-start(bf16[768,2560]{1,0:T(8,128)(2,1)} %h_own.1), channel_id=1, source_target_pairs={{0,2},{2,0},{1,3},{3,1},{4,6},{6,4},{5,7},{7,5},{8,10},{10,8},{9,1... | collective-permute-start | bytes 11796488 | tf_op jit(solution)/shard_map/ppermute | solution.py:25
  2.1 12.4 %collective-permute-start.1 = (bf16[768,2560]{1,0:T(8,128)(2,1)}, bf16[768,2560]{1,0:T(8,128)(2,1)}, u32[]{:S(2)}, u32[]{:S(2)}) collective-permute-start(bf16[768,2560]{1,0:T(8,128)(2,1)} %g_own.1), channel_id=1, source_target_pairs={{0,2},{2,0},{1,3},{3,1},{4,6},{6,4},{5,7},{7,5},{8,10},{10,8},{9,1... | collective-permute-start | bytes 11796488 | tf_op jit(solution)/shard_map/ppermute | solution.py:25
  22.8 24.6 %collective-permute-start.4 = (bf16[4,80,1280]{2,1,0:T(8,128)(2,1)}, bf16[4,80,1280]{2,1,0:T(8,128)(2,1)S(1)}, u32[]{:S(2)}, u32[]{:S(2)}) collective-permute-start(bf16[4,80,1280]{2,1,0:T(8,128)(2,1)} %get-tuple-element.25.after), channel_id=1, source_target_pairs={{0,34},{2,8},{10,40},{8,18},{16,50},{18,24},{26,56},{24,2},{34,64}... | collective-permute-start | bytes 2457608 | tf_op jit(solution)/shard_map/ppermute | solution.py:37
  24.5 22.9 %collective-permute-start.5 = (bf16[4,80,1280]{2,1,0:T(8,128)(2,1)}, bf16[4,80,1280]{2,1,0:T(8,128)(2,1)S(1)}, u32[]{:S(2)}, u32[]{:S(2)}) collective-permute-start(bf16[4,80,1280]{2,1,0:T(8,128)(2,1)} %get-tuple-element.32), channel_id=1, source_target_pairs={{0,64},{2,18},{10,74},{8,24},{16,80},{18,2},{26,90},{24,8},{34,98}... | collective-permute-start | bytes 2457608 | tf_op jit(solution)/shard_map/ppermute | solution.py:37
  27.2 20.3 %collective-permute-start.6 = (bf16[4,80,1280]{2,1,0:T(8,128)(2,1)}, bf16[4,80,1280]{2,1,0:T(8,128)(2,1)S(1)}, u32[]{:S(2)}, u32[]{:S(2)}) collective-permute-start(bf16[4,80,1280]{2,1,0:T(8,128)(2,1)} %get-tuple-element.33), channel_id=1, source_target_pairs={{0,98},{2,24},{10,104},{8,2},{16,114},{18,8},{26,120},{24,18},{34,... | collective-permute-start | bytes 2457608 | tf_op jit(solution)/shard_map/ppermute | solution.py:37
  44.4 23.1 %collective-permute-start.2 = (bf16[2,160,1280]{2,1,0:T(8,128)(2,1)}, bf16[2,160,1280]{2,1,0:T(8,128)(2,1)S(1)}, u32[]{:S(2)}, u32[]{:S(2)}) collective-permute-start(bf16[2,160,1280]{2,1,0:T(8,128)(2,1)} %get-tuple-element.29), channel_id=1, source_target_pairs={{0,34},{2,8},{10,40},{8,18},{16,50},{18,24},{26,56},{24,2},{34,64}... | collective-permute-start | bytes 2457608 | tf_op jit(solution)/shard_map/ppermute | solution.py:37
  44.8 22.7 %collective-permute-start.3 = (bf16[2,160,1280]{2,1,0:T(8,128)(2,1)}, bf16[2,160,1280]{2,1,0:T(8,128)(2,1)}, u32[]{:S(2)}, u32[]{:S(2)}) collective-permute-start(bf16[2,160,1280]{2,1,0:T(8,128)(2,1)} %get-tuple-element.30), channel_id=1, source_target_pairs={{0,98},{2,24},{10,104},{8,2},{16,114},{18,8},{26,120},{24,18},{34,... | collective-permute-start | bytes 2457608 | tf_op jit(solution)/shard_map/ppermute | solution.py:37
  49.7 12.2 %collective-permute-start.7 = (bf16[80,1280]{1,0:T(8,128)(2,1)}, bf16[80,1280]{1,0:T(8,128)(2,1)S(1)}, u32[]{:S(2)}, u32[]{:S(2)}) collective-permute-start(bf16[80,1280]{1,0:T(8,128)(2,1)} %get-tuple-element.34), channel_id=1, source_target_pairs={{0,10},{2,32},{10,16},{8,42},{16,26},{18,48},{26,0},{24,58},{34,40... | collective-permute-start | bytes 614408 | tf_op jit(solution)/shard_map/ppermute | solution.py:37
  51.3 10.5 %collective-permute-start.8 = (bf16[80,1280]{1,0:T(8,128)(2,1)}, bf16[80,1280]{1,0:T(8,128)(2,1)S(1)}, u32[]{:S(2)}, u32[]{:S(2)}) collective-permute-start(bf16[80,1280]{1,0:T(8,128)(2,1)} %get-tuple-element.35), channel_id=1, source_target_pairs={{0,16},{2,66},{10,26},{8,72},{16,0},{18,82},{26,10},{24,88},{34,50... | collective-permute-start | bytes 614408 | tf_op jit(solution)/shard_map/ppermute | solution.py:37
  54.6 7.8 %collective-permute-start.9 = (bf16[80,1280]{1,0:T(8,128)(2,1)S(1)}, bf16[80,1280]{1,0:T(8,128)(2,1)S(1)}, u32[]{:S(2)}, u32[]{:S(2)}) collective-permute-start(bf16[80,1280]{1,0:T(8,128)(2,1)S(1)} %get-tuple-element.36), channel_id=1, source_target_pairs={{0,26},{2,96},{10,0},{8,106},{16,10},{18,112},{26,16},{24,122},{34... | collective-permute-start | bytes 614408 | tf_op jit(solution)/shard_map/ppermute | solution.py:37
  63.6 11.2 %collective-permute-start.14 = (f32[40,1280]{1,0:T(8,128)S(1)}, f32[40,1280]{1,0:T(8,128)S(1)}, u32[]{:S(2)}, u32[]{:S(2)}) collective-permute-start(f32[40,1280]{1,0:T(8,128)S(1)} %get-tuple-element.41), channel_id=1, source_target_pairs={{0,4},{4,0},{1,5},{5,1},{2,6},{6,2},{3,7},{7,3},{8,12},{12,8},{9,1... | collective-permute-start | bytes 614408 | tf_op jit(solution)/shard_map/ppermute | solution.py:25
  64.8 12.9 %collective-permute-start.12 = (f32[40,1280]{1,0:T(8,128)S(1)}, f32[40,1280]{1,0:T(8,128)S(1)}, u32[]{:S(2)}, u32[]{:S(2)}) collective-permute-start(f32[40,1280]{1,0:T(8,128)S(1)} %get-tuple-element.40.a), channel_id=1, source_target_pairs={{0,1},{1,0},{2,3},{3,2},{4,5},{5,4},{6,7},{7,6},{8,9},{9,8},{10,11... | collective-permute-start | bytes 614408 | tf_op jit(solution)/shard_map/ppermute | solution.py:25
  67.4 12.3 %collective-permute-start.13 = (f32[40,1280]{1,0:T(8,128)S(1)}, f32[40,1280]{1,0:T(8,128)S(1)}, u32[]{:S(2)}, u32[]{:S(2)}) collective-permute-start(f32[40,1280]{1,0:T(8,128)S(1)} %get-tuple-element.41), channel_id=1, source_target_pairs={{0,5},{1,4},{4,1},{5,0},{2,7},{3,6},{6,3},{7,2},{8,13},{9,12},{12,... | collective-permute-start | bytes 614408 | tf_op jit(solution)/shard_map/ppermute | solution.py:505
  71.0 24.3 %collective-permute-start.10 = (bf16[4,160,1280]{2,1,0:T(8,128)(2,1)}, bf16[4,160,1280]{2,1,0:T(8,128)(2,1)S(1)}, u32[]{:S(2)}, u32[]{:S(2)}) collective-permute-start(bf16[4,160,1280]{2,1,0:T(8,128)(2,1)} %get-tuple-element.37), channel_id=1, source_target_pairs={{0,34},{2,8},{10,40},{8,18},{16,50},{18,24},{26,56},{24,2},{34,64}... | collective-permute-start | bytes 4915208 | tf_op jit(solution)/shard_map/ppermute | solution.py:37
  73.7 26.0 %collective-permute-start.11 = (bf16[4,160,1280]{2,1,0:T(8,128)(2,1)}, bf16[4,160,1280]{2,1,0:T(8,128)(2,1)S(1)}, u32[]{:S(2)}, u32[]{:S(2)}) collective-permute-start(bf16[4,160,1280]{2,1,0:T(8,128)(2,1)} %get-tuple-element.38), channel_id=1, source_target_pairs={{0,98},{2,24},{10,104},{8,2},{16,114},{18,8},{26,120},{24,18},{34,... | collective-permute-start | bytes 4915208 | tf_op jit(solution)/shard_map/ppermute | solution.py:37
  83.7 23.1 %all-to-all-start = ((bf16[128,16,128]{2,1,0:T(8,128)(2,1)}), bf16[128,16,128]{2,1,0:T(8,128)(2,1)}, u32[]{:S(2)}, u32[]{:S(2)}) async-start(bf16[128,16,128]{2,1,0:T(8,128)(2,1)} %left_product.1.refs_3_), calls=%async_computation | async-start | bytes 1048576 | tf_op jit(solution)/shard_map/all_to_all | solution.py:508
  102.5 10.1 %collective-permute-start.15 = (bf16[160,1280]{1,0:T(8,128)(2,1)}, bf16[160,1280]{1,0:T(8,128)(2,1)S(1)}, u32[]{:S(2)}, u32[]{:S(2)}) collective-permute-start(bf16[160,1280]{1,0:T(8,128)(2,1)} %get-tuple-element.43.late), channel_id=1, source_target_pairs={{0,10},{2,32},{10,16},{8,42},{16,26},{18,48},{26,0},{24,58},{34,40... | collective-permute-start | bytes 1228808 | tf_op jit(solution)/shard_map/ppermute | solution.py:37
  102.5 14.3 %collective-permute-start.16 = (bf16[160,1280]{1,0:T(8,128)(2,1)}, bf16[160,1280]{1,0:T(8,128)(2,1)S(1)}, u32[]{:S(2)}, u32[]{:S(2)}) collective-permute-start(bf16[160,1280]{1,0:T(8,128)(2,1)} %get-tuple-element.44), channel_id=1, source_target_pairs={{0,16},{2,66},{10,26},{8,72},{16,0},{18,82},{26,10},{24,88},{34,50... | collective-permute-start | bytes 1228808 | tf_op jit(solution)/shard_map/ppermute | solution.py:37
  106.8 10.0 %collective-permute-start.17 = (bf16[160,1280]{1,0:T(8,128)(2,1)}, bf16[160,1280]{1,0:T(8,128)(2,1)S(1)}, u32[]{:S(2)}, u32[]{:S(2)}) collective-permute-start(bf16[160,1280]{1,0:T(8,128)(2,1)} %get-tuple-element.45), channel_id=1, source_target_pairs={{0,26},{2,96},{10,0},{8,106},{16,10},{18,112},{26,16},{24,122},{34... | collective-permute-start | bytes 1228808 | tf_op jit(solution)/shard_map/ppermute | solution.py:37
  118.4 6.3 %collective-permute-start.18 = (bf16[80,1280]{1,0:T(8,128)(2,1)S(1)}, bf16[80,1280]{1,0:T(8,128)(2,1)S(1)}, u32[]{:S(2)}, u32[]{:S(2)}) collective-permute-start(bf16[80,1280]{1,0:T(8,128)(2,1)S(1)} %get-tuple-element.47), channel_id=1, source_target_pairs={{0,4},{4,0},{1,5},{5,1},{2,6},{6,2},{3,7},{7,3},{8,12},{12,8},{9,1... | collective-permute-start | bytes 614408 | tf_op jit(solution)/shard_map/ppermute | solution.py:25
  124.8 2.4 %collective-permute-start.19 = (f32[40,1280]{1,0:T(8,128)S(1)}, f32[40,1280]{1,0:T(8,128)S(1)}, u32[]{:S(2)}, u32[]{:S(2)}) collective-permute-start(f32[40,1280]{1,0:T(8,128)S(1)} %dynamic-slice_bitcast_fusion), channel_id=1, source_target_pairs={{0,2},{2,0},{1,3},{3,1},{4,6},{6,4},{5,7},{7,5},{8,10},{10,8},{9,1... | collective-permute-start | bytes 614408 | tf_op jit(solution)/shard_map/ppermute | solution.py:25

commit v18 on v17

--- a/solution.py
+++ b/solution.py
@@ -104,7 +104,9 @@
     out[...] = contract(lhs[m], rhs[...])
 
 
-def cross_kernel(place, a, b, partial, own, ahead1, ahead2, ahead3, held, buffer, held_sems, sem):
+def cross_kernel(place, a, b, partial, after, *rest):
+    del after
+    own, ahead1, ahead2, ahead3, held, buffer, held_sems, sem = rest
     m = pl.program_id(0)
 
     @pl.when(m == 0)
@@ -145,7 +147,7 @@
     )(place, grads, acts)
 
 
-def cross_term(place, grads_next, acts_next, partial):
+def cross_term(place, grads_next, acts_next, partial, after):
     tokens, half = grads_next.shape[0], grads_next.shape[1] // 2
     out = pltpu.HBM((4, half // 16, half), BF)
     return pl.pallas_call(
@@ -158,6 +160,7 @@
                 pl.BlockSpec((tokens, TILE), lambda m, p: (0, p[1] * 2 + m)),
                 pl.BlockSpec((tokens, half), lambda m, p: (0, p[1] ^ p[0])),
                 ANY,
+                pl.BlockSpec(memory_space=pltpu.HBM),
             ],
             out_specs=[pl.BlockSpec(memory_space=pltpu.HBM)] * 4,
             scratch_shapes=[
@@ -172,40 +175,97 @@
             flops=2 * tokens * half * half, bytes_accessed=10 * tokens * half, transcendentals=0
         ),
         name="cross_term",
-    )(place, grads_next, acts_next, partial)
-
-
-def factor_kernel(place, h_own, g_own, h_next, g_next, after, *rest):
+    )(place, grads_next, acts_next, partial, after)
+
+
+def factor_fetch(place, pairs, step, lhs, lhs_sems, rhs=None, rhs_sem=None):
+    at = pl.ds(pl.multiple_of(step * TILE, TILE), TILE)
+    for owner in range(2):
+
+        @pl.when(place[0] == owner)
+        def _():
+            for k, pair in pairs:
+                slot = step & 1
+                target = lhs.at[slot, k]
+                pltpu.make_async_copy(pair[owner].at[:, at], target, lhs_sems.at[slot, k]).start()
+                if rhs is not None:
+                    half = rhs.shape[2]
+                    columns = pl.ds(pl.multiple_of(place[1] * half, half), half)
+                    pltpu.make_async_copy(pair[owner].at[:, columns], rhs.at[k], rhs_sem).start()
+
+
+def factor_own_kernel(place, h_own, g_own, after, out, lhs, rhs, lhs_sems, rhs_sem):
     del after
-    own, right, far_a, far_b, left, lhs, rhs, buffer, lhs_sems, rhs_sem, sem = rest
     m = pl.program_id(0)
-    half = rhs.shape[2]
-
-    def fetch(step, with_rhs):
-        slot = step & 1
-        at = pl.ds(pl.multiple_of(step * TILE, TILE), TILE)
-        columns = pl.ds(pl.multiple_of(place[1] * half, half), half)
-        for owner, refs in enumerate(((h_own, h_next), (g_own, g_next))):
-
-            @pl.when(place[0] == owner)
-            def _():
-                for k, ref in enumerate(refs):
-                    pltpu.make_async_copy(ref.at[:, at], lhs.at[slot, k], lhs_sems.at[slot]).start()
-                    if with_rhs:
-                        pltpu.make_async_copy(ref.at[:, columns], rhs.at[k], rhs_sem).start()
-
-    pl.when(m == 0)(lambda: fetch(0, True))
-    pl.when(m < 3)(lambda: fetch(m + 1, False))
+    pairs = [(0, (h_own, g_own))]
+    pl.when(m == 0)(lambda: factor_fetch(place, pairs, 0, lhs, lhs_sems, rhs, rhs_sem))
+    pl.when(m == 0)(lambda: factor_fetch(place, pairs, 1, lhs, lhs_sems))
+    wait_all(lhs.at[m, 0], lhs_sems.at[m, 0])
+    pl.when(m == 0)(lambda: wait_all(rhs, rhs_sem))
+    out[...] = contract(lhs[m, 0], rhs[0])
+
+
+def factor_own(place, acts, grads, after):
+    tokens, width = acts.shape
+    half = width // 2
+    hbm = pl.BlockSpec(memory_space=pltpu.HBM)
+    return pl.pallas_call(
+        factor_own_kernel,
+        out_shape=pltpu.HBM((half, half), F32),
+        grid_spec=pltpu.PrefetchScalarGridSpec(
+            num_scalar_prefetch=1,
+            grid=(2,),
+            in_specs=[hbm, hbm, ANY],
+            out_specs=pl.BlockSpec((TILE, half), lambda m, p: (m, 0)),
+            scratch_shapes=[
+                pltpu.VMEM((2, 1, tokens, TILE), BF),
+                pltpu.VMEM((1, tokens, half), BF),
+                pltpu.SemaphoreType.DMA((2, 1)),
+                pltpu.SemaphoreType.DMA,
+            ],
+        ),
+        compiler_params=pltpu.CompilerParams(vmem_limit_bytes=20 * 2**20),
+        cost_estimate=pl.CostEstimate(flops=0, bytes_accessed=0, transcendentals=0),
+        name="factor_own",
+    )(place, acts, grads, after)
+
+
+def factor_kernel(place, h_own, g_own, h_next, g_next, partial, after, *rest):
+    del after
+    own, right, far_a, far_b, left, lhs, rhs, held, buffer = rest[:9]
+    lhs_sems, rhs_sem, held_sems, sem = rest[9:]
+    m = pl.program_id(0)
+    both = [(0, (h_own, g_own)), (1, (h_next, g_next))]
+
+    @pl.when(m == 0)
+    def _():
+        for k in range(2):
+            rows = partial.at[pl.ds(k * TILE, TILE)]
+            pltpu.make_async_copy(rows, held.at[k], held_sems.at[k]).start()
+        factor_fetch(place, both[1:], 0, lhs, lhs_sems)
+        factor_fetch(place, both, 1, lhs, lhs_sems, rhs, rhs_sem)
+
+    pl.when((m == 1) | (m == 2))(lambda: factor_fetch(place, both, m + 1, lhs, lhs_sems))
     slot = m & 1
-    wait_all(lhs.at[slot], lhs_sems.at[slot])
+    wait_all(lhs.at[slot, 1], lhs_sems.at[slot, 1])
+    pl.when(m > 0)(lambda: wait_all(lhs.at[slot, 0], lhs_sems.at[slot, 0]))
     pl.when(m == 0)(lambda: wait_all(rhs, rhs_sem))
-
-    buffer[m] = (contract(lhs[slot, 0], rhs[0]) + contract(lhs[slot, 1], rhs[1])).astype(BF)
+    tile = contract(lhs[slot, 1], rhs[1])
+
+    @pl.when(m < 2)
+    def _():
+        wait_all(held.at[m], held_sems.at[m])
+        buffer[m] = (held[m] + tile).astype(BF)
+
+    @pl.when(m >= 2)
+    def _():
+        buffer[m] = (contract(lhs[slot, 0], rhs[0]) + tile).astype(BF)
+
     place_tile(place, buffer, sem, [own, right, (far_a, far_b), left], m, 1)
     pl.when(m == 3)(lambda: wait_all(buffer, sem))
 
 
-def factor_term(place, acts, grads, acts_next, grads_next, after):
+def factor_term(place, acts, grads, acts_next, grads_next, partial, after):
     tokens, width = acts.shape
     half = width // 2
     hbm = pl.BlockSpec(memory_space=pltpu.HBM)
@@ -217,23 +277,25 @@
         grid_spec=pltpu.PrefetchScalarGridSpec(
             num_scalar_prefetch=1,
             grid=(4,),
-            in_specs=[hbm] * 2 + [ANY] * 3,
+            in_specs=[hbm] * 6,
             out_specs=[hbm] * 5,
             scratch_shapes=[
                 pltpu.VMEM((2, 2, tokens, TILE), BF),
                 pltpu.VMEM((2, tokens, half), BF),
+                pltpu.VMEM((2, TILE, half), F32),
                 pltpu.VMEM((4, TILE, half), BF),
+                pltpu.SemaphoreType.DMA((2, 2)),
+                pltpu.SemaphoreType.DMA,
                 pltpu.SemaphoreType.DMA((2,)),
                 pltpu.SemaphoreType.DMA,
-                pltpu.SemaphoreType.DMA,
-            ],
-        ),
-        compiler_params=pltpu.CompilerParams(vmem_limit_bytes=30 * 2**20),
+            ],
+        ),
+        compiler_params=pltpu.CompilerParams(vmem_limit_bytes=36 * 2**20),
         cost_estimate=pl.CostEstimate(
             flops=4 * tokens * width * half, bytes_accessed=16 * tokens * half, transcendentals=0
         ),
         name="factor_term",
-    )(place, acts, grads, acts_next, grads_next, after)
+    )(place, acts, grads, acts_next, grads_next, partial, after)
 
 
 def add(first, *rest):
@@ -482,12 +544,13 @@
 
     grads_next, acts_next = in_hbm(shift(out_grad, "c", 1)), in_hbm(shift(hidden, "c", 1))
     partial = cross_own(place, out_grad, hidden)
-
-    own, m1, m2, m3 = cross_term(place, grads_next, acts_next, partial)
+    factor_partial = in_hbm(factor_own(place, hidden, out_grad, partial))
+
+    own, m1, m2, m3 = cross_term(place, grads_next, acts_next, partial, factor_partial)
     m_parts = [own, turn(m1, 1, 0), turn(m2, 2, 0), turn(m3, 3, 0)]
 
     f_own, right, far_a, far_b, left = factor_term(
-        place, hidden, out_grad, acts_next, grads_next, in_hbm(m1)
+        place, hidden, out_grad, acts_next, grads_next, factor_partial, in_hbm(m1)
     )
     from_left, from_right = turn(far_a, 1, 0), turn(far_b, -1, 0)
 

time: 128 us -> 129 us (level); the launches traced: 128 us -> 127 us
  waiting for transfers between devices: 36.2 us -> 28.9 us
  Pallas kernels: 53.4 us -> 59.6 us
    pallas_call x0 -> x1, Pallas kernels: none -> 7.18 us  [factor_own(): pl.pallas_call(factor_own_kernel, out_shape=pltpu.HBM((half, half), F32),...]
    ppermute x6, waiting for transfers between devices: 14.1 us -> 6.99 us  [shift(): return lax.ppermute(x, axis, [(i, (i + step) % size) for i in range(size)])]
  transfers between devices with their start and end apart: 21 -> 21, of which waited for: 10 -> 10; matrix products, arithmetic and copies ran while one was open for 0% -> 0% of each run, Pallas kernels for 34% -> 39%
where the time goes in v18:
time: 129 us; the launch traced here: 127 us
  Pallas kernels  59.6 us (46%)
  starting transfers between devices  36.8 us (29%)
  waiting for transfers between devices  28.9 us (22%)
    ppermute x13, starting transfers between devices, turn(): return lax.ppermute(x, ('z', 'y', 'c'), pairs)  22.8 us
    ppermute x13, waiting for transfers between devices, turn(): return lax.ppermute(x, ('z', 'y', 'c'), pairs)  19.8 us
    pallas_call x1, Pallas kernels, factor_term(): pl.pallas_call(factor_kernel, out_shape=[out, out, side, side, out], grid...  14.9 us
    pallas_call x1, Pallas kernels, cross_term(): pl.pallas_call(cross_kernel, out_shape=[out] * 4, grid_spec=pltpu.Prefetc...  8.3 us
    ppermute x6, starting transfers between devices, shift(): return lax.ppermute(x, axis, [(i, (i + step) % size) for i in range(size)])  7.4 us
    pallas_call x1, Pallas kernels, factor_own(): pl.pallas_call(factor_own_kernel, out_shape=pltpu.HBM((half, half), F32),...  7.18 us
    ppermute x6, waiting for transfers between devices, shift(): return lax.ppermute(x, axis, [(i, (i + step) % size) for i in range(size)])  6.99 us
    pallas_call x2, Pallas kernels, left_product(): pl.pallas_call(functools.partial(left_kernel, own), out_shape=total if ow...  6.95 us
  transfers between devices with their start and end apart: 21, of which 10 were waited for; matrix products, arithmetic and copies ran while one was open for 0% of the time, Pallas kernels for 39%

profile of v18, /device:TPU:1, one launch (start us, length us, event | category | flops | bytes accessed | tf_op | source)
XLA Modules:
  0.0 127.1 jit_solution(2508433560296975422)
XLA Ops:
  0.6 1.5 %collective-permute-start = (bf16[768,2560]{1,0:T(8,128)(2,1)}, bf16[768,2560]{1,0:T(8,128)(2,1)}, u32[]{:S(2)}, u32[]{:S(2)}) collective-permute-start(bf16[768,2560]{1,0:T(8,128)(2,1)} %h_own.3), channel_id=1, source_target_pairs={{0,2},{2,0},{1,3},{3,1},{4,6},{6,4},{5,7},{7,5},{8,10},{10,8},{9,1... | collective-permute-start | bytes 11796488 | tf_op jit(solution)/shard_map/ppermute | solution.py:25
  2.1 0.1 collective-permute-start.1
  2.2 0.1 pad_add_fusion.place
  2.3 5.4 %cross_own.1.after.partial = f32[1280,1280]{1,0:T(8,128)S(1)} custom-call(s32[4]{0:T(128)S(1)} %pad_add_fusion.place, bf16[768,2560]{1,0:T(8,128)(2,1)} %g_own.3, bf16[768,2560]{1,0:T(8,128)(2,1)} %h_own.3), custom_call_target="tpu_custom_call" | custom-call | flops 2516582400 | bytes 7864320 | tf_op jit(solution)/shard_map/cross_own/pallas_call | solution.py:127
  7.7 7.2 %factor_own.1.after.partial = f32[1280,1280]{1,0:T(8,128)} custom-call(s32[4]{0:T(128)S(1)} %pad_add_fusion.place, bf16[768,2560]{1,0:T(8,128)(2,1)} %h_own.3, bf16[768,2560]{1,0:T(8,128)(2,1)} %g_own.3, f32[1280,1280]{1,0:T(8,128)S(1)} %cross_own.1.after.partial), custom_call_target="tpu_custom_call" | custom-call | tf_op jit(solution)/shard_map/factor_own/pallas_call | solution.py:212
  14.9 0.0 collective-permute-done.b.h_next
  14.9 0.0 collective-permute-done.1.a.g_next
  14.9 8.3 %cross_term.1 = (bf16[4,80,1280]{2,1,0:T(8,128)(2,1)}, bf16[4,80,1280]{2,1,0:T(8,128)(2,1)}, bf16[4,80,1280]{2,1,0:T(8,128)(2,1)}, bf16[4,80,1280]{2,1,0:T(8,128)(2,1)}) custom-call(s32[4]{0:T(128)S(1)} %pad_add_fusion.place, bf16[768,2560]{1,0:T(8,128)(2,1)} %collective-permute-done.1.a.g_next, bf16[768,2560]{1,0:T(8,128)(2,1)} %collective-permute-done.b.h_next, ...), custom_call_target="tpu_custom_call" | custom-call | flops 2516582400 | bytes 9830400 | tf_op jit(solution)/shard_map/cross_term/pallas_call | solution.py:153
  23.3 1.7 %collective-permute-start.4 = (bf16[4,80,1280]{2,1,0:T(8,128)(2,1)}, bf16[4,80,1280]{2,1,0:T(8,128)(2,1)S(1)}, u32[]{:S(2)}, u32[]{:S(2)}) collective-permute-start(bf16[4,80,1280]{2,1,0:T(8,128)(2,1)} %get-tuple-element.25.after), channel_id=1, source_target_pairs={{0,34},{2,8},{10,40},{8,18},{16,50},{18,24},{26,56},{24,2},{34,64}... | collective-permute-start | bytes 2457608 | tf_op jit(solution)/shard_map/ppermute | solution.py:37
  25.0 2.6 %collective-permute-start.5 = (bf16[4,80,1280]{2,1,0:T(8,128)(2,1)}, bf16[4,80,1280]{2,1,0:T(8,128)(2,1)S(1)}, u32[]{:S(2)}, u32[]{:S(2)}) collective-permute-start(bf16[4,80,1280]{2,1,0:T(8,128)(2,1)} %get-tuple-element.32), channel_id=1, source_target_pairs={{0,64},{2,18},{10,74},{8,24},{16,80},{18,2},{26,90},{24,8},{34,98}... | collective-permute-start | bytes 2457608 | tf_op jit(solution)/shard_map/ppermute | solution.py:37
  27.6 1.3 %collective-permute-start.6 = (bf16[4,80,1280]{2,1,0:T(8,128)(2,1)}, bf16[4,80,1280]{2,1,0:T(8,128)(2,1)S(1)}, u32[]{:S(2)}, u32[]{:S(2)}) collective-permute-start(bf16[4,80,1280]{2,1,0:T(8,128)(2,1)} %get-tuple-element.33), channel_id=1, source_target_pairs={{0,98},{2,24},{10,104},{8,2},{16,114},{18,8},{26,120},{24,18},{34,... | collective-permute-start | bytes 2457608 | tf_op jit(solution)/shard_map/ppermute | solution.py:37
  29.0 14.9 %factor_term.1 = (bf16[4,160,1280]{2,1,0:T(8,128)(2,1)}, bf16[4,160,1280]{2,1,0:T(8,128)(2,1)}, bf16[2,160,1280]{2,1,0:T(8,128)(2,1)}, bf16[2,160,1280]{2,1,0:T(8,128)(2,1)}, bf16[4,160,1280]{2,1,0:T(8,128)(2,1)}) custom-call(s32[4]{0:T(128)S(1)} %pad_add_fusion.place, bf16[768,2560]{1,0:T(8,128)(2,1)} %h_own.3, bf16[768,2560]{1,0:T(8,128)(2,1)} %g_own.3, ...), custom_call_target="tpu_custom_call" | custom-call | flops 10066329600 | bytes 15728640 | tf_op jit(solution)/shard_map/factor_term/pallas_call | solution.py:274
  43.9 0.5 collective-permute-start.2
  44.4 2.5 %collective-permute-start.3 = (bf16[2,160,1280]{2,1,0:T(8,128)(2,1)}, bf16[2,160,1280]{2,1,0:T(8,128)(2,1)}, u32[]{:S(2)}, u32[]{:S(2)}) collective-permute-start(bf16[2,160,1280]{2,1,0:T(8,128)(2,1)} %get-tuple-element.30), channel_id=1, source_target_pairs={{0,98},{2,24},{10,104},{8,2},{16,114},{18,8},{26,120},{24,18},{34,... | collective-permute-start | bytes 2457608 | tf_op jit(solution)/shard_map/ppermute | solution.py:37
  46.9 0.0 collective-permute-done.4.refs_1_
  46.9 0.0 collective-permute-done.5.refs_2_
  46.9 0.0 collective-permute-done.6.refs_3_
  46.9 2.2 %fold.2 = (f32[80,1280]{1,0:T(8,128)}, bf16[80,1280]{1,0:T(8,128)(2,1)}, bf16[80,1280]{1,0:T(8,128)(2,1)}, bf16[80,1280]{1,0:T(8,128)(2,1)S(1)}) custom-call(s32[1]{0:T(128)} %bitcast.1.me, bf16[4,80,1280]{2,1,0:T(8,128)(2,1)} %get-tuple-element.31.refs_0_, bf16[4,80,1280]{2,1,0:T(8,128)(2,1)S(1)} %collective-permute-done.4.refs_1_, ...), custom_call_target="tpu_custom_call" | custom-call | tf_op jit(solution)/shard_map/fold/pallas_call | solution.py:323
  49.1 1.9 %collective-permute-start.7 = (bf16[80,1280]{1,0:T(8,128)(2,1)}, bf16[80,1280]{1,0:T(8,128)(2,1)S(1)}, u32[]{:S(2)}, u32[]{:S(2)}) collective-permute-start(bf16[80,1280]{1,0:T(8,128)(2,1)} %get-tuple-element.34), channel_id=1, source_target_pairs={{0,10},{2,32},{10,16},{8,42},{16,26},{18,48},{26,0},{24,58},{34,40... | collective-permute-start | bytes 614408 | tf_op jit(solution)/shard_map/ppermute | solution.py:37
  51.1 3.3 %collective-permute-start.8 = (bf16[80,1280]{1,0:T(8,128)(2,1)}, bf16[80,1280]{1,0:T(8,128)(2,1)S(1)}, u32[]{:S(2)}, u32[]{:S(2)}) collective-permute-start(bf16[80,1280]{1,0:T(8,128)(2,1)} %get-tuple-element.35), channel_id=1, source_target_pairs={{0,16},{2,66},{10,26},{8,72},{16,0},{18,82},{26,10},{24,88},{34,50... | collective-permute-start | bytes 614408 | tf_op jit(solution)/shard_map/ppermute | solution.py:37
  54.4 1.1 collective-permute-start.9
  55.4 6.2 %collective-permute-done.7.refs_0_.refs_1_ = bf16[80,1280]{1,0:T(8,128)(2,1)S(1)} collective-permute-done((bf16[80,1280]{1,0:T(8,128)(2,1)}, bf16[80,1280]{1,0:T(8,128)(2,1)S(1)}, u32[]{:S(2)}, u32[]{:S(2)}) %collective-permute-start.7) | collective-permute-done | bytes 204832 | tf_op jit(solution)/shard_map/ppermute | solution.py:37
  61.6 0.2 collective-permute-done.9.refs_2_.refs_3_
  61.8 1.2 settle.2
  62.9 1.3 %collective-permute-start.14 = (f32[40,1280]{1,0:T(8,128)S(1)}, f32[40,1280]{1,0:T(8,128)S(1)}, u32[]{:S(2)}, u32[]{:S(2)}) collective-permute-start(f32[40,1280]{1,0:T(8,128)S(1)} %get-tuple-element.41), channel_id=1, source_target_pairs={{0,4},{4,0},{1,5},{5,1},{2,6},{6,2},{3,7},{7,3},{8,12},{12,8},{9,1... | collective-permute-start | bytes 614408 | tf_op jit(solution)/shard_map/ppermute | solution.py:25
  64.2 4.3 %collective-permute-start.12 = (f32[40,1280]{1,0:T(8,128)S(1)}, f32[40,1280]{1,0:T(8,128)S(1)}, u32[]{:S(2)}, u32[]{:S(2)}) collective-permute-start(f32[40,1280]{1,0:T(8,128)S(1)} %get-tuple-element.40.a), channel_id=1, source_target_pairs={{0,1},{1,0},{2,3},{3,2},{4,5},{5,4},{6,7},{7,6},{8,9},{9,8},{10,11... | collective-permute-start | bytes 614408 | tf_op jit(solution)/shard_map/ppermute | solution.py:25
  68.6 3.5 %grow.1 = (bf16[4,160,1280]{2,1,0:T(8,128)(2,1)}, bf16[4,160,1280]{2,1,0:T(8,128)(2,1)}) custom-call(bf16[4,160,1280]{2,1,0:T(8,128)(2,1)} %get-tuple-element.27.right, bf16[4,160,1280]{2,1,0:T(8,128)(2,1)} %get-tuple-element.28.left, bf16[2,160,1280]{2,1,0:T(8,128)(2,1)S(1)} %collective-permute-done.2.from_left, ...), custom_call_target="tpu_custom_call", output_to_operand_aliasing={{0}: (0, {}), {1}: (1, {})} | custom-call | tf_op jit(solution)/shard_map/grow/pallas_call | solution.py:390
  72.1 2.4 %collective-permute-start.10 = (bf16[4,160,1280]{2,1,0:T(8,128)(2,1)}, bf16[4,160,1280]{2,1,0:T(8,128)(2,1)S(1)}, u32[]{:S(2)}, u32[]{:S(2)}) collective-permute-start(bf16[4,160,1280]{2,1,0:T(8,128)(2,1)} %get-tuple-element.37), channel_id=1, source_target_pairs={{0,34},{2,8},{10,40},{8,18},{16,50},{18,24},{26,56},{24,2},{34,64}... | collective-permute-start | bytes 4915208 | tf_op jit(solution)/shard_map/ppermute | solution.py:37
  74.5 0.8 collective-permute-start.11
  75.3 2.9 %left_own.1.rest_0_ = f32[80,1280]{1,0:T(8,128)S(1)} custom-call(s32[4]{0:T(128)S(1)} %pad_add_fusion.place, f32[40,1280]{1,0:T(8,128)S(1)} %get-tuple-element.40.a, f32[40,1280]{1,0:T(8,128)S(1)} %collective-permute-done.14.b, bf16[2560,1280]{1,0:T(8,128)(2,1)} %left.3), custom_call_target="tpu_custom_call" | custom-call | tf_op jit(solution)/shard_map/left_own/pallas_call | solution.py:465
  78.2 0.3 collective-permute-done.12.a
  78.6 2.1 %collective-permute-done.13.b = f32[40,1280]{1,0:T(8,128)S(1)} collective-permute-done((f32[40,1280]{1,0:T(8,128)S(1)}, f32[40,1280]{1,0:T(8,128)S(1)}, u32[]{:S(2)}, u32[]{:S(2)}) %collective-permute-start.13) | collective-permute-done | bytes 204832 | tf_op jit(solution)/shard_map/ppermute | solution.py:568
  80.7 4.0 %left_product.1.refs_3_ = bf16[128,16,128]{2,1,0:T(8,128)(2,1)} custom-call(s32[4]{0:T(128)S(1)} %pad_add_fusion.place, f32[40,1280]{1,0:T(8,128)S(1)} %collective-permute-done.12.a, f32[40,1280]{1,0:T(8,128)S(1)} %collective-permute-done.13.b, bf16[2560,1280]{1,0:T(8,128)(2,1)} %left.3, f32[80,1280]{1,0:T(8,128)S(1)} %left_own.1.rest_0_), custom_call_target="tpu_custom_call" | custom-call | flops 16777216000 | tf_op jit(solution)/shard_map/left_product/pallas_call | solution.py:465
  84.7 6.5 %all-to-all-start = ((bf16[128,16,128]{2,1,0:T(8,128)(2,1)}), bf16[128,16,128]{2,1,0:T(8,128)(2,1)}, u32[]{:S(2)}, u32[]{:S(2)}) async-start(bf16[128,16,128]{2,1,0:T(8,128)(2,1)} %left_product.1.refs_3_), calls=%async_computation | async-start | bytes 1048576 | tf_op jit(solution)/shard_map/all_to_all | solution.py:571
  91.3 4.1 %collective-permute-done.10.refs_1_ = bf16[4,160,1280]{2,1,0:T(8,128)(2,1)S(1)} collective-permute-done((bf16[4,160,1280]{2,1,0:T(8,128)(2,1)}, bf16[4,160,1280]{2,1,0:T(8,128)(2,1)S(1)}, u32[]{:S(2)}, u32[]{:S(2)}) %collective-permute-start.10) | collective-permute-done | bytes 1638432 | tf_op jit(solution)/shard_map/ppermute | solution.py:37
  95.3 5.1 %collective-permute-done.11.refs_2_ = bf16[4,160,1280]{2,1,0:T(8,128)(2,1)S(1)} collective-permute-done((bf16[4,160,1280]{2,1,0:T(8,128)(2,1)}, bf16[4,160,1280]{2,1,0:T(8,128)(2,1)S(1)}, u32[]{:S(2)}, u32[]{:S(2)}) %collective-permute-start.11) | collective-permute-done | bytes 1638432 | tf_op jit(solution)/shard_map/ppermute | solution.py:37
  100.4 2.8 %fold.3 = (f32[160,1280]{1,0:T(8,128)}, bf16[160,1280]{1,0:T(8,128)(2,1)}, bf16[160,1280]{1,0:T(8,128)(2,1)}, bf16[160,1280]{1,0:T(8,128)(2,1)}) custom-call(s32[1]{0:T(128)} %bitcast.1.me, bf16[4,160,1280]{2,1,0:T(8,128)(2,1)} %get-tuple-element.26.refs_4_.refs_0_, bf16[4,160,1280]{2,1,0:T(8,128)(2,1)S(1)} %collective-permute-done.10.refs_1_, ...), custom_call_target="tpu_custom_call" | custom-call | tf_op jit(solution)/shard_map/fold/pallas_call | solution.py:323
  103.2 0.1 collective-permute-start.15
  103.3 4.5 %collective-permute-start.16 = (bf16[160,1280]{1,0:T(8,128)(2,1)}, bf16[160,1280]{1,0:T(8,128)(2,1)S(1)}, u32[]{:S(2)}, u32[]{:S(2)}) collective-permute-start(bf16[160,1280]{1,0:T(8,128)(2,1)} %get-tuple-element.44), channel_id=1, source_target_pairs={{0,16},{2,66},{10,26},{8,72},{16,0},{18,82},{26,10},{24,88},{34,50... | collective-permute-start | bytes 1228808 | tf_op jit(solution)/shard_map/ppermute | solution.py:37
  107.8 5.7 %right_product.1.refs_4_ = f32[40,1280]{1,0:T(8,128)} custom-call(s32[4]{0:T(128)S(1)} %pad_add_fusion.place, bf16[128,16,128]{2,1,0:T(8,128)(2,1)} %all-to-all-done.blocks, bf16[2560,1280]{1,0:T(8,128)(2,1)} %right.1, bf16[160,1280]{1,0:T(8,128)(2,1)} %get-tuple-element.43.late), custom_call_target="tpu_custom_call" | custom-call | flops 41943040000 | bytes 6553600 | tf_op jit(solution)/shard_map/right_product/pallas_call | solution.py:507
  113.5 4.2 %collective-permute-done.16.refs_2_ = bf16[160,1280]{1,0:T(8,128)(2,1)S(1)} collective-permute-done((bf16[160,1280]{1,0:T(8,128)(2,1)}, bf16[160,1280]{1,0:T(8,128)(2,1)S(1)}, u32[]{:S(2)}, u32[]{:S(2)}) %collective-permute-start.16) | collective-permute-done | bytes 409632 | tf_op jit(solution)/shard_map/ppermute | solution.py:37
  117.8 0.1 collective-permute-done.17.refs_3_
  117.9 1.5 %settle.3 = (f32[80,1280]{1,0:T(8,128)S(1)}, bf16[80,1280]{1,0:T(8,128)(2,1)S(1)}) custom-call(s32[1]{0:T(128)} %bitcast.xl, f32[160,1280]{1,0:T(8,128)} %get-tuple-element.42.refs_0_, bf16[160,1280]{1,0:T(8,128)(2,1)S(1)} %collective-permute-done.15.refs_1_, bf16[160,1280]{1,0:T(8,128)(2,1)S(1)} %collective-permute-done.16.refs_2_, ...), custom_call_target="tpu_custom_call" | custom-call | tf_op jit(solution)/shard_map/settle/pallas_call | solution.py:357
  119.3 0.1 collective-permute-start.18
  119.4 5.2 %collective-permute-done.18 = bf16[80,1280]{1,0:T(8,128)(2,1)S(1)} collective-permute-done((bf16[80,1280]{1,0:T(8,128)(2,1)S(1)}, bf16[80,1280]{1,0:T(8,128)(2,1)S(1)}, u32[]{:S(2)}, u32[]{:S(2)}) %collective-permute-start.18) | collective-permute-done | bytes 204832 | tf_op jit(solution)/shard_map/ppermute | solution.py:25
  124.7 0.1 collective-permute-start.19
  124.8 1.4 %collective-permute-done.19 = f32[40,1280]{1,0:T(8,128)S(1)} collective-permute-done((f32[40,1280]{1,0:T(8,128)S(1)}, f32[40,1280]{1,0:T(8,128)S(1)}, u32[]{:S(2)}, u32[]{:S(2)}) %collective-permute-start.19) | collective-permute-done | bytes 204832 | tf_op jit(solution)/shard_map/ppermute | solution.py:25
  126.3 0.8 maximum_bitcast_fusion
  (11 shorter events, 0.1 us)
Async XLA Ops:
  0.6 14.3 %collective-permute-start = (bf16[768,2560]{1,0:T(8,128)(2,1)}, bf16[768,2560]{1,0:T(8,128)(2,1)}, u32[]{:S(2)}, u32[]{:S(2)}) collective-permute-start(bf16[768,2560]{1,0:T(8,128)(2,1)} %h_own.3), channel_id=1, source_target_pairs={{0,2},{2,0},{1,3},{3,1},{4,6},{6,4},{5,7},{7,5},{8,10},{10,8},{9,1... | collective-permute-start | bytes 11796488 | tf_op jit(solution)/shard_map/ppermute | solution.py:25
  2.1 12.8 %collective-permute-start.1 = (bf16[768,2560]{1,0:T(8,128)(2,1)}, bf16[768,2560]{1,0:T(8,128)(2,1)}, u32[]{:S(2)}, u32[]{:S(2)}) collective-permute-start(bf16[768,2560]{1,0:T(8,128)(2,1)} %g_own.3), channel_id=1, source_target_pairs={{0,2},{2,0},{1,3},{3,1},{4,6},{6,4},{5,7},{7,5},{8,10},{10,8},{9,1... | collective-permute-start | bytes 11796488 | tf_op jit(solution)/shard_map/ppermute | solution.py:25
  23.3 23.7 %collective-permute-start.4 = (bf16[4,80,1280]{2,1,0:T(8,128)(2,1)}, bf16[4,80,1280]{2,1,0:T(8,128)(2,1)S(1)}, u32[]{:S(2)}, u32[]{:S(2)}) collective-permute-start(bf16[4,80,1280]{2,1,0:T(8,128)(2,1)} %get-tuple-element.25.after), channel_id=1, source_target_pairs={{0,34},{2,8},{10,40},{8,18},{16,50},{18,24},{26,56},{24,2},{34,64}... | collective-permute-start | bytes 2457608 | tf_op jit(solution)/shard_map/ppermute | solution.py:37
  25.0 21.9 %collective-permute-start.5 = (bf16[4,80,1280]{2,1,0:T(8,128)(2,1)}, bf16[4,80,1280]{2,1,0:T(8,128)(2,1)S(1)}, u32[]{:S(2)}, u32[]{:S(2)}) collective-permute-start(bf16[4,80,1280]{2,1,0:T(8,128)(2,1)} %get-tuple-element.32), channel_id=1, source_target_pairs={{0,64},{2,18},{10,74},{8,24},{16,80},{18,2},{26,90},{24,8},{34,98}... | collective-permute-start | bytes 2457608 | tf_op jit(solution)/shard_map/ppermute | solution.py:37
  27.6 19.3 %collective-permute-start.6 = (bf16[4,80,1280]{2,1,0:T(8,128)(2,1)}, bf16[4,80,1280]{2,1,0:T(8,128)(2,1)S(1)}, u32[]{:S(2)}, u32[]{:S(2)}) collective-permute-start(bf16[4,80,1280]{2,1,0:T(8,128)(2,1)} %get-tuple-element.33), channel_id=1, source_target_pairs={{0,98},{2,24},{10,104},{8,2},{16,114},{18,8},{26,120},{24,18},{34,... | collective-permute-start | bytes 2457608 | tf_op jit(solution)/shard_map/ppermute | solution.py:37
  43.9 24.7 %collective-permute-start.2 = (bf16[2,160,1280]{2,1,0:T(8,128)(2,1)}, bf16[2,160,1280]{2,1,0:T(8,128)(2,1)S(1)}, u32[]{:S(2)}, u32[]{:S(2)}) collective-permute-start(bf16[2,160,1280]{2,1,0:T(8,128)(2,1)} %get-tuple-element.29), channel_id=1, source_target_pairs={{0,34},{2,8},{10,40},{8,18},{16,50},{18,24},{26,56},{24,2},{34,64}... | collective-permute-start | bytes 2457608 | tf_op jit(solution)/shard_map/ppermute | solution.py:37
  44.4 24.2 %collective-permute-start.3 = (bf16[2,160,1280]{2,1,0:T(8,128)(2,1)}, bf16[2,160,1280]{2,1,0:T(8,128)(2,1)}, u32[]{:S(2)}, u32[]{:S(2)}) collective-permute-start(bf16[2,160,1280]{2,1,0:T(8,128)(2,1)} %get-tuple-element.30), channel_id=1, source_target_pairs={{0,98},{2,24},{10,104},{8,2},{16,114},{18,8},{26,120},{24,18},{34,... | collective-permute-start | bytes 2457608 | tf_op jit(solution)/shard_map/ppermute | solution.py:37
  49.1 12.5 %collective-permute-start.7 = (bf16[80,1280]{1,0:T(8,128)(2,1)}, bf16[80,1280]{1,0:T(8,128)(2,1)S(1)}, u32[]{:S(2)}, u32[]{:S(2)}) collective-permute-start(bf16[80,1280]{1,0:T(8,128)(2,1)} %get-tuple-element.34), channel_id=1, source_target_pairs={{0,10},{2,32},{10,16},{8,42},{16,26},{18,48},{26,0},{24,58},{34,40... | collective-permute-start | bytes 614408 | tf_op jit(solution)/shard_map/ppermute | solution.py:37
  51.1 10.5 %collective-permute-start.8 = (bf16[80,1280]{1,0:T(8,128)(2,1)}, bf16[80,1280]{1,0:T(8,128)(2,1)S(1)}, u32[]{:S(2)}, u32[]{:S(2)}) collective-permute-start(bf16[80,1280]{1,0:T(8,128)(2,1)} %get-tuple-element.35), channel_id=1, source_target_pairs={{0,16},{2,66},{10,26},{8,72},{16,0},{18,82},{26,10},{24,88},{34,50... | collective-permute-start | bytes 614408 | tf_op jit(solution)/shard_map/ppermute | solution.py:37
  54.4 7.4 %collective-permute-start.9 = (bf16[80,1280]{1,0:T(8,128)(2,1)S(1)}, bf16[80,1280]{1,0:T(8,128)(2,1)S(1)}, u32[]{:S(2)}, u32[]{:S(2)}) collective-permute-start(bf16[80,1280]{1,0:T(8,128)(2,1)S(1)} %get-tuple-element.36), channel_id=1, source_target_pairs={{0,26},{2,96},{10,0},{8,106},{16,10},{18,112},{26,16},{24,122},{34... | collective-permute-start | bytes 614408 | tf_op jit(solution)/shard_map/ppermute | solution.py:37
  62.9 12.3 %collective-permute-start.14 = (f32[40,1280]{1,0:T(8,128)S(1)}, f32[40,1280]{1,0:T(8,128)S(1)}, u32[]{:S(2)}, u32[]{:S(2)}) collective-permute-start(f32[40,1280]{1,0:T(8,128)S(1)} %get-tuple-element.41), channel_id=1, source_target_pairs={{0,4},{4,0},{1,5},{5,1},{2,6},{6,2},{3,7},{7,3},{8,12},{12,8},{9,1... | collective-permute-start | bytes 614408 | tf_op jit(solution)/shard_map/ppermute | solution.py:25
  64.2 14.3 %collective-permute-start.12 = (f32[40,1280]{1,0:T(8,128)S(1)}, f32[40,1280]{1,0:T(8,128)S(1)}, u32[]{:S(2)}, u32[]{:S(2)}) collective-permute-start(f32[40,1280]{1,0:T(8,128)S(1)} %get-tuple-element.40.a), channel_id=1, source_target_pairs={{0,1},{1,0},{2,3},{3,2},{4,5},{5,4},{6,7},{7,6},{8,9},{9,8},{10,11... | collective-permute-start | bytes 614408 | tf_op jit(solution)/shard_map/ppermute | solution.py:25
  68.6 12.1 %collective-permute-start.13 = (f32[40,1280]{1,0:T(8,128)S(1)}, f32[40,1280]{1,0:T(8,128)S(1)}, u32[]{:S(2)}, u32[]{:S(2)}) collective-permute-start(f32[40,1280]{1,0:T(8,128)S(1)} %get-tuple-element.41), channel_id=1, source_target_pairs={{0,5},{1,4},{4,1},{5,0},{2,7},{3,6},{6,3},{7,2},{8,13},{9,12},{12,... | collective-permute-start | bytes 614408 | tf_op jit(solution)/shard_map/ppermute | solution.py:568
  72.1 23.2 %collective-permute-start.10 = (bf16[4,160,1280]{2,1,0:T(8,128)(2,1)}, bf16[4,160,1280]{2,1,0:T(8,128)(2,1)S(1)}, u32[]{:S(2)}, u32[]{:S(2)}) collective-permute-start(bf16[4,160,1280]{2,1,0:T(8,128)(2,1)} %get-tuple-element.37), channel_id=1, source_target_pairs={{0,34},{2,8},{10,40},{8,18},{16,50},{18,24},{26,56},{24,2},{34,64}... | collective-permute-start | bytes 4915208 | tf_op jit(solution)/shard_map/ppermute | solution.py:37
  74.5 25.9 %collective-permute-start.11 = (bf16[4,160,1280]{2,1,0:T(8,128)(2,1)}, bf16[4,160,1280]{2,1,0:T(8,128)(2,1)S(1)}, u32[]{:S(2)}, u32[]{:S(2)}) collective-permute-start(bf16[4,160,1280]{2,1,0:T(8,128)(2,1)} %get-tuple-element.38), channel_id=1, source_target_pairs={{0,98},{2,24},{10,104},{8,2},{16,114},{18,8},{26,120},{24,18},{34,... | collective-permute-start | bytes 4915208 | tf_op jit(solution)/shard_map/ppermute | solution.py:37
  84.7 23.1 %all-to-all-start = ((bf16[128,16,128]{2,1,0:T(8,128)(2,1)}), bf16[128,16,128]{2,1,0:T(8,128)(2,1)}, u32[]{:S(2)}, u32[]{:S(2)}) async-start(bf16[128,16,128]{2,1,0:T(8,128)(2,1)} %left_product.1.refs_3_), calls=%async_computation | async-start | bytes 1048576 | tf_op jit(solution)/shard_map/all_to_all | solution.py:571
  103.2 10.3 %collective-permute-start.15 = (bf16[160,1280]{1,0:T(8,128)(2,1)}, bf16[160,1280]{1,0:T(8,128)(2,1)S(1)}, u32[]{:S(2)}, u32[]{:S(2)}) collective-permute-start(bf16[160,1280]{1,0:T(8,128)(2,1)} %get-tuple-element.43.late), channel_id=1, source_target_pairs={{0,10},{2,32},{10,16},{8,42},{16,26},{18,48},{26,0},{24,58},{34,40... | collective-permute-start | bytes 1228808 | tf_op jit(solution)/shard_map/ppermute | solution.py:37
  103.3 14.5 %collective-permute-start.16 = (bf16[160,1280]{1,0:T(8,128)(2,1)}, bf16[160,1280]{1,0:T(8,128)(2,1)S(1)}, u32[]{:S(2)}, u32[]{:S(2)}) collective-permute-start(bf16[160,1280]{1,0:T(8,128)(2,1)} %get-tuple-element.44), channel_id=1, source_target_pairs={{0,16},{2,66},{10,26},{8,72},{16,0},{18,82},{26,10},{24,88},{34,50... | collective-permute-start | bytes 1228808 | tf_op jit(solution)/shard_map/ppermute | solution.py:37
  107.8 10.0 %collective-permute-start.17 = (bf16[160,1280]{1,0:T(8,128)(2,1)}, bf16[160,1280]{1,0:T(8,128)(2,1)S(1)}, u32[]{:S(2)}, u32[]{:S(2)}) collective-permute-start(bf16[160,1280]{1,0:T(8,128)(2,1)} %get-tuple-element.45), channel_id=1, source_target_pairs={{0,26},{2,96},{10,0},{8,106},{16,10},{18,112},{26,16},{24,122},{34... | collective-permute-start | bytes 1228808 | tf_op jit(solution)/shard_map/ppermute | solution.py:37
  119.3 5.3 %collective-permute-start.18 = (bf16[80,1280]{1,0:T(8,128)(2,1)S(1)}, bf16[80,1280]{1,0:T(8,128)(2,1)S(1)}, u32[]{:S(2)}, u32[]{:S(2)}) collective-permute-start(bf16[80,1280]{1,0:T(8,128)(2,1)S(1)} %get-tuple-element.47), channel_id=1, source_target_pairs={{0,4},{4,0},{1,5},{5,1},{2,6},{6,2},{3,7},{7,3},{8,12},{12,8},{9,1... | collective-permute-start | bytes 614408 | tf_op jit(solution)/shard_map/ppermute | solution.py:25
  124.7 1.5 %collective-permute-start.19 = (f32[40,1280]{1,0:T(8,128)S(1)}, f32[40,1280]{1,0:T(8,128)S(1)}, u32[]{:S(2)}, u32[]{:S(2)}) collective-permute-start(f32[40,1280]{1,0:T(8,128)S(1)} %dynamic-slice_bitcast_fusion), channel_id=1, source_target_pairs={{0,2},{2,0},{1,3},{3,1},{4,6},{6,4},{5,7},{7,5},{8,10},{10,8},{9,1... | collective-permute-start | bytes 614408 | tf_op jit(solution)/shard_map/ppermute | solution.py:25

commit v19 on v17

--- a/solution.py
+++ b/solution.py
@@ -87,7 +87,30 @@
     pltpu.make_async_copy(buffer, buffer, sem).wait()
 
 
-def own_kernel(place, a, b, out, lhs, rhs, lhs_sems, rhs_sem):
+def cut_kernel(place, x, out):
+    del place
+    out[...] = x[...]
+
+
+def cut(place, x, index):
+    tokens, width = x.shape
+    block = (tokens // 4, width // 2)
+    return pl.pallas_call(
+        cut_kernel,
+        out_shape=pltpu.HBM((tokens, width // 2), x.dtype),
+        grid_spec=pltpu.PrefetchScalarGridSpec(
+            num_scalar_prefetch=1,
+            grid=(4,),
+            in_specs=[pl.BlockSpec(block, lambda m, p: (m, index(p)))],
+            out_specs=pl.BlockSpec(block, lambda m, p: (m, 0)),
+        ),
+        compiler_params=pltpu.CompilerParams(vmem_limit_bytes=4 * 2**20),
+        cost_estimate=pl.CostEstimate(flops=0, bytes_accessed=0, transcendentals=0),
+        name="cut",
+    )(place, x)
+
+
+def own_kernel(place, a, b, out, rest, lhs, rhs, part, lhs_sems, rhs_sem, part_sems):
     m = pl.program_id(0)
     half = rhs.shape[1]
 
@@ -99,9 +122,21 @@
             at = pl.ds(pl.multiple_of(place[1] * half + k * TILE, TILE), TILE)
             pltpu.make_async_copy(a.at[:, at], lhs.at[k], lhs_sems.at[k]).start()
         wait_all(rhs, rhs_sem)
+        at = pl.ds(pl.multiple_of(place[1] * half, half), half)
+        for owner, ref in enumerate((b, a)):
+
+            @pl.when(place[0] == owner)
+            def _():
+                pltpu.make_async_copy(ref.at[:, at], part, part_sems.at[0]).start()
+
+    @pl.when(m == 1)
+    def _():
+        wait_all(part, part_sems.at[0])
+        pltpu.make_async_copy(part, rest, part_sems.at[1]).start()
 
     wait_all(lhs.at[m], lhs_sems.at[m])
     out[...] = contract(lhs[m], rhs[...])
+    pl.when(m == 1)(lambda: wait_all(part, part_sems.at[1]))
 
 
 def cross_kernel(place, a, b, partial, own, ahead1, ahead2, ahead3, held, buffer, held_sems, sem):
@@ -124,17 +159,22 @@
     tokens, half = grads.shape[0], grads.shape[1] // 2
     return pl.pallas_call(
         own_kernel,
-        out_shape=jax.ShapeDtypeStruct((half, half), F32),
+        out_shape=[jax.ShapeDtypeStruct((half, half), F32), pltpu.HBM((tokens, half), BF)],
         grid_spec=pltpu.PrefetchScalarGridSpec(
             num_scalar_prefetch=1,
             grid=(2,),
             in_specs=[pl.BlockSpec(memory_space=pltpu.HBM)] * 2,
-            out_specs=pl.BlockSpec((TILE, half), lambda m, p: (m, 0)),
+            out_specs=[
+                pl.BlockSpec((TILE, half), lambda m, p: (m, 0)),
+                pl.BlockSpec(memory_space=pltpu.HBM),
+            ],
             scratch_shapes=[
                 pltpu.VMEM((2, tokens, TILE), BF),
                 pltpu.VMEM((tokens, half), BF),
+                pltpu.VMEM((tokens, half), BF),
                 pltpu.SemaphoreType.DMA((2,)),
                 pltpu.SemaphoreType.DMA,
+                pltpu.SemaphoreType.DMA((2,)),
             ],
         ),
         compiler_params=pltpu.CompilerParams(vmem_limit_bytes=28 * 2**20),
@@ -146,7 +186,7 @@
 
 
 def cross_term(place, grads_next, acts_next, partial):
-    tokens, half = grads_next.shape[0], grads_next.shape[1] // 2
+    tokens, half = grads_next.shape
     out = pltpu.HBM((4, half // 16, half), BF)
     return pl.pallas_call(
         cross_kernel,
@@ -155,8 +195,8 @@
             num_scalar_prefetch=1,
             grid=(2,),
             in_specs=[
-                pl.BlockSpec((tokens, TILE), lambda m, p: (0, p[1] * 2 + m)),
-                pl.BlockSpec((tokens, half), lambda m, p: (0, p[1] ^ p[0])),
+                pl.BlockSpec((tokens, TILE), lambda m, p: (0, m)),
+                pl.BlockSpec((tokens, half), lambda m, p: (0, 0)),
                 ANY,
             ],
             out_specs=[pl.BlockSpec(memory_space=pltpu.HBM)] * 4,
@@ -175,24 +215,33 @@
     )(place, grads_next, acts_next, partial)
 
 
-def factor_kernel(place, h_own, g_own, h_next, g_next, after, *rest):
+def factor_kernel(place, h_own, g_own, h_next, g_next, x_next, after, *rest):
     del after
     own, right, far_a, far_b, left, lhs, rhs, buffer, lhs_sems, rhs_sem, sem = rest
     m = pl.program_id(0)
     half = rhs.shape[2]
 
+    def lanes(step, wide):
+        return pl.ds(pl.multiple_of(step * wide, wide), wide)
+
     def fetch(step, with_rhs):
         slot = step & 1
-        at = pl.ds(pl.multiple_of(step * TILE, TILE), TILE)
-        columns = pl.ds(pl.multiple_of(place[1] * half, half), half)
-        for owner, refs in enumerate(((h_own, h_next), (g_own, g_next))):
+
+        def left_block(ref, k, at):
+            pltpu.make_async_copy(ref.at[:, lanes(at, TILE)], lhs.at[slot, k], lhs_sems.at[slot]).start()
+
+        for owner, (mine, theirs) in enumerate(((h_own, h_next), (g_own, g_next))):
 
             @pl.when(place[0] == owner)
             def _():
-                for k, ref in enumerate(refs):
-                    pltpu.make_async_copy(ref.at[:, at], lhs.at[slot, k], lhs_sems.at[slot]).start()
-                    if with_rhs:
-                        pltpu.make_async_copy(ref.at[:, columns], rhs.at[k], rhs_sem).start()
+                left_block(mine, 0, step)
+                pl.when((step >> 1) == place[1])(lambda: left_block(theirs, 1, step & 1))
+                if with_rhs:
+                    at = lanes(place[1], half)
+                    pltpu.make_async_copy(mine.at[:, at], rhs.at[0], rhs_sem).start()
+                    pltpu.make_async_copy(theirs, rhs.at[1], rhs_sem).start()
+
+        pl.when((step >> 1) != place[1])(lambda: left_block(x_next, 1, step & 1))
 
     pl.when(m == 0)(lambda: fetch(0, True))
     pl.when(m < 3)(lambda: fetch(m + 1, False))
@@ -205,7 +254,7 @@
     pl.when(m == 3)(lambda: wait_all(buffer, sem))
 
 
-def factor_term(place, acts, grads, acts_next, grads_next, after):
+def factor_term(place, acts, grads, acts_next, grads_next, rest_next, after):
     tokens, width = acts.shape
     half = width // 2
     hbm = pl.BlockSpec(memory_space=pltpu.HBM)
@@ -217,7 +266,7 @@
         grid_spec=pltpu.PrefetchScalarGridSpec(
             num_scalar_prefetch=1,
             grid=(4,),
-            in_specs=[hbm] * 2 + [ANY] * 3,
+            in_specs=[hbm] * 2 + [ANY] * 4,
             out_specs=[hbm] * 5,
             scratch_shapes=[
                 pltpu.VMEM((2, 2, tokens, TILE), BF),
@@ -233,7 +282,7 @@
             flops=4 * tokens * width * half, bytes_accessed=16 * tokens * half, transcendentals=0
         ),
         name="factor_term",
-    )(place, acts, grads, acts_next, grads_next, after)
+    )(place, acts, grads, acts_next, grads_next, rest_next, after)
 
 
 def add(first, *rest):
@@ -480,14 +529,16 @@
     place = jnp.stack([o, h, z, y]).astype(jnp.int32)
     second_me = jnp.where(h == 0, y, z).astype(jnp.int32)[None]
 
-    grads_next, acts_next = in_hbm(shift(out_grad, "c", 1)), in_hbm(shift(hidden, "c", 1))
-    partial = cross_own(place, out_grad, hidden)
+    grads_next = in_hbm(shift(cut(place, out_grad, lambda p: 1 - p[1]), "c", 1))
+    acts_next = in_hbm(shift(cut(place, hidden, lambda p: (1 - p[1]) ^ p[0]), "c", 1))
+    partial, rest = cross_own(place, out_grad, hidden)
+    rest_next = in_hbm(shift(rest, "c", 1))
 
     own, m1, m2, m3 = cross_term(place, grads_next, acts_next, partial)
     m_parts = [own, turn(m1, 1, 0), turn(m2, 2, 0), turn(m3, 3, 0)]
 
     f_own, right, far_a, far_b, left = factor_term(
-        place, hidden, out_grad, acts_next, grads_next, in_hbm(m1)
+        place, hidden, out_grad, acts_next, grads_next, rest_next, in_hbm(m1)
     )
     from_left, from_right = turn(far_a, 1, 0), turn(far_b, -1, 0)
 

time: 128 us -> 134 us (1.047)
  Pallas kernels: 53.4 us -> 62.2 us
  waiting for transfers between devices: 36.2 us -> 30.5 us
  local copies, waits for them, and re-layouts: 0.02 us -> 3.18 us
    pallas_call x1 -> x3, Pallas kernels: 5.43 us -> 14.1 us  [the longest x2 8.56 us: cut(): pl.pallas_call(cut_kernel, out_shape=pltpu.HBM((tokens, width // 2), x.dt...]
    ppermute x6 -> x7, waiting for transfers between devices: 14.1 us -> 8.02 us  [shift(): return lax.ppermute(x, axis, [(i, (i + step) % size) for i in range(size)])]
    unnamed x0 -> x6, local copies, waits for them, and re-layouts: none -> 3.16 us
    ppermute x6 -> x7, starting transfers between devices: 6.8 us -> 6.88 us  [shift(): return lax.ppermute(x, axis, [(i, (i + step) % size) for i in range(size)])]
  transfers between devices with their start and end apart: 21 -> 22, of which waited for: 10 -> 10; matrix products, arithmetic and copies ran while one was open for 0% -> 0% of each run, Pallas kernels for 34% -> 42%
where the time goes in v19:
time: 134 us; the launch traced here: 133 us
  Pallas kernels  62.2 us (46%)
  starting transfers between devices  35.9 us (27%)
  waiting for transfers between devices  30.5 us (23%)
  local copies, waits for them, and re-layouts  3.18 us (2%)
    ppermute x13, starting transfers between devices, turn(): return lax.ppermute(x, ('z', 'y', 'c'), pairs)  22.6 us
    ppermute x13, waiting for transfers between devices, turn(): return lax.ppermute(x, ('z', 'y', 'c'), pairs)  20.3 us
    pallas_call x1, Pallas kernels, factor_term(): pl.pallas_call(factor_kernel, out_shape=[out, out, side, side, out], grid...  15.9 us
    pallas_call x2, Pallas kernels, cut(): pl.pallas_call(cut_kernel, out_shape=pltpu.HBM((tokens, width // 2), x.dt...  8.56 us
    pallas_call x1, Pallas kernels, cross_term(): pl.pallas_call(cross_kernel, out_shape=[out] * 4, grid_spec=pltpu.Prefetc...  8.29 us
    ppermute x7, waiting for transfers between devices, shift(): return lax.ppermute(x, axis, [(i, (i + step) % size) for i in range(size)])  8.02 us
    pallas_call x2, Pallas kernels, left_product(): pl.pallas_call(functools.partial(left_kernel, own), out_shape=total if ow...  6.96 us
    ppermute x7, starting transfers between devices, shift(): return lax.ppermute(x, axis, [(i, (i + step) % size) for i in range(size)])  6.88 us
  transfers between devices with their start and end apart: 22, of which 10 were waited for; matrix products, arithmetic and copies ran while one was open for 0% of the time, Pallas kernels for 42%

profile of v19, /device:TPU:1, one launch (start us, length us, event | category | flops | bytes accessed | tf_op | source)
XLA Modules:
  0.0 133.4 jit_solution(6192453201259993717)
XLA Ops:
  0.6 0.1 pad_add_fusion.place
  0.7 4.3 %cut.2 = bf16[768,1280]{1,0:T(8,128)(2,1)} custom-call(s32[4]{0:T(128)S(1)} %pad_add_fusion.place, bf16[768,2560]{1,0:T(8,128)(2,1)} %h_own.1), custom_call_target="tpu_custom_call" | custom-call | tf_op jit(solution)/shard_map/cut/pallas_call | solution.py:98
  5.0 1.4 %collective-permute-start = (bf16[768,1280]{1,0:T(8,128)(2,1)}, bf16[768,1280]{1,0:T(8,128)(2,1)S(1)}, u32[]{:S(2)}, u32[]{:S(2)}) collective-permute-start(bf16[768,1280]{1,0:T(8,128)(2,1)} %cut.2), channel_id=1, source_target_pairs={{0,2},{2,0},{1,3},{3,1},{4,6},{6,4},{5,7},{7,5},{8,10},{10,8},{9,1... | collective-permute-start | bytes 5898248 | tf_op jit(solution)/shard_map/ppermute | solution.py:25
  6.4 4.3 %cut.3 = bf16[768,1280]{1,0:T(8,128)(2,1)} custom-call(s32[4]{0:T(128)S(1)} %pad_add_fusion.place, bf16[768,2560]{1,0:T(8,128)(2,1)} %g_own.1), custom_call_target="tpu_custom_call" | custom-call | tf_op jit(solution)/shard_map/cut/pallas_call | solution.py:98
  10.7 5.5 %cross_own.1 = (f32[1280,1280]{1,0:T(8,128)S(1)}, bf16[768,1280]{1,0:T(8,128)(2,1)}) custom-call(s32[4]{0:T(128)S(1)} %pad_add_fusion.place, bf16[768,2560]{1,0:T(8,128)(2,1)} %g_own.1, bf16[768,2560]{1,0:T(8,128)(2,1)} %h_own.1), custom_call_target="tpu_custom_call" | custom-call | flops 2516582400 | bytes 7864320 | tf_op jit(solution)/shard_map/cross_own/pallas_call | solution.py:160
  16.3 0.6 collective-permute-start.2
  16.9 1.3 copy-done
  18.1 0.6 copy-done.1
  18.7 8.3 %cross_term.1 = (bf16[4,80,1280]{2,1,0:T(8,128)(2,1)}, bf16[4,80,1280]{2,1,0:T(8,128)(2,1)}, bf16[4,80,1280]{2,1,0:T(8,128)(2,1)}, bf16[4,80,1280]{2,1,0:T(8,128)(2,1)}) custom-call(s32[4]{0:T(128)S(1)} %pad_add_fusion.place, bf16[768,1280]{1,0:T(8,128)(2,1)} %copy-done.1, bf16[768,1280]{1,0:T(8,128)(2,1)} %copy-done, f32[1280,1280]{1,0:T(8,128)S(1)} %get-tuple-element.28.partial), custom_call_target="tpu_custom_call" | custom-call | flops 2516582400 | bytes 9830400 | tf_op jit(solution)/shard_map/cross_term/pallas_call | solution.py:191
  27.0 1.4 %collective-permute-start.5 = (bf16[4,80,1280]{2,1,0:T(8,128)(2,1)}, bf16[4,80,1280]{2,1,0:T(8,128)(2,1)S(1)}, u32[]{:S(2)}, u32[]{:S(2)}) collective-permute-start(bf16[4,80,1280]{2,1,0:T(8,128)(2,1)} %get-tuple-element.29.after), channel_id=1, source_target_pairs={{0,34},{2,8},{10,40},{8,18},{16,50},{18,24},{26,56},{24,2},{34,64}... | collective-permute-start | bytes 2457608 | tf_op jit(solution)/shard_map/ppermute | solution.py:37
  28.4 2.6 %collective-permute-start.6 = (bf16[4,80,1280]{2,1,0:T(8,128)(2,1)}, bf16[4,80,1280]{2,1,0:T(8,128)(2,1)S(1)}, u32[]{:S(2)}, u32[]{:S(2)}) collective-permute-start(bf16[4,80,1280]{2,1,0:T(8,128)(2,1)} %get-tuple-element.36), channel_id=1, source_target_pairs={{0,64},{2,18},{10,74},{8,24},{16,80},{18,2},{26,90},{24,8},{34,98}... | collective-permute-start | bytes 2457608 | tf_op jit(solution)/shard_map/ppermute | solution.py:37
  31.0 1.7 %collective-permute-start.7 = (bf16[4,80,1280]{2,1,0:T(8,128)(2,1)}, bf16[4,80,1280]{2,1,0:T(8,128)(2,1)S(1)}, u32[]{:S(2)}, u32[]{:S(2)}) collective-permute-start(bf16[4,80,1280]{2,1,0:T(8,128)(2,1)} %get-tuple-element.37), channel_id=1, source_target_pairs={{0,98},{2,24},{10,104},{8,2},{16,114},{18,8},{26,120},{24,18},{34,... | collective-permute-start | bytes 2457608 | tf_op jit(solution)/shard_map/ppermute | solution.py:37
  32.7 1.3 copy-done.2
  34.0 15.9 %factor_term.1 = (bf16[4,160,1280]{2,1,0:T(8,128)(2,1)}, bf16[4,160,1280]{2,1,0:T(8,128)(2,1)}, bf16[2,160,1280]{2,1,0:T(8,128)(2,1)}, bf16[2,160,1280]{2,1,0:T(8,128)(2,1)}, bf16[4,160,1280]{2,1,0:T(8,128)(2,1)}) custom-call(s32[4]{0:T(128)S(1)} %pad_add_fusion.place, bf16[768,2560]{1,0:T(8,128)(2,1)} %h_own.1, bf16[768,2560]{1,0:T(8,128)(2,1)} %g_own.1, ...), custom_call_target="tpu_custom_call" | custom-call | flops 10066329600 | bytes 15728640 | tf_op jit(solution)/shard_map/factor_term/pallas_call | solution.py:263
  50.0 0.1 collective-permute-start.3
  50.1 2.9 %collective-permute-start.4 = (bf16[2,160,1280]{2,1,0:T(8,128)(2,1)}, bf16[2,160,1280]{2,1,0:T(8,128)(2,1)}, u32[]{:S(2)}, u32[]{:S(2)}) collective-permute-start(bf16[2,160,1280]{2,1,0:T(8,128)(2,1)} %get-tuple-element.34), channel_id=1, source_target_pairs={{0,98},{2,24},{10,104},{8,2},{16,114},{18,8},{26,120},{24,18},{34,... | collective-permute-start | bytes 2457608 | tf_op jit(solution)/shard_map/ppermute | solution.py:37
  53.0 2.2 %fold.2 = (f32[80,1280]{1,0:T(8,128)}, bf16[80,1280]{1,0:T(8,128)(2,1)}, bf16[80,1280]{1,0:T(8,128)(2,1)}, bf16[80,1280]{1,0:T(8,128)(2,1)S(1)}) custom-call(s32[1]{0:T(128)} %bitcast.1.me, bf16[4,80,1280]{2,1,0:T(8,128)(2,1)} %get-tuple-element.35.refs_0_, bf16[4,80,1280]{2,1,0:T(8,128)(2,1)S(1)} %collective-permute-done.5.refs_1_, ...), custom_call_target="tpu_custom_call" | custom-call | tf_op jit(solution)/shard_map/fold/pallas_call | solution.py:310
  55.2 1.3 collective-permute-start.8
  56.5 3.3 %collective-permute-start.9 = (bf16[80,1280]{1,0:T(8,128)(2,1)}, bf16[80,1280]{1,0:T(8,128)(2,1)S(1)}, u32[]{:S(2)}, u32[]{:S(2)}) collective-permute-start(bf16[80,1280]{1,0:T(8,128)(2,1)} %get-tuple-element.39), channel_id=1, source_target_pairs={{0,16},{2,66},{10,26},{8,72},{16,0},{18,82},{26,10},{24,88},{34,50... | collective-permute-start | bytes 614408 | tf_op jit(solution)/shard_map/ppermute | solution.py:37
  59.8 1.7 %collective-permute-start.10 = (bf16[80,1280]{1,0:T(8,128)(2,1)S(1)}, bf16[80,1280]{1,0:T(8,128)(2,1)S(1)}, u32[]{:S(2)}, u32[]{:S(2)}) collective-permute-start(bf16[80,1280]{1,0:T(8,128)(2,1)S(1)} %get-tuple-element.40), channel_id=1, source_target_pairs={{0,26},{2,96},{10,0},{8,106},{16,10},{18,112},{26,16},{24,122},{34... | collective-permute-start | bytes 614408 | tf_op jit(solution)/shard_map/ppermute | solution.py:37
  61.5 5.5 %collective-permute-done.8.refs_0_.refs_1_ = bf16[80,1280]{1,0:T(8,128)(2,1)S(1)} collective-permute-done((bf16[80,1280]{1,0:T(8,128)(2,1)}, bf16[80,1280]{1,0:T(8,128)(2,1)S(1)}, u32[]{:S(2)}, u32[]{:S(2)}) %collective-permute-start.8) | collective-permute-done | bytes 204832 | tf_op jit(solution)/shard_map/ppermute | solution.py:37
  67.0 0.9 collective-permute-done.10.refs_2_.refs_3_
  67.9 1.2 settle.2
  69.1 1.3 collective-permute-start.15
  70.4 2.6 %collective-permute-start.13 = (f32[40,1280]{1,0:T(8,128)S(1)}, f32[40,1280]{1,0:T(8,128)S(1)}, u32[]{:S(2)}, u32[]{:S(2)}) collective-permute-start(f32[40,1280]{1,0:T(8,128)S(1)} %get-tuple-element.44.a), channel_id=1, source_target_pairs={{0,1},{1,0},{2,3},{3,2},{4,5},{5,4},{6,7},{7,6},{8,9},{9,8},{10,11... | collective-permute-start | bytes 614408 | tf_op jit(solution)/shard_map/ppermute | solution.py:25
  73.0 0.1 collective-permute-start.14
  73.0 3.6 %grow.1 = (bf16[4,160,1280]{2,1,0:T(8,128)(2,1)}, bf16[4,160,1280]{2,1,0:T(8,128)(2,1)}) custom-call(bf16[4,160,1280]{2,1,0:T(8,128)(2,1)} %get-tuple-element.31.right, bf16[4,160,1280]{2,1,0:T(8,128)(2,1)} %get-tuple-element.32.left, bf16[2,160,1280]{2,1,0:T(8,128)(2,1)S(1)} %collective-permute-done.3.from_left, ...), custom_call_target="tpu_custom_call", output_to_operand_aliasing={{0}: (0, {}), {1}: (1, {})} | custom-call | tf_op jit(solution)/shard_map/grow/pallas_call | solution.py:377
  76.6 2.4 %collective-permute-start.11 = (bf16[4,160,1280]{2,1,0:T(8,128)(2,1)}, bf16[4,160,1280]{2,1,0:T(8,128)(2,1)S(1)}, u32[]{:S(2)}, u32[]{:S(2)}) collective-permute-start(bf16[4,160,1280]{2,1,0:T(8,128)(2,1)} %get-tuple-element.41), channel_id=1, source_target_pairs={{0,34},{2,8},{10,40},{8,18},{16,50},{18,24},{26,56},{24,2},{34,64}... | collective-permute-start | bytes 4915208 | tf_op jit(solution)/shard_map/ppermute | solution.py:37
  79.0 0.8 collective-permute-start.12
  79.8 2.9 %left_own.1.rest_0_ = f32[80,1280]{1,0:T(8,128)S(1)} custom-call(s32[4]{0:T(128)S(1)} %pad_add_fusion.place, f32[40,1280]{1,0:T(8,128)S(1)} %get-tuple-element.44.a, f32[40,1280]{1,0:T(8,128)S(1)} %collective-permute-done.15.b, bf16[2560,1280]{1,0:T(8,128)(2,1)} %left.3), custom_call_target="tpu_custom_call" | custom-call | tf_op jit(solution)/shard_map/left_own/pallas_call | solution.py:452
  82.7 0.3 collective-permute-done.13.a
  83.0 2.2 %collective-permute-done.14.b = f32[40,1280]{1,0:T(8,128)S(1)} collective-permute-done((f32[40,1280]{1,0:T(8,128)S(1)}, f32[40,1280]{1,0:T(8,128)S(1)}, u32[]{:S(2)}, u32[]{:S(2)}) %collective-permute-start.14) | collective-permute-done | bytes 204832 | tf_op jit(solution)/shard_map/ppermute | solution.py:556
  85.2 4.0 %left_product.1.refs_3_ = bf16[128,16,128]{2,1,0:T(8,128)(2,1)} custom-call(s32[4]{0:T(128)S(1)} %pad_add_fusion.place, f32[40,1280]{1,0:T(8,128)S(1)} %collective-permute-done.13.a, f32[40,1280]{1,0:T(8,128)S(1)} %collective-permute-done.14.b, bf16[2560,1280]{1,0:T(8,128)(2,1)} %left.3, f32[80,1280]{1,0:T(8,128)S(1)} %left_own.1.rest_0_), custom_call_target="tpu_custom_call" | custom-call | flops 16777216000 | tf_op jit(solution)/shard_map/left_product/pallas_call | solution.py:452
  89.2 6.3 %all-to-all-start = ((bf16[128,16,128]{2,1,0:T(8,128)(2,1)}), bf16[128,16,128]{2,1,0:T(8,128)(2,1)}, u32[]{:S(2)}, u32[]{:S(2)}) async-start(bf16[128,16,128]{2,1,0:T(8,128)(2,1)} %left_product.1.refs_3_), calls=%async_computation | async-start | bytes 1048576 | tf_op jit(solution)/shard_map/all_to_all | solution.py:559
  95.5 5.5 %collective-permute-done.11.refs_1_ = bf16[4,160,1280]{2,1,0:T(8,128)(2,1)S(1)} collective-permute-done((bf16[4,160,1280]{2,1,0:T(8,128)(2,1)}, bf16[4,160,1280]{2,1,0:T(8,128)(2,1)S(1)}, u32[]{:S(2)}, u32[]{:S(2)}) %collective-permute-start.11) | collective-permute-done | bytes 1638432 | tf_op jit(solution)/shard_map/ppermute | solution.py:37
  101.0 4.0 %collective-permute-done.12.refs_2_ = bf16[4,160,1280]{2,1,0:T(8,128)(2,1)S(1)} collective-permute-done((bf16[4,160,1280]{2,1,0:T(8,128)(2,1)}, bf16[4,160,1280]{2,1,0:T(8,128)(2,1)S(1)}, u32[]{:S(2)}, u32[]{:S(2)}) %collective-permute-start.12) | collective-permute-done | bytes 1638432 | tf_op jit(solution)/shard_map/ppermute | solution.py:37
  105.1 2.8 %fold.3 = (f32[160,1280]{1,0:T(8,128)}, bf16[160,1280]{1,0:T(8,128)(2,1)}, bf16[160,1280]{1,0:T(8,128)(2,1)}, bf16[160,1280]{1,0:T(8,128)(2,1)}) custom-call(s32[1]{0:T(128)} %bitcast.1.me, bf16[4,160,1280]{2,1,0:T(8,128)(2,1)} %get-tuple-element.30.refs_4_.refs_0_, bf16[4,160,1280]{2,1,0:T(8,128)(2,1)S(1)} %collective-permute-done.11.refs_1_, ...), custom_call_target="tpu_custom_call" | custom-call | tf_op jit(solution)/shard_map/fold/pallas_call | solution.py:310
  107.9 0.6 collective-permute-start.16
  108.4 3.9 %collective-permute-start.17 = (bf16[160,1280]{1,0:T(8,128)(2,1)}, bf16[160,1280]{1,0:T(8,128)(2,1)S(1)}, u32[]{:S(2)}, u32[]{:S(2)}) collective-permute-start(bf16[160,1280]{1,0:T(8,128)(2,1)} %get-tuple-element.48), channel_id=1, source_target_pairs={{0,16},{2,66},{10,26},{8,72},{16,0},{18,82},{26,10},{24,88},{34,50... | collective-permute-start | bytes 1228808 | tf_op jit(solution)/shard_map/ppermute | solution.py:37
  112.3 5.7 %right_product.1.refs_4_ = f32[40,1280]{1,0:T(8,128)} custom-call(s32[4]{0:T(128)S(1)} %pad_add_fusion.place, bf16[128,16,128]{2,1,0:T(8,128)(2,1)} %all-to-all-done.blocks, bf16[2560,1280]{1,0:T(8,128)(2,1)} %right.1, bf16[160,1280]{1,0:T(8,128)(2,1)} %get-tuple-element.47.late), custom_call_target="tpu_custom_call" | custom-call | flops 41943040000 | bytes 6553600 | tf_op jit(solution)/shard_map/right_product/pallas_call | solution.py:494
  118.0 4.2 %collective-permute-done.17.refs_2_ = bf16[160,1280]{1,0:T(8,128)(2,1)S(1)} collective-permute-done((bf16[160,1280]{1,0:T(8,128)(2,1)}, bf16[160,1280]{1,0:T(8,128)(2,1)S(1)}, u32[]{:S(2)}, u32[]{:S(2)}) %collective-permute-start.17) | collective-permute-done | bytes 409632 | tf_op jit(solution)/shard_map/ppermute | solution.py:37
  122.2 0.1 collective-permute-done.18.refs_3_
  122.3 1.5 %settle.3 = (f32[80,1280]{1,0:T(8,128)S(1)}, bf16[80,1280]{1,0:T(8,128)(2,1)S(1)}) custom-call(s32[1]{0:T(128)} %bitcast.xl, f32[160,1280]{1,0:T(8,128)} %get-tuple-element.46.refs_0_, bf16[160,1280]{1,0:T(8,128)(2,1)S(1)} %collective-permute-done.16.refs_1_, bf16[160,1280]{1,0:T(8,128)(2,1)S(1)} %collective-permute-done.17.refs_2_, ...), custom_call_target="tpu_custom_call" | custom-call | tf_op jit(solution)/shard_map/settle/pallas_call | solution.py:344
  123.8 0.1 collective-permute-start.19
  123.9 6.6 %collective-permute-done.19 = bf16[80,1280]{1,0:T(8,128)(2,1)S(1)} collective-permute-done((bf16[80,1280]{1,0:T(8,128)(2,1)S(1)}, bf16[80,1280]{1,0:T(8,128)(2,1)S(1)}, u32[]{:S(2)}, u32[]{:S(2)}) %collective-permute-start.19) | collective-permute-done | bytes 204832 | tf_op jit(solution)/shard_map/ppermute | solution.py:25
  130.6 0.9 collective-permute-start.20
  131.5 1.1 collective-permute-done.20
  132.7 0.8 maximum_bitcast_fusion
  (20 shorter events, 0.1 us)
Async XLA Ops:
  5.0 11.8 %collective-permute-start = (bf16[768,1280]{1,0:T(8,128)(2,1)}, bf16[768,1280]{1,0:T(8,128)(2,1)S(1)}, u32[]{:S(2)}, u32[]{:S(2)}) collective-permute-start(bf16[768,1280]{1,0:T(8,128)(2,1)} %cut.2), channel_id=1, source_target_pairs={{0,2},{2,0},{1,3},{3,1},{4,6},{6,4},{5,7},{7,5},{8,10},{10,8},{9,1... | collective-permute-start | bytes 5898248 | tf_op jit(solution)/shard_map/ppermute | solution.py:25
  10.7 6.2 %collective-permute-start.1 = (bf16[768,1280]{1,0:T(8,128)(2,1)}, bf16[768,1280]{1,0:T(8,128)(2,1)S(1)}, u32[]{:S(2)}, u32[]{:S(2)}) collective-permute-start(bf16[768,1280]{1,0:T(8,128)(2,1)} %cut.3), channel_id=1, source_target_pairs={{0,2},{2,0},{1,3},{3,1},{4,6},{6,4},{5,7},{7,5},{8,10},{10,8},{9,1... | collective-permute-start | bytes 5898248 | tf_op jit(solution)/shard_map/ppermute | solution.py:25
  16.3 16.5 %collective-permute-start.2 = (bf16[768,1280]{1,0:T(8,128)(2,1)}, bf16[768,1280]{1,0:T(8,128)(2,1)S(1)}, u32[]{:S(2)}, u32[]{:S(2)}) collective-permute-start(bf16[768,1280]{1,0:T(8,128)(2,1)} %get-tuple-element.27), channel_id=1, source_target_pairs={{0,2},{2,0},{1,3},{3,1},{4,6},{6,4},{5,7},{7,5},{8,10},{10,8},{9,1... | collective-permute-start | bytes 5898248 | tf_op jit(solution)/shard_map/ppermute | solution.py:25
  16.9 1.3 copy-start
  16.9 1.9 %copy-start.1 = (bf16[768,1280]{1,0:T(8,128)(2,1)}, bf16[768,1280]{1,0:T(8,128)(2,1)S(1)}, u32[]{:S(2)}) copy-start(bf16[768,1280]{1,0:T(8,128)(2,1)S(1)} %collective-permute-done.1.a.g_next) | copy-start | bytes 5898244
  27.0 26.0 %collective-permute-start.5 = (bf16[4,80,1280]{2,1,0:T(8,128)(2,1)}, bf16[4,80,1280]{2,1,0:T(8,128)(2,1)S(1)}, u32[]{:S(2)}, u32[]{:S(2)}) collective-permute-start(bf16[4,80,1280]{2,1,0:T(8,128)(2,1)} %get-tuple-element.29.after), channel_id=1, source_target_pairs={{0,34},{2,8},{10,40},{8,18},{16,50},{18,24},{26,56},{24,2},{34,64}... | collective-permute-start | bytes 2457608 | tf_op jit(solution)/shard_map/ppermute | solution.py:37
  28.4 24.6 %collective-permute-start.6 = (bf16[4,80,1280]{2,1,0:T(8,128)(2,1)}, bf16[4,80,1280]{2,1,0:T(8,128)(2,1)S(1)}, u32[]{:S(2)}, u32[]{:S(2)}) collective-permute-start(bf16[4,80,1280]{2,1,0:T(8,128)(2,1)} %get-tuple-element.36), channel_id=1, source_target_pairs={{0,64},{2,18},{10,74},{8,24},{16,80},{18,2},{26,90},{24,8},{34,98}... | collective-permute-start | bytes 2457608 | tf_op jit(solution)/shard_map/ppermute | solution.py:37
  31.0 22.0 %collective-permute-start.7 = (bf16[4,80,1280]{2,1,0:T(8,128)(2,1)}, bf16[4,80,1280]{2,1,0:T(8,128)(2,1)S(1)}, u32[]{:S(2)}, u32[]{:S(2)}) collective-permute-start(bf16[4,80,1280]{2,1,0:T(8,128)(2,1)} %get-tuple-element.37), channel_id=1, source_target_pairs={{0,98},{2,24},{10,104},{8,2},{16,114},{18,8},{26,120},{24,18},{34,... | collective-permute-start | bytes 2457608 | tf_op jit(solution)/shard_map/ppermute | solution.py:37
  32.7 1.3 copy-start.2
  50.0 23.1 %collective-permute-start.3 = (bf16[2,160,1280]{2,1,0:T(8,128)(2,1)}, bf16[2,160,1280]{2,1,0:T(8,128)(2,1)S(1)}, u32[]{:S(2)}, u32[]{:S(2)}) collective-permute-start(bf16[2,160,1280]{2,1,0:T(8,128)(2,1)} %get-tuple-element.33), channel_id=1, source_target_pairs={{0,34},{2,8},{10,40},{8,18},{16,50},{18,24},{26,56},{24,2},{34,64}... | collective-permute-start | bytes 2457608 | tf_op jit(solution)/shard_map/ppermute | solution.py:37
  50.1 23.0 %collective-permute-start.4 = (bf16[2,160,1280]{2,1,0:T(8,128)(2,1)}, bf16[2,160,1280]{2,1,0:T(8,128)(2,1)}, u32[]{:S(2)}, u32[]{:S(2)}) collective-permute-start(bf16[2,160,1280]{2,1,0:T(8,128)(2,1)} %get-tuple-element.34), channel_id=1, source_target_pairs={{0,98},{2,24},{10,104},{8,2},{16,114},{18,8},{26,120},{24,18},{34,... | collective-permute-start | bytes 2457608 | tf_op jit(solution)/shard_map/ppermute | solution.py:37
  55.2 11.8 %collective-permute-start.8 = (bf16[80,1280]{1,0:T(8,128)(2,1)}, bf16[80,1280]{1,0:T(8,128)(2,1)S(1)}, u32[]{:S(2)}, u32[]{:S(2)}) collective-permute-start(bf16[80,1280]{1,0:T(8,128)(2,1)} %get-tuple-element.38), channel_id=1, source_target_pairs={{0,10},{2,32},{10,16},{8,42},{16,26},{18,48},{26,0},{24,58},{34,40... | collective-permute-start | bytes 614408 | tf_op jit(solution)/shard_map/ppermute | solution.py:37
  56.5 10.5 %collective-permute-start.9 = (bf16[80,1280]{1,0:T(8,128)(2,1)}, bf16[80,1280]{1,0:T(8,128)(2,1)S(1)}, u32[]{:S(2)}, u32[]{:S(2)}) collective-permute-start(bf16[80,1280]{1,0:T(8,128)(2,1)} %get-tuple-element.39), channel_id=1, source_target_pairs={{0,16},{2,66},{10,26},{8,72},{16,0},{18,82},{26,10},{24,88},{34,50... | collective-permute-start | bytes 614408 | tf_op jit(solution)/shard_map/ppermute | solution.py:37
  59.8 8.1 %collective-permute-start.10 = (bf16[80,1280]{1,0:T(8,128)(2,1)S(1)}, bf16[80,1280]{1,0:T(8,128)(2,1)S(1)}, u32[]{:S(2)}, u32[]{:S(2)}) collective-permute-start(bf16[80,1280]{1,0:T(8,128)(2,1)S(1)} %get-tuple-element.40), channel_id=1, source_target_pairs={{0,26},{2,96},{10,0},{8,106},{16,10},{18,112},{26,16},{24,122},{34... | collective-permute-start | bytes 614408 | tf_op jit(solution)/shard_map/ppermute | solution.py:37
  69.1 10.7 %collective-permute-start.15 = (f32[40,1280]{1,0:T(8,128)S(1)}, f32[40,1280]{1,0:T(8,128)S(1)}, u32[]{:S(2)}, u32[]{:S(2)}) collective-permute-start(f32[40,1280]{1,0:T(8,128)S(1)} %get-tuple-element.45), channel_id=1, source_target_pairs={{0,4},{4,0},{1,5},{5,1},{2,6},{6,2},{3,7},{7,3},{8,12},{12,8},{9,1... | collective-permute-start | bytes 614408 | tf_op jit(solution)/shard_map/ppermute | solution.py:25
  70.4 12.7 %collective-permute-start.13 = (f32[40,1280]{1,0:T(8,128)S(1)}, f32[40,1280]{1,0:T(8,128)S(1)}, u32[]{:S(2)}, u32[]{:S(2)}) collective-permute-start(f32[40,1280]{1,0:T(8,128)S(1)} %get-tuple-element.44.a), channel_id=1, source_target_pairs={{0,1},{1,0},{2,3},{3,2},{4,5},{5,4},{6,7},{7,6},{8,9},{9,8},{10,11... | collective-permute-start | bytes 614408 | tf_op jit(solution)/shard_map/ppermute | solution.py:25
  73.0 12.2 %collective-permute-start.14 = (f32[40,1280]{1,0:T(8,128)S(1)}, f32[40,1280]{1,0:T(8,128)S(1)}, u32[]{:S(2)}, u32[]{:S(2)}) collective-permute-start(f32[40,1280]{1,0:T(8,128)S(1)} %get-tuple-element.45), channel_id=1, source_target_pairs={{0,5},{1,4},{4,1},{5,0},{2,7},{3,6},{6,3},{7,2},{8,13},{9,12},{12,... | collective-permute-start | bytes 614408 | tf_op jit(solution)/shard_map/ppermute | solution.py:556
  76.6 24.4 %collective-permute-start.11 = (bf16[4,160,1280]{2,1,0:T(8,128)(2,1)}, bf16[4,160,1280]{2,1,0:T(8,128)(2,1)S(1)}, u32[]{:S(2)}, u32[]{:S(2)}) collective-permute-start(bf16[4,160,1280]{2,1,0:T(8,128)(2,1)} %get-tuple-element.41), channel_id=1, source_target_pairs={{0,34},{2,8},{10,40},{8,18},{16,50},{18,24},{26,56},{24,2},{34,64}... | collective-permute-start | bytes 4915208 | tf_op jit(solution)/shard_map/ppermute | solution.py:37
  79.0 26.0 %collective-permute-start.12 = (bf16[4,160,1280]{2,1,0:T(8,128)(2,1)}, bf16[4,160,1280]{2,1,0:T(8,128)(2,1)S(1)}, u32[]{:S(2)}, u32[]{:S(2)}) collective-permute-start(bf16[4,160,1280]{2,1,0:T(8,128)(2,1)} %get-tuple-element.42), channel_id=1, source_target_pairs={{0,98},{2,24},{10,104},{8,2},{16,114},{18,8},{26,120},{24,18},{34,... | collective-permute-start | bytes 4915208 | tf_op jit(solution)/shard_map/ppermute | solution.py:37
  89.2 23.1 %all-to-all-start = ((bf16[128,16,128]{2,1,0:T(8,128)(2,1)}), bf16[128,16,128]{2,1,0:T(8,128)(2,1)}, u32[]{:S(2)}, u32[]{:S(2)}) async-start(bf16[128,16,128]{2,1,0:T(8,128)(2,1)} %left_product.1.refs_3_), calls=%async_computation | async-start | bytes 1048576 | tf_op jit(solution)/shard_map/all_to_all | solution.py:559
  107.9 10.1 %collective-permute-start.16 = (bf16[160,1280]{1,0:T(8,128)(2,1)}, bf16[160,1280]{1,0:T(8,128)(2,1)S(1)}, u32[]{:S(2)}, u32[]{:S(2)}) collective-permute-start(bf16[160,1280]{1,0:T(8,128)(2,1)} %get-tuple-element.47.late), channel_id=1, source_target_pairs={{0,10},{2,32},{10,16},{8,42},{16,26},{18,48},{26,0},{24,58},{34,40... | collective-permute-start | bytes 1228808 | tf_op jit(solution)/shard_map/ppermute | solution.py:37
  108.4 13.8 %collective-permute-start.17 = (bf16[160,1280]{1,0:T(8,128)(2,1)}, bf16[160,1280]{1,0:T(8,128)(2,1)S(1)}, u32[]{:S(2)}, u32[]{:S(2)}) collective-permute-start(bf16[160,1280]{1,0:T(8,128)(2,1)} %get-tuple-element.48), channel_id=1, source_target_pairs={{0,16},{2,66},{10,26},{8,72},{16,0},{18,82},{26,10},{24,88},{34,50... | collective-permute-start | bytes 1228808 | tf_op jit(solution)/shard_map/ppermute | solution.py:37
  112.3 10.0 %collective-permute-start.18 = (bf16[160,1280]{1,0:T(8,128)(2,1)}, bf16[160,1280]{1,0:T(8,128)(2,1)S(1)}, u32[]{:S(2)}, u32[]{:S(2)}) collective-permute-start(bf16[160,1280]{1,0:T(8,128)(2,1)} %get-tuple-element.49), channel_id=1, source_target_pairs={{0,26},{2,96},{10,0},{8,106},{16,10},{18,112},{26,16},{24,122},{34... | collective-permute-start | bytes 1228808 | tf_op jit(solution)/shard_map/ppermute | solution.py:37
  123.8 6.7 %collective-permute-start.19 = (bf16[80,1280]{1,0:T(8,128)(2,1)S(1)}, bf16[80,1280]{1,0:T(8,128)(2,1)S(1)}, u32[]{:S(2)}, u32[]{:S(2)}) collective-permute-start(bf16[80,1280]{1,0:T(8,128)(2,1)S(1)} %get-tuple-element.51), channel_id=1, source_target_pairs={{0,4},{4,0},{1,5},{5,1},{2,6},{6,2},{3,7},{7,3},{8,12},{12,8},{9,1... | collective-permute-start | bytes 614408 | tf_op jit(solution)/shard_map/ppermute | solution.py:25
  130.6 2.0 %collective-permute-start.20 = (f32[40,1280]{1,0:T(8,128)S(1)}, f32[40,1280]{1,0:T(8,128)S(1)}, u32[]{:S(2)}, u32[]{:S(2)}) collective-permute-start(f32[40,1280]{1,0:T(8,128)S(1)} %dynamic-slice_bitcast_fusion), channel_id=1, source_target_pairs={{0,2},{2,0},{1,3},{3,1},{4,6},{6,4},{5,7},{7,5},{8,10},{10,8},{9,1... | collective-permute-start | bytes 614408 | tf_op jit(solution)/shard_map/ppermute | solution.py:25

commit v20 on v17

--- a/solution.py
+++ b/solution.py
@@ -484,7 +484,7 @@
     partial = cross_own(place, out_grad, hidden)
 
     own, m1, m2, m3 = cross_term(place, grads_next, acts_next, partial)
-    m_parts = [own, turn(m1, 1, 0), turn(m2, 2, 0), turn(m3, 3, 0)]
+    m_parts = [own, turn(m1, 1, 0), turn(m3, 3, 0), turn(m2, 2, 0)]
 
     f_own, right, far_a, far_b, left = factor_term(
         place, hidden, out_grad, acts_next, grads_next, in_hbm(m1)
@@ -494,7 +494,7 @@
     my_xl = xl.astype(jnp.int32)[None]
 
     def second_sends(pieces):
-        return [turn(piece, s, 1) for s, piece in enumerate(pieces, 1)]
+        return [turn(pieces[s - 1], s, 1) for s in (1, 3, 2)]
 
     m, *m_pieces = fold(second_me, m_parts, in_hbm(f_own))
     m_received = second_sends(m_pieces)

time: 128 us -> 126 us (0.984)
  waiting for transfers between devices: 36.2 us -> 34.9 us
    ppermute x13, starting transfers between devices: 23.1 us -> 21.8 us  [turn(): return lax.ppermute(x, ('z', 'y', 'c'), pairs)]
  transfers between devices with their start and end apart: 21 -> 21, of which waited for: 10 -> 9; matrix products, arithmetic and copies ran while one was open for 0% -> 0% of each run, Pallas kernels for 34% -> 35%
where the time goes in v20:
time: 126 us
  Pallas kernels  53.4 us (42%)
  starting transfers between devices  35.8 us (28%)
  waiting for transfers between devices  34.9 us (28%)
    ppermute x13, starting transfers between devices, turn(): return lax.ppermute(x, ('z', 'y', 'c'), pairs)  21.8 us
    ppermute x13, waiting for transfers between devices, turn(): return lax.ppermute(x, ('z', 'y', 'c'), pairs)  18.9 us
    pallas_call x1, Pallas kernels, factor_term(): pl.pallas_call(factor_kernel, out_shape=[out, out, side, side, out], grid...  15.9 us
    ppermute x6, waiting for transfers between devices, shift(): return lax.ppermute(x, axis, [(i, (i + step) % size) for i in range(size)])  14.5 us
    pallas_call x1, Pallas kernels, cross_term(): pl.pallas_call(cross_kernel, out_shape=[out] * 4, grid_spec=pltpu.Prefetc...  8.31 us
    all_to_all x1, starting transfers between devices, per_device(): lax.all_to_all(products, ('o', 'c', 'z', 'y', 'xl'), 0, 0, tiled=True)  7.46 us
    pallas_call x2, Pallas kernels, left_product(): pl.pallas_call(functools.partial(left_kernel, own), out_shape=total if ow...  6.95 us
    ppermute x6, starting transfers between devices, shift(): return lax.ppermute(x, axis, [(i, (i + step) % size) for i in range(size)])  6.39 us
  transfers between devices with their start and end apart: 21, of which 9 were waited for; matrix products, arithmetic and copies ran while one was open for 0% of the time, Pallas kernels for 35%

profile of v20, /device:TPU:1, one launch (start us, length us, event | category | flops | bytes accessed | tf_op | source)
XLA Modules:
  0.0 125.8 jit_solution(5070532302567437693)
XLA Ops:
  0.6 1.5 %collective-permute-start = (bf16[768,2560]{1,0:T(8,128)(2,1)}, bf16[768,2560]{1,0:T(8,128)(2,1)}, u32[]{:S(2)}, u32[]{:S(2)}) collective-permute-start(bf16[768,2560]{1,0:T(8,128)(2,1)} %h_own.1), channel_id=1, source_target_pairs={{0,2},{2,0},{1,3},{3,1},{4,6},{6,4},{5,7},{7,5},{8,10},{10,8},{9,1... | collective-permute-start | bytes 11796488 | tf_op jit(solution)/shard_map/ppermute | solution.py:25
  2.1 0.1 collective-permute-start.1
  2.2 0.1 pad_add_fusion.place
  2.3 5.4 %cross_own.1.partial = f32[1280,1280]{1,0:T(8,128)S(1)} custom-call(s32[4]{0:T(128)S(1)} %pad_add_fusion.place, bf16[768,2560]{1,0:T(8,128)(2,1)} %g_own.1, bf16[768,2560]{1,0:T(8,128)(2,1)} %h_own.1), custom_call_target="tpu_custom_call" | custom-call | flops 2516582400 | bytes 7864320 | tf_op jit(solution)/shard_map/cross_own/pallas_call | solution.py:125
  7.7 1.1 collective-permute-done.b.h_next
  8.9 5.6 %collective-permute-done.1.a.g_next = bf16[768,2560]{1,0:T(8,128)(2,1)} collective-permute-done((bf16[768,2560]{1,0:T(8,128)(2,1)}, bf16[768,2560]{1,0:T(8,128)(2,1)}, u32[]{:S(2)}, u32[]{:S(2)}) %collective-permute-start.1) | collective-permute-done | bytes 3932192 | tf_op jit(solution)/shard_map/ppermute | solution.py:25
  14.5 8.3 %cross_term.1 = (bf16[4,80,1280]{2,1,0:T(8,128)(2,1)}, bf16[4,80,1280]{2,1,0:T(8,128)(2,1)}, bf16[4,80,1280]{2,1,0:T(8,128)(2,1)}, bf16[4,80,1280]{2,1,0:T(8,128)(2,1)}) custom-call(s32[4]{0:T(128)S(1)} %pad_add_fusion.place, bf16[768,2560]{1,0:T(8,128)(2,1)} %collective-permute-done.1.a.g_next, bf16[768,2560]{1,0:T(8,128)(2,1)} %collective-permute-done.b.h_next, ...), custom_call_target="tpu_custom_call" | custom-call | flops 2516582400 | bytes 9830400 | tf_op jit(solution)/shard_map/cross_term/pallas_call | solution.py:151
  22.8 1.7 %collective-permute-start.4 = (bf16[4,80,1280]{2,1,0:T(8,128)(2,1)}, bf16[4,80,1280]{2,1,0:T(8,128)(2,1)S(1)}, u32[]{:S(2)}, u32[]{:S(2)}) collective-permute-start(bf16[4,80,1280]{2,1,0:T(8,128)(2,1)} %get-tuple-element.25.after), channel_id=1, source_target_pairs={{0,34},{2,8},{10,40},{8,18},{16,50},{18,24},{26,56},{24,2},{34,64}... | collective-permute-start | bytes 2457608 | tf_op jit(solution)/shard_map/ppermute | solution.py:37
  24.5 1.5 %collective-permute-start.5 = (bf16[4,80,1280]{2,1,0:T(8,128)(2,1)}, bf16[4,80,1280]{2,1,0:T(8,128)(2,1)S(1)}, u32[]{:S(2)}, u32[]{:S(2)}) collective-permute-start(bf16[4,80,1280]{2,1,0:T(8,128)(2,1)} %get-tuple-element.32), channel_id=1, source_target_pairs={{0,98},{2,24},{10,104},{8,2},{16,114},{18,8},{26,120},{24,18},{34,... | collective-permute-start | bytes 2457608 | tf_op jit(solution)/shard_map/ppermute | solution.py:37
  26.1 1.6 %collective-permute-start.6 = (bf16[4,80,1280]{2,1,0:T(8,128)(2,1)}, bf16[4,80,1280]{2,1,0:T(8,128)(2,1)S(1)}, u32[]{:S(2)}, u32[]{:S(2)}) collective-permute-start(bf16[4,80,1280]{2,1,0:T(8,128)(2,1)} %get-tuple-element.33), channel_id=1, source_target_pairs={{0,64},{2,18},{10,74},{8,24},{16,80},{18,2},{26,90},{24,8},{34,98}... | collective-permute-start | bytes 2457608 | tf_op jit(solution)/shard_map/ppermute | solution.py:37
  27.6 15.9 %factor_term.1 = (bf16[4,160,1280]{2,1,0:T(8,128)(2,1)}, bf16[4,160,1280]{2,1,0:T(8,128)(2,1)}, bf16[2,160,1280]{2,1,0:T(8,128)(2,1)}, bf16[2,160,1280]{2,1,0:T(8,128)(2,1)}, bf16[4,160,1280]{2,1,0:T(8,128)(2,1)}) custom-call(s32[4]{0:T(128)S(1)} %pad_add_fusion.place, bf16[768,2560]{1,0:T(8,128)(2,1)} %h_own.1, bf16[768,2560]{1,0:T(8,128)(2,1)} %g_own.1, ...), custom_call_target="tpu_custom_call" | custom-call | flops 10066329600 | bytes 15728640 | tf_op jit(solution)/shard_map/factor_term/pallas_call | solution.py:214
  43.5 1.0 collective-permute-start.2
  44.5 2.0 %collective-permute-start.3 = (bf16[2,160,1280]{2,1,0:T(8,128)(2,1)}, bf16[2,160,1280]{2,1,0:T(8,128)(2,1)}, u32[]{:S(2)}, u32[]{:S(2)}) collective-permute-start(bf16[2,160,1280]{2,1,0:T(8,128)(2,1)} %get-tuple-element.30), channel_id=1, source_target_pairs={{0,98},{2,24},{10,104},{8,2},{16,114},{18,8},{26,120},{24,18},{34,... | collective-permute-start | bytes 2457608 | tf_op jit(solution)/shard_map/ppermute | solution.py:37
  46.5 0.0 collective-permute-done.4.refs_1_
  46.5 0.0 collective-permute-done.5.refs_2_
  46.5 0.0 collective-permute-done.6.refs_3_
  46.6 2.2 %fold.2 = (f32[80,1280]{1,0:T(8,128)}, bf16[80,1280]{1,0:T(8,128)(2,1)}, bf16[80,1280]{1,0:T(8,128)(2,1)S(1)}, bf16[80,1280]{1,0:T(8,128)(2,1)}) custom-call(s32[1]{0:T(128)} %bitcast.1.me, bf16[4,80,1280]{2,1,0:T(8,128)(2,1)} %get-tuple-element.31.refs_0_, bf16[4,80,1280]{2,1,0:T(8,128)(2,1)S(1)} %collective-permute-done.4.refs_1_, ...), custom_call_target="tpu_custom_call" | custom-call | tf_op jit(solution)/shard_map/fold/pallas_call | solution.py:261
  48.8 2.2 %collective-permute-start.7 = (bf16[80,1280]{1,0:T(8,128)(2,1)}, bf16[80,1280]{1,0:T(8,128)(2,1)S(1)}, u32[]{:S(2)}, u32[]{:S(2)}) collective-permute-start(bf16[80,1280]{1,0:T(8,128)(2,1)} %get-tuple-element.34), channel_id=1, source_target_pairs={{0,10},{2,32},{10,16},{8,42},{16,26},{18,48},{26,0},{24,58},{34,40... | collective-permute-start | bytes 614408 | tf_op jit(solution)/shard_map/ppermute | solution.py:37
  51.0 2.2 %collective-permute-start.8 = (bf16[80,1280]{1,0:T(8,128)(2,1)}, bf16[80,1280]{1,0:T(8,128)(2,1)S(1)}, u32[]{:S(2)}, u32[]{:S(2)}) collective-permute-start(bf16[80,1280]{1,0:T(8,128)(2,1)} %get-tuple-element.35), channel_id=1, source_target_pairs={{0,26},{2,96},{10,0},{8,106},{16,10},{18,112},{26,16},{24,122},{34... | collective-permute-start | bytes 614408 | tf_op jit(solution)/shard_map/ppermute | solution.py:37
  53.2 1.1 collective-permute-start.9
  54.3 7.2 %collective-permute-done.7.refs_0_.refs_1_ = bf16[80,1280]{1,0:T(8,128)(2,1)S(1)} collective-permute-done((bf16[80,1280]{1,0:T(8,128)(2,1)}, bf16[80,1280]{1,0:T(8,128)(2,1)S(1)}, u32[]{:S(2)}, u32[]{:S(2)}) %collective-permute-start.7) | collective-permute-done | bytes 204832 | tf_op jit(solution)/shard_map/ppermute | solution.py:37
  61.5 0.0 collective-permute-done.8.refs_1_.refs_2_
  61.5 0.0 collective-permute-done.9.refs_2_.refs_3_
  61.5 1.2 settle.2
  62.7 1.3 %collective-permute-start.14 = (f32[40,1280]{1,0:T(8,128)S(1)}, f32[40,1280]{1,0:T(8,128)S(1)}, u32[]{:S(2)}, u32[]{:S(2)}) collective-permute-start(f32[40,1280]{1,0:T(8,128)S(1)} %get-tuple-element.41), channel_id=1, source_target_pairs={{0,4},{4,0},{1,5},{5,1},{2,6},{6,2},{3,7},{7,3},{8,12},{12,8},{9,1... | collective-permute-start | bytes 614408 | tf_op jit(solution)/shard_map/ppermute | solution.py:25
  64.0 2.5 %collective-permute-start.12 = (f32[40,1280]{1,0:T(8,128)S(1)}, f32[40,1280]{1,0:T(8,128)S(1)}, u32[]{:S(2)}, u32[]{:S(2)}) collective-permute-start(f32[40,1280]{1,0:T(8,128)S(1)} %get-tuple-element.40.a), channel_id=1, source_target_pairs={{0,1},{1,0},{2,3},{3,2},{4,5},{5,4},{6,7},{7,6},{8,9},{9,8},{10,11... | collective-permute-start | bytes 614408 | tf_op jit(solution)/shard_map/ppermute | solution.py:25
  66.4 0.2 collective-permute-start.13
  66.6 3.5 %grow.1 = (bf16[4,160,1280]{2,1,0:T(8,128)(2,1)}, bf16[4,160,1280]{2,1,0:T(8,128)(2,1)}) custom-call(bf16[4,160,1280]{2,1,0:T(8,128)(2,1)} %get-tuple-element.27.right, bf16[4,160,1280]{2,1,0:T(8,128)(2,1)} %get-tuple-element.28.left, bf16[2,160,1280]{2,1,0:T(8,128)(2,1)S(1)} %collective-permute-done.2.from_left, ...), custom_call_target="tpu_custom_call", output_to_operand_aliasing={{0}: (0, {}), {1}: (1, {})} | custom-call | tf_op jit(solution)/shard_map/grow/pallas_call | solution.py:328
  70.2 2.2 %collective-permute-start.10 = (bf16[4,160,1280]{2,1,0:T(8,128)(2,1)}, bf16[4,160,1280]{2,1,0:T(8,128)(2,1)S(1)}, u32[]{:S(2)}, u32[]{:S(2)}) collective-permute-start(bf16[4,160,1280]{2,1,0:T(8,128)(2,1)} %get-tuple-element.37), channel_id=1, source_target_pairs={{0,34},{2,8},{10,40},{8,18},{16,50},{18,24},{26,56},{24,2},{34,64}... | collective-permute-start | bytes 4915208 | tf_op jit(solution)/shard_map/ppermute | solution.py:37
  72.3 1.5 %collective-permute-start.11 = (bf16[4,160,1280]{2,1,0:T(8,128)(2,1)}, bf16[4,160,1280]{2,1,0:T(8,128)(2,1)S(1)}, u32[]{:S(2)}, u32[]{:S(2)}) collective-permute-start(bf16[4,160,1280]{2,1,0:T(8,128)(2,1)} %get-tuple-element.38), channel_id=1, source_target_pairs={{0,98},{2,24},{10,104},{8,2},{16,114},{18,8},{26,120},{24,18},{34,... | collective-permute-start | bytes 4915208 | tf_op jit(solution)/shard_map/ppermute | solution.py:37
  73.9 2.9 %left_own.1.rest_0_ = f32[80,1280]{1,0:T(8,128)S(1)} custom-call(s32[4]{0:T(128)S(1)} %pad_add_fusion.place, f32[40,1280]{1,0:T(8,128)S(1)} %get-tuple-element.40.a, f32[40,1280]{1,0:T(8,128)S(1)} %collective-permute-done.14.b, bf16[2560,1280]{1,0:T(8,128)(2,1)} %left.3), custom_call_target="tpu_custom_call" | custom-call | tf_op jit(solution)/shard_map/left_own/pallas_call | solution.py:403
  76.8 1.5 %collective-permute-done.13.b = f32[40,1280]{1,0:T(8,128)S(1)} collective-permute-done((f32[40,1280]{1,0:T(8,128)S(1)}, f32[40,1280]{1,0:T(8,128)S(1)}, u32[]{:S(2)}, u32[]{:S(2)}) %collective-permute-start.13) | collective-permute-done | bytes 204832 | tf_op jit(solution)/shard_map/ppermute | solution.py:505
  78.3 4.0 %left_product.1.refs_3_ = bf16[128,16,128]{2,1,0:T(8,128)(2,1)} custom-call(s32[4]{0:T(128)S(1)} %pad_add_fusion.place, f32[40,1280]{1,0:T(8,128)S(1)} %collective-permute-done.12.a, f32[40,1280]{1,0:T(8,128)S(1)} %collective-permute-done.13.b, bf16[2560,1280]{1,0:T(8,128)(2,1)} %left.3, f32[80,1280]{1,0:T(8,128)S(1)} %left_own.1.rest_0_), custom_call_target="tpu_custom_call" | custom-call | flops 16777216000 | tf_op jit(solution)/shard_map/left_product/pallas_call | solution.py:403
  82.4 7.5 %all-to-all-start = ((bf16[128,16,128]{2,1,0:T(8,128)(2,1)}), bf16[128,16,128]{2,1,0:T(8,128)(2,1)}, u32[]{:S(2)}, u32[]{:S(2)}) async-start(bf16[128,16,128]{2,1,0:T(8,128)(2,1)} %left_product.1.refs_3_), calls=%async_computation | async-start | bytes 1048576 | tf_op jit(solution)/shard_map/all_to_all | solution.py:508
  89.8 3.6 %collective-permute-done.10.refs_1_ = bf16[4,160,1280]{2,1,0:T(8,128)(2,1)S(1)} collective-permute-done((bf16[4,160,1280]{2,1,0:T(8,128)(2,1)}, bf16[4,160,1280]{2,1,0:T(8,128)(2,1)S(1)}, u32[]{:S(2)}, u32[]{:S(2)}) %collective-permute-start.10) | collective-permute-done | bytes 1638432 | tf_op jit(solution)/shard_map/ppermute | solution.py:37
  93.4 3.9 %collective-permute-done.11.refs_2_ = bf16[4,160,1280]{2,1,0:T(8,128)(2,1)S(1)} collective-permute-done((bf16[4,160,1280]{2,1,0:T(8,128)(2,1)}, bf16[4,160,1280]{2,1,0:T(8,128)(2,1)S(1)}, u32[]{:S(2)}, u32[]{:S(2)}) %collective-permute-start.11) | collective-permute-done | bytes 1638432 | tf_op jit(solution)/shard_map/ppermute | solution.py:37
  97.3 2.8 %fold.3 = (f32[160,1280]{1,0:T(8,128)}, bf16[160,1280]{1,0:T(8,128)(2,1)}, bf16[160,1280]{1,0:T(8,128)(2,1)}, bf16[160,1280]{1,0:T(8,128)(2,1)}) custom-call(s32[1]{0:T(128)} %bitcast.1.me, bf16[4,160,1280]{2,1,0:T(8,128)(2,1)} %get-tuple-element.26.refs_4_.refs_0_, bf16[4,160,1280]{2,1,0:T(8,128)(2,1)S(1)} %collective-permute-done.10.refs_1_, ...), custom_call_target="tpu_custom_call" | custom-call | tf_op jit(solution)/shard_map/fold/pallas_call | solution.py:261
  100.1 2.5 %collective-permute-start.15 = (bf16[160,1280]{1,0:T(8,128)(2,1)}, bf16[160,1280]{1,0:T(8,128)(2,1)S(1)}, u32[]{:S(2)}, u32[]{:S(2)}) collective-permute-start(bf16[160,1280]{1,0:T(8,128)(2,1)} %get-tuple-element.43.late), channel_id=1, source_target_pairs={{0,10},{2,32},{10,16},{8,42},{16,26},{18,48},{26,0},{24,58},{34,40... | collective-permute-start | bytes 1228808 | tf_op jit(solution)/shard_map/ppermute | solution.py:37
  102.6 1.1 collective-permute-start.16
  103.7 1.1 collective-permute-start.17
  104.8 5.7 %right_product.1.refs_4_ = f32[40,1280]{1,0:T(8,128)} custom-call(s32[4]{0:T(128)S(1)} %pad_add_fusion.place, bf16[128,16,128]{2,1,0:T(8,128)(2,1)} %all-to-all-done.blocks, bf16[2560,1280]{1,0:T(8,128)(2,1)} %right.1, bf16[160,1280]{1,0:T(8,128)(2,1)} %get-tuple-element.43.late), custom_call_target="tpu_custom_call" | custom-call | flops 41943040000 | bytes 6553600 | tf_op jit(solution)/shard_map/right_product/pallas_call | solution.py:445
  110.5 4.2 %collective-permute-done.17.refs_3_ = bf16[160,1280]{1,0:T(8,128)(2,1)S(1)} collective-permute-done((bf16[160,1280]{1,0:T(8,128)(2,1)}, bf16[160,1280]{1,0:T(8,128)(2,1)S(1)}, u32[]{:S(2)}, u32[]{:S(2)}) %collective-permute-start.17) | collective-permute-done | bytes 409632 | tf_op jit(solution)/shard_map/ppermute | solution.py:37
  114.7 1.5 %settle.3 = (f32[80,1280]{1,0:T(8,128)S(1)}, bf16[80,1280]{1,0:T(8,128)(2,1)S(1)}) custom-call(s32[1]{0:T(128)} %bitcast.xl, f32[160,1280]{1,0:T(8,128)} %get-tuple-element.42.refs_0_, bf16[160,1280]{1,0:T(8,128)(2,1)S(1)} %collective-permute-done.15.refs_1_, bf16[160,1280]{1,0:T(8,128)(2,1)S(1)} %collective-permute-done.16.refs_2_, ...), custom_call_target="tpu_custom_call" | custom-call | tf_op jit(solution)/shard_map/settle/pallas_call | solution.py:295
  116.2 0.1 collective-permute-start.18
  116.3 6.6 %collective-permute-done.18 = bf16[80,1280]{1,0:T(8,128)(2,1)S(1)} collective-permute-done((bf16[80,1280]{1,0:T(8,128)(2,1)S(1)}, bf16[80,1280]{1,0:T(8,128)(2,1)S(1)}, u32[]{:S(2)}, u32[]{:S(2)}) %collective-permute-start.18) | collective-permute-done | bytes 204832 | tf_op jit(solution)/shard_map/ppermute | solution.py:25
  123.0 0.9 collective-permute-start.19
  123.9 1.1 collective-permute-done.19
  125.0 0.8 maximum_bitcast_fusion
  (10 shorter events, 0.1 us)
Async XLA Ops:
  0.6 8.3 %collective-permute-start = (bf16[768,2560]{1,0:T(8,128)(2,1)}, bf16[768,2560]{1,0:T(8,128)(2,1)}, u32[]{:S(2)}, u32[]{:S(2)}) collective-permute-start(bf16[768,2560]{1,0:T(8,128)(2,1)} %h_own.1), channel_id=1, source_target_pairs={{0,2},{2,0},{1,3},{3,1},{4,6},{6,4},{5,7},{7,5},{8,10},{10,8},{9,1... | collective-permute-start | bytes 11796488 | tf_op jit(solution)/shard_map/ppermute | solution.py:25
  2.1 12.4 %collective-permute-start.1 = (bf16[768,2560]{1,0:T(8,128)(2,1)}, bf16[768,2560]{1,0:T(8,128)(2,1)}, u32[]{:S(2)}, u32[]{:S(2)}) collective-permute-start(bf16[768,2560]{1,0:T(8,128)(2,1)} %g_own.1), channel_id=1, source_target_pairs={{0,2},{2,0},{1,3},{3,1},{4,6},{6,4},{5,7},{7,5},{8,10},{10,8},{9,1... | collective-permute-start | bytes 11796488 | tf_op jit(solution)/shard_map/ppermute | solution.py:25
  22.8 23.7 %collective-permute-start.4 = (bf16[4,80,1280]{2,1,0:T(8,128)(2,1)}, bf16[4,80,1280]{2,1,0:T(8,128)(2,1)S(1)}, u32[]{:S(2)}, u32[]{:S(2)}) collective-permute-start(bf16[4,80,1280]{2,1,0:T(8,128)(2,1)} %get-tuple-element.25.after), channel_id=1, source_target_pairs={{0,34},{2,8},{10,40},{8,18},{16,50},{18,24},{26,56},{24,2},{34,64}... | collective-permute-start | bytes 2457608 | tf_op jit(solution)/shard_map/ppermute | solution.py:37
  24.5 22.0 %collective-permute-start.5 = (bf16[4,80,1280]{2,1,0:T(8,128)(2,1)}, bf16[4,80,1280]{2,1,0:T(8,128)(2,1)S(1)}, u32[]{:S(2)}, u32[]{:S(2)}) collective-permute-start(bf16[4,80,1280]{2,1,0:T(8,128)(2,1)} %get-tuple-element.32), channel_id=1, source_target_pairs={{0,98},{2,24},{10,104},{8,2},{16,114},{18,8},{26,120},{24,18},{34,... | collective-permute-start | bytes 2457608 | tf_op jit(solution)/shard_map/ppermute | solution.py:37
  26.1 20.5 %collective-permute-start.6 = (bf16[4,80,1280]{2,1,0:T(8,128)(2,1)}, bf16[4,80,1280]{2,1,0:T(8,128)(2,1)S(1)}, u32[]{:S(2)}, u32[]{:S(2)}) collective-permute-start(bf16[4,80,1280]{2,1,0:T(8,128)(2,1)} %get-tuple-element.33), channel_id=1, source_target_pairs={{0,64},{2,18},{10,74},{8,24},{16,80},{18,2},{26,90},{24,8},{34,98}... | collective-permute-start | bytes 2457608 | tf_op jit(solution)/shard_map/ppermute | solution.py:37
  43.5 23.1 %collective-permute-start.2 = (bf16[2,160,1280]{2,1,0:T(8,128)(2,1)}, bf16[2,160,1280]{2,1,0:T(8,128)(2,1)S(1)}, u32[]{:S(2)}, u32[]{:S(2)}) collective-permute-start(bf16[2,160,1280]{2,1,0:T(8,128)(2,1)} %get-tuple-element.29), channel_id=1, source_target_pairs={{0,34},{2,8},{10,40},{8,18},{16,50},{18,24},{26,56},{24,2},{34,64}... | collective-permute-start | bytes 2457608 | tf_op jit(solution)/shard_map/ppermute | solution.py:37
  44.5 22.1 %collective-permute-start.3 = (bf16[2,160,1280]{2,1,0:T(8,128)(2,1)}, bf16[2,160,1280]{2,1,0:T(8,128)(2,1)}, u32[]{:S(2)}, u32[]{:S(2)}) collective-permute-start(bf16[2,160,1280]{2,1,0:T(8,128)(2,1)} %get-tuple-element.30), channel_id=1, source_target_pairs={{0,98},{2,24},{10,104},{8,2},{16,114},{18,8},{26,120},{24,18},{34,... | collective-permute-start | bytes 2457608 | tf_op jit(solution)/shard_map/ppermute | solution.py:37
  48.8 12.7 %collective-permute-start.7 = (bf16[80,1280]{1,0:T(8,128)(2,1)}, bf16[80,1280]{1,0:T(8,128)(2,1)S(1)}, u32[]{:S(2)}, u32[]{:S(2)}) collective-permute-start(bf16[80,1280]{1,0:T(8,128)(2,1)} %get-tuple-element.34), channel_id=1, source_target_pairs={{0,10},{2,32},{10,16},{8,42},{16,26},{18,48},{26,0},{24,58},{34,40... | collective-permute-start | bytes 614408 | tf_op jit(solution)/shard_map/ppermute | solution.py:37
  51.0 10.5 %collective-permute-start.8 = (bf16[80,1280]{1,0:T(8,128)(2,1)}, bf16[80,1280]{1,0:T(8,128)(2,1)S(1)}, u32[]{:S(2)}, u32[]{:S(2)}) collective-permute-start(bf16[80,1280]{1,0:T(8,128)(2,1)} %get-tuple-element.35), channel_id=1, source_target_pairs={{0,26},{2,96},{10,0},{8,106},{16,10},{18,112},{26,16},{24,122},{34... | collective-permute-start | bytes 614408 | tf_op jit(solution)/shard_map/ppermute | solution.py:37
  53.2 8.3 %collective-permute-start.9 = (bf16[80,1280]{1,0:T(8,128)(2,1)S(1)}, bf16[80,1280]{1,0:T(8,128)(2,1)S(1)}, u32[]{:S(2)}, u32[]{:S(2)}) collective-permute-start(bf16[80,1280]{1,0:T(8,128)(2,1)S(1)} %get-tuple-element.36), channel_id=1, source_target_pairs={{0,16},{2,66},{10,26},{8,72},{16,0},{18,82},{26,10},{24,88},{34,50... | collective-permute-start | bytes 614408 | tf_op jit(solution)/shard_map/ppermute | solution.py:37
  62.7 11.2 %collective-permute-start.14 = (f32[40,1280]{1,0:T(8,128)S(1)}, f32[40,1280]{1,0:T(8,128)S(1)}, u32[]{:S(2)}, u32[]{:S(2)}) collective-permute-start(f32[40,1280]{1,0:T(8,128)S(1)} %get-tuple-element.41), channel_id=1, source_target_pairs={{0,4},{4,0},{1,5},{5,1},{2,6},{6,2},{3,7},{7,3},{8,12},{12,8},{9,1... | collective-permute-start | bytes 614408 | tf_op jit(solution)/shard_map/ppermute | solution.py:25
  64.0 12.8 %collective-permute-start.12 = (f32[40,1280]{1,0:T(8,128)S(1)}, f32[40,1280]{1,0:T(8,128)S(1)}, u32[]{:S(2)}, u32[]{:S(2)}) collective-permute-start(f32[40,1280]{1,0:T(8,128)S(1)} %get-tuple-element.40.a), channel_id=1, source_target_pairs={{0,1},{1,0},{2,3},{3,2},{4,5},{5,4},{6,7},{7,6},{8,9},{9,8},{10,11... | collective-permute-start | bytes 614408 | tf_op jit(solution)/shard_map/ppermute | solution.py:25
  66.4 11.9 %collective-permute-start.13 = (f32[40,1280]{1,0:T(8,128)S(1)}, f32[40,1280]{1,0:T(8,128)S(1)}, u32[]{:S(2)}, u32[]{:S(2)}) collective-permute-start(f32[40,1280]{1,0:T(8,128)S(1)} %get-tuple-element.41), channel_id=1, source_target_pairs={{0,5},{1,4},{4,1},{5,0},{2,7},{3,6},{6,3},{7,2},{8,13},{9,12},{12,... | collective-permute-start | bytes 614408 | tf_op jit(solution)/shard_map/ppermute | solution.py:505
  70.2 23.2 %collective-permute-start.10 = (bf16[4,160,1280]{2,1,0:T(8,128)(2,1)}, bf16[4,160,1280]{2,1,0:T(8,128)(2,1)S(1)}, u32[]{:S(2)}, u32[]{:S(2)}) collective-permute-start(bf16[4,160,1280]{2,1,0:T(8,128)(2,1)} %get-tuple-element.37), channel_id=1, source_target_pairs={{0,34},{2,8},{10,40},{8,18},{16,50},{18,24},{26,56},{24,2},{34,64}... | collective-permute-start | bytes 4915208 | tf_op jit(solution)/shard_map/ppermute | solution.py:37
  72.3 24.9 %collective-permute-start.11 = (bf16[4,160,1280]{2,1,0:T(8,128)(2,1)}, bf16[4,160,1280]{2,1,0:T(8,128)(2,1)S(1)}, u32[]{:S(2)}, u32[]{:S(2)}) collective-permute-start(bf16[4,160,1280]{2,1,0:T(8,128)(2,1)} %get-tuple-element.38), channel_id=1, source_target_pairs={{0,98},{2,24},{10,104},{8,2},{16,114},{18,8},{26,120},{24,18},{34,... | collective-permute-start | bytes 4915208 | tf_op jit(solution)/shard_map/ppermute | solution.py:37
  82.4 22.4 %all-to-all-start = ((bf16[128,16,128]{2,1,0:T(8,128)(2,1)}), bf16[128,16,128]{2,1,0:T(8,128)(2,1)}, u32[]{:S(2)}, u32[]{:S(2)}) async-start(bf16[128,16,128]{2,1,0:T(8,128)(2,1)} %left_product.1.refs_3_), calls=%async_computation | async-start | bytes 1048576 | tf_op jit(solution)/shard_map/all_to_all | solution.py:508
  100.1 10.4 %collective-permute-start.15 = (bf16[160,1280]{1,0:T(8,128)(2,1)}, bf16[160,1280]{1,0:T(8,128)(2,1)S(1)}, u32[]{:S(2)}, u32[]{:S(2)}) collective-permute-start(bf16[160,1280]{1,0:T(8,128)(2,1)} %get-tuple-element.43.late), channel_id=1, source_target_pairs={{0,10},{2,32},{10,16},{8,42},{16,26},{18,48},{26,0},{24,58},{34,40... | collective-permute-start | bytes 1228808 | tf_op jit(solution)/shard_map/ppermute | solution.py:37
  102.6 7.9 %collective-permute-start.16 = (bf16[160,1280]{1,0:T(8,128)(2,1)}, bf16[160,1280]{1,0:T(8,128)(2,1)S(1)}, u32[]{:S(2)}, u32[]{:S(2)}) collective-permute-start(bf16[160,1280]{1,0:T(8,128)(2,1)} %get-tuple-element.44), channel_id=1, source_target_pairs={{0,26},{2,96},{10,0},{8,106},{16,10},{18,112},{26,16},{24,122},{34... | collective-permute-start | bytes 1228808 | tf_op jit(solution)/shard_map/ppermute | solution.py:37
  103.7 11.0 %collective-permute-start.17 = (bf16[160,1280]{1,0:T(8,128)(2,1)}, bf16[160,1280]{1,0:T(8,128)(2,1)S(1)}, u32[]{:S(2)}, u32[]{:S(2)}) collective-permute-start(bf16[160,1280]{1,0:T(8,128)(2,1)} %get-tuple-element.45), channel_id=1, source_target_pairs={{0,16},{2,66},{10,26},{8,72},{16,0},{18,82},{26,10},{24,88},{34,50... | collective-permute-start | bytes 1228808 | tf_op jit(solution)/shard_map/ppermute | solution.py:37
  116.2 6.7 %collective-permute-start.18 = (bf16[80,1280]{1,0:T(8,128)(2,1)S(1)}, bf16[80,1280]{1,0:T(8,128)(2,1)S(1)}, u32[]{:S(2)}, u32[]{:S(2)}) collective-permute-start(bf16[80,1280]{1,0:T(8,128)(2,1)S(1)} %get-tuple-element.47), channel_id=1, source_target_pairs={{0,4},{4,0},{1,5},{5,1},{2,6},{6,2},{3,7},{7,3},{8,12},{12,8},{9,1... | collective-permute-start | bytes 614408 | tf_op jit(solution)/shard_map/ppermute | solution.py:25
  123.0 2.0 %collective-permute-start.19 = (f32[40,1280]{1,0:T(8,128)S(1)}, f32[40,1280]{1,0:T(8,128)S(1)}, u32[]{:S(2)}, u32[]{:S(2)}) collective-permute-start(f32[40,1280]{1,0:T(8,128)S(1)} %dynamic-slice_bitcast_fusion), channel_id=1, source_target_pairs={{0,2},{2,0},{1,3},{3,1},{4,6},{6,4},{5,7},{7,5},{8,10},{10,8},{9,1... | collective-permute-start | bytes 614408 | tf_op jit(solution)/shard_map/ppermute | solution.py:25

commit v21 on v20

--- a/solution.py
+++ b/solution.py
@@ -210,15 +210,16 @@
     half = width // 2
     hbm = pl.BlockSpec(memory_space=pltpu.HBM)
     out = pltpu.HBM((4, width // 16, half), BF)
+    held = pltpu.VMEM((4, width // 16, half), BF)
     side = pltpu.HBM((2, width // 16, half), BF)
     return pl.pallas_call(
         factor_kernel,
-        out_shape=[out, out, side, side, out],
+        out_shape=[out, held, side, side, held],
         grid_spec=pltpu.PrefetchScalarGridSpec(
             num_scalar_prefetch=1,
             grid=(4,),
             in_specs=[hbm] * 2 + [ANY] * 3,
-            out_specs=[hbm] * 5,
+            out_specs=[hbm, VMEM, hbm, hbm, VMEM],
             scratch_shapes=[
                 pltpu.VMEM((2, 2, tokens, TILE), BF),
                 pltpu.VMEM((2, tokens, half), BF),
@@ -311,36 +312,23 @@
 
 
 def grow_kernel(right, left, from_left, from_right, *refs):
-    out_right, out_left, held, sems, out_sem = refs[-5:]
-    jobs = [(right, 0, from_left, 0, out_right), (left, 2, from_right, 0, out_left)]
-    jobs += [(right, 1, from_left, 1, out_right), (left, 3, from_right, 1, out_left)]
-    for n, (x, at, _, _, _) in enumerate(jobs):
-        pltpu.make_async_copy(x.at[at], held.at[n], sems.at[n]).start()
-    for n, (_, at, received, k, out) in enumerate(jobs):
-        wait_all(held.at[n], sems.at[n])
-        held[n] = add(held[n], received[k]).astype(BF)
-        pltpu.make_async_copy(held.at[n], out.at[at], out_sem).start()
-    wait_all(held, out_sem)
+    out_right, out_left = refs[-2:]
+    for k in range(2):
+        out_right[k] = add(right[k], from_left[k]).astype(BF)
+        out_left[2 + k] = add(left[2 + k], from_right[k]).astype(BF)
 
 
 def grow(right, left, from_left, from_right, *after):
-    hbm = pl.BlockSpec(memory_space=pltpu.HBM)
     return pl.pallas_call(
         grow_kernel,
-        out_shape=[pltpu.HBM(x.shape, x.dtype) for x in (right, left)],
-        grid=(1,),
-        in_specs=[hbm, hbm, VMEM, VMEM] + [ANY] * len(after),
-        out_specs=[hbm, hbm],
-        scratch_shapes=[
-            pltpu.VMEM(right.shape, right.dtype),
-            pltpu.SemaphoreType.DMA((4,)),
-            pltpu.SemaphoreType.DMA,
-        ],
+        out_shape=[pltpu.VMEM(x.shape, x.dtype) for x in (right, left)],
+        in_specs=[VMEM] * 4 + [ANY] * len(after),
+        out_specs=[VMEM, VMEM],
         input_output_aliases={0: 0, 1: 1},
         compiler_params=pltpu.CompilerParams(vmem_limit_bytes=8 * 2**20),
         cost_estimate=pl.CostEstimate(flops=0, bytes_accessed=0, transcendentals=0),
         name="grow",
-    )(in_hbm(right), in_hbm(left), from_left, from_right, *after)
+    )(right, left, from_left, from_right, *after)
 
 
 def fetch_tiles(step, source, held, sems):

time: 126 us -> 128 us (1.016); the launches traced: 126 us -> 126 us
  waiting for transfers between devices: 34.9 us -> 29.6 us
  Pallas kernels: 53.4 us -> 57.1 us
  starting transfers between devices: 35.8 us -> 38 us
    ppermute x13, waiting for transfers between devices: 18.9 us -> 14.7 us  [turn(): return lax.ppermute(x, ('z', 'y', 'c'), pairs)]
    pallas_call x2, Pallas kernels: 5.02 us -> 8.38 us  [fold(): pl.pallas_call(functools.partial(fold_kernel, len(parts)), out_shape=[plt...]
    ppermute x13, starting transfers between devices: 21.8 us -> 24.2 us  [turn(): return lax.ppermute(x, ('z', 'y', 'c'), pairs)]
  transfers between devices with their start and end apart: 21 -> 21, of which waited for: 9 -> 12; matrix products, arithmetic and copies ran while one was open for 0% -> 0% of each run, Pallas kernels for 35% -> 37%
where the time goes in v21:
time: 128 us; the launch traced here: 126 us
  Pallas kernels  57.1 us (45%)
  starting transfers between devices  38 us (30%)
  waiting for transfers between devices  29.6 us (23%)
    ppermute x13, starting transfers between devices, turn(): return lax.ppermute(x, ('z', 'y', 'c'), pairs)  24.2 us
    pallas_call x1, Pallas kernels, factor_term(): pl.pallas_call(factor_kernel, out_shape=[out, held, side, side, held], gr...  17 us
    ppermute x13, waiting for transfers between devices, turn(): return lax.ppermute(x, ('z', 'y', 'c'), pairs)  14.7 us
    ppermute x6, waiting for transfers between devices, shift(): return lax.ppermute(x, axis, [(i, (i + step) % size) for i in range(size)])  13.6 us
    pallas_call x2, Pallas kernels, fold(): pl.pallas_call(functools.partial(fold_kernel, len(parts)), out_shape=[plt...  8.38 us
    pallas_call x1, Pallas kernels, cross_term(): pl.pallas_call(cross_kernel, out_shape=[out] * 4, grid_spec=pltpu.Prefetc...  8.31 us
    all_to_all x1, starting transfers between devices, per_device(): lax.all_to_all(products, ('o', 'c', 'z', 'y', 'xl'), 0, 0, tiled=True)  8.01 us
    pallas_call x2, Pallas kernels, left_product(): pl.pallas_call(functools.partial(left_kernel, own), out_shape=total if ow...  6.92 us
  transfers between devices with their start and end apart: 21, of which 12 were waited for; matrix products, arithmetic and copies ran while one was open for 0% of the time, Pallas kernels for 37%

profile of v21, /device:TPU:1, one launch (start us, length us, event | category | flops | bytes accessed | tf_op | source)
XLA Modules:
  0.0 126.4 jit_solution(4609751241141661201)
XLA Ops:
  0.6 1.5 %collective-permute-start = (bf16[768,2560]{1,0:T(8,128)(2,1)}, bf16[768,2560]{1,0:T(8,128)(2,1)}, u32[]{:S(2)}, u32[]{:S(2)}) collective-permute-start(bf16[768,2560]{1,0:T(8,128)(2,1)} %h_own.1), channel_id=1, source_target_pairs={{0,2},{2,0},{1,3},{3,1},{4,6},{6,4},{5,7},{7,5},{8,10},{10,8},{9,1... | collective-permute-start | bytes 11796488 | tf_op jit(solution)/shard_map/ppermute | solution.py:25
  2.1 0.1 collective-permute-start.1
  2.2 0.1 pad_add_fusion.place
  2.3 5.4 %cross_own.1.partial = f32[1280,1280]{1,0:T(8,128)S(1)} custom-call(s32[4]{0:T(128)S(1)} %pad_add_fusion.place, bf16[768,2560]{1,0:T(8,128)(2,1)} %g_own.1, bf16[768,2560]{1,0:T(8,128)(2,1)} %h_own.1), custom_call_target="tpu_custom_call" | custom-call | flops 2516582400 | bytes 7864320 | tf_op jit(solution)/shard_map/cross_own/pallas_call | solution.py:125
  7.7 1.1 collective-permute-done.b.h_next
  8.9 5.6 %collective-permute-done.1.a.g_next = bf16[768,2560]{1,0:T(8,128)(2,1)} collective-permute-done((bf16[768,2560]{1,0:T(8,128)(2,1)}, bf16[768,2560]{1,0:T(8,128)(2,1)}, u32[]{:S(2)}, u32[]{:S(2)}) %collective-permute-start.1) | collective-permute-done | bytes 3932192 | tf_op jit(solution)/shard_map/ppermute | solution.py:25
  14.5 8.3 %cross_term.1 = (bf16[4,80,1280]{2,1,0:T(8,128)(2,1)}, bf16[4,80,1280]{2,1,0:T(8,128)(2,1)}, bf16[4,80,1280]{2,1,0:T(8,128)(2,1)}, bf16[4,80,1280]{2,1,0:T(8,128)(2,1)}) custom-call(s32[4]{0:T(128)S(1)} %pad_add_fusion.place, bf16[768,2560]{1,0:T(8,128)(2,1)} %collective-permute-done.1.a.g_next, bf16[768,2560]{1,0:T(8,128)(2,1)} %collective-permute-done.b.h_next, ...), custom_call_target="tpu_custom_call" | custom-call | flops 2516582400 | bytes 9830400 | tf_op jit(solution)/shard_map/cross_term/pallas_call | solution.py:151
  22.8 1.7 %collective-permute-start.4 = (bf16[4,80,1280]{2,1,0:T(8,128)(2,1)}, bf16[4,80,1280]{2,1,0:T(8,128)(2,1)}, u32[]{:S(2)}, u32[]{:S(2)}) collective-permute-start(bf16[4,80,1280]{2,1,0:T(8,128)(2,1)} %get-tuple-element.25.after), channel_id=1, source_target_pairs={{0,34},{2,8},{10,40},{8,18},{16,50},{18,24},{26,56},{24,2},{34,64}... | collective-permute-start | bytes 2457608 | tf_op jit(solution)/shard_map/ppermute | solution.py:37
  24.5 1.5 %collective-permute-start.5 = (bf16[4,80,1280]{2,1,0:T(8,128)(2,1)}, bf16[4,80,1280]{2,1,0:T(8,128)(2,1)}, u32[]{:S(2)}, u32[]{:S(2)}) collective-permute-start(bf16[4,80,1280]{2,1,0:T(8,128)(2,1)} %get-tuple-element.32), channel_id=1, source_target_pairs={{0,98},{2,24},{10,104},{8,2},{16,114},{18,8},{26,120},{24,18},{34,... | collective-permute-start | bytes 2457608 | tf_op jit(solution)/shard_map/ppermute | solution.py:37
  26.1 1.6 %collective-permute-start.6 = (bf16[4,80,1280]{2,1,0:T(8,128)(2,1)}, bf16[4,80,1280]{2,1,0:T(8,128)(2,1)}, u32[]{:S(2)}, u32[]{:S(2)}) collective-permute-start(bf16[4,80,1280]{2,1,0:T(8,128)(2,1)} %get-tuple-element.33), channel_id=1, source_target_pairs={{0,64},{2,18},{10,74},{8,24},{16,80},{18,2},{26,90},{24,8},{34,98}... | collective-permute-start | bytes 2457608 | tf_op jit(solution)/shard_map/ppermute | solution.py:37
  27.6 17.0 %factor_term.1 = (bf16[4,160,1280]{2,1,0:T(8,128)(2,1)}, bf16[4,160,1280]{2,1,0:T(8,128)(2,1)S(1)}, bf16[2,160,1280]{2,1,0:T(8,128)(2,1)}, bf16[2,160,1280]{2,1,0:T(8,128)(2,1)}, bf16[4,160,1280]{2,1,0:T(8,128)(2,1)S(1)}) custom-call(s32[4]{0:T(128)S(1)} %pad_add_fusion.place, bf16[768,2560]{1,0:T(8,128)(2,1)} %h_own.1, bf16[768,2560]{1,0:T(8,128)(2,1)} %g_own.1, ...), custom_call_target="tpu_custom_call" | custom-call | flops 10066329600 | bytes 15728640 | tf_op jit(solution)/shard_map/factor_term/pallas_call | solution.py:215
  44.6 1.0 collective-permute-start.2
  45.6 2.0 %collective-permute-start.3 = (bf16[2,160,1280]{2,1,0:T(8,128)(2,1)}, bf16[2,160,1280]{2,1,0:T(8,128)(2,1)}, u32[]{:S(2)}, u32[]{:S(2)}) collective-permute-start(bf16[2,160,1280]{2,1,0:T(8,128)(2,1)} %get-tuple-element.30), channel_id=1, source_target_pairs={{0,98},{2,24},{10,104},{8,2},{16,114},{18,8},{26,120},{24,18},{34,... | collective-permute-start | bytes 2457608 | tf_op jit(solution)/shard_map/ppermute | solution.py:37
  47.6 0.0 collective-permute-done.5.refs_2_
  47.6 3.9 %fold.2 = (f32[80,1280]{1,0:T(8,128)}, bf16[80,1280]{1,0:T(8,128)(2,1)}, bf16[80,1280]{1,0:T(8,128)(2,1)}, bf16[80,1280]{1,0:T(8,128)(2,1)}) custom-call(s32[1]{0:T(128)} %bitcast.1.me, bf16[4,80,1280]{2,1,0:T(8,128)(2,1)} %get-tuple-element.31.refs_0_, bf16[4,80,1280]{2,1,0:T(8,128)(2,1)} %collective-permute-done.4.refs_1_, ...), custom_call_target="tpu_custom_call" | custom-call | tf_op jit(solution)/shard_map/fold/pallas_call | solution.py:262
  51.6 2.2 %collective-permute-start.7 = (bf16[80,1280]{1,0:T(8,128)(2,1)}, bf16[80,1280]{1,0:T(8,128)(2,1)S(1)}, u32[]{:S(2)}, u32[]{:S(2)}) collective-permute-start(bf16[80,1280]{1,0:T(8,128)(2,1)} %get-tuple-element.34), channel_id=1, source_target_pairs={{0,10},{2,32},{10,16},{8,42},{16,26},{18,48},{26,0},{24,58},{34,40... | collective-permute-start | bytes 614408 | tf_op jit(solution)/shard_map/ppermute | solution.py:37
  53.8 2.2 %collective-permute-start.8 = (bf16[80,1280]{1,0:T(8,128)(2,1)}, bf16[80,1280]{1,0:T(8,128)(2,1)}, u32[]{:S(2)}, u32[]{:S(2)}) collective-permute-start(bf16[80,1280]{1,0:T(8,128)(2,1)} %get-tuple-element.35), channel_id=1, source_target_pairs={{0,26},{2,96},{10,0},{8,106},{16,10},{18,112},{26,16},{24,122},{34... | collective-permute-start | bytes 614408 | tf_op jit(solution)/shard_map/ppermute | solution.py:37
  56.0 1.1 collective-permute-start.9
  57.1 3.8 %collective-permute-done.7.refs_0_.refs_1_ = bf16[80,1280]{1,0:T(8,128)(2,1)S(1)} collective-permute-done((bf16[80,1280]{1,0:T(8,128)(2,1)}, bf16[80,1280]{1,0:T(8,128)(2,1)S(1)}, u32[]{:S(2)}, u32[]{:S(2)}) %collective-permute-start.7) | collective-permute-done | bytes 204832 | tf_op jit(solution)/shard_map/ppermute | solution.py:37
  60.9 2.1 %collective-permute-done.8.refs_1_.refs_2_ = bf16[80,1280]{1,0:T(8,128)(2,1)} collective-permute-done((bf16[80,1280]{1,0:T(8,128)(2,1)}, bf16[80,1280]{1,0:T(8,128)(2,1)}, u32[]{:S(2)}, u32[]{:S(2)}) %collective-permute-start.8) | collective-permute-done | bytes 204832 | tf_op jit(solution)/shard_map/ppermute | solution.py:37
  62.9 0.2 collective-permute-done.9.refs_2_.refs_3_
  63.1 1.3 %settle.2 = (f32[40,1280]{1,0:T(8,128)S(1)}, f32[40,1280]{1,0:T(8,128)S(1)}) custom-call(s32[1]{0:T(128)} %bitcast.xl, f32[80,1280]{1,0:T(8,128)} %get-tuple-element.39.refs_0_, bf16[80,1280]{1,0:T(8,128)(2,1)S(1)} %collective-permute-done.7.refs_0_.refs_1_, bf16[80,1280]{1,0:T(8,128)(2,1)} %collective-permute-done.8.refs_1_.refs_2_, ...), custom_call_target="tpu_custom_call" | custom-call | tf_op jit(solution)/shard_map/settle/pallas_call | solution.py:296
  64.4 1.3 %collective-permute-start.14 = (f32[40,1280]{1,0:T(8,128)S(1)}, f32[40,1280]{1,0:T(8,128)S(1)}, u32[]{:S(2)}, u32[]{:S(2)}) collective-permute-start(f32[40,1280]{1,0:T(8,128)S(1)} %get-tuple-element.41), channel_id=1, source_target_pairs={{0,4},{4,0},{1,5},{5,1},{2,6},{6,2},{3,7},{7,3},{8,12},{12,8},{9,1... | collective-permute-start | bytes 614408 | tf_op jit(solution)/shard_map/ppermute | solution.py:25
  65.7 2.2 %collective-permute-start.12 = (f32[40,1280]{1,0:T(8,128)S(1)}, f32[40,1280]{1,0:T(8,128)S(1)}, u32[]{:S(2)}, u32[]{:S(2)}) collective-permute-start(f32[40,1280]{1,0:T(8,128)S(1)} %get-tuple-element.40.a), channel_id=1, source_target_pairs={{0,1},{1,0},{2,3},{3,2},{4,5},{5,4},{6,7},{7,6},{8,9},{9,8},{10,11... | collective-permute-start | bytes 614408 | tf_op jit(solution)/shard_map/ppermute | solution.py:25
  68.0 0.4 collective-permute-start.13
  68.4 2.6 %grow.1 = (bf16[4,160,1280]{2,1,0:T(8,128)(2,1)S(1)}, bf16[4,160,1280]{2,1,0:T(8,128)(2,1)S(1)}) custom-call(bf16[4,160,1280]{2,1,0:T(8,128)(2,1)S(1)} %get-tuple-element.27.right, bf16[4,160,1280]{2,1,0:T(8,128)(2,1)S(1)} %get-tuple-element.28.left, ...), custom_call_target="tpu_custom_call", output_to_operand_aliasing={{0}: (0, {}), {1}: (1, {})} | custom-call | tf_op jit(solution)/shard_map/grow/pallas_call | solution.py:322
  71.0 2.6 %collective-permute-start.10 = (bf16[4,160,1280]{2,1,0:T(8,128)(2,1)S(1)}, bf16[4,160,1280]{2,1,0:T(8,128)(2,1)}, u32[]{:S(2)}, u32[]{:S(2)}) collective-permute-start(bf16[4,160,1280]{2,1,0:T(8,128)(2,1)S(1)} %get-tuple-element.37), channel_id=1, source_target_pairs={{0,34},{2,8},{10,40},{8,18},{16,50},{18,24},{26,56},{24,2},{34,64}... | collective-permute-start | bytes 4915208 | tf_op jit(solution)/shard_map/ppermute | solution.py:37
  73.6 1.7 %collective-permute-start.11 = (bf16[4,160,1280]{2,1,0:T(8,128)(2,1)S(1)}, bf16[4,160,1280]{2,1,0:T(8,128)(2,1)}, u32[]{:S(2)}, u32[]{:S(2)}) collective-permute-start(bf16[4,160,1280]{2,1,0:T(8,128)(2,1)S(1)} %get-tuple-element.38), channel_id=1, source_target_pairs={{0,98},{2,24},{10,104},{8,2},{16,114},{18,8},{26,120},{24,18},{34,... | collective-permute-start | bytes 4915208 | tf_op jit(solution)/shard_map/ppermute | solution.py:37
  75.3 2.9 %left_own.1.rest_0_ = f32[80,1280]{1,0:T(8,128)S(1)} custom-call(s32[4]{0:T(128)S(1)} %pad_add_fusion.place, f32[40,1280]{1,0:T(8,128)S(1)} %get-tuple-element.40.a, f32[40,1280]{1,0:T(8,128)S(1)} %collective-permute-done.14.b, bf16[2560,1280]{1,0:T(8,128)(2,1)} %left.3), custom_call_target="tpu_custom_call" | custom-call | tf_op jit(solution)/shard_map/left_own/pallas_call | solution.py:391
  78.3 1.3 %collective-permute-done.13.b = f32[40,1280]{1,0:T(8,128)S(1)} collective-permute-done((f32[40,1280]{1,0:T(8,128)S(1)}, f32[40,1280]{1,0:T(8,128)S(1)}, u32[]{:S(2)}, u32[]{:S(2)}) %collective-permute-start.13) | collective-permute-done | bytes 204832 | tf_op jit(solution)/shard_map/ppermute | solution.py:493
  79.6 4.0 %left_product.1.refs_3_ = bf16[128,16,128]{2,1,0:T(8,128)(2,1)} custom-call(s32[4]{0:T(128)S(1)} %pad_add_fusion.place, f32[40,1280]{1,0:T(8,128)S(1)} %collective-permute-done.12.a, f32[40,1280]{1,0:T(8,128)S(1)} %collective-permute-done.13.b, bf16[2560,1280]{1,0:T(8,128)(2,1)} %left.3, f32[80,1280]{1,0:T(8,128)S(1)} %left_own.1.rest_0_), custom_call_target="tpu_custom_call" | custom-call | flops 16777216000 | tf_op jit(solution)/shard_map/left_product/pallas_call | solution.py:391
  83.6 8.0 %all-to-all-start = ((bf16[128,16,128]{2,1,0:T(8,128)(2,1)}), bf16[128,16,128]{2,1,0:T(8,128)(2,1)}, u32[]{:S(2)}, u32[]{:S(2)}) async-start(bf16[128,16,128]{2,1,0:T(8,128)(2,1)} %left_product.1.refs_3_), calls=%async_computation | async-start | bytes 1048576 | tf_op jit(solution)/shard_map/all_to_all | solution.py:496
  91.6 2.5 %collective-permute-done.10.refs_1_ = bf16[4,160,1280]{2,1,0:T(8,128)(2,1)} collective-permute-done((bf16[4,160,1280]{2,1,0:T(8,128)(2,1)S(1)}, bf16[4,160,1280]{2,1,0:T(8,128)(2,1)}, u32[]{:S(2)}, u32[]{:S(2)}) %collective-permute-start.10) | collective-permute-done | bytes 1638432 | tf_op jit(solution)/shard_map/ppermute | solution.py:37
  94.1 2.1 %collective-permute-done.11.refs_2_ = bf16[4,160,1280]{2,1,0:T(8,128)(2,1)} collective-permute-done((bf16[4,160,1280]{2,1,0:T(8,128)(2,1)S(1)}, bf16[4,160,1280]{2,1,0:T(8,128)(2,1)}, u32[]{:S(2)}, u32[]{:S(2)}) %collective-permute-start.11) | collective-permute-done | bytes 1638432 | tf_op jit(solution)/shard_map/ppermute | solution.py:37
  96.2 4.5 %fold.3 = (f32[160,1280]{1,0:T(8,128)}, bf16[160,1280]{1,0:T(8,128)(2,1)S(1)}, bf16[160,1280]{1,0:T(8,128)(2,1)S(1)}, bf16[160,1280]{1,0:T(8,128)(2,1)S(1)}) custom-call(s32[1]{0:T(128)} %bitcast.1.me, bf16[4,160,1280]{2,1,0:T(8,128)(2,1)} %get-tuple-element.26.refs_4_.refs_0_, bf16[4,160,1280]{2,1,0:T(8,128)(2,1)} %collective-permute-done.10.refs_1_, ...), custom_call_target="tpu_custom_call" | custom-call | tf_op jit(solution)/shard_map/fold/pallas_call | solution.py:262
  100.7 2.9 %collective-permute-start.15 = (bf16[160,1280]{1,0:T(8,128)(2,1)S(1)}, bf16[160,1280]{1,0:T(8,128)(2,1)S(1)}, u32[]{:S(2)}, u32[]{:S(2)}) collective-permute-start(bf16[160,1280]{1,0:T(8,128)(2,1)S(1)} %get-tuple-element.43.late), channel_id=1, source_target_pairs={{0,10},{2,32},{10,16},{8,42},{16,26},{18,48},{26,0},{24,58},{34,40... | collective-permute-start | bytes 1228808 | tf_op jit(solution)/shard_map/ppermute | solution.py:37
  103.6 2.5 %collective-permute-start.16 = (bf16[160,1280]{1,0:T(8,128)(2,1)S(1)}, bf16[160,1280]{1,0:T(8,128)(2,1)S(1)}, u32[]{:S(2)}, u32[]{:S(2)}) collective-permute-start(bf16[160,1280]{1,0:T(8,128)(2,1)S(1)} %get-tuple-element.44), channel_id=1, source_target_pairs={{0,26},{2,96},{10,0},{8,106},{16,10},{18,112},{26,16},{24,122},{34... | collective-permute-start | bytes 1228808 | tf_op jit(solution)/shard_map/ppermute | solution.py:37
  106.1 1.1 collective-permute-start.17
  107.2 5.7 %right_product.1.refs_4_ = f32[40,1280]{1,0:T(8,128)} custom-call(s32[4]{0:T(128)S(1)} %pad_add_fusion.place, bf16[128,16,128]{2,1,0:T(8,128)(2,1)} %all-to-all-done.blocks, bf16[2560,1280]{1,0:T(8,128)(2,1)} %right.1, bf16[160,1280]{1,0:T(8,128)(2,1)S(1)} %get-tuple-element.43.late), custom_call_target="tpu_custom_call" | custom-call | flops 41943040000 | bytes 6553600 | tf_op jit(solution)/shard_map/right_product/pallas_call | solution.py:433
  112.9 2.5 %collective-permute-done.16.refs_2_ = bf16[160,1280]{1,0:T(8,128)(2,1)S(1)} collective-permute-done((bf16[160,1280]{1,0:T(8,128)(2,1)S(1)}, bf16[160,1280]{1,0:T(8,128)(2,1)S(1)}, u32[]{:S(2)}, u32[]{:S(2)}) %collective-permute-start.16) | collective-permute-done | bytes 409632 | tf_op jit(solution)/shard_map/ppermute | solution.py:37
  115.4 1.5 %collective-permute-done.17.refs_3_ = bf16[160,1280]{1,0:T(8,128)(2,1)S(1)} collective-permute-done((bf16[160,1280]{1,0:T(8,128)(2,1)S(1)}, bf16[160,1280]{1,0:T(8,128)(2,1)S(1)}, u32[]{:S(2)}, u32[]{:S(2)}) %collective-permute-start.17) | collective-permute-done | bytes 409632 | tf_op jit(solution)/shard_map/ppermute | solution.py:37
  116.9 1.5 %settle.3 = (f32[80,1280]{1,0:T(8,128)S(1)}, bf16[80,1280]{1,0:T(8,128)(2,1)S(1)}) custom-call(s32[1]{0:T(128)} %bitcast.xl, f32[160,1280]{1,0:T(8,128)} %get-tuple-element.42.refs_0_, bf16[160,1280]{1,0:T(8,128)(2,1)S(1)} %collective-permute-done.15.refs_1_, bf16[160,1280]{1,0:T(8,128)(2,1)S(1)} %collective-permute-done.16.refs_2_, ...), custom_call_target="tpu_custom_call" | custom-call | tf_op jit(solution)/shard_map/settle/pallas_call | solution.py:296
  118.4 0.1 collective-permute-start.18
  118.6 5.4 %collective-permute-done.18 = bf16[80,1280]{1,0:T(8,128)(2,1)S(1)} collective-permute-done((bf16[80,1280]{1,0:T(8,128)(2,1)S(1)}, bf16[80,1280]{1,0:T(8,128)(2,1)S(1)}, u32[]{:S(2)}, u32[]{:S(2)}) %collective-permute-start.18) | collective-permute-done | bytes 204832 | tf_op jit(solution)/shard_map/ppermute | solution.py:25
  124.0 0.1 add_multiply_fusion
  124.0 0.1 collective-permute-start.19
  124.1 1.4 %collective-permute-done.19 = f32[40,1280]{1,0:T(8,128)S(1)} collective-permute-done((f32[40,1280]{1,0:T(8,128)S(1)}, f32[40,1280]{1,0:T(8,128)S(1)}, u32[]{:S(2)}, u32[]{:S(2)}) %collective-permute-start.19) | collective-permute-done | bytes 204832 | tf_op jit(solution)/shard_map/ppermute | solution.py:25
  125.6 0.8 maximum_bitcast_fusion
  (10 shorter events, 0.1 us)
Async XLA Ops:
  0.6 8.3 %collective-permute-start = (bf16[768,2560]{1,0:T(8,128)(2,1)}, bf16[768,2560]{1,0:T(8,128)(2,1)}, u32[]{:S(2)}, u32[]{:S(2)}) collective-permute-start(bf16[768,2560]{1,0:T(8,128)(2,1)} %h_own.1), channel_id=1, source_target_pairs={{0,2},{2,0},{1,3},{3,1},{4,6},{6,4},{5,7},{7,5},{8,10},{10,8},{9,1... | collective-permute-start | bytes 11796488 | tf_op jit(solution)/shard_map/ppermute | solution.py:25
  2.1 12.4 %collective-permute-start.1 = (bf16[768,2560]{1,0:T(8,128)(2,1)}, bf16[768,2560]{1,0:T(8,128)(2,1)}, u32[]{:S(2)}, u32[]{:S(2)}) collective-permute-start(bf16[768,2560]{1,0:T(8,128)(2,1)} %g_own.1), channel_id=1, source_target_pairs={{0,2},{2,0},{1,3},{3,1},{4,6},{6,4},{5,7},{7,5},{8,10},{10,8},{9,1... | collective-permute-start | bytes 11796488 | tf_op jit(solution)/shard_map/ppermute | solution.py:25
  22.8 24.8 %collective-permute-start.4 = (bf16[4,80,1280]{2,1,0:T(8,128)(2,1)}, bf16[4,80,1280]{2,1,0:T(8,128)(2,1)}, u32[]{:S(2)}, u32[]{:S(2)}) collective-permute-start(bf16[4,80,1280]{2,1,0:T(8,128)(2,1)} %get-tuple-element.25.after), channel_id=1, source_target_pairs={{0,34},{2,8},{10,40},{8,18},{16,50},{18,24},{26,56},{24,2},{34,64}... | collective-permute-start | bytes 2457608 | tf_op jit(solution)/shard_map/ppermute | solution.py:37
  24.5 23.1 %collective-permute-start.5 = (bf16[4,80,1280]{2,1,0:T(8,128)(2,1)}, bf16[4,80,1280]{2,1,0:T(8,128)(2,1)}, u32[]{:S(2)}, u32[]{:S(2)}) collective-permute-start(bf16[4,80,1280]{2,1,0:T(8,128)(2,1)} %get-tuple-element.32), channel_id=1, source_target_pairs={{0,98},{2,24},{10,104},{8,2},{16,114},{18,8},{26,120},{24,18},{34,... | collective-permute-start | bytes 2457608 | tf_op jit(solution)/shard_map/ppermute | solution.py:37
  26.1 21.6 %collective-permute-start.6 = (bf16[4,80,1280]{2,1,0:T(8,128)(2,1)}, bf16[4,80,1280]{2,1,0:T(8,128)(2,1)}, u32[]{:S(2)}, u32[]{:S(2)}) collective-permute-start(bf16[4,80,1280]{2,1,0:T(8,128)(2,1)} %get-tuple-element.33), channel_id=1, source_target_pairs={{0,64},{2,18},{10,74},{8,24},{16,80},{18,2},{26,90},{24,8},{34,98}... | collective-permute-start | bytes 2457608 | tf_op jit(solution)/shard_map/ppermute | solution.py:37
  44.6 23.8 %collective-permute-start.2 = (bf16[2,160,1280]{2,1,0:T(8,128)(2,1)}, bf16[2,160,1280]{2,1,0:T(8,128)(2,1)}, u32[]{:S(2)}, u32[]{:S(2)}) collective-permute-start(bf16[2,160,1280]{2,1,0:T(8,128)(2,1)} %get-tuple-element.29), channel_id=1, source_target_pairs={{0,34},{2,8},{10,40},{8,18},{16,50},{18,24},{26,56},{24,2},{34,64}... | collective-permute-start | bytes 2457608 | tf_op jit(solution)/shard_map/ppermute | solution.py:37
  45.6 22.8 %collective-permute-start.3 = (bf16[2,160,1280]{2,1,0:T(8,128)(2,1)}, bf16[2,160,1280]{2,1,0:T(8,128)(2,1)}, u32[]{:S(2)}, u32[]{:S(2)}) collective-permute-start(bf16[2,160,1280]{2,1,0:T(8,128)(2,1)} %get-tuple-element.30), channel_id=1, source_target_pairs={{0,98},{2,24},{10,104},{8,2},{16,114},{18,8},{26,120},{24,18},{34,... | collective-permute-start | bytes 2457608 | tf_op jit(solution)/shard_map/ppermute | solution.py:37
  51.6 9.3 %collective-permute-start.7 = (bf16[80,1280]{1,0:T(8,128)(2,1)}, bf16[80,1280]{1,0:T(8,128)(2,1)S(1)}, u32[]{:S(2)}, u32[]{:S(2)}) collective-permute-start(bf16[80,1280]{1,0:T(8,128)(2,1)} %get-tuple-element.34), channel_id=1, source_target_pairs={{0,10},{2,32},{10,16},{8,42},{16,26},{18,48},{26,0},{24,58},{34,40... | collective-permute-start | bytes 614408 | tf_op jit(solution)/shard_map/ppermute | solution.py:37
  53.8 9.2 %collective-permute-start.8 = (bf16[80,1280]{1,0:T(8,128)(2,1)}, bf16[80,1280]{1,0:T(8,128)(2,1)}, u32[]{:S(2)}, u32[]{:S(2)}) collective-permute-start(bf16[80,1280]{1,0:T(8,128)(2,1)} %get-tuple-element.35), channel_id=1, source_target_pairs={{0,26},{2,96},{10,0},{8,106},{16,10},{18,112},{26,16},{24,122},{34... | collective-permute-start | bytes 614408 | tf_op jit(solution)/shard_map/ppermute | solution.py:37
  56.0 7.2 %collective-permute-start.9 = (bf16[80,1280]{1,0:T(8,128)(2,1)}, bf16[80,1280]{1,0:T(8,128)(2,1)}, u32[]{:S(2)}, u32[]{:S(2)}) collective-permute-start(bf16[80,1280]{1,0:T(8,128)(2,1)} %get-tuple-element.36), channel_id=1, source_target_pairs={{0,16},{2,66},{10,26},{8,72},{16,0},{18,82},{26,10},{24,88},{34,50... | collective-permute-start | bytes 614408 | tf_op jit(solution)/shard_map/ppermute | solution.py:37
  64.4 10.9 %collective-permute-start.14 = (f32[40,1280]{1,0:T(8,128)S(1)}, f32[40,1280]{1,0:T(8,128)S(1)}, u32[]{:S(2)}, u32[]{:S(2)}) collective-permute-start(f32[40,1280]{1,0:T(8,128)S(1)} %get-tuple-element.41), channel_id=1, source_target_pairs={{0,4},{4,0},{1,5},{5,1},{2,6},{6,2},{3,7},{7,3},{8,12},{12,8},{9,1... | collective-permute-start | bytes 614408 | tf_op jit(solution)/shard_map/ppermute | solution.py:25
  65.7 12.5 %collective-permute-start.12 = (f32[40,1280]{1,0:T(8,128)S(1)}, f32[40,1280]{1,0:T(8,128)S(1)}, u32[]{:S(2)}, u32[]{:S(2)}) collective-permute-start(f32[40,1280]{1,0:T(8,128)S(1)} %get-tuple-element.40.a), channel_id=1, source_target_pairs={{0,1},{1,0},{2,3},{3,2},{4,5},{5,4},{6,7},{7,6},{8,9},{9,8},{10,11... | collective-permute-start | bytes 614408 | tf_op jit(solution)/shard_map/ppermute | solution.py:25
  68.0 11.6 %collective-permute-start.13 = (f32[40,1280]{1,0:T(8,128)S(1)}, f32[40,1280]{1,0:T(8,128)S(1)}, u32[]{:S(2)}, u32[]{:S(2)}) collective-permute-start(f32[40,1280]{1,0:T(8,128)S(1)} %get-tuple-element.41), channel_id=1, source_target_pairs={{0,5},{1,4},{4,1},{5,0},{2,7},{3,6},{6,3},{7,2},{8,13},{9,12},{12,... | collective-permute-start | bytes 614408 | tf_op jit(solution)/shard_map/ppermute | solution.py:493
  71.0 23.1 %collective-permute-start.10 = (bf16[4,160,1280]{2,1,0:T(8,128)(2,1)S(1)}, bf16[4,160,1280]{2,1,0:T(8,128)(2,1)}, u32[]{:S(2)}, u32[]{:S(2)}) collective-permute-start(bf16[4,160,1280]{2,1,0:T(8,128)(2,1)S(1)} %get-tuple-element.37), channel_id=1, source_target_pairs={{0,34},{2,8},{10,40},{8,18},{16,50},{18,24},{26,56},{24,2},{34,64}... | collective-permute-start | bytes 4915208 | tf_op jit(solution)/shard_map/ppermute | solution.py:37
  73.6 22.6 %collective-permute-start.11 = (bf16[4,160,1280]{2,1,0:T(8,128)(2,1)S(1)}, bf16[4,160,1280]{2,1,0:T(8,128)(2,1)}, u32[]{:S(2)}, u32[]{:S(2)}) collective-permute-start(bf16[4,160,1280]{2,1,0:T(8,128)(2,1)S(1)} %get-tuple-element.38), channel_id=1, source_target_pairs={{0,98},{2,24},{10,104},{8,2},{16,114},{18,8},{26,120},{24,18},{34,... | collective-permute-start | bytes 4915208 | tf_op jit(solution)/shard_map/ppermute | solution.py:37
  83.6 23.7 %all-to-all-start = ((bf16[128,16,128]{2,1,0:T(8,128)(2,1)}), bf16[128,16,128]{2,1,0:T(8,128)(2,1)}, u32[]{:S(2)}, u32[]{:S(2)}) async-start(bf16[128,16,128]{2,1,0:T(8,128)(2,1)} %left_product.1.refs_3_), calls=%async_computation | async-start | bytes 1048576 | tf_op jit(solution)/shard_map/all_to_all | solution.py:496
  100.7 12.2 %collective-permute-start.15 = (bf16[160,1280]{1,0:T(8,128)(2,1)S(1)}, bf16[160,1280]{1,0:T(8,128)(2,1)S(1)}, u32[]{:S(2)}, u32[]{:S(2)}) collective-permute-start(bf16[160,1280]{1,0:T(8,128)(2,1)S(1)} %get-tuple-element.43.late), channel_id=1, source_target_pairs={{0,10},{2,32},{10,16},{8,42},{16,26},{18,48},{26,0},{24,58},{34,40... | collective-permute-start | bytes 1228808 | tf_op jit(solution)/shard_map/ppermute | solution.py:37
  103.6 11.8 %collective-permute-start.16 = (bf16[160,1280]{1,0:T(8,128)(2,1)S(1)}, bf16[160,1280]{1,0:T(8,128)(2,1)S(1)}, u32[]{:S(2)}, u32[]{:S(2)}) collective-permute-start(bf16[160,1280]{1,0:T(8,128)(2,1)S(1)} %get-tuple-element.44), channel_id=1, source_target_pairs={{0,26},{2,96},{10,0},{8,106},{16,10},{18,112},{26,16},{24,122},{34... | collective-permute-start | bytes 1228808 | tf_op jit(solution)/shard_map/ppermute | solution.py:37
  106.1 10.8 %collective-permute-start.17 = (bf16[160,1280]{1,0:T(8,128)(2,1)S(1)}, bf16[160,1280]{1,0:T(8,128)(2,1)S(1)}, u32[]{:S(2)}, u32[]{:S(2)}) collective-permute-start(bf16[160,1280]{1,0:T(8,128)(2,1)S(1)} %get-tuple-element.45), channel_id=1, source_target_pairs={{0,16},{2,66},{10,26},{8,72},{16,0},{18,82},{26,10},{24,88},{34,50... | collective-permute-start | bytes 1228808 | tf_op jit(solution)/shard_map/ppermute | solution.py:37
  118.4 5.5 %collective-permute-start.18 = (bf16[80,1280]{1,0:T(8,128)(2,1)S(1)}, bf16[80,1280]{1,0:T(8,128)(2,1)S(1)}, u32[]{:S(2)}, u32[]{:S(2)}) collective-permute-start(bf16[80,1280]{1,0:T(8,128)(2,1)S(1)} %get-tuple-element.47), channel_id=1, source_target_pairs={{0,4},{4,0},{1,5},{5,1},{2,6},{6,2},{3,7},{7,3},{8,12},{12,8},{9,1... | collective-permute-start | bytes 614408 | tf_op jit(solution)/shard_map/ppermute | solution.py:25
  124.0 1.5 %collective-permute-start.19 = (f32[40,1280]{1,0:T(8,128)S(1)}, f32[40,1280]{1,0:T(8,128)S(1)}, u32[]{:S(2)}, u32[]{:S(2)}) collective-permute-start(f32[40,1280]{1,0:T(8,128)S(1)} %dynamic-slice_bitcast_fusion), channel_id=1, source_target_pairs={{0,2},{2,0},{1,3},{3,1},{4,6},{6,4},{5,7},{7,5},{8,10},{10,8},{9,1... | collective-permute-start | bytes 614408 | tf_op jit(solution)/shard_map/ppermute | solution.py:25

commit v22 on v20

--- a/solution.py
+++ b/solution.py
@@ -504,7 +504,7 @@
     mine, theirs = settle(my_xl, [in_hbm(m), *m_received], F32)
     across = lax.ppermute(theirs, ("xl", "o"), [(i, 3 - i) for i in range(4)])
     products = left_product(place, mine, shift(theirs, "xl", 1), left_inverse)
-    products = left_product(place, shift(mine, "o", 1), across, left_inverse, products)
+    products = left_product(place, across, shift(mine, "o", 1), left_inverse, products)
     blocks = lax.all_to_all(products, ("o", "c", "z", "y", "xl"), 0, 0, tiled=True)
     f, *f_pieces = fold(second_me, f_parts, in_hbm(products))
     update = right_product(place, blocks, right_inverse, f_pieces[0])

time: 126 us -> 126 us (level)
  waiting for transfers between devices: 34.9 us -> 33.1 us
  starting transfers between devices: 35.8 us -> 37.3 us
    ppermute x6, waiting for transfers between devices: 14.5 us -> 12.8 us  [shift(): return lax.ppermute(x, axis, [(i, (i + step) % size) for i in range(size)])]
    ppermute x1, starting transfers between devices: 0.18 us -> 1.81 us  [per_device(): across = lax.ppermute(theirs, ('xl', 'o'), [(i, 3 - i) for i in range(4)])]
    ppermute x1, waiting for transfers between devices: 1.53 us -> 0.01 us  [per_device(): across = lax.ppermute(theirs, ('xl', 'o'), [(i, 3 - i) for i in range(4)])]
    ppermute x13, waiting for transfers between devices: 18.9 us -> 20.3 us  [turn(): return lax.ppermute(x, ('z', 'y', 'c'), pairs)]
  transfers between devices with their start and end apart: 21 -> 21, of which waited for: 9 -> 8; matrix products, arithmetic and copies ran while one was open for 0% -> 0% of each run, Pallas kernels for 35% -> 35%
where the time goes in v22:
time: 126 us
  Pallas kernels  53.4 us (42%)
  starting transfers between devices  37.3 us (30%)
  waiting for transfers between devices  33.1 us (26%)
    ppermute x13, starting transfers between devices, turn(): return lax.ppermute(x, ('z', 'y', 'c'), pairs)  20.7 us
    ppermute x13, waiting for transfers between devices, turn(): return lax.ppermute(x, ('z', 'y', 'c'), pairs)  20.3 us
    pallas_call x1, Pallas kernels, factor_term(): pl.pallas_call(factor_kernel, out_shape=[out, out, side, side, out], grid...  15.9 us
    ppermute x6, waiting for transfers between devices, shift(): return lax.ppermute(x, axis, [(i, (i + step) % size) for i in range(size)])  12.8 us
    all_to_all x1, starting transfers between devices, per_device(): lax.all_to_all(products, ('o', 'c', 'z', 'y', 'xl'), 0, 0, tiled=True)  8.5 us
    pallas_call x1, Pallas kernels, cross_term(): pl.pallas_call(cross_kernel, out_shape=[out] * 4, grid_spec=pltpu.Prefetc...  8.31 us
    pallas_call x2, Pallas kernels, left_product(): pl.pallas_call(functools.partial(left_kernel, own), out_shape=total if ow...  6.95 us
    ppermute x6, starting transfers between devices, shift(): return lax.ppermute(x, axis, [(i, (i + step) % size) for i in range(size)])  6.28 us
  transfers between devices with their start and end apart: 21, of which 8 were waited for; matrix products, arithmetic and copies ran while one was open for 0% of the time, Pallas kernels for 35%

profile of v22, /device:TPU:1, one launch (start us, length us, event | category | flops | bytes accessed | tf_op | source)
XLA Modules:
  0.0 125.6 jit_solution(13813918168874772148)
XLA Ops:
  0.6 1.5 %collective-permute-start = (bf16[768,2560]{1,0:T(8,128)(2,1)}, bf16[768,2560]{1,0:T(8,128)(2,1)}, u32[]{:S(2)}, u32[]{:S(2)}) collective-permute-start(bf16[768,2560]{1,0:T(8,128)(2,1)} %h_own.1), channel_id=1, source_target_pairs={{0,2},{2,0},{1,3},{3,1},{4,6},{6,4},{5,7},{7,5},{8,10},{10,8},{9,1... | collective-permute-start | bytes 11796488 | tf_op jit(solution)/shard_map/ppermute | solution.py:25
  2.1 0.1 collective-permute-start.1
  2.2 0.1 pad_add_fusion.place
  2.3 5.4 %cross_own.1.partial = f32[1280,1280]{1,0:T(8,128)S(1)} custom-call(s32[4]{0:T(128)S(1)} %pad_add_fusion.place, bf16[768,2560]{1,0:T(8,128)(2,1)} %g_own.1, bf16[768,2560]{1,0:T(8,128)(2,1)} %h_own.1), custom_call_target="tpu_custom_call" | custom-call | flops 2516582400 | bytes 7864320 | tf_op jit(solution)/shard_map/cross_own/pallas_call | solution.py:125
  7.7 1.1 collective-permute-done.b.h_next
  8.9 5.6 %collective-permute-done.1.a.g_next = bf16[768,2560]{1,0:T(8,128)(2,1)} collective-permute-done((bf16[768,2560]{1,0:T(8,128)(2,1)}, bf16[768,2560]{1,0:T(8,128)(2,1)}, u32[]{:S(2)}, u32[]{:S(2)}) %collective-permute-start.1) | collective-permute-done | bytes 3932192 | tf_op jit(solution)/shard_map/ppermute | solution.py:25
  14.5 8.3 %cross_term.1 = (bf16[4,80,1280]{2,1,0:T(8,128)(2,1)}, bf16[4,80,1280]{2,1,0:T(8,128)(2,1)}, bf16[4,80,1280]{2,1,0:T(8,128)(2,1)}, bf16[4,80,1280]{2,1,0:T(8,128)(2,1)}) custom-call(s32[4]{0:T(128)S(1)} %pad_add_fusion.place, bf16[768,2560]{1,0:T(8,128)(2,1)} %collective-permute-done.1.a.g_next, bf16[768,2560]{1,0:T(8,128)(2,1)} %collective-permute-done.b.h_next, ...), custom_call_target="tpu_custom_call" | custom-call | flops 2516582400 | bytes 9830400 | tf_op jit(solution)/shard_map/cross_term/pallas_call | solution.py:151
  22.8 1.7 %collective-permute-start.4 = (bf16[4,80,1280]{2,1,0:T(8,128)(2,1)}, bf16[4,80,1280]{2,1,0:T(8,128)(2,1)S(1)}, u32[]{:S(2)}, u32[]{:S(2)}) collective-permute-start(bf16[4,80,1280]{2,1,0:T(8,128)(2,1)} %get-tuple-element.25.after), channel_id=1, source_target_pairs={{0,34},{2,8},{10,40},{8,18},{16,50},{18,24},{26,56},{24,2},{34,64}... | collective-permute-start | bytes 2457608 | tf_op jit(solution)/shard_map/ppermute | solution.py:37
  24.5 1.5 %collective-permute-start.5 = (bf16[4,80,1280]{2,1,0:T(8,128)(2,1)}, bf16[4,80,1280]{2,1,0:T(8,128)(2,1)S(1)}, u32[]{:S(2)}, u32[]{:S(2)}) collective-permute-start(bf16[4,80,1280]{2,1,0:T(8,128)(2,1)} %get-tuple-element.32), channel_id=1, source_target_pairs={{0,98},{2,24},{10,104},{8,2},{16,114},{18,8},{26,120},{24,18},{34,... | collective-permute-start | bytes 2457608 | tf_op jit(solution)/shard_map/ppermute | solution.py:37
  26.1 1.6 %collective-permute-start.6 = (bf16[4,80,1280]{2,1,0:T(8,128)(2,1)}, bf16[4,80,1280]{2,1,0:T(8,128)(2,1)S(1)}, u32[]{:S(2)}, u32[]{:S(2)}) collective-permute-start(bf16[4,80,1280]{2,1,0:T(8,128)(2,1)} %get-tuple-element.33), channel_id=1, source_target_pairs={{0,64},{2,18},{10,74},{8,24},{16,80},{18,2},{26,90},{24,8},{34,98}... | collective-permute-start | bytes 2457608 | tf_op jit(solution)/shard_map/ppermute | solution.py:37
  27.6 15.9 %factor_term.1 = (bf16[4,160,1280]{2,1,0:T(8,128)(2,1)}, bf16[4,160,1280]{2,1,0:T(8,128)(2,1)}, bf16[2,160,1280]{2,1,0:T(8,128)(2,1)}, bf16[2,160,1280]{2,1,0:T(8,128)(2,1)}, bf16[4,160,1280]{2,1,0:T(8,128)(2,1)}) custom-call(s32[4]{0:T(128)S(1)} %pad_add_fusion.place, bf16[768,2560]{1,0:T(8,128)(2,1)} %h_own.1, bf16[768,2560]{1,0:T(8,128)(2,1)} %g_own.1, ...), custom_call_target="tpu_custom_call" | custom-call | flops 10066329600 | bytes 15728640 | tf_op jit(solution)/shard_map/factor_term/pallas_call | solution.py:214
  43.5 1.0 collective-permute-start.2
  44.5 2.0 %collective-permute-start.3 = (bf16[2,160,1280]{2,1,0:T(8,128)(2,1)}, bf16[2,160,1280]{2,1,0:T(8,128)(2,1)}, u32[]{:S(2)}, u32[]{:S(2)}) collective-permute-start(bf16[2,160,1280]{2,1,0:T(8,128)(2,1)} %get-tuple-element.30), channel_id=1, source_target_pairs={{0,98},{2,24},{10,104},{8,2},{16,114},{18,8},{26,120},{24,18},{34,... | collective-permute-start | bytes 2457608 | tf_op jit(solution)/shard_map/ppermute | solution.py:37
  46.5 0.0 collective-permute-done.4.refs_1_
  46.5 0.0 collective-permute-done.5.refs_2_
  46.6 2.2 %fold.2 = (f32[80,1280]{1,0:T(8,128)}, bf16[80,1280]{1,0:T(8,128)(2,1)}, bf16[80,1280]{1,0:T(8,128)(2,1)S(1)}, bf16[80,1280]{1,0:T(8,128)(2,1)}) custom-call(s32[1]{0:T(128)} %bitcast.1.me, bf16[4,80,1280]{2,1,0:T(8,128)(2,1)} %get-tuple-element.31.refs_0_, bf16[4,80,1280]{2,1,0:T(8,128)(2,1)S(1)} %collective-permute-done.4.refs_1_, ...), custom_call_target="tpu_custom_call" | custom-call | tf_op jit(solution)/shard_map/fold/pallas_call | solution.py:261
  48.8 2.2 %collective-permute-start.7 = (bf16[80,1280]{1,0:T(8,128)(2,1)}, bf16[80,1280]{1,0:T(8,128)(2,1)S(1)}, u32[]{:S(2)}, u32[]{:S(2)}) collective-permute-start(bf16[80,1280]{1,0:T(8,128)(2,1)} %get-tuple-element.34), channel_id=1, source_target_pairs={{0,10},{2,32},{10,16},{8,42},{16,26},{18,48},{26,0},{24,58},{34,40... | collective-permute-start | bytes 614408 | tf_op jit(solution)/shard_map/ppermute | solution.py:37
  51.0 2.2 %collective-permute-start.8 = (bf16[80,1280]{1,0:T(8,128)(2,1)}, bf16[80,1280]{1,0:T(8,128)(2,1)S(1)}, u32[]{:S(2)}, u32[]{:S(2)}) collective-permute-start(bf16[80,1280]{1,0:T(8,128)(2,1)} %get-tuple-element.35), channel_id=1, source_target_pairs={{0,26},{2,96},{10,0},{8,106},{16,10},{18,112},{26,16},{24,122},{34... | collective-permute-start | bytes 614408 | tf_op jit(solution)/shard_map/ppermute | solution.py:37
  53.2 1.1 collective-permute-start.9
  54.3 7.2 %collective-permute-done.7.refs_0_.refs_1_ = bf16[80,1280]{1,0:T(8,128)(2,1)S(1)} collective-permute-done((bf16[80,1280]{1,0:T(8,128)(2,1)}, bf16[80,1280]{1,0:T(8,128)(2,1)S(1)}, u32[]{:S(2)}, u32[]{:S(2)}) %collective-permute-start.7) | collective-permute-done | bytes 204832 | tf_op jit(solution)/shard_map/ppermute | solution.py:37
  61.5 0.0 collective-permute-done.8.refs_1_.refs_2_
  61.5 1.2 settle.2
  62.7 1.3 %collective-permute-start.14 = (f32[40,1280]{1,0:T(8,128)S(1)}, f32[40,1280]{1,0:T(8,128)S(1)}, u32[]{:S(2)}, u32[]{:S(2)}) collective-permute-start(f32[40,1280]{1,0:T(8,128)S(1)} %get-tuple-element.40), channel_id=1, source_target_pairs={{0,4},{4,0},{1,5},{5,1},{2,6},{6,2},{3,7},{7,3},{8,12},{12,8},{9,1... | collective-permute-start | bytes 614408 | tf_op jit(solution)/shard_map/ppermute | solution.py:25
  64.0 1.8 %collective-permute-start.12 = (f32[40,1280]{1,0:T(8,128)S(1)}, f32[40,1280]{1,0:T(8,128)S(1)}, u32[]{:S(2)}, u32[]{:S(2)}) collective-permute-start(f32[40,1280]{1,0:T(8,128)S(1)} %get-tuple-element.40), channel_id=1, source_target_pairs={{0,5},{1,4},{4,1},{5,0},{2,7},{3,6},{6,3},{7,2},{8,13},{9,12},{12,... | collective-permute-start | bytes 614408 | tf_op jit(solution)/shard_map/ppermute | solution.py:505
  65.8 0.7 collective-permute-start.13
  66.5 3.5 %grow.1 = (bf16[4,160,1280]{2,1,0:T(8,128)(2,1)}, bf16[4,160,1280]{2,1,0:T(8,128)(2,1)}) custom-call(bf16[4,160,1280]{2,1,0:T(8,128)(2,1)} %get-tuple-element.27.right, bf16[4,160,1280]{2,1,0:T(8,128)(2,1)} %get-tuple-element.28.left, bf16[2,160,1280]{2,1,0:T(8,128)(2,1)S(1)} %collective-permute-done.2.from_left, ...), custom_call_target="tpu_custom_call", output_to_operand_aliasing={{0}: (0, {}), {1}: (1, {})} | custom-call | tf_op jit(solution)/shard_map/grow/pallas_call | solution.py:328
  70.0 1.9 %collective-permute-start.10 = (bf16[4,160,1280]{2,1,0:T(8,128)(2,1)}, bf16[4,160,1280]{2,1,0:T(8,128)(2,1)S(1)}, u32[]{:S(2)}, u32[]{:S(2)}) collective-permute-start(bf16[4,160,1280]{2,1,0:T(8,128)(2,1)} %get-tuple-element.37), channel_id=1, source_target_pairs={{0,34},{2,8},{10,40},{8,18},{16,50},{18,24},{26,56},{24,2},{34,64}... | collective-permute-start | bytes 4915208 | tf_op jit(solution)/shard_map/ppermute | solution.py:37
  71.9 1.5 %collective-permute-start.11 = (bf16[4,160,1280]{2,1,0:T(8,128)(2,1)}, bf16[4,160,1280]{2,1,0:T(8,128)(2,1)S(1)}, u32[]{:S(2)}, u32[]{:S(2)}) collective-permute-start(bf16[4,160,1280]{2,1,0:T(8,128)(2,1)} %get-tuple-element.38), channel_id=1, source_target_pairs={{0,98},{2,24},{10,104},{8,2},{16,114},{18,8},{26,120},{24,18},{34,... | collective-permute-start | bytes 4915208 | tf_op jit(solution)/shard_map/ppermute | solution.py:37
  73.4 2.9 %left_own.1.rest_0_ = f32[80,1280]{1,0:T(8,128)S(1)} custom-call(s32[4]{0:T(128)S(1)} %pad_add_fusion.place, f32[40,1280]{1,0:T(8,128)S(1)} %get-tuple-element.41.a, f32[40,1280]{1,0:T(8,128)S(1)} %collective-permute-done.14.b, bf16[2560,1280]{1,0:T(8,128)(2,1)} %left.3), custom_call_target="tpu_custom_call" | custom-call | tf_op jit(solution)/shard_map/left_own/pallas_call | solution.py:403
  76.4 0.0 collective-permute-done.12.a
  76.4 4.0 %left_product.1.refs_3_ = bf16[128,16,128]{2,1,0:T(8,128)(2,1)} custom-call(s32[4]{0:T(128)S(1)} %pad_add_fusion.place, f32[40,1280]{1,0:T(8,128)S(1)} %collective-permute-done.12.a, f32[40,1280]{1,0:T(8,128)S(1)} %collective-permute-done.13.b, bf16[2560,1280]{1,0:T(8,128)(2,1)} %left.3, f32[80,1280]{1,0:T(8,128)S(1)} %left_own.1.rest_0_), custom_call_target="tpu_custom_call" | custom-call | flops 16777216000 | tf_op jit(solution)/shard_map/left_product/pallas_call | solution.py:403
  80.4 8.5 %all-to-all-start = ((bf16[128,16,128]{2,1,0:T(8,128)(2,1)}), bf16[128,16,128]{2,1,0:T(8,128)(2,1)}, u32[]{:S(2)}, u32[]{:S(2)}) async-start(bf16[128,16,128]{2,1,0:T(8,128)(2,1)} %left_product.1.refs_3_), calls=%async_computation | async-start | bytes 1048576 | tf_op jit(solution)/shard_map/all_to_all | solution.py:508
  88.9 4.4 %collective-permute-done.10.refs_1_ = bf16[4,160,1280]{2,1,0:T(8,128)(2,1)S(1)} collective-permute-done((bf16[4,160,1280]{2,1,0:T(8,128)(2,1)}, bf16[4,160,1280]{2,1,0:T(8,128)(2,1)S(1)}, u32[]{:S(2)}, u32[]{:S(2)}) %collective-permute-start.10) | collective-permute-done | bytes 1638432 | tf_op jit(solution)/shard_map/ppermute | solution.py:37
  93.4 4.4 %collective-permute-done.11.refs_2_ = bf16[4,160,1280]{2,1,0:T(8,128)(2,1)S(1)} collective-permute-done((bf16[4,160,1280]{2,1,0:T(8,128)(2,1)}, bf16[4,160,1280]{2,1,0:T(8,128)(2,1)S(1)}, u32[]{:S(2)}, u32[]{:S(2)}) %collective-permute-start.11) | collective-permute-done | bytes 1638432 | tf_op jit(solution)/shard_map/ppermute | solution.py:37
  97.8 2.8 %fold.3 = (f32[160,1280]{1,0:T(8,128)}, bf16[160,1280]{1,0:T(8,128)(2,1)}, bf16[160,1280]{1,0:T(8,128)(2,1)}, bf16[160,1280]{1,0:T(8,128)(2,1)}) custom-call(s32[1]{0:T(128)} %bitcast.1.me, bf16[4,160,1280]{2,1,0:T(8,128)(2,1)} %get-tuple-element.26.refs_4_.refs_0_, bf16[4,160,1280]{2,1,0:T(8,128)(2,1)S(1)} %collective-permute-done.10.refs_1_, ...), custom_call_target="tpu_custom_call" | custom-call | tf_op jit(solution)/shard_map/fold/pallas_call | solution.py:261
  100.6 1.7 %collective-permute-start.15 = (bf16[160,1280]{1,0:T(8,128)(2,1)}, bf16[160,1280]{1,0:T(8,128)(2,1)S(1)}, u32[]{:S(2)}, u32[]{:S(2)}) collective-permute-start(bf16[160,1280]{1,0:T(8,128)(2,1)} %get-tuple-element.43.late), channel_id=1, source_target_pairs={{0,10},{2,32},{10,16},{8,42},{16,26},{18,48},{26,0},{24,58},{34,40... | collective-permute-start | bytes 1228808 | tf_op jit(solution)/shard_map/ppermute | solution.py:37
  102.2 1.4 %collective-permute-start.16 = (bf16[160,1280]{1,0:T(8,128)(2,1)}, bf16[160,1280]{1,0:T(8,128)(2,1)S(1)}, u32[]{:S(2)}, u32[]{:S(2)}) collective-permute-start(bf16[160,1280]{1,0:T(8,128)(2,1)} %get-tuple-element.44), channel_id=1, source_target_pairs={{0,26},{2,96},{10,0},{8,106},{16,10},{18,112},{26,16},{24,122},{34... | collective-permute-start | bytes 1228808 | tf_op jit(solution)/shard_map/ppermute | solution.py:37
  103.6 0.9 collective-permute-start.17
  104.5 0.0 all-to-all-done.blocks
  104.5 5.7 %right_product.1.refs_4_ = f32[40,1280]{1,0:T(8,128)} custom-call(s32[4]{0:T(128)S(1)} %pad_add_fusion.place, bf16[128,16,128]{2,1,0:T(8,128)(2,1)} %all-to-all-done.blocks, bf16[2560,1280]{1,0:T(8,128)(2,1)} %right.1, bf16[160,1280]{1,0:T(8,128)(2,1)} %get-tuple-element.43.late), custom_call_target="tpu_custom_call" | custom-call | flops 41943040000 | bytes 6553600 | tf_op jit(solution)/shard_map/right_product/pallas_call | solution.py:445
  110.2 0.0 collective-permute-done.15.refs_1_
  110.2 4.2 %collective-permute-done.17.refs_3_ = bf16[160,1280]{1,0:T(8,128)(2,1)S(1)} collective-permute-done((bf16[160,1280]{1,0:T(8,128)(2,1)}, bf16[160,1280]{1,0:T(8,128)(2,1)S(1)}, u32[]{:S(2)}, u32[]{:S(2)}) %collective-permute-start.17) | collective-permute-done | bytes 409632 | tf_op jit(solution)/shard_map/ppermute | solution.py:37
  114.4 1.5 %settle.3 = (f32[80,1280]{1,0:T(8,128)S(1)}, bf16[80,1280]{1,0:T(8,128)(2,1)S(1)}) custom-call(s32[1]{0:T(128)} %bitcast.xl, f32[160,1280]{1,0:T(8,128)} %get-tuple-element.42.refs_0_, bf16[160,1280]{1,0:T(8,128)(2,1)S(1)} %collective-permute-done.15.refs_1_, bf16[160,1280]{1,0:T(8,128)(2,1)S(1)} %collective-permute-done.16.refs_2_, ...), custom_call_target="tpu_custom_call" | custom-call | tf_op jit(solution)/shard_map/settle/pallas_call | solution.py:295
  115.9 1.6 %collective-permute-start.18 = (bf16[80,1280]{1,0:T(8,128)(2,1)S(1)}, bf16[80,1280]{1,0:T(8,128)(2,1)S(1)}, u32[]{:S(2)}, u32[]{:S(2)}) collective-permute-start(bf16[80,1280]{1,0:T(8,128)(2,1)S(1)} %get-tuple-element.47), channel_id=1, source_target_pairs={{0,4},{4,0},{1,5},{5,1},{2,6},{6,2},{3,7},{7,3},{8,12},{12,8},{9,1... | collective-permute-start | bytes 614408 | tf_op jit(solution)/shard_map/ppermute | solution.py:25
  117.5 4.9 %collective-permute-done.18 = bf16[80,1280]{1,0:T(8,128)(2,1)S(1)} collective-permute-done((bf16[80,1280]{1,0:T(8,128)(2,1)S(1)}, bf16[80,1280]{1,0:T(8,128)(2,1)S(1)}, u32[]{:S(2)}, u32[]{:S(2)}) %collective-permute-start.18) | collective-permute-done | bytes 204832 | tf_op jit(solution)/shard_map/ppermute | solution.py:25
  122.5 1.2 collective-permute-start.19
  123.7 1.1 collective-permute-done.19
  124.8 0.8 maximum_bitcast_fusion
  (10 shorter events, 0.1 us)
Async XLA Ops:
  0.6 8.3 %collective-permute-start = (bf16[768,2560]{1,0:T(8,128)(2,1)}, bf16[768,2560]{1,0:T(8,128)(2,1)}, u32[]{:S(2)}, u32[]{:S(2)}) collective-permute-start(bf16[768,2560]{1,0:T(8,128)(2,1)} %h_own.1), channel_id=1, source_target_pairs={{0,2},{2,0},{1,3},{3,1},{4,6},{6,4},{5,7},{7,5},{8,10},{10,8},{9,1... | collective-permute-start | bytes 11796488 | tf_op jit(solution)/shard_map/ppermute | solution.py:25
  2.1 12.4 %collective-permute-start.1 = (bf16[768,2560]{1,0:T(8,128)(2,1)}, bf16[768,2560]{1,0:T(8,128)(2,1)}, u32[]{:S(2)}, u32[]{:S(2)}) collective-permute-start(bf16[768,2560]{1,0:T(8,128)(2,1)} %g_own.1), channel_id=1, source_target_pairs={{0,2},{2,0},{1,3},{3,1},{4,6},{6,4},{5,7},{7,5},{8,10},{10,8},{9,1... | collective-permute-start | bytes 11796488 | tf_op jit(solution)/shard_map/ppermute | solution.py:25
  22.8 23.7 %collective-permute-start.4 = (bf16[4,80,1280]{2,1,0:T(8,128)(2,1)}, bf16[4,80,1280]{2,1,0:T(8,128)(2,1)S(1)}, u32[]{:S(2)}, u32[]{:S(2)}) collective-permute-start(bf16[4,80,1280]{2,1,0:T(8,128)(2,1)} %get-tuple-element.25.after), channel_id=1, source_target_pairs={{0,34},{2,8},{10,40},{8,18},{16,50},{18,24},{26,56},{24,2},{34,64}... | collective-permute-start | bytes 2457608 | tf_op jit(solution)/shard_map/ppermute | solution.py:37
  24.5 22.0 %collective-permute-start.5 = (bf16[4,80,1280]{2,1,0:T(8,128)(2,1)}, bf16[4,80,1280]{2,1,0:T(8,128)(2,1)S(1)}, u32[]{:S(2)}, u32[]{:S(2)}) collective-permute-start(bf16[4,80,1280]{2,1,0:T(8,128)(2,1)} %get-tuple-element.32), channel_id=1, source_target_pairs={{0,98},{2,24},{10,104},{8,2},{16,114},{18,8},{26,120},{24,18},{34,... | collective-permute-start | bytes 2457608 | tf_op jit(solution)/shard_map/ppermute | solution.py:37
  26.1 20.5 %collective-permute-start.6 = (bf16[4,80,1280]{2,1,0:T(8,128)(2,1)}, bf16[4,80,1280]{2,1,0:T(8,128)(2,1)S(1)}, u32[]{:S(2)}, u32[]{:S(2)}) collective-permute-start(bf16[4,80,1280]{2,1,0:T(8,128)(2,1)} %get-tuple-element.33), channel_id=1, source_target_pairs={{0,64},{2,18},{10,74},{8,24},{16,80},{18,2},{26,90},{24,8},{34,98}... | collective-permute-start | bytes 2457608 | tf_op jit(solution)/shard_map/ppermute | solution.py:37
  43.5 22.9 %collective-permute-start.2 = (bf16[2,160,1280]{2,1,0:T(8,128)(2,1)}, bf16[2,160,1280]{2,1,0:T(8,128)(2,1)S(1)}, u32[]{:S(2)}, u32[]{:S(2)}) collective-permute-start(bf16[2,160,1280]{2,1,0:T(8,128)(2,1)} %get-tuple-element.29), channel_id=1, source_target_pairs={{0,34},{2,8},{10,40},{8,18},{16,50},{18,24},{26,56},{24,2},{34,64}... | collective-permute-start | bytes 2457608 | tf_op jit(solution)/shard_map/ppermute | solution.py:37
  44.5 21.9 %collective-permute-start.3 = (bf16[2,160,1280]{2,1,0:T(8,128)(2,1)}, bf16[2,160,1280]{2,1,0:T(8,128)(2,1)}, u32[]{:S(2)}, u32[]{:S(2)}) collective-permute-start(bf16[2,160,1280]{2,1,0:T(8,128)(2,1)} %get-tuple-element.30), channel_id=1, source_target_pairs={{0,98},{2,24},{10,104},{8,2},{16,114},{18,8},{26,120},{24,18},{34,... | collective-permute-start | bytes 2457608 | tf_op jit(solution)/shard_map/ppermute | solution.py:37
  48.8 12.7 %collective-permute-start.7 = (bf16[80,1280]{1,0:T(8,128)(2,1)}, bf16[80,1280]{1,0:T(8,128)(2,1)S(1)}, u32[]{:S(2)}, u32[]{:S(2)}) collective-permute-start(bf16[80,1280]{1,0:T(8,128)(2,1)} %get-tuple-element.34), channel_id=1, source_target_pairs={{0,10},{2,32},{10,16},{8,42},{16,26},{18,48},{26,0},{24,58},{34,40... | collective-permute-start | bytes 614408 | tf_op jit(solution)/shard_map/ppermute | solution.py:37
  51.0 10.5 %collective-permute-start.8 = (bf16[80,1280]{1,0:T(8,128)(2,1)}, bf16[80,1280]{1,0:T(8,128)(2,1)S(1)}, u32[]{:S(2)}, u32[]{:S(2)}) collective-permute-start(bf16[80,1280]{1,0:T(8,128)(2,1)} %get-tuple-element.35), channel_id=1, source_target_pairs={{0,26},{2,96},{10,0},{8,106},{16,10},{18,112},{26,16},{24,122},{34... | collective-permute-start | bytes 614408 | tf_op jit(solution)/shard_map/ppermute | solution.py:37
  53.2 8.3 %collective-permute-start.9 = (bf16[80,1280]{1,0:T(8,128)(2,1)S(1)}, bf16[80,1280]{1,0:T(8,128)(2,1)S(1)}, u32[]{:S(2)}, u32[]{:S(2)}) collective-permute-start(bf16[80,1280]{1,0:T(8,128)(2,1)S(1)} %get-tuple-element.36), channel_id=1, source_target_pairs={{0,16},{2,66},{10,26},{8,72},{16,0},{18,82},{26,10},{24,88},{34,50... | collective-permute-start | bytes 614408 | tf_op jit(solution)/shard_map/ppermute | solution.py:37
  62.7 10.7 %collective-permute-start.14 = (f32[40,1280]{1,0:T(8,128)S(1)}, f32[40,1280]{1,0:T(8,128)S(1)}, u32[]{:S(2)}, u32[]{:S(2)}) collective-permute-start(f32[40,1280]{1,0:T(8,128)S(1)} %get-tuple-element.40), channel_id=1, source_target_pairs={{0,4},{4,0},{1,5},{5,1},{2,6},{6,2},{3,7},{7,3},{8,12},{12,8},{9,1... | collective-permute-start | bytes 614408 | tf_op jit(solution)/shard_map/ppermute | solution.py:25
  64.0 12.4 %collective-permute-start.12 = (f32[40,1280]{1,0:T(8,128)S(1)}, f32[40,1280]{1,0:T(8,128)S(1)}, u32[]{:S(2)}, u32[]{:S(2)}) collective-permute-start(f32[40,1280]{1,0:T(8,128)S(1)} %get-tuple-element.40), channel_id=1, source_target_pairs={{0,5},{1,4},{4,1},{5,0},{2,7},{3,6},{6,3},{7,2},{8,13},{9,12},{12,... | collective-permute-start | bytes 614408 | tf_op jit(solution)/shard_map/ppermute | solution.py:505
  65.8 10.6 %collective-permute-start.13 = (f32[40,1280]{1,0:T(8,128)S(1)}, f32[40,1280]{1,0:T(8,128)S(1)}, u32[]{:S(2)}, u32[]{:S(2)}) collective-permute-start(f32[40,1280]{1,0:T(8,128)S(1)} %get-tuple-element.41.a), channel_id=1, source_target_pairs={{0,1},{1,0},{2,3},{3,2},{4,5},{5,4},{6,7},{7,6},{8,9},{9,8},{10,11... | collective-permute-start | bytes 614408 | tf_op jit(solution)/shard_map/ppermute | solution.py:25
  70.0 23.4 %collective-permute-start.10 = (bf16[4,160,1280]{2,1,0:T(8,128)(2,1)}, bf16[4,160,1280]{2,1,0:T(8,128)(2,1)S(1)}, u32[]{:S(2)}, u32[]{:S(2)}) collective-permute-start(bf16[4,160,1280]{2,1,0:T(8,128)(2,1)} %get-tuple-element.37), channel_id=1, source_target_pairs={{0,34},{2,8},{10,40},{8,18},{16,50},{18,24},{26,56},{24,2},{34,64}... | collective-permute-start | bytes 4915208 | tf_op jit(solution)/shard_map/ppermute | solution.py:37
  71.9 25.9 %collective-permute-start.11 = (bf16[4,160,1280]{2,1,0:T(8,128)(2,1)}, bf16[4,160,1280]{2,1,0:T(8,128)(2,1)S(1)}, u32[]{:S(2)}, u32[]{:S(2)}) collective-permute-start(bf16[4,160,1280]{2,1,0:T(8,128)(2,1)} %get-tuple-element.38), channel_id=1, source_target_pairs={{0,98},{2,24},{10,104},{8,2},{16,114},{18,8},{26,120},{24,18},{34,... | collective-permute-start | bytes 4915208 | tf_op jit(solution)/shard_map/ppermute | solution.py:37
  80.4 24.1 %all-to-all-start = ((bf16[128,16,128]{2,1,0:T(8,128)(2,1)}), bf16[128,16,128]{2,1,0:T(8,128)(2,1)}, u32[]{:S(2)}, u32[]{:S(2)}) async-start(bf16[128,16,128]{2,1,0:T(8,128)(2,1)} %left_product.1.refs_3_), calls=%async_computation | async-start | bytes 1048576 | tf_op jit(solution)/shard_map/all_to_all | solution.py:508
  100.6 9.6 %collective-permute-start.15 = (bf16[160,1280]{1,0:T(8,128)(2,1)}, bf16[160,1280]{1,0:T(8,128)(2,1)S(1)}, u32[]{:S(2)}, u32[]{:S(2)}) collective-permute-start(bf16[160,1280]{1,0:T(8,128)(2,1)} %get-tuple-element.43.late), channel_id=1, source_target_pairs={{0,10},{2,32},{10,16},{8,42},{16,26},{18,48},{26,0},{24,58},{34,40... | collective-permute-start | bytes 1228808 | tf_op jit(solution)/shard_map/ppermute | solution.py:37
  102.2 8.0 %collective-permute-start.16 = (bf16[160,1280]{1,0:T(8,128)(2,1)}, bf16[160,1280]{1,0:T(8,128)(2,1)S(1)}, u32[]{:S(2)}, u32[]{:S(2)}) collective-permute-start(bf16[160,1280]{1,0:T(8,128)(2,1)} %get-tuple-element.44), channel_id=1, source_target_pairs={{0,26},{2,96},{10,0},{8,106},{16,10},{18,112},{26,16},{24,122},{34... | collective-permute-start | bytes 1228808 | tf_op jit(solution)/shard_map/ppermute | solution.py:37
  103.6 10.8 %collective-permute-start.17 = (bf16[160,1280]{1,0:T(8,128)(2,1)}, bf16[160,1280]{1,0:T(8,128)(2,1)S(1)}, u32[]{:S(2)}, u32[]{:S(2)}) collective-permute-start(bf16[160,1280]{1,0:T(8,128)(2,1)} %get-tuple-element.45), channel_id=1, source_target_pairs={{0,16},{2,66},{10,26},{8,72},{16,0},{18,82},{26,10},{24,88},{34,50... | collective-permute-start | bytes 1228808 | tf_op jit(solution)/shard_map/ppermute | solution.py:37
  115.9 6.5 %collective-permute-start.18 = (bf16[80,1280]{1,0:T(8,128)(2,1)S(1)}, bf16[80,1280]{1,0:T(8,128)(2,1)S(1)}, u32[]{:S(2)}, u32[]{:S(2)}) collective-permute-start(bf16[80,1280]{1,0:T(8,128)(2,1)S(1)} %get-tuple-element.47), channel_id=1, source_target_pairs={{0,4},{4,0},{1,5},{5,1},{2,6},{6,2},{3,7},{7,3},{8,12},{12,8},{9,1... | collective-permute-start | bytes 614408 | tf_op jit(solution)/shard_map/ppermute | solution.py:25
  122.5 2.3 %collective-permute-start.19 = (f32[40,1280]{1,0:T(8,128)S(1)}, f32[40,1280]{1,0:T(8,128)S(1)}, u32[]{:S(2)}, u32[]{:S(2)}) collective-permute-start(f32[40,1280]{1,0:T(8,128)S(1)} %dynamic-slice_bitcast_fusion), channel_id=1, source_target_pairs={{0,2},{2,0},{1,3},{3,1},{4,6},{6,4},{5,7},{7,5},{8,10},{10,8},{9,1... | collective-permute-start | bytes 614408 | tf_op jit(solution)/shard_map/ppermute | solution.py:25

commit v23 on v22

--- a/solution.py
+++ b/solution.py
@@ -243,35 +243,32 @@
     return total
 
 
-def fold_kernel(count, me, *refs):
-    own, *others = refs[-6:-2]
-    held, sems = refs[-2:]
-    steps = [(1, others[0]), (2, others[1]), (3, others[2]), (0, own)]
-    for r, _ in steps:
-        pltpu.make_async_copy(refs[0].at[(me[0] + r) & 3], held.at[r], sems.at[r]).start()
-    for r, out in steps:
-        wait_all(held.at[r], sems.at[r])
+def fold_kernel(count, ahead, me, *refs):
+    outs, (held, sems) = refs[-2 - len(ahead) : -2], refs[-2:]
+    for n, r in enumerate(ahead):
+        pltpu.make_async_copy(refs[0].at[(me[0] + r) & 3], held.at[n], sems.at[n]).start()
+    for n, r in enumerate(ahead):
+        wait_all(held.at[n], sems.at[n])
         at = (me[0] + r) & 3
-        out[...] = add(held[r], *[part[at] for part in refs[1:count]]).astype(out.dtype)
-
-
-def fold(me, parts, *after):
+        outs[n][...] = add(held[n], *[part[at] for part in refs[1:count]]).astype(outs[n].dtype)
+
+
+def fold(me, parts, ahead, dtype, *after):
     _, rows, width = parts[0].shape
-    whole = pl.BlockSpec((rows, width), lambda s, m: (0, 0))
-    return pl.pallas_call(
-        functools.partial(fold_kernel, len(parts)),
-        out_shape=[pltpu.HBM((rows, width), F32)]
-        + [pltpu.VMEM((rows, width), BF)] * 3,
+    n = len(ahead)
+    return pl.pallas_call(
+        functools.partial(fold_kernel, len(parts), ahead),
+        out_shape=[pltpu.VMEM((rows, width), dtype)] * n,
         grid_spec=pltpu.PrefetchScalarGridSpec(
             num_scalar_prefetch=1,
             grid=(1,),
             in_specs=[pl.BlockSpec(memory_space=pltpu.HBM)]
             + [VMEM] * (len(parts) - 1)
             + [ANY] * len(after),
-            out_specs=[whole] + [VMEM] * 3,
-            scratch_shapes=[pltpu.VMEM((4, rows, width), BF), pltpu.SemaphoreType.DMA((4,))],
-        ),
-        compiler_params=pltpu.CompilerParams(vmem_limit_bytes=12 * 2**20),
+            out_specs=[VMEM] * n,
+            scratch_shapes=[pltpu.VMEM((n, rows, width), BF), pltpu.SemaphoreType.DMA((n,))],
+        ),
+        compiler_params=pltpu.CompilerParams(vmem_limit_bytes=8 * 2**20),
         cost_estimate=pl.CostEstimate(flops=0, bytes_accessed=0, transcendentals=0),
         name="fold",
     )(me, in_hbm(parts[0]), *parts[1:], *after)
@@ -298,8 +295,7 @@
         grid_spec=pltpu.PrefetchScalarGridSpec(
             num_scalar_prefetch=1,
             grid=(1,),
-            in_specs=[pl.BlockSpec((rows, width), lambda s, x: (0, 0))]
-            + [VMEM] * (len(parts) - 1)
+            in_specs=[VMEM] * len(parts)
             + [ANY] * len(after),
             out_specs=[half] * 2,
             scratch_shapes=[pltpu.VMEM((rows, width), F32)],
@@ -496,19 +492,21 @@
     def second_sends(pieces):
         return [turn(pieces[s - 1], s, 1) for s in (1, 3, 2)]
 
-    m, *m_pieces = fold(second_me, m_parts, in_hbm(f_own))
+    m_pieces = fold(second_me, m_parts, (1, 2, 3), BF, in_hbm(f_own))
+    (m,) = fold(second_me, m_parts, (0,), F32, m_pieces[0])
     m_received = second_sends(m_pieces)
     right, left = grow(right, left, from_left, from_right, *m_received)
     f_parts = [f_own, turn(right, 1, 0), turn(left, -1, 0)]
 
-    mine, theirs = settle(my_xl, [in_hbm(m), *m_received], F32)
+    mine, theirs = settle(my_xl, [m, *m_received], F32)
     across = lax.ppermute(theirs, ("xl", "o"), [(i, 3 - i) for i in range(4)])
     products = left_product(place, mine, shift(theirs, "xl", 1), left_inverse)
     products = left_product(place, across, shift(mine, "o", 1), left_inverse, products)
     blocks = lax.all_to_all(products, ("o", "c", "z", "y", "xl"), 0, 0, tiled=True)
-    f, *f_pieces = fold(second_me, f_parts, in_hbm(products))
+    f_pieces = fold(second_me, f_parts, (1, 2, 3), BF, in_hbm(products))
+    (f,) = fold(second_me, f_parts, (0,), F32, f_pieces[0])
     update = right_product(place, blocks, right_inverse, f_pieces[0])
-    f_mine, f_theirs = settle(my_xl, [in_hbm(f), *second_sends(f_pieces)], BF, in_hbm(update))
+    f_mine, f_theirs = settle(my_xl, [f, *second_sends(f_pieces)], BF, in_hbm(update))
 
     f = add(f_mine, shift(f_theirs, "xl", 1))
     f = f * jnp.where(first, 1.0 / token_total, 1.0).astype(F32)

time: 126 us -> 126 us (level)
  Pallas kernels: 53.4 us -> 55.1 us
  waiting for transfers between devices: 33.1 us -> 31.4 us
    ppermute x13, waiting for transfers between devices: 20.3 us -> 18.3 us  [turn(): return lax.ppermute(x, ('z', 'y', 'c'), pairs)]
    pallas_call x2 -> x4, Pallas kernels: 5.02 us -> 6.57 us  [fold(): pl.pallas_call(functools.partial(fold_kernel, len(parts), ahead), out_sha...]
  transfers between devices with their start and end apart: 21 -> 21, of which waited for: 8 -> 9; matrix products, arithmetic and copies ran while one was open for 0% -> 0% of each run, Pallas kernels for 35% -> 36%
where the time goes in v23:
time: 126 us; the launch traced here: 125 us
  Pallas kernels  55.1 us (44%)
  starting transfers between devices  37.2 us (30%)
  waiting for transfers between devices  31.4 us (25%)
    ppermute x13, starting transfers between devices, turn(): return lax.ppermute(x, ('z', 'y', 'c'), pairs)  21.1 us
    ppermute x13, waiting for transfers between devices, turn(): return lax.ppermute(x, ('z', 'y', 'c'), pairs)  18.3 us
    pallas_call x1, Pallas kernels, factor_term(): pl.pallas_call(factor_kernel, out_shape=[out, out, side, side, out], grid...  15.9 us
    ppermute x6, waiting for transfers between devices, shift(): return lax.ppermute(x, axis, [(i, (i + step) % size) for i in range(size)])  13.1 us
    pallas_call x1, Pallas kernels, cross_term(): pl.pallas_call(cross_kernel, out_shape=[out] * 4, grid_spec=pltpu.Prefetc...  8.31 us
    all_to_all x1, starting transfers between devices, per_device(): lax.all_to_all(products, ('o', 'c', 'z', 'y', 'xl'), 0, 0, tiled=True)  8.28 us
    pallas_call x2, Pallas kernels, left_product(): pl.pallas_call(functools.partial(left_kernel, own), out_shape=total if ow...  6.95 us
    pallas_call x4, Pallas kernels, fold(): pl.pallas_call(functools.partial(fold_kernel, len(parts), ahead), out_sha...  6.57 us
  transfers between devices with their start and end apart: 21, of which 9 were waited for; matrix products, arithmetic and copies ran while one was open for 0% of the time, Pallas kernels for 36%

profile of v23, /device:TPU:1, one launch (start us, length us, event | category | flops | bytes accessed | tf_op | source)
XLA Modules:
  0.0 125.4 jit_solution(8666414429363083869)
XLA Ops:
  0.6 1.5 %collective-permute-start = (bf16[768,2560]{1,0:T(8,128)(2,1)}, bf16[768,2560]{1,0:T(8,128)(2,1)}, u32[]{:S(2)}, u32[]{:S(2)}) collective-permute-start(bf16[768,2560]{1,0:T(8,128)(2,1)} %h_own.1), channel_id=1, source_target_pairs={{0,2},{2,0},{1,3},{3,1},{4,6},{6,4},{5,7},{7,5},{8,10},{10,8},{9,1... | collective-permute-start | bytes 11796488 | tf_op jit(solution)/shard_map/ppermute | solution.py:25
  2.1 0.1 collective-permute-start.1
  2.2 0.1 pad_add_fusion.place
  2.3 5.4 %cross_own.1.partial = f32[1280,1280]{1,0:T(8,128)S(1)} custom-call(s32[4]{0:T(128)S(1)} %pad_add_fusion.place, bf16[768,2560]{1,0:T(8,128)(2,1)} %g_own.1, bf16[768,2560]{1,0:T(8,128)(2,1)} %h_own.1), custom_call_target="tpu_custom_call" | custom-call | flops 2516582400 | bytes 7864320 | tf_op jit(solution)/shard_map/cross_own/pallas_call | solution.py:125
  7.7 1.1 collective-permute-done.b.h_next
  8.9 5.6 %collective-permute-done.1.a.g_next = bf16[768,2560]{1,0:T(8,128)(2,1)} collective-permute-done((bf16[768,2560]{1,0:T(8,128)(2,1)}, bf16[768,2560]{1,0:T(8,128)(2,1)}, u32[]{:S(2)}, u32[]{:S(2)}) %collective-permute-start.1) | collective-permute-done | bytes 3932192 | tf_op jit(solution)/shard_map/ppermute | solution.py:25
  14.5 8.3 %cross_term.1 = (bf16[4,80,1280]{2,1,0:T(8,128)(2,1)}, bf16[4,80,1280]{2,1,0:T(8,128)(2,1)}, bf16[4,80,1280]{2,1,0:T(8,128)(2,1)}, bf16[4,80,1280]{2,1,0:T(8,128)(2,1)}) custom-call(s32[4]{0:T(128)S(1)} %pad_add_fusion.place, bf16[768,2560]{1,0:T(8,128)(2,1)} %collective-permute-done.1.a.g_next, bf16[768,2560]{1,0:T(8,128)(2,1)} %collective-permute-done.b.h_next, ...), custom_call_target="tpu_custom_call" | custom-call | flops 2516582400 | bytes 9830400 | tf_op jit(solution)/shard_map/cross_term/pallas_call | solution.py:151
  22.8 1.7 %collective-permute-start.4 = (bf16[4,80,1280]{2,1,0:T(8,128)(2,1)}, bf16[4,80,1280]{2,1,0:T(8,128)(2,1)S(1)}, u32[]{:S(2)}, u32[]{:S(2)}) collective-permute-start(bf16[4,80,1280]{2,1,0:T(8,128)(2,1)} %get-tuple-element.23.after), channel_id=1, source_target_pairs={{0,34},{2,8},{10,40},{8,18},{16,50},{18,24},{26,56},{24,2},{34,64}... | collective-permute-start | bytes 2457608 | tf_op jit(solution)/shard_map/ppermute | solution.py:37
  24.5 1.5 %collective-permute-start.5 = (bf16[4,80,1280]{2,1,0:T(8,128)(2,1)}, bf16[4,80,1280]{2,1,0:T(8,128)(2,1)S(1)}, u32[]{:S(2)}, u32[]{:S(2)}) collective-permute-start(bf16[4,80,1280]{2,1,0:T(8,128)(2,1)} %get-tuple-element.30), channel_id=1, source_target_pairs={{0,98},{2,24},{10,104},{8,2},{16,114},{18,8},{26,120},{24,18},{34,... | collective-permute-start | bytes 2457608 | tf_op jit(solution)/shard_map/ppermute | solution.py:37
  26.1 1.6 %collective-permute-start.6 = (bf16[4,80,1280]{2,1,0:T(8,128)(2,1)}, bf16[4,80,1280]{2,1,0:T(8,128)(2,1)S(1)}, u32[]{:S(2)}, u32[]{:S(2)}) collective-permute-start(bf16[4,80,1280]{2,1,0:T(8,128)(2,1)} %get-tuple-element.31), channel_id=1, source_target_pairs={{0,64},{2,18},{10,74},{8,24},{16,80},{18,2},{26,90},{24,8},{34,98}... | collective-permute-start | bytes 2457608 | tf_op jit(solution)/shard_map/ppermute | solution.py:37
  27.6 15.9 %factor_term.1 = (bf16[4,160,1280]{2,1,0:T(8,128)(2,1)}, bf16[4,160,1280]{2,1,0:T(8,128)(2,1)}, bf16[2,160,1280]{2,1,0:T(8,128)(2,1)}, bf16[2,160,1280]{2,1,0:T(8,128)(2,1)}, bf16[4,160,1280]{2,1,0:T(8,128)(2,1)}) custom-call(s32[4]{0:T(128)S(1)} %pad_add_fusion.place, bf16[768,2560]{1,0:T(8,128)(2,1)} %h_own.1, bf16[768,2560]{1,0:T(8,128)(2,1)} %g_own.1, ...), custom_call_target="tpu_custom_call" | custom-call | flops 10066329600 | bytes 15728640 | tf_op jit(solution)/shard_map/factor_term/pallas_call | solution.py:214
  43.5 1.0 collective-permute-start.2
  44.5 2.0 %collective-permute-start.3 = (bf16[2,160,1280]{2,1,0:T(8,128)(2,1)}, bf16[2,160,1280]{2,1,0:T(8,128)(2,1)}, u32[]{:S(2)}, u32[]{:S(2)}) collective-permute-start(bf16[2,160,1280]{2,1,0:T(8,128)(2,1)} %get-tuple-element.28), channel_id=1, source_target_pairs={{0,98},{2,24},{10,104},{8,2},{16,114},{18,8},{26,120},{24,18},{34,... | collective-permute-start | bytes 2457608 | tf_op jit(solution)/shard_map/ppermute | solution.py:37
  46.5 0.0 collective-permute-done.4.refs_1_
  46.5 0.0 collective-permute-done.5.refs_2_
  46.5 0.0 collective-permute-done.6.refs_3_
  46.6 2.0 %fold.4 = (bf16[80,1280]{1,0:T(8,128)(2,1)}, bf16[80,1280]{1,0:T(8,128)(2,1)}, bf16[80,1280]{1,0:T(8,128)(2,1)}) custom-call(s32[1]{0:T(128)} %bitcast.1.me, bf16[4,80,1280]{2,1,0:T(8,128)(2,1)} %get-tuple-element.29.refs_0_, bf16[4,80,1280]{2,1,0:T(8,128)(2,1)S(1)} %collective-permute-done.4.refs_1_, ...), custom_call_target="tpu_custom_call" | custom-call | tf_op jit(solution)/shard_map/fold/pallas_call | solution.py:259
  48.5 2.3 %collective-permute-start.7 = (bf16[80,1280]{1,0:T(8,128)(2,1)}, bf16[80,1280]{1,0:T(8,128)(2,1)S(1)}, u32[]{:S(2)}, u32[]{:S(2)}) collective-permute-start(bf16[80,1280]{1,0:T(8,128)(2,1)} %get-tuple-element.32.refs_4_), channel_id=1, source_target_pairs={{0,10},{2,32},{10,16},{8,42},{16,26},{18,48},{26,0},{24,58},{34,40... | collective-permute-start | bytes 614408 | tf_op jit(solution)/shard_map/ppermute | solution.py:37
  50.8 2.2 %collective-permute-start.8 = (bf16[80,1280]{1,0:T(8,128)(2,1)}, bf16[80,1280]{1,0:T(8,128)(2,1)}, u32[]{:S(2)}, u32[]{:S(2)}) collective-permute-start(bf16[80,1280]{1,0:T(8,128)(2,1)} %get-tuple-element.33), channel_id=1, source_target_pairs={{0,26},{2,96},{10,0},{8,106},{16,10},{18,112},{26,16},{24,122},{34... | collective-permute-start | bytes 614408 | tf_op jit(solution)/shard_map/ppermute | solution.py:37
  53.0 1.1 collective-permute-start.9
  54.1 1.1 fold.5.refs_0_
  55.2 4.1 %collective-permute-done.7.refs_0_.refs_1_ = bf16[80,1280]{1,0:T(8,128)(2,1)S(1)} collective-permute-done((bf16[80,1280]{1,0:T(8,128)(2,1)}, bf16[80,1280]{1,0:T(8,128)(2,1)S(1)}, u32[]{:S(2)}, u32[]{:S(2)}) %collective-permute-start.7) | collective-permute-done | bytes 204832 | tf_op jit(solution)/shard_map/ppermute | solution.py:37
  59.3 2.0 %collective-permute-done.9.refs_2_.refs_3_ = bf16[80,1280]{1,0:T(8,128)(2,1)} collective-permute-done((bf16[80,1280]{1,0:T(8,128)(2,1)}, bf16[80,1280]{1,0:T(8,128)(2,1)}, u32[]{:S(2)}, u32[]{:S(2)}) %collective-permute-start.9) | collective-permute-done | bytes 204832 | tf_op jit(solution)/shard_map/ppermute | solution.py:37
  61.3 1.2 settle.2
  62.4 1.3 %collective-permute-start.14 = (f32[40,1280]{1,0:T(8,128)S(1)}, f32[40,1280]{1,0:T(8,128)S(1)}, u32[]{:S(2)}, u32[]{:S(2)}) collective-permute-start(f32[40,1280]{1,0:T(8,128)S(1)} %get-tuple-element.37), channel_id=1, source_target_pairs={{0,4},{4,0},{1,5},{5,1},{2,6},{6,2},{3,7},{7,3},{8,12},{12,8},{9,1... | collective-permute-start | bytes 614408 | tf_op jit(solution)/shard_map/ppermute | solution.py:25
  63.7 1.9 %collective-permute-start.12 = (f32[40,1280]{1,0:T(8,128)S(1)}, f32[40,1280]{1,0:T(8,128)S(1)}, u32[]{:S(2)}, u32[]{:S(2)}) collective-permute-start(f32[40,1280]{1,0:T(8,128)S(1)} %get-tuple-element.37), channel_id=1, source_target_pairs={{0,5},{1,4},{4,1},{5,0},{2,7},{3,6},{6,3},{7,2},{8,13},{9,12},{12,... | collective-permute-start | bytes 614408 | tf_op jit(solution)/shard_map/ppermute | solution.py:502
  65.6 0.6 collective-permute-start.13
  66.2 3.5 %grow.1 = (bf16[4,160,1280]{2,1,0:T(8,128)(2,1)}, bf16[4,160,1280]{2,1,0:T(8,128)(2,1)}) custom-call(bf16[4,160,1280]{2,1,0:T(8,128)(2,1)} %get-tuple-element.25.right, bf16[4,160,1280]{2,1,0:T(8,128)(2,1)} %get-tuple-element.26.left, bf16[2,160,1280]{2,1,0:T(8,128)(2,1)S(1)} %collective-permute-done.2.from_left, ...), custom_call_target="tpu_custom_call", output_to_operand_aliasing={{0}: (0, {}), {1}: (1, {})} | custom-call | tf_op jit(solution)/shard_map/grow/pallas_call | solution.py:324
  69.8 2.3 %collective-permute-start.10 = (bf16[4,160,1280]{2,1,0:T(8,128)(2,1)}, bf16[4,160,1280]{2,1,0:T(8,128)(2,1)S(1)}, u32[]{:S(2)}, u32[]{:S(2)}) collective-permute-start(bf16[4,160,1280]{2,1,0:T(8,128)(2,1)} %get-tuple-element.35), channel_id=1, source_target_pairs={{0,34},{2,8},{10,40},{8,18},{16,50},{18,24},{26,56},{24,2},{34,64}... | collective-permute-start | bytes 4915208 | tf_op jit(solution)/shard_map/ppermute | solution.py:37
  72.0 1.5 %collective-permute-start.11 = (bf16[4,160,1280]{2,1,0:T(8,128)(2,1)}, bf16[4,160,1280]{2,1,0:T(8,128)(2,1)S(1)}, u32[]{:S(2)}, u32[]{:S(2)}) collective-permute-start(bf16[4,160,1280]{2,1,0:T(8,128)(2,1)} %get-tuple-element.36), channel_id=1, source_target_pairs={{0,98},{2,24},{10,104},{8,2},{16,114},{18,8},{26,120},{24,18},{34,... | collective-permute-start | bytes 4915208 | tf_op jit(solution)/shard_map/ppermute | solution.py:37
  73.6 2.9 %left_own.1.rest_0_ = f32[80,1280]{1,0:T(8,128)S(1)} custom-call(s32[4]{0:T(128)S(1)} %pad_add_fusion.place, f32[40,1280]{1,0:T(8,128)S(1)} %get-tuple-element.38.a, f32[40,1280]{1,0:T(8,128)S(1)} %collective-permute-done.14.b, bf16[2560,1280]{1,0:T(8,128)(2,1)} %left.3), custom_call_target="tpu_custom_call" | custom-call | tf_op jit(solution)/shard_map/left_own/pallas_call | solution.py:399
  76.5 4.0 %left_product.1.refs_3_ = bf16[128,16,128]{2,1,0:T(8,128)(2,1)} custom-call(s32[4]{0:T(128)S(1)} %pad_add_fusion.place, f32[40,1280]{1,0:T(8,128)S(1)} %collective-permute-done.12.a, f32[40,1280]{1,0:T(8,128)S(1)} %collective-permute-done.13.b, bf16[2560,1280]{1,0:T(8,128)(2,1)} %left.3, f32[80,1280]{1,0:T(8,128)S(1)} %left_own.1.rest_0_), custom_call_target="tpu_custom_call" | custom-call | flops 16777216000 | tf_op jit(solution)/shard_map/left_product/pallas_call | solution.py:399
  80.5 8.3 %all-to-all-start = ((bf16[128,16,128]{2,1,0:T(8,128)(2,1)}), bf16[128,16,128]{2,1,0:T(8,128)(2,1)}, u32[]{:S(2)}, u32[]{:S(2)}) async-start(bf16[128,16,128]{2,1,0:T(8,128)(2,1)} %left_product.1.refs_3_), calls=%async_computation | async-start | bytes 1048576 | tf_op jit(solution)/shard_map/all_to_all | solution.py:505
  88.8 4.8 %collective-permute-done.10.refs_1_ = bf16[4,160,1280]{2,1,0:T(8,128)(2,1)S(1)} collective-permute-done((bf16[4,160,1280]{2,1,0:T(8,128)(2,1)}, bf16[4,160,1280]{2,1,0:T(8,128)(2,1)S(1)}, u32[]{:S(2)}, u32[]{:S(2)}) %collective-permute-start.10) | collective-permute-done | bytes 1638432 | tf_op jit(solution)/shard_map/ppermute | solution.py:37
  93.7 4.3 %collective-permute-done.11.refs_2_ = bf16[4,160,1280]{2,1,0:T(8,128)(2,1)S(1)} collective-permute-done((bf16[4,160,1280]{2,1,0:T(8,128)(2,1)}, bf16[4,160,1280]{2,1,0:T(8,128)(2,1)S(1)}, u32[]{:S(2)}, u32[]{:S(2)}) %collective-permute-start.11) | collective-permute-done | bytes 1638432 | tf_op jit(solution)/shard_map/ppermute | solution.py:37
  98.0 2.4 %fold.6 = (bf16[160,1280]{1,0:T(8,128)(2,1)}, bf16[160,1280]{1,0:T(8,128)(2,1)}, bf16[160,1280]{1,0:T(8,128)(2,1)}) custom-call(s32[1]{0:T(128)} %bitcast.1.me, bf16[4,160,1280]{2,1,0:T(8,128)(2,1)} %get-tuple-element.24.refs_4_.refs_0_, bf16[4,160,1280]{2,1,0:T(8,128)(2,1)S(1)} %collective-permute-done.10.refs_1_, ...), custom_call_target="tpu_custom_call" | custom-call | tf_op jit(solution)/shard_map/fold/pallas_call | solution.py:259
  100.3 1.6 %collective-permute-start.15 = (bf16[160,1280]{1,0:T(8,128)(2,1)}, bf16[160,1280]{1,0:T(8,128)(2,1)}, u32[]{:S(2)}, u32[]{:S(2)}) collective-permute-start(bf16[160,1280]{1,0:T(8,128)(2,1)} %get-tuple-element.39.refs_3_.late), channel_id=1, source_target_pairs={{0,10},{2,32},{10,16},{8,42},{16,26},{18,48},{26,0},{24,58},{34,40... | collective-permute-start | bytes 1228808 | tf_op jit(solution)/shard_map/ppermute | solution.py:37
  101.9 1.4 %collective-permute-start.16 = (bf16[160,1280]{1,0:T(8,128)(2,1)}, bf16[160,1280]{1,0:T(8,128)(2,1)}, u32[]{:S(2)}, u32[]{:S(2)}) collective-permute-start(bf16[160,1280]{1,0:T(8,128)(2,1)} %get-tuple-element.40), channel_id=1, source_target_pairs={{0,26},{2,96},{10,0},{8,106},{16,10},{18,112},{26,16},{24,122},{34... | collective-permute-start | bytes 1228808 | tf_op jit(solution)/shard_map/ppermute | solution.py:37
  103.3 0.9 collective-permute-start.17
  104.2 5.7 %right_product.1.refs_4_ = f32[40,1280]{1,0:T(8,128)} custom-call(s32[4]{0:T(128)S(1)} %pad_add_fusion.place, bf16[128,16,128]{2,1,0:T(8,128)(2,1)} %all-to-all-done.blocks, bf16[2560,1280]{1,0:T(8,128)(2,1)} %right.1, bf16[160,1280]{1,0:T(8,128)(2,1)} %get-tuple-element.39.refs_3_.late), custom_call_target="tpu_custom_call" | custom-call | flops 41943040000 | bytes 6553600 | tf_op jit(solution)/shard_map/right_product/pallas_call | solution.py:441
  109.9 1.2 fold.7.refs_0_
  111.1 3.1 %collective-permute-done.17.refs_3_ = bf16[160,1280]{1,0:T(8,128)(2,1)} collective-permute-done((bf16[160,1280]{1,0:T(8,128)(2,1)}, bf16[160,1280]{1,0:T(8,128)(2,1)}, u32[]{:S(2)}, u32[]{:S(2)}) %collective-permute-start.17) | collective-permute-done | bytes 409632 | tf_op jit(solution)/shard_map/ppermute | solution.py:37
  114.2 1.6 %settle.3 = (f32[80,1280]{1,0:T(8,128)S(1)}, bf16[80,1280]{1,0:T(8,128)(2,1)S(1)}) custom-call(s32[1]{0:T(128)} %bitcast.xl, f32[160,1280]{1,0:T(8,128)S(1)} %fold.7.refs_0_, bf16[160,1280]{1,0:T(8,128)(2,1)} %collective-permute-done.15.refs_1_, bf16[160,1280]{1,0:T(8,128)(2,1)} %collective-permute-done.16.refs_2_, ...), custom_call_target="tpu_custom_call" | custom-call | tf_op jit(solution)/shard_map/settle/pallas_call | solution.py:292
  115.8 1.5 %collective-permute-start.18 = (bf16[80,1280]{1,0:T(8,128)(2,1)S(1)}, bf16[80,1280]{1,0:T(8,128)(2,1)S(1)}, u32[]{:S(2)}, u32[]{:S(2)}) collective-permute-start(bf16[80,1280]{1,0:T(8,128)(2,1)S(1)} %get-tuple-element.43), channel_id=1, source_target_pairs={{0,4},{4,0},{1,5},{5,1},{2,6},{6,2},{3,7},{7,3},{8,12},{12,8},{9,1... | collective-permute-start | bytes 614408 | tf_op jit(solution)/shard_map/ppermute | solution.py:25
  117.3 5.2 %collective-permute-done.18 = bf16[80,1280]{1,0:T(8,128)(2,1)S(1)} collective-permute-done((bf16[80,1280]{1,0:T(8,128)(2,1)S(1)}, bf16[80,1280]{1,0:T(8,128)(2,1)S(1)}, u32[]{:S(2)}, u32[]{:S(2)}) %collective-permute-start.18) | collective-permute-done | bytes 204832 | tf_op jit(solution)/shard_map/ppermute | solution.py:25
  122.6 1.0 collective-permute-start.19
  123.5 1.1 collective-permute-done.19
  124.7 0.8 maximum_bitcast_fusion
  (12 shorter events, 0.1 us)
Async XLA Ops:
  0.6 8.3 %collective-permute-start = (bf16[768,2560]{1,0:T(8,128)(2,1)}, bf16[768,2560]{1,0:T(8,128)(2,1)}, u32[]{:S(2)}, u32[]{:S(2)}) collective-permute-start(bf16[768,2560]{1,0:T(8,128)(2,1)} %h_own.1), channel_id=1, source_target_pairs={{0,2},{2,0},{1,3},{3,1},{4,6},{6,4},{5,7},{7,5},{8,10},{10,8},{9,1... | collective-permute-start | bytes 11796488 | tf_op jit(solution)/shard_map/ppermute | solution.py:25
  2.1 12.4 %collective-permute-start.1 = (bf16[768,2560]{1,0:T(8,128)(2,1)}, bf16[768,2560]{1,0:T(8,128)(2,1)}, u32[]{:S(2)}, u32[]{:S(2)}) collective-permute-start(bf16[768,2560]{1,0:T(8,128)(2,1)} %g_own.1), channel_id=1, source_target_pairs={{0,2},{2,0},{1,3},{3,1},{4,6},{6,4},{5,7},{7,5},{8,10},{10,8},{9,1... | collective-permute-start | bytes 11796488 | tf_op jit(solution)/shard_map/ppermute | solution.py:25
  22.8 23.7 %collective-permute-start.4 = (bf16[4,80,1280]{2,1,0:T(8,128)(2,1)}, bf16[4,80,1280]{2,1,0:T(8,128)(2,1)S(1)}, u32[]{:S(2)}, u32[]{:S(2)}) collective-permute-start(bf16[4,80,1280]{2,1,0:T(8,128)(2,1)} %get-tuple-element.23.after), channel_id=1, source_target_pairs={{0,34},{2,8},{10,40},{8,18},{16,50},{18,24},{26,56},{24,2},{34,64}... | collective-permute-start | bytes 2457608 | tf_op jit(solution)/shard_map/ppermute | solution.py:37
  24.5 22.0 %collective-permute-start.5 = (bf16[4,80,1280]{2,1,0:T(8,128)(2,1)}, bf16[4,80,1280]{2,1,0:T(8,128)(2,1)S(1)}, u32[]{:S(2)}, u32[]{:S(2)}) collective-permute-start(bf16[4,80,1280]{2,1,0:T(8,128)(2,1)} %get-tuple-element.30), channel_id=1, source_target_pairs={{0,98},{2,24},{10,104},{8,2},{16,114},{18,8},{26,120},{24,18},{34,... | collective-permute-start | bytes 2457608 | tf_op jit(solution)/shard_map/ppermute | solution.py:37
  26.1 20.5 %collective-permute-start.6 = (bf16[4,80,1280]{2,1,0:T(8,128)(2,1)}, bf16[4,80,1280]{2,1,0:T(8,128)(2,1)S(1)}, u32[]{:S(2)}, u32[]{:S(2)}) collective-permute-start(bf16[4,80,1280]{2,1,0:T(8,128)(2,1)} %get-tuple-element.31), channel_id=1, source_target_pairs={{0,64},{2,18},{10,74},{8,24},{16,80},{18,2},{26,90},{24,8},{34,98}... | collective-permute-start | bytes 2457608 | tf_op jit(solution)/shard_map/ppermute | solution.py:37
  43.5 22.7 %collective-permute-start.2 = (bf16[2,160,1280]{2,1,0:T(8,128)(2,1)}, bf16[2,160,1280]{2,1,0:T(8,128)(2,1)S(1)}, u32[]{:S(2)}, u32[]{:S(2)}) collective-permute-start(bf16[2,160,1280]{2,1,0:T(8,128)(2,1)} %get-tuple-element.27), channel_id=1, source_target_pairs={{0,34},{2,8},{10,40},{8,18},{16,50},{18,24},{26,56},{24,2},{34,64}... | collective-permute-start | bytes 2457608 | tf_op jit(solution)/shard_map/ppermute | solution.py:37
  44.5 21.7 %collective-permute-start.3 = (bf16[2,160,1280]{2,1,0:T(8,128)(2,1)}, bf16[2,160,1280]{2,1,0:T(8,128)(2,1)}, u32[]{:S(2)}, u32[]{:S(2)}) collective-permute-start(bf16[2,160,1280]{2,1,0:T(8,128)(2,1)} %get-tuple-element.28), channel_id=1, source_target_pairs={{0,98},{2,24},{10,104},{8,2},{16,114},{18,8},{26,120},{24,18},{34,... | collective-permute-start | bytes 2457608 | tf_op jit(solution)/shard_map/ppermute | solution.py:37
  48.5 10.7 %collective-permute-start.7 = (bf16[80,1280]{1,0:T(8,128)(2,1)}, bf16[80,1280]{1,0:T(8,128)(2,1)S(1)}, u32[]{:S(2)}, u32[]{:S(2)}) collective-permute-start(bf16[80,1280]{1,0:T(8,128)(2,1)} %get-tuple-element.32.refs_4_), channel_id=1, source_target_pairs={{0,10},{2,32},{10,16},{8,42},{16,26},{18,48},{26,0},{24,58},{34,40... | collective-permute-start | bytes 614408 | tf_op jit(solution)/shard_map/ppermute | solution.py:37
  50.8 8.4 %collective-permute-start.8 = (bf16[80,1280]{1,0:T(8,128)(2,1)}, bf16[80,1280]{1,0:T(8,128)(2,1)}, u32[]{:S(2)}, u32[]{:S(2)}) collective-permute-start(bf16[80,1280]{1,0:T(8,128)(2,1)} %get-tuple-element.33), channel_id=1, source_target_pairs={{0,26},{2,96},{10,0},{8,106},{16,10},{18,112},{26,16},{24,122},{34... | collective-permute-start | bytes 614408 | tf_op jit(solution)/shard_map/ppermute | solution.py:37
  53.0 8.2 %collective-permute-start.9 = (bf16[80,1280]{1,0:T(8,128)(2,1)}, bf16[80,1280]{1,0:T(8,128)(2,1)}, u32[]{:S(2)}, u32[]{:S(2)}) collective-permute-start(bf16[80,1280]{1,0:T(8,128)(2,1)} %get-tuple-element.34), channel_id=1, source_target_pairs={{0,16},{2,66},{10,26},{8,72},{16,0},{18,82},{26,10},{24,88},{34,50... | collective-permute-start | bytes 614408 | tf_op jit(solution)/shard_map/ppermute | solution.py:37
  62.4 11.1 %collective-permute-start.14 = (f32[40,1280]{1,0:T(8,128)S(1)}, f32[40,1280]{1,0:T(8,128)S(1)}, u32[]{:S(2)}, u32[]{:S(2)}) collective-permute-start(f32[40,1280]{1,0:T(8,128)S(1)} %get-tuple-element.37), channel_id=1, source_target_pairs={{0,4},{4,0},{1,5},{5,1},{2,6},{6,2},{3,7},{7,3},{8,12},{12,8},{9,1... | collective-permute-start | bytes 614408 | tf_op jit(solution)/shard_map/ppermute | solution.py:25
  63.7 12.8 %collective-permute-start.12 = (f32[40,1280]{1,0:T(8,128)S(1)}, f32[40,1280]{1,0:T(8,128)S(1)}, u32[]{:S(2)}, u32[]{:S(2)}) collective-permute-start(f32[40,1280]{1,0:T(8,128)S(1)} %get-tuple-element.37), channel_id=1, source_target_pairs={{0,5},{1,4},{4,1},{5,0},{2,7},{3,6},{6,3},{7,2},{8,13},{9,12},{12,... | collective-permute-start | bytes 614408 | tf_op jit(solution)/shard_map/ppermute | solution.py:502
  65.6 10.9 %collective-permute-start.13 = (f32[40,1280]{1,0:T(8,128)S(1)}, f32[40,1280]{1,0:T(8,128)S(1)}, u32[]{:S(2)}, u32[]{:S(2)}) collective-permute-start(f32[40,1280]{1,0:T(8,128)S(1)} %get-tuple-element.38.a), channel_id=1, source_target_pairs={{0,1},{1,0},{2,3},{3,2},{4,5},{5,4},{6,7},{7,6},{8,9},{9,8},{10,11... | collective-permute-start | bytes 614408 | tf_op jit(solution)/shard_map/ppermute | solution.py:25
  69.8 23.9 %collective-permute-start.10 = (bf16[4,160,1280]{2,1,0:T(8,128)(2,1)}, bf16[4,160,1280]{2,1,0:T(8,128)(2,1)S(1)}, u32[]{:S(2)}, u32[]{:S(2)}) collective-permute-start(bf16[4,160,1280]{2,1,0:T(8,128)(2,1)} %get-tuple-element.35), channel_id=1, source_target_pairs={{0,34},{2,8},{10,40},{8,18},{16,50},{18,24},{26,56},{24,2},{34,64}... | collective-permute-start | bytes 4915208 | tf_op jit(solution)/shard_map/ppermute | solution.py:37
  72.0 25.9 %collective-permute-start.11 = (bf16[4,160,1280]{2,1,0:T(8,128)(2,1)}, bf16[4,160,1280]{2,1,0:T(8,128)(2,1)S(1)}, u32[]{:S(2)}, u32[]{:S(2)}) collective-permute-start(bf16[4,160,1280]{2,1,0:T(8,128)(2,1)} %get-tuple-element.36), channel_id=1, source_target_pairs={{0,98},{2,24},{10,104},{8,2},{16,114},{18,8},{26,120},{24,18},{34,... | collective-permute-start | bytes 4915208 | tf_op jit(solution)/shard_map/ppermute | solution.py:37
  80.5 23.7 %all-to-all-start = ((bf16[128,16,128]{2,1,0:T(8,128)(2,1)}), bf16[128,16,128]{2,1,0:T(8,128)(2,1)}, u32[]{:S(2)}, u32[]{:S(2)}) async-start(bf16[128,16,128]{2,1,0:T(8,128)(2,1)} %left_product.1.refs_3_), calls=%async_computation | async-start | bytes 1048576 | tf_op jit(solution)/shard_map/all_to_all | solution.py:505
  100.3 10.8 %collective-permute-start.15 = (bf16[160,1280]{1,0:T(8,128)(2,1)}, bf16[160,1280]{1,0:T(8,128)(2,1)}, u32[]{:S(2)}, u32[]{:S(2)}) collective-permute-start(bf16[160,1280]{1,0:T(8,128)(2,1)} %get-tuple-element.39.refs_3_.late), channel_id=1, source_target_pairs={{0,10},{2,32},{10,16},{8,42},{16,26},{18,48},{26,0},{24,58},{34,40... | collective-permute-start | bytes 1228808 | tf_op jit(solution)/shard_map/ppermute | solution.py:37
  101.9 9.2 %collective-permute-start.16 = (bf16[160,1280]{1,0:T(8,128)(2,1)}, bf16[160,1280]{1,0:T(8,128)(2,1)}, u32[]{:S(2)}, u32[]{:S(2)}) collective-permute-start(bf16[160,1280]{1,0:T(8,128)(2,1)} %get-tuple-element.40), channel_id=1, source_target_pairs={{0,26},{2,96},{10,0},{8,106},{16,10},{18,112},{26,16},{24,122},{34... | collective-permute-start | bytes 1228808 | tf_op jit(solution)/shard_map/ppermute | solution.py:37
  103.3 10.9 %collective-permute-start.17 = (bf16[160,1280]{1,0:T(8,128)(2,1)}, bf16[160,1280]{1,0:T(8,128)(2,1)}, u32[]{:S(2)}, u32[]{:S(2)}) collective-permute-start(bf16[160,1280]{1,0:T(8,128)(2,1)} %get-tuple-element.41), channel_id=1, source_target_pairs={{0,16},{2,66},{10,26},{8,72},{16,0},{18,82},{26,10},{24,88},{34,50... | collective-permute-start | bytes 1228808 | tf_op jit(solution)/shard_map/ppermute | solution.py:37
  115.8 6.7 %collective-permute-start.18 = (bf16[80,1280]{1,0:T(8,128)(2,1)S(1)}, bf16[80,1280]{1,0:T(8,128)(2,1)S(1)}, u32[]{:S(2)}, u32[]{:S(2)}) collective-permute-start(bf16[80,1280]{1,0:T(8,128)(2,1)S(1)} %get-tuple-element.43), channel_id=1, source_target_pairs={{0,4},{4,0},{1,5},{5,1},{2,6},{6,2},{3,7},{7,3},{8,12},{12,8},{9,1... | collective-permute-start | bytes 614408 | tf_op jit(solution)/shard_map/ppermute | solution.py:25
  122.6 2.1 %collective-permute-start.19 = (f32[40,1280]{1,0:T(8,128)S(1)}, f32[40,1280]{1,0:T(8,128)S(1)}, u32[]{:S(2)}, u32[]{:S(2)}) collective-permute-start(f32[40,1280]{1,0:T(8,128)S(1)} %dynamic-slice_bitcast_fusion), channel_id=1, source_target_pairs={{0,2},{2,0},{1,3},{3,1},{4,6},{6,4},{5,7},{7,5},{8,10},{10,8},{9,1... | collective-permute-start | bytes 614408 | tf_op jit(solution)/shard_map/ppermute | solution.py:25

commit v24 on v22

--- a/solution.py
+++ b/solution.py
@@ -190,17 +190,19 @@
             @pl.when(place[0] == owner)
             def _():
                 for k, ref in enumerate(refs):
-                    pltpu.make_async_copy(ref.at[:, at], lhs.at[slot, k], lhs_sems.at[slot]).start()
+                    pltpu.make_async_copy(ref.at[:, at], lhs.at[slot, k], lhs_sems.at[slot, k]).start()
                     if with_rhs:
-                        pltpu.make_async_copy(ref.at[:, columns], rhs.at[k], rhs_sem).start()
+                        pltpu.make_async_copy(ref.at[:, columns], rhs.at[k], rhs_sem.at[k]).start()
 
     pl.when(m == 0)(lambda: fetch(0, True))
     pl.when(m < 3)(lambda: fetch(m + 1, False))
     slot = m & 1
-    wait_all(lhs.at[slot], lhs_sems.at[slot])
-    pl.when(m == 0)(lambda: wait_all(rhs, rhs_sem))
-
-    buffer[m] = (contract(lhs[slot, 0], rhs[0]) + contract(lhs[slot, 1], rhs[1])).astype(BF)
+    terms = []
+    for k in range(2):
+        wait_all(lhs.at[slot, k], lhs_sems.at[slot, k])
+        pl.when(m == 0)(functools.partial(wait_all, rhs.at[k], rhs_sem.at[k]))
+        terms.append(contract(lhs[slot, k], rhs[k]))
+    buffer[m] = (terms[0] + terms[1]).astype(BF)
     place_tile(place, buffer, sem, [own, right, (far_a, far_b), left], m, 1)
     pl.when(m == 3)(lambda: wait_all(buffer, sem))
 
@@ -223,8 +225,8 @@
                 pltpu.VMEM((2, 2, tokens, TILE), BF),
                 pltpu.VMEM((2, tokens, half), BF),
                 pltpu.VMEM((4, TILE, half), BF),
+                pltpu.SemaphoreType.DMA((2, 2)),
                 pltpu.SemaphoreType.DMA((2,)),
-                pltpu.SemaphoreType.DMA,
                 pltpu.SemaphoreType.DMA,
             ],
         ),

time: 126 us -> 127 us (level)
  no operation moved by 1% of the time
where the time goes in v24:
time: 127 us; the launch traced here: 126 us
  Pallas kernels  54.1 us (43%)
  starting transfers between devices  36.7 us (29%)
  waiting for transfers between devices  33.8 us (27%)
    ppermute x13, waiting for transfers between devices, turn(): return lax.ppermute(x, ('z', 'y', 'c'), pairs)  20.9 us
    ppermute x13, starting transfers between devices, turn(): return lax.ppermute(x, ('z', 'y', 'c'), pairs)  20.7 us
    pallas_call x1, Pallas kernels, factor_term(): pl.pallas_call(factor_kernel, out_shape=[out, out, side, side, out], grid...  16.5 us
    ppermute x6, waiting for transfers between devices, shift(): return lax.ppermute(x, axis, [(i, (i + step) % size) for i in range(size)])  12.9 us
    pallas_call x1, Pallas kernels, cross_term(): pl.pallas_call(cross_kernel, out_shape=[out] * 4, grid_spec=pltpu.Prefetc...  8.31 us
    all_to_all x1, starting transfers between devices, per_device(): lax.all_to_all(products, ('o', 'c', 'z', 'y', 'xl'), 0, 0, tiled=True)  8.05 us
    pallas_call x2, Pallas kernels, left_product(): pl.pallas_call(functools.partial(left_kernel, own), out_shape=total if ow...  6.95 us
    ppermute x6, starting transfers between devices, shift(): return lax.ppermute(x, axis, [(i, (i + step) % size) for i in range(size)])  6.12 us
  transfers between devices with their start and end apart: 21, of which 8 were waited for; matrix products, arithmetic and copies ran while one was open for 0% of the time, Pallas kernels for 35%

profile of v24, /device:TPU:1, one launch (start us, length us, event | category | flops | bytes accessed | tf_op | source)
XLA Modules:
  0.0 126.2 jit_solution(262255541446856041)
XLA Ops:
  0.6 1.5 %collective-permute-start = (bf16[768,2560]{1,0:T(8,128)(2,1)}, bf16[768,2560]{1,0:T(8,128)(2,1)}, u32[]{:S(2)}, u32[]{:S(2)}) collective-permute-start(bf16[768,2560]{1,0:T(8,128)(2,1)} %h_own.1), channel_id=1, source_target_pairs={{0,2},{2,0},{1,3},{3,1},{4,6},{6,4},{5,7},{7,5},{8,10},{10,8},{9,1... | collective-permute-start | bytes 11796488 | tf_op jit(solution)/shard_map/ppermute | solution.py:25
  2.1 0.1 collective-permute-start.1
  2.2 0.1 pad_add_fusion.place
  2.3 5.4 %cross_own.1.partial = f32[1280,1280]{1,0:T(8,128)S(1)} custom-call(s32[4]{0:T(128)S(1)} %pad_add_fusion.place, bf16[768,2560]{1,0:T(8,128)(2,1)} %g_own.1, bf16[768,2560]{1,0:T(8,128)(2,1)} %h_own.1), custom_call_target="tpu_custom_call" | custom-call | flops 2516582400 | bytes 7864320 | tf_op jit(solution)/shard_map/cross_own/pallas_call | solution.py:125
  7.7 1.1 collective-permute-done.b.h_next
  8.9 5.6 %collective-permute-done.1.a.g_next = bf16[768,2560]{1,0:T(8,128)(2,1)} collective-permute-done((bf16[768,2560]{1,0:T(8,128)(2,1)}, bf16[768,2560]{1,0:T(8,128)(2,1)}, u32[]{:S(2)}, u32[]{:S(2)}) %collective-permute-start.1) | collective-permute-done | bytes 3932192 | tf_op jit(solution)/shard_map/ppermute | solution.py:25
  14.5 8.3 %cross_term.1 = (bf16[4,80,1280]{2,1,0:T(8,128)(2,1)}, bf16[4,80,1280]{2,1,0:T(8,128)(2,1)}, bf16[4,80,1280]{2,1,0:T(8,128)(2,1)}, bf16[4,80,1280]{2,1,0:T(8,128)(2,1)}) custom-call(s32[4]{0:T(128)S(1)} %pad_add_fusion.place, bf16[768,2560]{1,0:T(8,128)(2,1)} %collective-permute-done.1.a.g_next, bf16[768,2560]{1,0:T(8,128)(2,1)} %collective-permute-done.b.h_next, ...), custom_call_target="tpu_custom_call" | custom-call | flops 2516582400 | bytes 9830400 | tf_op jit(solution)/shard_map/cross_term/pallas_call | solution.py:151
  22.8 1.7 %collective-permute-start.4 = (bf16[4,80,1280]{2,1,0:T(8,128)(2,1)}, bf16[4,80,1280]{2,1,0:T(8,128)(2,1)S(1)}, u32[]{:S(2)}, u32[]{:S(2)}) collective-permute-start(bf16[4,80,1280]{2,1,0:T(8,128)(2,1)} %get-tuple-element.25.after), channel_id=1, source_target_pairs={{0,34},{2,8},{10,40},{8,18},{16,50},{18,24},{26,56},{24,2},{34,64}... | collective-permute-start | bytes 2457608 | tf_op jit(solution)/shard_map/ppermute | solution.py:37
  24.5 1.5 %collective-permute-start.5 = (bf16[4,80,1280]{2,1,0:T(8,128)(2,1)}, bf16[4,80,1280]{2,1,0:T(8,128)(2,1)S(1)}, u32[]{:S(2)}, u32[]{:S(2)}) collective-permute-start(bf16[4,80,1280]{2,1,0:T(8,128)(2,1)} %get-tuple-element.32), channel_id=1, source_target_pairs={{0,98},{2,24},{10,104},{8,2},{16,114},{18,8},{26,120},{24,18},{34,... | collective-permute-start | bytes 2457608 | tf_op jit(solution)/shard_map/ppermute | solution.py:37
  26.1 1.6 %collective-permute-start.6 = (bf16[4,80,1280]{2,1,0:T(8,128)(2,1)}, bf16[4,80,1280]{2,1,0:T(8,128)(2,1)S(1)}, u32[]{:S(2)}, u32[]{:S(2)}) collective-permute-start(bf16[4,80,1280]{2,1,0:T(8,128)(2,1)} %get-tuple-element.33), channel_id=1, source_target_pairs={{0,64},{2,18},{10,74},{8,24},{16,80},{18,2},{26,90},{24,8},{34,98}... | collective-permute-start | bytes 2457608 | tf_op jit(solution)/shard_map/ppermute | solution.py:37
  27.6 16.5 %factor_term.1 = (bf16[4,160,1280]{2,1,0:T(8,128)(2,1)}, bf16[4,160,1280]{2,1,0:T(8,128)(2,1)}, bf16[2,160,1280]{2,1,0:T(8,128)(2,1)}, bf16[2,160,1280]{2,1,0:T(8,128)(2,1)}, bf16[4,160,1280]{2,1,0:T(8,128)(2,1)}) custom-call(s32[4]{0:T(128)S(1)} %pad_add_fusion.place, bf16[768,2560]{1,0:T(8,128)(2,1)} %h_own.1, bf16[768,2560]{1,0:T(8,128)(2,1)} %g_own.1, ...), custom_call_target="tpu_custom_call" | custom-call | flops 10066329600 | bytes 15728640 | tf_op jit(solution)/shard_map/factor_term/pallas_call | solution.py:216
  44.2 1.0 collective-permute-start.2
  45.2 2.0 %collective-permute-start.3 = (bf16[2,160,1280]{2,1,0:T(8,128)(2,1)}, bf16[2,160,1280]{2,1,0:T(8,128)(2,1)}, u32[]{:S(2)}, u32[]{:S(2)}) collective-permute-start(bf16[2,160,1280]{2,1,0:T(8,128)(2,1)} %get-tuple-element.30), channel_id=1, source_target_pairs={{0,98},{2,24},{10,104},{8,2},{16,114},{18,8},{26,120},{24,18},{34,... | collective-permute-start | bytes 2457608 | tf_op jit(solution)/shard_map/ppermute | solution.py:37
  47.2 0.0 collective-permute-done.4.refs_1_
  47.2 0.0 collective-permute-done.5.refs_2_
  47.2 0.0 collective-permute-done.6.refs_3_
  47.2 2.2 %fold.2 = (f32[80,1280]{1,0:T(8,128)}, bf16[80,1280]{1,0:T(8,128)(2,1)}, bf16[80,1280]{1,0:T(8,128)(2,1)S(1)}, bf16[80,1280]{1,0:T(8,128)(2,1)}) custom-call(s32[1]{0:T(128)} %bitcast.1.me, bf16[4,80,1280]{2,1,0:T(8,128)(2,1)} %get-tuple-element.31.refs_0_, bf16[4,80,1280]{2,1,0:T(8,128)(2,1)S(1)} %collective-permute-done.4.refs_1_, ...), custom_call_target="tpu_custom_call" | custom-call | tf_op jit(solution)/shard_map/fold/pallas_call | solution.py:263
  49.4 2.2 %collective-permute-start.7 = (bf16[80,1280]{1,0:T(8,128)(2,1)}, bf16[80,1280]{1,0:T(8,128)(2,1)S(1)}, u32[]{:S(2)}, u32[]{:S(2)}) collective-permute-start(bf16[80,1280]{1,0:T(8,128)(2,1)} %get-tuple-element.34), channel_id=1, source_target_pairs={{0,10},{2,32},{10,16},{8,42},{16,26},{18,48},{26,0},{24,58},{34,40... | collective-permute-start | bytes 614408 | tf_op jit(solution)/shard_map/ppermute | solution.py:37
  51.6 2.2 %collective-permute-start.8 = (bf16[80,1280]{1,0:T(8,128)(2,1)}, bf16[80,1280]{1,0:T(8,128)(2,1)S(1)}, u32[]{:S(2)}, u32[]{:S(2)}) collective-permute-start(bf16[80,1280]{1,0:T(8,128)(2,1)} %get-tuple-element.35), channel_id=1, source_target_pairs={{0,26},{2,96},{10,0},{8,106},{16,10},{18,112},{26,16},{24,122},{34... | collective-permute-start | bytes 614408 | tf_op jit(solution)/shard_map/ppermute | solution.py:37
  53.8 1.1 collective-permute-start.9
  54.9 7.2 %collective-permute-done.7.refs_0_.refs_1_ = bf16[80,1280]{1,0:T(8,128)(2,1)S(1)} collective-permute-done((bf16[80,1280]{1,0:T(8,128)(2,1)}, bf16[80,1280]{1,0:T(8,128)(2,1)S(1)}, u32[]{:S(2)}, u32[]{:S(2)}) %collective-permute-start.7) | collective-permute-done | bytes 204832 | tf_op jit(solution)/shard_map/ppermute | solution.py:37
  62.1 0.0 collective-permute-done.8.refs_1_.refs_2_
  62.1 0.0 collective-permute-done.9.refs_2_.refs_3_
  62.2 1.2 settle.2
  63.3 1.3 %collective-permute-start.14 = (f32[40,1280]{1,0:T(8,128)S(1)}, f32[40,1280]{1,0:T(8,128)S(1)}, u32[]{:S(2)}, u32[]{:S(2)}) collective-permute-start(f32[40,1280]{1,0:T(8,128)S(1)} %get-tuple-element.40), channel_id=1, source_target_pairs={{0,4},{4,0},{1,5},{5,1},{2,6},{6,2},{3,7},{7,3},{8,12},{12,8},{9,1... | collective-permute-start | bytes 614408 | tf_op jit(solution)/shard_map/ppermute | solution.py:25
  64.6 1.8 %collective-permute-start.12 = (f32[40,1280]{1,0:T(8,128)S(1)}, f32[40,1280]{1,0:T(8,128)S(1)}, u32[]{:S(2)}, u32[]{:S(2)}) collective-permute-start(f32[40,1280]{1,0:T(8,128)S(1)} %get-tuple-element.40), channel_id=1, source_target_pairs={{0,5},{1,4},{4,1},{5,0},{2,7},{3,6},{6,3},{7,2},{8,13},{9,12},{12,... | collective-permute-start | bytes 614408 | tf_op jit(solution)/shard_map/ppermute | solution.py:507
  66.4 0.7 collective-permute-start.13
  67.1 0.0 collective-permute-done.2.from_left
  67.1 3.5 %grow.1 = (bf16[4,160,1280]{2,1,0:T(8,128)(2,1)}, bf16[4,160,1280]{2,1,0:T(8,128)(2,1)}) custom-call(bf16[4,160,1280]{2,1,0:T(8,128)(2,1)} %get-tuple-element.27.right, bf16[4,160,1280]{2,1,0:T(8,128)(2,1)} %get-tuple-element.28.left, bf16[2,160,1280]{2,1,0:T(8,128)(2,1)S(1)} %collective-permute-done.2.from_left, ...), custom_call_target="tpu_custom_call", output_to_operand_aliasing={{0}: (0, {}), {1}: (1, {})} | custom-call | tf_op jit(solution)/shard_map/grow/pallas_call | solution.py:330
  70.6 2.0 %collective-permute-start.10 = (bf16[4,160,1280]{2,1,0:T(8,128)(2,1)}, bf16[4,160,1280]{2,1,0:T(8,128)(2,1)S(1)}, u32[]{:S(2)}, u32[]{:S(2)}) collective-permute-start(bf16[4,160,1280]{2,1,0:T(8,128)(2,1)} %get-tuple-element.37), channel_id=1, source_target_pairs={{0,34},{2,8},{10,40},{8,18},{16,50},{18,24},{26,56},{24,2},{34,64}... | collective-permute-start | bytes 4915208 | tf_op jit(solution)/shard_map/ppermute | solution.py:37
  72.5 1.5 %collective-permute-start.11 = (bf16[4,160,1280]{2,1,0:T(8,128)(2,1)}, bf16[4,160,1280]{2,1,0:T(8,128)(2,1)S(1)}, u32[]{:S(2)}, u32[]{:S(2)}) collective-permute-start(bf16[4,160,1280]{2,1,0:T(8,128)(2,1)} %get-tuple-element.38), channel_id=1, source_target_pairs={{0,98},{2,24},{10,104},{8,2},{16,114},{18,8},{26,120},{24,18},{34,... | collective-permute-start | bytes 4915208 | tf_op jit(solution)/shard_map/ppermute | solution.py:37
  74.1 2.9 %left_own.1.rest_0_ = f32[80,1280]{1,0:T(8,128)S(1)} custom-call(s32[4]{0:T(128)S(1)} %pad_add_fusion.place, f32[40,1280]{1,0:T(8,128)S(1)} %get-tuple-element.41.a, f32[40,1280]{1,0:T(8,128)S(1)} %collective-permute-done.14.b, bf16[2560,1280]{1,0:T(8,128)(2,1)} %left.3), custom_call_target="tpu_custom_call" | custom-call | tf_op jit(solution)/shard_map/left_own/pallas_call | solution.py:405
  77.0 4.0 %left_product.1.refs_3_ = bf16[128,16,128]{2,1,0:T(8,128)(2,1)} custom-call(s32[4]{0:T(128)S(1)} %pad_add_fusion.place, f32[40,1280]{1,0:T(8,128)S(1)} %collective-permute-done.12.a, f32[40,1280]{1,0:T(8,128)S(1)} %collective-permute-done.13.b, bf16[2560,1280]{1,0:T(8,128)(2,1)} %left.3, f32[80,1280]{1,0:T(8,128)S(1)} %left_own.1.rest_0_), custom_call_target="tpu_custom_call" | custom-call | flops 16777216000 | tf_op jit(solution)/shard_map/left_product/pallas_call | solution.py:405
  81.1 8.0 %all-to-all-start = ((bf16[128,16,128]{2,1,0:T(8,128)(2,1)}), bf16[128,16,128]{2,1,0:T(8,128)(2,1)}, u32[]{:S(2)}, u32[]{:S(2)}) async-start(bf16[128,16,128]{2,1,0:T(8,128)(2,1)} %left_product.1.refs_3_), calls=%async_computation | async-start | bytes 1048576 | tf_op jit(solution)/shard_map/all_to_all | solution.py:510
  89.1 5.4 %collective-permute-done.10.refs_1_ = bf16[4,160,1280]{2,1,0:T(8,128)(2,1)S(1)} collective-permute-done((bf16[4,160,1280]{2,1,0:T(8,128)(2,1)}, bf16[4,160,1280]{2,1,0:T(8,128)(2,1)S(1)}, u32[]{:S(2)}, u32[]{:S(2)}) %collective-permute-start.10) | collective-permute-done | bytes 1638432 | tf_op jit(solution)/shard_map/ppermute | solution.py:37
  94.5 4.0 %collective-permute-done.11.refs_2_ = bf16[4,160,1280]{2,1,0:T(8,128)(2,1)S(1)} collective-permute-done((bf16[4,160,1280]{2,1,0:T(8,128)(2,1)}, bf16[4,160,1280]{2,1,0:T(8,128)(2,1)S(1)}, u32[]{:S(2)}, u32[]{:S(2)}) %collective-permute-start.11) | collective-permute-done | bytes 1638432 | tf_op jit(solution)/shard_map/ppermute | solution.py:37
  98.5 2.8 %fold.3 = (f32[160,1280]{1,0:T(8,128)}, bf16[160,1280]{1,0:T(8,128)(2,1)}, bf16[160,1280]{1,0:T(8,128)(2,1)}, bf16[160,1280]{1,0:T(8,128)(2,1)}) custom-call(s32[1]{0:T(128)} %bitcast.1.me, bf16[4,160,1280]{2,1,0:T(8,128)(2,1)} %get-tuple-element.26.refs_4_.refs_0_, bf16[4,160,1280]{2,1,0:T(8,128)(2,1)S(1)} %collective-permute-done.10.refs_1_, ...), custom_call_target="tpu_custom_call" | custom-call | tf_op jit(solution)/shard_map/fold/pallas_call | solution.py:263
  101.3 1.5 %collective-permute-start.15 = (bf16[160,1280]{1,0:T(8,128)(2,1)}, bf16[160,1280]{1,0:T(8,128)(2,1)S(1)}, u32[]{:S(2)}, u32[]{:S(2)}) collective-permute-start(bf16[160,1280]{1,0:T(8,128)(2,1)} %get-tuple-element.43.late), channel_id=1, source_target_pairs={{0,10},{2,32},{10,16},{8,42},{16,26},{18,48},{26,0},{24,58},{34,40... | collective-permute-start | bytes 1228808 | tf_op jit(solution)/shard_map/ppermute | solution.py:37
  102.9 1.5 %collective-permute-start.16 = (bf16[160,1280]{1,0:T(8,128)(2,1)}, bf16[160,1280]{1,0:T(8,128)(2,1)S(1)}, u32[]{:S(2)}, u32[]{:S(2)}) collective-permute-start(bf16[160,1280]{1,0:T(8,128)(2,1)} %get-tuple-element.44), channel_id=1, source_target_pairs={{0,26},{2,96},{10,0},{8,106},{16,10},{18,112},{26,16},{24,122},{34... | collective-permute-start | bytes 1228808 | tf_op jit(solution)/shard_map/ppermute | solution.py:37
  104.4 0.8 collective-permute-start.17
  105.2 5.7 %right_product.1.refs_4_ = f32[40,1280]{1,0:T(8,128)} custom-call(s32[4]{0:T(128)S(1)} %pad_add_fusion.place, bf16[128,16,128]{2,1,0:T(8,128)(2,1)} %all-to-all-done.blocks, bf16[2560,1280]{1,0:T(8,128)(2,1)} %right.1, bf16[160,1280]{1,0:T(8,128)(2,1)} %get-tuple-element.43.late), custom_call_target="tpu_custom_call" | custom-call | flops 41943040000 | bytes 6553600 | tf_op jit(solution)/shard_map/right_product/pallas_call | solution.py:447
  110.9 4.2 %collective-permute-done.17.refs_3_ = bf16[160,1280]{1,0:T(8,128)(2,1)S(1)} collective-permute-done((bf16[160,1280]{1,0:T(8,128)(2,1)}, bf16[160,1280]{1,0:T(8,128)(2,1)S(1)}, u32[]{:S(2)}, u32[]{:S(2)}) %collective-permute-start.17) | collective-permute-done | bytes 409632 | tf_op jit(solution)/shard_map/ppermute | solution.py:37
  115.1 1.5 %settle.3 = (f32[80,1280]{1,0:T(8,128)S(1)}, bf16[80,1280]{1,0:T(8,128)(2,1)S(1)}) custom-call(s32[1]{0:T(128)} %bitcast.xl, f32[160,1280]{1,0:T(8,128)} %get-tuple-element.42.refs_0_, bf16[160,1280]{1,0:T(8,128)(2,1)S(1)} %collective-permute-done.15.refs_1_, bf16[160,1280]{1,0:T(8,128)(2,1)S(1)} %collective-permute-done.16.refs_2_, ...), custom_call_target="tpu_custom_call" | custom-call | tf_op jit(solution)/shard_map/settle/pallas_call | solution.py:297
  116.6 1.5 %collective-permute-start.18 = (bf16[80,1280]{1,0:T(8,128)(2,1)S(1)}, bf16[80,1280]{1,0:T(8,128)(2,1)S(1)}, u32[]{:S(2)}, u32[]{:S(2)}) collective-permute-start(bf16[80,1280]{1,0:T(8,128)(2,1)S(1)} %get-tuple-element.47), channel_id=1, source_target_pairs={{0,4},{4,0},{1,5},{5,1},{2,6},{6,2},{3,7},{7,3},{8,12},{12,8},{9,1... | collective-permute-start | bytes 614408 | tf_op jit(solution)/shard_map/ppermute | solution.py:25
  118.1 5.1 %collective-permute-done.18 = bf16[80,1280]{1,0:T(8,128)(2,1)S(1)} collective-permute-done((bf16[80,1280]{1,0:T(8,128)(2,1)S(1)}, bf16[80,1280]{1,0:T(8,128)(2,1)S(1)}, u32[]{:S(2)}, u32[]{:S(2)}) %collective-permute-start.18) | collective-permute-done | bytes 204832 | tf_op jit(solution)/shard_map/ppermute | solution.py:25
  123.2 1.1 collective-permute-start.19
  124.3 1.1 collective-permute-done.19
  125.4 0.8 maximum_bitcast_fusion
  (10 shorter events, 0.1 us)
Async XLA Ops:
  0.6 8.3 %collective-permute-start = (bf16[768,2560]{1,0:T(8,128)(2,1)}, bf16[768,2560]{1,0:T(8,128)(2,1)}, u32[]{:S(2)}, u32[]{:S(2)}) collective-permute-start(bf16[768,2560]{1,0:T(8,128)(2,1)} %h_own.1), channel_id=1, source_target_pairs={{0,2},{2,0},{1,3},{3,1},{4,6},{6,4},{5,7},{7,5},{8,10},{10,8},{9,1... | collective-permute-start | bytes 11796488 | tf_op jit(solution)/shard_map/ppermute | solution.py:25
  2.1 12.4 %collective-permute-start.1 = (bf16[768,2560]{1,0:T(8,128)(2,1)}, bf16[768,2560]{1,0:T(8,128)(2,1)}, u32[]{:S(2)}, u32[]{:S(2)}) collective-permute-start(bf16[768,2560]{1,0:T(8,128)(2,1)} %g_own.1), channel_id=1, source_target_pairs={{0,2},{2,0},{1,3},{3,1},{4,6},{6,4},{5,7},{7,5},{8,10},{10,8},{9,1... | collective-permute-start | bytes 11796488 | tf_op jit(solution)/shard_map/ppermute | solution.py:25
  22.8 24.4 %collective-permute-start.4 = (bf16[4,80,1280]{2,1,0:T(8,128)(2,1)}, bf16[4,80,1280]{2,1,0:T(8,128)(2,1)S(1)}, u32[]{:S(2)}, u32[]{:S(2)}) collective-permute-start(bf16[4,80,1280]{2,1,0:T(8,128)(2,1)} %get-tuple-element.25.after), channel_id=1, source_target_pairs={{0,34},{2,8},{10,40},{8,18},{16,50},{18,24},{26,56},{24,2},{34,64}... | collective-permute-start | bytes 2457608 | tf_op jit(solution)/shard_map/ppermute | solution.py:37
  24.5 22.7 %collective-permute-start.5 = (bf16[4,80,1280]{2,1,0:T(8,128)(2,1)}, bf16[4,80,1280]{2,1,0:T(8,128)(2,1)S(1)}, u32[]{:S(2)}, u32[]{:S(2)}) collective-permute-start(bf16[4,80,1280]{2,1,0:T(8,128)(2,1)} %get-tuple-element.32), channel_id=1, source_target_pairs={{0,98},{2,24},{10,104},{8,2},{16,114},{18,8},{26,120},{24,18},{34,... | collective-permute-start | bytes 2457608 | tf_op jit(solution)/shard_map/ppermute | solution.py:37
  26.1 21.1 %collective-permute-start.6 = (bf16[4,80,1280]{2,1,0:T(8,128)(2,1)}, bf16[4,80,1280]{2,1,0:T(8,128)(2,1)S(1)}, u32[]{:S(2)}, u32[]{:S(2)}) collective-permute-start(bf16[4,80,1280]{2,1,0:T(8,128)(2,1)} %get-tuple-element.33), channel_id=1, source_target_pairs={{0,64},{2,18},{10,74},{8,24},{16,80},{18,2},{26,90},{24,8},{34,98}... | collective-permute-start | bytes 2457608 | tf_op jit(solution)/shard_map/ppermute | solution.py:37
  44.2 22.9 %collective-permute-start.2 = (bf16[2,160,1280]{2,1,0:T(8,128)(2,1)}, bf16[2,160,1280]{2,1,0:T(8,128)(2,1)S(1)}, u32[]{:S(2)}, u32[]{:S(2)}) collective-permute-start(bf16[2,160,1280]{2,1,0:T(8,128)(2,1)} %get-tuple-element.29), channel_id=1, source_target_pairs={{0,34},{2,8},{10,40},{8,18},{16,50},{18,24},{26,56},{24,2},{34,64}... | collective-permute-start | bytes 2457608 | tf_op jit(solution)/shard_map/ppermute | solution.py:37
  45.2 21.9 %collective-permute-start.3 = (bf16[2,160,1280]{2,1,0:T(8,128)(2,1)}, bf16[2,160,1280]{2,1,0:T(8,128)(2,1)}, u32[]{:S(2)}, u32[]{:S(2)}) collective-permute-start(bf16[2,160,1280]{2,1,0:T(8,128)(2,1)} %get-tuple-element.30), channel_id=1, source_target_pairs={{0,98},{2,24},{10,104},{8,2},{16,114},{18,8},{26,120},{24,18},{34,... | collective-permute-start | bytes 2457608 | tf_op jit(solution)/shard_map/ppermute | solution.py:37
  49.4 12.7 %collective-permute-start.7 = (bf16[80,1280]{1,0:T(8,128)(2,1)}, bf16[80,1280]{1,0:T(8,128)(2,1)S(1)}, u32[]{:S(2)}, u32[]{:S(2)}) collective-permute-start(bf16[80,1280]{1,0:T(8,128)(2,1)} %get-tuple-element.34), channel_id=1, source_target_pairs={{0,10},{2,32},{10,16},{8,42},{16,26},{18,48},{26,0},{24,58},{34,40... | collective-permute-start | bytes 614408 | tf_op jit(solution)/shard_map/ppermute | solution.py:37
  51.6 10.5 %collective-permute-start.8 = (bf16[80,1280]{1,0:T(8,128)(2,1)}, bf16[80,1280]{1,0:T(8,128)(2,1)S(1)}, u32[]{:S(2)}, u32[]{:S(2)}) collective-permute-start(bf16[80,1280]{1,0:T(8,128)(2,1)} %get-tuple-element.35), channel_id=1, source_target_pairs={{0,26},{2,96},{10,0},{8,106},{16,10},{18,112},{26,16},{24,122},{34... | collective-permute-start | bytes 614408 | tf_op jit(solution)/shard_map/ppermute | solution.py:37
  53.8 8.3 %collective-permute-start.9 = (bf16[80,1280]{1,0:T(8,128)(2,1)S(1)}, bf16[80,1280]{1,0:T(8,128)(2,1)S(1)}, u32[]{:S(2)}, u32[]{:S(2)}) collective-permute-start(bf16[80,1280]{1,0:T(8,128)(2,1)S(1)} %get-tuple-element.36), channel_id=1, source_target_pairs={{0,16},{2,66},{10,26},{8,72},{16,0},{18,82},{26,10},{24,88},{34,50... | collective-permute-start | bytes 614408 | tf_op jit(solution)/shard_map/ppermute | solution.py:37
  63.3 10.8 %collective-permute-start.14 = (f32[40,1280]{1,0:T(8,128)S(1)}, f32[40,1280]{1,0:T(8,128)S(1)}, u32[]{:S(2)}, u32[]{:S(2)}) collective-permute-start(f32[40,1280]{1,0:T(8,128)S(1)} %get-tuple-element.40), channel_id=1, source_target_pairs={{0,4},{4,0},{1,5},{5,1},{2,6},{6,2},{3,7},{7,3},{8,12},{12,8},{9,1... | collective-permute-start | bytes 614408 | tf_op jit(solution)/shard_map/ppermute | solution.py:25
  64.6 12.4 %collective-permute-start.12 = (f32[40,1280]{1,0:T(8,128)S(1)}, f32[40,1280]{1,0:T(8,128)S(1)}, u32[]{:S(2)}, u32[]{:S(2)}) collective-permute-start(f32[40,1280]{1,0:T(8,128)S(1)} %get-tuple-element.40), channel_id=1, source_target_pairs={{0,5},{1,4},{4,1},{5,0},{2,7},{3,6},{6,3},{7,2},{8,13},{9,12},{12,... | collective-permute-start | bytes 614408 | tf_op jit(solution)/shard_map/ppermute | solution.py:507
  66.4 10.6 %collective-permute-start.13 = (f32[40,1280]{1,0:T(8,128)S(1)}, f32[40,1280]{1,0:T(8,128)S(1)}, u32[]{:S(2)}, u32[]{:S(2)}) collective-permute-start(f32[40,1280]{1,0:T(8,128)S(1)} %get-tuple-element.41.a), channel_id=1, source_target_pairs={{0,1},{1,0},{2,3},{3,2},{4,5},{5,4},{6,7},{7,6},{8,9},{9,8},{10,11... | collective-permute-start | bytes 614408 | tf_op jit(solution)/shard_map/ppermute | solution.py:25
  70.6 23.9 %collective-permute-start.10 = (bf16[4,160,1280]{2,1,0:T(8,128)(2,1)}, bf16[4,160,1280]{2,1,0:T(8,128)(2,1)S(1)}, u32[]{:S(2)}, u32[]{:S(2)}) collective-permute-start(bf16[4,160,1280]{2,1,0:T(8,128)(2,1)} %get-tuple-element.37), channel_id=1, source_target_pairs={{0,34},{2,8},{10,40},{8,18},{16,50},{18,24},{26,56},{24,2},{34,64}... | collective-permute-start | bytes 4915208 | tf_op jit(solution)/shard_map/ppermute | solution.py:37
  72.5 26.0 %collective-permute-start.11 = (bf16[4,160,1280]{2,1,0:T(8,128)(2,1)}, bf16[4,160,1280]{2,1,0:T(8,128)(2,1)S(1)}, u32[]{:S(2)}, u32[]{:S(2)}) collective-permute-start(bf16[4,160,1280]{2,1,0:T(8,128)(2,1)} %get-tuple-element.38), channel_id=1, source_target_pairs={{0,98},{2,24},{10,104},{8,2},{16,114},{18,8},{26,120},{24,18},{34,... | collective-permute-start | bytes 4915208 | tf_op jit(solution)/shard_map/ppermute | solution.py:37
  81.1 24.1 %all-to-all-start = ((bf16[128,16,128]{2,1,0:T(8,128)(2,1)}), bf16[128,16,128]{2,1,0:T(8,128)(2,1)}, u32[]{:S(2)}, u32[]{:S(2)}) async-start(bf16[128,16,128]{2,1,0:T(8,128)(2,1)} %left_product.1.refs_3_), calls=%async_computation | async-start | bytes 1048576 | tf_op jit(solution)/shard_map/all_to_all | solution.py:510
  101.3 9.5 %collective-permute-start.15 = (bf16[160,1280]{1,0:T(8,128)(2,1)}, bf16[160,1280]{1,0:T(8,128)(2,1)S(1)}, u32[]{:S(2)}, u32[]{:S(2)}) collective-permute-start(bf16[160,1280]{1,0:T(8,128)(2,1)} %get-tuple-element.43.late), channel_id=1, source_target_pairs={{0,10},{2,32},{10,16},{8,42},{16,26},{18,48},{26,0},{24,58},{34,40... | collective-permute-start | bytes 1228808 | tf_op jit(solution)/shard_map/ppermute | solution.py:37
  102.9 8.0 %collective-permute-start.16 = (bf16[160,1280]{1,0:T(8,128)(2,1)}, bf16[160,1280]{1,0:T(8,128)(2,1)S(1)}, u32[]{:S(2)}, u32[]{:S(2)}) collective-permute-start(bf16[160,1280]{1,0:T(8,128)(2,1)} %get-tuple-element.44), channel_id=1, source_target_pairs={{0,26},{2,96},{10,0},{8,106},{16,10},{18,112},{26,16},{24,122},{34... | collective-permute-start | bytes 1228808 | tf_op jit(solution)/shard_map/ppermute | solution.py:37
  104.4 10.7 %collective-permute-start.17 = (bf16[160,1280]{1,0:T(8,128)(2,1)}, bf16[160,1280]{1,0:T(8,128)(2,1)S(1)}, u32[]{:S(2)}, u32[]{:S(2)}) collective-permute-start(bf16[160,1280]{1,0:T(8,128)(2,1)} %get-tuple-element.45), channel_id=1, source_target_pairs={{0,16},{2,66},{10,26},{8,72},{16,0},{18,82},{26,10},{24,88},{34,50... | collective-permute-start | bytes 1228808 | tf_op jit(solution)/shard_map/ppermute | solution.py:37
  116.6 6.6 %collective-permute-start.18 = (bf16[80,1280]{1,0:T(8,128)(2,1)S(1)}, bf16[80,1280]{1,0:T(8,128)(2,1)S(1)}, u32[]{:S(2)}, u32[]{:S(2)}) collective-permute-start(bf16[80,1280]{1,0:T(8,128)(2,1)S(1)} %get-tuple-element.47), channel_id=1, source_target_pairs={{0,4},{4,0},{1,5},{5,1},{2,6},{6,2},{3,7},{7,3},{8,12},{12,8},{9,1... | collective-permute-start | bytes 614408 | tf_op jit(solution)/shard_map/ppermute | solution.py:25
  123.2 2.2 %collective-permute-start.19 = (f32[40,1280]{1,0:T(8,128)S(1)}, f32[40,1280]{1,0:T(8,128)S(1)}, u32[]{:S(2)}, u32[]{:S(2)}) collective-permute-start(f32[40,1280]{1,0:T(8,128)S(1)} %dynamic-slice_bitcast_fusion), channel_id=1, source_target_pairs={{0,2},{2,0},{1,3},{3,1},{4,6},{6,4},{5,7},{7,5},{8,10},{10,8},{9,1... | collective-permute-start | bytes 614408 | tf_op jit(solution)/shard_map/ppermute | solution.py:25
